TPU v7x, 32 devices: a whole 2x2x4 slice. The times are simulated.
32 devices in a mesh: blk: 8 (over z, y), rep: 4 (over x, core).
Axes of the slice: x: 2, y: 2, z: 4, core: 2. Of those that a mesh axis runs over, the one named last changes fastest.
Arguments:
- segment_ids: int32 [8192], P('rep'), parts along dimension 0, may hold values from 0 to 511, as said below
- block_mask: int32 [32, 8], P('rep'), parts along dimension 0, may hold values from 0 to 1, as said below
- queries: bfloat16 [8192, 640], P(('rep', 'blk')), parts along dimension 0, may hold values from -256 to 256
- keys: bfloat16 [8192, 640], P(('rep', 'blk')), parts along dimension 0, may hold values from -8 to 8
- values: bfloat16 [8192, 640], P(('rep', 'blk')), parts along dimension 0, may hold values from -6 to 6
- tokens: bfloat16 [8192, 1280], P(('rep', 'blk')), parts along dimension 0, may hold values from -6 to 6
- out_weight: bfloat16 [640, 1280], replicated, may hold values from -6 to 6
- owners: int32 [2048], P(('rep', 'blk')), parts along dimension 0, may hold values from 0 to 7, as said below
- offsets: int32 [2048], P(('rep', 'blk')), parts along dimension 0, may hold values from 0 to 127, as said below
Outputs:
- received: bfloat16 [4096, 5120], P(('rep', 'blk')), parts along dimension 0
There are 4 independent parts, one for each index of `rep`. A program takes and returns all parts, laid end to end along the dimension named above; an argument that names none is the same for every part. Nothing has to cross between parts.
Inputs may be any that keep to these rules, and one draw needn't show every extreme that they name: `segment_ids`: never falls; every segment has a multiple of 4 patches and at most 768. `block_mask`: 1 exactly where the two blocks share a segment id. `owners`: the merged rows of one block name one owner at most 16 times; each owner is named by at most 128 rows. Rows that name the same owner have distinct offsets.
All inputs are finite; a program needn't handle non-finite values.
Results may differ from a plain program's by a relative error of at most 0.0065.
Values may be sent and summed in bfloat16 or wider, within the bound.
No kernel may reach another device: no remote copies, remote signals or barrier semaphores. Data moves between devices by JAX's collectives and lax.ppermute only.
A program may use at most 64 MiB of HBM per device.

v0:
```python
import jax
import jax.numpy as jnp
from jax import lax
from jax.sharding import PartitionSpec as P

HEADS = 8
SPAN = 3


NEG = -1e30


def shifted(block, axis, distance):
    devices = range(lax.axis_size(axis))
    route = [(i - distance, i) for i in devices if i - distance in devices]
    return lax.ppermute(block, axis, route)


def attend(state, query_heads, key_part, value_part, allowed, scale):
    peak, total, accum = state
    scores = (
        jnp.einsum("rhd,khd->hrk", query_heads, key_part, preferred_element_type=jnp.float32)
        * scale
    )
    scores = jnp.where(allowed[None], scores, NEG)
    new_peak = jnp.maximum(peak, jnp.max(scores, axis=2, keepdims=True))
    weights = jnp.where(allowed[None], jnp.exp(scores - new_peak), 0.0)
    factor = jnp.exp(peak - new_peak)
    total = total * factor + jnp.sum(weights, axis=2, keepdims=True)
    accum = accum * factor + jnp.einsum(
        "hrk,khd->hrd", weights.astype(jnp.bfloat16), value_part, preferred_element_type=jnp.float32
    )
    return (new_peak, total, accum)


def block_flag(mask_row, column, nblocks):
    inside = (column >= 0) & (column < nblocks)
    return jnp.where(inside, mask_row[jnp.clip(column, 0, nblocks - 1)], 0)


def per_device(segment_ids, block_mask, queries, keys, values, tokens, out_weight, owners, offsets):
    rows = queries.shape[0]
    features = queries.shape[1]
    width = tokens.shape[1]
    hdim = features // HEADS
    nblocks = lax.axis_size("blk")
    block_index = lax.axis_index("blk")
    scale = 1.0 / jnp.sqrt(jnp.float32(hdim))
    pairs = (keys, values)
    fetched = {0: pairs}
    for dist in [d for d in range(-SPAN, SPAN + 1) if d != 0]:
        fetched[dist] = shifted((pairs[0], pairs[1]), "blk", -dist)
    mask_row = lax.dynamic_index_in_dim(block_mask, block_index, 0, keepdims=False)
    query_seg = lax.dynamic_slice_in_dim(segment_ids, block_index * rows, rows, 0)
    query_heads = queries.reshape(rows, HEADS, hdim)

    def seg_of(column):
        return lax.dynamic_slice_in_dim(
            segment_ids, jnp.clip(column, 0, nblocks - 1) * rows, rows, 0
        )

    state = (
        jnp.full((HEADS, rows, 1), NEG, jnp.float32),
        jnp.zeros((HEADS, rows, 1), jnp.float32),
        jnp.zeros((HEADS, rows, hdim), jnp.float32),
    )
    own_allowed = (query_seg[:, None] == query_seg[None, :]) & (
        block_flag(mask_row, block_index, nblocks) > 0
    )
    state = attend(
        state,
        query_heads,
        keys.reshape(rows, HEADS, hdim),
        values.reshape(rows, HEADS, hdim),
        own_allowed,
        scale,
    )
    for dist in range(1, SPAN + 1):
        lower = block_index - dist
        upper = block_index + dist
        flag_low = block_flag(mask_row, lower, nblocks)
        flag_high = block_flag(mask_row, upper, nblocks)
        key_cat = jnp.concatenate([fetched[-dist][0], fetched[dist][0]], axis=0).reshape(
            2 * rows, HEADS, hdim
        )
        value_cat = jnp.concatenate([fetched[-dist][1], fetched[dist][1]], axis=0).reshape(
            2 * rows, HEADS, hdim
        )
        seg_cat = jnp.concatenate([seg_of(lower), seg_of(upper)])
        flag_cat = jnp.concatenate(
            [jnp.full((rows,), flag_low, jnp.int32), jnp.full((rows,), flag_high, jnp.int32)]
        )
        allowed = (query_seg[:, None] == seg_cat[None, :]) & (flag_cat[None, :] > 0)
        state = lax.cond(
            flag_low + flag_high > 0,
            lambda carry: attend(carry, query_heads, key_cat, value_cat, allowed, scale),
            lambda carry: carry,
            state,
        )
    peak, total, accum = state
    attended = jnp.transpose(accum / total, (1, 0, 2)).reshape(rows, features).astype(jnp.bfloat16)
    mrows = rows // 4
    capacity = 2 * mrows
    pair_rows = max(2, 2 * mrows // nblocks)
    onehot = (owners[:, None] == jnp.arange(nblocks)[None, :]).astype(jnp.int32)
    ranks = jnp.sum((jnp.cumsum(onehot, axis=0) - 1) * onehot, axis=1)
    slot_index = owners * pair_rows + ranks
    outgoing_offsets = (
        jnp.full((nblocks * pair_rows,), capacity, jnp.int32).at[slot_index].set(offsets)
    )
    hidden = (
        tokens.astype(jnp.float32)
        + jnp.dot(attended, out_weight, preferred_element_type=jnp.float32)
    ).astype(jnp.bfloat16)
    merged = hidden.reshape(mrows, 4 * width)
    outgoing = jnp.zeros((nblocks * pair_rows, 4 * width), jnp.bfloat16).at[slot_index].set(merged)
    arrived, arrived_offsets = (
        lax.all_to_all(
            outgoing.reshape(nblocks, pair_rows, 4 * width),
            "blk",
            split_axis=0,
            concat_axis=0,
            tiled=True,
        ),
        lax.all_to_all(
            outgoing_offsets.reshape(nblocks, pair_rows),
            "blk",
            split_axis=0,
            concat_axis=0,
            tiled=True,
        ),
    )
    buffer = jnp.zeros((capacity, 4 * width), jnp.bfloat16)
    return buffer.at[arrived_offsets.reshape(-1)].set(arrived.reshape(-1, 4 * width), mode="drop")


def solution(mesh):
    placed = (
        P("rep"),
        P("rep", None),
        P(("rep", "blk"), None),
        P(("rep", "blk"), None),
        P(("rep", "blk"), None),
        P(("rep", "blk"), None),
        P(),
        P(("rep", "blk")),
        P(("rep", "blk")),
    )
    return jax.shard_map(
        per_device, mesh=mesh, in_specs=placed, out_specs=P(("rep", "blk"), None), check_vma=False
    )
```

profile of v0, /device:TPU:0, one launch (start us, length us, event | category | flops | bytes accessed | tf_op | source)
XLA Modules:
  0.0 133.0 jit_solution(4713034760253775346)
XLA Ops:
  0.0 5.0 %collective-permute-start = (bf16[256,640]{1,0:T(8,128)(2,1)}, bf16[256,640]{1,0:T(8,128)(2,1)S(1)}, u32[]{:S(2)}, u32[]{:S(2)}) collective-permute-start(bf16[256,640]{1,0:T(8,128)(2,1)} %param.18), channel_id=1, source_target_pairs={{0,4},{4,8},{8,12},{12,16},{16,20},{20,24},{24,28},{1,5},{5,9},{9,... | collective-permute-start | bytes 983048 | tf_op jit(solution)/shard_map/ppermute | solution.py:16
  6.3 5.3 %collective-permute-start.2 = (bf16[256,640]{1,0:T(8,128)(2,1)}, bf16[256,640]{1,0:T(8,128)(2,1)}, u32[]{:S(2)}, u32[]{:S(2)}) collective-permute-start(bf16[256,640]{1,0:T(8,128)(2,1)} %param.19), channel_id=1, source_target_pairs={{0,4},{4,8},{8,12},{12,16},{16,20},{20,24},{24,28},{1,5},{5,9},{9,... | collective-permute-start | bytes 983048 | tf_op jit(solution)/shard_map/ppermute | solution.py:16
  12.9 1.9 %copy.40 = bf16[256,640]{0,1:T(8,128)(2,1)} copy(bf16[256,640]{1,0:T(8,128)(2,1)} %param.18) | data formatting | bytes 655360 | tf_op args[3]
  14.8 6.4 %collective-permute-start.4 = (bf16[256,640]{0,1:T(8,128)(2,1)}, bf16[256,640]{0,1:T(8,128)(2,1)}, u32[]{:S(2)}, u32[]{:S(2)}) collective-permute-start(bf16[256,640]{0,1:T(8,128)(2,1)} %copy.40), channel_id=1, source_target_pairs={{0,8},{4,12},{8,16},{12,20},{16,24},{20,28},{1,9},{5,13},{9,17},{1... | collective-permute-start | bytes 983048 | tf_op jit(solution)/shard_map/ppermute | solution.py:16
  25.1 3.3 %all-to-all-start = ((s32[8,1,16]{2,1,0:T(1,128)}), s32[8,1,16]{2,1,0:T(1,128)S(1)}, u32[]{:S(2)}, u32[]{:S(2)}) async-start(s32[8,1,16]{2,1,0:T(1,128)} %bitcast.16), calls=%async_computation | async-start | bytes 8192 | tf_op jit(solution)/shard_map/all_to_all | solution.py:125
  28.4 1.9 %copy.41 = bf16[256,640]{0,1:T(8,128)(2,1)} copy(bf16[256,640]{1,0:T(8,128)(2,1)} %param.19) | data formatting | bytes 655360 | tf_op args[4]
  30.3 1.6 %fusion.62 = (s32[1,1]{1,0:T(1,128)}, s32[1,1]{1,0:T(1,128)}, s32[1,1]{1,0:T(1,128)}, s32[1,1]{1,0:T(1,128)}, s32[1,1]{1,0:T(1,128)}, /*index=5*/s32[1,1]{1,0:T(1,128)}, s32[1,1]{1,0:T(1,128)}) fusion(s32[8,8]{1,0:T(8,128)} %param.16, s32[]{:T(128)S(6)} %select_n.99, s32[]{:T(128)S(6)} %min.55, s32[]{:T(128)S(6)} %min.51, s32[]{:T(128)S(6)} %min.49, ...), kind=kLoop, calls=%fused_computation.98 | loop fusion | bytes 88 | tf_op jit(solution)/shard_map/dynamic_slice | solution.py:38
  34.9 1.5 %fusion.41 = (f32[8,256]{1,0:T(8,128)S(1)}, f32[8,256,256]{1,2,0:T(8,128)S(1)}) fusion(pred[256,256]{0,1:T(8,128)(4,1)S(1)} %compare_and_fusion.3, bf16[256,8,80]{0,2,1:T(8,128)(2,1)S(1)} %bitcast.76, bf16[256,8,80]{0,2,1:T(8,128)(2,1)} %bitcast.26), kind=kOutput, calls=%fused_computation.57 | convolution fusion | flops 85456896 | bytes 2826240 | tf_op jit(solution)/shard_map/rhd,khd->hrk/dot_general | solution.py:22
  36.9 2.5 %convolution_add_fusion.1 = f32[8,256,80]{1,2,0:T(8,128)} fusion(bf16[256,8,80]{0,2,1:T(8,128)(2,1)} %bitcast.29, f32[8,256,256]{1,2,0:T(8,128)S(1)} %get-tuple-element.172, f32[8,256]{1,0:T(8,128)S(1)} %get-tuple-element.163, pred[256,256]{0,1:T(8,128)(4,1)S(1)} %compare_and_fusion.3, f32[8,256]{1,0:T(8,128)S(1)} %get-tuple-element.161), kind=kOutput, calls=%fused_computation.60 | convolution fusion | flops 86671360 | bytes 3162112 | tf_op jit(solution)/shard_map/hrk,khd->hrd/dot_general | solution.py:30
  44.8 5.3 %collective-permute-start.6 = (bf16[256,640]{0,1:T(8,128)(2,1)}, bf16[256,640]{0,1:T(8,128)(2,1)}, u32[]{:S(2)}, u32[]{:S(2)}) collective-permute-start(bf16[256,640]{0,1:T(8,128)(2,1)} %copy.41), channel_id=1, source_target_pairs={{0,8},{4,12},{8,16},{12,20},{16,24},{20,28},{1,9},{5,13},{9,17},{1... | collective-permute-start | bytes 983048 | tf_op jit(solution)/shard_map/ppermute | solution.py:16
  51.8 6.6 %collective-permute-start.8 = (bf16[256,640]{0,1:T(8,128)(2,1)}, bf16[256,640]{0,1:T(8,128)(2,1)}, u32[]{:S(2)}, u32[]{:S(2)}) collective-permute-start(bf16[256,640]{0,1:T(8,128)(2,1)} %copy.40), channel_id=1, source_target_pairs={{0,12},{4,16},{8,20},{12,24},{16,28},{1,13},{5,17},{9,21},{13,25},... | collective-permute-start | bytes 983048 | tf_op jit(solution)/shard_map/ppermute | solution.py:16
  61.9 4.7 %conditional.3 = ((f32[8,256,1]{1,0,2:T(8,128)S(1)}, f32[8,256,1]{1,0,2:T(8,128)S(1)}, f32[8,256,80]{1,2,0:T(8,128)})) conditional(s32[]{:T(128)} %convert_element_type.43, (f32[8,256,1]{1,0,2:T(8,128)S(1)}, f32[8,256,1]{1,0,2:T(8,128)S(1)}, f32[8,256,80]{1,2,0:T(8,128)}) %tuple.25, (pred[256,512]{1,0:T(8,128)(4,1)S(1)}, ...), branch_computations={%region_5.6_spmd, %region_6.9_spmd} | conditional | flops 349509632 | bytes 23920756 | solution.py:94
  62.9 1.5 %fusion.2 = f32[8,256]{1,0:T(8,128)S(1)} fusion(f32[8,256,512]{2,1,0:T(8,128)S(1)} %get-tuple-element.151, f32[8,256]{1,0:T(8,128)S(1)} %bitcast.91, pred[256,512]{1,0:T(8,128)(4,1)S(1)} %get-tuple-element.98), kind=kLoop, calls=%fused_computation.7 | loop fusion | flops 5240832 | bytes 4341760 | tf_op jit(solution)/shard_map/cond/branch_1_fun/reduce_sum | solution.py:29
  66.6 6.2 %collective-permute-start.10 = (bf16[256,640]{0,1:T(8,128)(2,1)}, bf16[256,640]{0,1:T(8,128)(2,1)}, u32[]{:S(2)}, u32[]{:S(2)}) collective-permute-start(bf16[256,640]{0,1:T(8,128)(2,1)} %copy.41), channel_id=1, source_target_pairs={{0,12},{4,16},{8,20},{12,24},{16,28},{1,13},{5,17},{9,21},{13,25},... | collective-permute-start | bytes 983048 | tf_op jit(solution)/shard_map/ppermute | solution.py:16
  76.5 5.0 %conditional.4 = ((f32[8,256,1]{1,0,2:T(8,128)S(1)}, f32[8,256,1]{1,0,2:T(8,128)S(1)}, f32[8,256,80]{1,2,0:T(8,128)})) conditional(s32[]{:T(128)} %convert_element_type.42, (f32[8,256,1]{1,0,2:T(8,128)S(1)}, f32[8,256,1]{1,0,2:T(8,128)S(1)}, f32[8,256,80]{1,2,0:T(8,128)}) %get-tuple-element.189, (s32[512]{0:T(512)S(1)}, s32[256,512]{1,0:T(8,128)S(1)}, ...), branch_computations={%region_9.10_spmd, %region_10.13_spmd} | conditional | flops 349772288 | bytes 21961824 | solution.py:94
  77.8 1.5 %fusion.15 = f32[8,256]{1,0:T(8,128)S(1)} fusion(f32[8,256,512]{2,1,0:T(8,128)S(1)} %get-tuple-element.153, f32[8,256]{1,0:T(8,128)S(1)} %bitcast.89, pred[256,512]{1,0:T(8,128)(4,1)S(1)} %compare_and_fusion), kind=kLoop, calls=%fused_computation.22 | loop fusion | flops 5240832 | bytes 4341760 | tf_op jit(solution)/shard_map/cond/branch_1_fun/reduce_sum | solution.py:29
  79.4 1.3 fusion.19
  84.3 4.8 %conditional.5 = ((f32[8,256,1]{1,0,2:T(8,128)S(1)}, f32[8,256,80]{1,2,0:T(8,128)})) conditional(s32[]{:T(128)} %convert_element_type.41, (f32[8,256,1]{1,0,2:T(8,128)S(1)}, f32[8,256,80]{1,2,0:T(8,128)}) %tuple.28, (s32[512]{0:T(512)S(1)}, s32[256,512]{1,0:T(8,128)S(1)}, s32[]{:T(128)}, s32[]{:T(128)}, s32[512]{0:T(512)S(1)}, ...), branch_computations={%region_13.14_spmd, %region_14.17_spmd} | conditional | flops 349772288 | bytes 21945432 | solution.py:94
  85.5 1.5 %fusion.28 = f32[8,256]{1,0:T(8,128)S(1)} fusion(f32[8,256,512]{2,1,0:T(8,128)S(1)} %get-tuple-element.149, f32[8,256]{1,0:T(8,128)S(1)} %fusion.35, pred[256,512]{1,0:T(8,128)(4,1)S(1)} %compare_and_fusion.1), kind=kLoop, calls=%fused_computation.39 | loop fusion | flops 5240832 | bytes 4341760 | tf_op jit(solution)/shard_map/cond/branch_1_fun/reduce_sum | solution.py:29
  87.0 1.3 fusion.32
  91.5 2.7 %scatter_custom_fusion.1 = bf16[128,5120]{1,0:T(8,128)(2,1)} fusion(s32[64]{0:T(128)S(1)} %compare_select_fusion.1, bf16[64,5120]{1,0:T(8,128)(2,1)S(1)} %reshape.190, bf16[]{:T(256)} %constant.147.clone.1), kind=kCustom, calls=%fused_computation.74 | custom fusion | bytes 1310722 | tf_op jit(solution)/shard_map/scatter | solution.py:116
  94.2 5.4 %all-to-all-start.1 = ((bf16[8,16,5120]{2,1,0:T(8,128)(2,1)}), bf16[8,16,5120]{2,1,0:T(8,128)(2,1)S(1)}, u32[]{:S(2)}, u32[]{:S(2)}) async-start(bf16[8,16,5120]{2,1,0:T(8,128)(2,1)} %bitcast.35), calls=%async_computation.1 | async-start | bytes 2621440 | tf_op jit(solution)/shard_map/all_to_all | solution.py:118
  100.8 28.7 %all-to-all-done.1 = bf16[8,16,5120]{2,1,0:T(8,128)(2,1)S(1)} async-done(((bf16[8,16,5120]{2,1,0:T(8,128)(2,1)}), bf16[8,16,5120]{2,1,0:T(8,128)(2,1)S(1)}, u32[]{:S(2)}, u32[]{:S(2)}) %all-to-all-start.1) | async-done | bytes 1310752 | tf_op jit(solution)/shard_map/all_to_all | solution.py:118
  129.5 3.5 %scatter_custom_fusion.2 = bf16[128,5120]{1,0:T(8,128)(2,1)} fusion(s32[128]{0:T(128)S(1)} %fusion.54, bf16[128,5120]{1,0:T(8,128)(2,1)S(1)} %bitcast.84, bf16[]{:T(256)} %constant.147.clone.1), kind=kCustom, calls=%fused_computation.72 | custom fusion | bytes 1310722 | tf_op jit(solution)/shard_map/scatter | solution.py:134
  (90 shorter events, 32.8 us)
Async XLA Ops:
  0.0 90.3 %copy-start = (bf16[640,1280]{1,0:T(8,128)(2,1)S(1)}, bf16[640,1280]{1,0:T(8,128)(2,1)}, u32[]{:S(2)}) copy-start(bf16[640,1280]{1,0:T(8,128)(2,1)} %param.21) | copy-start | bytes 4915204
  0.0 43.5 %collective-permute-start = (bf16[256,640]{1,0:T(8,128)(2,1)}, bf16[256,640]{1,0:T(8,128)(2,1)S(1)}, u32[]{:S(2)}, u32[]{:S(2)}) collective-permute-start(bf16[256,640]{1,0:T(8,128)(2,1)} %param.18), channel_id=1, source_target_pairs={{0,4},{4,8},{8,12},{12,16},{16,20},{20,24},{24,28},{1,5},{5,9},{9,... | collective-permute-start | bytes 983048 | tf_op jit(solution)/shard_map/ppermute | solution.py:16
  5.0 39.8 %collective-permute-start.1 = (bf16[256,640]{1,0:T(8,128)(2,1)}, bf16[256,640]{1,0:T(8,128)(2,1)S(1)}, u32[]{:S(2)}, u32[]{:S(2)}) collective-permute-start(bf16[256,640]{1,0:T(8,128)(2,1)} %param.18), channel_id=1, source_target_pairs={{4,0},{8,4},{12,8},{16,12},{20,16},{24,20},{28,24},{5,1},{9,5},{13... | collective-permute-start | bytes 983048 | tf_op jit(solution)/shard_map/ppermute | solution.py:16
  6.3 43.8 %collective-permute-start.2 = (bf16[256,640]{1,0:T(8,128)(2,1)}, bf16[256,640]{1,0:T(8,128)(2,1)}, u32[]{:S(2)}, u32[]{:S(2)}) collective-permute-start(bf16[256,640]{1,0:T(8,128)(2,1)} %param.19), channel_id=1, source_target_pairs={{0,4},{4,8},{8,12},{12,16},{16,20},{20,24},{24,28},{1,5},{5,9},{9,... | collective-permute-start | bytes 983048 | tf_op jit(solution)/shard_map/ppermute | solution.py:16
  11.6 40.2 %collective-permute-start.3 = (bf16[256,640]{1,0:T(8,128)(2,1)}, bf16[256,640]{1,0:T(8,128)(2,1)}, u32[]{:S(2)}, u32[]{:S(2)}) collective-permute-start(bf16[256,640]{1,0:T(8,128)(2,1)} %param.19), channel_id=1, source_target_pairs={{4,0},{8,4},{12,8},{16,12},{20,16},{24,20},{28,24},{5,1},{9,5},{13... | collective-permute-start | bytes 983048 | tf_op jit(solution)/shard_map/ppermute | solution.py:16
  14.8 43.6 %collective-permute-start.4 = (bf16[256,640]{0,1:T(8,128)(2,1)}, bf16[256,640]{0,1:T(8,128)(2,1)}, u32[]{:S(2)}, u32[]{:S(2)}) collective-permute-start(bf16[256,640]{0,1:T(8,128)(2,1)} %copy.40), channel_id=1, source_target_pairs={{0,8},{4,12},{8,16},{12,20},{16,24},{20,28},{1,9},{5,13},{9,17},{1... | collective-permute-start | bytes 983048 | tf_op jit(solution)/shard_map/ppermute | solution.py:16
  25.1 69.1 %all-to-all-start = ((s32[8,1,16]{2,1,0:T(1,128)}), s32[8,1,16]{2,1,0:T(1,128)S(1)}, u32[]{:S(2)}, u32[]{:S(2)}) async-start(s32[8,1,16]{2,1,0:T(1,128)} %bitcast.16), calls=%async_computation | async-start | bytes 8192 | tf_op jit(solution)/shard_map/all_to_all | solution.py:125
  43.5 23.1 %collective-permute-start.5 = (bf16[256,640]{0,1:T(8,128)(2,1)}, bf16[256,640]{0,1:T(8,128)(2,1)}, u32[]{:S(2)}, u32[]{:S(2)}) collective-permute-start(bf16[256,640]{0,1:T(8,128)(2,1)} %copy.40), channel_id=1, source_target_pairs={{8,0},{12,4},{16,8},{20,12},{24,16},{28,20},{9,1},{13,5},{17,9},{2... | collective-permute-start | bytes 983048 | tf_op jit(solution)/shard_map/ppermute | solution.py:16
  44.8 28.0 %collective-permute-start.6 = (bf16[256,640]{0,1:T(8,128)(2,1)}, bf16[256,640]{0,1:T(8,128)(2,1)}, u32[]{:S(2)}, u32[]{:S(2)}) collective-permute-start(bf16[256,640]{0,1:T(8,128)(2,1)} %copy.41), channel_id=1, source_target_pairs={{0,8},{4,12},{8,16},{12,20},{16,24},{20,28},{1,9},{5,13},{9,17},{1... | collective-permute-start | bytes 983048 | tf_op jit(solution)/shard_map/ppermute | solution.py:16
  50.2 25.1 %collective-permute-start.7 = (bf16[256,640]{0,1:T(8,128)(2,1)}, bf16[256,640]{0,1:T(8,128)(2,1)}, u32[]{:S(2)}, u32[]{:S(2)}) collective-permute-start(bf16[256,640]{0,1:T(8,128)(2,1)} %copy.41), channel_id=1, source_target_pairs={{8,0},{12,4},{16,8},{20,12},{24,16},{28,20},{9,1},{13,5},{17,9},{2... | collective-permute-start | bytes 983048 | tf_op jit(solution)/shard_map/ppermute | solution.py:16
  51.8 29.7 %collective-permute-start.8 = (bf16[256,640]{0,1:T(8,128)(2,1)}, bf16[256,640]{0,1:T(8,128)(2,1)}, u32[]{:S(2)}, u32[]{:S(2)}) collective-permute-start(bf16[256,640]{0,1:T(8,128)(2,1)} %copy.40), channel_id=1, source_target_pairs={{0,12},{4,16},{8,20},{12,24},{16,28},{1,13},{5,17},{9,21},{13,25},... | collective-permute-start | bytes 983048 | tf_op jit(solution)/shard_map/ppermute | solution.py:16
  58.4 23.1 %collective-permute-start.9 = (bf16[256,640]{0,1:T(8,128)(2,1)}, bf16[256,640]{0,1:T(8,128)(2,1)}, u32[]{:S(2)}, u32[]{:S(2)}) collective-permute-start(bf16[256,640]{0,1:T(8,128)(2,1)} %copy.40), channel_id=1, source_target_pairs={{12,0},{16,4},{20,8},{24,12},{28,16},{13,1},{17,5},{21,9},{25,13},... | collective-permute-start | bytes 983048 | tf_op jit(solution)/shard_map/ppermute | solution.py:16
  61.9 2.5 %copy-start.1 = (bf16[512,8,80]{0,2,1:T(8,128)(2,1)S(1)}, bf16[512,8,80]{0,2,1:T(8,128)(2,1)}, u32[]{:S(2)}) copy-start(bf16[512,8,80]{0,2,1:T(8,128)(2,1)} %get-tuple-element.103) | copy-start | bytes 1966084 | tf_op jit(solution)/shard_map/cond
  61.9 2.5 %copy-start.2 = (f32[8,256,80]{1,2,0:T(8,128)S(1)}, f32[8,256,80]{1,2,0:T(8,128)}, u32[]{:S(2)}) copy-start(f32[8,256,80]{1,2,0:T(8,128)} %get-tuple-element.102) | copy-start | bytes 1966084 | tf_op jit(solution)/shard_map/cond
  65.8 0.8 copy-start.3
  66.6 16.0 %collective-permute-start.10 = (bf16[256,640]{0,1:T(8,128)(2,1)}, bf16[256,640]{0,1:T(8,128)(2,1)}, u32[]{:S(2)}, u32[]{:S(2)}) collective-permute-start(bf16[256,640]{0,1:T(8,128)(2,1)} %copy.41), channel_id=1, source_target_pairs={{0,12},{4,16},{8,20},{12,24},{16,28},{1,13},{5,17},{9,21},{13,25},... | collective-permute-start | bytes 983048 | tf_op jit(solution)/shard_map/ppermute | solution.py:16
  72.8 10.4 %collective-permute-start.11 = (bf16[256,640]{0,1:T(8,128)(2,1)}, bf16[256,640]{0,1:T(8,128)(2,1)}, u32[]{:S(2)}, u32[]{:S(2)}) collective-permute-start(bf16[256,640]{0,1:T(8,128)(2,1)} %copy.41), channel_id=1, source_target_pairs={{12,0},{16,4},{20,8},{24,12},{28,16},{13,1},{17,5},{21,9},{25,13},... | collective-permute-start | bytes 983048 | tf_op jit(solution)/shard_map/ppermute | solution.py:16
  76.8 2.6 %copy-start.4 = (f32[8,256,80]{1,2,0:T(8,128)S(1)}, f32[8,256,80]{1,2,0:T(8,128)}, u32[]{:S(2)}) copy-start(f32[8,256,80]{1,2,0:T(8,128)} %get-tuple-element.113) | copy-start | bytes 1966084 | tf_op jit(solution)/shard_map/cond
  80.7 0.8 copy-start.5
  84.3 6.0 %copy-start.8 = (bf16[256,1280]{1,0:T(8,128)(2,1)S(1)}, bf16[256,1280]{1,0:T(8,128)(2,1)}, u32[]{:S(2)}) copy-start(bf16[256,1280]{1,0:T(8,128)(2,1)} %param.20) | copy-start | bytes 1966084
  84.5 2.6 %copy-start.6 = (f32[8,256,80]{1,2,0:T(8,128)S(1)}, f32[8,256,80]{1,2,0:T(8,128)}, u32[]{:S(2)}) copy-start(f32[8,256,80]{1,2,0:T(8,128)} %get-tuple-element.124) | copy-start | bytes 1966084 | tf_op jit(solution)/shard_map/cond
  88.3 0.8 copy-start.7
  94.2 35.3 %all-to-all-start.1 = ((bf16[8,16,5120]{2,1,0:T(8,128)(2,1)}), bf16[8,16,5120]{2,1,0:T(8,128)(2,1)S(1)}, u32[]{:S(2)}, u32[]{:S(2)}) async-start(bf16[8,16,5120]{2,1,0:T(8,128)(2,1)} %bitcast.35), calls=%async_computation.1 | async-start | bytes 2621440 | tf_op jit(solution)/shard_map/all_to_all | solution.py:118
where the time goes:
time: 135 us; the launch traced here: 133 us
  starting transfers between devices  51.2 us (38%)
  waiting for transfers between devices  29.3 us (22%)
  local copies, waits for them, and re-layouts  20.3 us (15%)
  other arithmetic  15.4 us (11%)
  matrix products  11.5 us (9%)
  between operations  4.91 us (4%)
    ppermute x12, starting transfers between devices, shifted(): return lax.ppermute(block, axis, route)  42.5 us
    all_to_all x1, waiting for transfers between devices, per_device(): lax.all_to_all(outgoing.reshape(nblocks, pair_rows, 4 * width), 'blk', sp...  28.7 us
    dot_general x4, matrix products, attend(): jnp.einsum('hrk,khd->hrd', weights.astype(jnp.bfloat16), value_part, pref...  6.36 us
    all_to_all x1, starting transfers between devices, per_device(): lax.all_to_all(outgoing.reshape(nblocks, pair_rows, 4 * width), 'blk', sp...  5.43 us
    reduce_sum x4, other arithmetic, attend(): total = total * factor + jnp.sum(weights, axis=2, keepdims=True)  5.11 us
    unnamed x7, local copies, waits for them, and re-layouts  4.9 us
    dot_general x4, matrix products, attend(): jnp.einsum('rhd,khd->hrk', query_heads, key_part, preferred_element_type=...  4.42 us
    scatter x1, local copies, waits for them, and re-layouts, per_device(): buffer.at[arrived_offsets.reshape(-1)]  3.48 us
  transfers between devices with their start and end apart: 14, of which 2 were waited for; matrix products, arithmetic and copies ran while one was open for 30% of the time, Pallas kernels for 0%

commit v1 on v0

v1 whole, which is shorter than its diff:
```python
import functools

import jax
import jax.numpy as jnp
from jax import lax
from jax.experimental import pallas as pl
from jax.experimental.pallas import tpu as pltpu
from jax.sharding import PartitionSpec as P

HEADS = 8
SPAN = 3
NEG = -1e30
LOG2E = 1.4426950408889634
VMEM_LIMIT = 40 * 1024 * 1024


def params():
    return pltpu.CompilerParams(vmem_limit_bytes=VMEM_LIMIT)


def vmem():
    return pl.BlockSpec(memory_space=pltpu.VMEM)


def smem():
    return pl.BlockSpec(memory_space=pltpu.SMEM)


def split_heads_kernel(q_ref, k_ref, v_ref, out_ref):
    hdim = q_ref.shape[1] // HEADS
    for part, ref in enumerate((q_ref, k_ref, v_ref)):
        turned = ref[...].T
        for head in range(HEADS):
            out_ref[head, part * hdim : (part + 1) * hdim, :] = turned[
                head * hdim : (head + 1) * hdim, :
            ]


def split_heads(queries, keys, values):
    rows, features = queries.shape
    hdim = features // HEADS
    return pl.pallas_call(
        split_heads_kernel,
        out_shape=jax.ShapeDtypeStruct((HEADS, 3 * hdim, rows), queries.dtype),
        in_specs=[vmem()] * 3,
        out_specs=vmem(),
        compiler_params=params(),
    )(queries, keys, values)


def attention_kernel(halo, low_ref, count_ref, x_ref, *refs):
    if halo:
        below_ref, above_ref, seg_ref, out_ref, key_s, value_s, seg_s = refs
    else:
        seg_ref, out_ref, key_s, seg_s = refs
    blocks, triple, rows = x_ref.shape
    hdim = triple // 3
    base = SPAN if halo else 0
    factor = LOG2E / (hdim**0.5)
    extended = blocks + 2 * base

    for b in range(extended):
        if b < base:
            key_s[b] = below_ref[b, :hdim, :].T
            value_s[b] = below_ref[b, hdim:, :]
        elif b >= base + blocks:
            key_s[b] = above_ref[b - base - blocks, :hdim, :].T
            value_s[b] = above_ref[b - base - blocks, hdim:, :]
        else:
            key_s[b] = x_ref[b - base, hdim : 2 * hdim, :].T
            if halo:
                value_s[b] = x_ref[b - base, 2 * hdim :, :]
        seg_s[b] = jnp.broadcast_to(seg_ref[b], (128, rows)).T

    def value_block(b):
        return value_s[b] if halo else x_ref[b, 2 * hdim :, :]

    def one_block(i, carry):
        low = low_ref[i]
        count = count_ref[i]
        query = x_ref[i, :hdim, :]
        query_seg = seg_ref[i + base]

        for size in range(1, 2 * SPAN + 2):

            @pl.when(count == size)
            def _():
                key = key_s[pl.ds(low, size)].reshape(size * rows, hdim)
                scores = jnp.dot(key, query, preferred_element_type=jnp.float32)
                key_seg = seg_s[pl.ds(low, size)].reshape(size * rows, 128)
                key_seg = jnp.concatenate([key_seg] * (rows // 128), axis=1)
                scores = jnp.where(key_seg == query_seg, scores, NEG)
                peak = jnp.max(scores, axis=0, keepdims=True)
                weights = jnp.exp2((scores - peak) * factor)
                total = jnp.sum(weights, axis=0, keepdims=True)
                weights = weights.astype(jnp.bfloat16)
                mixed = jnp.zeros((hdim, rows), jnp.float32)
                for b in range(size):
                    mixed += jnp.dot(
                        value_block(low + b),
                        weights[b * rows : (b + 1) * rows],
                        preferred_element_type=jnp.float32,
                    )
                out_ref[i] = (mixed / total).astype(out_ref.dtype)

        return carry

    lax.fori_loop(0, blocks, one_block, 0)


def attention(low, count, x, halos, segs):
    blocks, triple, rows = x.shape
    hdim = triple // 3
    extended = segs.shape[0]
    scratch = [pltpu.VMEM((extended, rows, hdim), jnp.bfloat16)]
    if halos:
        scratch.append(pltpu.VMEM((extended, hdim, rows), jnp.bfloat16))
    scratch.append(pltpu.VMEM((extended, rows, 128), jnp.float32))
    return pl.pallas_call(
        functools.partial(attention_kernel, bool(halos)),
        out_shape=jax.ShapeDtypeStruct((blocks, hdim, rows), jnp.bfloat16),
        in_specs=[smem(), smem()] + [vmem()] * (2 + len(halos)),
        out_specs=vmem(),
        scratch_shapes=scratch,
        compiler_params=params(),
    )(low, count, x, *halos, segs)


def project_kernel(slot_ref, attended_ref, weight_ref, tokens_ref, out_ref):
    slots = out_ref.shape[0]
    rows, width = tokens_ref.shape
    hidden = tokens_ref[...].astype(jnp.float32) + lax.dot_general(
        attended_ref[...],
        weight_ref[...],
        (((0,), (0,)), ((), ())),
        preferred_element_type=jnp.float32,
    )
    hidden = hidden.astype(jnp.bfloat16)
    slot = lax.broadcasted_iota(jnp.int32, (slots, rows), 0)
    place = lax.broadcasted_iota(jnp.int32, (slots, rows), 1) % 4
    mine = slot_ref[...] == slot
    for j in range(4):
        pick = jnp.where(mine & (place == j), 1.0, 0.0).astype(jnp.bfloat16)
        out_ref[:, j * width : (j + 1) * width] = jnp.dot(
            pick, hidden, preferred_element_type=jnp.float32
        ).astype(jnp.bfloat16)


def project(slot_of_patch, attended, out_weight, tokens, slots):
    rows, width = tokens.shape
    return pl.pallas_call(
        project_kernel,
        out_shape=jax.ShapeDtypeStruct((slots, 4 * width), jnp.bfloat16),
        in_specs=[vmem()] * 4,
        out_specs=vmem(),
        compiler_params=params(),
    )(slot_of_patch, attended, out_weight, tokens)


def place_kernel(offsets_ref, arrived_ref, out_ref):
    capacity = out_ref.shape[0]
    slots = arrived_ref.shape[0]
    row = lax.broadcasted_iota(jnp.int32, (capacity, slots), 0)
    pick = jnp.where(offsets_ref[...] == row, 1.0, 0.0).astype(jnp.bfloat16)
    out_ref[...] = jnp.dot(
        pick, arrived_ref[...], preferred_element_type=jnp.float32
    ).astype(jnp.bfloat16)


def place(offsets, arrived, capacity):
    slots, merged = arrived.shape
    step = merged // 4
    return pl.pallas_call(
        place_kernel,
        grid=(4,),
        out_shape=jax.ShapeDtypeStruct((capacity, merged), jnp.bfloat16),
        in_specs=[
            pl.BlockSpec((1, slots), lambda i: (0, 0)),
            pl.BlockSpec((slots, step), lambda i: (0, i)),
        ],
        out_specs=pl.BlockSpec((capacity, step), lambda i: (0, i)),
        compiler_params=params(),
    )(offsets, arrived)


def per_device(segment_ids, block_mask, queries, keys, values, tokens, out_weight, owners, offsets):
    rows, features = queries.shape
    hdim = features // HEADS
    nblocks = lax.axis_size("blk")
    block_index = lax.axis_index("blk")
    ngroups = nblocks // HEADS
    groups = None
    if ngroups > 1:
        groups = [[g * HEADS + h for h in range(HEADS)] for g in range(ngroups)]
    exchange = functools.partial(
        lax.all_to_all, axis_name="blk", split_axis=0, concat_axis=0, tiled=True
    )

    x = exchange(split_heads(queries, keys, values), axis_index_groups=groups)

    first = block_index // HEADS * HEADS
    segs = segment_ids.reshape(nblocks, 1, rows)
    base = 0
    halos = ()
    if ngroups > 1:
        base = SPAN
        up = [(i, i + HEADS) for i in range(nblocks - HEADS)]
        down = [(i + HEADS, i) for i in range(nblocks - HEADS)]
        halos = (
            lax.ppermute(x[HEADS - SPAN :, hdim:], "blk", up),
            lax.ppermute(x[:SPAN, hdim:], "blk", down),
        )
        segs = jnp.pad(segs, ((SPAN, SPAN), (0, 0), (0, 0)), constant_values=-1)
        segs = lax.dynamic_slice_in_dim(segs, first, HEADS + 2 * SPAN, 0)
    segs = segs.astype(jnp.float32)

    mask = lax.dynamic_slice_in_dim(block_mask, first, HEADS, 0)
    block = first + jnp.arange(HEADS)[:, None]
    other = jnp.arange(nblocks)[None, :]
    present = (mask > 0) & (jnp.abs(block - other) <= SPAN)
    low = jnp.min(jnp.where(present, other, nblocks), axis=1) - first + base
    count = jnp.sum(present.astype(jnp.int32), axis=1)

    attended = exchange(attention(low, count, x, halos, segs), axis_index_groups=groups)

    mrows = rows // 4
    capacity = 2 * mrows
    pair_rows = max(2, 2 * mrows // nblocks)
    slots = nblocks * pair_rows
    onehot = (owners[:, None] == jnp.arange(nblocks)[None, :]).astype(jnp.int32)
    ranks = jnp.sum((jnp.cumsum(onehot, axis=0) - 1) * onehot, axis=1)
    slot_index = owners * pair_rows + ranks
    match = slot_index[:, None] == jnp.arange(slots)[None, :]
    outgoing_offsets = capacity + jnp.sum(
        jnp.where(match, offsets[:, None] - capacity, 0), axis=0
    )
    arrived_offsets = exchange(outgoing_offsets)
    slot_of_patch = jnp.repeat(slot_index, 4)[None, :]

    outgoing = project(
        slot_of_patch, attended.reshape(features, rows), out_weight, tokens, slots
    )
    arrived = exchange(outgoing)
    return place(arrived_offsets[None, :], arrived, capacity)


def solution(mesh):
    placed = (
        P("rep"),
        P("rep", None),
        P(("rep", "blk"), None),
        P(("rep", "blk"), None),
        P(("rep", "blk"), None),
        P(("rep", "blk"), None),
        P(),
        P(("rep", "blk")),
        P(("rep", "blk")),
    )
    return jax.shard_map(
        per_device, mesh=mesh, in_specs=placed, out_specs=P(("rep", "blk"), None), check_vma=False
    )
```

time: 135 us -> 105 us (0.78)
  waiting for transfers between devices: 29.3 us -> 66.3 us
  starting transfers between devices: 51.2 us -> 18.2 us
  local copies, waits for them, and re-layouts: 20.3 us -> 4.41 us
  other arithmetic: 15.4 us -> 1.3 us
  Pallas kernels: 0 us -> 13.9 us
  matrix products: 11.5 us -> 0 us
  between operations: 4.91 us -> 0.15 us
    ppermute x12 -> x0, starting transfers between devices: 42.5 us -> none  [shifted(): return lax.ppermute(block, axis, route)]
    all_to_all x2 -> x4, waiting for transfers between devices: 28.7 us -> 66.3 us  [the longest x1 29 us: per_device(): arrived = exchange(outgoing)]
    pallas_call x0 -> x4, Pallas kernels: none -> 13.9 us  [the longest x1 8.14 us: attention(): pl.pallas_call(functools.partial(attention_kernel, bool(halos)), out_shap...]
    dot_general x9 -> x0, matrix products: 11.5 us -> none  [the longest x4 6.36 us: attend(): jnp.einsum('hrk,khd->hrd', weights.astype(jnp.bfloat16), value_part, pref...]
    all_to_all x2 -> x4, starting transfers between devices: 8.71 us -> 18.2 us  [the longest x1 7.42 us: per_device(): x = exchange(split_heads(queries, keys, values), axis_index_groups=groups)]
    scatter x3 -> x0, local copies, waits for them, and re-layouts: 7.08 us -> none  [the longest x1 3.48 us: per_device(): buffer.at[arrived_offsets.reshape(-1)]]
    concatenate x9 -> x0, other arithmetic: 5.68 us -> none  [the longest x3 3.36 us: per_device(): jnp.concatenate([fetched[-dist][1], fetched[dist][1]], axis=0)]
    reduce_sum x4 -> x2, other arithmetic: 5.11 us -> 0.28 us  [the longest x1 0.19 us: per_device(): count = jnp.sum(present.astype(jnp.int32), axis=1)]
  transfers between devices with their start and end apart: 14 -> 4, of which waited for: 2 -> 4; matrix products, arithmetic and copies ran while one was open for 30% -> 3% of each run, Pallas kernels for 0% -> 2%
where the time goes in v1:
time: 105 us; the launch traced here: 104 us
  waiting for transfers between devices  66.3 us (63%)
  starting transfers between devices  18.2 us (17%)
  Pallas kernels  13.9 us (13%)
  local copies, waits for them, and re-layouts  4.41 us (4%)
  other arithmetic  1.3 us (1%)
    all_to_all x1, waiting for transfers between devices, per_device(): arrived = exchange(outgoing)  29 us
    all_to_all x1, waiting for transfers between devices, per_device(): x = exchange(split_heads(queries, keys, values), axis_index_groups=groups)  23.9 us
    all_to_all x1, waiting for transfers between devices, per_device(): exchange(attention(low, count, x, halos, segs), axis_index_groups=groups)  9.47 us
    pallas_call x1, Pallas kernels, attention(): pl.pallas_call(functools.partial(attention_kernel, bool(halos)), out_shap...  8.14 us
    all_to_all x1, starting transfers between devices, per_device(): x = exchange(split_heads(queries, keys, values), axis_index_groups=groups)  7.42 us
    all_to_all x1, waiting for transfers between devices, per_device(): arrived_offsets = exchange(outgoing_offsets)  3.97 us
    all_to_all x1, starting transfers between devices, per_device(): arrived_offsets = exchange(outgoing_offsets)  3.64 us
    all_to_all x1, starting transfers between devices, per_device(): arrived = exchange(outgoing)  3.57 us
  transfers between devices with their start and end apart: 4, of which 4 were waited for; matrix products, arithmetic and copies ran while one was open for 3% of the time, Pallas kernels for 2%

profile of v1, /device:TPU:0, one launch (start us, length us, event | category | flops | bytes accessed | tf_op | source)
XLA Modules:
  0.0 104.3 jit_solution(18210812498290454018)
XLA Ops:
  0.0 1.0 copy-done.2
  1.0 1.0 copy-done.3
  1.9 1.0 copy-done.4
  2.9 1.3 %shard_map.91 = bf16[8,240,256]{2,1,0:T(8,128)(2,1)} custom-call(bf16[256,640]{1,0:T(8,128)(2,1)S(1)} %copy-done.2, bf16[256,640]{1,0:T(8,128)(2,1)S(1)} %copy-done.3, bf16[256,640]{1,0:T(8,128)(2,1)S(1)} %copy-done.4), custom_call_target="tpu_custom_call" | custom-call | tf_op jit(solution)/shard_map/pallas_call | solution.py:42
  4.2 7.4 %all-to-all-start.1 = ((bf16[8,240,256]{2,1,0:T(8,128)(2,1)}), bf16[8,240,256]{2,1,0:T(8,128)(2,1)S(1)}, u32[]{:S(2)}, u32[]{:S(2)}) async-start(bf16[8,240,256]{2,1,0:T(8,128)(2,1)} %shard_map.91), calls=%async_computation.1 | async-start | bytes 1966080 | tf_op jit(solution)/shard_map/all_to_all | solution.py:199
  11.7 0.1 reduce_window_sum.11
  11.9 0.2 convert_reduce_fusion
  12.1 23.9 %all-to-all-done.1.x_ref = bf16[8,240,256]{2,1,0:T(8,128)(2,1)S(1)} async-done(((bf16[8,240,256]{2,1,0:T(8,128)(2,1)}), bf16[8,240,256]{2,1,0:T(8,128)(2,1)S(1)}, u32[]{:S(2)}, u32[]{:S(2)}) %all-to-all-start.1) | async-done | bytes 983072 | tf_op jit(solution)/shard_map/all_to_all | solution.py:199
  36.0 8.1 %shard_map.92 = bf16[8,80,256]{2,1,0:T(8,128)(2,1)} custom-call(s32[8]{0:T(128)S(1)} %broadcast_subtract_fusion.low_ref, s32[8]{0:T(128)S(1)} %get-tuple-element.5.count_ref, bf16[8,240,256]{2,1,0:T(8,128)(2,1)S(1)} %all-to-all-done.1.x_ref, f32[8,1,256]{2,1,0:T(1,128)S(1)} %bitcast.8), custom_call_target="tpu_custom_call" | custom-call | tf_op jit(solution)/shard_map/pallas_call | solution.py:119
  44.1 3.6 %all-to-all-start.2 = ((bf16[8,80,256]{2,1,0:T(8,128)(2,1)}), bf16[8,80,256]{2,1,0:T(8,128)(2,1)S(1)}, u32[]{:S(2)}, u32[]{:S(2)}) async-start(bf16[8,80,256]{2,1,0:T(8,128)(2,1)} %shard_map.92), calls=%async_computation.2 | async-start | bytes 655360 | tf_op jit(solution)/shard_map/all_to_all | solution.py:224
  47.7 0.2 select_reduce_fusion.1
  47.9 0.1 select_reduce_fusion
  48.0 0.7 add.38
  48.7 9.5 %all-to-all-done.2 = bf16[8,80,256]{2,1,0:T(8,128)(2,1)S(1)} async-done(((bf16[8,80,256]{2,1,0:T(8,128)(2,1)}), bf16[8,80,256]{2,1,0:T(8,128)(2,1)S(1)}, u32[]{:S(2)}, u32[]{:S(2)}) %all-to-all-start.2) | async-done | bytes 327712 | tf_op jit(solution)/shard_map/all_to_all | solution.py:224
  58.2 3.6 %all-to-all-start = ((s32[8,16,1]{1,2,0:T(1,128)}), s32[8,16,1]{1,2,0:T(1,128)S(1)}, u32[]{:S(2)}, u32[]{:S(2)}) async-start(s32[8,16,1]{1,2,0:T(1,128)} %bitcast), calls=%async_computation | async-start | bytes 8192 | tf_op jit(solution)/shard_map/all_to_all | solution.py:237
  61.9 0.1 broadcast_in_dim_reshape.3.slot_ref
  62.0 2.3 %shard_map.93 = bf16[128,5120]{1,0:T(8,128)(2,1)} custom-call(s32[1,256]{1,0:T(1,128)S(1)} %broadcast_in_dim_reshape.3.slot_ref, bf16[640,256]{1,0:T(8,128)(2,1)S(1)} %bitcast.7, bf16[640,1280]{1,0:T(8,128)(2,1)S(1)} %copy-done, bf16[256,1280]{1,0:T(8,128)(2,1)S(1)} %copy-done.1), custom_call_target="tpu_custom_call" | custom-call | tf_op jit(solution)/shard_map/pallas_call | solution.py:151
  64.3 4.0 %all-to-all-done = s32[8,16,1]{1,2,0:T(1,128)S(1)} async-done(((s32[8,16,1]{1,2,0:T(1,128)}), s32[8,16,1]{1,2,0:T(1,128)S(1)}, u32[]{:S(2)}, u32[]{:S(2)}) %all-to-all-start) | async-done | bytes 544 | tf_op jit(solution)/shard_map/all_to_all | solution.py:237
  68.2 3.6 %all-to-all-start.3 = ((bf16[8,16,5120]{2,1,0:T(8,128)(2,1)}), bf16[8,16,5120]{2,1,0:T(8,128)(2,1)S(1)}, u32[]{:S(2)}, u32[]{:S(2)}) async-start(bf16[8,16,5120]{2,1,0:T(8,128)(2,1)} %bitcast.3), calls=%async_computation.3 | async-start | bytes 2621440 | tf_op jit(solution)/shard_map/all_to_all | solution.py:243
  71.8 0.5 broadcast.37
  72.4 0.6 reduce.3
  73.0 0.1 broadcast_in_dim.37.offsets_ref
  73.1 29.0 %all-to-all-done.3 = bf16[8,16,5120]{2,1,0:T(8,128)(2,1)S(1)} async-done(((bf16[8,16,5120]{2,1,0:T(8,128)(2,1)}), bf16[8,16,5120]{2,1,0:T(8,128)(2,1)S(1)}, u32[]{:S(2)}, u32[]{:S(2)}) %all-to-all-start.3) | async-done | bytes 1310752 | tf_op jit(solution)/shard_map/all_to_all | solution.py:243
  102.1 2.3 %shard_map.94 = bf16[128,5120]{1,0:T(8,128)(2,1)} custom-call(s32[1,128]{1,0:T(1,128)S(1)} %broadcast_in_dim.37.offsets_ref, bf16[128,5120]{1,0:T(8,128)(2,1)S(1)} %bitcast.6), custom_call_target="tpu_custom_call" | custom-call | tf_op jit(solution)/shard_map/pallas_call | solution.py:173
  (22 shorter events, 0.2 us)
Async XLA Ops:
  0.0 1.0 copy-start.2
  1.0 1.0 copy-start.3
  1.9 1.0 copy-start.4
  4.2 7.5 %copy-start.5 = (s32[2048]{0:T(1024)S(1)}, s32[2048]{0:T(1024)}, u32[]{:S(2)}) copy-start(s32[2048]{0:T(1024)} %param.9) | copy-start | bytes 24580
  4.2 7.5 %copy-start.6 = (s32[64]{0:T(128)S(1)}, s32[64]{0:T(128)}, u32[]{:S(2)}) copy-start(s32[64]{0:T(128)} %param.16) | copy-start | bytes 772
  4.2 7.7 %copy-start.7 = (s32[8,8]{1,0:T(8,128)S(1)}, s32[8,8]{1,0:T(8,128)}, u32[]{:S(2)}) copy-start(s32[8,8]{1,0:T(8,128)} %param.10) | copy-start | bytes 772
  4.2 57.8 %copy-start.1 = (bf16[256,1280]{1,0:T(8,128)(2,1)S(1)}, bf16[256,1280]{1,0:T(8,128)(2,1)}, u32[]{:S(2)}) copy-start(bf16[256,1280]{1,0:T(8,128)(2,1)} %tokens_ref.1) | copy-start | bytes 1966084
  4.2 31.8 %all-to-all-start.1 = ((bf16[8,240,256]{2,1,0:T(8,128)(2,1)}), bf16[8,240,256]{2,1,0:T(8,128)(2,1)S(1)}, u32[]{:S(2)}, u32[]{:S(2)}) async-start(bf16[8,240,256]{2,1,0:T(8,128)(2,1)} %shard_map.91), calls=%async_computation.1 | async-start | bytes 1966080 | tf_op jit(solution)/shard_map/all_to_all | solution.py:199
  11.6 36.3 %copy-start.8 = (s32[64]{0:T(128)S(1)}, s32[64]{0:T(128)}, u32[]{:S(2)}) copy-start(s32[64]{0:T(128)} %param.17) | copy-start | bytes 772
  11.6 50.4 %copy-start = (bf16[640,1280]{1,0:T(8,128)(2,1)S(1)}, bf16[640,1280]{1,0:T(8,128)(2,1)}, u32[]{:S(2)}) copy-start(bf16[640,1280]{1,0:T(8,128)(2,1)} %weight_ref.1) | copy-start | bytes 4915204
  44.1 14.0 %all-to-all-start.2 = ((bf16[8,80,256]{2,1,0:T(8,128)(2,1)}), bf16[8,80,256]{2,1,0:T(8,128)(2,1)S(1)}, u32[]{:S(2)}, u32[]{:S(2)}) async-start(bf16[8,80,256]{2,1,0:T(8,128)(2,1)} %shard_map.92), calls=%async_computation.2 | async-start | bytes 655360 | tf_op jit(solution)/shard_map/all_to_all | solution.py:224
  58.2 10.1 %all-to-all-start = ((s32[8,16,1]{1,2,0:T(1,128)}), s32[8,16,1]{1,2,0:T(1,128)S(1)}, u32[]{:S(2)}, u32[]{:S(2)}) async-start(s32[8,16,1]{1,2,0:T(1,128)} %bitcast), calls=%async_computation | async-start | bytes 8192 | tf_op jit(solution)/shard_map/all_to_all | solution.py:237
  68.2 33.8 %all-to-all-start.3 = ((bf16[8,16,5120]{2,1,0:T(8,128)(2,1)}), bf16[8,16,5120]{2,1,0:T(8,128)(2,1)S(1)}, u32[]{:S(2)}, u32[]{:S(2)}) async-start(bf16[8,16,5120]{2,1,0:T(8,128)(2,1)} %bitcast.3), calls=%async_computation.3 | async-start | bytes 2621440 | tf_op jit(solution)/shard_map/all_to_all | solution.py:243

commit v2 on v1

v2 whole, which is shorter than its diff:
```python
import functools

import jax
import jax.numpy as jnp
from jax import lax
from jax.experimental import pallas as pl
from jax.experimental.pallas import tpu as pltpu
from jax.sharding import PartitionSpec as P

HEADS = 8
SPAN = 3
NEG = -1e30
LOG2E = 1.4426950408889634
VMEM_LIMIT = 40 * 1024 * 1024


def params():
    return pltpu.CompilerParams(vmem_limit_bytes=VMEM_LIMIT)


def vmem():
    return pl.BlockSpec(memory_space=pltpu.VMEM)


def smem():
    return pl.BlockSpec(memory_space=pltpu.SMEM)


def split_heads_kernel(q_hbm, k_hbm, v_hbm, out_ref, held, sems):
    hdim = q_hbm.shape[1] // HEADS
    copies = [
        pltpu.make_async_copy(ref, held.at[part], sems.at[part])
        for part, ref in enumerate((q_hbm, k_hbm, v_hbm))
    ]
    for copy in copies:
        copy.start()
    for part, copy in enumerate(copies):
        copy.wait()
        turned = held[part].T
        for head in range(HEADS):
            out_ref[head, part * hdim : (part + 1) * hdim, :] = turned[
                head * hdim : (head + 1) * hdim, :
            ]


def split_heads(queries, keys, values):
    rows, features = queries.shape
    hdim = features // HEADS
    return pl.pallas_call(
        split_heads_kernel,
        out_shape=jax.ShapeDtypeStruct((HEADS, 3 * hdim, rows), queries.dtype),
        in_specs=[pl.BlockSpec(memory_space=pl.ANY)] * 3,
        out_specs=vmem(),
        scratch_shapes=[
            pltpu.VMEM((3, rows, features), queries.dtype),
            pltpu.SemaphoreType.DMA((3,)),
        ],
        compiler_params=pltpu.CompilerParams(vmem_limit_bytes=60 * 1024 * 1024),
    )(queries, keys, values)


def attention_kernel(halo, pair_rows, low_ref, count_ref, x_ref, slot_ref, *refs):
    if halo:
        below_ref, above_ref, seg_ref, out_ref, key_s, value_s, seg_s, picked_s = refs
    else:
        seg_ref, out_ref, key_s, seg_s, picked_s = refs
    blocks, triple, rows = x_ref.shape
    hdim = triple // 3
    slots = out_ref.shape[2]
    base = SPAN if halo else 0
    factor = LOG2E / (hdim**0.5)
    extended = blocks + 2 * base

    for b in range(extended):
        if b < base:
            key_s[b] = below_ref[b, :hdim, :].T
            value_s[b] = below_ref[b, hdim:, :]
        elif b >= base + blocks:
            key_s[b] = above_ref[b - base - blocks, :hdim, :].T
            value_s[b] = above_ref[b - base - blocks, hdim:, :]
        else:
            key_s[b] = x_ref[b - base, hdim : 2 * hdim, :].T
            if halo:
                value_s[b] = x_ref[b - base, 2 * hdim :, :]
        seg_s[b] = jnp.broadcast_to(seg_ref[b], (128, rows)).T

    def value_block(b):
        return value_s[b] if halo else x_ref[b, 2 * hdim :, :]

    slot = lax.broadcasted_iota(jnp.int32, (slots, rows), 0)
    quarter = lax.broadcasted_iota(jnp.int32, (slots, rows), 1) % 4

    def one_block(i, carry):
        low = low_ref[i]
        count = count_ref[i]
        query = x_ref[i, :hdim, :]
        query_seg = seg_ref[i + base]
        mine = slot_ref[i] == slot

        for size in range(1, 2 * SPAN + 2):

            @pl.when(count == size)
            def _():
                key = key_s[pl.ds(low, size)].reshape(size * rows, hdim)
                scores = jnp.dot(key, query, preferred_element_type=jnp.float32)
                key_seg = seg_s[pl.ds(low, size)].reshape(size * rows, 128)
                key_seg = jnp.concatenate([key_seg] * (rows // 128), axis=1)
                scores = jnp.where(key_seg == query_seg, scores, NEG)
                peak = jnp.max(scores, axis=0, keepdims=True)
                weights = jnp.exp2((scores - peak) * factor)
                total = jnp.sum(weights, axis=0, keepdims=True)
                weights = weights.astype(jnp.bfloat16)
                mixed = jnp.zeros((hdim, rows), jnp.float32)
                for b in range(size):
                    mixed += jnp.dot(
                        value_block(low + b),
                        weights[b * rows : (b + 1) * rows],
                        preferred_element_type=jnp.float32,
                    )
                attended = (mixed / total).astype(jnp.bfloat16)
                for j in range(4):
                    pick = jnp.where(mine & (quarter == j), 1.0, 0.0).astype(jnp.bfloat16)
                    picked_s[i, j * hdim : (j + 1) * hdim, :] = lax.dot_general(
                        attended,
                        pick,
                        (((1,), (1,)), ((), ())),
                        preferred_element_type=jnp.float32,
                    )

        return carry

    lax.fori_loop(0, blocks, one_block, 0)

    group = lax.broadcasted_iota(jnp.int32, (4 * hdim, slots), 1) // pair_rows % blocks
    for first in range(blocks):
        chosen = picked_s[0]
        for b in range(1, blocks):
            chosen = jnp.where(group == (first + b) % blocks, picked_s[b], chosen)
        out_ref[first] = chosen.astype(out_ref.dtype)


def attention(low, count, x, slot, halos, segs, slots, pair_rows):
    blocks, triple, rows = x.shape
    hdim = triple // 3
    extended = segs.shape[0]
    scratch = [pltpu.VMEM((extended, rows, hdim), jnp.bfloat16)]
    if halos:
        scratch.append(pltpu.VMEM((extended, hdim, rows), jnp.bfloat16))
    scratch.append(pltpu.VMEM((extended, rows, 128), jnp.float32))
    scratch.append(pltpu.VMEM((blocks, 4 * hdim, slots), jnp.float32))
    return pl.pallas_call(
        functools.partial(attention_kernel, bool(halos), pair_rows),
        out_shape=jax.ShapeDtypeStruct((blocks, 4 * hdim, slots), jnp.bfloat16),
        in_specs=[smem(), smem()] + [vmem()] * (3 + len(halos)),
        out_specs=vmem(),
        scratch_shapes=scratch,
        compiler_params=params(),
    )(low, count, x, slot, *halos, segs)


def arrange_kernel(slot_ref, tokens_ref, out_ref):
    slots = out_ref.shape[0]
    rows, width = tokens_ref.shape
    tokens = tokens_ref[...]
    slot = lax.broadcasted_iota(jnp.int32, (slots, rows), 0)
    quarter = lax.broadcasted_iota(jnp.int32, (slots, rows), 1) % 4
    mine = slot_ref[...] == slot
    for j in range(4):
        pick = jnp.where(mine & (quarter == j), 1.0, 0.0).astype(jnp.bfloat16)
        out_ref[:, j * width : (j + 1) * width] = jnp.dot(
            pick, tokens, preferred_element_type=jnp.float32
        ).astype(jnp.bfloat16)


def arrange(slot_of_patch, tokens, slots):
    rows, width = tokens.shape
    return pl.pallas_call(
        arrange_kernel,
        out_shape=jax.ShapeDtypeStruct((slots, 4 * width), jnp.bfloat16),
        in_specs=[vmem()] * 2,
        out_specs=vmem(),
        compiler_params=params(),
    )(slot_of_patch, tokens)


def finish_kernel(token_offsets_ref, offsets_ref, weight_ref, tokens_ref, attended_ref, out_hbm, held, sems):
    capacity, merged = out_hbm.shape
    groups, lanes = offsets_ref.shape
    width = merged // 4
    hdim = attended_ref.shape[1] // 4

    def pick(offsets):
        row = lax.broadcasted_iota(jnp.int32, (capacity, offsets.shape[1]), 0)
        return jnp.where(offsets == row, 1.0, 0.0).astype(jnp.bfloat16)

    token_pick = pick(token_offsets_ref[...])
    picks = [pick(offsets_ref[g : g + 1, :]) for g in range(groups)]
    copies = []
    for j in range(4):
        attended = jnp.zeros((capacity, HEADS * hdim), jnp.float32)
        for g in range(groups):
            turned = jnp.concatenate(
                [
                    attended_ref[g * HEADS + h, j * hdim : (j + 1) * hdim, :]
                    for h in range(HEADS)
                ],
                axis=0,
            )
            attended += lax.dot_general(
                picks[g], turned, (((1,), (1,)), ((), ())), preferred_element_type=jnp.float32
            )
        columns = slice(j * width, (j + 1) * width)
        hidden = jnp.dot(
            token_pick, tokens_ref[:, columns], preferred_element_type=jnp.float32
        ) + jnp.dot(
            attended.astype(jnp.bfloat16), weight_ref[...], preferred_element_type=jnp.float32
        )
        held[j] = hidden.astype(jnp.bfloat16)
        copy = pltpu.make_async_copy(held.at[j], out_hbm.at[:, columns], sems.at[j])
        copy.start()
        copies.append(copy)
    for copy in copies:
        copy.wait()


def finish(token_offsets, offsets, out_weight, tokens, attended, capacity):
    merged = tokens.shape[1]
    return pl.pallas_call(
        finish_kernel,
        out_shape=jax.ShapeDtypeStruct((capacity, merged), jnp.bfloat16),
        in_specs=[vmem()] * 5,
        out_specs=pl.BlockSpec(memory_space=pl.ANY),
        scratch_shapes=[
            pltpu.VMEM((4, capacity, merged // 4), jnp.bfloat16),
            pltpu.SemaphoreType.DMA((4,)),
        ],
        compiler_params=params(),
    )(token_offsets, offsets, out_weight, tokens, attended)


def per_device(segment_ids, block_mask, queries, keys, values, tokens, out_weight, owners, offsets):
    rows, features = queries.shape
    hdim = features // HEADS
    nblocks = lax.axis_size("blk")
    block_index = lax.axis_index("blk")
    ngroups = nblocks // HEADS
    groups = None
    if ngroups > 1:
        groups = [[g * HEADS + h for h in range(HEADS)] for g in range(ngroups)]
    exchange = functools.partial(
        lax.all_to_all, axis_name="blk", split_axis=0, concat_axis=0, tiled=True
    )

    x = exchange(split_heads(queries, keys, values), axis_index_groups=groups)

    mrows = rows // 4
    capacity = 2 * mrows
    pair_rows = max(2, 2 * mrows // nblocks)
    slots = nblocks * pair_rows
    onehot = (owners[:, None] == jnp.arange(nblocks)[None, :]).astype(jnp.int32)
    ranks = jnp.sum((jnp.cumsum(onehot, axis=0) - 1) * onehot, axis=1)
    slot_index = owners * pair_rows + ranks
    match = slot_index[:, None] == jnp.arange(slots)[None, :]
    outgoing_offsets = capacity + jnp.sum(
        jnp.where(match, offsets[:, None] - capacity, 0), axis=0
    )
    outgoing_offsets = outgoing_offsets.reshape(nblocks, pair_rows)
    outgoing_slots = jnp.broadcast_to(slot_index[None, :], (HEADS, mrows))
    if ngroups == 1:
        both = exchange(jnp.concatenate([outgoing_slots, outgoing_offsets], axis=1))
        slots_of, arrived_offsets = both[:, :mrows], both[:, mrows:]
    else:
        slots_of = exchange(outgoing_slots, axis_index_groups=groups)
        arrived_offsets = exchange(outgoing_offsets)

    outgoing = arrange(jnp.repeat(slot_index, 4)[None, :], tokens, slots)
    arrived_tokens = exchange(outgoing)

    first = block_index // HEADS * HEADS
    segs = segment_ids.reshape(nblocks, 1, rows)
    base = 0
    halos = ()
    if ngroups > 1:
        base = SPAN
        up = [(i, i + HEADS) for i in range(nblocks - HEADS)]
        down = [(i + HEADS, i) for i in range(nblocks - HEADS)]
        halos = (
            lax.ppermute(x[HEADS - SPAN :, hdim:], "blk", up),
            lax.ppermute(x[:SPAN, hdim:], "blk", down),
        )
        segs = jnp.pad(segs, ((SPAN, SPAN), (0, 0), (0, 0)), constant_values=-1)
        segs = lax.dynamic_slice_in_dim(segs, first, HEADS + 2 * SPAN, 0)
    segs = segs.astype(jnp.float32)

    mask = lax.dynamic_slice_in_dim(block_mask, first, HEADS, 0)
    block = first + jnp.arange(HEADS)[:, None]
    other = jnp.arange(nblocks)[None, :]
    present = (mask > 0) & (jnp.abs(block - other) <= SPAN)
    low = jnp.min(jnp.where(present, other, nblocks), axis=1) - first + base
    count = jnp.sum(present.astype(jnp.int32), axis=1)

    turn = jnp.arange(HEADS)[:, None] * pair_rows
    slots_of = jnp.repeat((slots_of + turn) % slots, 4, axis=1)[:, None, :]
    sent = attention(low, count, x, slots_of, halos, segs, slots, pair_rows)
    if ngroups > 1:
        sent = jnp.stack([jnp.roll(sent[o], -o * pair_rows, axis=1) for o in range(HEADS)])
        sent = sent.reshape(HEADS, 4 * hdim, ngroups, HEADS * pair_rows)
        sent = jnp.transpose(sent, (2, 0, 1, 3)).reshape(nblocks, 4 * hdim, HEADS * pair_rows)
        lane_offsets = arrived_offsets
    else:
        lane_offsets = jnp.roll(arrived_offsets, block_index, axis=0)
    arrived = exchange(sent)
    return finish(
        arrived_offsets.reshape(1, slots),
        lane_offsets.reshape(ngroups, HEADS * pair_rows),
        out_weight,
        arrived_tokens,
        arrived,
        capacity,
    )


def solution(mesh):
    placed = (
        P("rep"),
        P("rep", None),
        P(("rep", "blk"), None),
        P(("rep", "blk"), None),
        P(("rep", "blk"), None),
        P(("rep", "blk"), None),
        P(),
        P(("rep", "blk")),
        P(("rep", "blk")),
    )
    return jax.shard_map(
        per_device, mesh=mesh, in_specs=placed, out_specs=P(("rep", "blk"), None), check_vma=False
    )
```

time: 105 us -> 105 us (level)
  Pallas kernels: 13.9 us -> 17.5 us
  waiting for transfers between devices: 66.3 us -> 62.7 us
  local copies, waits for them, and re-layouts: 4.41 us -> 2.11 us
  other arithmetic: 1.3 us -> 3.42 us
    all_to_all x1, starting transfers between devices: 7.42 us -> 3.56 us  [per_device(): x = exchange(split_heads(queries, keys, values), axis_index_groups=groups)]
    all_to_all x3, starting transfers between devices: 10.8 us -> 14.6 us  [the longest x1 7.28 us: per_device(): both = exchange(jnp.concatenate([outgoing_slots, outgoing_offsets], axis=1))]
    pallas_call x3, Pallas kernels: 12.7 us -> 15.1 us  [the longest x1 10.9 us: attention(): pl.pallas_call(functools.partial(attention_kernel, bool(halos), pair_rows...]
    all_to_all x1, waiting for transfers between devices: 23.9 us -> 21.5 us  [per_device(): x = exchange(split_heads(queries, keys, values), axis_index_groups=groups)]
    unnamed x18 -> x8, local copies, waits for them, and re-layouts: 2.94 us -> 1.44 us
    all_to_all x3, waiting for transfers between devices: 42.4 us -> 41.2 us  [the longest x1 20 us: per_device(): arrived_tokens = exchange(outgoing)]
    pallas_call x1, Pallas kernels: 1.25 us -> 2.37 us  [split_heads(): pl.pallas_call(split_heads_kernel, out_shape=jax.ShapeDtypeStruct((HEADS,...]
  transfers between devices with their start and end apart: 4 -> 4, of which waited for: 4 -> 4; matrix products, arithmetic and copies ran while one was open for 3% -> 1% of each run, Pallas kernels for 2% -> 14%
where the time goes in v2:
time: 105 us; the launch traced here: 104 us
  waiting for transfers between devices  62.7 us (60%)
  starting transfers between devices  18.2 us (17%)
  Pallas kernels  17.5 us (17%)
  other arithmetic  3.42 us (3%)
  local copies, waits for them, and re-layouts  2.11 us (2%)
    all_to_all x1, waiting for transfers between devices, per_device(): x = exchange(split_heads(queries, keys, values), axis_index_groups=groups)  21.5 us
    all_to_all x1, waiting for transfers between devices, per_device(): arrived_tokens = exchange(outgoing)  20 us
    all_to_all x1, waiting for transfers between devices, per_device(): arrived = exchange(sent)  17.2 us
    pallas_call x1, Pallas kernels, attention(): pl.pallas_call(functools.partial(attention_kernel, bool(halos), pair_rows...  10.9 us
    all_to_all x1, starting transfers between devices, per_device(): both = exchange(jnp.concatenate([outgoing_slots, outgoing_offsets], axis=1))  7.28 us
    all_to_all x1, waiting for transfers between devices, per_device(): both = exchange(jnp.concatenate([outgoing_slots, outgoing_offsets], axis=1))  4 us
    all_to_all x1, starting transfers between devices, per_device(): arrived_tokens = exchange(outgoing)  3.7 us
    all_to_all x1, starting transfers between devices, per_device(): arrived = exchange(sent)  3.64 us
  transfers between devices with their start and end apart: 4, of which 4 were waited for; matrix products, arithmetic and copies ran while one was open for 1% of the time, Pallas kernels for 14%

profile of v2, /device:TPU:0, one launch (start us, length us, event | category | flops | bytes accessed | tf_op | source)
XLA Modules:
  0.0 104.1 jit_solution(13785519341661135125)
XLA Ops:
  0.0 0.7 fusion
  0.7 0.1 reduce_window_sum.11
  0.8 0.8 select_reduce_fusion.1
  1.7 0.7 multiply_add_fusion
  2.4 0.1 select_reduce_fusion
  2.5 0.7 pad_add_fusion
  3.2 7.3 %all-to-all-start = ((s32[8,1,80]{2,1,0:T(1,128)}), s32[8,1,80]{2,1,0:T(1,128)S(1)}, u32[]{:S(2)}, u32[]{:S(2)}) async-start(s32[8,1,80]{2,1,0:T(1,128)} %bitcast), calls=%async_computation | async-start | bytes 8192 | tf_op jit(solution)/shard_map/all_to_all | solution.py:270
  10.5 2.4 %shard_map.92 = bf16[8,240,256]{2,1,0:T(8,128)(2,1)} custom-call(bf16[256,640]{1,0:T(8,128)(2,1)} %q_hbm.1, bf16[256,640]{1,0:T(8,128)(2,1)} %k_hbm.1, bf16[256,640]{1,0:T(8,128)(2,1)} %v_hbm.1), custom_call_target="tpu_custom_call" | custom-call | tf_op jit(solution)/shard_map/pallas_call | solution.py:49
  12.9 4.0 %all-to-all-done = s32[8,1,80]{2,1,0:T(1,128)S(1)} async-done(((s32[8,1,80]{2,1,0:T(1,128)}), s32[8,1,80]{2,1,0:T(1,128)S(1)}, u32[]{:S(2)}, u32[]{:S(2)}) %all-to-all-start) | async-done | bytes 2592 | tf_op jit(solution)/shard_map/all_to_all | solution.py:270
  16.9 3.6 %all-to-all-start.2 = ((bf16[8,240,256]{2,1,0:T(8,128)(2,1)}), bf16[8,240,256]{2,1,0:T(8,128)(2,1)S(1)}, u32[]{:S(2)}, u32[]{:S(2)}) async-start(bf16[8,240,256]{2,1,0:T(8,128)(2,1)} %shard_map.92), calls=%async_computation.2 | async-start | bytes 1966080 | tf_op jit(solution)/shard_map/all_to_all | solution.py:254
  20.5 0.1 broadcast_in_dim_reshape.6.slot_ref
  20.6 1.6 %shard_map.91 = bf16[128,5120]{1,0:T(8,128)(2,1)} custom-call(s32[1,256]{1,0:T(1,128)S(1)} %broadcast_in_dim_reshape.6.slot_ref, bf16[256,1280]{1,0:T(8,128)(2,1)S(1)} %copy-done.1), custom_call_target="tpu_custom_call" | custom-call | tf_op jit(solution)/shard_map/pallas_call | solution.py:177
  22.2 21.5 %all-to-all-done.2.x_ref = bf16[8,240,256]{2,1,0:T(8,128)(2,1)S(1)} async-done(((bf16[8,240,256]{2,1,0:T(8,128)(2,1)}), bf16[8,240,256]{2,1,0:T(8,128)(2,1)S(1)}, u32[]{:S(2)}, u32[]{:S(2)}) %all-to-all-start.2) | async-done | bytes 983072 | tf_op jit(solution)/shard_map/all_to_all | solution.py:254
  43.8 3.7 %all-to-all-start.1 = ((bf16[8,16,5120]{2,1,0:T(8,128)(2,1)}), bf16[8,16,5120]{2,1,0:T(8,128)(2,1)S(1)}, u32[]{:S(2)}, u32[]{:S(2)}) async-start(bf16[8,16,5120]{2,1,0:T(8,128)(2,1)} %bitcast.2), calls=%async_computation.1 | async-start | bytes 2621440 | tf_op jit(solution)/shard_map/all_to_all | solution.py:277
  47.6 0.2 convert_reduce_fusion
  47.8 0.1 copy.14
  48.0 10.9 %shard_map.93 = bf16[8,320,128]{2,1,0:T(8,128)(2,1)} custom-call(s32[8]{0:T(128)S(1)} %broadcast_subtract_fusion.low_ref, s32[8]{0:T(128)S(1)} %get-tuple-element.5.count_ref, bf16[8,240,256]{2,1,0:T(8,128)(2,1)S(1)} %all-to-all-done.2.x_ref, s32[8,1,256]{2,1,0:T(1,128)S(1)} %copy.15.slot_ref, f32[8,1,256]{2,1,0:T(1,128)S(1)} %bitcast.7), custom_call_target="tpu_custom_call" | custom-call | tf_op jit(solution)/shard_map/pallas_call | solution.py:151
  58.9 20.0 %all-to-all-done.1 = bf16[8,16,5120]{2,1,0:T(8,128)(2,1)S(1)} async-done(((bf16[8,16,5120]{2,1,0:T(8,128)(2,1)}), bf16[8,16,5120]{2,1,0:T(8,128)(2,1)S(1)}, u32[]{:S(2)}, u32[]{:S(2)}) %all-to-all-start.1) | async-done | bytes 1310752 | tf_op jit(solution)/shard_map/all_to_all | solution.py:277
  78.9 3.6 %all-to-all-start.3 = ((bf16[8,320,128]{2,1,0:T(8,128)(2,1)}), bf16[8,320,128]{2,1,0:T(8,128)(2,1)S(1)}, u32[]{:S(2)}, u32[]{:S(2)}) async-start(bf16[8,320,128]{2,1,0:T(8,128)(2,1)} %shard_map.93), calls=%async_computation.3 | async-start | bytes 1310720 | tf_op jit(solution)/shard_map/all_to_all | solution.py:312
  82.6 0.1 reshape.43.token_offsets_ref
  82.7 0.1 reshape.44.offsets_ref
  82.8 17.2 %all-to-all-done.3.attended_ref = bf16[8,320,128]{2,1,0:T(8,128)(2,1)S(1)} async-done(((bf16[8,320,128]{2,1,0:T(8,128)(2,1)}), bf16[8,320,128]{2,1,0:T(8,128)(2,1)S(1)}, u32[]{:S(2)}, u32[]{:S(2)}) %all-to-all-start.3) | async-done | bytes 655392 | tf_op jit(solution)/shard_map/all_to_all | solution.py:312
  100.0 1.4 %copy-done = bf16[640,1280]{1,0:T(8,128)(2,1)S(1)} copy-done((bf16[640,1280]{1,0:T(8,128)(2,1)S(1)}, bf16[640,1280]{1,0:T(8,128)(2,1)}, u32[]{:S(2)}) %copy-start) | copy-done | bytes 1638424
  101.4 2.6 %shard_map.94 = bf16[128,5120]{1,0:T(8,128)(2,1)} custom-call(s32[1,128]{1,0:T(1,128)S(1)} %reshape.43.token_offsets_ref, s32[1,128]{1,0:T(1,128)S(1)} %reshape.44.offsets_ref, bf16[640,1280]{1,0:T(8,128)(2,1)S(1)} %copy-done, bf16[128,5120]{1,0:T(8,128)(2,1)S(1)} %bitcast.6, bf16[8,320,128]{2,1,0:T(8,128)(2,1)S(1)} %all-to-all-done.3.attended_ref), custom_call_target="tpu_custom_call" | custom-call | tf_op jit(solution)/shard_map/pallas_call | solution.py:228
  (20 shorter events, 0.4 us)
Async XLA Ops:
  3.2 13.7 %all-to-all-start = ((s32[8,1,80]{2,1,0:T(1,128)}), s32[8,1,80]{2,1,0:T(1,128)S(1)}, u32[]{:S(2)}, u32[]{:S(2)}) async-start(s32[8,1,80]{2,1,0:T(1,128)} %bitcast), calls=%async_computation | async-start | bytes 8192 | tf_op jit(solution)/shard_map/all_to_all | solution.py:270
  12.9 7.8 %copy-start.1 = (bf16[256,1280]{1,0:T(8,128)(2,1)S(1)}, bf16[256,1280]{1,0:T(8,128)(2,1)}, u32[]{:S(2)}) copy-start(bf16[256,1280]{1,0:T(8,128)(2,1)} %tokens_ref.1) | copy-start | bytes 1966084
  16.9 26.9 %all-to-all-start.2 = ((bf16[8,240,256]{2,1,0:T(8,128)(2,1)}), bf16[8,240,256]{2,1,0:T(8,128)(2,1)S(1)}, u32[]{:S(2)}, u32[]{:S(2)}) async-start(bf16[8,240,256]{2,1,0:T(8,128)(2,1)} %shard_map.92), calls=%async_computation.2 | async-start | bytes 1966080 | tf_op jit(solution)/shard_map/all_to_all | solution.py:254
  43.8 3.7 %copy-start.2 = (s32[2048]{0:T(1024)S(1)}, s32[2048]{0:T(1024)}, u32[]{:S(2)}) copy-start(s32[2048]{0:T(1024)} %param.9) | copy-start | bytes 24580
  43.8 3.8 %copy-start.3 = (s32[8,8]{1,0:T(8,128)S(1)}, s32[8,8]{1,0:T(8,128)}, u32[]{:S(2)}) copy-start(s32[8,8]{1,0:T(8,128)} %param.10) | copy-start | bytes 772
  43.8 35.1 %all-to-all-start.1 = ((bf16[8,16,5120]{2,1,0:T(8,128)(2,1)}), bf16[8,16,5120]{2,1,0:T(8,128)(2,1)S(1)}, u32[]{:S(2)}, u32[]{:S(2)}) async-start(bf16[8,16,5120]{2,1,0:T(8,128)(2,1)} %bitcast.2), calls=%async_computation.1 | async-start | bytes 2621440 | tf_op jit(solution)/shard_map/all_to_all | solution.py:277
  78.9 21.1 %all-to-all-start.3 = ((bf16[8,320,128]{2,1,0:T(8,128)(2,1)}), bf16[8,320,128]{2,1,0:T(8,128)(2,1)S(1)}, u32[]{:S(2)}, u32[]{:S(2)}) async-start(bf16[8,320,128]{2,1,0:T(8,128)(2,1)} %shard_map.93), calls=%async_computation.3 | async-start | bytes 1310720 | tf_op jit(solution)/shard_map/all_to_all | solution.py:312
  100.0 1.4 %copy-start = (bf16[640,1280]{1,0:T(8,128)(2,1)S(1)}, bf16[640,1280]{1,0:T(8,128)(2,1)}, u32[]{:S(2)}) copy-start(bf16[640,1280]{1,0:T(8,128)(2,1)} %weight_ref.1) | copy-start | bytes 4915204

commit v3 on v2

--- a/solution.py
+++ b/solution.py
@@ -158,36 +158,46 @@
     )(low, count, x, slot, *halos, segs)
 
 
-def arrange_kernel(slot_ref, tokens_ref, out_ref):
-    slots = out_ref.shape[0]
+def arrange_kernel(slot_ref, tokens_ref, *out_refs):
+    slots = out_refs[0].shape[0]
     rows, width = tokens_ref.shape
     tokens = tokens_ref[...]
-    slot = lax.broadcasted_iota(jnp.int32, (slots, rows), 0)
-    quarter = lax.broadcasted_iota(jnp.int32, (slots, rows), 1) % 4
+    total = len(out_refs) * slots
+    slot = lax.broadcasted_iota(jnp.int32, (total, rows), 0)
+    quarter = lax.broadcasted_iota(jnp.int32, (total, rows), 1) % 4
     mine = slot_ref[...] == slot
     for j in range(4):
         pick = jnp.where(mine & (quarter == j), 1.0, 0.0).astype(jnp.bfloat16)
-        out_ref[:, j * width : (j + 1) * width] = jnp.dot(
-            pick, tokens, preferred_element_type=jnp.float32
-        ).astype(jnp.bfloat16)
-
-
-def arrange(slot_of_patch, tokens, slots):
+        picked = jnp.dot(pick, tokens, preferred_element_type=jnp.float32).astype(jnp.bfloat16)
+        for d, out_ref in enumerate(out_refs):
+            out_ref[:, j * width : (j + 1) * width] = picked[d * slots : (d + 1) * slots]
+
+
+def arrange(slot_of_patch, tokens, pieces, slots):
     rows, width = tokens.shape
     return pl.pallas_call(
         arrange_kernel,
-        out_shape=jax.ShapeDtypeStruct((slots, 4 * width), jnp.bfloat16),
+        out_shape=[jax.ShapeDtypeStruct((slots // pieces, 4 * width), jnp.bfloat16)] * pieces,
         in_specs=[vmem()] * 2,
-        out_specs=vmem(),
+        out_specs=[vmem()] * pieces,
         compiler_params=params(),
     )(slot_of_patch, tokens)
 
 
-def finish_kernel(token_offsets_ref, offsets_ref, weight_ref, tokens_ref, attended_ref, out_hbm, held, sems):
+def finish_kernel(token_offsets_ref, offsets_ref, weight_hbm, attended_ref, *refs):
+    *token_refs, out_hbm, weight, held, weight_sems, sems = refs
     capacity, merged = out_hbm.shape
     groups, lanes = offsets_ref.shape
     width = merged // 4
     hdim = attended_ref.shape[1] // 4
+    part = weight.shape[0] // 4
+    loads = []
+    for j in range(4):
+        piece = pl.ds(j * part, part)
+        loads.append(
+            pltpu.make_async_copy(weight_hbm.at[piece], weight.at[piece], weight_sems.at[j])
+        )
+        loads[j].start()
 
     def pick(offsets):
         row = lax.broadcasted_iota(jnp.int32, (capacity, offsets.shape[1]), 0)
@@ -195,7 +205,7 @@
 
     token_pick = pick(token_offsets_ref[...])
     picks = [pick(offsets_ref[g : g + 1, :]) for g in range(groups)]
-    copies = []
+    placed = []
     for j in range(4):
         attended = jnp.zeros((capacity, HEADS * hdim), jnp.float32)
         for g in range(groups):
@@ -209,11 +219,15 @@
             attended += lax.dot_general(
                 picks[g], turned, (((1,), (1,)), ((), ())), preferred_element_type=jnp.float32
             )
+        placed.append(attended.astype(jnp.bfloat16))
+    for load in loads:
+        load.wait()
+    copies = []
+    for j in range(4):
         columns = slice(j * width, (j + 1) * width)
-        hidden = jnp.dot(
-            token_pick, tokens_ref[:, columns], preferred_element_type=jnp.float32
-        ) + jnp.dot(
-            attended.astype(jnp.bfloat16), weight_ref[...], preferred_element_type=jnp.float32
+        tokens = jnp.concatenate([ref[:, columns] for ref in token_refs], axis=0)
+        hidden = jnp.dot(token_pick, tokens, preferred_element_type=jnp.float32) + jnp.dot(
+            placed[j], weight[...], preferred_element_type=jnp.float32
         )
         held[j] = hidden.astype(jnp.bfloat16)
         copy = pltpu.make_async_copy(held.at[j], out_hbm.at[:, columns], sems.at[j])
@@ -223,19 +237,23 @@
         copy.wait()
 
 
-def finish(token_offsets, offsets, out_weight, tokens, attended, capacity):
-    merged = tokens.shape[1]
+def finish(token_offsets, offsets, out_weight, attended, tokens, capacity):
+    merged = tokens[0].shape[1]
     return pl.pallas_call(
         finish_kernel,
         out_shape=jax.ShapeDtypeStruct((capacity, merged), jnp.bfloat16),
-        in_specs=[vmem()] * 5,
+        in_specs=[vmem()] * 2
+        + [pl.BlockSpec(memory_space=pl.ANY)]
+        + [vmem()] * (1 + len(tokens)),
         out_specs=pl.BlockSpec(memory_space=pl.ANY),
         scratch_shapes=[
+            pltpu.VMEM(out_weight.shape, out_weight.dtype),
             pltpu.VMEM((4, capacity, merged // 4), jnp.bfloat16),
+            pltpu.SemaphoreType.DMA((4,)),
             pltpu.SemaphoreType.DMA((4,)),
         ],
         compiler_params=params(),
-    )(token_offsets, offsets, out_weight, tokens, attended)
+    )(token_offsets, offsets, out_weight, attended, *tokens)
 
 
 def per_device(segment_ids, block_mask, queries, keys, values, tokens, out_weight, owners, offsets):
@@ -244,6 +262,7 @@
     nblocks = lax.axis_size("blk")
     block_index = lax.axis_index("blk")
     ngroups = nblocks // HEADS
+    first = block_index // HEADS * HEADS
     groups = None
     if ngroups > 1:
         groups = [[g * HEADS + h for h in range(HEADS)] for g in range(ngroups)]
@@ -251,32 +270,40 @@
         lax.all_to_all, axis_name="blk", split_axis=0, concat_axis=0, tiled=True
     )
 
-    x = exchange(split_heads(queries, keys, values), axis_index_groups=groups)
+    split = split_heads(queries, keys, values)
+    split, tokens = lax.optimization_barrier((split, tokens))
+    x = exchange(split, axis_index_groups=groups)
 
     mrows = rows // 4
     capacity = 2 * mrows
     pair_rows = max(2, 2 * mrows // nblocks)
     slots = nblocks * pair_rows
-    onehot = (owners[:, None] == jnp.arange(nblocks)[None, :]).astype(jnp.int32)
-    ranks = jnp.sum((jnp.cumsum(onehot, axis=0) - 1) * onehot, axis=1)
-    slot_index = owners * pair_rows + ranks
-    match = slot_index[:, None] == jnp.arange(slots)[None, :]
-    outgoing_offsets = capacity + jnp.sum(
-        jnp.where(match, offsets[:, None] - capacity, 0), axis=0
-    )
-    outgoing_offsets = outgoing_offsets.reshape(nblocks, pair_rows)
-    outgoing_slots = jnp.broadcast_to(slot_index[None, :], (HEADS, mrows))
-    if ngroups == 1:
-        both = exchange(jnp.concatenate([outgoing_slots, outgoing_offsets], axis=1))
-        slots_of, arrived_offsets = both[:, :mrows], both[:, mrows:]
+
+    def ranks_of(owners):
+        onehot = (owners[..., None] == jnp.arange(nblocks)).astype(jnp.int32)
+        return jnp.sum((jnp.cumsum(onehot, axis=-2) - 1) * onehot, axis=-1)
+
+    pieces = nblocks if ngroups == 1 else 1
+    own_slots = owners * pair_rows + ranks_of(owners)
+    if pieces > 1:
+        own_slots = (own_slots - block_index * pair_rows) % slots
+    outgoing = arrange(jnp.repeat(own_slots, 4)[None, :], tokens, pieces, slots)
+    if pieces > 1:
+        arrived_tokens = [outgoing[0]] + [
+            lax.ppermute(outgoing[d], "blk", [(i, (i + d) % nblocks) for i in range(nblocks)])
+            for d in range(1, nblocks)
+        ]
     else:
-        slots_of = exchange(outgoing_slots, axis_index_groups=groups)
-        arrived_offsets = exchange(outgoing_offsets)
-
-    outgoing = arrange(jnp.repeat(slot_index, 4)[None, :], tokens, slots)
-    arrived_tokens = exchange(outgoing)
-
-    first = block_index // HEADS * HEADS
+        arrived_tokens = [exchange(outgoing[0])]
+
+    meta = lax.all_gather(jnp.stack([owners, offsets]), "blk")
+    all_owners, all_offsets = meta[:, 0], meta[:, 1]
+    all_ranks = ranks_of(all_owners)
+    here = (all_owners == block_index)[..., None] & (all_ranks[..., None] == jnp.arange(pair_rows))
+    arrived_offsets = capacity + jnp.sum(
+        jnp.where(here, all_offsets[..., None] - capacity, 0), axis=1
+    )
+
     segs = segment_ids.reshape(nblocks, 1, rows)
     base = 0
     halos = ()
@@ -299,6 +326,7 @@
     low = jnp.min(jnp.where(present, other, nblocks), axis=1) - first + base
     count = jnp.sum(present.astype(jnp.int32), axis=1)
 
+    slots_of = lax.dynamic_slice_in_dim(all_owners * pair_rows + all_ranks, first, HEADS, 0)
     turn = jnp.arange(HEADS)[:, None] * pair_rows
     slots_of = jnp.repeat((slots_of + turn) % slots, 4, axis=1)[:, None, :]
     sent = attention(low, count, x, slots_of, halos, segs, slots, pair_rows)
@@ -306,16 +334,17 @@
         sent = jnp.stack([jnp.roll(sent[o], -o * pair_rows, axis=1) for o in range(HEADS)])
         sent = sent.reshape(HEADS, 4 * hdim, ngroups, HEADS * pair_rows)
         sent = jnp.transpose(sent, (2, 0, 1, 3)).reshape(nblocks, 4 * hdim, HEADS * pair_rows)
-        lane_offsets = arrived_offsets
+        lane_offsets = token_offsets = arrived_offsets
     else:
         lane_offsets = jnp.roll(arrived_offsets, block_index, axis=0)
+        token_offsets = jnp.roll(arrived_offsets[::-1], block_index + 1, axis=0)
     arrived = exchange(sent)
     return finish(
-        arrived_offsets.reshape(1, slots),
+        token_offsets.reshape(1, slots),
         lane_offsets.reshape(ngroups, HEADS * pair_rows),
         out_weight,
+        arrived,
         arrived_tokens,
-        arrived,
         capacity,
     )
 

time: 105 us -> 104 us (level)
  the two profiles are of different devices: /device:TPU:0 before, /device:TPU:14 now
where the time goes in v3:
time: 104 us
  blocking collectives  30.9 us (30%)
  waiting for transfers between devices  30.5 us (29%)
  Pallas kernels  19.1 us (18%)
  starting transfers between devices  18.7 us (18%)
  other arithmetic  2.19 us (2%)
  local copies, waits for them, and re-layouts  2 us (2%)
    all_gather x1, blocking collectives, per_device(): meta = lax.all_gather(jnp.stack([owners, offsets]), 'blk')  30.9 us
    ppermute x7, waiting for transfers between devices, per_device(): lax.ppermute(outgoing[d], 'blk', [(i, (i + d) % nblocks) for i in range(n...  30.5 us
    pallas_call x1, Pallas kernels, attention(): pl.pallas_call(functools.partial(attention_kernel, bool(halos), pair_rows...  10.9 us
    ppermute x7, starting transfers between devices, per_device(): lax.ppermute(outgoing[d], 'blk', [(i, (i + d) % nblocks) for i in range(n...  7.32 us
    all_to_all x1, starting transfers between devices, per_device(): x = exchange(split, axis_index_groups=groups)  6.23 us
    all_to_all x1, starting transfers between devices, per_device(): arrived = exchange(sent)  5.17 us
    pallas_call x1, Pallas kernels, finish(): pl.pallas_call(finish_kernel, out_shape=jax.ShapeDtypeStruct((capacity, m...  4.45 us
    pallas_call x1, Pallas kernels, split_heads(): pl.pallas_call(split_heads_kernel, out_shape=jax.ShapeDtypeStruct((HEADS,...  2.4 us
  transfers between devices with their start and end apart: 9, of which 6 were waited for; matrix products, arithmetic and copies ran while one was open for 3% of the time, Pallas kernels for 1%

profile of v3, /device:TPU:14, one launch (start us, length us, event | category | flops | bytes accessed | tf_op | source)
XLA Modules:
  0.0 103.6 jit_solution(5884003486247121304)
XLA Ops:
  0.0 2.4 %shard_map.91 = bf16[8,240,256]{2,1,0:T(8,128)(2,1)} custom-call(bf16[256,640]{1,0:T(8,128)(2,1)} %q_hbm.1, bf16[256,640]{1,0:T(8,128)(2,1)} %k_hbm.1, bf16[256,640]{1,0:T(8,128)(2,1)} %v_hbm.1), custom_call_target="tpu_custom_call" | custom-call | tf_op jit(solution)/shard_map/pallas_call | solution.py:49
  2.4 6.2 %all-to-all-start = ((bf16[8,240,256]{2,1,0:T(8,128)(2,1)}), bf16[8,240,256]{2,1,0:T(8,128)(2,1)S(1)}, u32[]{:S(2)}, u32[]{:S(2)}) async-start(bf16[8,240,256]{2,1,0:T(8,128)(2,1)} %shard_map.91), calls=%async_computation | async-start | bytes 1966080 | tf_op jit(solution)/shard_map/all_to_all | solution.py:275
  8.7 30.9 %all-gather.1 = s32[8,2,64]{2,1,0:T(2,128)S(1)} all-gather(s32[1,2,64]{2,1,0:T(2,128)S(1)} %add_bitcast_fusion), channel_id=2, replica_groups=mesh['blk'=8,'rep'=4] {'blk'}, dimensions={0}, use_global_device_ids=true | all-gather | bytes 4608 | tf_op jit(solution)/shard_map/all_gather | solution.py:299
  39.9 1.3 %fusion.11 = s32[8,64]{0,1:T(8,128)S(1)} fusion(s32[8,64]{0,1:T(8,128)S(1)} %bitcast.11), kind=kOutput, calls=%fused_computation.38 | output fusion | flops 282112 | bytes 4096 | tf_op jit(solution)/shard_map/jit(cumsum)/reduce_window_sum | solution.py:284
  41.4 0.2 convert_reduce_fusion
  41.6 0.2 select_reduce_fusion.1
  41.8 10.9 %shard_map.92 = bf16[8,320,128]{2,1,0:T(8,128)(2,1)} custom-call(s32[8]{0:T(128)S(1)} %broadcast_subtract_fusion.low_ref, s32[8]{0:T(128)S(1)} %get-tuple-element.26.count_ref, bf16[8,240,256]{2,1,0:T(8,128)(2,1)S(1)} %all-to-all-done.x_ref, s32[8,1,256]{2,1,0:T(1,128)S(1)} %copy.21.slot_ref, f32[8,1,256]{2,1,0:T(1,128)S(1)} %bitcast.10), custom_call_target="tpu_custom_call" | custom-call | tf_op jit(solution)/shard_map/pallas_call | solution.py:151
  52.7 5.2 %all-to-all-start.1 = ((bf16[8,320,128]{2,1,0:T(8,128)(2,1)}), bf16[8,320,128]{2,1,0:T(8,128)(2,1)S(1)}, u32[]{:S(2)}, u32[]{:S(2)}) async-start(bf16[8,320,128]{2,1,0:T(8,128)(2,1)} %shard_map.92), calls=%async_computation.1 | async-start | bytes 1310720 | tf_op jit(solution)/shard_map/all_to_all | solution.py:341
  58.0 0.1 broadcast_in_dim_reshape.7.slot_ref
  58.1 1.4 %shard_map.93 = (bf16[16,5120]{1,0:T(8,128)(2,1)S(1)}, bf16[16,5120]{1,0:T(8,128)(2,1)S(1)}, bf16[16,5120]{1,0:T(8,128)(2,1)}, bf16[16,5120]{1,0:T(8,128)(2,1)},...) custom-call(s32[1,256]{1,0:T(1,128)S(1)} %broadcast_in_dim_reshape.7, ...), custom_call_target="tpu_custom_call" | custom-call | tf_op jit(solution)/shard_map/pallas_call | solution.py:178
  59.5 0.6 copy-done.2
  60.1 0.7 copy-done.3
  60.8 1.5 %collective-permute-start = (bf16[16,5120]{1,0:T(8,128)(2,1)S(1)}, bf16[16,5120]{1,0:T(8,128)(2,1)S(1)}, u32[]{:S(2)}, u32[]{:S(2)}) collective-permute-start(bf16[16,5120]{1,0:T(8,128)(2,1)S(1)} %get-tuple-element.19), channel_id=1, source_target_pairs={{0,4},{4,8},{8,12},{12,16},{16,20},{20,24},{24,28},{28,0},{1,5},{5... | collective-permute-start | bytes 491528 | tf_op jit(solution)/shard_map/ppermute | solution.py:293
  62.2 1.5 %collective-permute-start.1 = (bf16[16,5120]{1,0:T(8,128)(2,1)}, bf16[16,5120]{1,0:T(8,128)(2,1)S(1)}, u32[]{:S(2)}, u32[]{:S(2)}) collective-permute-start(bf16[16,5120]{1,0:T(8,128)(2,1)} %get-tuple-element.20), channel_id=1, source_target_pairs={{0,8},{4,12},{8,16},{12,20},{16,24},{20,28},{24,0},{28,4},{1,9},{5... | collective-permute-start | bytes 491528 | tf_op jit(solution)/shard_map/ppermute | solution.py:293
  63.7 1.5 %collective-permute-start.2 = (bf16[16,5120]{1,0:T(8,128)(2,1)}, bf16[16,5120]{1,0:T(8,128)(2,1)S(1)}, u32[]{:S(2)}, u32[]{:S(2)}) collective-permute-start(bf16[16,5120]{1,0:T(8,128)(2,1)} %get-tuple-element.21), channel_id=1, source_target_pairs={{0,12},{4,16},{8,20},{12,24},{16,28},{20,0},{24,4},{28,8},{1,13},{... | collective-permute-start | bytes 491528 | tf_op jit(solution)/shard_map/ppermute | solution.py:293
  65.2 1.5 %collective-permute-start.3 = (bf16[16,5120]{1,0:T(8,128)(2,1)}, bf16[16,5120]{1,0:T(8,128)(2,1)S(1)}, u32[]{:S(2)}, u32[]{:S(2)}) collective-permute-start(bf16[16,5120]{1,0:T(8,128)(2,1)} %get-tuple-element.22), channel_id=1, source_target_pairs={{0,16},{4,20},{8,24},{12,28},{16,0},{20,4},{24,8},{28,12},{1,17},{... | collective-permute-start | bytes 491528 | tf_op jit(solution)/shard_map/ppermute | solution.py:293
  66.6 1.5 %collective-permute-start.4 = (bf16[16,5120]{1,0:T(8,128)(2,1)}, bf16[16,5120]{1,0:T(8,128)(2,1)S(1)}, u32[]{:S(2)}, u32[]{:S(2)}) collective-permute-start(bf16[16,5120]{1,0:T(8,128)(2,1)} %get-tuple-element.23), channel_id=1, source_target_pairs={{0,20},{4,24},{8,28},{12,0},{16,4},{20,8},{24,12},{28,16},{1,21},{... | collective-permute-start | bytes 491528 | tf_op jit(solution)/shard_map/ppermute | solution.py:293
  68.2 0.2 select_reduce_fusion
  68.5 19.8 %collective-permute-done.refs_1_ = bf16[16,5120]{1,0:T(8,128)(2,1)S(1)} collective-permute-done((bf16[16,5120]{1,0:T(8,128)(2,1)S(1)}, bf16[16,5120]{1,0:T(8,128)(2,1)S(1)}, u32[]{:S(2)}, u32[]{:S(2)}) %collective-permute-start) | collective-permute-done | bytes 163872 | tf_op jit(solution)/shard_map/ppermute | solution.py:293
  88.3 3.6 %collective-permute-done.1.refs_2_ = bf16[16,5120]{1,0:T(8,128)(2,1)S(1)} collective-permute-done((bf16[16,5120]{1,0:T(8,128)(2,1)}, bf16[16,5120]{1,0:T(8,128)(2,1)S(1)}, u32[]{:S(2)}, u32[]{:S(2)}) %collective-permute-start.1) | collective-permute-done | bytes 163872 | tf_op jit(solution)/shard_map/ppermute | solution.py:293
  92.1 3.3 %collective-permute-done.2.refs_3_ = bf16[16,5120]{1,0:T(8,128)(2,1)S(1)} collective-permute-done((bf16[16,5120]{1,0:T(8,128)(2,1)}, bf16[16,5120]{1,0:T(8,128)(2,1)S(1)}, u32[]{:S(2)}, u32[]{:S(2)}) %collective-permute-start.2) | collective-permute-done | bytes 163872 | tf_op jit(solution)/shard_map/ppermute | solution.py:293
  95.4 2.0 %collective-permute-done.3.refs_4_ = bf16[16,5120]{1,0:T(8,128)(2,1)S(1)} collective-permute-done((bf16[16,5120]{1,0:T(8,128)(2,1)}, bf16[16,5120]{1,0:T(8,128)(2,1)S(1)}, u32[]{:S(2)}, u32[]{:S(2)}) %collective-permute-start.3) | collective-permute-done | bytes 163872 | tf_op jit(solution)/shard_map/ppermute | solution.py:293
  97.4 1.7 %collective-permute-done.5.refs_6_ = bf16[16,5120]{1,0:T(8,128)(2,1)S(1)} collective-permute-done((bf16[16,5120]{1,0:T(8,128)(2,1)}, bf16[16,5120]{1,0:T(8,128)(2,1)S(1)}, u32[]{:S(2)}, u32[]{:S(2)}) %collective-permute-start.5) | collective-permute-done | bytes 163872 | tf_op jit(solution)/shard_map/ppermute | solution.py:293
  99.2 4.4 %shard_map.94 = bf16[128,5120]{1,0:T(8,128)(2,1)} custom-call(s32[1,128]{1,0:T(1,128)S(1)} %reshape.47.token_offsets_ref, s32[1,128]{1,0:T(1,128)S(1)} %reshape.48.offsets_ref, bf16[640,1280]{1,0:T(8,128)(2,1)S(1)} %copy-done, bf16[8,320,128]{2,1,0:T(8,128)(2,1)S(1)} %all-to-all-done.1.attended_ref, bf16[16,5120]{1,0:T(8,128)(2,1)S(1)} %get-tuple-element.18.refs_0_, ...), custom_call_target="tpu_custom_call" | custom-call | tf_op jit(solution)/shard_map/pallas_call | solution.py:242
  (44 shorter events, 0.9 us)
Async XLA Ops:
  0.0 8.7 %copy-start.5 = (s32[2048]{0:T(1024)S(1)}, s32[2048]{0:T(1024)}, u32[]{:S(2)}) copy-start(s32[2048]{0:T(1024)} %param.11) | copy-start | bytes 24580
  0.0 8.7 %copy-start.4 = (s32[64]{0:T(128)S(1)}, s32[64]{0:T(128)}, u32[]{:S(2)}) copy-start(s32[64]{0:T(128)} %param.18) | copy-start | bytes 772
  0.0 8.7 %copy-start.7 = (s32[64]{0:T(128)S(1)}, s32[64]{0:T(128)}, u32[]{:S(2)}) copy-start(s32[64]{0:T(128)} %param.19) | copy-start | bytes 772
  2.4 39.0 %copy-start.6 = (s32[8,8]{1,0:T(8,128)S(1)}, s32[8,8]{1,0:T(8,128)}, u32[]{:S(2)}) copy-start(s32[8,8]{1,0:T(8,128)} %param.12) | copy-start | bytes 772
  2.4 39.4 %all-to-all-start = ((bf16[8,240,256]{2,1,0:T(8,128)(2,1)}), bf16[8,240,256]{2,1,0:T(8,128)(2,1)S(1)}, u32[]{:S(2)}, u32[]{:S(2)}) async-start(bf16[8,240,256]{2,1,0:T(8,128)(2,1)} %shard_map.91), calls=%async_computation | async-start | bytes 1966080 | tf_op jit(solution)/shard_map/all_to_all | solution.py:275
  41.3 16.8 %copy-start.1 = (bf16[256,1280]{1,0:T(8,128)(2,1)S(1)}, bf16[256,1280]{1,0:T(8,128)(2,1)}, u32[]{:S(2)}) copy-start(bf16[256,1280]{1,0:T(8,128)(2,1)} %tokens_ref) | copy-start | bytes 1966084
  41.8 57.4 %copy-start = (bf16[640,1280]{1,0:T(8,128)(2,1)S(1)}, bf16[640,1280]{1,0:T(8,128)(2,1)}, u32[]{:S(2)}) copy-start(bf16[640,1280]{1,0:T(8,128)(2,1)} %weight_hbm.1) | copy-start | bytes 4915204
  52.7 46.5 %all-to-all-start.1 = ((bf16[8,320,128]{2,1,0:T(8,128)(2,1)}), bf16[8,320,128]{2,1,0:T(8,128)(2,1)S(1)}, u32[]{:S(2)}, u32[]{:S(2)}) async-start(bf16[8,320,128]{2,1,0:T(8,128)(2,1)} %shard_map.92), calls=%async_computation.1 | async-start | bytes 1310720 | tf_op jit(solution)/shard_map/all_to_all | solution.py:341
  59.5 0.7 copy-start.2
  60.1 0.7 copy-start.3
  60.8 27.5 %collective-permute-start = (bf16[16,5120]{1,0:T(8,128)(2,1)S(1)}, bf16[16,5120]{1,0:T(8,128)(2,1)S(1)}, u32[]{:S(2)}, u32[]{:S(2)}) collective-permute-start(bf16[16,5120]{1,0:T(8,128)(2,1)S(1)} %get-tuple-element.19), channel_id=1, source_target_pairs={{0,4},{4,8},{8,12},{12,16},{16,20},{20,24},{24,28},{28,0},{1,5},{5... | collective-permute-start | bytes 491528 | tf_op jit(solution)/shard_map/ppermute | solution.py:293
  62.2 29.7 %collective-permute-start.1 = (bf16[16,5120]{1,0:T(8,128)(2,1)}, bf16[16,5120]{1,0:T(8,128)(2,1)S(1)}, u32[]{:S(2)}, u32[]{:S(2)}) collective-permute-start(bf16[16,5120]{1,0:T(8,128)(2,1)} %get-tuple-element.20), channel_id=1, source_target_pairs={{0,8},{4,12},{8,16},{12,20},{16,24},{20,28},{24,0},{28,4},{1,9},{5... | collective-permute-start | bytes 491528 | tf_op jit(solution)/shard_map/ppermute | solution.py:293
  63.7 31.7 %collective-permute-start.2 = (bf16[16,5120]{1,0:T(8,128)(2,1)}, bf16[16,5120]{1,0:T(8,128)(2,1)S(1)}, u32[]{:S(2)}, u32[]{:S(2)}) collective-permute-start(bf16[16,5120]{1,0:T(8,128)(2,1)} %get-tuple-element.21), channel_id=1, source_target_pairs={{0,12},{4,16},{8,20},{12,24},{16,28},{20,0},{24,4},{28,8},{1,13},{... | collective-permute-start | bytes 491528 | tf_op jit(solution)/shard_map/ppermute | solution.py:293
  65.2 32.2 %collective-permute-start.3 = (bf16[16,5120]{1,0:T(8,128)(2,1)}, bf16[16,5120]{1,0:T(8,128)(2,1)S(1)}, u32[]{:S(2)}, u32[]{:S(2)}) collective-permute-start(bf16[16,5120]{1,0:T(8,128)(2,1)} %get-tuple-element.22), channel_id=1, source_target_pairs={{0,16},{4,20},{8,24},{12,28},{16,0},{20,4},{24,8},{28,12},{1,17},{... | collective-permute-start | bytes 491528 | tf_op jit(solution)/shard_map/ppermute | solution.py:293
  66.6 30.8 %collective-permute-start.4 = (bf16[16,5120]{1,0:T(8,128)(2,1)}, bf16[16,5120]{1,0:T(8,128)(2,1)S(1)}, u32[]{:S(2)}, u32[]{:S(2)}) collective-permute-start(bf16[16,5120]{1,0:T(8,128)(2,1)} %get-tuple-element.23), channel_id=1, source_target_pairs={{0,20},{4,24},{8,28},{12,0},{16,4},{20,8},{24,12},{28,16},{1,21},{... | collective-permute-start | bytes 491528 | tf_op jit(solution)/shard_map/ppermute | solution.py:293
  88.3 10.8 %collective-permute-start.5 = (bf16[16,5120]{1,0:T(8,128)(2,1)}, bf16[16,5120]{1,0:T(8,128)(2,1)S(1)}, u32[]{:S(2)}, u32[]{:S(2)}) collective-permute-start(bf16[16,5120]{1,0:T(8,128)(2,1)} %copy-done.3), channel_id=1, source_target_pairs={{0,24},{4,28},{8,0},{12,4},{16,8},{20,12},{24,16},{28,20},{1,25},{... | collective-permute-start | bytes 491528 | tf_op jit(solution)/shard_map/ppermute | solution.py:293
  91.9 7.3 %collective-permute-start.6 = (bf16[16,5120]{1,0:T(8,128)(2,1)}, bf16[16,5120]{1,0:T(8,128)(2,1)}, u32[]{:S(2)}, u32[]{:S(2)}) collective-permute-start(bf16[16,5120]{1,0:T(8,128)(2,1)} %copy-done.2), channel_id=1, source_target_pairs={{0,28},{4,0},{8,4},{12,8},{16,12},{20,16},{24,20},{28,24},{1,29},{... | collective-permute-start | bytes 491528 | tf_op jit(solution)/shard_map/ppermute | solution.py:293

commit v4 on v3

--- a/solution.py
+++ b/solution.py
@@ -26,14 +26,33 @@
     return pl.BlockSpec(memory_space=pltpu.SMEM)
 
 
-def split_heads_kernel(q_hbm, k_hbm, v_hbm, out_ref, held, sems):
-    hdim = q_hbm.shape[1] // HEADS
+def split_heads_kernel(pair_rows, owners_ref, offsets_ref, q_hbm, k_hbm, v_hbm, out_ref, slot_ref, held, sems):
+    rows, features = q_hbm.shape
+    hdim = features // HEADS
+    mrows = rows // 4
     copies = [
         pltpu.make_async_copy(ref, held.at[part], sems.at[part])
         for part, ref in enumerate((q_hbm, k_hbm, v_hbm))
     ]
     for copy in copies:
         copy.start()
+
+    owner = jnp.broadcast_to(owners_ref[...].astype(jnp.float32), (mrows, mrows))
+    earlier = lax.broadcasted_iota(jnp.int32, (mrows, mrows), 0)
+    later = lax.broadcasted_iota(jnp.int32, (mrows, mrows), 1)
+    column = jnp.sum(jnp.where(earlier == later, owner, 0.0), axis=1, keepdims=True)
+    ahead = jnp.where((owner == column) & (earlier < later), 1.0, 0.0)
+    slot = owner[:1] * pair_rows + jnp.sum(ahead, axis=0, keepdims=True)
+    line = lax.broadcasted_iota(jnp.int32, (16, mrows), 0)
+    meta = jnp.where(line == 0, slot, jnp.where(line == 1, offsets_ref[...].astype(jnp.float32), 0.0))
+    row = lax.broadcasted_iota(jnp.int32, (mrows, rows), 0)
+    patch = lax.broadcasted_iota(jnp.int32, (mrows, rows), 1)
+    spread = jnp.where(patch // 4 == row, 1.0, 0.0).astype(jnp.bfloat16)
+    meta = jnp.dot(meta.astype(jnp.bfloat16), spread, preferred_element_type=jnp.float32)
+    slot_ref[...] = meta[:1].astype(jnp.int32)
+    for head in range(HEADS):
+        out_ref[head, 3 * hdim :, :] = meta.astype(jnp.bfloat16)
+
     for part, copy in enumerate(copies):
         copy.wait()
         turned = held[part].T
@@ -43,28 +62,32 @@
             ]
 
 
-def split_heads(queries, keys, values):
+def split_heads(owners, offsets, queries, keys, values, pair_rows):
     rows, features = queries.shape
     hdim = features // HEADS
     return pl.pallas_call(
-        split_heads_kernel,
-        out_shape=jax.ShapeDtypeStruct((HEADS, 3 * hdim, rows), queries.dtype),
-        in_specs=[pl.BlockSpec(memory_space=pl.ANY)] * 3,
-        out_specs=vmem(),
+        functools.partial(split_heads_kernel, pair_rows),
+        out_shape=(
+            jax.ShapeDtypeStruct((HEADS, 3 * hdim + 16, rows), queries.dtype),
+            jax.ShapeDtypeStruct((1, rows), jnp.int32),
+        ),
+        in_specs=[vmem()] * 2 + [pl.BlockSpec(memory_space=pl.ANY)] * 3,
+        out_specs=(vmem(), vmem()),
         scratch_shapes=[
             pltpu.VMEM((3, rows, features), queries.dtype),
             pltpu.SemaphoreType.DMA((3,)),
         ],
         compiler_params=pltpu.CompilerParams(vmem_limit_bytes=60 * 1024 * 1024),
-    )(queries, keys, values)
-
-
-def attention_kernel(halo, pair_rows, low_ref, count_ref, x_ref, slot_ref, *refs):
+    )(owners, offsets, queries, keys, values)
+
+
+def attention_kernel(halo, pair_rows, low_ref, count_ref, x_ref, *refs):
     if halo:
         below_ref, above_ref, seg_ref, out_ref, key_s, value_s, seg_s, picked_s = refs
     else:
         seg_ref, out_ref, key_s, seg_s, picked_s = refs
-    blocks, triple, rows = x_ref.shape
+    blocks, lines, rows = x_ref.shape
+    triple = lines - 16
     hdim = triple // 3
     slots = out_ref.shape[2]
     base = SPAN if halo else 0
@@ -81,11 +104,11 @@
         else:
             key_s[b] = x_ref[b - base, hdim : 2 * hdim, :].T
             if halo:
-                value_s[b] = x_ref[b - base, 2 * hdim :, :]
+                value_s[b] = x_ref[b - base, 2 * hdim : triple, :]
         seg_s[b] = jnp.broadcast_to(seg_ref[b], (128, rows)).T
 
     def value_block(b):
-        return value_s[b] if halo else x_ref[b, 2 * hdim :, :]
+        return value_s[b] if halo else x_ref[b, 2 * hdim : triple, :]
 
     slot = lax.broadcasted_iota(jnp.int32, (slots, rows), 0)
     quarter = lax.broadcasted_iota(jnp.int32, (slots, rows), 1) % 4
@@ -95,7 +118,8 @@
         count = count_ref[i]
         query = x_ref[i, :hdim, :]
         query_seg = seg_ref[i + base]
-        mine = slot_ref[i] == slot
+        place = x_ref[i, triple:, :].astype(jnp.float32)[:1].astype(jnp.int32) + i * pair_rows
+        mine = jnp.where(place >= slots, place - slots, place) == slot
 
         for size in range(1, 2 * SPAN + 2):
 
@@ -139,9 +163,9 @@
         out_ref[first] = chosen.astype(out_ref.dtype)
 
 
-def attention(low, count, x, slot, halos, segs, slots, pair_rows):
-    blocks, triple, rows = x.shape
-    hdim = triple // 3
+def attention(low, count, x, halos, segs, slots, pair_rows):
+    blocks, lines, rows = x.shape
+    hdim = (lines - 16) // 3
     extended = segs.shape[0]
     scratch = [pltpu.VMEM((extended, rows, hdim), jnp.bfloat16)]
     if halos:
@@ -151,11 +175,14 @@
     return pl.pallas_call(
         functools.partial(attention_kernel, bool(halos), pair_rows),
         out_shape=jax.ShapeDtypeStruct((blocks, 4 * hdim, slots), jnp.bfloat16),
-        in_specs=[smem(), smem()] + [vmem()] * (3 + len(halos)),
+        in_specs=[smem(), smem()] + [vmem()] * (2 + len(halos)),
         out_specs=vmem(),
         scratch_shapes=scratch,
         compiler_params=params(),
-    )(low, count, x, slot, *halos, segs)
+        cost_estimate=pl.CostEstimate(
+            flops=8_000_000_000, bytes_accessed=8_000_000, transcendentals=3_000_000
+        ),
+    )(low, count, x, *halos, segs)
 
 
 def arrange_kernel(slot_ref, tokens_ref, *out_refs):
@@ -270,39 +297,48 @@
         lax.all_to_all, axis_name="blk", split_axis=0, concat_axis=0, tiled=True
     )
 
-    split = split_heads(queries, keys, values)
-    split, tokens = lax.optimization_barrier((split, tokens))
-    x = exchange(split, axis_index_groups=groups)
-
     mrows = rows // 4
     capacity = 2 * mrows
     pair_rows = max(2, 2 * mrows // nblocks)
     slots = nblocks * pair_rows
-
-    def ranks_of(owners):
-        onehot = (owners[..., None] == jnp.arange(nblocks)).astype(jnp.int32)
-        return jnp.sum((jnp.cumsum(onehot, axis=-2) - 1) * onehot, axis=-1)
+    assert slots <= 256
+
+    split, own_slots = split_heads(
+        owners[None, :], offsets[None, :], queries, keys, values, pair_rows
+    )
+    split, own_slots = lax.optimization_barrier((split, own_slots))
+    x = exchange(split, axis_index_groups=groups)
 
     pieces = nblocks if ngroups == 1 else 1
-    own_slots = owners * pair_rows + ranks_of(owners)
     if pieces > 1:
         own_slots = (own_slots - block_index * pair_rows) % slots
-    outgoing = arrange(jnp.repeat(own_slots, 4)[None, :], tokens, pieces, slots)
+    outgoing = arrange(own_slots, tokens, pieces, slots)
     if pieces > 1:
-        arrived_tokens = [outgoing[0]] + [
-            lax.ppermute(outgoing[d], "blk", [(i, (i + d) % nblocks) for i in range(nblocks)])
-            for d in range(1, nblocks)
-        ]
+        arrived_tokens = {0: outgoing[0]}
+        for d in (4, 3, 5, 2, 6, 1, 7):
+            route = [(i, (i + d) % nblocks) for i in range(nblocks)]
+            arrived_tokens[d] = lax.ppermute(outgoing[d], "blk", route)
+        early = (4, 3, 5, 2)
+        x, *done = lax.optimization_barrier((x, *[arrived_tokens[d] for d in early]))
+        arrived_tokens.update(zip(early, done))
+        arrived_tokens = [arrived_tokens[d] for d in range(nblocks)]
     else:
         arrived_tokens = [exchange(outgoing[0])]
 
-    meta = lax.all_gather(jnp.stack([owners, offsets]), "blk")
-    all_owners, all_offsets = meta[:, 0], meta[:, 1]
-    all_ranks = ranks_of(all_owners)
-    here = (all_owners == block_index)[..., None] & (all_ranks[..., None] == jnp.arange(pair_rows))
-    arrived_offsets = capacity + jnp.sum(
-        jnp.where(here, all_offsets[..., None] - capacity, 0), axis=1
-    )
+    if pieces > 1:
+        meta = x[:, 3 * hdim : 3 * hdim + 2, ::4].astype(jnp.int32)
+        all_slots, all_offsets = meta[:, 0], meta[:, 1]
+        wanted = block_index * pair_rows + jnp.arange(pair_rows)
+        here = all_slots[..., None] == wanted
+        arrived_offsets = capacity + jnp.sum(
+            jnp.where(here, all_offsets[..., None] - capacity, 0), axis=1
+        )
+    else:
+        match = own_slots[0, ::4, None] == jnp.arange(slots)
+        outgoing_offsets = capacity + jnp.sum(
+            jnp.where(match, offsets[:, None] - capacity, 0), axis=0
+        )
+        arrived_offsets = exchange(outgoing_offsets.reshape(nblocks, pair_rows))
 
     segs = segment_ids.reshape(nblocks, 1, rows)
     base = 0
@@ -312,8 +348,8 @@
         up = [(i, i + HEADS) for i in range(nblocks - HEADS)]
         down = [(i + HEADS, i) for i in range(nblocks - HEADS)]
         halos = (
-            lax.ppermute(x[HEADS - SPAN :, hdim:], "blk", up),
-            lax.ppermute(x[:SPAN, hdim:], "blk", down),
+            lax.ppermute(x[HEADS - SPAN :, hdim : 3 * hdim], "blk", up),
+            lax.ppermute(x[:SPAN, hdim : 3 * hdim], "blk", down),
         )
         segs = jnp.pad(segs, ((SPAN, SPAN), (0, 0), (0, 0)), constant_values=-1)
         segs = lax.dynamic_slice_in_dim(segs, first, HEADS + 2 * SPAN, 0)
@@ -326,10 +362,7 @@
     low = jnp.min(jnp.where(present, other, nblocks), axis=1) - first + base
     count = jnp.sum(present.astype(jnp.int32), axis=1)
 
-    slots_of = lax.dynamic_slice_in_dim(all_owners * pair_rows + all_ranks, first, HEADS, 0)
-    turn = jnp.arange(HEADS)[:, None] * pair_rows
-    slots_of = jnp.repeat((slots_of + turn) % slots, 4, axis=1)[:, None, :]
-    sent = attention(low, count, x, slots_of, halos, segs, slots, pair_rows)
+    sent = attention(low, count, x, halos, segs, slots, pair_rows)
     if ngroups > 1:
         sent = jnp.stack([jnp.roll(sent[o], -o * pair_rows, axis=1) for o in range(HEADS)])
         sent = sent.reshape(HEADS, 4 * hdim, ngroups, HEADS * pair_rows)

time: 104 us -> 103 us (level)
  blocking collectives: 30.9 us -> 0 us
  waiting for transfers between devices: 30.5 us -> 52.9 us
  local copies, waits for them, and re-layouts: 2 us -> 9.53 us
  starting transfers between devices: 18.7 us -> 20.8 us
  other arithmetic: 2.19 us -> 0.54 us
    all_gather x1 -> x0, blocking collectives: 30.9 us -> none  [per_device(): meta = lax.all_gather(jnp.stack([owners, offsets]), 'blk')]
    ppermute x7, waiting for transfers between devices: 30.5 us -> 52.9 us  [per_device(): arrived_tokens[d] = lax.ppermute(outgoing[d], 'blk', route)]
    unnamed x17 -> x34, local copies, waits for them, and re-layouts: 1.43 us -> 9.13 us
    another operation x2 -> x0, other arithmetic: 1.41 us -> none  [ranks_of(): return jnp.sum((jnp.cumsum(onehot, axis=-2) - 1) * onehot, axis=-1)]
    all_to_all x1, starting transfers between devices: 5.17 us -> 6.42 us  [per_device(): arrived = exchange(sent)]
  transfers between devices with their start and end apart: 9 -> 9, of which waited for: 6 -> 5; matrix products, arithmetic and copies ran while one was open for 3% -> 1% of each run, Pallas kernels for 1% -> 1%
where the time goes in v4:
time: 103 us; the launch traced here: 102 us
  waiting for transfers between devices  52.9 us (51%)
  starting transfers between devices  20.8 us (20%)
  Pallas kernels  18.2 us (18%)
  local copies, waits for them, and re-layouts  9.53 us (9%)
    ppermute x7, waiting for transfers between devices, per_device(): arrived_tokens[d] = lax.ppermute(outgoing[d], 'blk', route)  52.9 us
    pallas_call x1, Pallas kernels, attention(): pl.pallas_call(functools.partial(attention_kernel, bool(halos), pair_rows...  9.9 us
    unnamed x34, local copies, waits for them, and re-layouts  9.13 us
    ppermute x7, starting transfers between devices, per_device(): arrived_tokens[d] = lax.ppermute(outgoing[d], 'blk', route)  8.13 us
    all_to_all x1, starting transfers between devices, per_device(): arrived = exchange(sent)  6.42 us
    all_to_all x1, starting transfers between devices, per_device(): x = exchange(split, axis_index_groups=groups)  6.23 us
    pallas_call x1, Pallas kernels, finish(): pl.pallas_call(finish_kernel, out_shape=jax.ShapeDtypeStruct((capacity, m...  4.6 us
    pallas_call x1, Pallas kernels, split_heads(): pl.pallas_call(functools.partial(split_heads_kernel, pair_rows), out_shap...  3.13 us
  transfers between devices with their start and end apart: 9, of which 5 were waited for; matrix products, arithmetic and copies ran while one was open for 1% of the time, Pallas kernels for 1%

profile of v4, /device:TPU:14, one launch (start us, length us, event | category | flops | bytes accessed | tf_op | source)
XLA Modules:
  0.0 102.1 jit_solution(2772736623964285404)
XLA Ops:
  0.0 3.1 %shard_map.91 = (bf16[8,256,256]{2,1,0:T(8,128)(2,1)}, s32[1,256]{1,0:T(1,128)}) custom-call(s32[1,64]{1,0:T(1,128)} %bitcast.8, s32[1,64]{1,0:T(1,128)} %bitcast.9, bf16[256,640]{1,0:T(8,128)(2,1)} %q_hbm.1, bf16[256,640]{1,0:T(8,128)(2,1)} %k_hbm.1, bf16[256,640]{1,0:T(8,128)(2,1)} %v_hbm.1), custom_call_target="tpu_custom_call" | custom-call | tf_op jit(solution)/shard_map/pallas_call | solution.py:68
  3.2 6.2 %all-to-all-start = ((bf16[8,256,256]{2,1,0:T(8,128)(2,1)}), bf16[8,256,256]{2,1,0:T(8,128)(2,1)S(1)}, u32[]{:S(2)}, u32[]{:S(2)}) async-start(bf16[8,256,256]{2,1,0:T(8,128)(2,1)} %get-tuple-element.21), calls=%async_computation | async-start | bytes 2097152 | tf_op jit(solution)/shard_map/all_to_all | solution.py:310
  10.6 0.7 copy-done.12
  11.3 0.7 copy-done.13
  11.9 2.4 %collective-permute-start = (bf16[16,5120]{1,0:T(8,128)(2,1)S(1)}, bf16[16,5120]{1,0:T(8,128)(2,1)S(1)}, u32[]{:S(2)}, u32[]{:S(2)}) collective-permute-start(bf16[16,5120]{1,0:T(8,128)(2,1)S(1)} %get-tuple-element.23), channel_id=1, source_target_pairs={{0,16},{4,20},{8,24},{12,28},{16,0},{20,4},{24,8},{28,12},{1,17},{... | collective-permute-start | bytes 491528 | tf_op jit(solution)/shard_map/ppermute | solution.py:320
  14.9 2.4 %collective-permute-start.2 = (bf16[16,5120]{1,0:T(8,128)(2,1)S(1)}, bf16[16,5120]{1,0:T(8,128)(2,1)S(1)}, u32[]{:S(2)}, u32[]{:S(2)}) collective-permute-start(bf16[16,5120]{1,0:T(8,128)(2,1)S(1)} %get-tuple-element.25), channel_id=1, source_target_pairs={{0,20},{4,24},{8,28},{12,0},{16,4},{20,8},{24,12},{28,16},{1,21},{... | collective-permute-start | bytes 491528 | tf_op jit(solution)/shard_map/ppermute | solution.py:320
  17.5 28.8 %collective-permute-done.refs_4_ = bf16[16,5120]{1,0:T(8,128)(2,1)S(1)} collective-permute-done((bf16[16,5120]{1,0:T(8,128)(2,1)S(1)}, bf16[16,5120]{1,0:T(8,128)(2,1)S(1)}, u32[]{:S(2)}, u32[]{:S(2)}) %collective-permute-start) | collective-permute-done | bytes 163872 | tf_op jit(solution)/shard_map/ppermute | solution.py:320
  46.3 0.7 copy-done.3
  47.0 2.8 %collective-permute-done.1.refs_3_ = bf16[16,5120]{1,0:T(8,128)(2,1)S(1)} collective-permute-done((bf16[16,5120]{1,0:T(8,128)(2,1)S(1)}, bf16[16,5120]{1,0:T(8,128)(2,1)S(1)}, u32[]{:S(2)}, u32[]{:S(2)}) %collective-permute-start.1) | collective-permute-done | bytes 163872 | tf_op jit(solution)/shard_map/ppermute | solution.py:320
  49.8 0.7 copy-done.5
  50.5 0.7 copy-done.7
  51.1 2.1 %collective-permute-done.3.refs_2_ = bf16[16,5120]{1,0:T(8,128)(2,1)S(1)} collective-permute-done((bf16[16,5120]{1,0:T(8,128)(2,1)S(1)}, bf16[16,5120]{1,0:T(8,128)(2,1)S(1)}, u32[]{:S(2)}, u32[]{:S(2)}) %collective-permute-start.3) | collective-permute-done | bytes 163872 | tf_op jit(solution)/shard_map/ppermute | solution.py:320
  53.9 9.9 %shard_map.93 = bf16[8,320,128]{2,1,0:T(8,128)(2,1)S(1)} custom-call(s32[8]{0:T(128)S(1)} %broadcast_subtract_fusion.low_ref, s32[8]{0:T(128)S(1)} %get-tuple-element.36.count_ref, bf16[8,256,256]{2,1,0:T(8,128)(2,1)S(1)} %all-to-all-done.x_ref, f32[8,1,256]{2,1,0:T(1,128)S(1)} %bitcast.5), custom_call_target="tpu_custom_call" | custom-call | flops 8000000000 | bytes 8000000 | tf_op jit(solution)/shard_map/pallas_call | solution.py:175
  63.8 0.8 copy-done.2
  64.6 6.4 %all-to-all-start.1 = ((bf16[8,320,128]{2,1,0:T(8,128)(2,1)}), bf16[8,320,128]{2,1,0:T(8,128)(2,1)S(1)}, u32[]{:S(2)}, u32[]{:S(2)}) async-start(bf16[8,320,128]{2,1,0:T(8,128)(2,1)} %copy-done.2), calls=%async_computation.1 | async-start | bytes 1310720 | tf_op jit(solution)/shard_map/all_to_all | solution.py:374
  71.0 1.5 %collective-permute-start.4 = (bf16[16,5120]{1,0:T(8,128)(2,1)}, bf16[16,5120]{1,0:T(8,128)(2,1)}, u32[]{:S(2)}, u32[]{:S(2)}) collective-permute-start(bf16[16,5120]{1,0:T(8,128)(2,1)} %copy-done.13), channel_id=1, source_target_pairs={{0,4},{4,8},{8,12},{12,16},{16,20},{20,24},{24,28},{28,0},{1,5},{5... | collective-permute-start | bytes 491528 | tf_op jit(solution)/shard_map/ppermute | solution.py:320
  72.5 0.8 collective-permute-start.5
  74.7 17.2 %collective-permute-done.4.refs_1_ = bf16[16,5120]{1,0:T(8,128)(2,1)} collective-permute-done((bf16[16,5120]{1,0:T(8,128)(2,1)}, bf16[16,5120]{1,0:T(8,128)(2,1)}, u32[]{:S(2)}, u32[]{:S(2)}) %collective-permute-start.4) | collective-permute-done | bytes 163872 | tf_op jit(solution)/shard_map/ppermute | solution.py:320
  91.9 2.0 %collective-permute-done.5.refs_6_ = bf16[16,5120]{1,0:T(8,128)(2,1)} collective-permute-done((bf16[16,5120]{1,0:T(8,128)(2,1)}, bf16[16,5120]{1,0:T(8,128)(2,1)}, u32[]{:S(2)}, u32[]{:S(2)}) %collective-permute-start.5) | collective-permute-done | bytes 163872 | tf_op jit(solution)/shard_map/ppermute | solution.py:320
  93.9 0.9 copy-done.4
  94.8 0.9 copy-done.6
  95.7 0.9 copy-done.8
  96.6 0.9 copy-done.10
  97.5 4.6 %shard_map.94 = bf16[128,5120]{1,0:T(8,128)(2,1)} custom-call(s32[1,128]{1,0:T(1,128)S(1)} %reshape.39.token_offsets_ref, s32[1,128]{1,0:T(1,128)S(1)} %reshape.40.offsets_ref, bf16[640,1280]{1,0:T(8,128)(2,1)S(1)} %copy-done, bf16[8,320,128]{2,1,0:T(8,128)(2,1)S(1)} %all-to-all-done.1.attended_ref, bf16[16,5120]{1,0:T(8,128)(2,1)S(1)} %get-tuple-element.28.refs_0_, ...), custom_call_target="tpu_custom_call" | custom-call | tf_op jit(solution)/shard_map/pallas_call | solution.py:269
  (49 shorter events, 4.0 us)
Async XLA Ops:
  0.0 9.4 %copy-start.1 = (bf16[256,1280]{1,0:T(8,128)(2,1)S(1)}, bf16[256,1280]{1,0:T(8,128)(2,1)}, u32[]{:S(2)}) copy-start(bf16[256,1280]{1,0:T(8,128)(2,1)} %tokens_ref.1) | copy-start | bytes 1966084
  3.1 6.3 %copy-start.16 = (s32[1,256]{1,0:T(1,128)S(1)}, s32[1,256]{1,0:T(1,128)}, u32[]{:S(2)}) copy-start(s32[1,256]{1,0:T(1,128)} %get-tuple-element.22) | copy-start | bytes 3076
  3.1 14.1 %copy-start.14 = (s32[2048]{0:T(1024)S(1)}, s32[2048]{0:T(1024)}, u32[]{:S(2)}) copy-start(s32[2048]{0:T(1024)} %param.11) | copy-start | bytes 24580
  3.2 14.1 %copy-start.15 = (s32[8,8]{1,0:T(8,128)S(1)}, s32[8,8]{1,0:T(8,128)}, u32[]{:S(2)}) copy-start(s32[8,8]{1,0:T(8,128)} %param.12) | copy-start | bytes 772
  3.2 50.7 %all-to-all-start = ((bf16[8,256,256]{2,1,0:T(8,128)(2,1)}), bf16[8,256,256]{2,1,0:T(8,128)(2,1)S(1)}, u32[]{:S(2)}, u32[]{:S(2)}) async-start(bf16[8,256,256]{2,1,0:T(8,128)(2,1)} %get-tuple-element.21), calls=%async_computation | async-start | bytes 2097152 | tf_op jit(solution)/shard_map/all_to_all | solution.py:310
  10.6 0.7 copy-start.12
  11.3 0.7 copy-start.13
  11.9 34.3 %collective-permute-start = (bf16[16,5120]{1,0:T(8,128)(2,1)S(1)}, bf16[16,5120]{1,0:T(8,128)(2,1)S(1)}, u32[]{:S(2)}, u32[]{:S(2)}) collective-permute-start(bf16[16,5120]{1,0:T(8,128)(2,1)S(1)} %get-tuple-element.23), channel_id=1, source_target_pairs={{0,16},{4,20},{8,24},{12,28},{16,0},{20,4},{24,8},{28,12},{1,17},{... | collective-permute-start | bytes 491528 | tf_op jit(solution)/shard_map/ppermute | solution.py:320
  14.3 35.5 %collective-permute-start.1 = (bf16[16,5120]{1,0:T(8,128)(2,1)S(1)}, bf16[16,5120]{1,0:T(8,128)(2,1)S(1)}, u32[]{:S(2)}, u32[]{:S(2)}) collective-permute-start(bf16[16,5120]{1,0:T(8,128)(2,1)S(1)} %get-tuple-element.24), channel_id=1, source_target_pairs={{0,12},{4,16},{8,20},{12,24},{16,28},{20,0},{24,4},{28,8},{1,13},{... | collective-permute-start | bytes 491528 | tf_op jit(solution)/shard_map/ppermute | solution.py:320
  14.9 35.6 %collective-permute-start.2 = (bf16[16,5120]{1,0:T(8,128)(2,1)S(1)}, bf16[16,5120]{1,0:T(8,128)(2,1)S(1)}, u32[]{:S(2)}, u32[]{:S(2)}) collective-permute-start(bf16[16,5120]{1,0:T(8,128)(2,1)S(1)} %get-tuple-element.25), channel_id=1, source_target_pairs={{0,20},{4,24},{8,28},{12,0},{16,4},{20,8},{24,12},{28,16},{1,21},{... | collective-permute-start | bytes 491528 | tf_op jit(solution)/shard_map/ppermute | solution.py:320
  17.2 36.0 %collective-permute-start.3 = (bf16[16,5120]{1,0:T(8,128)(2,1)S(1)}, bf16[16,5120]{1,0:T(8,128)(2,1)S(1)}, u32[]{:S(2)}, u32[]{:S(2)}) collective-permute-start(bf16[16,5120]{1,0:T(8,128)(2,1)S(1)} %get-tuple-element.26), channel_id=1, source_target_pairs={{0,8},{4,12},{8,16},{12,20},{16,24},{20,28},{24,0},{28,4},{1,9},{5... | collective-permute-start | bytes 491528 | tf_op jit(solution)/shard_map/ppermute | solution.py:320
  46.3 0.7 copy-start.3
  49.8 0.7 copy-start.5
  50.5 0.7 copy-start.7
  53.9 40.0 %copy-start = (bf16[640,1280]{1,0:T(8,128)(2,1)S(1)}, bf16[640,1280]{1,0:T(8,128)(2,1)}, u32[]{:S(2)}) copy-start(bf16[640,1280]{1,0:T(8,128)(2,1)} %weight_hbm.1) | copy-start | bytes 4915204
  63.8 0.8 copy-start.2
  64.6 29.2 %all-to-all-start.1 = ((bf16[8,320,128]{2,1,0:T(8,128)(2,1)}), bf16[8,320,128]{2,1,0:T(8,128)(2,1)S(1)}, u32[]{:S(2)}, u32[]{:S(2)}) async-start(bf16[8,320,128]{2,1,0:T(8,128)(2,1)} %copy-done.2), calls=%async_computation.1 | async-start | bytes 1310720 | tf_op jit(solution)/shard_map/all_to_all | solution.py:374
  71.0 20.8 %collective-permute-start.4 = (bf16[16,5120]{1,0:T(8,128)(2,1)}, bf16[16,5120]{1,0:T(8,128)(2,1)}, u32[]{:S(2)}, u32[]{:S(2)}) collective-permute-start(bf16[16,5120]{1,0:T(8,128)(2,1)} %copy-done.13), channel_id=1, source_target_pairs={{0,4},{4,8},{8,12},{12,16},{16,20},{20,24},{24,28},{28,0},{1,5},{5... | collective-permute-start | bytes 491528 | tf_op jit(solution)/shard_map/ppermute | solution.py:320
  72.5 21.3 %collective-permute-start.5 = (bf16[16,5120]{1,0:T(8,128)(2,1)}, bf16[16,5120]{1,0:T(8,128)(2,1)}, u32[]{:S(2)}, u32[]{:S(2)}) collective-permute-start(bf16[16,5120]{1,0:T(8,128)(2,1)} %copy-done.12), channel_id=1, source_target_pairs={{0,24},{4,28},{8,0},{12,4},{16,8},{20,12},{24,16},{28,20},{1,25},{... | collective-permute-start | bytes 491528 | tf_op jit(solution)/shard_map/ppermute | solution.py:320
  73.3 20.6 %collective-permute-start.6 = (bf16[16,5120]{1,0:T(8,128)(2,1)}, bf16[16,5120]{1,0:T(8,128)(2,1)}, u32[]{:S(2)}, u32[]{:S(2)}) collective-permute-start(bf16[16,5120]{1,0:T(8,128)(2,1)} %copy-done.11), channel_id=1, source_target_pairs={{0,28},{4,0},{8,4},{12,8},{16,12},{20,16},{24,20},{28,24},{1,29},{... | collective-permute-start | bytes 491528 | tf_op jit(solution)/shard_map/ppermute | solution.py:320
  93.9 0.9 copy-start.4
  94.8 0.9 copy-start.6
  95.7 0.9 copy-start.8
  96.6 0.9 copy-start.10
  (2 other events, 1.3 us)

commit v5 on v4

v5 whole, which is shorter than its diff:
```python
import functools

import jax
import jax.numpy as jnp
from jax import lax
from jax.experimental import pallas as pl
from jax.experimental.pallas import tpu as pltpu
from jax.sharding import PartitionSpec as P

HEADS = 8
SPAN = 3
NEG = -1e30
LOG2E = 1.4426950408889634
META = 16
MIB = 1024 * 1024


def vmem():
    return pl.BlockSpec(memory_space=pltpu.VMEM)


def smem():
    return pl.BlockSpec(memory_space=pltpu.SMEM)


def hbm():
    return pl.BlockSpec(memory_space=pltpu.HBM)


def limit(mib):
    return pltpu.CompilerParams(vmem_limit_bytes=mib * MIB)


def prepare_kernel(pair_rows, head_ref, owners_ref, offsets_ref, q_hbm, k_hbm, v_hbm, *refs):
    outs, (slot_ref, held, turned, pieces, load_sems, store_sems) = refs[:HEADS], refs[HEADS:]
    rows, features = q_hbm.shape
    hdim = features // HEADS
    mrows = rows // 4
    loads = [
        pltpu.make_async_copy(ref, held.at[part], load_sems.at[part])
        for part, ref in enumerate((q_hbm, k_hbm, v_hbm))
    ]
    for load in loads:
        load.start()

    owner = jnp.broadcast_to(owners_ref[...].astype(jnp.float32), (mrows, mrows))
    earlier = lax.broadcasted_iota(jnp.int32, (mrows, mrows), 0)
    later = lax.broadcasted_iota(jnp.int32, (mrows, mrows), 1)
    column = jnp.sum(jnp.where(earlier == later, owner, 0.0), axis=1, keepdims=True)
    ahead = jnp.where((owner == column) & (earlier < later), 1.0, 0.0)
    slot = owner[:1] * pair_rows + jnp.sum(ahead, axis=0, keepdims=True)
    line = lax.broadcasted_iota(jnp.int32, (META, mrows), 0)
    offset = offsets_ref[...].astype(jnp.float32)
    meta = jnp.where(line == 0, slot, jnp.where(line == 1, offset, 0.0))
    row = lax.broadcasted_iota(jnp.int32, (mrows, rows), 0)
    patch = lax.broadcasted_iota(jnp.int32, (mrows, rows), 1)
    spread = jnp.where(patch // 4 == row, 1.0, 0.0).astype(jnp.bfloat16)
    meta = jnp.dot(meta.astype(jnp.bfloat16), spread, preferred_element_type=jnp.float32)
    slot_ref[...] = meta[:1].astype(jnp.int32)
    meta = meta.astype(jnp.bfloat16)

    for part, load in enumerate(loads):
        load.wait()
        turned[part] = held[part].T
    stores = []
    for d in range(HEADS):
        start = pl.multiple_of(head_ref[d] * hdim, 16)
        for part in range(3):
            pieces[d, part * hdim : (part + 1) * hdim, :] = turned[part, pl.ds(start, hdim), :]
        pieces[d, 3 * hdim :, :] = meta
        stores.append(pltpu.make_async_copy(pieces.at[d], outs[d], store_sems.at[d]))
        stores[d].start()
    for store in stores:
        store.wait()


def prepare(head, owners, offsets, queries, keys, values, pair_rows):
    rows, features = queries.shape
    lines = 3 * features // HEADS + META
    piece = jax.ShapeDtypeStruct((lines, rows), queries.dtype)
    *pieces, slot = pl.pallas_call(
        functools.partial(prepare_kernel, pair_rows),
        out_shape=[piece] * HEADS + [jax.ShapeDtypeStruct((1, rows), jnp.int32)],
        in_specs=[smem()] + [vmem()] * 2 + [hbm()] * 3,
        out_specs=[hbm()] * HEADS + [vmem()],
        scratch_shapes=[
            pltpu.VMEM((3, rows, features), queries.dtype),
            pltpu.VMEM((3, features, rows), queries.dtype),
            pltpu.VMEM((HEADS, lines, rows), queries.dtype),
            pltpu.SemaphoreType.DMA((3,)),
            pltpu.SemaphoreType.DMA((HEADS,)),
        ],
        compiler_params=limit(16),
    )(head, owners, offsets, queries, keys, values)
    return pieces, slot


def arrange_kernel(slot_ref, tokens_ref, *refs):
    *outs, held, sems = refs
    slots = outs[0].shape[0]
    rows, width = tokens_ref.shape
    tokens = tokens_ref[...]
    total = len(outs) * slots
    slot = lax.broadcasted_iota(jnp.int32, (total, rows), 0)
    quarter = lax.broadcasted_iota(jnp.int32, (1, rows), 1) % 4
    for j in range(4):
        mine = jnp.where(quarter == j, slot_ref[...], -1) == slot
        pick = jnp.where(mine, 1.0, 0.0).astype(jnp.bfloat16)
        held[:, j * width : (j + 1) * width] = jnp.dot(
            pick, tokens, preferred_element_type=jnp.float32
        ).astype(jnp.bfloat16)
    stores = [
        pltpu.make_async_copy(held.at[pl.ds(d * slots, slots)], out, sems.at[d])
        for d, out in enumerate(outs)
    ]
    for store in stores:
        store.start()
    for store in stores:
        store.wait()


def arrange(slot_of_patch, tokens, pieces, slots):
    rows, width = tokens.shape
    return pl.pallas_call(
        arrange_kernel,
        out_shape=[jax.ShapeDtypeStruct((slots // pieces, 4 * width), jnp.bfloat16)] * pieces,
        in_specs=[vmem()] * 2,
        out_specs=[hbm()] * pieces,
        scratch_shapes=[
            pltpu.VMEM((slots, 4 * width), jnp.bfloat16),
            pltpu.SemaphoreType.DMA((pieces,)),
        ],
        compiler_params=limit(16),
    )(slot_of_patch, tokens)


def attention_kernel(halo, pair_rows, source_ref, turn_ref, low_ref, count_ref, seg_ref, *refs):
    pieces, refs = refs[:HEADS], refs[HEADS:]
    if halo:
        below_ref, above_ref, *refs = refs
    outs, (x_s, key_s, value_s, seg_s, picked_s, sent_s, load_sems, store_sems) = (
        refs[:HEADS],
        refs[HEADS:],
    )
    blocks, lines, rows = x_s.shape
    triple = lines - META
    hdim = triple // 3
    slots = outs[0].shape[1]
    base = SPAN if halo else 0
    factor = LOG2E / (hdim**0.5)
    loads = [
        pltpu.make_async_copy(pieces[d], x_s.at[source_ref[d]], load_sems.at[d])
        for d in range(HEADS)
    ]
    for load in loads:
        load.start()
    for b in range(blocks + 2 * base):
        seg_s[b] = jnp.broadcast_to(seg_ref[b], (128, rows)).T
    for load in loads:
        load.wait()

    for b in range(blocks + 2 * base):
        if b < base:
            key_s[b] = below_ref[b, :hdim, :].T
            value_s[b] = below_ref[b, hdim:, :]
        elif b >= base + blocks:
            key_s[b] = above_ref[b - base - blocks, :hdim, :].T
            value_s[b] = above_ref[b - base - blocks, hdim:, :]
        else:
            key_s[b] = x_s[b - base, hdim : 2 * hdim, :].T
            value_s[b] = x_s[b - base, 2 * hdim : triple, :]

    slot = lax.broadcasted_iota(jnp.int32, (slots, rows), 0)
    quarter = lax.broadcasted_iota(jnp.int32, (1, rows), 1) % 4

    def one_block(i, carry):
        low = low_ref[i]
        count = count_ref[i]
        query = x_s[i, :hdim, :]
        query_seg = seg_ref[i + base]
        place = x_s[i, triple:, :].astype(jnp.float32)[:1].astype(jnp.int32) + i * pair_rows
        place = jnp.where(place >= slots, place - slots, place)

        for size in range(1, 2 * SPAN + 2):

            @pl.when(count == size)
            def _():
                key = key_s[pl.ds(low, size)].reshape(size * rows, hdim)
                scores = jnp.dot(key, query, preferred_element_type=jnp.float32)
                key_seg = seg_s[pl.ds(low, size)].reshape(size * rows, 128)
                key_seg = jnp.concatenate([key_seg] * (rows // 128), axis=1)
                scores = jnp.where(key_seg == query_seg, scores, NEG)
                peak = jnp.max(scores, axis=0, keepdims=True)
                weights = jnp.exp2((scores - peak) * factor)
                total = jnp.sum(weights, axis=0, keepdims=True)
                weights = weights.astype(jnp.bfloat16)
                mixed = jnp.zeros((hdim, rows), jnp.float32)
                for b in range(size):
                    mixed += jnp.dot(
                        value_s[low + b],
                        weights[b * rows : (b + 1) * rows],
                        preferred_element_type=jnp.float32,
                    )
                attended = (mixed / total).astype(jnp.bfloat16)
                for j in range(4):
                    mine = jnp.where(quarter == j, place, -1) == slot
                    pick = jnp.where(mine, 1.0, 0.0).astype(jnp.bfloat16)
                    picked_s[i, j * hdim : (j + 1) * hdim, :] = lax.dot_general(
                        attended,
                        pick,
                        (((1,), (1,)), ((), ())),
                        preferred_element_type=jnp.float32,
                    )

        return carry

    lax.fori_loop(0, blocks, one_block, 0)

    step = 32
    group = lax.broadcasted_iota(jnp.int32, (step, slots), 1) // pair_rows
    group = (group - turn_ref[0] + slots) % blocks
    for line in range(0, 4 * hdim, step):
        chosen = [picked_s[b, line : line + step, :] for b in range(blocks)]
        shift = 1
        while shift < blocks:
            moved = (group & shift) > 0
            chosen = [
                jnp.where(moved, chosen[(b + shift) % blocks], chosen[b]) for b in range(blocks)
            ]
            shift *= 2
        for d in range(blocks):
            sent_s[d, line : line + step, :] = chosen[-d % blocks].astype(sent_s.dtype)
    stores = [
        pltpu.make_async_copy(sent_s.at[d], outs[d], store_sems.at[d]) for d in range(HEADS)
    ]
    for store in stores:
        store.start()
    for store in stores:
        store.wait()


def attention(source, turn, low, count, segs, pieces, halos, slots, pair_rows):
    lines, rows = pieces[0].shape
    hdim = (lines - META) // 3
    extended = segs.shape[0]
    out = jax.ShapeDtypeStruct((4 * hdim, slots), jnp.bfloat16)
    return pl.pallas_call(
        functools.partial(attention_kernel, bool(halos), pair_rows),
        out_shape=[out] * HEADS,
        in_specs=[smem()] * 4 + [vmem()] + [hbm()] * HEADS + [vmem()] * len(halos),
        out_specs=[hbm()] * HEADS,
        scratch_shapes=[
            pltpu.VMEM((HEADS, lines, rows), jnp.bfloat16),
            pltpu.VMEM((extended, rows, hdim), jnp.bfloat16),
            pltpu.VMEM((extended, hdim, rows), jnp.bfloat16),
            pltpu.VMEM((extended, rows, 128), jnp.float32),
            pltpu.VMEM((HEADS, 4 * hdim, slots), jnp.float32),
            pltpu.VMEM((HEADS, 4 * hdim, slots), jnp.bfloat16),
            pltpu.SemaphoreType.DMA((HEADS,)),
            pltpu.SemaphoreType.DMA((HEADS,)),
        ],
        compiler_params=limit(24),
        cost_estimate=pl.CostEstimate(
            flops=8_000_000_000, bytes_accessed=8_000_000, transcendentals=3_000_000
        ),
    )(source, turn, low, count, segs, *pieces, *halos)


def finish_kernel(ring, source_ref, token_offsets_ref, offsets_ref, weight_hbm, *refs):
    *refs, out_hbm, weight, attended_s, tokens_s, held, weight_sems, att_sems, token_sems, sems = refs
    if ring:
        attended_refs, token_refs = refs[:HEADS], refs[HEADS:]
    else:
        attended_refs, token_refs = refs[:1], refs[1:]
    capacity, merged = out_hbm.shape
    groups, lanes = offsets_ref.shape
    width = merged // 4
    hdim = attended_s.shape[1] // 4
    slots = tokens_s.shape[0] // len(token_refs)

    attended_loads, weight_loads, token_loads = [], [], []
    if ring:
        for d, ref in enumerate(attended_refs):
            attended_loads.append(pltpu.make_async_copy(ref, attended_s.at[d], att_sems.at[d]))
    else:
        attended_loads.append(
            pltpu.make_async_copy(attended_refs[0], attended_s, att_sems.at[0])
        )
    for h in range(HEADS):
        head = pl.multiple_of((source_ref[h] if ring else h) * hdim, 16)
        weight_loads.append(
            pltpu.make_async_copy(
                weight_hbm.at[pl.ds(head, hdim)],
                weight.at[pl.ds(h * hdim, hdim)],
                weight_sems.at[h],
            )
        )
    for d, ref in enumerate(token_refs):
        token_loads.append(
            pltpu.make_async_copy(ref, tokens_s.at[pl.ds(d * slots, slots)], token_sems.at[d])
        )
    for load in attended_loads + weight_loads + token_loads:
        load.start()

    def pick(offsets):
        row = lax.broadcasted_iota(jnp.int32, (capacity, offsets.shape[1]), 0)
        return jnp.where(offsets == row, 1.0, 0.0).astype(jnp.bfloat16)

    token_pick = pick(token_offsets_ref[...])
    picks = [pick(offsets_ref[g : g + 1, :]) for g in range(groups)]
    for load in attended_loads:
        load.wait()
    placed = []
    for j in range(4):
        attended = jnp.zeros((capacity, HEADS * hdim), jnp.float32)
        for g in range(groups):
            turned = jnp.concatenate(
                [
                    attended_s[g * HEADS + h, j * hdim : (j + 1) * hdim, :]
                    for h in range(HEADS)
                ],
                axis=0,
            )
            attended += lax.dot_general(
                picks[g], turned, (((1,), (1,)), ((), ())), preferred_element_type=jnp.float32
            )
        placed.append(attended.astype(jnp.bfloat16))
    for load in weight_loads + token_loads:
        load.wait()
    stores = []
    for j in range(4):
        columns = slice(j * width, (j + 1) * width)
        hidden = jnp.dot(
            token_pick, tokens_s[:, columns], preferred_element_type=jnp.float32
        ) + jnp.dot(placed[j], weight[...], preferred_element_type=jnp.float32)
        held[j] = hidden.astype(jnp.bfloat16)
        stores.append(pltpu.make_async_copy(held.at[j], out_hbm.at[:, columns], sems.at[j]))
        stores[j].start()
    for store in stores:
        store.wait()


def finish(source, token_offsets, offsets, out_weight, attended, tokens, capacity):
    ring = len(attended) == HEADS
    merged = tokens[0].shape[1]
    features, width = out_weight.shape
    shape = (HEADS, *attended[0].shape) if ring else attended[0].shape
    return pl.pallas_call(
        functools.partial(finish_kernel, ring),
        out_shape=jax.ShapeDtypeStruct((capacity, merged), jnp.bfloat16),
        in_specs=[smem()] + [vmem()] * 2 + [hbm()] * (1 + len(attended) + len(tokens)),
        out_specs=hbm(),
        scratch_shapes=[
            pltpu.VMEM((features, width), jnp.bfloat16),
            pltpu.VMEM(shape, jnp.bfloat16),
            pltpu.VMEM((len(tokens) * tokens[0].shape[0], merged), jnp.bfloat16),
            pltpu.VMEM((4, capacity, width), jnp.bfloat16),
            pltpu.SemaphoreType.DMA((HEADS,)),
            pltpu.SemaphoreType.DMA((len(attended),)),
            pltpu.SemaphoreType.DMA((len(tokens),)),
            pltpu.SemaphoreType.DMA((4,)),
        ],
        compiler_params=limit(40),
    )(source, token_offsets, offsets, out_weight, *attended, *tokens)


FAR_FIRST = (4, 5, 3, 2, 6, 1, 7)
BESIDE_INPUTS = (4, 5)
BESIDE_ATTENTION = (3, 2, 6)


def per_device(segment_ids, block_mask, queries, keys, values, tokens, out_weight, owners, offsets):
    rows, features = queries.shape
    hdim = features // HEADS
    nblocks = lax.axis_size("blk")
    block_index = lax.axis_index("blk")
    ngroups = nblocks // HEADS
    ring = ngroups == 1
    first = block_index // HEADS * HEADS
    groups = [[g * HEADS + h for h in range(HEADS)] for g in range(ngroups)]
    exchange = functools.partial(
        lax.all_to_all, axis_name="blk", split_axis=0, concat_axis=0, tiled=True
    )

    def send(block, distance):
        route = [(i, (i + distance) % nblocks) for i in range(nblocks)]
        return lax.ppermute(block, "blk", route)

    mrows = rows // 4
    capacity = 2 * mrows
    pair_rows = max(2, 2 * mrows // nblocks)
    slots = nblocks * pair_rows
    assert slots <= 256

    steps = jnp.arange(HEADS)
    turn = block_index if ring else 0
    head = (turn + steps) % HEADS
    source = (turn - steps) % HEADS if ring else steps

    split, own_slots = prepare(
        head, owners[None, :], offsets[None, :], queries, keys, values, pair_rows
    )
    if ring:
        pieces = [split[0]] + [None] * (HEADS - 1)
        for d in FAR_FIRST:
            pieces[d] = send(split[d], d)
        own_slots = (own_slots - block_index * pair_rows) % slots
        outgoing = arrange(own_slots, tokens, nblocks, slots)
        arrived_tokens = [outgoing[0]] + [None] * (nblocks - 1)
        for d in BESIDE_INPUTS:
            arrived_tokens[d] = send(outgoing[d], d)
        held = lax.optimization_barrier(
            (pieces, [arrived_tokens[d] for d in BESIDE_INPUTS], list(outgoing))
        )
        pieces, outgoing = held[0], held[2]
        for d, block in zip(BESIDE_INPUTS, held[1]):
            arrived_tokens[d] = block
        for d in BESIDE_ATTENTION:
            arrived_tokens[d] = send(outgoing[d], d)
        x = jnp.stack([piece[3 * hdim :, ::4] for piece in pieces])
        meta = x[:, :2].astype(jnp.int32)
        all_slots, all_offsets = meta[:, 0], meta[:, 1]
        wanted = block_index * pair_rows + jnp.arange(pair_rows)
        here = all_slots[..., None] == wanted
        token_offsets = capacity + jnp.sum(
            jnp.where(here, all_offsets[..., None] - capacity, 0), axis=1
        )
        lane_offsets = token_offsets[(2 * block_index - steps) % HEADS]
    else:
        x = exchange(jnp.stack(split), axis_index_groups=groups)
        pieces = list(x)
        outgoing = arrange(own_slots, tokens, 1, slots)
        arrived_tokens = [exchange(outgoing[0])]
        match = own_slots[0, ::4, None] == jnp.arange(slots)
        outgoing_offsets = capacity + jnp.sum(
            jnp.where(match, offsets[:, None] - capacity, 0), axis=0
        )
        lane_offsets = token_offsets = exchange(outgoing_offsets.reshape(nblocks, pair_rows))

    segs = segment_ids.reshape(nblocks, 1, rows)
    base = 0
    halos = ()
    if not ring:
        base = SPAN
        up = [(i, i + HEADS) for i in range(nblocks - HEADS)]
        down = [(i + HEADS, i) for i in range(nblocks - HEADS)]
        halos = (
            lax.ppermute(x[HEADS - SPAN :, hdim : 3 * hdim], "blk", up),
            lax.ppermute(x[:SPAN, hdim : 3 * hdim], "blk", down),
        )
        segs = jnp.pad(segs, ((SPAN, SPAN), (0, 0), (0, 0)), constant_values=-1)
        segs = lax.dynamic_slice_in_dim(segs, first, HEADS + 2 * SPAN, 0)
    segs = segs.astype(jnp.float32)

    mask = lax.dynamic_slice_in_dim(block_mask, first, HEADS, 0)
    block = first + jnp.arange(HEADS)[:, None]
    other = jnp.arange(nblocks)[None, :]
    present = (mask > 0) & (jnp.abs(block - other) <= SPAN)
    low = jnp.min(jnp.where(present, other, nblocks), axis=1) - first + base
    count = jnp.sum(present.astype(jnp.int32), axis=1)

    turn = jnp.reshape(turn, (1,)).astype(jnp.int32)
    sent = attention(source, turn, low, count, segs, pieces, halos, slots, pair_rows)
    if ring:
        held = lax.optimization_barrier((sent, [arrived_tokens[d] for d in BESIDE_ATTENTION]))
        sent = held[0]
        for d, block in zip(BESIDE_ATTENTION, held[1]):
            arrived_tokens[d] = block
        arrived = [sent[0]] + [None] * (HEADS - 1)
        for d in FAR_FIRST:
            arrived[d] = send(sent[d], d)
        for d in FAR_FIRST:
            if arrived_tokens[d] is None:
                arrived_tokens[d] = send(outgoing[d], d)
    else:
        sent = jnp.stack([jnp.roll(sent[o], -o * pair_rows, axis=1) for o in range(HEADS)])
        sent = sent.reshape(HEADS, 4 * hdim, ngroups, HEADS * pair_rows)
        sent = jnp.transpose(sent, (2, 0, 1, 3)).reshape(nblocks, 4 * hdim, HEADS * pair_rows)
        arrived = [exchange(sent)]
    return finish(
        source,
        token_offsets.reshape(1, slots),
        lane_offsets.reshape(ngroups, HEADS * pair_rows),
        out_weight,
        arrived,
        arrived_tokens,
        capacity,
    )


def solution(mesh):
    placed = (
        P("rep"),
        P("rep", None),
        P(("rep", "blk"), None),
        P(("rep", "blk"), None),
        P(("rep", "blk"), None),
        P(("rep", "blk"), None),
        P(),
        P(("rep", "blk")),
        P(("rep", "blk")),
    )
    return jax.shard_map(
        per_device, mesh=mesh, in_specs=placed, out_specs=P(("rep", "blk"), None), check_vma=False
    )
```

time: 103 us -> 105 us (1.019)
  waiting for transfers between devices: 52.9 us -> 29.2 us
  starting transfers between devices: 20.8 us -> 33.3 us
  Pallas kernels: 18.2 us -> 25.1 us
  local copies, waits for them, and re-layouts: 9.53 us -> 14.4 us
    ppermute x7 -> x21, starting transfers between devices: 8.13 us -> 33.3 us  [send(): return lax.ppermute(block, 'blk', route)]
    ppermute x7 -> x21, waiting for transfers between devices: 52.9 us -> 29.2 us  [send(): return lax.ppermute(block, 'blk', route)]
    all_to_all x2 -> x0, starting transfers between devices: 12.7 us -> none  [the longest x1 6.42 us: per_device(): arrived = exchange(sent)]
    pallas_call x2, Pallas kernels: 7.73 us -> 11.4 us  [the longest x1 8.35 us: finish(): pl.pallas_call(functools.partial(finish_kernel, ring), out_shape=jax.Shap...]
    unnamed x34 -> x43, local copies, waits for them, and re-layouts: 9.13 us -> 12.5 us
    pallas_call x1, Pallas kernels: 9.9 us -> 11.8 us  [attention(): pl.pallas_call(functools.partial(attention_kernel, bool(halos), pair_rows...]
    pallas_call x1, Pallas kernels: 0.52 us -> 1.94 us  [arrange(): pl.pallas_call(arrange_kernel, out_shape=[jax.ShapeDtypeStruct((slots //...]
  transfers between devices with their start and end apart: 9 -> 21, of which waited for: 5 -> 10; matrix products, arithmetic and copies ran while one was open for 1% -> 2% of each run, Pallas kernels for 1% -> 13%
where the time goes in v5:
time: 105 us; the launch traced here: 104 us
  starting transfers between devices  33.3 us (32%)
  waiting for transfers between devices  29.2 us (28%)
  Pallas kernels  25.1 us (24%)
  local copies, waits for them, and re-layouts  14.4 us (14%)
  other arithmetic  1.27 us (1%)
    ppermute x21, starting transfers between devices, send(): return lax.ppermute(block, 'blk', route)  33.3 us
    ppermute x21, waiting for transfers between devices, send(): return lax.ppermute(block, 'blk', route)  29.2 us
    unnamed x43, local copies, waits for them, and re-layouts  12.5 us
    pallas_call x1, Pallas kernels, attention(): pl.pallas_call(functools.partial(attention_kernel, bool(halos), pair_rows...  11.8 us
    pallas_call x1, Pallas kernels, finish(): pl.pallas_call(functools.partial(finish_kernel, ring), out_shape=jax.Shap...  8.35 us
    pallas_call x1, Pallas kernels, prepare(): pl.pallas_call(functools.partial(prepare_kernel, pair_rows), out_shape=[p...  3.04 us
  transfers between devices with their start and end apart: 21, of which 10 were waited for; matrix products, arithmetic and copies ran while one was open for 2% of the time, Pallas kernels for 13%

profile of v5, /device:TPU:14, one launch (start us, length us, event | category | flops | bytes accessed | tf_op | source)
XLA Modules:
  0.0 103.5 jit_solution(1729411723203785886)
XLA Ops:
  4.2 3.0 %shard_map.91 = (bf16[256,256]{1,0:T(8,128)(2,1)S(1)}, bf16[256,256]{1,0:T(8,128)(2,1)S(1)}, bf16[256,256]{1,0:T(8,128)(2,1)S(1)}, bf16[256,256]{1,0:T(8,128)(2,...) custom-call(s32[8]{0:T(128)S(1)} %and_select_fusion.2.head_ref, ...), custom_call_target="tpu_custom_call" | custom-call | tf_op jit(solution)/shard_map/pallas_call | solution.py:81
  7.3 1.6 %collective-permute-start = (bf16[256,256]{1,0:T(8,128)(2,1)S(1)}, bf16[256,256]{1,0:T(8,128)(2,1)S(1)}, u32[]{:S(2)}, u32[]{:S(2)}) collective-permute-start(bf16[256,256]{1,0:T(8,128)(2,1)S(1)} %get-tuple-element.57), channel_id=1, source_target_pairs={{0,4},{4,8},{8,12},{12,16},{16,20},{20,24},{24,28},{28,0},{1,5},{5... | collective-permute-start | bytes 393224 | tf_op jit(solution)/shard_map/ppermute | solution.py:387
  8.9 1.6 %collective-permute-start.1 = (bf16[256,256]{1,0:T(8,128)(2,1)S(1)}, bf16[256,256]{1,0:T(8,128)(2,1)S(1)}, u32[]{:S(2)}, u32[]{:S(2)}) collective-permute-start(bf16[256,256]{1,0:T(8,128)(2,1)S(1)} %get-tuple-element.58), channel_id=1, source_target_pairs={{0,8},{4,12},{8,16},{12,20},{16,24},{20,28},{24,0},{28,4},{1,9},{5... | collective-permute-start | bytes 393224 | tf_op jit(solution)/shard_map/ppermute | solution.py:387
  11.6 1.7 %collective-permute-start.3 = (bf16[256,256]{1,0:T(8,128)(2,1)S(1)}, bf16[256,256]{1,0:T(8,128)(2,1)S(1)}, u32[]{:S(2)}, u32[]{:S(2)}) collective-permute-start(bf16[256,256]{1,0:T(8,128)(2,1)S(1)} %get-tuple-element.60), channel_id=1, source_target_pairs={{0,16},{4,20},{8,24},{12,28},{16,0},{20,4},{24,8},{28,12},{1,17},{... | collective-permute-start | bytes 393224 | tf_op jit(solution)/shard_map/ppermute | solution.py:387
  13.3 1.3 %collective-permute-start.4 = (bf16[256,256]{1,0:T(8,128)(2,1)S(1)}, bf16[256,256]{1,0:T(8,128)(2,1)S(1)}, u32[]{:S(2)}, u32[]{:S(2)}) collective-permute-start(bf16[256,256]{1,0:T(8,128)(2,1)S(1)} %get-tuple-element.61), channel_id=1, source_target_pairs={{0,20},{4,24},{8,28},{12,0},{16,4},{20,8},{24,12},{28,16},{1,21},{... | collective-permute-start | bytes 393224 | tf_op jit(solution)/shard_map/ppermute | solution.py:387
  16.7 1.9 %shard_map.92 = (bf16[16,5120]{1,0:T(8,128)(2,1)S(1)}, bf16[16,5120]{1,0:T(8,128)(2,1)}, bf16[16,5120]{1,0:T(8,128)(2,1)}, bf16[16,5120]{1,0:T(8,128)(2,1)}, bf1...) custom-call(s32[1,256]{1,0:T(1,128)S(1)} %and_select_fusion.slot_ref, ...), custom_call_target="tpu_custom_call" | custom-call | tf_op jit(solution)/shard_map/pallas_call | solution.py:124
  18.6 1.4 %collective-permute-start.5 = (bf16[256,256]{1,0:T(8,128)(2,1)S(1)}, bf16[256,256]{1,0:T(8,128)(2,1)S(1)}, u32[]{:S(2)}, u32[]{:S(2)}) collective-permute-start(bf16[256,256]{1,0:T(8,128)(2,1)S(1)} %get-tuple-element.62), channel_id=1, source_target_pairs={{0,24},{4,28},{8,0},{12,4},{16,8},{20,12},{24,16},{28,20},{1,25},{... | collective-permute-start | bytes 393224 | tf_op jit(solution)/shard_map/ppermute | solution.py:387
  20.0 8.5 %collective-permute-done.1.refs_2_ = bf16[256,256]{1,0:T(8,128)(2,1)S(1)} collective-permute-done((bf16[256,256]{1,0:T(8,128)(2,1)S(1)}, bf16[256,256]{1,0:T(8,128)(2,1)S(1)}, u32[]{:S(2)}, u32[]{:S(2)}) %collective-permute-start.1) | collective-permute-done | bytes 131104 | tf_op jit(solution)/shard_map/ppermute | solution.py:387
  28.6 2.8 %collective-permute-done.2.refs_3_ = bf16[256,256]{1,0:T(8,128)(2,1)S(1)} collective-permute-done((bf16[256,256]{1,0:T(8,128)(2,1)S(1)}, bf16[256,256]{1,0:T(8,128)(2,1)S(1)}, u32[]{:S(2)}, u32[]{:S(2)}) %collective-permute-start.2) | collective-permute-done | bytes 131104 | tf_op jit(solution)/shard_map/ppermute | solution.py:387
  31.4 2.8 %collective-permute-done.3.refs_4_ = bf16[256,256]{1,0:T(8,128)(2,1)S(1)} collective-permute-done((bf16[256,256]{1,0:T(8,128)(2,1)S(1)}, bf16[256,256]{1,0:T(8,128)(2,1)S(1)}, u32[]{:S(2)}, u32[]{:S(2)}) %collective-permute-start.3) | collective-permute-done | bytes 131104 | tf_op jit(solution)/shard_map/ppermute | solution.py:387
  35.0 6.2 %collective-permute-done.6.refs_7_ = bf16[256,256]{1,0:T(8,128)(2,1)S(1)} collective-permute-done((bf16[256,256]{1,0:T(8,128)(2,1)S(1)}, bf16[256,256]{1,0:T(8,128)(2,1)S(1)}, u32[]{:S(2)}, u32[]{:S(2)}) %collective-permute-start.6) | collective-permute-done | bytes 131104 | tf_op jit(solution)/shard_map/ppermute | solution.py:387
  41.2 1.9 %collective-permute-done.8.refs_13_ = bf16[16,5120]{1,0:T(8,128)(2,1)S(1)} collective-permute-done((bf16[16,5120]{1,0:T(8,128)(2,1)S(1)}, bf16[16,5120]{1,0:T(8,128)(2,1)S(1)}, u32[]{:S(2)}, u32[]{:S(2)}) %collective-permute-start.8) | collective-permute-done | bytes 163872 | tf_op jit(solution)/shard_map/ppermute | solution.py:387
  47.1 4.8 %collective-permute-start.9 = (bf16[16,5120]{1,0:T(8,128)(2,1)}, bf16[16,5120]{1,0:T(8,128)(2,1)S(1)}, u32[]{:S(2)}, u32[]{:S(2)}) collective-permute-start(bf16[16,5120]{1,0:T(8,128)(2,1)} %get-tuple-element.89), channel_id=1, source_target_pairs={{0,12},{4,16},{8,20},{12,24},{16,28},{20,0},{24,4},{28,8},{1,13},{... | collective-permute-start | bytes 491528 | tf_op jit(solution)/shard_map/ppermute | solution.py:387
  51.9 1.5 %collective-permute-start.10 = (bf16[16,5120]{1,0:T(8,128)(2,1)}, bf16[16,5120]{1,0:T(8,128)(2,1)S(1)}, u32[]{:S(2)}, u32[]{:S(2)}) collective-permute-start(bf16[16,5120]{1,0:T(8,128)(2,1)} %get-tuple-element.90), channel_id=1, source_target_pairs={{0,8},{4,12},{8,16},{12,20},{16,24},{20,28},{24,0},{28,4},{1,9},{5... | collective-permute-start | bytes 491528 | tf_op jit(solution)/shard_map/ppermute | solution.py:387
  54.0 3.7 %collective-permute-start.19 = (bf16[16,5120]{1,0:T(8,128)(2,1)}, bf16[16,5120]{1,0:T(8,128)(2,1)S(1)}, u32[]{:S(2)}, u32[]{:S(2)}) collective-permute-start(bf16[16,5120]{1,0:T(8,128)(2,1)} %get-tuple-element.100), channel_id=1, source_target_pairs={{0,4},{4,8},{8,12},{12,16},{16,20},{20,24},{24,28},{28,0},{1,5},{5... | collective-permute-start | bytes 491528 | tf_op jit(solution)/shard_map/ppermute | solution.py:387
  62.2 11.8 %shard_map.93 = (bf16[320,128]{1,0:T(8,128)(2,1)S(1)}, bf16[320,128]{1,0:T(8,128)(2,1)S(1)}, bf16[320,128]{1,0:T(8,128)(2,1)S(1)}, bf16[320,128]{1,0:T(8,128)(2,...) custom-call(s32[8]{0:T(128)S(1)} %and_select_fusion.3.source_ref, ...), custom_call_target="tpu_custom_call" | custom-call | flops 8000000000 | bytes 8000000 | tf_op jit(solution)/shard_map/pallas_call | solution.py:247
  74.0 3.0 %collective-permute-start.12 = (bf16[320,128]{1,0:T(8,128)(2,1)S(1)}, bf16[320,128]{1,0:T(8,128)(2,1)S(1)}, u32[]{:S(2)}, u32[]{:S(2)}) collective-permute-start(bf16[320,128]{1,0:T(8,128)(2,1)S(1)} %get-tuple-element.93), channel_id=1, source_target_pairs={{0,4},{4,8},{8,12},{12,16},{16,20},{20,24},{24,28},{28,0},{1,5},{5... | collective-permute-start | bytes 245768 | tf_op jit(solution)/shard_map/ppermute | solution.py:387
  77.0 2.0 %collective-permute-start.13 = (bf16[320,128]{1,0:T(8,128)(2,1)S(1)}, bf16[320,128]{1,0:T(8,128)(2,1)S(1)}, u32[]{:S(2)}, u32[]{:S(2)}) collective-permute-start(bf16[320,128]{1,0:T(8,128)(2,1)S(1)} %get-tuple-element.94), channel_id=1, source_target_pairs={{0,8},{4,12},{8,16},{12,20},{16,24},{20,28},{24,0},{28,4},{1,9},{5... | collective-permute-start | bytes 245768 | tf_op jit(solution)/shard_map/ppermute | solution.py:387
  79.3 3.2 %collective-permute-start.14 = (bf16[320,128]{1,0:T(8,128)(2,1)}, bf16[320,128]{1,0:T(8,128)(2,1)S(1)}, u32[]{:S(2)}, u32[]{:S(2)}) collective-permute-start(bf16[320,128]{1,0:T(8,128)(2,1)} %get-tuple-element.95), channel_id=1, source_target_pairs={{0,12},{4,16},{8,20},{12,24},{16,28},{20,0},{24,4},{28,8},{1,13},{... | collective-permute-start | bytes 245768 | tf_op jit(solution)/shard_map/ppermute | solution.py:387
  82.5 2.8 %collective-permute-start.16 = (bf16[320,128]{1,0:T(8,128)(2,1)}, bf16[320,128]{1,0:T(8,128)(2,1)S(1)}, u32[]{:S(2)}, u32[]{:S(2)}) collective-permute-start(bf16[320,128]{1,0:T(8,128)(2,1)} %get-tuple-element.97), channel_id=1, source_target_pairs={{0,20},{4,24},{8,28},{12,0},{16,4},{20,8},{24,12},{28,16},{1,21},{... | collective-permute-start | bytes 245768 | tf_op jit(solution)/shard_map/ppermute | solution.py:387
  85.3 2.9 %collective-permute-start.17 = (bf16[320,128]{1,0:T(8,128)(2,1)}, bf16[320,128]{1,0:T(8,128)(2,1)S(1)}, u32[]{:S(2)}, u32[]{:S(2)}) collective-permute-start(bf16[320,128]{1,0:T(8,128)(2,1)} %get-tuple-element.98), channel_id=1, source_target_pairs={{0,24},{4,28},{8,0},{12,4},{16,8},{20,12},{24,16},{28,20},{1,25},{... | collective-permute-start | bytes 245768 | tf_op jit(solution)/shard_map/ppermute | solution.py:387
  89.1 1.7 %collective-permute-done.16.refs_5_ = bf16[320,128]{1,0:T(8,128)(2,1)S(1)} collective-permute-done((bf16[320,128]{1,0:T(8,128)(2,1)}, bf16[320,128]{1,0:T(8,128)(2,1)S(1)}, u32[]{:S(2)}, u32[]{:S(2)}) %collective-permute-start.16) | collective-permute-done | bytes 81952 | tf_op jit(solution)/shard_map/ppermute | solution.py:387
  90.8 3.3 %collective-permute-done.17.refs_6_ = bf16[320,128]{1,0:T(8,128)(2,1)S(1)} collective-permute-done((bf16[320,128]{1,0:T(8,128)(2,1)}, bf16[320,128]{1,0:T(8,128)(2,1)S(1)}, u32[]{:S(2)}, u32[]{:S(2)}) %collective-permute-start.17) | collective-permute-done | bytes 81952 | tf_op jit(solution)/shard_map/ppermute | solution.py:387
  95.2 8.3 %shard_map.94 = bf16[128,5120]{1,0:T(8,128)(2,1)} custom-call(s32[8]{0:T(128)S(1)} %and_select_fusion.3.source_ref, s32[1,128]{1,0:T(1,128)S(1)} %add.95.token_offsets_ref, s32[1,128]{1,0:T(1,128)S(1)} %reshape.101.offsets_ref, bf16[640,1280]{1,0:T(8,128)(2,1)S(1)} %copy-done, bf16[320,128]{1,0:T(8,128)(2,1)S(1)} %get-tuple-element.92.refs_0_, ...), custom_call_target="tpu_custom_call" | custom-call | tf_op jit(solution)/shard_map/pallas_call | solution.py:348
  (91 shorter events, 19.5 us)
Async XLA Ops:
  0.0 34.2 %copy-start.17 = (s32[2048]{0:T(1024)S(1)}, s32[2048]{0:T(1024)}, u32[]{:S(2)}) copy-start(s32[2048]{0:T(1024)} %param.9) | copy-start | bytes 24580
  7.3 11.3 %collective-permute-start = (bf16[256,256]{1,0:T(8,128)(2,1)S(1)}, bf16[256,256]{1,0:T(8,128)(2,1)S(1)}, u32[]{:S(2)}, u32[]{:S(2)}) collective-permute-start(bf16[256,256]{1,0:T(8,128)(2,1)S(1)} %get-tuple-element.57), channel_id=1, source_target_pairs={{0,4},{4,8},{8,12},{12,16},{16,20},{20,24},{24,28},{28,0},{1,5},{5... | collective-permute-start | bytes 393224 | tf_op jit(solution)/shard_map/ppermute | solution.py:387
  8.9 19.7 %collective-permute-start.1 = (bf16[256,256]{1,0:T(8,128)(2,1)S(1)}, bf16[256,256]{1,0:T(8,128)(2,1)S(1)}, u32[]{:S(2)}, u32[]{:S(2)}) collective-permute-start(bf16[256,256]{1,0:T(8,128)(2,1)S(1)} %get-tuple-element.58), channel_id=1, source_target_pairs={{0,8},{4,12},{8,16},{12,20},{16,24},{20,28},{24,0},{28,4},{1,9},{5... | collective-permute-start | bytes 393224 | tf_op jit(solution)/shard_map/ppermute | solution.py:387
  10.4 20.9 %collective-permute-start.2 = (bf16[256,256]{1,0:T(8,128)(2,1)S(1)}, bf16[256,256]{1,0:T(8,128)(2,1)S(1)}, u32[]{:S(2)}, u32[]{:S(2)}) collective-permute-start(bf16[256,256]{1,0:T(8,128)(2,1)S(1)} %get-tuple-element.59), channel_id=1, source_target_pairs={{0,12},{4,16},{8,20},{12,24},{16,28},{20,0},{24,4},{28,8},{1,13},{... | collective-permute-start | bytes 393224 | tf_op jit(solution)/shard_map/ppermute | solution.py:387
  11.6 22.6 %collective-permute-start.3 = (bf16[256,256]{1,0:T(8,128)(2,1)S(1)}, bf16[256,256]{1,0:T(8,128)(2,1)S(1)}, u32[]{:S(2)}, u32[]{:S(2)}) collective-permute-start(bf16[256,256]{1,0:T(8,128)(2,1)S(1)} %get-tuple-element.60), channel_id=1, source_target_pairs={{0,16},{4,20},{8,24},{12,28},{16,0},{20,4},{24,8},{28,12},{1,17},{... | collective-permute-start | bytes 393224 | tf_op jit(solution)/shard_map/ppermute | solution.py:387
  13.3 20.9 %collective-permute-start.4 = (bf16[256,256]{1,0:T(8,128)(2,1)S(1)}, bf16[256,256]{1,0:T(8,128)(2,1)S(1)}, u32[]{:S(2)}, u32[]{:S(2)}) collective-permute-start(bf16[256,256]{1,0:T(8,128)(2,1)S(1)} %get-tuple-element.61), channel_id=1, source_target_pairs={{0,20},{4,24},{8,28},{12,0},{16,4},{20,8},{24,12},{28,16},{1,21},{... | collective-permute-start | bytes 393224 | tf_op jit(solution)/shard_map/ppermute | solution.py:387
  18.6 16.4 %collective-permute-start.5 = (bf16[256,256]{1,0:T(8,128)(2,1)S(1)}, bf16[256,256]{1,0:T(8,128)(2,1)S(1)}, u32[]{:S(2)}, u32[]{:S(2)}) collective-permute-start(bf16[256,256]{1,0:T(8,128)(2,1)S(1)} %get-tuple-element.62), channel_id=1, source_target_pairs={{0,24},{4,28},{8,0},{12,4},{16,8},{20,12},{24,16},{28,20},{1,25},{... | collective-permute-start | bytes 393224 | tf_op jit(solution)/shard_map/ppermute | solution.py:387
  28.6 12.6 %collective-permute-start.6 = (bf16[256,256]{1,0:T(8,128)(2,1)S(1)}, bf16[256,256]{1,0:T(8,128)(2,1)S(1)}, u32[]{:S(2)}, u32[]{:S(2)}) collective-permute-start(bf16[256,256]{1,0:T(8,128)(2,1)S(1)} %get-tuple-element.63), channel_id=1, source_target_pairs={{0,28},{4,0},{8,4},{12,8},{16,12},{20,16},{24,20},{28,24},{1,29},{... | collective-permute-start | bytes 393224 | tf_op jit(solution)/shard_map/ppermute | solution.py:387
  31.4 15.7 %copy-start.7 = (bf16[256,256]{1,0:T(8,128)(2,1)}, bf16[256,256]{1,0:T(8,128)(2,1)S(1)}, u32[]{:S(2)}) copy-start(bf16[256,256]{1,0:T(8,128)(2,1)S(1)} %collective-permute-done.2.refs_3_) | copy-start | bytes 393220
  31.4 9.8 %collective-permute-start.7 = (bf16[16,5120]{1,0:T(8,128)(2,1)S(1)}, bf16[16,5120]{1,0:T(8,128)(2,1)S(1)}, u32[]{:S(2)}, u32[]{:S(2)}) collective-permute-start(bf16[16,5120]{1,0:T(8,128)(2,1)S(1)} %get-tuple-element.65), channel_id=1, source_target_pairs={{0,16},{4,20},{8,24},{12,28},{16,0},{20,4},{24,8},{28,12},{1,17},{... | collective-permute-start | bytes 491528 | tf_op jit(solution)/shard_map/ppermute | solution.py:387
  34.2 8.9 %collective-permute-start.8 = (bf16[16,5120]{1,0:T(8,128)(2,1)S(1)}, bf16[16,5120]{1,0:T(8,128)(2,1)S(1)}, u32[]{:S(2)}, u32[]{:S(2)}) collective-permute-start(bf16[16,5120]{1,0:T(8,128)(2,1)S(1)} %get-tuple-element.66), channel_id=1, source_target_pairs={{0,20},{4,24},{8,28},{12,0},{16,4},{20,8},{24,12},{28,16},{1,21},{... | collective-permute-start | bytes 491528 | tf_op jit(solution)/shard_map/ppermute | solution.py:387
  47.1 26.9 %collective-permute-start.9 = (bf16[16,5120]{1,0:T(8,128)(2,1)}, bf16[16,5120]{1,0:T(8,128)(2,1)S(1)}, u32[]{:S(2)}, u32[]{:S(2)}) collective-permute-start(bf16[16,5120]{1,0:T(8,128)(2,1)} %get-tuple-element.89), channel_id=1, source_target_pairs={{0,12},{4,16},{8,20},{12,24},{16,28},{20,0},{24,4},{28,8},{1,13},{... | collective-permute-start | bytes 491528 | tf_op jit(solution)/shard_map/ppermute | solution.py:387
  51.9 22.1 %collective-permute-start.10 = (bf16[16,5120]{1,0:T(8,128)(2,1)}, bf16[16,5120]{1,0:T(8,128)(2,1)S(1)}, u32[]{:S(2)}, u32[]{:S(2)}) collective-permute-start(bf16[16,5120]{1,0:T(8,128)(2,1)} %get-tuple-element.90), channel_id=1, source_target_pairs={{0,8},{4,12},{8,16},{12,20},{16,24},{20,28},{24,0},{28,4},{1,9},{5... | collective-permute-start | bytes 491528 | tf_op jit(solution)/shard_map/ppermute | solution.py:387
  53.4 20.6 %collective-permute-start.11 = (bf16[16,5120]{1,0:T(8,128)(2,1)}, bf16[16,5120]{1,0:T(8,128)(2,1)S(1)}, u32[]{:S(2)}, u32[]{:S(2)}) collective-permute-start(bf16[16,5120]{1,0:T(8,128)(2,1)} %get-tuple-element.91), channel_id=1, source_target_pairs={{0,24},{4,28},{8,0},{12,4},{16,8},{20,12},{24,16},{28,20},{1,25},{... | collective-permute-start | bytes 491528 | tf_op jit(solution)/shard_map/ppermute | solution.py:387
  54.0 28.5 %collective-permute-start.19 = (bf16[16,5120]{1,0:T(8,128)(2,1)}, bf16[16,5120]{1,0:T(8,128)(2,1)S(1)}, u32[]{:S(2)}, u32[]{:S(2)}) collective-permute-start(bf16[16,5120]{1,0:T(8,128)(2,1)} %get-tuple-element.100), channel_id=1, source_target_pairs={{0,4},{4,8},{8,12},{12,16},{16,20},{20,24},{24,28},{28,0},{1,5},{5... | collective-permute-start | bytes 491528 | tf_op jit(solution)/shard_map/ppermute | solution.py:387
  57.7 24.8 %collective-permute-start.20 = (bf16[16,5120]{1,0:T(8,128)(2,1)}, bf16[16,5120]{1,0:T(8,128)(2,1)S(1)}, u32[]{:S(2)}, u32[]{:S(2)}) collective-permute-start(bf16[16,5120]{1,0:T(8,128)(2,1)} %get-tuple-element.106), channel_id=1, source_target_pairs={{0,28},{4,0},{8,4},{12,8},{16,12},{20,16},{24,20},{28,24},{1,29},{... | collective-permute-start | bytes 491528 | tf_op jit(solution)/shard_map/ppermute | solution.py:387
  62.2 33.0 %copy-start = (bf16[640,1280]{1,0:T(8,128)(2,1)S(1)}, bf16[640,1280]{1,0:T(8,128)(2,1)}, u32[]{:S(2)}) copy-start(bf16[640,1280]{1,0:T(8,128)(2,1)} %weight_hbm.1) | copy-start | bytes 4915204
  74.0 11.3 %collective-permute-start.12 = (bf16[320,128]{1,0:T(8,128)(2,1)S(1)}, bf16[320,128]{1,0:T(8,128)(2,1)S(1)}, u32[]{:S(2)}, u32[]{:S(2)}) collective-permute-start(bf16[320,128]{1,0:T(8,128)(2,1)S(1)} %get-tuple-element.93), channel_id=1, source_target_pairs={{0,4},{4,8},{8,12},{12,16},{16,20},{20,24},{24,28},{28,0},{1,5},{5... | collective-permute-start | bytes 245768 | tf_op jit(solution)/shard_map/ppermute | solution.py:387
  77.0 11.3 %collective-permute-start.13 = (bf16[320,128]{1,0:T(8,128)(2,1)S(1)}, bf16[320,128]{1,0:T(8,128)(2,1)S(1)}, u32[]{:S(2)}, u32[]{:S(2)}) collective-permute-start(bf16[320,128]{1,0:T(8,128)(2,1)S(1)} %get-tuple-element.94), channel_id=1, source_target_pairs={{0,8},{4,12},{8,16},{12,20},{16,24},{20,28},{24,0},{28,4},{1,9},{5... | collective-permute-start | bytes 245768 | tf_op jit(solution)/shard_map/ppermute | solution.py:387
  79.3 9.7 %collective-permute-start.14 = (bf16[320,128]{1,0:T(8,128)(2,1)}, bf16[320,128]{1,0:T(8,128)(2,1)S(1)}, u32[]{:S(2)}, u32[]{:S(2)}) collective-permute-start(bf16[320,128]{1,0:T(8,128)(2,1)} %get-tuple-element.95), channel_id=1, source_target_pairs={{0,12},{4,16},{8,20},{12,24},{16,28},{20,0},{24,4},{28,8},{1,13},{... | collective-permute-start | bytes 245768 | tf_op jit(solution)/shard_map/ppermute | solution.py:387
  82.4 6.7 %collective-permute-start.15 = (bf16[320,128]{1,0:T(8,128)(2,1)}, bf16[320,128]{1,0:T(8,128)(2,1)S(1)}, u32[]{:S(2)}, u32[]{:S(2)}) collective-permute-start(bf16[320,128]{1,0:T(8,128)(2,1)} %get-tuple-element.96), channel_id=1, source_target_pairs={{0,16},{4,20},{8,24},{12,28},{16,0},{20,4},{24,8},{28,12},{1,17},{... | collective-permute-start | bytes 245768 | tf_op jit(solution)/shard_map/ppermute | solution.py:387
  82.5 8.3 %collective-permute-start.16 = (bf16[320,128]{1,0:T(8,128)(2,1)}, bf16[320,128]{1,0:T(8,128)(2,1)S(1)}, u32[]{:S(2)}, u32[]{:S(2)}) collective-permute-start(bf16[320,128]{1,0:T(8,128)(2,1)} %get-tuple-element.97), channel_id=1, source_target_pairs={{0,20},{4,24},{8,28},{12,0},{16,4},{20,8},{24,12},{28,16},{1,21},{... | collective-permute-start | bytes 245768 | tf_op jit(solution)/shard_map/ppermute | solution.py:387
  85.3 8.8 %collective-permute-start.17 = (bf16[320,128]{1,0:T(8,128)(2,1)}, bf16[320,128]{1,0:T(8,128)(2,1)S(1)}, u32[]{:S(2)}, u32[]{:S(2)}) collective-permute-start(bf16[320,128]{1,0:T(8,128)(2,1)} %get-tuple-element.98), channel_id=1, source_target_pairs={{0,24},{4,28},{8,0},{12,4},{16,8},{20,12},{24,16},{28,20},{1,25},{... | collective-permute-start | bytes 245768 | tf_op jit(solution)/shard_map/ppermute | solution.py:387
  88.2 6.9 %collective-permute-start.18 = (bf16[320,128]{1,0:T(8,128)(2,1)}, bf16[320,128]{1,0:T(8,128)(2,1)}, u32[]{:S(2)}, u32[]{:S(2)}) collective-permute-start(bf16[320,128]{1,0:T(8,128)(2,1)} %get-tuple-element.99), channel_id=1, source_target_pairs={{0,28},{4,0},{8,4},{12,8},{16,12},{20,16},{24,20},{28,24},{1,29},{... | collective-permute-start | bytes 245768 | tf_op jit(solution)/shard_map/ppermute | solution.py:387
  (15 other events, 12.5 us)

commit v6 on v1

v6 whole, which is shorter than its diff:
```python
import functools

import jax
import jax.numpy as jnp
from jax import lax
from jax.experimental import pallas as pl
from jax.experimental.pallas import tpu as pltpu
from jax.sharding import PartitionSpec as P

HEADS = 8
HALF = HEADS // 2
SPAN = 3
WINDOW = 2 * SPAN + 2
NEG = -1e30
LOG2E = 1.4426950408889634
MIB = 1024 * 1024


def vmem():
    return pl.BlockSpec(memory_space=pltpu.VMEM)


def smem():
    return pl.BlockSpec(memory_space=pltpu.SMEM)


def anywhere():
    return pl.BlockSpec(memory_space=pl.ANY)


def limit(mib):
    return pltpu.CompilerParams(vmem_limit_bytes=mib * MIB)


def prepare_kernel(
    pair_rows, half_ref, owners_ref, offsets_ref, q_hbm, k_hbm, v_hbm,
    own_q, own_kv, swap_q, swap_kv, meta_ref, held, turned, sems,
):
    rows, features = q_hbm.shape
    part = features // 2
    mrows = rows // 4
    loads = [
        pltpu.make_async_copy(ref, held.at[i], sems.at[i])
        for i, ref in enumerate((k_hbm, v_hbm, q_hbm))
    ]
    for load in loads:
        load.start()

    owner = jnp.broadcast_to(owners_ref[...].astype(jnp.float32), (mrows, mrows))
    earlier = lax.broadcasted_iota(jnp.int32, (mrows, mrows), 0)
    later = lax.broadcasted_iota(jnp.int32, (mrows, mrows), 1)
    column = jnp.sum(jnp.where(earlier == later, owner, 0.0), axis=1, keepdims=True)
    ahead = jnp.where((owner == column) & (earlier < later), 1.0, 0.0)
    slot = owner[:1] * pair_rows + jnp.sum(ahead, axis=0, keepdims=True)
    line = lax.broadcasted_iota(jnp.int32, (8, mrows), 0)
    offset = offsets_ref[...].astype(jnp.float32)
    meta = jnp.where(line == 0, slot, jnp.where(line == 1, offset, 0.0))
    row = lax.broadcasted_iota(jnp.int32, (mrows, rows), 0)
    patch = lax.broadcasted_iota(jnp.int32, (mrows, rows), 1)
    spread = jnp.where(patch // 4 == row, 1.0, 0.0).astype(jnp.bfloat16)
    meta_ref[...] = jnp.dot(
        meta.astype(jnp.bfloat16), spread, preferred_element_type=jnp.float32
    )

    mine = pl.multiple_of(half_ref[0] * part, 16)
    other = pl.multiple_of((1 - half_ref[0]) * part, 16)
    for i in range(3):
        loads[i].wait()
        turned[i] = held[i].T
        if i < 2:
            own_kv[i * part : (i + 1) * part, :] = turned[i, pl.ds(mine, part), :]
            swap_kv[i * part : (i + 1) * part, :] = turned[i, pl.ds(other, part), :]
        else:
            own_q[...] = turned[i, pl.ds(mine, part), :]
            swap_q[...] = turned[i, pl.ds(other, part), :]


def prepare(half, owners, offsets, queries, keys, values, pair_rows):
    rows, features = queries.shape
    part = features // 2
    single = jax.ShapeDtypeStruct((part, rows), queries.dtype)
    double = jax.ShapeDtypeStruct((2 * part, rows), queries.dtype)
    return pl.pallas_call(
        functools.partial(prepare_kernel, pair_rows),
        out_shape=[single, double, single, double, jax.ShapeDtypeStruct((8, rows), jnp.float32)],
        in_specs=[smem()] + [vmem()] * 2 + [anywhere()] * 3,
        out_specs=[vmem()] * 5,
        scratch_shapes=[
            pltpu.VMEM((3, rows, features), queries.dtype),
            pltpu.VMEM((3, features, rows), queries.dtype),
            pltpu.SemaphoreType.DMA((3,)),
        ],
        compiler_params=limit(60),
    )(half, owners, offsets, queries, keys, values)


def attention_kernel(place_ref, half_ref, low_ref, count_ref, seg_ref, own_q, other_q, *refs):
    blocks, refs = refs[:WINDOW], refs[WINDOW:]
    own_out, other_out, query_s, key_s, value_s, seg_s, out_s = refs
    half = half_ref[0]
    part, rows = own_q.shape
    hdim = part // HALF
    factor = LOG2E / (hdim**0.5)
    query_s[half] = own_q[...]
    query_s[1 - half] = other_q[...]
    first = jnp.minimum(low_ref[0], low_ref[1])
    last = jnp.maximum(low_ref[0] + count_ref[0], low_ref[1] + count_ref[1])
    for b in range(WINDOW):
        seg_s[b] = jnp.broadcast_to(seg_ref[b], (128, rows)).T
    for i, block in enumerate(blocks):
        place = place_ref[i]

        @pl.when((place >= first) & (place < last))
        def _(block=block, place=place):
            for h in range(HALF):
                key_s[h, place] = block[h * hdim : (h + 1) * hdim, :].T
            value_s[place] = block[part:, :]

    def one_head(i, carry):
        which = i // HALF
        h = i % HALF
        low = low_ref[which]
        count = count_ref[which]
        lines = pl.ds(pl.multiple_of(h * hdim, 16), hdim)
        query = query_s[which, lines, :]
        query_seg = seg_ref[SPAN + which]

        for size in range(1, 2 * SPAN + 2):

            @pl.when(count == size)
            def _():
                key = key_s[h, pl.ds(low, size)].reshape(size * rows, hdim)
                scores = jnp.dot(key, query, preferred_element_type=jnp.float32)
                key_seg = seg_s[pl.ds(low, size)].reshape(size * rows, 128)
                key_seg = jnp.concatenate([key_seg] * (rows // 128), axis=1)
                scores = jnp.where(key_seg == query_seg, scores, NEG)
                peak = jnp.max(scores, axis=0, keepdims=True)
                weights = jnp.exp2((scores - peak) * factor)
                total = jnp.sum(weights, axis=0, keepdims=True)
                weights = weights.astype(jnp.bfloat16)
                mixed = jnp.zeros((hdim, rows), jnp.float32)
                for b in range(size):
                    mixed += jnp.dot(
                        value_s[low + b, lines, :],
                        weights[b * rows : (b + 1) * rows],
                        preferred_element_type=jnp.float32,
                    )
                out_s[which, lines, :] = (mixed / total).astype(out_s.dtype)

        return carry

    lax.fori_loop(0, 2 * HALF, one_head, 0)
    own_out[...] = out_s[half]
    other_out[...] = out_s[1 - half]


def attention(place, half, low, count, segs, own_q, other_q, blocks):
    part, rows = own_q.shape
    hdim = part // HALF
    return pl.pallas_call(
        attention_kernel,
        out_shape=[jax.ShapeDtypeStruct((part, rows), jnp.bfloat16)] * 2,
        in_specs=[smem()] * 4 + [vmem()] * (3 + WINDOW),
        out_specs=[vmem()] * 2,
        scratch_shapes=[
            pltpu.VMEM((2, part, rows), jnp.bfloat16),
            pltpu.VMEM((HALF, WINDOW, rows, hdim), jnp.bfloat16),
            pltpu.VMEM((WINDOW, part, rows), jnp.bfloat16),
            pltpu.VMEM((WINDOW, rows, 128), jnp.float32),
            pltpu.VMEM((2, part, rows), jnp.bfloat16),
        ],
        compiler_params=limit(24),
    )(place, half, low, count, segs, own_q, other_q, *blocks)


def project_kernel(
    capacity, half_ref, meta_ref, own_ref, other_ref, weight_ref, tokens_ref, out_ref
):
    slots = out_ref.shape[0]
    rows, width = tokens_ref.shape
    part = own_ref.shape[0]
    half = half_ref[0]
    hidden = tokens_ref[...].astype(jnp.float32)
    for ref, which in ((own_ref, half), (other_ref, 1 - half)):
        hidden += lax.dot_general(
            ref[...],
            weight_ref[pl.ds(pl.multiple_of(which * part, 16), part), :],
            (((0,), (0,)), ((), ())),
            preferred_element_type=jnp.float32,
        )
    hidden = hidden.astype(jnp.bfloat16)
    slot = lax.broadcasted_iota(jnp.int32, (slots, rows), 0).astype(jnp.float32)
    quarter = lax.broadcasted_iota(jnp.int32, (1, rows), 1) % 4
    for j in range(4):
        mine = jnp.where(quarter == j, meta_ref[:1], -1.0) == slot
        if j == 0:
            offset = jnp.where(mine, meta_ref[1:2] - capacity, 0.0)
            offset = capacity + jnp.sum(offset, axis=1, keepdims=True)
            out_ref[:, 4 * width :] = jnp.broadcast_to(offset, (slots, 128)).astype(jnp.bfloat16)
        pick = jnp.where(mine, 1.0, 0.0).astype(jnp.bfloat16)
        out_ref[:, j * width : (j + 1) * width] = jnp.dot(
            pick, hidden, preferred_element_type=jnp.float32
        ).astype(jnp.bfloat16)


def project(half, meta, own, other, out_weight, tokens, slots, capacity):
    rows, width = tokens.shape
    return pl.pallas_call(
        functools.partial(project_kernel, float(capacity)),
        out_shape=jax.ShapeDtypeStruct((slots, 4 * width + 128), jnp.bfloat16),
        in_specs=[smem()] + [vmem()] * 5,
        out_specs=vmem(),
        compiler_params=limit(24),
    )(half, meta, own, other, out_weight, tokens)


def place_kernel(arrived_ref, out_hbm, held, sems):
    capacity, merged = out_hbm.shape
    slots = arrived_ref.shape[0]
    step = merged // 4
    row = lax.broadcasted_iota(jnp.int32, (slots, capacity), 1).astype(jnp.float32)
    offset = arrived_ref[:, merged : merged + 128].astype(jnp.float32)[:, :1]
    pick = jnp.where(offset == row, 1.0, 0.0).astype(jnp.bfloat16)
    stores = []
    for j in range(4):
        columns = slice(j * step, (j + 1) * step)
        held[j] = lax.dot_general(
            pick,
            arrived_ref[:, columns],
            (((0,), (0,)), ((), ())),
            preferred_element_type=jnp.float32,
        ).astype(jnp.bfloat16)
        stores.append(pltpu.make_async_copy(held.at[j], out_hbm.at[:, columns], sems.at[j]))
        stores[j].start()
    for store in stores:
        store.wait()


def place(arrived, capacity, merged):
    return pl.pallas_call(
        place_kernel,
        out_shape=jax.ShapeDtypeStruct((capacity, merged), jnp.bfloat16),
        in_specs=[vmem()],
        out_specs=anywhere(),
        scratch_shapes=[
            pltpu.VMEM((4, capacity, merged // 4), jnp.bfloat16),
            pltpu.SemaphoreType.DMA((4,)),
        ],
        compiler_params=limit(24),
    )(arrived)


def per_device(segment_ids, block_mask, queries, keys, values, tokens, out_weight, owners, offsets):
    rows = queries.shape[0]
    width = tokens.shape[1]
    nblocks = lax.axis_size("blk")
    block_index = lax.axis_index("blk")
    half = block_index % 2
    pair = block_index - half
    mrows = rows // 4
    capacity = 2 * mrows
    pair_rows = max(2, 2 * mrows // nblocks)
    slots = nblocks * pair_rows
    assert slots <= 256

    def route(step):
        return [(i, i + step(i)) for i in range(nblocks) if 0 <= i + step(i) < nblocks]

    swap = functools.partial(
        lax.ppermute, axis_name="blk", perm=route(lambda i: 1 - 2 * (i % 2))
    )
    ahead = functools.partial(
        lax.ppermute, axis_name="blk", perm=route(lambda i: 2 if i % 2 else -2)
    )
    back = functools.partial(
        lax.ppermute, axis_name="blk", perm=route(lambda i: -2 if i % 2 else 2)
    )

    halves = half[None].astype(jnp.int32)
    own_q, own_kv, swap_q, swap_kv, meta = prepare(
        halves, owners[None, :], offsets[None, :], queries, keys, values, pair_rows
    )
    other_kv = swap(swap_kv)
    ahead_own = ahead(own_kv)
    back_own = back(own_kv)
    other_q = swap(swap_q)
    back_other = back(other_kv)
    ahead_other = ahead(other_kv)
    ahead_far = ahead(ahead_own)
    back_far = back(back_other)
    blocks = (own_kv, other_kv, ahead_own, ahead_other, back_own, back_other, ahead_far, back_far)
    places = jnp.where(
        half == 0,
        jnp.array([3, 4, 5, 6, 1, 2, 7, 0], jnp.int32),
        jnp.array([4, 3, 2, 1, 6, 5, 0, 7], jnp.int32),
    )

    segs = jnp.pad(segment_ids.reshape(nblocks, 1, rows), ((SPAN, SPAN), (0, 0), (0, 0)))
    segs = lax.dynamic_slice_in_dim(segs, pair, WINDOW, 0).astype(jnp.float32)
    mask = lax.dynamic_slice_in_dim(block_mask, pair, 2, 0)
    block = pair + jnp.arange(2)[:, None]
    other = jnp.arange(nblocks)[None, :]
    present = (mask > 0) & (jnp.abs(block - other) <= SPAN)
    low = jnp.min(jnp.where(present, other, nblocks), axis=1) - pair + SPAN
    count = jnp.sum(present.astype(jnp.int32), axis=1)

    own, other = attention(places, halves, low, count, segs, own_q, other_q, blocks)
    other = swap(other)
    outgoing = project(halves, meta, own, other, out_weight, tokens, slots, capacity)
    arrived = lax.all_to_all(outgoing, "blk", split_axis=0, concat_axis=0, tiled=True)
    return place(arrived, capacity, 4 * width)


def solution(mesh):
    placed = (
        P("rep"),
        P("rep", None),
        P(("rep", "blk"), None),
        P(("rep", "blk"), None),
        P(("rep", "blk"), None),
        P(("rep", "blk"), None),
        P(),
        P(("rep", "blk")),
        P(("rep", "blk")),
    )
    return jax.shard_map(
        per_device, mesh=mesh, in_specs=placed, out_specs=P(("rep", "blk"), None), check_vma=False
    )
```

time: 105 us -> 87.3 us (0.83)
  waiting for transfers between devices: 66.3 us -> 16.8 us
  blocking collectives: 0 us -> 32.5 us
  local copies, waits for them, and re-layouts: 4.41 us -> 1.9 us
  starting transfers between devices: 18.2 us -> 19.6 us
    all_to_all x4 -> x0, waiting for transfers between devices: 66.3 us -> none  [the longest x1 29 us: per_device(): arrived = exchange(outgoing)]
    all_to_all x0 -> x1, blocking collectives: none -> 32.5 us  [per_device(): lax.all_to_all(outgoing, 'blk', split_axis=0, concat_axis=0, tiled=True)]
    ppermute x0 -> x9, starting transfers between devices: none -> 19.6 us  [the longest x1 4.39 us: per_device(): back_far = back(back_other)]
    all_to_all x4 -> x0, starting transfers between devices: 18.2 us -> none  [the longest x1 7.42 us: per_device(): x = exchange(split_heads(queries, keys, values), axis_index_groups=groups)]
    ppermute x0 -> x9, waiting for transfers between devices: none -> 16.8 us  [the longest x1 4.99 us: per_device(): other = swap(other)]
    unnamed x18 -> x10, local copies, waits for them, and re-layouts: 2.94 us -> 1.9 us
  transfers between devices with their start and end apart: 4 -> 9, of which waited for: 4 -> 5; matrix products, arithmetic and copies ran while one was open for 3% -> 3% of each run, Pallas kernels for 2% -> 0%
where the time goes in v6:
time: 87.3 us; the launch traced here: 86.9 us
  blocking collectives  32.5 us (37%)
  starting transfers between devices  19.6 us (22%)
  waiting for transfers between devices  16.8 us (19%)
  Pallas kernels  13.6 us (16%)
  other arithmetic  2.3 us (3%)
  local copies, waits for them, and re-layouts  1.9 us (2%)
    all_to_all x1, blocking collectives, per_device(): lax.all_to_all(outgoing, 'blk', split_axis=0, concat_axis=0, tiled=True)  32.5 us
    pallas_call x1, Pallas kernels, attention(): pl.pallas_call(attention_kernel, out_shape=[jax.ShapeDtypeStruct((part, r...  7.76 us
    ppermute x1, waiting for transfers between devices, per_device(): other = swap(other)  4.99 us
    ppermute x1, starting transfers between devices, per_device(): back_far = back(back_other)  4.39 us
    ppermute x1, waiting for transfers between devices, per_device(): ahead_far = ahead(ahead_own)  4.33 us
    ppermute x1, starting transfers between devices, per_device(): back_own = back(own_kv)  3.49 us
    ppermute x1, waiting for transfers between devices, per_device(): ahead_other = ahead(other_kv)  3.24 us
    ppermute x1, starting transfers between devices, per_device(): back_other = back(other_kv)  3.23 us
  transfers between devices with their start and end apart: 9, of which 5 were waited for; matrix products, arithmetic and copies ran while one was open for 3% of the time, Pallas kernels for 0%

profile of v6, /device:TPU:0, one launch (start us, length us, event | category | flops | bytes accessed | tf_op | source)
XLA Modules:
  0.0 86.9 jit_solution(7962063645905769793)
XLA Ops:
  0.0 2.9 %shard_map.109 = (bf16[320,256]{1,0:T(8,128)(2,1)}, bf16[640,256]{1,0:T(8,128)(2,1)}, bf16[320,256]{1,0:T(8,128)(2,1)}, bf16[640,256]{1,0:T(8,128)(2,1)}, f32[8,256]{1,0:T(8,128)}) custom-call(s32[1]{0:T(128)} %bitcast.half_ref, s32[1,64]{1,0:T(1,128)} %bitcast.9, s32[1,64]{1,0:T(1,128)} %bitcast.10, bf16[256,640]{1,0:T(8,128)(2,1)} %q_hbm.1, ...), custom_call_target="tpu_custom_call" | custom-call | tf_op jit(solution)/shard_map/pallas_call | solution.py:83
  2.9 3.0 %collective-permute-start.1 = (bf16[640,256]{1,0:T(8,128)(2,1)}, bf16[640,256]{1,0:T(8,128)(2,1)S(1)}, u32[]{:S(2)}, u32[]{:S(2)}) collective-permute-start(bf16[640,256]{1,0:T(8,128)(2,1)} %get-tuple-element.16), channel_id=1, source_target_pairs={{0,4},{4,0},{8,12},{12,8},{16,20},{20,16},{24,28},{28,24},{1,5},{5... | collective-permute-start | bytes 983048 | tf_op jit(solution)/shard_map/ppermute | solution.py:283
  6.0 3.5 %collective-permute-start.4 = (bf16[640,256]{1,0:T(8,128)(2,1)}, bf16[640,256]{1,0:T(8,128)(2,1)S(1)}, u32[]{:S(2)}, u32[]{:S(2)}) collective-permute-start(bf16[640,256]{1,0:T(8,128)(2,1)} %get-tuple-element.15.refs_0_), channel_id=1, source_target_pairs={{0,8},{8,16},{12,4},{16,24},{20,12},{28,20},{1,9},{9,17},{13,5},{1... | collective-permute-start | bytes 983048 | tf_op jit(solution)/shard_map/ppermute | solution.py:285
  9.5 1.3 %collective-permute-start.2 = (bf16[640,256]{1,0:T(8,128)(2,1)}, bf16[640,256]{1,0:T(8,128)(2,1)S(1)}, u32[]{:S(2)}, u32[]{:S(2)}) collective-permute-start(bf16[640,256]{1,0:T(8,128)(2,1)} %get-tuple-element.15.refs_0_), channel_id=1, source_target_pairs={{4,12},{8,0},{12,20},{16,8},{20,28},{24,16},{5,13},{9,1},{13,21},{... | collective-permute-start | bytes 983048 | tf_op jit(solution)/shard_map/ppermute | solution.py:284
  10.8 1.2 %collective-permute-start = (bf16[320,256]{1,0:T(8,128)(2,1)}, bf16[320,256]{1,0:T(8,128)(2,1)S(1)}, u32[]{:S(2)}, u32[]{:S(2)}) collective-permute-start(bf16[320,256]{1,0:T(8,128)(2,1)} %get-tuple-element.14), channel_id=1, source_target_pairs={{0,4},{4,0},{8,12},{12,8},{16,20},{20,16},{24,28},{28,24},{1,5},{5... | collective-permute-start | bytes 491528 | tf_op jit(solution)/shard_map/ppermute | solution.py:286
  12.0 2.7 %collective-permute-done.1.refs_1_ = bf16[640,256]{1,0:T(8,128)(2,1)S(1)} collective-permute-done((bf16[640,256]{1,0:T(8,128)(2,1)}, bf16[640,256]{1,0:T(8,128)(2,1)S(1)}, u32[]{:S(2)}, u32[]{:S(2)}) %collective-permute-start.1) | collective-permute-done | bytes 327712 | tf_op jit(solution)/shard_map/ppermute | solution.py:283
  14.7 3.2 %collective-permute-start.5 = (bf16[640,256]{1,0:T(8,128)(2,1)S(1)}, bf16[640,256]{1,0:T(8,128)(2,1)S(1)}, u32[]{:S(2)}, u32[]{:S(2)}) collective-permute-start(bf16[640,256]{1,0:T(8,128)(2,1)S(1)} %collective-permute-done.1.refs_1_), channel_id=1, source_target_pairs={{0,8},{8,16},{12,4},{16,24},{20,12},{28,20},{1,9},{9,17},{13,5},{1... | collective-permute-start | bytes 983048 | tf_op jit(solution)/shard_map/ppermute | solution.py:287
  18.0 0.9 %convert_reduce_fusion = (s32[2]{0:T(128)S(1)}, s32[2]{0:T(128)S(1)}) fusion(s32[2]{0:T(128)S(1)} %iota_add_fusion, s32[8,8]{1,0:T(8,128)} %param.12, s32[]{:T(128)S(6)} %select_n.28), kind=kLoop, calls=%fused_computation.3 | loop fusion | flops 140 | bytes 92 | tf_op jit(solution)/shard_map/reduce_sum | solution.py:305
  18.9 0.7 broadcast_select_fusion.place_ref
  19.5 1.3 %collective-permute-start.3 = (bf16[640,256]{1,0:T(8,128)(2,1)S(1)}, bf16[640,256]{1,0:T(8,128)(2,1)S(1)}, u32[]{:S(2)}, u32[]{:S(2)}) collective-permute-start(bf16[640,256]{1,0:T(8,128)(2,1)S(1)} %collective-permute-done.1.refs_1_), channel_id=1, source_target_pairs={{4,12},{8,0},{12,20},{16,8},{20,28},{24,16},{5,13},{9,1},{13,21},{... | collective-permute-start | bytes 983048 | tf_op jit(solution)/shard_map/ppermute | solution.py:288
  20.8 1.3 %collective-permute-start.6 = (bf16[640,256]{1,0:T(8,128)(2,1)S(1)}, bf16[640,256]{1,0:T(8,128)(2,1)S(1)}, u32[]{:S(2)}, u32[]{:S(2)}) collective-permute-start(bf16[640,256]{1,0:T(8,128)(2,1)S(1)} %collective-permute-done.2.refs_2_), channel_id=1, source_target_pairs={{4,12},{8,0},{12,20},{16,8},{20,28},{24,16},{5,13},{9,1},{13,21},{... | collective-permute-start | bytes 983048 | tf_op jit(solution)/shard_map/ppermute | solution.py:289
  22.1 1.5 %collective-permute-done.5.refs_5_ = bf16[640,256]{1,0:T(8,128)(2,1)S(1)} collective-permute-done((bf16[640,256]{1,0:T(8,128)(2,1)S(1)}, bf16[640,256]{1,0:T(8,128)(2,1)S(1)}, u32[]{:S(2)}, u32[]{:S(2)}) %collective-permute-start.5) | collective-permute-done | bytes 327712 | tf_op jit(solution)/shard_map/ppermute | solution.py:287
  23.7 4.4 %collective-permute-start.7 = (bf16[640,256]{1,0:T(8,128)(2,1)S(1)}, bf16[640,256]{1,0:T(8,128)(2,1)S(1)}, u32[]{:S(2)}, u32[]{:S(2)}) collective-permute-start(bf16[640,256]{1,0:T(8,128)(2,1)S(1)} %collective-permute-done.5.refs_5_), channel_id=1, source_target_pairs={{0,8},{8,16},{12,4},{16,24},{20,12},{28,20},{1,9},{9,17},{13,5},{1... | collective-permute-start | bytes 983048 | tf_op jit(solution)/shard_map/ppermute | solution.py:290
  28.1 0.7 fusion.seg_ref
  28.8 3.2 %collective-permute-done.3.refs_3_ = bf16[640,256]{1,0:T(8,128)(2,1)S(1)} collective-permute-done((bf16[640,256]{1,0:T(8,128)(2,1)S(1)}, bf16[640,256]{1,0:T(8,128)(2,1)S(1)}, u32[]{:S(2)}, u32[]{:S(2)}) %collective-permute-start.3) | collective-permute-done | bytes 327712 | tf_op jit(solution)/shard_map/ppermute | solution.py:288
  32.1 4.3 %collective-permute-done.6.refs_6_ = bf16[640,256]{1,0:T(8,128)(2,1)S(1)} collective-permute-done((bf16[640,256]{1,0:T(8,128)(2,1)S(1)}, bf16[640,256]{1,0:T(8,128)(2,1)S(1)}, u32[]{:S(2)}, u32[]{:S(2)}) %collective-permute-start.6) | collective-permute-done | bytes 327712 | tf_op jit(solution)/shard_map/ppermute | solution.py:289
  36.4 1.0 %copy-done.2 = bf16[640,256]{1,0:T(8,128)(2,1)S(1)} copy-done((bf16[640,256]{1,0:T(8,128)(2,1)S(1)}, bf16[640,256]{1,0:T(8,128)(2,1)}, u32[]{:S(2)}) %copy-start.2) | copy-done | bytes 327704
  37.4 0.9 %copy-done.3 = bf16[320,256]{1,0:T(8,128)(2,1)S(1)} copy-done((bf16[320,256]{1,0:T(8,128)(2,1)S(1)}, bf16[320,256]{1,0:T(8,128)(2,1)}, u32[]{:S(2)}) %copy-start.3) | copy-done | bytes 163864
  38.3 7.8 %shard_map.110 = (bf16[320,256]{1,0:T(8,128)(2,1)S(1)}, bf16[320,256]{1,0:T(8,128)(2,1)S(1)}) custom-call(s32[8]{0:T(128)S(1)} %broadcast_select_fusion.place_ref, s32[1]{0:T(128)} %bitcast.half_ref, s32[2]{0:T(128)S(1)} %subtract_add_fusion.low_ref, s32[2]{0:T(128)S(1)} %get-tuple-element.19.count_ref, f32[8,1,256]{2,1,0:T(1,128)S(1)} %fusion.seg_ref, ...), custom_call_target="tpu_custom_call" | custom-call | tf_op jit(solution)/shard_map/pallas_call | solution.py:160
  46.1 0.4 collective-permute-start.8
  46.5 5.0 %collective-permute-done.8.other_ref = bf16[320,256]{1,0:T(8,128)(2,1)S(1)} collective-permute-done((bf16[320,256]{1,0:T(8,128)(2,1)S(1)}, bf16[320,256]{1,0:T(8,128)(2,1)S(1)}, u32[]{:S(2)}, u32[]{:S(2)}) %collective-permute-start.8) | collective-permute-done | bytes 163872 | tf_op jit(solution)/shard_map/ppermute | solution.py:308
  51.5 1.5 %shard_map.111 = bf16[128,5248]{1,0:T(8,128)(2,1)S(1)} custom-call(s32[1]{0:T(128)} %bitcast.half_ref, f32[8,256]{1,0:T(8,128)S(1)} %copy-done.4, bf16[320,256]{1,0:T(8,128)(2,1)S(1)} %get-tuple-element.17.own_ref, bf16[320,256]{1,0:T(8,128)(2,1)S(1)} %collective-permute-done.8.other_ref, bf16[640,1280]{1,0:T(8,128)(2,1)S(1)} %copy-done, ...), custom_call_target="tpu_custom_call" | custom-call | tf_op jit(solution)/shard_map/pallas_call | solution.py:208
  53.0 32.5 %all_to_all.11 = bf16[8,16,5248]{2,1,0:T(8,128)(2,1)S(1)} all-to-all(bf16[8,16,5248]{2,1,0:T(8,128)(2,1)S(1)} %bitcast.6), channel_id=1, replica_groups=mesh['blk'=8,'rep'=4] {'blk'}, dimensions={0} | all-to-all | bytes 2686976 | tf_op jit(solution)/shard_map/all_to_all | solution.py:310
  85.4 1.4 %shard_map.112 = bf16[128,5120]{1,0:T(8,128)(2,1)} custom-call(bf16[128,5248]{1,0:T(8,128)(2,1)S(1)} %bitcast.7), custom_call_target="tpu_custom_call" | custom-call | tf_op jit(solution)/shard_map/pallas_call | solution.py:240
  (14 shorter events, 0.0 us)
Async XLA Ops:
  2.9 11.8 %collective-permute-start.1 = (bf16[640,256]{1,0:T(8,128)(2,1)}, bf16[640,256]{1,0:T(8,128)(2,1)S(1)}, u32[]{:S(2)}, u32[]{:S(2)}) collective-permute-start(bf16[640,256]{1,0:T(8,128)(2,1)} %get-tuple-element.16), channel_id=1, source_target_pairs={{0,4},{4,0},{8,12},{12,8},{16,20},{20,16},{24,28},{28,24},{1,5},{5... | collective-permute-start | bytes 983048 | tf_op jit(solution)/shard_map/ppermute | solution.py:283
  6.0 22.8 %collective-permute-start.4 = (bf16[640,256]{1,0:T(8,128)(2,1)}, bf16[640,256]{1,0:T(8,128)(2,1)S(1)}, u32[]{:S(2)}, u32[]{:S(2)}) collective-permute-start(bf16[640,256]{1,0:T(8,128)(2,1)} %get-tuple-element.15.refs_0_), channel_id=1, source_target_pairs={{0,8},{8,16},{12,4},{16,24},{20,12},{28,20},{1,9},{9,17},{13,5},{1... | collective-permute-start | bytes 983048 | tf_op jit(solution)/shard_map/ppermute | solution.py:285
  9.5 11.4 %collective-permute-start.2 = (bf16[640,256]{1,0:T(8,128)(2,1)}, bf16[640,256]{1,0:T(8,128)(2,1)S(1)}, u32[]{:S(2)}, u32[]{:S(2)}) collective-permute-start(bf16[640,256]{1,0:T(8,128)(2,1)} %get-tuple-element.15.refs_0_), channel_id=1, source_target_pairs={{4,12},{8,0},{12,20},{16,8},{20,28},{24,16},{5,13},{9,1},{13,21},{... | collective-permute-start | bytes 983048 | tf_op jit(solution)/shard_map/ppermute | solution.py:284
  10.8 18.0 %collective-permute-start = (bf16[320,256]{1,0:T(8,128)(2,1)}, bf16[320,256]{1,0:T(8,128)(2,1)S(1)}, u32[]{:S(2)}, u32[]{:S(2)}) collective-permute-start(bf16[320,256]{1,0:T(8,128)(2,1)} %get-tuple-element.14), channel_id=1, source_target_pairs={{0,4},{4,0},{8,12},{12,8},{16,20},{20,16},{24,28},{28,24},{1,5},{5... | collective-permute-start | bytes 491528 | tf_op jit(solution)/shard_map/ppermute | solution.py:286
  14.7 8.9 %collective-permute-start.5 = (bf16[640,256]{1,0:T(8,128)(2,1)S(1)}, bf16[640,256]{1,0:T(8,128)(2,1)S(1)}, u32[]{:S(2)}, u32[]{:S(2)}) collective-permute-start(bf16[640,256]{1,0:T(8,128)(2,1)S(1)} %collective-permute-done.1.refs_1_), channel_id=1, source_target_pairs={{0,8},{8,16},{12,4},{16,24},{20,12},{28,20},{1,9},{9,17},{13,5},{1... | collective-permute-start | bytes 983048 | tf_op jit(solution)/shard_map/ppermute | solution.py:287
  19.5 12.5 %collective-permute-start.3 = (bf16[640,256]{1,0:T(8,128)(2,1)S(1)}, bf16[640,256]{1,0:T(8,128)(2,1)S(1)}, u32[]{:S(2)}, u32[]{:S(2)}) collective-permute-start(bf16[640,256]{1,0:T(8,128)(2,1)S(1)} %collective-permute-done.1.refs_1_), channel_id=1, source_target_pairs={{4,12},{8,0},{12,20},{16,8},{20,28},{24,16},{5,13},{9,1},{13,21},{... | collective-permute-start | bytes 983048 | tf_op jit(solution)/shard_map/ppermute | solution.py:288
  20.8 15.6 %collective-permute-start.6 = (bf16[640,256]{1,0:T(8,128)(2,1)S(1)}, bf16[640,256]{1,0:T(8,128)(2,1)S(1)}, u32[]{:S(2)}, u32[]{:S(2)}) collective-permute-start(bf16[640,256]{1,0:T(8,128)(2,1)S(1)} %collective-permute-done.2.refs_2_), channel_id=1, source_target_pairs={{4,12},{8,0},{12,20},{16,8},{20,28},{24,16},{5,13},{9,1},{13,21},{... | collective-permute-start | bytes 983048 | tf_op jit(solution)/shard_map/ppermute | solution.py:289
  23.7 12.7 %collective-permute-start.7 = (bf16[640,256]{1,0:T(8,128)(2,1)S(1)}, bf16[640,256]{1,0:T(8,128)(2,1)S(1)}, u32[]{:S(2)}, u32[]{:S(2)}) collective-permute-start(bf16[640,256]{1,0:T(8,128)(2,1)S(1)} %collective-permute-done.5.refs_5_), channel_id=1, source_target_pairs={{0,8},{8,16},{12,4},{16,24},{20,12},{28,20},{1,9},{9,17},{13,5},{1... | collective-permute-start | bytes 983048 | tf_op jit(solution)/shard_map/ppermute | solution.py:290
  36.4 1.0 %copy-start.2 = (bf16[640,256]{1,0:T(8,128)(2,1)S(1)}, bf16[640,256]{1,0:T(8,128)(2,1)}, u32[]{:S(2)}) copy-start(bf16[640,256]{1,0:T(8,128)(2,1)} %get-tuple-element.15.refs_0_) | copy-start | bytes 983044
  37.4 0.9 %copy-start.3 = (bf16[320,256]{1,0:T(8,128)(2,1)S(1)}, bf16[320,256]{1,0:T(8,128)(2,1)}, u32[]{:S(2)}) copy-start(bf16[320,256]{1,0:T(8,128)(2,1)} %get-tuple-element.13.own_q) | copy-start | bytes 491524
  38.3 13.2 %copy-start = (bf16[640,1280]{1,0:T(8,128)(2,1)S(1)}, bf16[640,1280]{1,0:T(8,128)(2,1)}, u32[]{:S(2)}) copy-start(bf16[640,1280]{1,0:T(8,128)(2,1)} %weight_ref.1) | copy-start | bytes 4915204
  38.3 13.2 %copy-start.1 = (bf16[256,1280]{1,0:T(8,128)(2,1)S(1)}, bf16[256,1280]{1,0:T(8,128)(2,1)}, u32[]{:S(2)}) copy-start(bf16[256,1280]{1,0:T(8,128)(2,1)} %tokens_ref.1) | copy-start | bytes 1966084
  38.3 13.2 %copy-start.4 = (f32[8,256]{1,0:T(8,128)S(1)}, f32[8,256]{1,0:T(8,128)}, u32[]{:S(2)}) copy-start(f32[8,256]{1,0:T(8,128)} %get-tuple-element.12.meta_ref) | copy-start | bytes 24580
  46.1 5.4 %collective-permute-start.8 = (bf16[320,256]{1,0:T(8,128)(2,1)S(1)}, bf16[320,256]{1,0:T(8,128)(2,1)S(1)}, u32[]{:S(2)}, u32[]{:S(2)}) collective-permute-start(bf16[320,256]{1,0:T(8,128)(2,1)S(1)} %get-tuple-element.18), channel_id=1, source_target_pairs={{0,4},{4,0},{8,12},{12,8},{16,20},{20,16},{24,28},{28,24},{1,5},{5... | collective-permute-start | bytes 491528 | tf_op jit(solution)/shard_map/ppermute | solution.py:308

commit v7 on v6

--- a/solution.py
+++ b/solution.py
@@ -11,6 +11,7 @@
 HALF = HEADS // 2
 SPAN = 3
 WINDOW = 2 * SPAN + 2
+NEAR = WINDOW // 2
 NEG = -1e30
 LOG2E = 1.4426950408889634
 MIB = 1024 * 1024
@@ -94,83 +95,117 @@
     )(half, owners, offsets, queries, keys, values)
 
 
-def attention_kernel(place_ref, half_ref, low_ref, count_ref, seg_ref, own_q, other_q, *refs):
-    blocks, refs = refs[:WINDOW], refs[WINDOW:]
-    own_out, other_out, query_s, key_s, value_s, seg_s, out_s = refs
-    half = half_ref[0]
-    part, rows = own_q.shape
+def attention_kernel(number, which, ends, need_ref, place_ref, seg_ref, query_seg_ref, *refs):
+    queries, refs = refs[:number], refs[number:]
+    blocks, refs = refs[:NEAR], refs[NEAR:]
+    follows = which is not None
+    if follows:
+        (accum_b, peak_b, total_b), refs = refs[:3], refs[3:]
+    if ends:
+        out_ref, key_s, value_s, seg_s, chosen_s = refs
+    else:
+        accum_ref, peak_ref, total_ref, key_s, value_s, seg_s, chosen_s = refs
+    part, rows = queries[0].shape
     hdim = part // HALF
     factor = LOG2E / (hdim**0.5)
-    query_s[half] = own_q[...]
-    query_s[1 - half] = other_q[...]
-    first = jnp.minimum(low_ref[0], low_ref[1])
-    last = jnp.maximum(low_ref[0] + count_ref[0], low_ref[1] + count_ref[1])
-    for b in range(WINDOW):
-        seg_s[b] = jnp.broadcast_to(seg_ref[b], (128, rows)).T
-    for i, block in enumerate(blocks):
-        place = place_ref[i]
-
-        @pl.when((place >= first) & (place < last))
-        def _(block=block, place=place):
+    for b in range(NEAR):
+        wanted = need_ref[0, b]
+        for n in range(1, number):
+            wanted = wanted + need_ref[n, b]
+
+        @pl.when(wanted > 0)
+        def _(b=b):
+            seg_s[b] = jnp.broadcast_to(seg_ref[place_ref[b]], (128, rows)).T
             for h in range(HALF):
-                key_s[h, place] = block[h * hdim : (h + 1) * hdim, :].T
-            value_s[place] = block[part:, :]
-
-    def one_head(i, carry):
-        which = i // HALF
-        h = i % HALF
-        low = low_ref[which]
-        count = count_ref[which]
-        lines = pl.ds(pl.multiple_of(h * hdim, 16), hdim)
-        query = query_s[which, lines, :]
-        query_seg = seg_ref[SPAN + which]
-
-        for size in range(1, 2 * SPAN + 2):
-
-            @pl.when(count == size)
-            def _():
-                key = key_s[h, pl.ds(low, size)].reshape(size * rows, hdim)
-                scores = jnp.dot(key, query, preferred_element_type=jnp.float32)
-                key_seg = seg_s[pl.ds(low, size)].reshape(size * rows, 128)
-                key_seg = jnp.concatenate([key_seg] * (rows // 128), axis=1)
-                scores = jnp.where(key_seg == query_seg, scores, NEG)
-                peak = jnp.max(scores, axis=0, keepdims=True)
-                weights = jnp.exp2((scores - peak) * factor)
-                total = jnp.sum(weights, axis=0, keepdims=True)
-                weights = weights.astype(jnp.bfloat16)
-                mixed = jnp.zeros((hdim, rows), jnp.float32)
-                for b in range(size):
-                    mixed += jnp.dot(
-                        value_s[low + b, lines, :],
-                        weights[b * rows : (b + 1) * rows],
-                        preferred_element_type=jnp.float32,
-                    )
-                out_s[which, lines, :] = (mixed / total).astype(out_s.dtype)
-
-        return carry
-
-    lax.fori_loop(0, 2 * HALF, one_head, 0)
-    own_out[...] = out_s[half]
-    other_out[...] = out_s[1 - half]
-
-
-def attention(place, half, low, count, segs, own_q, other_q, blocks):
-    part, rows = own_q.shape
+                key_s[h, b] = blocks[b][h * hdim : (h + 1) * hdim, :].T
+            value_s[b] = blocks[b][part:, :]
+
+    for n in range(number):
+        size = 0
+        for b in range(NEAR):
+            chosen_s[size] = b
+            size = size + need_ref[n, b]
+        query_seg = query_seg_ref[n]
+
+        def one_head(h, carry, n=n, size=size, query_seg=query_seg):
+            lines = pl.ds(pl.multiple_of(h * hdim, 16), hdim)
+            query = queries[n][lines, :]
+
+            def finish(peak, total, accum):
+                if ends:
+                    out_ref[lines, :] = (accum / total).astype(out_ref.dtype)
+                else:
+                    peak_ref[n, h] = peak
+                    total_ref[n, h] = total
+                    accum_ref[n, lines, :] = accum
+
+            if follows:
+
+                @pl.when(size == 0)
+                def _():
+                    finish(peak_b[which, h], total_b[which, h], accum_b[which, lines, :])
+
+            for fixed in range(1, NEAR + 1):
+
+                @pl.when(size == fixed)
+                def _():
+                    picked = [chosen_s[b] for b in range(fixed)]
+                    scores = []
+                    for b in picked:
+                        score = jnp.dot(key_s[h, b], query, preferred_element_type=jnp.float32)
+                        key_seg = jnp.concatenate([seg_s[b]] * (rows // 128), axis=1)
+                        scores.append(jnp.where(key_seg == query_seg, score, NEG))
+                    peak = jnp.max(scores[0], axis=0, keepdims=True)
+                    for score in scores[1:]:
+                        peak = jnp.maximum(peak, jnp.max(score, axis=0, keepdims=True))
+                    if follows:
+                        peak = jnp.maximum(peak, peak_b[which, h])
+                        scaled = jnp.exp2((peak_b[which, h] - peak) * factor)
+                        total = total_b[which, h] * scaled
+                        accum = accum_b[which, lines, :] * scaled
+                    else:
+                        total = jnp.zeros((1, rows), jnp.float32)
+                        accum = jnp.zeros((hdim, rows), jnp.float32)
+                    for b, score in zip(picked, scores):
+                        weights = jnp.exp2((score - peak) * factor)
+                        total += jnp.sum(weights, axis=0, keepdims=True)
+                        accum += jnp.dot(
+                            value_s[b, lines, :],
+                            weights.astype(jnp.bfloat16),
+                            preferred_element_type=jnp.float32,
+                        )
+                    finish(peak, total, accum)
+
+            return carry
+
+        lax.fori_loop(0, HALF, one_head, 0)
+
+
+def attention(need, places, segs, query_segs, queries, blocks, before, which, ends):
+    number = len(queries)
+    part, rows = queries[0].shape
     hdim = part // HALF
+    if ends:
+        outs = jax.ShapeDtypeStruct((part, rows), jnp.bfloat16)
+    else:
+        row = jax.ShapeDtypeStruct((number, HALF, 1, rows), jnp.float32)
+        outs = [jax.ShapeDtypeStruct((number, part, rows), jnp.float32), row, row]
     return pl.pallas_call(
-        attention_kernel,
-        out_shape=[jax.ShapeDtypeStruct((part, rows), jnp.bfloat16)] * 2,
-        in_specs=[smem()] * 4 + [vmem()] * (3 + WINDOW),
-        out_specs=[vmem()] * 2,
+        functools.partial(attention_kernel, number, which, ends),
+        out_shape=outs,
+        in_specs=[smem()] * 2 + [vmem()] * (2 + number + NEAR + (3 if before is not None else 0)),
+        out_specs=vmem() if ends else [vmem()] * 3,
         scratch_shapes=[
-            pltpu.VMEM((2, part, rows), jnp.bfloat16),
-            pltpu.VMEM((HALF, WINDOW, rows, hdim), jnp.bfloat16),
-            pltpu.VMEM((WINDOW, part, rows), jnp.bfloat16),
-            pltpu.VMEM((WINDOW, rows, 128), jnp.float32),
-            pltpu.VMEM((2, part, rows), jnp.bfloat16),
+            pltpu.VMEM((HALF, NEAR, rows, hdim), jnp.bfloat16),
+            pltpu.VMEM((NEAR, part, rows), jnp.bfloat16),
+            pltpu.VMEM((NEAR, rows, 128), jnp.float32),
+            pltpu.SMEM((NEAR + 1,), jnp.int32),
         ],
-        compiler_params=limit(24),
-    )(place, half, low, count, segs, own_q, other_q, *blocks)
+        compiler_params=limit(16),
+        cost_estimate=pl.CostEstimate(
+            flops=2_000_000_000 * number, bytes_accessed=2_000_000, transcendentals=1_000_000
+        ),
+    )(need, places, segs, query_segs, *queries, *blocks, *(before or ()))
 
 
 def project_kernel(
@@ -269,6 +304,9 @@
     swap = functools.partial(
         lax.ppermute, axis_name="blk", perm=route(lambda i: 1 - 2 * (i % 2))
     )
+    across = functools.partial(
+        lax.ppermute, axis_name="blk", perm=route(lambda i: 1 if i % 2 else -1)
+    )
     ahead = functools.partial(
         lax.ppermute, axis_name="blk", perm=route(lambda i: 2 if i % 2 else -2)
     )
@@ -276,36 +314,48 @@
         lax.ppermute, axis_name="blk", perm=route(lambda i: -2 if i % 2 else 2)
     )
 
-    halves = half[None].astype(jnp.int32)
     own_q, own_kv, swap_q, swap_kv, meta = prepare(
-        halves, owners[None, :], offsets[None, :], queries, keys, values, pair_rows
+        half[None].astype(jnp.int32), owners[None, :], offsets[None, :],
+        queries, keys, values, pair_rows,
     )
     other_kv = swap(swap_kv)
+    back_other = across(swap_kv)
     ahead_own = ahead(own_kv)
     back_own = back(own_kv)
     other_q = swap(swap_q)
-    back_other = back(other_kv)
     ahead_other = ahead(other_kv)
     ahead_far = ahead(ahead_own)
     back_far = back(back_other)
-    blocks = (own_kv, other_kv, ahead_own, ahead_other, back_own, back_other, ahead_far, back_far)
+    near = (own_kv, other_kv, ahead_own, back_own)
+    far = (ahead_other, back_other, ahead_far, back_far)
     places = jnp.where(
         half == 0,
-        jnp.array([3, 4, 5, 6, 1, 2, 7, 0], jnp.int32),
-        jnp.array([4, 3, 2, 1, 6, 5, 0, 7], jnp.int32),
+        jnp.array([3, 4, 5, 1, 6, 2, 7, 0], jnp.int32),
+        jnp.array([4, 3, 2, 6, 1, 5, 0, 7], jnp.int32),
     )
 
     segs = jnp.pad(segment_ids.reshape(nblocks, 1, rows), ((SPAN, SPAN), (0, 0), (0, 0)))
     segs = lax.dynamic_slice_in_dim(segs, pair, WINDOW, 0).astype(jnp.float32)
-    mask = lax.dynamic_slice_in_dim(block_mask, pair, 2, 0)
-    block = pair + jnp.arange(2)[:, None]
-    other = jnp.arange(nblocks)[None, :]
-    present = (mask > 0) & (jnp.abs(block - other) <= SPAN)
-    low = jnp.min(jnp.where(present, other, nblocks), axis=1) - pair + SPAN
-    count = jnp.sum(present.astype(jnp.int32), axis=1)
-
-    own, other = attention(places, halves, low, count, segs, own_q, other_q, blocks)
+    query_segs = segs[places[:2]]
+    pair_mask = lax.dynamic_slice_in_dim(block_mask, pair, 2, 0)
+    pair_mask = jnp.pad(pair_mask, ((0, 0), (SPAN, SPAN)))
+    pair_mask = lax.dynamic_slice_in_dim(pair_mask, pair, WINDOW, 1)
+    apart = jnp.arange(WINDOW)[None, :] - SPAN - jnp.arange(2)[:, None]
+    need = ((pair_mask > 0) & (jnp.abs(apart) <= SPAN)).astype(jnp.int32)
+    need = need[places[:2] - SPAN][:, places]
+
+    state = attention(
+        need[:, :NEAR], places[:NEAR], segs, query_segs, (own_q, other_q), near, None, None, False
+    )
+    far_need, far_places = need[:, NEAR:], places[NEAR:]
+    other = attention(
+        far_need[1:], far_places, segs, query_segs[1:], (other_q,), far, state, 1, True
+    )
     other = swap(other)
+    own = attention(
+        far_need[:1], far_places, segs, query_segs[:1], (own_q,), far, state, 0, True
+    )
+    halves = half[None].astype(jnp.int32)
     outgoing = project(halves, meta, own, other, out_weight, tokens, slots, capacity)
     arrived = lax.all_to_all(outgoing, "blk", split_axis=0, concat_axis=0, tiled=True)
     return place(arrived, capacity, 4 * width)

time: 87.3 us -> 88.7 us (1.016)
  waiting for transfers between devices: 16.8 us -> 6.76 us
  starting transfers between devices: 19.6 us -> 25.6 us
  Pallas kernels: 13.6 us -> 17.1 us
  local copies, waits for them, and re-layouts: 1.9 us -> 3.91 us
    ppermute x1, waiting for transfers between devices: 4.33 us -> 0.01 us  [per_device(): ahead_far = ahead(ahead_own)]
    ppermute x1, starting transfers between devices: 1.2 us -> 5.4 us  [per_device(): other_q = swap(swap_q)]
    ppermute x1, waiting for transfers between devices: 4.99 us -> 0.83 us  [per_device(): other = swap(other)]
    pallas_call x1 -> x3, Pallas kernels: 7.76 us -> 11.2 us  [attention(): pl.pallas_call(functools.partial(attention_kernel, number, which, ends),...]
    ppermute x1, waiting for transfers between devices: 3.24 us -> 0.01 us  [per_device(): ahead_other = ahead(other_kv)]
    ppermute x1, waiting for transfers between devices: 2.75 us -> 5.91 us  [per_device(): other_kv = swap(swap_kv)]
    ppermute x1, starting transfers between devices: 3.23 us -> 0.67 us  [per_device(): back_other = across(swap_kv)]
    ppermute x1, starting transfers between devices: 4.39 us -> 6.66 us  [per_device(): back_far = back(back_other)]
  transfers between devices with their start and end apart: 9 -> 9, of which waited for: 5 -> 2; matrix products, arithmetic and copies ran while one was open for 3% -> 4% of each run, Pallas kernels for 0% -> 10%
where the time goes in v7:
time: 88.7 us; the launch traced here: 88.3 us
  blocking collectives  33.2 us (37%)
  starting transfers between devices  25.6 us (29%)
  Pallas kernels  17.1 us (19%)
  waiting for transfers between devices  6.76 us (8%)
  local copies, waits for them, and re-layouts  3.91 us (4%)
  other arithmetic  1.47 us (2%)
    all_to_all x1, blocking collectives, per_device(): lax.all_to_all(outgoing, 'blk', split_axis=0, concat_axis=0, tiled=True)  33.2 us
    pallas_call x3, Pallas kernels, attention(): pl.pallas_call(functools.partial(attention_kernel, number, which, ends),...  11.2 us
    ppermute x1, starting transfers between devices, per_device(): back_far = back(back_other)  6.66 us
    ppermute x1, waiting for transfers between devices, per_device(): other_kv = swap(swap_kv)  5.91 us
    ppermute x1, starting transfers between devices, per_device(): back_own = back(own_kv)  5.58 us
    ppermute x1, starting transfers between devices, per_device(): other_q = swap(swap_q)  5.4 us
    pallas_call x1, Pallas kernels, prepare(): pl.pallas_call(functools.partial(prepare_kernel, pair_rows), out_shape=[s...  2.96 us
    ppermute x1, starting transfers between devices, per_device(): other = swap(other)  2.53 us
  transfers between devices with their start and end apart: 9, of which 2 were waited for; matrix products, arithmetic and copies ran while one was open for 4% of the time, Pallas kernels for 10%

profile of v7, /device:TPU:0, one launch (start us, length us, event | category | flops | bytes accessed | tf_op | source)
XLA Modules:
  0.0 88.3 jit_solution(8730835283297503472)
XLA Ops:
  0.0 3.0 %shard_map.109 = (bf16[320,256]{1,0:T(8,128)(2,1)}, bf16[640,256]{1,0:T(8,128)(2,1)}, bf16[320,256]{1,0:T(8,128)(2,1)}, bf16[640,256]{1,0:T(8,128)(2,1)}, f32[8,256]{1,0:T(8,128)}) custom-call(s32[1]{0:T(128)} %bitcast.half_ref, s32[1,64]{1,0:T(1,128)} %bitcast.21, s32[1,64]{1,0:T(1,128)} %bitcast.22, bf16[256,640]{1,0:T(8,128)(2,1)} %q_hbm.1, ...), custom_call_target="tpu_custom_call" | custom-call | tf_op jit(solution)/shard_map/pallas_call | solution.py:84
  3.0 1.3 %collective-permute-start.3 = (bf16[640,256]{1,0:T(8,128)(2,1)}, bf16[640,256]{1,0:T(8,128)(2,1)S(1)}, u32[]{:S(2)}, u32[]{:S(2)}) collective-permute-start(bf16[640,256]{1,0:T(8,128)(2,1)} %get-tuple-element.16.refs_2_), channel_id=1, source_target_pairs={{4,12},{8,0},{12,20},{16,8},{20,28},{24,16},{5,13},{9,1},{13,21},{... | collective-permute-start | bytes 983048 | tf_op jit(solution)/shard_map/ppermute | solution.py:323
  4.3 5.6 %collective-permute-start.7 = (bf16[640,256]{1,0:T(8,128)(2,1)}, bf16[640,256]{1,0:T(8,128)(2,1)S(1)}, u32[]{:S(2)}, u32[]{:S(2)}) collective-permute-start(bf16[640,256]{1,0:T(8,128)(2,1)} %get-tuple-element.16.refs_2_), channel_id=1, source_target_pairs={{0,8},{8,16},{12,4},{16,24},{20,12},{28,20},{1,9},{9,17},{13,5},{1... | collective-permute-start | bytes 983048 | tf_op jit(solution)/shard_map/ppermute | solution.py:324
  9.9 1.0 %collective-permute-start = (bf16[640,256]{1,0:T(8,128)(2,1)}, bf16[640,256]{1,0:T(8,128)(2,1)S(1)}, u32[]{:S(2)}, u32[]{:S(2)}) collective-permute-start(bf16[640,256]{1,0:T(8,128)(2,1)} %get-tuple-element.15), channel_id=1, source_target_pairs={{0,4},{4,0},{8,12},{12,8},{16,20},{20,16},{24,28},{28,24},{1,5},{5... | collective-permute-start | bytes 983048 | tf_op jit(solution)/shard_map/ppermute | solution.py:321
  10.8 0.7 collective-permute-start.2
  11.5 5.4 %collective-permute-start.6 = (bf16[320,256]{1,0:T(8,128)(2,1)}, bf16[320,256]{1,0:T(8,128)(2,1)S(1)}, u32[]{:S(2)}, u32[]{:S(2)}) collective-permute-start(bf16[320,256]{1,0:T(8,128)(2,1)} %get-tuple-element.17), channel_id=1, source_target_pairs={{0,4},{4,0},{8,12},{12,8},{16,20},{20,16},{24,28},{28,24},{1,5},{5... | collective-permute-start | bytes 491528 | tf_op jit(solution)/shard_map/ppermute | solution.py:325
  16.9 0.7 compare_select_fusion.1
  17.7 0.6 gather_fusion
  19.0 0.7 fusion.seg_ref
  19.7 0.6 gather_fusion.2
  20.4 5.9 %collective-permute-done.refs_3_ = bf16[640,256]{1,0:T(8,128)(2,1)S(1)} collective-permute-done((bf16[640,256]{1,0:T(8,128)(2,1)}, bf16[640,256]{1,0:T(8,128)(2,1)S(1)}, u32[]{:S(2)}, u32[]{:S(2)}) %collective-permute-start) | collective-permute-done | bytes 327712 | tf_op jit(solution)/shard_map/ppermute | solution.py:321
  26.3 1.3 %collective-permute-start.1 = (bf16[640,256]{1,0:T(8,128)(2,1)S(1)}, bf16[640,256]{1,0:T(8,128)(2,1)S(1)}, u32[]{:S(2)}, u32[]{:S(2)}) collective-permute-start(bf16[640,256]{1,0:T(8,128)(2,1)S(1)} %collective-permute-done.refs_3_), channel_id=1, source_target_pairs={{4,12},{8,0},{12,20},{16,8},{20,28},{24,16},{5,13},{9,1},{13,21},{... | collective-permute-start | bytes 983048 | tf_op jit(solution)/shard_map/ppermute | solution.py:326
  27.6 1.3 %collective-permute-start.4 = (bf16[640,256]{1,0:T(8,128)(2,1)S(1)}, bf16[640,256]{1,0:T(8,128)(2,1)S(1)}, u32[]{:S(2)}, u32[]{:S(2)}) collective-permute-start(bf16[640,256]{1,0:T(8,128)(2,1)S(1)} %collective-permute-done.3.refs_4_), channel_id=1, source_target_pairs={{4,12},{8,0},{12,20},{16,8},{20,28},{24,16},{5,13},{9,1},{13,21},{... | collective-permute-start | bytes 983048 | tf_op jit(solution)/shard_map/ppermute | solution.py:327
  28.9 6.7 %collective-permute-start.5 = (bf16[640,256]{1,0:T(8,128)(2,1)S(1)}, bf16[640,256]{1,0:T(8,128)(2,1)S(1)}, u32[]{:S(2)}, u32[]{:S(2)}) collective-permute-start(bf16[640,256]{1,0:T(8,128)(2,1)S(1)} %collective-permute-done.2.refs_2_), channel_id=1, source_target_pairs={{0,8},{8,16},{12,4},{16,24},{20,12},{28,20},{1,9},{9,17},{13,5},{1... | collective-permute-start | bytes 983048 | tf_op jit(solution)/shard_map/ppermute | solution.py:328
  35.6 1.0 %copy-done.4 = bf16[640,256]{1,0:T(8,128)(2,1)S(1)} copy-done((bf16[640,256]{1,0:T(8,128)(2,1)S(1)}, bf16[640,256]{1,0:T(8,128)(2,1)}, u32[]{:S(2)}) %copy-start.4) | copy-done | bytes 327704
  36.6 0.9 %copy-done.5 = bf16[320,256]{1,0:T(8,128)(2,1)S(1)} copy-done((bf16[320,256]{1,0:T(8,128)(2,1)S(1)}, bf16[320,256]{1,0:T(8,128)(2,1)}, u32[]{:S(2)}) %copy-start.5) | copy-done | bytes 163864
  37.5 6.3 %shard_map.110 = (f32[2,320,256]{2,1,0:T(8,128)S(1)}, f32[2,4,1,256]{3,2,1,0:T(1,128)S(1)}, f32[2,4,1,256]{3,2,1,0:T(1,128)S(1)}) custom-call(s32[2,4]{1,0:T(2,128)S(1)} %bitcast.18, s32[4]{0:T(128)S(1)} %get-tuple-element.27.place_ref, f32[8,1,256]{2,1,0:T(1,128)S(1)} %fusion.seg_ref, f32[2,1,256]{2,1,0:T(1,128)S(1)} %reshape.28.query_seg_ref, ...), custom_call_target="tpu_custom_call" | custom-call | flops 4000000000 | bytes 2000000 | tf_op jit(solution)/shard_map/pallas_call | solution.py:193
  43.8 2.4 %shard_map.112 = bf16[320,256]{1,0:T(8,128)(2,1)S(1)} custom-call(s32[1,4]{1,0:T(1,128)S(1)} %get-tuple-element.23.need_ref, s32[4]{0:T(128)S(1)} %get-tuple-element.28.place_ref, f32[8,1,256]{2,1,0:T(1,128)S(1)} %fusion.seg_ref, f32[1,1,256]{2,1,0:T(1,128)S(1)} %get-tuple-element.21.query_seg_ref, ...), custom_call_target="tpu_custom_call" | custom-call | flops 2000000000 | bytes 2000000 | tf_op jit(solution)/shard_map/pallas_call | solution.py:193
  46.3 2.5 %collective-permute-start.8 = (bf16[320,256]{1,0:T(8,128)(2,1)S(1)}, bf16[320,256]{1,0:T(8,128)(2,1)S(1)}, u32[]{:S(2)}, u32[]{:S(2)}) collective-permute-start(bf16[320,256]{1,0:T(8,128)(2,1)S(1)} %shard_map.112), channel_id=1, source_target_pairs={{0,4},{4,0},{8,12},{12,8},{16,20},{20,16},{24,28},{28,24},{1,5},{5... | collective-permute-start | bytes 491528 | tf_op jit(solution)/shard_map/ppermute | solution.py:354
  48.8 2.4 %shard_map.111.own_ref = bf16[320,256]{1,0:T(8,128)(2,1)S(1)} custom-call(s32[1,4]{1,0:T(1,128)S(1)} %get-tuple-element.24.need_ref, s32[4]{0:T(128)S(1)} %get-tuple-element.28.place_ref, f32[8,1,256]{2,1,0:T(1,128)S(1)} %fusion.seg_ref, f32[1,1,256]{2,1,0:T(1,128)S(1)} %get-tuple-element.22.query_seg_ref, bf16[320,256]{1,0:T(8,128)(2,1)S(1)} %copy-done.6, ...), custom_call_target="tpu_custom_call" | custom-call | flops 2000000000 | bytes 2000000 | tf_op jit(solution)/shard_map/pallas_call | solution.py:193
  51.3 0.8 collective-permute-done.8.other_ref
  52.1 1.5 %shard_map.113 = bf16[128,5248]{1,0:T(8,128)(2,1)S(1)} custom-call(s32[1]{0:T(128)} %bitcast.half_ref, f32[8,256]{1,0:T(8,128)S(1)} %copy-done.3, bf16[320,256]{1,0:T(8,128)(2,1)S(1)} %shard_map.111.own_ref, bf16[320,256]{1,0:T(8,128)(2,1)S(1)} %collective-permute-done.8.other_ref, bf16[640,1280]{1,0:T(8,128)(2,1)S(1)} %copy-done.1, ...), custom_call_target="tpu_custom_call" | custom-call | tf_op jit(solution)/shard_map/pallas_call | solution.py:243
  53.6 33.2 %all_to_all.11 = bf16[8,16,5248]{2,1,0:T(8,128)(2,1)S(1)} all-to-all(bf16[8,16,5248]{2,1,0:T(8,128)(2,1)S(1)} %bitcast.15), channel_id=1, replica_groups=mesh['blk'=8,'rep'=4] {'blk'}, dimensions={0} | all-to-all | bytes 2686976 | tf_op jit(solution)/shard_map/all_to_all | solution.py:360
  86.9 1.4 %shard_map.114 = bf16[128,5120]{1,0:T(8,128)(2,1)} custom-call(bf16[128,5248]{1,0:T(8,128)(2,1)S(1)} %bitcast.16), custom_call_target="tpu_custom_call" | custom-call | tf_op jit(solution)/shard_map/pallas_call | solution.py:275
  (33 shorter events, 1.0 us)
Async XLA Ops:
  0.0 17.6 %copy-start = (s32[8,8]{1,0:T(8,128)S(1)}, s32[8,8]{1,0:T(8,128)}, u32[]{:S(2)}) copy-start(s32[8,8]{1,0:T(8,128)} %param.12) | copy-start | bytes 772
  3.0 24.6 %collective-permute-start.3 = (bf16[640,256]{1,0:T(8,128)(2,1)}, bf16[640,256]{1,0:T(8,128)(2,1)S(1)}, u32[]{:S(2)}, u32[]{:S(2)}) collective-permute-start(bf16[640,256]{1,0:T(8,128)(2,1)} %get-tuple-element.16.refs_2_), channel_id=1, source_target_pairs={{4,12},{8,0},{12,20},{16,8},{20,28},{24,16},{5,13},{9,1},{13,21},{... | collective-permute-start | bytes 983048 | tf_op jit(solution)/shard_map/ppermute | solution.py:323
  4.3 31.3 %collective-permute-start.7 = (bf16[640,256]{1,0:T(8,128)(2,1)}, bf16[640,256]{1,0:T(8,128)(2,1)S(1)}, u32[]{:S(2)}, u32[]{:S(2)}) collective-permute-start(bf16[640,256]{1,0:T(8,128)(2,1)} %get-tuple-element.16.refs_2_), channel_id=1, source_target_pairs={{0,8},{8,16},{12,4},{16,24},{20,12},{28,20},{1,9},{9,17},{13,5},{1... | collective-permute-start | bytes 983048 | tf_op jit(solution)/shard_map/ppermute | solution.py:324
  9.9 16.5 %collective-permute-start = (bf16[640,256]{1,0:T(8,128)(2,1)}, bf16[640,256]{1,0:T(8,128)(2,1)S(1)}, u32[]{:S(2)}, u32[]{:S(2)}) collective-permute-start(bf16[640,256]{1,0:T(8,128)(2,1)} %get-tuple-element.15), channel_id=1, source_target_pairs={{0,4},{4,0},{8,12},{12,8},{16,20},{20,16},{24,28},{28,24},{1,5},{5... | collective-permute-start | bytes 983048 | tf_op jit(solution)/shard_map/ppermute | solution.py:321
  10.8 18.1 %collective-permute-start.2 = (bf16[640,256]{1,0:T(8,128)(2,1)}, bf16[640,256]{1,0:T(8,128)(2,1)S(1)}, u32[]{:S(2)}, u32[]{:S(2)}) collective-permute-start(bf16[640,256]{1,0:T(8,128)(2,1)} %get-tuple-element.15), channel_id=1, source_target_pairs={{4,8},{8,4},{12,16},{16,12},{20,24},{24,20},{5,9},{9,5},{13,17},{1... | collective-permute-start | bytes 983048 | tf_op jit(solution)/shard_map/ppermute | solution.py:322
  11.5 24.1 %collective-permute-start.6 = (bf16[320,256]{1,0:T(8,128)(2,1)}, bf16[320,256]{1,0:T(8,128)(2,1)S(1)}, u32[]{:S(2)}, u32[]{:S(2)}) collective-permute-start(bf16[320,256]{1,0:T(8,128)(2,1)} %get-tuple-element.17), channel_id=1, source_target_pairs={{0,4},{4,0},{8,12},{12,8},{16,20},{20,16},{24,28},{28,24},{1,5},{5... | collective-permute-start | bytes 491528 | tf_op jit(solution)/shard_map/ppermute | solution.py:325
  26.3 17.5 %collective-permute-start.1 = (bf16[640,256]{1,0:T(8,128)(2,1)S(1)}, bf16[640,256]{1,0:T(8,128)(2,1)S(1)}, u32[]{:S(2)}, u32[]{:S(2)}) collective-permute-start(bf16[640,256]{1,0:T(8,128)(2,1)S(1)} %collective-permute-done.refs_3_), channel_id=1, source_target_pairs={{4,12},{8,0},{12,20},{16,8},{20,28},{24,16},{5,13},{9,1},{13,21},{... | collective-permute-start | bytes 983048 | tf_op jit(solution)/shard_map/ppermute | solution.py:326
  27.6 16.2 %collective-permute-start.4 = (bf16[640,256]{1,0:T(8,128)(2,1)S(1)}, bf16[640,256]{1,0:T(8,128)(2,1)S(1)}, u32[]{:S(2)}, u32[]{:S(2)}) collective-permute-start(bf16[640,256]{1,0:T(8,128)(2,1)S(1)} %collective-permute-done.3.refs_4_), channel_id=1, source_target_pairs={{4,12},{8,0},{12,20},{16,8},{20,28},{24,16},{5,13},{9,1},{13,21},{... | collective-permute-start | bytes 983048 | tf_op jit(solution)/shard_map/ppermute | solution.py:327
  28.9 14.9 %collective-permute-start.5 = (bf16[640,256]{1,0:T(8,128)(2,1)S(1)}, bf16[640,256]{1,0:T(8,128)(2,1)S(1)}, u32[]{:S(2)}, u32[]{:S(2)}) collective-permute-start(bf16[640,256]{1,0:T(8,128)(2,1)S(1)} %collective-permute-done.2.refs_2_), channel_id=1, source_target_pairs={{0,8},{8,16},{12,4},{16,24},{20,12},{28,20},{1,9},{9,17},{13,5},{1... | collective-permute-start | bytes 983048 | tf_op jit(solution)/shard_map/ppermute | solution.py:328
  35.6 1.0 %copy-start.4 = (bf16[640,256]{1,0:T(8,128)(2,1)S(1)}, bf16[640,256]{1,0:T(8,128)(2,1)}, u32[]{:S(2)}) copy-start(bf16[640,256]{1,0:T(8,128)(2,1)} %get-tuple-element.16.refs_2_) | copy-start | bytes 983044
  36.6 0.9 %copy-start.5 = (bf16[320,256]{1,0:T(8,128)(2,1)S(1)}, bf16[320,256]{1,0:T(8,128)(2,1)}, u32[]{:S(2)}) copy-start(bf16[320,256]{1,0:T(8,128)(2,1)} %get-tuple-element.14.refs_0_) | copy-start | bytes 491524
  43.8 5.0 %copy-start.6 = (bf16[320,256]{1,0:T(8,128)(2,1)S(1)}, bf16[320,256]{1,0:T(8,128)(2,1)}, u32[]{:S(2)}) copy-start(bf16[320,256]{1,0:T(8,128)(2,1)} %get-tuple-element.14.refs_0_) | copy-start | bytes 491524
  46.3 5.8 %collective-permute-start.8 = (bf16[320,256]{1,0:T(8,128)(2,1)S(1)}, bf16[320,256]{1,0:T(8,128)(2,1)S(1)}, u32[]{:S(2)}, u32[]{:S(2)}) collective-permute-start(bf16[320,256]{1,0:T(8,128)(2,1)S(1)} %shard_map.112), channel_id=1, source_target_pairs={{0,4},{4,0},{8,12},{12,8},{16,20},{20,16},{24,28},{28,24},{1,5},{5... | collective-permute-start | bytes 491528 | tf_op jit(solution)/shard_map/ppermute | solution.py:354
  48.8 3.3 %copy-start.1 = (bf16[640,1280]{1,0:T(8,128)(2,1)S(1)}, bf16[640,1280]{1,0:T(8,128)(2,1)}, u32[]{:S(2)}) copy-start(bf16[640,1280]{1,0:T(8,128)(2,1)} %weight_ref.1) | copy-start | bytes 4915204
  48.8 3.3 %copy-start.2 = (bf16[256,1280]{1,0:T(8,128)(2,1)S(1)}, bf16[256,1280]{1,0:T(8,128)(2,1)}, u32[]{:S(2)}) copy-start(bf16[256,1280]{1,0:T(8,128)(2,1)} %tokens_ref.1) | copy-start | bytes 1966084
  48.8 3.3 %copy-start.3 = (f32[8,256]{1,0:T(8,128)S(1)}, f32[8,256]{1,0:T(8,128)}, u32[]{:S(2)}) copy-start(f32[8,256]{1,0:T(8,128)} %get-tuple-element.13.meta_ref) | copy-start | bytes 24580

commit v8 on v6

--- a/solution.py
+++ b/solution.py
@@ -10,7 +10,6 @@
 HEADS = 8
 HALF = HEADS // 2
 SPAN = 3
-WINDOW = 2 * SPAN + 2
 NEG = -1e30
 LOG2E = 1.4426950408889634
 MIB = 1024 * 1024
@@ -33,7 +32,7 @@
 
 
 def prepare_kernel(
-    pair_rows, half_ref, owners_ref, offsets_ref, q_hbm, k_hbm, v_hbm,
+    pair_rows, where_ref, owners_ref, offsets_ref, q_hbm, k_hbm, v_hbm,
     own_q, own_kv, swap_q, swap_kv, meta_ref, held, turned, sems,
 ):
     rows, features = q_hbm.shape
@@ -62,8 +61,9 @@
         meta.astype(jnp.bfloat16), spread, preferred_element_type=jnp.float32
     )
 
-    mine = pl.multiple_of(half_ref[0] * part, 16)
-    other = pl.multiple_of((1 - half_ref[0]) * part, 16)
+    half = where_ref[0] % 2
+    mine = pl.multiple_of(half * part, 16)
+    other = pl.multiple_of((1 - half) * part, 16)
     for i in range(3):
         loads[i].wait()
         turned[i] = held[i].T
@@ -75,7 +75,7 @@
             swap_q[...] = turned[i, pl.ds(other, part), :]
 
 
-def prepare(half, owners, offsets, queries, keys, values, pair_rows):
+def prepare(where, owners, offsets, queries, keys, values, pair_rows):
     rows, features = queries.shape
     part = features // 2
     single = jax.ShapeDtypeStruct((part, rows), queries.dtype)
@@ -91,95 +91,163 @@
             pltpu.SemaphoreType.DMA((3,)),
         ],
         compiler_params=limit(60),
-    )(half, owners, offsets, queries, keys, values)
-
-
-def attention_kernel(place_ref, half_ref, low_ref, count_ref, seg_ref, own_q, other_q, *refs):
-    blocks, refs = refs[:WINDOW], refs[WINDOW:]
-    own_out, other_out, query_s, key_s, value_s, seg_s, out_s = refs
-    half = half_ref[0]
-    part, rows = own_q.shape
+    )(where, owners, offsets, queries, keys, values)
+
+
+PLACES = ((3, 1), (4, -1), (5, -3), (1, 5), (6, -5), (2, 3), (7, -7), (0, 7))
+
+
+def attention_kernel(kinds, numbers, which, ends, where_ref, mask_ref, seg_ref, *refs):
+    queries, refs = refs[: len(kinds)], refs[len(kinds) :]
+    blocks, refs = refs[: len(numbers)], refs[len(numbers) :]
+    follows = which is not None
+    if follows:
+        before, refs = refs[0], refs[1:]
+    out_ref, query_s, key_s, value_s, chosen_s = refs
+    part, rows = queries[0].shape
     hdim = part // HALF
+    wide = value_s.shape[2]
+    nblocks = mask_ref.shape[0]
     factor = LOG2E / (hdim**0.5)
-    query_s[half] = own_q[...]
-    query_s[1 - half] = other_q[...]
-    first = jnp.minimum(low_ref[0], low_ref[1])
-    last = jnp.maximum(low_ref[0] + count_ref[0], low_ref[1] + count_ref[1])
-    for b in range(WINDOW):
-        seg_s[b] = jnp.broadcast_to(seg_ref[b], (128, rows)).T
-    for i, block in enumerate(blocks):
-        place = place_ref[i]
-
-        @pl.when((place >= first) & (place < last))
-        def _(block=block, place=place):
+    me = where_ref[0]
+    half = me % 2
+    column = [me - half - SPAN + PLACES[b][0] + PLACES[b][1] * half for b in numbers]
+    asker = [me if kind == 0 else me + 1 - 2 * half for kind in kinds]
+
+    def needed(n, b):
+        inside = (column[b] >= 0) & (column[b] < nblocks)
+        inside &= jnp.abs(column[b] - asker[n]) <= SPAN
+        allowed = mask_ref[asker[n], jnp.clip(column[b], 0, nblocks - 1)] > 0
+        return (inside & allowed).astype(jnp.int32)
+
+    need = [[needed(n, b) for b in range(len(numbers))] for n in range(len(kinds))]
+
+    def segment(block):
+        start = pl.multiple_of(jnp.clip(block, 0, nblocks - 1) * rows, 128)
+        return seg_ref[:, pl.ds(start, rows)].astype(jnp.float32)
+
+    for b in range(len(numbers)):
+        wanted = need[0][b]
+        for n in range(1, len(kinds)):
+            wanted = wanted + need[n][b]
+
+        @pl.when(wanted > 0)
+        def _(b=b):
+            key_s[b] = blocks[b][:part, :]
             for h in range(HALF):
-                key_s[h, place] = block[h * hdim : (h + 1) * hdim, :].T
-            value_s[place] = block[part:, :]
-
-    def one_head(i, carry):
-        which = i // HALF
-        h = i % HALF
-        low = low_ref[which]
-        count = count_ref[which]
-        lines = pl.ds(pl.multiple_of(h * hdim, 16), hdim)
-        query = query_s[which, lines, :]
-        query_seg = seg_ref[SPAN + which]
-
-        for size in range(1, 2 * SPAN + 2):
-
-            @pl.when(count == size)
+                lines = slice(part + h * hdim, part + (h + 1) * hdim)
+                value_s[b, h, :hdim, :] = blocks[b][lines, :]
+                value_s[b, h, hdim:, :] = jnp.ones((wide - hdim, rows), jnp.bfloat16)
+
+    for n in range(len(kinds)):
+        size = 0
+        for b in range(len(numbers)):
+            chosen_s[size] = b
+            size = size + need[n][b]
+        for h in range(HALF):
+            query_s[h] = queries[n][h * hdim : (h + 1) * hdim, :].T
+        query_seg = jnp.broadcast_to(segment(asker[n]), (128, rows)).T
+        query_seg = jnp.concatenate([query_seg] * (rows // 128), axis=1)
+
+        def finish(h, peak, accum, n=n):
+            if ends:
+                turned = accum.T
+                lines = pl.ds(pl.multiple_of(h * hdim, 16), hdim)
+                out_ref[lines, :] = (turned[:hdim] / turned[hdim : hdim + 1]).astype(out_ref.dtype)
+            else:
+                peak = jnp.broadcast_to(peak, (rows, 128 - wide))
+                out_ref[n, h] = jnp.concatenate([accum, peak], axis=1)
+
+        if follows:
+
+            @pl.when(size == 0)
             def _():
-                key = key_s[h, pl.ds(low, size)].reshape(size * rows, hdim)
-                scores = jnp.dot(key, query, preferred_element_type=jnp.float32)
-                key_seg = seg_s[pl.ds(low, size)].reshape(size * rows, 128)
-                key_seg = jnp.concatenate([key_seg] * (rows // 128), axis=1)
-                scores = jnp.where(key_seg == query_seg, scores, NEG)
-                peak = jnp.max(scores, axis=0, keepdims=True)
-                weights = jnp.exp2((scores - peak) * factor)
-                total = jnp.sum(weights, axis=0, keepdims=True)
-                weights = weights.astype(jnp.bfloat16)
-                mixed = jnp.zeros((hdim, rows), jnp.float32)
-                for b in range(size):
-                    mixed += jnp.dot(
-                        value_s[low + b, lines, :],
-                        weights[b * rows : (b + 1) * rows],
-                        preferred_element_type=jnp.float32,
-                    )
-                out_s[which, lines, :] = (mixed / total).astype(out_s.dtype)
-
-        return carry
-
-    lax.fori_loop(0, 2 * HALF, one_head, 0)
-    own_out[...] = out_s[half]
-    other_out[...] = out_s[1 - half]
-
-
-def attention(place, half, low, count, segs, own_q, other_q, blocks):
-    part, rows = own_q.shape
+                def one_head(h, carry):
+                    state = before[which, h]
+                    finish(h, state[:, wide : wide + 1], state[:, :wide])
+                    return carry
+
+                lax.fori_loop(0, HALF, one_head, 0)
+
+        for fixed in range(1, len(numbers) + 1):
+
+            @pl.when(size == fixed)
+            def _():
+                picked = [chosen_s[b] for b in range(fixed)]
+                key_segs = [
+                    segment(sum(jnp.where(b == i, column[i], 0) for i in range(len(numbers))))
+                    for b in picked
+                ]
+
+                def one_head(h):
+                    lines = pl.ds(pl.multiple_of(h * hdim, 16), hdim)
+                    query = query_s[h]
+                    scores = []
+                    for b, key_seg in zip(picked, key_segs):
+                        score = jnp.dot(
+                            query, key_s[b, lines, :], preferred_element_type=jnp.float32
+                        )
+                        scores.append(jnp.where(query_seg == key_seg, score, NEG))
+                    peak = functools.reduce(jnp.maximum, scores)
+                    peak = jnp.max(peak, axis=1, keepdims=True)
+                    accum = jnp.zeros((rows, wide), jnp.float32)
+                    if follows:
+                        state = before[which, h]
+                        old = state[:, wide : wide + 1]
+                        peak = jnp.maximum(peak, old)
+                        accum = state[:, :wide] * jnp.exp2((old - peak) * factor)
+                    for b, score in zip(picked, scores):
+                        weights = jnp.exp2((score - peak) * factor).astype(jnp.bfloat16)
+                        accum += lax.dot_general(
+                            weights,
+                            value_s[b, h],
+                            (((1,), (1,)), ((), ())),
+                            preferred_element_type=jnp.float32,
+                        )
+                    finish(h, peak, accum)
+
+                def two_heads(i, carry):
+                    one_head(2 * i)
+                    one_head(2 * i + 1)
+                    return carry
+
+                lax.fori_loop(0, HALF // 2, two_heads, 0)
+
+
+def attention(where, mask, segs, queries, kinds, blocks, numbers, before, which, ends):
+    part, rows = queries[0].shape
     hdim = part // HALF
+    wide = hdim + 16
+    if ends:
+        out = jax.ShapeDtypeStruct((part, rows), jnp.bfloat16)
+    else:
+        out = jax.ShapeDtypeStruct((len(kinds), HALF, rows, 128), jnp.float32)
     return pl.pallas_call(
-        attention_kernel,
-        out_shape=[jax.ShapeDtypeStruct((part, rows), jnp.bfloat16)] * 2,
-        in_specs=[smem()] * 4 + [vmem()] * (3 + WINDOW),
-        out_specs=[vmem()] * 2,
+        functools.partial(attention_kernel, kinds, numbers, which, ends),
+        out_shape=out,
+        in_specs=[smem()] * 2
+        + [vmem()] * (1 + len(kinds) + len(numbers) + (which is not None)),
+        out_specs=vmem(),
         scratch_shapes=[
-            pltpu.VMEM((2, part, rows), jnp.bfloat16),
-            pltpu.VMEM((HALF, WINDOW, rows, hdim), jnp.bfloat16),
-            pltpu.VMEM((WINDOW, part, rows), jnp.bfloat16),
-            pltpu.VMEM((WINDOW, rows, 128), jnp.float32),
-            pltpu.VMEM((2, part, rows), jnp.bfloat16),
+            pltpu.VMEM((HALF, rows, hdim), jnp.bfloat16),
+            pltpu.VMEM((len(numbers), part, rows), jnp.bfloat16),
+            pltpu.VMEM((len(numbers), HALF, wide, rows), jnp.bfloat16),
+            pltpu.SMEM((len(numbers) + 1,), jnp.int32),
         ],
-        compiler_params=limit(24),
-    )(place, half, low, count, segs, own_q, other_q, *blocks)
+        compiler_params=limit(16),
+        cost_estimate=pl.CostEstimate(
+            flops=2_000_000_000 * len(kinds), bytes_accessed=2_000_000, transcendentals=1_000_000
+        ),
+    )(where, mask, segs, *queries, *blocks, *(() if which is None else (before,)))
 
 
 def project_kernel(
-    capacity, half_ref, meta_ref, own_ref, other_ref, weight_ref, tokens_ref, out_ref
+    capacity, where_ref, meta_ref, own_ref, other_ref, weight_ref, tokens_ref, out_ref
 ):
     slots = out_ref.shape[0]
     rows, width = tokens_ref.shape
     part = own_ref.shape[0]
-    half = half_ref[0]
+    half = where_ref[0] % 2
     hidden = tokens_ref[...].astype(jnp.float32)
     for ref, which in ((own_ref, half), (other_ref, 1 - half)):
         hidden += lax.dot_general(
@@ -203,7 +271,7 @@
         ).astype(jnp.bfloat16)
 
 
-def project(half, meta, own, other, out_weight, tokens, slots, capacity):
+def project(where, meta, own, other, out_weight, tokens, slots, capacity):
     rows, width = tokens.shape
     return pl.pallas_call(
         functools.partial(project_kernel, float(capacity)),
@@ -211,7 +279,7 @@
         in_specs=[smem()] + [vmem()] * 5,
         out_specs=vmem(),
         compiler_params=limit(24),
-    )(half, meta, own, other, out_weight, tokens)
+    )(where, meta, own, other, out_weight, tokens)
 
 
 def place_kernel(arrived_ref, out_hbm, held, sems):
@@ -255,8 +323,6 @@
     width = tokens.shape[1]
     nblocks = lax.axis_size("blk")
     block_index = lax.axis_index("blk")
-    half = block_index % 2
-    pair = block_index - half
     mrows = rows // 4
     capacity = 2 * mrows
     pair_rows = max(2, 2 * mrows // nblocks)
@@ -276,9 +342,9 @@
         lax.ppermute, axis_name="blk", perm=route(lambda i: -2 if i % 2 else 2)
     )
 
-    halves = half[None].astype(jnp.int32)
+    where = block_index[None].astype(jnp.int32)
     own_q, own_kv, swap_q, swap_kv, meta = prepare(
-        halves, owners[None, :], offsets[None, :], queries, keys, values, pair_rows
+        where, owners[None, :], offsets[None, :], queries, keys, values, pair_rows
     )
     other_kv = swap(swap_kv)
     ahead_own = ahead(own_kv)
@@ -288,25 +354,15 @@
     ahead_other = ahead(other_kv)
     ahead_far = ahead(ahead_own)
     back_far = back(back_other)
-    blocks = (own_kv, other_kv, ahead_own, ahead_other, back_own, back_other, ahead_far, back_far)
-    places = jnp.where(
-        half == 0,
-        jnp.array([3, 4, 5, 6, 1, 2, 7, 0], jnp.int32),
-        jnp.array([4, 3, 2, 1, 6, 5, 0, 7], jnp.int32),
-    )
-
-    segs = jnp.pad(segment_ids.reshape(nblocks, 1, rows), ((SPAN, SPAN), (0, 0), (0, 0)))
-    segs = lax.dynamic_slice_in_dim(segs, pair, WINDOW, 0).astype(jnp.float32)
-    mask = lax.dynamic_slice_in_dim(block_mask, pair, 2, 0)
-    block = pair + jnp.arange(2)[:, None]
-    other = jnp.arange(nblocks)[None, :]
-    present = (mask > 0) & (jnp.abs(block - other) <= SPAN)
-    low = jnp.min(jnp.where(present, other, nblocks), axis=1) - pair + SPAN
-    count = jnp.sum(present.astype(jnp.int32), axis=1)
-
-    own, other = attention(places, halves, low, count, segs, own_q, other_q, blocks)
+    near = (own_kv, other_kv, ahead_own, back_own)
+    far = (ahead_other, back_other, ahead_far, back_far)
+
+    fixed = (where, block_mask, segment_ids[None, :])
+    state = attention(*fixed, (own_q, other_q), (0, 1), near, (0, 1, 2, 3), None, None, False)
+    other = attention(*fixed, (other_q,), (1,), far, (4, 5, 6, 7), state, 1, True)
     other = swap(other)
-    outgoing = project(halves, meta, own, other, out_weight, tokens, slots, capacity)
+    own = attention(*fixed, (own_q,), (0,), far, (4, 5, 6, 7), state, 0, True)
+    outgoing = project(where, meta, own, other, out_weight, tokens, slots, capacity)
     arrived = lax.all_to_all(outgoing, "blk", split_axis=0, concat_axis=0, tiled=True)
     return place(arrived, capacity, 4 * width)
 

time: 87.3 us -> 86.6 us (level)
  waiting for transfers between devices: 16.8 us -> 11.6 us
  Pallas kernels: 13.6 us -> 17 us
  other arithmetic: 2.3 us -> 0 us
  local copies, waits for them, and re-layouts: 1.9 us -> 3.3 us
  starting transfers between devices: 19.6 us -> 21 us
  blocking collectives: 32.5 us -> 33.4 us
    ppermute x1, waiting for transfers between devices: 4.99 us -> 0.32 us  [per_device(): other = swap(other)]
    ppermute x1, waiting for transfers between devices: 4.33 us -> 0.01 us  [per_device(): ahead_far = ahead(ahead_own)]
    ppermute x1, waiting for transfers between devices: 2.75 us -> 6.63 us  [per_device(): other_kv = swap(swap_kv)]
    pallas_call x1 -> x3, Pallas kernels: 7.76 us -> 11.1 us  [attention(): pl.pallas_call(functools.partial(attention_kernel, kinds, numbers, which,...]
    ppermute x1, waiting for transfers between devices: 3.24 us -> 0.01 us  [per_device(): ahead_other = ahead(other_kv)]
    ppermute x1, waiting for transfers between devices: 0.01 us -> 2.71 us  [per_device(): back_own = back(own_kv)]
    ppermute x1, starting transfers between devices: 0.39 us -> 2.4 us  [per_device(): other = swap(other)]
    unnamed x10 -> x20, local copies, waits for them, and re-layouts: 1.9 us -> 3.3 us
  transfers between devices with their start and end apart: 9 -> 9, of which waited for: 5 -> 4; matrix products, arithmetic and copies ran while one was open for 3% -> 0% of each run, Pallas kernels for 0% -> 10%
where the time goes in v8:
time: 86.6 us
  blocking collectives  33.4 us (39%)
  starting transfers between devices  21 us (24%)
  Pallas kernels  17 us (20%)
  waiting for transfers between devices  11.6 us (13%)
  local copies, waits for them, and re-layouts  3.3 us (4%)
    all_to_all x1, blocking collectives, per_device(): lax.all_to_all(outgoing, 'blk', split_axis=0, concat_axis=0, tiled=True)  33.4 us
    pallas_call x3, Pallas kernels, attention(): pl.pallas_call(functools.partial(attention_kernel, kinds, numbers, which,...  11.1 us
    ppermute x1, waiting for transfers between devices, per_device(): other_kv = swap(swap_kv)  6.63 us
    ppermute x1, starting transfers between devices, per_device(): back_far = back(back_other)  4.39 us
    ppermute x1, starting transfers between devices, per_device(): back_other = back(other_kv)  3.71 us
    ppermute x1, starting transfers between devices, per_device(): back_own = back(own_kv)  3.48 us
    unnamed x20, local copies, waits for them, and re-layouts  3.3 us
    ppermute x1, starting transfers between devices, per_device(): other_kv = swap(swap_kv)  3.03 us
  transfers between devices with their start and end apart: 9, of which 4 were waited for; matrix products, arithmetic and copies ran while one was open for 0% of the time, Pallas kernels for 10%

profile of v8, /device:TPU:0, one launch (start us, length us, event | category | flops | bytes accessed | tf_op | source)
XLA Modules:
  0.0 86.6 jit_solution(15748460705619088161)
XLA Ops:
  0.0 3.0 %shard_map.91 = (bf16[320,256]{1,0:T(8,128)(2,1)}, bf16[640,256]{1,0:T(8,128)(2,1)}, bf16[320,256]{1,0:T(8,128)(2,1)}, bf16[640,256]{1,0:T(8,128)(2,1)}, f32[8,256]{1,0:T(8,128)}) custom-call(s32[1]{0:T(128)} %bitcast.where_ref, s32[1,64]{1,0:T(1,128)} %bitcast.11, s32[1,64]{1,0:T(1,128)} %bitcast.12, bf16[256,640]{1,0:T(8,128)(2,1)} %q_hbm.1, ...), custom_call_target="tpu_custom_call" | custom-call | tf_op jit(solution)/shard_map/pallas_call | solution.py:83
  3.0 3.0 %collective-permute-start = (bf16[640,256]{1,0:T(8,128)(2,1)}, bf16[640,256]{1,0:T(8,128)(2,1)S(1)}, u32[]{:S(2)}, u32[]{:S(2)}) collective-permute-start(bf16[640,256]{1,0:T(8,128)(2,1)} %get-tuple-element.12), channel_id=1, source_target_pairs={{0,4},{4,0},{8,12},{12,8},{16,20},{20,16},{24,28},{28,24},{1,5},{5... | collective-permute-start | bytes 983048 | tf_op jit(solution)/shard_map/ppermute | solution.py:349
  6.0 1.3 %collective-permute-start.3 = (bf16[640,256]{1,0:T(8,128)(2,1)}, bf16[640,256]{1,0:T(8,128)(2,1)S(1)}, u32[]{:S(2)}, u32[]{:S(2)}) collective-permute-start(bf16[640,256]{1,0:T(8,128)(2,1)} %get-tuple-element.13.refs_2_), channel_id=1, source_target_pairs={{4,12},{8,0},{12,20},{16,8},{20,28},{24,16},{5,13},{9,1},{13,21},{... | collective-permute-start | bytes 983048 | tf_op jit(solution)/shard_map/ppermute | solution.py:350
  7.3 6.6 %collective-permute-done.refs_3_ = bf16[640,256]{1,0:T(8,128)(2,1)S(1)} collective-permute-done((bf16[640,256]{1,0:T(8,128)(2,1)}, bf16[640,256]{1,0:T(8,128)(2,1)S(1)}, u32[]{:S(2)}, u32[]{:S(2)}) %collective-permute-start) | collective-permute-done | bytes 327712 | tf_op jit(solution)/shard_map/ppermute | solution.py:349
  13.9 3.7 %collective-permute-start.2 = (bf16[640,256]{1,0:T(8,128)(2,1)S(1)}, bf16[640,256]{1,0:T(8,128)(2,1)S(1)}, u32[]{:S(2)}, u32[]{:S(2)}) collective-permute-start(bf16[640,256]{1,0:T(8,128)(2,1)S(1)} %collective-permute-done.refs_3_), channel_id=1, source_target_pairs={{0,8},{8,16},{12,4},{16,24},{20,12},{28,20},{1,9},{9,17},{13,5},{1... | collective-permute-start | bytes 983048 | tf_op jit(solution)/shard_map/ppermute | solution.py:353
  17.6 3.5 %collective-permute-start.7 = (bf16[640,256]{1,0:T(8,128)(2,1)}, bf16[640,256]{1,0:T(8,128)(2,1)S(1)}, u32[]{:S(2)}, u32[]{:S(2)}) collective-permute-start(bf16[640,256]{1,0:T(8,128)(2,1)} %get-tuple-element.13.refs_2_), channel_id=1, source_target_pairs={{0,8},{8,16},{12,4},{16,24},{20,12},{28,20},{1,9},{9,17},{13,5},{1... | collective-permute-start | bytes 983048 | tf_op jit(solution)/shard_map/ppermute | solution.py:351
  21.1 0.1 collective-permute-start.6
  21.2 1.3 %collective-permute-start.1 = (bf16[640,256]{1,0:T(8,128)(2,1)S(1)}, bf16[640,256]{1,0:T(8,128)(2,1)S(1)}, u32[]{:S(2)}, u32[]{:S(2)}) collective-permute-start(bf16[640,256]{1,0:T(8,128)(2,1)S(1)} %collective-permute-done.refs_3_), channel_id=1, source_target_pairs={{4,12},{8,0},{12,20},{16,8},{20,28},{24,16},{5,13},{9,1},{13,21},{... | collective-permute-start | bytes 983048 | tf_op jit(solution)/shard_map/ppermute | solution.py:354
  22.5 1.3 %collective-permute-start.4 = (bf16[640,256]{1,0:T(8,128)(2,1)S(1)}, bf16[640,256]{1,0:T(8,128)(2,1)S(1)}, u32[]{:S(2)}, u32[]{:S(2)}) collective-permute-start(bf16[640,256]{1,0:T(8,128)(2,1)S(1)} %collective-permute-done.3.refs_4_), channel_id=1, source_target_pairs={{4,12},{8,0},{12,20},{16,8},{20,28},{24,16},{5,13},{9,1},{13,21},{... | collective-permute-start | bytes 983048 | tf_op jit(solution)/shard_map/ppermute | solution.py:355
  23.8 1.9 %collective-permute-done.2.refs_2_ = bf16[640,256]{1,0:T(8,128)(2,1)S(1)} collective-permute-done((bf16[640,256]{1,0:T(8,128)(2,1)S(1)}, bf16[640,256]{1,0:T(8,128)(2,1)S(1)}, u32[]{:S(2)}, u32[]{:S(2)}) %collective-permute-start.2) | collective-permute-done | bytes 327712 | tf_op jit(solution)/shard_map/ppermute | solution.py:353
  25.8 4.4 %collective-permute-start.5 = (bf16[640,256]{1,0:T(8,128)(2,1)S(1)}, bf16[640,256]{1,0:T(8,128)(2,1)S(1)}, u32[]{:S(2)}, u32[]{:S(2)}) collective-permute-start(bf16[640,256]{1,0:T(8,128)(2,1)S(1)} %collective-permute-done.2.refs_2_), channel_id=1, source_target_pairs={{0,8},{8,16},{12,4},{16,24},{20,12},{28,20},{1,9},{9,17},{13,5},{1... | collective-permute-start | bytes 983048 | tf_op jit(solution)/shard_map/ppermute | solution.py:356
  30.2 2.7 %collective-permute-done.7.refs_5_ = bf16[640,256]{1,0:T(8,128)(2,1)S(1)} collective-permute-done((bf16[640,256]{1,0:T(8,128)(2,1)}, bf16[640,256]{1,0:T(8,128)(2,1)S(1)}, u32[]{:S(2)}, u32[]{:S(2)}) %collective-permute-start.7) | collective-permute-done | bytes 327712 | tf_op jit(solution)/shard_map/ppermute | solution.py:351
  32.9 1.0 %copy-done.3 = bf16[640,256]{1,0:T(8,128)(2,1)S(1)} copy-done((bf16[640,256]{1,0:T(8,128)(2,1)S(1)}, bf16[640,256]{1,0:T(8,128)(2,1)}, u32[]{:S(2)}) %copy-start.3) | copy-done | bytes 327704
  33.9 0.9 %copy-done.4 = bf16[320,256]{1,0:T(8,128)(2,1)S(1)} copy-done((bf16[320,256]{1,0:T(8,128)(2,1)S(1)}, bf16[320,256]{1,0:T(8,128)(2,1)}, u32[]{:S(2)}) %copy-start.4) | copy-done | bytes 163864
  34.8 0.7 copy-done.6
  35.5 0.7 copy-done.8
  36.2 5.4 %shard_map.92.refs_5_ = f32[2,4,256,128]{3,2,1,0:T(8,128)S(1)} custom-call(s32[1]{0:T(128)} %bitcast.where_ref, s32[8,8]{1,0:T(8,128)S(1)} %copy-done.8, s32[1,2048]{1,0:T(1,128)S(1)} %bitcast.8, bf16[320,256]{1,0:T(8,128)(2,1)S(1)} %copy-done.4, bf16[320,256]{1,0:T(8,128)(2,1)S(1)} %collective-permute-done.6.refs_1_.refs_0_, ...), custom_call_target="tpu_custom_call" | custom-call | flops 4000000000 | bytes 2000000 | tf_op jit(solution)/shard_map/pallas_call | solution.py:225
  41.6 2.8 %shard_map.94 = bf16[320,256]{1,0:T(8,128)(2,1)S(1)} custom-call(s32[1]{0:T(128)} %bitcast.where_ref, s32[8,8]{1,0:T(8,128)S(1)} %copy-done.9, s32[1,2048]{1,0:T(1,128)S(1)} %bitcast.9, bf16[320,256]{1,0:T(8,128)(2,1)S(1)} %collective-permute-done.6.refs_1_.refs_0_, bf16[640,256]{1,0:T(8,128)(2,1)S(1)} %collective-permute-done.1.refs_1_, ...), custom_call_target="tpu_custom_call" | custom-call | flops 2000000000 | bytes 2000000 | tf_op jit(solution)/shard_map/pallas_call | solution.py:225
  44.4 2.4 %collective-permute-start.8 = (bf16[320,256]{1,0:T(8,128)(2,1)S(1)}, bf16[320,256]{1,0:T(8,128)(2,1)S(1)}, u32[]{:S(2)}, u32[]{:S(2)}) collective-permute-start(bf16[320,256]{1,0:T(8,128)(2,1)S(1)} %shard_map.94), channel_id=1, source_target_pairs={{0,4},{4,0},{8,12},{12,8},{16,20},{20,16},{24,28},{28,24},{1,5},{5... | collective-permute-start | bytes 491528 | tf_op jit(solution)/shard_map/ppermute | solution.py:363
  46.8 3.0 %shard_map.93.own_ref = bf16[320,256]{1,0:T(8,128)(2,1)S(1)} custom-call(s32[1]{0:T(128)} %bitcast.where_ref, s32[8,8]{1,0:T(8,128)S(1)} %copy-done.9, s32[1,2048]{1,0:T(1,128)S(1)} %bitcast.10, bf16[320,256]{1,0:T(8,128)(2,1)S(1)} %copy-done.5, bf16[640,256]{1,0:T(8,128)(2,1)S(1)} %collective-permute-done.1.refs_1_, ...), custom_call_target="tpu_custom_call" | custom-call | flops 2000000000 | bytes 2000000 | tf_op jit(solution)/shard_map/pallas_call | solution.py:225
  49.8 0.3 collective-permute-done.8.other_ref
  50.2 1.5 %shard_map.95 = bf16[128,5248]{1,0:T(8,128)(2,1)S(1)} custom-call(s32[1]{0:T(128)} %bitcast.where_ref, f32[8,256]{1,0:T(8,128)S(1)} %copy-done.2, bf16[320,256]{1,0:T(8,128)(2,1)S(1)} %shard_map.93.own_ref, bf16[320,256]{1,0:T(8,128)(2,1)S(1)} %collective-permute-done.8.other_ref, bf16[640,1280]{1,0:T(8,128)(2,1)S(1)} %copy-done, bf16[256,1280]{1,0:T(8,128)(2,1)S(1)} %copy-done.1), custom_call_target="tpu_custom_call" | custom-call | tf_op jit(solution)/shard_map/pallas_call | solution.py:276
  51.6 33.4 %all_to_all.11 = bf16[8,16,5248]{2,1,0:T(8,128)(2,1)S(1)} all-to-all(bf16[8,16,5248]{2,1,0:T(8,128)(2,1)S(1)} %bitcast.6), channel_id=1, replica_groups=mesh['blk'=8,'rep'=4] {'blk'}, dimensions={0} | all-to-all | bytes 2686976 | tf_op jit(solution)/shard_map/all_to_all | solution.py:366
  85.0 1.4 %shard_map.96 = bf16[128,5120]{1,0:T(8,128)(2,1)} custom-call(bf16[128,5248]{1,0:T(8,128)(2,1)S(1)} %bitcast.7), custom_call_target="tpu_custom_call" | custom-call | tf_op jit(solution)/shard_map/pallas_call | solution.py:308
  (21 shorter events, 0.0 us)
Async XLA Ops:
  3.0 11.0 %collective-permute-start = (bf16[640,256]{1,0:T(8,128)(2,1)}, bf16[640,256]{1,0:T(8,128)(2,1)S(1)}, u32[]{:S(2)}, u32[]{:S(2)}) collective-permute-start(bf16[640,256]{1,0:T(8,128)(2,1)} %get-tuple-element.12), channel_id=1, source_target_pairs={{0,4},{4,0},{8,12},{12,8},{16,20},{20,16},{24,28},{28,24},{1,5},{5... | collective-permute-start | bytes 983048 | tf_op jit(solution)/shard_map/ppermute | solution.py:349
  6.0 16.5 %collective-permute-start.3 = (bf16[640,256]{1,0:T(8,128)(2,1)}, bf16[640,256]{1,0:T(8,128)(2,1)S(1)}, u32[]{:S(2)}, u32[]{:S(2)}) collective-permute-start(bf16[640,256]{1,0:T(8,128)(2,1)} %get-tuple-element.13.refs_2_), channel_id=1, source_target_pairs={{4,12},{8,0},{12,20},{16,8},{20,28},{24,16},{5,13},{9,1},{13,21},{... | collective-permute-start | bytes 983048 | tf_op jit(solution)/shard_map/ppermute | solution.py:350
  13.9 11.8 %collective-permute-start.2 = (bf16[640,256]{1,0:T(8,128)(2,1)S(1)}, bf16[640,256]{1,0:T(8,128)(2,1)S(1)}, u32[]{:S(2)}, u32[]{:S(2)}) collective-permute-start(bf16[640,256]{1,0:T(8,128)(2,1)S(1)} %collective-permute-done.refs_3_), channel_id=1, source_target_pairs={{0,8},{8,16},{12,4},{16,24},{20,12},{28,20},{1,9},{9,17},{13,5},{1... | collective-permute-start | bytes 983048 | tf_op jit(solution)/shard_map/ppermute | solution.py:353
  17.6 15.3 %collective-permute-start.7 = (bf16[640,256]{1,0:T(8,128)(2,1)}, bf16[640,256]{1,0:T(8,128)(2,1)S(1)}, u32[]{:S(2)}, u32[]{:S(2)}) collective-permute-start(bf16[640,256]{1,0:T(8,128)(2,1)} %get-tuple-element.13.refs_2_), channel_id=1, source_target_pairs={{0,8},{8,16},{12,4},{16,24},{20,12},{28,20},{1,9},{9,17},{13,5},{1... | collective-permute-start | bytes 983048 | tf_op jit(solution)/shard_map/ppermute | solution.py:351
  21.1 9.0 %collective-permute-start.6 = (bf16[320,256]{1,0:T(8,128)(2,1)}, bf16[320,256]{1,0:T(8,128)(2,1)S(1)}, u32[]{:S(2)}, u32[]{:S(2)}) collective-permute-start(bf16[320,256]{1,0:T(8,128)(2,1)} %get-tuple-element.14), channel_id=1, source_target_pairs={{0,4},{4,0},{8,12},{12,8},{16,20},{20,16},{24,28},{28,24},{1,5},{5... | collective-permute-start | bytes 491528 | tf_op jit(solution)/shard_map/ppermute | solution.py:352
  21.2 20.4 %collective-permute-start.1 = (bf16[640,256]{1,0:T(8,128)(2,1)S(1)}, bf16[640,256]{1,0:T(8,128)(2,1)S(1)}, u32[]{:S(2)}, u32[]{:S(2)}) collective-permute-start(bf16[640,256]{1,0:T(8,128)(2,1)S(1)} %collective-permute-done.refs_3_), channel_id=1, source_target_pairs={{4,12},{8,0},{12,20},{16,8},{20,28},{24,16},{5,13},{9,1},{13,21},{... | collective-permute-start | bytes 983048 | tf_op jit(solution)/shard_map/ppermute | solution.py:354
  22.5 19.0 %collective-permute-start.4 = (bf16[640,256]{1,0:T(8,128)(2,1)S(1)}, bf16[640,256]{1,0:T(8,128)(2,1)S(1)}, u32[]{:S(2)}, u32[]{:S(2)}) collective-permute-start(bf16[640,256]{1,0:T(8,128)(2,1)S(1)} %collective-permute-done.3.refs_4_), channel_id=1, source_target_pairs={{4,12},{8,0},{12,20},{16,8},{20,28},{24,16},{5,13},{9,1},{13,21},{... | collective-permute-start | bytes 983048 | tf_op jit(solution)/shard_map/ppermute | solution.py:355
  25.8 15.8 %collective-permute-start.5 = (bf16[640,256]{1,0:T(8,128)(2,1)S(1)}, bf16[640,256]{1,0:T(8,128)(2,1)S(1)}, u32[]{:S(2)}, u32[]{:S(2)}) collective-permute-start(bf16[640,256]{1,0:T(8,128)(2,1)S(1)} %collective-permute-done.2.refs_2_), channel_id=1, source_target_pairs={{0,8},{8,16},{12,4},{16,24},{20,12},{28,20},{1,9},{9,17},{13,5},{1... | collective-permute-start | bytes 983048 | tf_op jit(solution)/shard_map/ppermute | solution.py:356
  32.9 1.0 %copy-start.3 = (bf16[640,256]{1,0:T(8,128)(2,1)S(1)}, bf16[640,256]{1,0:T(8,128)(2,1)}, u32[]{:S(2)}) copy-start(bf16[640,256]{1,0:T(8,128)(2,1)} %get-tuple-element.13.refs_2_) | copy-start | bytes 983044
  33.9 0.9 %copy-start.4 = (bf16[320,256]{1,0:T(8,128)(2,1)S(1)}, bf16[320,256]{1,0:T(8,128)(2,1)}, u32[]{:S(2)}) copy-start(bf16[320,256]{1,0:T(8,128)(2,1)} %get-tuple-element.11.refs_0_) | copy-start | bytes 491524
  34.8 0.7 copy-start.6
  35.5 0.7 copy-start.8
  36.2 5.4 %copy-start.7 = (s32[2048]{0:T(1024)S(1)}, s32[2048]{0:T(1024)}, u32[]{:S(2)}) copy-start(s32[2048]{0:T(1024)} %param.9) | copy-start | bytes 24580
  36.2 5.4 %copy-start.9 = (s32[8,8]{1,0:T(8,128)S(1)}, s32[8,8]{1,0:T(8,128)}, u32[]{:S(2)}) copy-start(s32[8,8]{1,0:T(8,128)} %mask_ref.5) | copy-start | bytes 772
  41.5 5.3 %copy-start.5 = (bf16[320,256]{1,0:T(8,128)(2,1)S(1)}, bf16[320,256]{1,0:T(8,128)(2,1)}, u32[]{:S(2)}) copy-start(bf16[320,256]{1,0:T(8,128)(2,1)} %get-tuple-element.11.refs_0_) | copy-start | bytes 491524
  44.4 5.7 %copy-start = (bf16[640,1280]{1,0:T(8,128)(2,1)S(1)}, bf16[640,1280]{1,0:T(8,128)(2,1)}, u32[]{:S(2)}) copy-start(bf16[640,1280]{1,0:T(8,128)(2,1)} %weight_ref.1) | copy-start | bytes 4915204
  44.4 5.7 %copy-start.1 = (bf16[256,1280]{1,0:T(8,128)(2,1)S(1)}, bf16[256,1280]{1,0:T(8,128)(2,1)}, u32[]{:S(2)}) copy-start(bf16[256,1280]{1,0:T(8,128)(2,1)} %tokens_ref.1) | copy-start | bytes 1966084
  44.4 5.7 %copy-start.2 = (f32[8,256]{1,0:T(8,128)S(1)}, f32[8,256]{1,0:T(8,128)}, u32[]{:S(2)}) copy-start(f32[8,256]{1,0:T(8,128)} %get-tuple-element.10.meta_ref) | copy-start | bytes 24580
  44.4 5.7 %collective-permute-start.8 = (bf16[320,256]{1,0:T(8,128)(2,1)S(1)}, bf16[320,256]{1,0:T(8,128)(2,1)S(1)}, u32[]{:S(2)}, u32[]{:S(2)}) collective-permute-start(bf16[320,256]{1,0:T(8,128)(2,1)S(1)} %shard_map.94), channel_id=1, source_target_pairs={{0,4},{4,0},{8,12},{12,8},{16,20},{20,16},{24,28},{28,24},{1,5},{5... | collective-permute-start | bytes 491528 | tf_op jit(solution)/shard_map/ppermute | solution.py:363

commit v9 on v8

--- a/solution.py
+++ b/solution.py
@@ -31,36 +31,14 @@
     return pltpu.CompilerParams(vmem_limit_bytes=mib * MIB)
 
 
-def prepare_kernel(
-    pair_rows, where_ref, owners_ref, offsets_ref, q_hbm, k_hbm, v_hbm,
-    own_q, own_kv, swap_q, swap_kv, meta_ref, held, turned, sems,
-):
-    rows, features = q_hbm.shape
-    part = features // 2
-    mrows = rows // 4
+def prepare_kernel(where_ref, q_hbm, k_hbm, v_hbm, own_q, own_kv, swap_q, swap_kv, held, turned, sems):
+    part = q_hbm.shape[1] // 2
     loads = [
         pltpu.make_async_copy(ref, held.at[i], sems.at[i])
         for i, ref in enumerate((k_hbm, v_hbm, q_hbm))
     ]
     for load in loads:
         load.start()
-
-    owner = jnp.broadcast_to(owners_ref[...].astype(jnp.float32), (mrows, mrows))
-    earlier = lax.broadcasted_iota(jnp.int32, (mrows, mrows), 0)
-    later = lax.broadcasted_iota(jnp.int32, (mrows, mrows), 1)
-    column = jnp.sum(jnp.where(earlier == later, owner, 0.0), axis=1, keepdims=True)
-    ahead = jnp.where((owner == column) & (earlier < later), 1.0, 0.0)
-    slot = owner[:1] * pair_rows + jnp.sum(ahead, axis=0, keepdims=True)
-    line = lax.broadcasted_iota(jnp.int32, (8, mrows), 0)
-    offset = offsets_ref[...].astype(jnp.float32)
-    meta = jnp.where(line == 0, slot, jnp.where(line == 1, offset, 0.0))
-    row = lax.broadcasted_iota(jnp.int32, (mrows, rows), 0)
-    patch = lax.broadcasted_iota(jnp.int32, (mrows, rows), 1)
-    spread = jnp.where(patch // 4 == row, 1.0, 0.0).astype(jnp.bfloat16)
-    meta_ref[...] = jnp.dot(
-        meta.astype(jnp.bfloat16), spread, preferred_element_type=jnp.float32
-    )
-
     half = where_ref[0] % 2
     mine = pl.multiple_of(half * part, 16)
     other = pl.multiple_of((1 - half) * part, 16)
@@ -75,23 +53,23 @@
             swap_q[...] = turned[i, pl.ds(other, part), :]
 
 
-def prepare(where, owners, offsets, queries, keys, values, pair_rows):
+def prepare(where, queries, keys, values):
     rows, features = queries.shape
     part = features // 2
     single = jax.ShapeDtypeStruct((part, rows), queries.dtype)
     double = jax.ShapeDtypeStruct((2 * part, rows), queries.dtype)
     return pl.pallas_call(
-        functools.partial(prepare_kernel, pair_rows),
-        out_shape=[single, double, single, double, jax.ShapeDtypeStruct((8, rows), jnp.float32)],
-        in_specs=[smem()] + [vmem()] * 2 + [anywhere()] * 3,
-        out_specs=[vmem()] * 5,
+        prepare_kernel,
+        out_shape=[single, double, single, double],
+        in_specs=[smem()] + [anywhere()] * 3,
+        out_specs=[vmem()] * 4,
         scratch_shapes=[
             pltpu.VMEM((3, rows, features), queries.dtype),
             pltpu.VMEM((3, features, rows), queries.dtype),
             pltpu.SemaphoreType.DMA((3,)),
         ],
-        compiler_params=limit(60),
-    )(where, owners, offsets, queries, keys, values)
+        compiler_params=limit(53),
+    )(where, queries, keys, values)
 
 
 PLACES = ((3, 1), (4, -1), (5, -3), (1, 5), (6, -5), (2, 3), (7, -7), (0, 7))
@@ -242,10 +220,24 @@
 
 
 def project_kernel(
-    capacity, where_ref, meta_ref, own_ref, other_ref, weight_ref, tokens_ref, out_ref
+    pair_rows, where_ref, owners_ref, offsets_ref, own_ref, other_ref, weight_ref, tokens_ref, out_ref
 ):
     slots = out_ref.shape[0]
     rows, width = tokens_ref.shape
+    mrows = rows // 4
+    capacity = 2 * mrows
+    owner = jnp.broadcast_to(owners_ref[...].astype(jnp.float32), (mrows, mrows))
+    earlier = lax.broadcasted_iota(jnp.int32, (mrows, mrows), 0)
+    later = lax.broadcasted_iota(jnp.int32, (mrows, mrows), 1)
+    column = jnp.sum(jnp.where(earlier == later, owner, 0.0), axis=1, keepdims=True)
+    ahead = jnp.where((owner == column) & (earlier < later), 1.0, 0.0)
+    slot = owner[:1] * pair_rows + jnp.sum(ahead, axis=0, keepdims=True)
+    line = lax.broadcasted_iota(jnp.int32, (16, mrows), 0)
+    meta = jnp.where(line == 0, slot, jnp.where(line == 1, offsets_ref[...].astype(jnp.float32), 0.0))
+    row = lax.broadcasted_iota(jnp.int32, (mrows, rows), 0)
+    patch = lax.broadcasted_iota(jnp.int32, (mrows, rows), 1)
+    spread = jnp.where(patch // 4 == row, 1.0, 0.0).astype(jnp.bfloat16)
+    meta = jnp.dot(meta.astype(jnp.bfloat16), spread, preferred_element_type=jnp.float32)
     part = own_ref.shape[0]
     half = where_ref[0] % 2
     hidden = tokens_ref[...].astype(jnp.float32)
@@ -260,9 +252,9 @@
     slot = lax.broadcasted_iota(jnp.int32, (slots, rows), 0).astype(jnp.float32)
     quarter = lax.broadcasted_iota(jnp.int32, (1, rows), 1) % 4
     for j in range(4):
-        mine = jnp.where(quarter == j, meta_ref[:1], -1.0) == slot
+        mine = jnp.where(quarter == j, meta[:1], -1.0) == slot
         if j == 0:
-            offset = jnp.where(mine, meta_ref[1:2] - capacity, 0.0)
+            offset = jnp.where(mine, meta[1:2] - capacity, 0.0)
             offset = capacity + jnp.sum(offset, axis=1, keepdims=True)
             out_ref[:, 4 * width :] = jnp.broadcast_to(offset, (slots, 128)).astype(jnp.bfloat16)
         pick = jnp.where(mine, 1.0, 0.0).astype(jnp.bfloat16)
@@ -271,15 +263,15 @@
         ).astype(jnp.bfloat16)
 
 
-def project(where, meta, own, other, out_weight, tokens, slots, capacity):
+def project(where, owners, offsets, own, other, out_weight, tokens, slots, pair_rows):
     rows, width = tokens.shape
     return pl.pallas_call(
-        functools.partial(project_kernel, float(capacity)),
+        functools.partial(project_kernel, pair_rows),
         out_shape=jax.ShapeDtypeStruct((slots, 4 * width + 128), jnp.bfloat16),
-        in_specs=[smem()] + [vmem()] * 5,
+        in_specs=[smem()] + [vmem()] * 6,
         out_specs=vmem(),
         compiler_params=limit(24),
-    )(where, meta, own, other, out_weight, tokens)
+    )(where, owners, offsets, own, other, out_weight, tokens)
 
 
 def place_kernel(arrived_ref, out_hbm, held, sems):
@@ -343,14 +335,13 @@
     )
 
     where = block_index[None].astype(jnp.int32)
-    own_q, own_kv, swap_q, swap_kv, meta = prepare(
-        where, owners[None, :], offsets[None, :], queries, keys, values, pair_rows
-    )
+    own_q, own_kv, swap_q, swap_kv = prepare(where, queries, keys, values)
     other_kv = swap(swap_kv)
     ahead_own = ahead(own_kv)
     back_own = back(own_kv)
     other_q = swap(swap_q)
-    back_other = back(other_kv)
+    ready, back_own = lax.optimization_barrier((other_kv, back_own))
+    back_other = back(ready)
     ahead_other = ahead(other_kv)
     ahead_far = ahead(ahead_own)
     back_far = back(back_other)
@@ -362,7 +353,9 @@
     other = attention(*fixed, (other_q,), (1,), far, (4, 5, 6, 7), state, 1, True)
     other = swap(other)
     own = attention(*fixed, (own_q,), (0,), far, (4, 5, 6, 7), state, 0, True)
-    outgoing = project(where, meta, own, other, out_weight, tokens, slots, capacity)
+    outgoing = project(
+        where, owners[None, :], offsets[None, :], own, other, out_weight, tokens, slots, pair_rows
+    )
     arrived = lax.all_to_all(outgoing, "blk", split_axis=0, concat_axis=0, tiled=True)
     return place(arrived, capacity, 4 * width)
 

time: 86.6 us -> 81.6 us (0.942)
  waiting for transfers between devices: 11.6 us -> 9.66 us
  local copies, waits for them, and re-layouts: 3.3 us -> 1.4 us
  Pallas kernels: 17 us -> 16.1 us
    ppermute x1, waiting for transfers between devices: 6.63 us -> 3.12 us  [per_device(): other_kv = swap(swap_kv)]
    unnamed x20 -> x12, local copies, waits for them, and re-layouts: 3.3 us -> 1.4 us
    ppermute x1, starting transfers between devices: 2.4 us -> 1.22 us  [per_device(): other = swap(other)]
    ppermute x1, waiting for transfers between devices: 1.95 us -> 3.05 us  [per_device(): back_other = back(ready)]
    pallas_call x2, Pallas kernels: 4.45 us -> 3.55 us  [the longest x1 2.07 us: prepare(): pl.pallas_call(prepare_kernel, out_shape=[single, double, single, double]...]
    ppermute x1, waiting for transfers between devices: 0.32 us -> 1.19 us  [per_device(): other = swap(other)]
  transfers between devices with their start and end apart: 9 -> 9, of which waited for: 4 -> 5; matrix products, arithmetic and copies ran while one was open for 0% -> 0% of each run, Pallas kernels for 10% -> 10%
where the time goes in v9:
time: 81.6 us; the launch traced here: 81 us
  blocking collectives  33 us (40%)
  starting transfers between devices  20.5 us (25%)
  Pallas kernels  16.1 us (20%)
  waiting for transfers between devices  9.66 us (12%)
  local copies, waits for them, and re-layouts  1.4 us (2%)
    all_to_all x1, blocking collectives, per_device(): lax.all_to_all(outgoing, 'blk', split_axis=0, concat_axis=0, tiled=True)  33 us
    pallas_call x3, Pallas kernels, attention(): pl.pallas_call(functools.partial(attention_kernel, kinds, numbers, which,...  11.1 us
    ppermute x1, starting transfers between devices, per_device(): back_other = back(ready)  4.39 us
    ppermute x1, starting transfers between devices, per_device(): back_far = back(back_other)  4.39 us
    ppermute x1, starting transfers between devices, per_device(): back_own = back(own_kv)  3.49 us
    ppermute x1, waiting for transfers between devices, per_device(): other_kv = swap(swap_kv)  3.12 us
    ppermute x1, waiting for transfers between devices, per_device(): back_other = back(ready)  3.05 us
    ppermute x1, starting transfers between devices, per_device(): other_kv = swap(swap_kv)  3.03 us
  transfers between devices with their start and end apart: 9, of which 5 were waited for; matrix products, arithmetic and copies ran while one was open for 0% of the time, Pallas kernels for 10%

profile of v9, /device:TPU:0, one launch (start us, length us, event | category | flops | bytes accessed | tf_op | source)
XLA Modules:
  0.0 81.0 jit_solution(10500752000887265689)
XLA Ops:
  0.0 2.1 %shard_map.91 = (bf16[320,256]{1,0:T(8,128)(2,1)S(1)}, bf16[640,256]{1,0:T(8,128)(2,1)S(1)}, bf16[320,256]{1,0:T(8,128)(2,1)S(1)}, bf16[640,256]{1,0:T(8,128)(2,1)}) custom-call(s32[1]{0:T(128)} %bitcast.where_ref, bf16[256,640]{1,0:T(8,128)(2,1)} %q_hbm.1, bf16[256,640]{1,0:T(8,128)(2,1)} %k_hbm.1, bf16[256,640]{1,0:T(8,128)(2,1)} %v_hbm.1), custom_call_target="tpu_custom_call" | custom-call | tf_op jit(solution)/shard_map/pallas_call | solution.py:61
  2.1 3.0 %collective-permute-start = (bf16[640,256]{1,0:T(8,128)(2,1)}, bf16[640,256]{1,0:T(8,128)(2,1)S(1)}, u32[]{:S(2)}, u32[]{:S(2)}) collective-permute-start(bf16[640,256]{1,0:T(8,128)(2,1)} %get-tuple-element.12), channel_id=1, source_target_pairs={{0,4},{4,0},{8,12},{12,8},{16,20},{20,16},{24,28},{28,24},{1,5},{5... | collective-permute-start | bytes 983048 | tf_op jit(solution)/shard_map/ppermute | solution.py:339
  5.1 3.5 %collective-permute-start.2 = (bf16[640,256]{1,0:T(8,128)(2,1)S(1)}, bf16[640,256]{1,0:T(8,128)(2,1)S(1)}, u32[]{:S(2)}, u32[]{:S(2)}) collective-permute-start(bf16[640,256]{1,0:T(8,128)(2,1)S(1)} %get-tuple-element.13.refs_2_), channel_id=1, source_target_pairs={{0,8},{8,16},{12,4},{16,24},{20,12},{28,20},{1,9},{9,17},{13,5},{1... | collective-permute-start | bytes 983048 | tf_op jit(solution)/shard_map/ppermute | solution.py:341
  8.6 1.3 %collective-permute-start.4 = (bf16[640,256]{1,0:T(8,128)(2,1)S(1)}, bf16[640,256]{1,0:T(8,128)(2,1)S(1)}, u32[]{:S(2)}, u32[]{:S(2)}) collective-permute-start(bf16[640,256]{1,0:T(8,128)(2,1)S(1)} %get-tuple-element.13.refs_2_), channel_id=1, source_target_pairs={{4,12},{8,0},{12,20},{16,8},{20,28},{24,16},{5,13},{9,1},{13,21},{... | collective-permute-start | bytes 983048 | tf_op jit(solution)/shard_map/ppermute | solution.py:340
  9.9 3.1 %collective-permute-done.refs_3_ = bf16[640,256]{1,0:T(8,128)(2,1)S(1)} collective-permute-done((bf16[640,256]{1,0:T(8,128)(2,1)}, bf16[640,256]{1,0:T(8,128)(2,1)S(1)}, u32[]{:S(2)}, u32[]{:S(2)}) %collective-permute-start) | collective-permute-done | bytes 327712 | tf_op jit(solution)/shard_map/ppermute | solution.py:339
  13.0 2.2 %collective-permute-done.2.refs_5_ = bf16[640,256]{1,0:T(8,128)(2,1)S(1)} collective-permute-done((bf16[640,256]{1,0:T(8,128)(2,1)S(1)}, bf16[640,256]{1,0:T(8,128)(2,1)S(1)}, u32[]{:S(2)}, u32[]{:S(2)}) %collective-permute-start.2) | collective-permute-done | bytes 327712 | tf_op jit(solution)/shard_map/ppermute | solution.py:341
  15.3 4.4 %collective-permute-start.3 = (bf16[640,256]{1,0:T(8,128)(2,1)S(1)}, bf16[640,256]{1,0:T(8,128)(2,1)S(1)}, u32[]{:S(2)}, u32[]{:S(2)}) collective-permute-start(bf16[640,256]{1,0:T(8,128)(2,1)S(1)} %collective-permute-done.refs_3_), channel_id=1, source_target_pairs={{0,8},{8,16},{12,4},{16,24},{20,12},{28,20},{1,9},{9,17},{13,5},{1... | collective-permute-start | bytes 983048 | tf_op jit(solution)/shard_map/ppermute | solution.py:344
  19.7 0.1 collective-permute-start.7
  19.7 1.3 %collective-permute-start.1 = (bf16[640,256]{1,0:T(8,128)(2,1)S(1)}, bf16[640,256]{1,0:T(8,128)(2,1)S(1)}, u32[]{:S(2)}, u32[]{:S(2)}) collective-permute-start(bf16[640,256]{1,0:T(8,128)(2,1)S(1)} %collective-permute-done.refs_3_), channel_id=1, source_target_pairs={{4,12},{8,0},{12,20},{16,8},{20,28},{24,16},{5,13},{9,1},{13,21},{... | collective-permute-start | bytes 983048 | tf_op jit(solution)/shard_map/ppermute | solution.py:345
  21.1 1.3 %collective-permute-start.5 = (bf16[640,256]{1,0:T(8,128)(2,1)S(1)}, bf16[640,256]{1,0:T(8,128)(2,1)S(1)}, u32[]{:S(2)}, u32[]{:S(2)}) collective-permute-start(bf16[640,256]{1,0:T(8,128)(2,1)S(1)} %collective-permute-done.4.refs_4_), channel_id=1, source_target_pairs={{4,12},{8,0},{12,20},{16,8},{20,28},{24,16},{5,13},{9,1},{13,21},{... | collective-permute-start | bytes 983048 | tf_op jit(solution)/shard_map/ppermute | solution.py:346
  22.4 3.1 %collective-permute-done.3.refs_2_ = bf16[640,256]{1,0:T(8,128)(2,1)S(1)} collective-permute-done((bf16[640,256]{1,0:T(8,128)(2,1)S(1)}, bf16[640,256]{1,0:T(8,128)(2,1)S(1)}, u32[]{:S(2)}, u32[]{:S(2)}) %collective-permute-start.3) | collective-permute-done | bytes 327712 | tf_op jit(solution)/shard_map/ppermute | solution.py:344
  25.4 4.4 %collective-permute-start.6 = (bf16[640,256]{1,0:T(8,128)(2,1)S(1)}, bf16[640,256]{1,0:T(8,128)(2,1)S(1)}, u32[]{:S(2)}, u32[]{:S(2)}) collective-permute-start(bf16[640,256]{1,0:T(8,128)(2,1)S(1)} %collective-permute-done.3.refs_2_), channel_id=1, source_target_pairs={{0,8},{8,16},{12,4},{16,24},{20,12},{28,20},{1,9},{9,17},{13,5},{1... | collective-permute-start | bytes 983048 | tf_op jit(solution)/shard_map/ppermute | solution.py:347
  29.8 0.0 copy-start.4
  29.8 0.7 copy-done.4
  30.5 0.7 copy-done.5
  31.2 5.4 %shard_map.92.refs_5_ = f32[2,4,256,128]{3,2,1,0:T(8,128)S(1)} custom-call(s32[1]{0:T(128)} %bitcast.where_ref, s32[8,8]{1,0:T(8,128)S(1)} %copy-done.5, s32[1,2048]{1,0:T(1,128)S(1)} %bitcast.10, bf16[320,256]{1,0:T(8,128)(2,1)S(1)} %get-tuple-element.11.refs_0_, bf16[320,256]{1,0:T(8,128)(2,1)S(1)} %collective-permute-done.7.refs_1_.refs_0_, ...), custom_call_target="tpu_custom_call" | custom-call | flops 4000000000 | bytes 2000000 | tf_op jit(solution)/shard_map/pallas_call | solution.py:203
  36.6 0.1 collective-permute-done.5.refs_3_
  36.6 2.8 %shard_map.94 = bf16[320,256]{1,0:T(8,128)(2,1)S(1)} custom-call(s32[1]{0:T(128)} %bitcast.where_ref, s32[8,8]{1,0:T(8,128)S(1)} %copy-done.5, s32[1,2048]{1,0:T(1,128)S(1)} %bitcast.11, bf16[320,256]{1,0:T(8,128)(2,1)S(1)} %collective-permute-done.7.refs_1_.refs_0_, bf16[640,256]{1,0:T(8,128)(2,1)S(1)} %collective-permute-done.1.refs_1_, ...), custom_call_target="tpu_custom_call" | custom-call | flops 2000000000 | bytes 2000000 | tf_op jit(solution)/shard_map/pallas_call | solution.py:203
  39.5 1.2 %collective-permute-start.8 = (bf16[320,256]{1,0:T(8,128)(2,1)S(1)}, bf16[320,256]{1,0:T(8,128)(2,1)S(1)}, u32[]{:S(2)}, u32[]{:S(2)}) collective-permute-start(bf16[320,256]{1,0:T(8,128)(2,1)S(1)} %shard_map.94), channel_id=1, source_target_pairs={{0,4},{4,0},{8,12},{12,8},{16,20},{20,16},{24,28},{28,24},{1,5},{5... | collective-permute-start | bytes 491528 | tf_op jit(solution)/shard_map/ppermute | solution.py:354
  40.7 3.0 %shard_map.93.own_ref = bf16[320,256]{1,0:T(8,128)(2,1)S(1)} custom-call(s32[1]{0:T(128)} %bitcast.where_ref, s32[8,8]{1,0:T(8,128)S(1)} %copy-done.5, s32[1,2048]{1,0:T(1,128)S(1)} %bitcast.12, bf16[320,256]{1,0:T(8,128)(2,1)S(1)} %get-tuple-element.11.refs_0_, bf16[640,256]{1,0:T(8,128)(2,1)S(1)} %collective-permute-done.1.refs_1_, ...), custom_call_target="tpu_custom_call" | custom-call | flops 2000000000 | bytes 2000000 | tf_op jit(solution)/shard_map/pallas_call | solution.py:203
  43.7 1.2 %collective-permute-done.8.other_ref = bf16[320,256]{1,0:T(8,128)(2,1)S(1)} collective-permute-done((bf16[320,256]{1,0:T(8,128)(2,1)S(1)}, bf16[320,256]{1,0:T(8,128)(2,1)S(1)}, u32[]{:S(2)}, u32[]{:S(2)}) %collective-permute-start.8) | collective-permute-done | bytes 163872 | tf_op jit(solution)/shard_map/ppermute | solution.py:354
  44.9 1.5 %shard_map.95 = bf16[128,5248]{1,0:T(8,128)(2,1)S(1)} custom-call(s32[1]{0:T(128)} %bitcast.where_ref, s32[1,64]{1,0:T(1,128)S(1)} %bitcast.8, s32[1,64]{1,0:T(1,128)S(1)} %bitcast.9, bf16[320,256]{1,0:T(8,128)(2,1)S(1)} %shard_map.93.own_ref, bf16[320,256]{1,0:T(8,128)(2,1)S(1)} %collective-permute-done.8.other_ref, bf16[640,1280]{1,0:T(8,128)(2,1)S(1)} %copy-done, ...), custom_call_target="tpu_custom_call" | custom-call | tf_op jit(solution)/shard_map/pallas_call | solution.py:268
  46.4 33.0 %all_to_all.11 = bf16[8,16,5248]{2,1,0:T(8,128)(2,1)S(1)} all-to-all(bf16[8,16,5248]{2,1,0:T(8,128)(2,1)S(1)} %bitcast.6), channel_id=1, replica_groups=mesh['blk'=8,'rep'=4] {'blk'}, dimensions={0} | all-to-all | bytes 2686976 | tf_op jit(solution)/shard_map/all_to_all | solution.py:359
  79.4 1.4 %shard_map.96 = bf16[128,5120]{1,0:T(8,128)(2,1)} custom-call(bf16[128,5248]{1,0:T(8,128)(2,1)S(1)} %bitcast.7), custom_call_target="tpu_custom_call" | custom-call | tf_op jit(solution)/shard_map/pallas_call | solution.py:300
  (13 shorter events, 0.0 us)
Async XLA Ops:
  2.1 11.0 %collective-permute-start = (bf16[640,256]{1,0:T(8,128)(2,1)}, bf16[640,256]{1,0:T(8,128)(2,1)S(1)}, u32[]{:S(2)}, u32[]{:S(2)}) collective-permute-start(bf16[640,256]{1,0:T(8,128)(2,1)} %get-tuple-element.12), channel_id=1, source_target_pairs={{0,4},{4,0},{8,12},{12,8},{16,20},{20,16},{24,28},{28,24},{1,5},{5... | collective-permute-start | bytes 983048 | tf_op jit(solution)/shard_map/ppermute | solution.py:339
  5.1 10.1 %collective-permute-start.2 = (bf16[640,256]{1,0:T(8,128)(2,1)S(1)}, bf16[640,256]{1,0:T(8,128)(2,1)S(1)}, u32[]{:S(2)}, u32[]{:S(2)}) collective-permute-start(bf16[640,256]{1,0:T(8,128)(2,1)S(1)} %get-tuple-element.13.refs_2_), channel_id=1, source_target_pairs={{0,8},{8,16},{12,4},{16,24},{20,12},{28,20},{1,9},{9,17},{13,5},{1... | collective-permute-start | bytes 983048 | tf_op jit(solution)/shard_map/ppermute | solution.py:341
  8.6 12.4 %collective-permute-start.4 = (bf16[640,256]{1,0:T(8,128)(2,1)S(1)}, bf16[640,256]{1,0:T(8,128)(2,1)S(1)}, u32[]{:S(2)}, u32[]{:S(2)}) collective-permute-start(bf16[640,256]{1,0:T(8,128)(2,1)S(1)} %get-tuple-element.13.refs_2_), channel_id=1, source_target_pairs={{4,12},{8,0},{12,20},{16,8},{20,28},{24,16},{5,13},{9,1},{13,21},{... | collective-permute-start | bytes 983048 | tf_op jit(solution)/shard_map/ppermute | solution.py:340
  15.3 10.1 %collective-permute-start.3 = (bf16[640,256]{1,0:T(8,128)(2,1)S(1)}, bf16[640,256]{1,0:T(8,128)(2,1)S(1)}, u32[]{:S(2)}, u32[]{:S(2)}) collective-permute-start(bf16[640,256]{1,0:T(8,128)(2,1)S(1)} %collective-permute-done.refs_3_), channel_id=1, source_target_pairs={{0,8},{8,16},{12,4},{16,24},{20,12},{28,20},{1,9},{9,17},{13,5},{1... | collective-permute-start | bytes 983048 | tf_op jit(solution)/shard_map/ppermute | solution.py:344
  19.7 10.1 %collective-permute-start.7 = (bf16[320,256]{1,0:T(8,128)(2,1)S(1)}, bf16[320,256]{1,0:T(8,128)(2,1)S(1)}, u32[]{:S(2)}, u32[]{:S(2)}) collective-permute-start(bf16[320,256]{1,0:T(8,128)(2,1)S(1)} %get-tuple-element.15), channel_id=1, source_target_pairs={{0,4},{4,0},{8,12},{12,8},{16,20},{20,16},{24,28},{28,24},{1,5},{5... | collective-permute-start | bytes 491528 | tf_op jit(solution)/shard_map/ppermute | solution.py:342
  19.7 16.9 %collective-permute-start.1 = (bf16[640,256]{1,0:T(8,128)(2,1)S(1)}, bf16[640,256]{1,0:T(8,128)(2,1)S(1)}, u32[]{:S(2)}, u32[]{:S(2)}) collective-permute-start(bf16[640,256]{1,0:T(8,128)(2,1)S(1)} %collective-permute-done.refs_3_), channel_id=1, source_target_pairs={{4,12},{8,0},{12,20},{16,8},{20,28},{24,16},{5,13},{9,1},{13,21},{... | collective-permute-start | bytes 983048 | tf_op jit(solution)/shard_map/ppermute | solution.py:345
  21.1 15.6 %collective-permute-start.5 = (bf16[640,256]{1,0:T(8,128)(2,1)S(1)}, bf16[640,256]{1,0:T(8,128)(2,1)S(1)}, u32[]{:S(2)}, u32[]{:S(2)}) collective-permute-start(bf16[640,256]{1,0:T(8,128)(2,1)S(1)} %collective-permute-done.4.refs_4_), channel_id=1, source_target_pairs={{4,12},{8,0},{12,20},{16,8},{20,28},{24,16},{5,13},{9,1},{13,21},{... | collective-permute-start | bytes 983048 | tf_op jit(solution)/shard_map/ppermute | solution.py:346
  25.4 11.2 %collective-permute-start.6 = (bf16[640,256]{1,0:T(8,128)(2,1)S(1)}, bf16[640,256]{1,0:T(8,128)(2,1)S(1)}, u32[]{:S(2)}, u32[]{:S(2)}) collective-permute-start(bf16[640,256]{1,0:T(8,128)(2,1)S(1)} %collective-permute-done.3.refs_2_), channel_id=1, source_target_pairs={{0,8},{8,16},{12,4},{16,24},{20,12},{28,20},{1,9},{9,17},{13,5},{1... | collective-permute-start | bytes 983048 | tf_op jit(solution)/shard_map/ppermute | solution.py:347
  29.8 0.7 copy-start.4
  30.5 0.7 copy-start.5
  39.4 5.4 %copy-start = (bf16[640,1280]{1,0:T(8,128)(2,1)S(1)}, bf16[640,1280]{1,0:T(8,128)(2,1)}, u32[]{:S(2)}) copy-start(bf16[640,1280]{1,0:T(8,128)(2,1)} %weight_ref.1) | copy-start | bytes 4915204
  39.5 5.4 %copy-start.1 = (bf16[256,1280]{1,0:T(8,128)(2,1)S(1)}, bf16[256,1280]{1,0:T(8,128)(2,1)}, u32[]{:S(2)}) copy-start(bf16[256,1280]{1,0:T(8,128)(2,1)} %tokens_ref.1) | copy-start | bytes 1966084
  39.5 5.4 %copy-start.2 = (s32[64]{0:T(128)S(1)}, s32[64]{0:T(128)}, u32[]{:S(2)}) copy-start(s32[64]{0:T(128)} %param.16) | copy-start | bytes 772
  39.5 5.4 %copy-start.3 = (s32[64]{0:T(128)S(1)}, s32[64]{0:T(128)}, u32[]{:S(2)}) copy-start(s32[64]{0:T(128)} %param.17) | copy-start | bytes 772
  39.5 5.4 %collective-permute-start.8 = (bf16[320,256]{1,0:T(8,128)(2,1)S(1)}, bf16[320,256]{1,0:T(8,128)(2,1)S(1)}, u32[]{:S(2)}, u32[]{:S(2)}) collective-permute-start(bf16[320,256]{1,0:T(8,128)(2,1)S(1)} %shard_map.94), channel_id=1, source_target_pairs={{0,4},{4,0},{8,12},{12,8},{16,20},{20,16},{24,28},{28,24},{1,5},{5... | collective-permute-start | bytes 491528 | tf_op jit(solution)/shard_map/ppermute | solution.py:354

commit v10 on v9

--- a/solution.py
+++ b/solution.py
@@ -29,6 +29,18 @@
 
 def limit(mib):
     return pltpu.CompilerParams(vmem_limit_bytes=mib * MIB)
+
+
+PLACES = ((3, 1), (4, -1), (5, -3), (1, 5), (6, -5), (2, 3), (7, -7), (0, 7))
+
+
+def asking(me, kind):
+    return me if kind == 0 else me + 1 - 2 * (me % 2)
+
+
+def key_block(me, number):
+    half = me % 2
+    return me - half - SPAN + PLACES[number][0] + PLACES[number][1] * half
 
 
 def prepare_kernel(where_ref, q_hbm, k_hbm, v_hbm, own_q, own_kv, swap_q, swap_kv, held, turned, sems):
@@ -39,7 +51,8 @@
     ]
     for load in loads:
         load.start()
-    half = where_ref[0] % 2
+    me = where_ref[0]
+    half = me % 2
     mine = pl.multiple_of(half * part, 16)
     other = pl.multiple_of((1 - half) * part, 16)
     for i in range(3):
@@ -72,37 +85,54 @@
     )(where, queries, keys, values)
 
 
-PLACES = ((3, 1), (4, -1), (5, -3), (1, 5), (6, -5), (2, 3), (7, -7), (0, 7))
-
-
-def attention_kernel(kinds, numbers, which, ends, where_ref, mask_ref, seg_ref, *refs):
+def survey_kernel(where_ref, mask_ref, segs_ref, seg_out, need_out):
+    seg_out[...] = segs_ref[...].astype(jnp.float32)
+    me = where_ref[0]
+    nblocks = mask_ref.shape[0]
+    bits = jnp.int32(0)
+    for kind in range(2):
+        asker = asking(me, kind)
+        for number in range(len(PLACES)):
+            block = key_block(me, number)
+            inside = (block >= 0) & (block < nblocks) & (jnp.abs(block - asker) <= SPAN)
+            allowed = mask_ref[asker, jnp.clip(block, 0, nblocks - 1)] > 0
+            bits += (inside & allowed).astype(jnp.int32) << (kind * len(PLACES) + number)
+    need_out[...] = jnp.full(need_out.shape, bits, jnp.int32)
+
+
+def survey(where, mask, segs):
+    return pl.pallas_call(
+        survey_kernel,
+        out_shape=[
+            jax.ShapeDtypeStruct(segs.shape, jnp.float32),
+            jax.ShapeDtypeStruct((8, 128), jnp.int32),
+        ],
+        in_specs=[smem()] * 2 + [vmem()],
+        out_specs=[vmem()] * 2,
+        compiler_params=limit(16),
+    )(where, mask, segs)
+
+
+def attention_kernel(kinds, numbers, follows, ends, where_ref, need_ref, seg_ref, *refs):
     queries, refs = refs[: len(kinds)], refs[len(kinds) :]
     blocks, refs = refs[: len(numbers)], refs[len(numbers) :]
-    follows = which is not None
     if follows:
         before, refs = refs[0], refs[1:]
     out_ref, query_s, key_s, value_s, chosen_s = refs
     part, rows = queries[0].shape
     hdim = part // HALF
     wide = value_s.shape[2]
-    nblocks = mask_ref.shape[0]
+    nblocks = seg_ref.shape[1] // rows
     factor = LOG2E / (hdim**0.5)
     me = where_ref[0]
-    half = me % 2
-    column = [me - half - SPAN + PLACES[b][0] + PLACES[b][1] * half for b in numbers]
-    asker = [me if kind == 0 else me + 1 - 2 * half for kind in kinds]
-
-    def needed(n, b):
-        inside = (column[b] >= 0) & (column[b] < nblocks)
-        inside &= jnp.abs(column[b] - asker[n]) <= SPAN
-        allowed = mask_ref[asker[n], jnp.clip(column[b], 0, nblocks - 1)] > 0
-        return (inside & allowed).astype(jnp.int32)
-
-    need = [[needed(n, b) for b in range(len(numbers))] for n in range(len(kinds))]
+    column = [key_block(me, b) for b in numbers]
+    asker = [asking(me, kind) for kind in kinds]
+    bits = jnp.max(need_ref[...])
+    need = [[(bits >> (kind * len(PLACES) + b)) & 1 for b in numbers] for kind in kinds]
 
     def segment(block):
         start = pl.multiple_of(jnp.clip(block, 0, nblocks - 1) * rows, 128)
-        return seg_ref[:, pl.ds(start, rows)].astype(jnp.float32)
+        return seg_ref[:, pl.ds(start, rows)]
 
     for b in range(len(numbers)):
         wanted = need[0][b]
@@ -141,7 +171,7 @@
             @pl.when(size == 0)
             def _():
                 def one_head(h, carry):
-                    state = before[which, h]
+                    state = before[0, h]
                     finish(h, state[:, wide : wide + 1], state[:, :wide])
                     return carry
 
@@ -170,7 +200,7 @@
                     peak = jnp.max(peak, axis=1, keepdims=True)
                     accum = jnp.zeros((rows, wide), jnp.float32)
                     if follows:
-                        state = before[which, h]
+                        state = before[0, h]
                         old = state[:, wide : wide + 1]
                         peak = jnp.maximum(peak, old)
                         accum = state[:, :wide] * jnp.exp2((old - peak) * factor)
@@ -192,19 +222,19 @@
                 lax.fori_loop(0, HALF // 2, two_heads, 0)
 
 
-def attention(where, mask, segs, queries, kinds, blocks, numbers, before, which, ends):
+def attention(where, need, segs, queries, kinds, blocks, numbers, before, ends):
     part, rows = queries[0].shape
     hdim = part // HALF
     wide = hdim + 16
+    follows = before is not None
     if ends:
         out = jax.ShapeDtypeStruct((part, rows), jnp.bfloat16)
     else:
         out = jax.ShapeDtypeStruct((len(kinds), HALF, rows, 128), jnp.float32)
     return pl.pallas_call(
-        functools.partial(attention_kernel, kinds, numbers, which, ends),
+        functools.partial(attention_kernel, kinds, numbers, follows, ends),
         out_shape=out,
-        in_specs=[smem()] * 2
-        + [vmem()] * (1 + len(kinds) + len(numbers) + (which is not None)),
+        in_specs=[smem()] + [vmem()] * (2 + len(kinds) + len(numbers) + follows),
         out_specs=vmem(),
         scratch_shapes=[
             pltpu.VMEM((HALF, rows, hdim), jnp.bfloat16),
@@ -216,13 +246,14 @@
         cost_estimate=pl.CostEstimate(
             flops=2_000_000_000 * len(kinds), bytes_accessed=2_000_000, transcendentals=1_000_000
         ),
-    )(where, mask, segs, *queries, *blocks, *(() if which is None else (before,)))
+    )(where, need, segs, *queries, *blocks, *((before,) if follows else ()))
 
 
 def project_kernel(
-    pair_rows, where_ref, owners_ref, offsets_ref, own_ref, other_ref, weight_ref, tokens_ref, out_ref
+    pair_rows, where_ref, owners_ref, offsets_ref, own_ref, other_ref, weight_ref, tokens_ref, *outs
 ):
-    slots = out_ref.shape[0]
+    piece = outs[0].shape[0]
+    slots = piece * len(outs)
     rows, width = tokens_ref.shape
     mrows = rows // 4
     capacity = 2 * mrows
@@ -249,48 +280,58 @@
             preferred_element_type=jnp.float32,
         )
     hidden = hidden.astype(jnp.bfloat16)
+    place = meta[:1]
+    if len(outs) > 1:
+        place = place - (where_ref[0] * pair_rows).astype(jnp.float32)
+        place = jnp.where(place < 0, place + slots, place)
     slot = lax.broadcasted_iota(jnp.int32, (slots, rows), 0).astype(jnp.float32)
     quarter = lax.broadcasted_iota(jnp.int32, (1, rows), 1) % 4
     for j in range(4):
-        mine = jnp.where(quarter == j, meta[:1], -1.0) == slot
+        mine = jnp.where(quarter == j, place, -1.0) == slot
         if j == 0:
             offset = jnp.where(mine, meta[1:2] - capacity, 0.0)
             offset = capacity + jnp.sum(offset, axis=1, keepdims=True)
-            out_ref[:, 4 * width :] = jnp.broadcast_to(offset, (slots, 128)).astype(jnp.bfloat16)
+            offset = jnp.broadcast_to(offset, (slots, 128)).astype(jnp.bfloat16)
+            for d, out in enumerate(outs):
+                out[:, 4 * width :] = offset[d * piece : (d + 1) * piece]
         pick = jnp.where(mine, 1.0, 0.0).astype(jnp.bfloat16)
-        out_ref[:, j * width : (j + 1) * width] = jnp.dot(
-            pick, hidden, preferred_element_type=jnp.float32
-        ).astype(jnp.bfloat16)
-
-
-def project(where, owners, offsets, own, other, out_weight, tokens, slots, pair_rows):
+        picked = jnp.dot(pick, hidden, preferred_element_type=jnp.float32).astype(jnp.bfloat16)
+        for d, out in enumerate(outs):
+            out[:, j * width : (j + 1) * width] = picked[d * piece : (d + 1) * piece]
+
+
+def project(where, owners, offsets, own, other, out_weight, tokens, pieces, slots, pair_rows):
     rows, width = tokens.shape
     return pl.pallas_call(
         functools.partial(project_kernel, pair_rows),
-        out_shape=jax.ShapeDtypeStruct((slots, 4 * width + 128), jnp.bfloat16),
+        out_shape=[jax.ShapeDtypeStruct((slots // pieces, 4 * width + 128), jnp.bfloat16)] * pieces,
         in_specs=[smem()] + [vmem()] * 6,
-        out_specs=vmem(),
+        out_specs=[vmem()] * pieces,
         compiler_params=limit(24),
     )(where, owners, offsets, own, other, out_weight, tokens)
 
 
-def place_kernel(arrived_ref, out_hbm, held, sems):
+def place_kernel(*refs):
+    *arrived, out_hbm, held, sems = refs
     capacity, merged = out_hbm.shape
-    slots = arrived_ref.shape[0]
     step = merged // 4
-    row = lax.broadcasted_iota(jnp.int32, (slots, capacity), 1).astype(jnp.float32)
-    offset = arrived_ref[:, merged : merged + 128].astype(jnp.float32)[:, :1]
+
+    def columns_of(start, size):
+        return jnp.concatenate([ref[:, start : start + size] for ref in arrived], axis=0)
+
+    offset = columns_of(merged, 128).astype(jnp.float32)[:, :1]
+    row = lax.broadcasted_iota(jnp.int32, (offset.shape[0], capacity), 1).astype(jnp.float32)
     pick = jnp.where(offset == row, 1.0, 0.0).astype(jnp.bfloat16)
     stores = []
     for j in range(4):
-        columns = slice(j * step, (j + 1) * step)
         held[j] = lax.dot_general(
             pick,
-            arrived_ref[:, columns],
+            columns_of(j * step, step),
             (((0,), (0,)), ((), ())),
             preferred_element_type=jnp.float32,
         ).astype(jnp.bfloat16)
-        stores.append(pltpu.make_async_copy(held.at[j], out_hbm.at[:, columns], sems.at[j]))
+        columns = out_hbm.at[:, pl.ds(j * step, step)]
+        stores.append(pltpu.make_async_copy(held.at[j], columns, sems.at[j]))
         stores[j].start()
     for store in stores:
         store.wait()
@@ -300,14 +341,14 @@
     return pl.pallas_call(
         place_kernel,
         out_shape=jax.ShapeDtypeStruct((capacity, merged), jnp.bfloat16),
-        in_specs=[vmem()],
+        in_specs=[vmem()] * len(arrived),
         out_specs=anywhere(),
         scratch_shapes=[
             pltpu.VMEM((4, capacity, merged // 4), jnp.bfloat16),
             pltpu.SemaphoreType.DMA((4,)),
         ],
         compiler_params=limit(24),
-    )(arrived)
+    )(*arrived)
 
 
 def per_device(segment_ids, block_mask, queries, keys, values, tokens, out_weight, owners, offsets):
@@ -336,27 +377,41 @@
 
     where = block_index[None].astype(jnp.int32)
     own_q, own_kv, swap_q, swap_kv = prepare(where, queries, keys, values)
+    segs, need = survey(where, block_mask, segment_ids[None, :])
     other_kv = swap(swap_kv)
     ahead_own = ahead(own_kv)
     back_own = back(own_kv)
     other_q = swap(swap_q)
-    ready, back_own = lax.optimization_barrier((other_kv, back_own))
+    ready, back_own, segs, need = lax.optimization_barrier((other_kv, back_own, segs, need))
     back_other = back(ready)
     ahead_other = ahead(other_kv)
     ahead_far = ahead(ahead_own)
+    near = (own_kv, other_kv, ahead_own, back_own)
+    near_numbers, far_numbers = (0, 1, 2, 3), (4, 5, 6, 7)
+    fixed = (where, need, segs)
+    own = attention(*fixed, (own_q,), (0,), near, near_numbers, None, False)
+    back_other, own = lax.optimization_barrier((back_other, own))
     back_far = back(back_other)
-    near = (own_kv, other_kv, ahead_own, back_own)
+    other = attention(*fixed, (other_q,), (1,), near, near_numbers, None, False)
     far = (ahead_other, back_other, ahead_far, back_far)
-
-    fixed = (where, block_mask, segment_ids[None, :])
-    state = attention(*fixed, (own_q, other_q), (0, 1), near, (0, 1, 2, 3), None, None, False)
-    other = attention(*fixed, (other_q,), (1,), far, (4, 5, 6, 7), state, 1, True)
+    other = attention(*fixed, (other_q,), (1,), far, far_numbers, other, True)
     other = swap(other)
-    own = attention(*fixed, (own_q,), (0,), far, (4, 5, 6, 7), state, 0, True)
+    own = attention(*fixed, (own_q,), (0,), far, far_numbers, own, True)
+
+    pieces = nblocks if nblocks <= 8 else 1
     outgoing = project(
-        where, owners[None, :], offsets[None, :], own, other, out_weight, tokens, slots, pair_rows
-    )
-    arrived = lax.all_to_all(outgoing, "blk", split_axis=0, concat_axis=0, tiled=True)
+        where, owners[None, :], offsets[None, :], own, other, out_weight, tokens,
+        pieces, slots, pair_rows,
+    )
+    if pieces > 1:
+        arrived = [outgoing[0]] + [None] * (nblocks - 1)
+        order = sorted(range(1, nblocks), key=lambda d: (min(d, nblocks - d) == 2, d))
+        for d in order:
+            arrived[d] = lax.ppermute(
+                outgoing[d], "blk", [(i, (i + d) % nblocks) for i in range(nblocks)]
+            )
+    else:
+        arrived = [lax.all_to_all(outgoing[0], "blk", split_axis=0, concat_axis=0, tiled=True)]
     return place(arrived, capacity, 4 * width)
 
 

time: 81.6 us -> 77.8 us (0.953)
  the two profiles are of different devices: /device:TPU:0 before, /device:TPU:14 now
where the time goes in v10:
time: 77.8 us; the launch traced here: 77.1 us
  waiting for transfers between devices  30.2 us (39%)
  starting transfers between devices  28.9 us (37%)
  Pallas kernels  16.2 us (21%)
  local copies, waits for them, and re-layouts  1.4 us (2%)
    ppermute x7, waiting for transfers between devices, per_device(): lax.ppermute(outgoing[d], 'blk', [(i, (i + d) % nblocks) for i in range(n...  21.9 us
    pallas_call x4, Pallas kernels, attention(): pl.pallas_call(functools.partial(attention_kernel, kinds, numbers, follow...  10.5 us
    ppermute x7, starting transfers between devices, per_device(): lax.ppermute(outgoing[d], 'blk', [(i, (i + d) % nblocks) for i in range(n...  8.01 us
    ppermute x1, starting transfers between devices, per_device(): back_far = back(back_other)  3.93 us
    ppermute x1, starting transfers between devices, per_device(): ahead_own = ahead(own_kv)  3.48 us
    ppermute x1, starting transfers between devices, per_device(): ahead_other = ahead(other_kv)  3.47 us
    ppermute x1, starting transfers between devices, per_device(): other_q = swap(swap_q)  2.71 us
    ppermute x1, waiting for transfers between devices, per_device(): other = swap(other)  2.51 us
  transfers between devices with their start and end apart: 16, of which 11 were waited for; matrix products, arithmetic and copies ran while one was open for 0% of the time, Pallas kernels for 11%

profile of v10, /device:TPU:14, one launch (start us, length us, event | category | flops | bytes accessed | tf_op | source)
XLA Modules:
  0.0 77.1 jit_solution(17757413726995263360)
XLA Ops:
  0.0 2.1 %shard_map.91 = (bf16[320,256]{1,0:T(8,128)(2,1)S(1)}, bf16[640,256]{1,0:T(8,128)(2,1)S(1)}, bf16[320,256]{1,0:T(8,128)(2,1)S(1)}, bf16[640,256]{1,0:T(8,128)(2,1)}) custom-call(s32[1]{0:T(128)} %bitcast.where_ref, bf16[256,640]{1,0:T(8,128)(2,1)} %q_hbm.1, bf16[256,640]{1,0:T(8,128)(2,1)} %k_hbm.1, bf16[256,640]{1,0:T(8,128)(2,1)} %v_hbm.1), custom_call_target="tpu_custom_call" | custom-call | tf_op jit(solution)/shard_map/pallas_call | solution.py:74
  2.7 2.3 %collective-permute-start.1 = (bf16[640,256]{1,0:T(8,128)(2,1)S(1)}, bf16[640,256]{1,0:T(8,128)(2,1)S(1)}, u32[]{:S(2)}, u32[]{:S(2)}) collective-permute-start(bf16[640,256]{1,0:T(8,128)(2,1)S(1)} %get-tuple-element.26.refs_1_), channel_id=1, source_target_pairs={{0,8},{8,16},{12,4},{16,24},{20,12},{28,20},{1,9},{9,17},{13,5},{1... | collective-permute-start | bytes 983048 | tf_op jit(solution)/shard_map/ppermute | solution.py:383
  5.0 3.5 %collective-permute-start.4 = (bf16[640,256]{1,0:T(8,128)(2,1)S(1)}, bf16[640,256]{1,0:T(8,128)(2,1)S(1)}, u32[]{:S(2)}, u32[]{:S(2)}) collective-permute-start(bf16[640,256]{1,0:T(8,128)(2,1)S(1)} %get-tuple-element.26.refs_1_), channel_id=1, source_target_pairs={{4,12},{8,0},{12,20},{16,8},{20,28},{24,16},{5,13},{9,1},{13,21},{... | collective-permute-start | bytes 983048 | tf_op jit(solution)/shard_map/ppermute | solution.py:382
  11.8 1.9 %collective-permute-done.1.refs_4_ = bf16[640,256]{1,0:T(8,128)(2,1)S(1)} collective-permute-done((bf16[640,256]{1,0:T(8,128)(2,1)S(1)}, bf16[640,256]{1,0:T(8,128)(2,1)S(1)}, u32[]{:S(2)}, u32[]{:S(2)}) %collective-permute-start.1) | collective-permute-done | bytes 327712 | tf_op jit(solution)/shard_map/ppermute | solution.py:383
  13.7 2.3 %collective-permute-start.3 = (bf16[640,256]{1,0:T(8,128)(2,1)S(1)}, bf16[640,256]{1,0:T(8,128)(2,1)S(1)}, u32[]{:S(2)}, u32[]{:S(2)}) collective-permute-start(bf16[640,256]{1,0:T(8,128)(2,1)S(1)} %collective-permute-done.refs_2_), channel_id=1, source_target_pairs={{0,8},{8,16},{12,4},{16,24},{20,12},{28,20},{1,9},{9,17},{13,5},{1... | collective-permute-start | bytes 983048 | tf_op jit(solution)/shard_map/ppermute | solution.py:386
  16.1 2.7 %collective-permute-start.7 = (bf16[320,256]{1,0:T(8,128)(2,1)S(1)}, bf16[320,256]{1,0:T(8,128)(2,1)S(1)}, u32[]{:S(2)}, u32[]{:S(2)}) collective-permute-start(bf16[320,256]{1,0:T(8,128)(2,1)S(1)} %get-tuple-element.36), channel_id=1, source_target_pairs={{0,4},{4,0},{8,12},{12,8},{16,20},{20,16},{24,28},{28,24},{1,5},{5... | collective-permute-start | bytes 491528 | tf_op jit(solution)/shard_map/ppermute | solution.py:384
  18.8 3.5 %collective-permute-start.2 = (bf16[640,256]{1,0:T(8,128)(2,1)S(1)}, bf16[640,256]{1,0:T(8,128)(2,1)S(1)}, u32[]{:S(2)}, u32[]{:S(2)}) collective-permute-start(bf16[640,256]{1,0:T(8,128)(2,1)S(1)} %collective-permute-done.refs_2_), channel_id=1, source_target_pairs={{4,12},{8,0},{12,20},{16,8},{20,28},{24,16},{5,13},{9,1},{13,21},{... | collective-permute-start | bytes 983048 | tf_op jit(solution)/shard_map/ppermute | solution.py:387
  22.3 1.9 %collective-permute-start.5 = (bf16[640,256]{1,0:T(8,128)(2,1)S(1)}, bf16[640,256]{1,0:T(8,128)(2,1)S(1)}, u32[]{:S(2)}, u32[]{:S(2)}) collective-permute-start(bf16[640,256]{1,0:T(8,128)(2,1)S(1)} %collective-permute-done.4.refs_3_), channel_id=1, source_target_pairs={{4,12},{8,0},{12,20},{16,8},{20,28},{24,16},{5,13},{9,1},{13,21},{... | collective-permute-start | bytes 983048 | tf_op jit(solution)/shard_map/ppermute | solution.py:388
  24.2 2.6 %shard_map.93.refs_5_ = f32[1,4,256,128]{3,2,1,0:T(8,128)S(1)} custom-call(s32[1]{0:T(128)} %bitcast.where_ref, s32[8,128]{1,0:T(8,128)S(1)} %get-tuple-element.29.need_ref, f32[1,2048]{1,0:T(1,128)S(1)} %get-tuple-element.30.seg_ref, bf16[320,256]{1,0:T(8,128)(2,1)S(1)} %get-tuple-element.31.refs_0_, bf16[640,256]{1,0:T(8,128)(2,1)S(1)} %get-tuple-element.26.refs_1_, ...), custom_call_target="tpu_custom_call" | custom-call | flops 2000000000 | bytes 2000000 | tf_op jit(solution)/shard_map/pallas_call | solution.py:234
  26.8 3.9 %collective-permute-start.6 = (bf16[640,256]{1,0:T(8,128)(2,1)S(1)}, bf16[640,256]{1,0:T(8,128)(2,1)S(1)}, u32[]{:S(2)}, u32[]{:S(2)}) collective-permute-start(bf16[640,256]{1,0:T(8,128)(2,1)S(1)} %collective-permute-done.3.refs_2_), channel_id=1, source_target_pairs={{0,8},{8,16},{12,4},{16,24},{20,12},{28,20},{1,9},{9,17},{13,5},{1... | collective-permute-start | bytes 983048 | tf_op jit(solution)/shard_map/ppermute | solution.py:394
  30.8 2.6 %shard_map.95.refs_5_ = f32[1,4,256,128]{3,2,1,0:T(8,128)S(1)} custom-call(s32[1]{0:T(128)} %bitcast.where_ref, s32[8,128]{1,0:T(8,128)S(1)} %get-tuple-element.29.need_ref, f32[1,2048]{1,0:T(1,128)S(1)} %get-tuple-element.30.seg_ref, bf16[320,256]{1,0:T(8,128)(2,1)S(1)} %collective-permute-done.7.refs_0_, bf16[640,256]{1,0:T(8,128)(2,1)S(1)} %get-tuple-element.26.refs_1_, ...), custom_call_target="tpu_custom_call" | custom-call | flops 2000000000 | bytes 2000000 | tf_op jit(solution)/shard_map/pallas_call | solution.py:234
  33.4 2.0 %collective-permute-done.5.refs_3_ = bf16[640,256]{1,0:T(8,128)(2,1)S(1)} collective-permute-done((bf16[640,256]{1,0:T(8,128)(2,1)S(1)}, bf16[640,256]{1,0:T(8,128)(2,1)S(1)}, u32[]{:S(2)}, u32[]{:S(2)}) %collective-permute-start.5) | collective-permute-done | bytes 327712 | tf_op jit(solution)/shard_map/ppermute | solution.py:388
  36.1 2.6 %shard_map.96 = bf16[320,256]{1,0:T(8,128)(2,1)S(1)} custom-call(s32[1]{0:T(128)} %bitcast.where_ref, s32[8,128]{1,0:T(8,128)S(1)} %get-tuple-element.29.need_ref, f32[1,2048]{1,0:T(1,128)S(1)} %get-tuple-element.30.seg_ref, bf16[320,256]{1,0:T(8,128)(2,1)S(1)} %collective-permute-done.7.refs_0_, bf16[640,256]{1,0:T(8,128)(2,1)S(1)} %collective-permute-done.2.refs_1_, ...), custom_call_target="tpu_custom_call" | custom-call | flops 2000000000 | bytes 2000000 | tf_op jit(solution)/shard_map/pallas_call | solution.py:234
  38.8 2.8 %shard_map.94.own_ref = bf16[320,256]{1,0:T(8,128)(2,1)S(1)} custom-call(s32[1]{0:T(128)} %bitcast.where_ref, s32[8,128]{1,0:T(8,128)S(1)} %get-tuple-element.29.need_ref, f32[1,2048]{1,0:T(1,128)S(1)} %get-tuple-element.30.seg_ref, bf16[320,256]{1,0:T(8,128)(2,1)S(1)} %get-tuple-element.31.refs_0_, bf16[640,256]{1,0:T(8,128)(2,1)S(1)} %collective-permute-done.2.refs_1_, ...), custom_call_target="tpu_custom_call" | custom-call | flops 2000000000 | bytes 2000000 | tf_op jit(solution)/shard_map/pallas_call | solution.py:234
  41.6 2.5 %collective-permute-done.8.other_ref = bf16[320,256]{1,0:T(8,128)(2,1)S(1)} collective-permute-done((bf16[320,256]{1,0:T(8,128)(2,1)S(1)}, bf16[320,256]{1,0:T(8,128)(2,1)S(1)}, u32[]{:S(2)}, u32[]{:S(2)}) %collective-permute-start.8) | collective-permute-done | bytes 163872 | tf_op jit(solution)/shard_map/ppermute | solution.py:398
  44.1 1.5 %shard_map.97 = (bf16[16,5248]{1,0:T(8,128)(2,1)S(1)}, bf16[16,5248]{1,0:T(8,128)(2,1)S(1)}, bf16[16,5248]{1,0:T(8,128)(2,1)S(1)}, bf16[16,5248]{1,0:T(8,128)(2,...) custom-call(s32[1]{0:T(128)} %bitcast.where_ref, ...), custom_call_target="tpu_custom_call" | custom-call | tf_op jit(solution)/shard_map/pallas_call | solution.py:305
  46.5 2.7 %collective-permute-start.11 = (bf16[16,5248]{1,0:T(8,128)(2,1)S(1)}, bf16[16,5248]{1,0:T(8,128)(2,1)S(1)}, u32[]{:S(2)}, u32[]{:S(2)}) collective-permute-start(bf16[16,5248]{1,0:T(8,128)(2,1)S(1)} %get-tuple-element.40), channel_id=1, source_target_pairs={{0,12},{4,16},{8,20},{12,24},{16,28},{20,0},{24,4},{28,8},{1,13},{... | collective-permute-start | bytes 503816 | tf_op jit(solution)/shard_map/ppermute | solution.py:410
  49.8 2.9 %collective-permute-start.13 = (bf16[16,5248]{1,0:T(8,128)(2,1)S(1)}, bf16[16,5248]{1,0:T(8,128)(2,1)S(1)}, u32[]{:S(2)}, u32[]{:S(2)}) collective-permute-start(bf16[16,5248]{1,0:T(8,128)(2,1)S(1)} %get-tuple-element.42), channel_id=1, source_target_pairs={{0,20},{4,24},{8,28},{12,0},{16,4},{20,8},{24,12},{28,16},{1,21},{... | collective-permute-start | bytes 503816 | tf_op jit(solution)/shard_map/ppermute | solution.py:410
  52.7 6.3 %collective-permute-done.10.refs_2_ = bf16[16,5248]{1,0:T(8,128)(2,1)S(1)} collective-permute-done((bf16[16,5248]{1,0:T(8,128)(2,1)S(1)}, bf16[16,5248]{1,0:T(8,128)(2,1)S(1)}, u32[]{:S(2)}, u32[]{:S(2)}) %collective-permute-start.10) | collective-permute-done | bytes 167968 | tf_op jit(solution)/shard_map/ppermute | solution.py:410
  59.1 7.5 %collective-permute-done.11.refs_3_ = bf16[16,5248]{1,0:T(8,128)(2,1)S(1)} collective-permute-done((bf16[16,5248]{1,0:T(8,128)(2,1)S(1)}, bf16[16,5248]{1,0:T(8,128)(2,1)S(1)}, u32[]{:S(2)}, u32[]{:S(2)}) %collective-permute-start.11) | collective-permute-done | bytes 167968 | tf_op jit(solution)/shard_map/ppermute | solution.py:410
  67.5 2.3 %collective-permute-done.12.refs_4_ = bf16[16,5248]{1,0:T(8,128)(2,1)S(1)} collective-permute-done((bf16[16,5248]{1,0:T(8,128)(2,1)S(1)}, bf16[16,5248]{1,0:T(8,128)(2,1)S(1)}, u32[]{:S(2)}, u32[]{:S(2)}) %collective-permute-start.12) | collective-permute-done | bytes 167968 | tf_op jit(solution)/shard_map/ppermute | solution.py:410
  69.7 4.1 %collective-permute-done.14.refs_6_ = bf16[16,5248]{1,0:T(8,128)(2,1)S(1)} collective-permute-done((bf16[16,5248]{1,0:T(8,128)(2,1)S(1)}, bf16[16,5248]{1,0:T(8,128)(2,1)S(1)}, u32[]{:S(2)}, u32[]{:S(2)}) %collective-permute-start.14) | collective-permute-done | bytes 167968 | tf_op jit(solution)/shard_map/ppermute | solution.py:410
  74.2 1.3 %collective-permute-done.9.refs_1_ = bf16[16,5248]{1,0:T(8,128)(2,1)S(1)} collective-permute-done((bf16[16,5248]{1,0:T(8,128)(2,1)S(1)}, bf16[16,5248]{1,0:T(8,128)(2,1)S(1)}, u32[]{:S(2)}, u32[]{:S(2)}) %collective-permute-start.9) | collective-permute-done | bytes 167968 | tf_op jit(solution)/shard_map/ppermute | solution.py:410
  75.5 1.4 %shard_map.98 = bf16[128,5120]{1,0:T(8,128)(2,1)} custom-call(bf16[16,5248]{1,0:T(8,128)(2,1)S(1)} %get-tuple-element.37.refs_0_, bf16[16,5248]{1,0:T(8,128)(2,1)S(1)} %collective-permute-done.9.refs_1_, bf16[16,5248]{1,0:T(8,128)(2,1)S(1)} %collective-permute-done.10.refs_2_, bf16[16,5248]{1,0:T(8,128)(2,1)S(1)} %collective-permute-done.11.refs_3_, ...), custom_call_target="tpu_custom_call" | custom-call | tf_op jit(solution)/shard_map/pallas_call | solution.py:341
  (28 shorter events, 7.5 us)
Async XLA Ops:
  2.1 9.7 %collective-permute-start = (bf16[640,256]{1,0:T(8,128)(2,1)}, bf16[640,256]{1,0:T(8,128)(2,1)S(1)}, u32[]{:S(2)}, u32[]{:S(2)}) collective-permute-start(bf16[640,256]{1,0:T(8,128)(2,1)} %get-tuple-element.25), channel_id=1, source_target_pairs={{0,4},{4,0},{8,12},{12,8},{16,20},{20,16},{24,28},{28,24},{1,5},{5... | collective-permute-start | bytes 983048 | tf_op jit(solution)/shard_map/ppermute | solution.py:381
  2.7 11.1 %collective-permute-start.1 = (bf16[640,256]{1,0:T(8,128)(2,1)S(1)}, bf16[640,256]{1,0:T(8,128)(2,1)S(1)}, u32[]{:S(2)}, u32[]{:S(2)}) collective-permute-start(bf16[640,256]{1,0:T(8,128)(2,1)S(1)} %get-tuple-element.26.refs_1_), channel_id=1, source_target_pairs={{0,8},{8,16},{12,4},{16,24},{20,12},{28,20},{1,9},{9,17},{13,5},{1... | collective-permute-start | bytes 983048 | tf_op jit(solution)/shard_map/ppermute | solution.py:383
  5.0 17.2 %collective-permute-start.4 = (bf16[640,256]{1,0:T(8,128)(2,1)S(1)}, bf16[640,256]{1,0:T(8,128)(2,1)S(1)}, u32[]{:S(2)}, u32[]{:S(2)}) collective-permute-start(bf16[640,256]{1,0:T(8,128)(2,1)S(1)} %get-tuple-element.26.refs_1_), channel_id=1, source_target_pairs={{4,12},{8,0},{12,20},{16,8},{20,28},{24,16},{5,13},{9,1},{13,21},{... | collective-permute-start | bytes 983048 | tf_op jit(solution)/shard_map/ppermute | solution.py:382
  8.5 0.7 copy-start.2
  9.2 0.7 copy-start.3
  13.7 13.1 %collective-permute-start.3 = (bf16[640,256]{1,0:T(8,128)(2,1)S(1)}, bf16[640,256]{1,0:T(8,128)(2,1)S(1)}, u32[]{:S(2)}, u32[]{:S(2)}) collective-permute-start(bf16[640,256]{1,0:T(8,128)(2,1)S(1)} %collective-permute-done.refs_2_), channel_id=1, source_target_pairs={{0,8},{8,16},{12,4},{16,24},{20,12},{28,20},{1,9},{9,17},{13,5},{1... | collective-permute-start | bytes 983048 | tf_op jit(solution)/shard_map/ppermute | solution.py:386
  16.1 14.7 %collective-permute-start.7 = (bf16[320,256]{1,0:T(8,128)(2,1)S(1)}, bf16[320,256]{1,0:T(8,128)(2,1)S(1)}, u32[]{:S(2)}, u32[]{:S(2)}) collective-permute-start(bf16[320,256]{1,0:T(8,128)(2,1)S(1)} %get-tuple-element.36), channel_id=1, source_target_pairs={{0,4},{4,0},{8,12},{12,8},{16,20},{20,16},{24,28},{28,24},{1,5},{5... | collective-permute-start | bytes 491528 | tf_op jit(solution)/shard_map/ppermute | solution.py:384
  18.8 16.6 %collective-permute-start.2 = (bf16[640,256]{1,0:T(8,128)(2,1)S(1)}, bf16[640,256]{1,0:T(8,128)(2,1)S(1)}, u32[]{:S(2)}, u32[]{:S(2)}) collective-permute-start(bf16[640,256]{1,0:T(8,128)(2,1)S(1)} %collective-permute-done.refs_2_), channel_id=1, source_target_pairs={{4,12},{8,0},{12,20},{16,8},{20,28},{24,16},{5,13},{9,1},{13,21},{... | collective-permute-start | bytes 983048 | tf_op jit(solution)/shard_map/ppermute | solution.py:387
  22.3 13.1 %collective-permute-start.5 = (bf16[640,256]{1,0:T(8,128)(2,1)S(1)}, bf16[640,256]{1,0:T(8,128)(2,1)S(1)}, u32[]{:S(2)}, u32[]{:S(2)}) collective-permute-start(bf16[640,256]{1,0:T(8,128)(2,1)S(1)} %collective-permute-done.4.refs_3_), channel_id=1, source_target_pairs={{4,12},{8,0},{12,20},{16,8},{20,28},{24,16},{5,13},{9,1},{13,21},{... | collective-permute-start | bytes 983048 | tf_op jit(solution)/shard_map/ppermute | solution.py:388
  26.8 9.3 %collective-permute-start.6 = (bf16[640,256]{1,0:T(8,128)(2,1)S(1)}, bf16[640,256]{1,0:T(8,128)(2,1)S(1)}, u32[]{:S(2)}, u32[]{:S(2)}) collective-permute-start(bf16[640,256]{1,0:T(8,128)(2,1)S(1)} %collective-permute-done.3.refs_2_), channel_id=1, source_target_pairs={{0,8},{8,16},{12,4},{16,24},{20,12},{28,20},{1,9},{9,17},{13,5},{1... | collective-permute-start | bytes 983048 | tf_op jit(solution)/shard_map/ppermute | solution.py:394
  38.7 5.4 %copy-start = (bf16[640,1280]{1,0:T(8,128)(2,1)S(1)}, bf16[640,1280]{1,0:T(8,128)(2,1)}, u32[]{:S(2)}) copy-start(bf16[640,1280]{1,0:T(8,128)(2,1)} %weight_ref.1) | copy-start | bytes 4915204
  38.7 5.4 %copy-start.1 = (bf16[256,1280]{1,0:T(8,128)(2,1)S(1)}, bf16[256,1280]{1,0:T(8,128)(2,1)}, u32[]{:S(2)}) copy-start(bf16[256,1280]{1,0:T(8,128)(2,1)} %tokens_ref.1) | copy-start | bytes 1966084
  38.7 5.4 %copy-start.4 = (s32[64]{0:T(128)S(1)}, s32[64]{0:T(128)}, u32[]{:S(2)}) copy-start(s32[64]{0:T(128)} %param.16) | copy-start | bytes 772
  38.7 5.4 %copy-start.5 = (s32[64]{0:T(128)S(1)}, s32[64]{0:T(128)}, u32[]{:S(2)}) copy-start(s32[64]{0:T(128)} %param.17) | copy-start | bytes 772
  38.7 5.4 %collective-permute-start.8 = (bf16[320,256]{1,0:T(8,128)(2,1)S(1)}, bf16[320,256]{1,0:T(8,128)(2,1)S(1)}, u32[]{:S(2)}, u32[]{:S(2)}) collective-permute-start(bf16[320,256]{1,0:T(8,128)(2,1)S(1)} %shard_map.96), channel_id=1, source_target_pairs={{0,4},{4,0},{8,12},{12,8},{16,20},{20,16},{24,28},{28,24},{1,5},{5... | collective-permute-start | bytes 491528 | tf_op jit(solution)/shard_map/ppermute | solution.py:398
  45.6 13.4 %collective-permute-start.10 = (bf16[16,5248]{1,0:T(8,128)(2,1)S(1)}, bf16[16,5248]{1,0:T(8,128)(2,1)S(1)}, u32[]{:S(2)}, u32[]{:S(2)}) collective-permute-start(bf16[16,5248]{1,0:T(8,128)(2,1)S(1)} %get-tuple-element.39), channel_id=1, source_target_pairs={{0,8},{4,12},{8,16},{12,20},{16,24},{20,28},{24,0},{28,4},{1,9},{5... | collective-permute-start | bytes 503816 | tf_op jit(solution)/shard_map/ppermute | solution.py:410
  46.5 20.0 %collective-permute-start.11 = (bf16[16,5248]{1,0:T(8,128)(2,1)S(1)}, bf16[16,5248]{1,0:T(8,128)(2,1)S(1)}, u32[]{:S(2)}, u32[]{:S(2)}) collective-permute-start(bf16[16,5248]{1,0:T(8,128)(2,1)S(1)} %get-tuple-element.40), channel_id=1, source_target_pairs={{0,12},{4,16},{8,20},{12,24},{16,28},{20,0},{24,4},{28,8},{1,13},{... | collective-permute-start | bytes 503816 | tf_op jit(solution)/shard_map/ppermute | solution.py:410
  49.2 20.5 %collective-permute-start.12 = (bf16[16,5248]{1,0:T(8,128)(2,1)S(1)}, bf16[16,5248]{1,0:T(8,128)(2,1)S(1)}, u32[]{:S(2)}, u32[]{:S(2)}) collective-permute-start(bf16[16,5248]{1,0:T(8,128)(2,1)S(1)} %get-tuple-element.41), channel_id=1, source_target_pairs={{0,16},{4,20},{8,24},{12,28},{16,0},{20,4},{24,8},{28,12},{1,17},{... | collective-permute-start | bytes 503816 | tf_op jit(solution)/shard_map/ppermute | solution.py:410
  49.8 19.9 %collective-permute-start.13 = (bf16[16,5248]{1,0:T(8,128)(2,1)S(1)}, bf16[16,5248]{1,0:T(8,128)(2,1)S(1)}, u32[]{:S(2)}, u32[]{:S(2)}) collective-permute-start(bf16[16,5248]{1,0:T(8,128)(2,1)S(1)} %get-tuple-element.42), channel_id=1, source_target_pairs={{0,20},{4,24},{8,28},{12,0},{16,4},{20,8},{24,12},{28,16},{1,21},{... | collective-permute-start | bytes 503816 | tf_op jit(solution)/shard_map/ppermute | solution.py:410
  52.7 21.1 %collective-permute-start.14 = (bf16[16,5248]{1,0:T(8,128)(2,1)S(1)}, bf16[16,5248]{1,0:T(8,128)(2,1)S(1)}, u32[]{:S(2)}, u32[]{:S(2)}) collective-permute-start(bf16[16,5248]{1,0:T(8,128)(2,1)S(1)} %get-tuple-element.43), channel_id=1, source_target_pairs={{0,24},{4,28},{8,0},{12,4},{16,8},{20,12},{24,16},{28,20},{1,25},{... | collective-permute-start | bytes 503816 | tf_op jit(solution)/shard_map/ppermute | solution.py:410
  59.1 15.1 %collective-permute-start.15 = (bf16[16,5248]{1,0:T(8,128)(2,1)S(1)}, bf16[16,5248]{1,0:T(8,128)(2,1)S(1)}, u32[]{:S(2)}, u32[]{:S(2)}) collective-permute-start(bf16[16,5248]{1,0:T(8,128)(2,1)S(1)} %get-tuple-element.44), channel_id=1, source_target_pairs={{0,28},{4,0},{8,4},{12,8},{16,12},{20,16},{24,20},{28,24},{1,29},{... | collective-permute-start | bytes 503816 | tf_op jit(solution)/shard_map/ppermute | solution.py:410
  66.5 9.0 %collective-permute-start.9 = (bf16[16,5248]{1,0:T(8,128)(2,1)S(1)}, bf16[16,5248]{1,0:T(8,128)(2,1)S(1)}, u32[]{:S(2)}, u32[]{:S(2)}) collective-permute-start(bf16[16,5248]{1,0:T(8,128)(2,1)S(1)} %get-tuple-element.38), channel_id=1, source_target_pairs={{0,4},{4,8},{8,12},{12,16},{16,20},{20,24},{24,28},{28,0},{1,5},{5... | collective-permute-start | bytes 503816 | tf_op jit(solution)/shard_map/ppermute | solution.py:410

commit v11 on v10

--- a/solution.py
+++ b/solution.py
@@ -381,22 +381,24 @@
     other_kv = swap(swap_kv)
     ahead_own = ahead(own_kv)
     back_own = back(own_kv)
+    ready, back_own, swap_q, segs, need = lax.optimization_barrier(
+        (other_kv, back_own, swap_q, segs, need)
+    )
+    back_other = back(ready)
     other_q = swap(swap_q)
-    ready, back_own, segs, need = lax.optimization_barrier((other_kv, back_own, segs, need))
-    back_other = back(ready)
+    back_far = back(back_other)
     ahead_other = ahead(other_kv)
     ahead_far = ahead(ahead_own)
     near = (own_kv, other_kv, ahead_own, back_own)
-    near_numbers, far_numbers = (0, 1, 2, 3), (4, 5, 6, 7)
+    near_numbers = (0, 1, 2, 3)
     fixed = (where, need, segs)
     own = attention(*fixed, (own_q,), (0,), near, near_numbers, None, False)
-    back_other, own = lax.optimization_barrier((back_other, own))
-    back_far = back(back_other)
     other = attention(*fixed, (other_q,), (1,), near, near_numbers, None, False)
-    far = (ahead_other, back_other, ahead_far, back_far)
-    other = attention(*fixed, (other_q,), (1,), far, far_numbers, other, True)
+    far = (ahead_other, back_other, ahead_far)
+    other = attention(*fixed, (other_q,), (1,), far, (4, 5, 6), other, True)
     other = swap(other)
-    own = attention(*fixed, (own_q,), (0,), far, far_numbers, own, True)
+    far = (ahead_other, back_other, back_far)
+    own = attention(*fixed, (own_q,), (0,), far, (4, 5, 7), own, True)
 
     pieces = nblocks if nblocks <= 8 else 1
     outgoing = project(

time: 77.8 us -> 77 us (0.990)
  waiting for transfers between devices: 30.2 us -> 29.3 us
  transfers between devices with their start and end apart: 16 -> 16, of which waited for: 11 -> 10; matrix products, arithmetic and copies ran while one was open for 0% -> 0% of each run, Pallas kernels for 11% -> 15%
where the time goes in v11:
time: 77 us; the launch traced here: 76.4 us
  waiting for transfers between devices  29.3 us (38%)
  starting transfers between devices  29.1 us (38%)
  Pallas kernels  16.2 us (21%)
  local copies, waits for them, and re-layouts  1.4 us (2%)
    ppermute x7, waiting for transfers between devices, per_device(): lax.ppermute(outgoing[d], 'blk', [(i, (i + d) % nblocks) for i in range(n...  22.2 us
    pallas_call x4, Pallas kernels, attention(): pl.pallas_call(functools.partial(attention_kernel, kinds, numbers, follow...  10.5 us
    ppermute x7, starting transfers between devices, per_device(): lax.ppermute(outgoing[d], 'blk', [(i, (i + d) % nblocks) for i in range(n...  7.9 us
    ppermute x1, starting transfers between devices, per_device(): back_far = back(back_other)  3.93 us
    ppermute x1, starting transfers between devices, per_device(): ahead_own = ahead(own_kv)  3.48 us
    ppermute x1, starting transfers between devices, per_device(): ahead_other = ahead(other_kv)  3.47 us
    ppermute x1, starting transfers between devices, per_device(): other_q = swap(swap_q)  2.71 us
    ppermute x1, starting transfers between devices, per_device(): back_other = back(ready)  2.35 us
  transfers between devices with their start and end apart: 16, of which 10 were waited for; matrix products, arithmetic and copies ran while one was open for 0% of the time, Pallas kernels for 15%

profile of v11, /device:TPU:14, one launch (start us, length us, event | category | flops | bytes accessed | tf_op | source)
XLA Modules:
  0.0 76.4 jit_solution(10991112445899447660)
XLA Ops:
  0.0 2.1 %shard_map.91 = (bf16[320,256]{1,0:T(8,128)(2,1)S(1)}, bf16[640,256]{1,0:T(8,128)(2,1)S(1)}, bf16[320,256]{1,0:T(8,128)(2,1)S(1)}, bf16[640,256]{1,0:T(8,128)(2,1)}) custom-call(s32[1]{0:T(128)} %bitcast.where_ref, bf16[256,640]{1,0:T(8,128)(2,1)} %q_hbm.1, bf16[256,640]{1,0:T(8,128)(2,1)} %k_hbm.1, bf16[256,640]{1,0:T(8,128)(2,1)} %v_hbm.1), custom_call_target="tpu_custom_call" | custom-call | tf_op jit(solution)/shard_map/pallas_call | solution.py:74
  2.7 2.3 %collective-permute-start.1 = (bf16[640,256]{1,0:T(8,128)(2,1)S(1)}, bf16[640,256]{1,0:T(8,128)(2,1)S(1)}, u32[]{:S(2)}, u32[]{:S(2)}) collective-permute-start(bf16[640,256]{1,0:T(8,128)(2,1)S(1)} %get-tuple-element.25.refs_1_), channel_id=1, source_target_pairs={{0,8},{8,16},{12,4},{16,24},{20,12},{28,20},{1,9},{9,17},{13,5},{1... | collective-permute-start | bytes 983048 | tf_op jit(solution)/shard_map/ppermute | solution.py:383
  5.0 3.5 %collective-permute-start.5 = (bf16[640,256]{1,0:T(8,128)(2,1)S(1)}, bf16[640,256]{1,0:T(8,128)(2,1)S(1)}, u32[]{:S(2)}, u32[]{:S(2)}) collective-permute-start(bf16[640,256]{1,0:T(8,128)(2,1)S(1)} %get-tuple-element.25.refs_1_), channel_id=1, source_target_pairs={{4,12},{8,0},{12,20},{16,8},{20,28},{24,16},{5,13},{9,1},{13,21},{... | collective-permute-start | bytes 983048 | tf_op jit(solution)/shard_map/ppermute | solution.py:382
  11.8 1.9 %collective-permute-done.1.refs_4_ = bf16[640,256]{1,0:T(8,128)(2,1)S(1)} collective-permute-done((bf16[640,256]{1,0:T(8,128)(2,1)S(1)}, bf16[640,256]{1,0:T(8,128)(2,1)S(1)}, u32[]{:S(2)}, u32[]{:S(2)}) %collective-permute-start.1) | collective-permute-done | bytes 327712 | tf_op jit(solution)/shard_map/ppermute | solution.py:383
  13.7 2.3 %collective-permute-start.3 = (bf16[640,256]{1,0:T(8,128)(2,1)S(1)}, bf16[640,256]{1,0:T(8,128)(2,1)S(1)}, u32[]{:S(2)}, u32[]{:S(2)}) collective-permute-start(bf16[640,256]{1,0:T(8,128)(2,1)S(1)} %collective-permute-done.refs_2_), channel_id=1, source_target_pairs={{0,8},{8,16},{12,4},{16,24},{20,12},{28,20},{1,9},{9,17},{13,5},{1... | collective-permute-start | bytes 983048 | tf_op jit(solution)/shard_map/ppermute | solution.py:387
  16.1 2.7 %collective-permute-start.6 = (bf16[320,256]{1,0:T(8,128)(2,1)S(1)}, bf16[320,256]{1,0:T(8,128)(2,1)S(1)}, u32[]{:S(2)}, u32[]{:S(2)}) collective-permute-start(bf16[320,256]{1,0:T(8,128)(2,1)S(1)} %get-tuple-element.34), channel_id=1, source_target_pairs={{0,4},{4,0},{8,12},{12,8},{16,20},{20,16},{24,28},{28,24},{1,5},{5... | collective-permute-start | bytes 491528 | tf_op jit(solution)/shard_map/ppermute | solution.py:388
  18.8 3.5 %collective-permute-start.2 = (bf16[640,256]{1,0:T(8,128)(2,1)S(1)}, bf16[640,256]{1,0:T(8,128)(2,1)S(1)}, u32[]{:S(2)}, u32[]{:S(2)}) collective-permute-start(bf16[640,256]{1,0:T(8,128)(2,1)S(1)} %collective-permute-done.refs_2_), channel_id=1, source_target_pairs={{4,12},{8,0},{12,20},{16,8},{20,28},{24,16},{5,13},{9,1},{13,21},{... | collective-permute-start | bytes 983048 | tf_op jit(solution)/shard_map/ppermute | solution.py:390
  22.3 1.9 %collective-permute-start.7 = (bf16[640,256]{1,0:T(8,128)(2,1)S(1)}, bf16[640,256]{1,0:T(8,128)(2,1)S(1)}, u32[]{:S(2)}, u32[]{:S(2)}) collective-permute-start(bf16[640,256]{1,0:T(8,128)(2,1)S(1)} %collective-permute-done.5.refs_3_), channel_id=1, source_target_pairs={{4,12},{8,0},{12,20},{16,8},{20,28},{24,16},{5,13},{9,1},{13,21},{... | collective-permute-start | bytes 983048 | tf_op jit(solution)/shard_map/ppermute | solution.py:391
  24.2 2.6 %shard_map.93.refs_4_ = f32[1,4,256,128]{3,2,1,0:T(8,128)S(1)} custom-call(s32[1]{0:T(128)} %bitcast.where_ref, s32[8,128]{1,0:T(8,128)S(1)} %get-tuple-element.29.need_ref, f32[1,2048]{1,0:T(1,128)S(1)} %get-tuple-element.30.seg_ref, bf16[320,256]{1,0:T(8,128)(2,1)S(1)} %get-tuple-element.31.refs_0_, bf16[640,256]{1,0:T(8,128)(2,1)S(1)} %get-tuple-element.25.refs_1_, ...), custom_call_target="tpu_custom_call" | custom-call | flops 2000000000 | bytes 2000000 | tf_op jit(solution)/shard_map/pallas_call | solution.py:234
  26.8 3.9 %collective-permute-start.4 = (bf16[640,256]{1,0:T(8,128)(2,1)S(1)}, bf16[640,256]{1,0:T(8,128)(2,1)S(1)}, u32[]{:S(2)}, u32[]{:S(2)}) collective-permute-start(bf16[640,256]{1,0:T(8,128)(2,1)S(1)} %collective-permute-done.3.refs_2_), channel_id=1, source_target_pairs={{0,8},{8,16},{12,4},{16,24},{20,12},{28,20},{1,9},{9,17},{13,5},{1... | collective-permute-start | bytes 983048 | tf_op jit(solution)/shard_map/ppermute | solution.py:389
  30.8 2.6 %shard_map.95.refs_4_ = f32[1,4,256,128]{3,2,1,0:T(8,128)S(1)} custom-call(s32[1]{0:T(128)} %bitcast.where_ref, s32[8,128]{1,0:T(8,128)S(1)} %get-tuple-element.29.need_ref, f32[1,2048]{1,0:T(1,128)S(1)} %get-tuple-element.30.seg_ref, bf16[320,256]{1,0:T(8,128)(2,1)S(1)} %collective-permute-done.6.refs_0_, bf16[640,256]{1,0:T(8,128)(2,1)S(1)} %get-tuple-element.25.refs_1_, ...), custom_call_target="tpu_custom_call" | custom-call | flops 2000000000 | bytes 2000000 | tf_op jit(solution)/shard_map/pallas_call | solution.py:234
  33.4 2.0 %collective-permute-done.7.refs_3_ = bf16[640,256]{1,0:T(8,128)(2,1)S(1)} collective-permute-done((bf16[640,256]{1,0:T(8,128)(2,1)S(1)}, bf16[640,256]{1,0:T(8,128)(2,1)S(1)}, u32[]{:S(2)}, u32[]{:S(2)}) %collective-permute-start.7) | collective-permute-done | bytes 327712 | tf_op jit(solution)/shard_map/ppermute | solution.py:391
  35.4 2.4 %shard_map.96 = bf16[320,256]{1,0:T(8,128)(2,1)S(1)} custom-call(s32[1]{0:T(128)} %bitcast.where_ref, s32[8,128]{1,0:T(8,128)S(1)} %get-tuple-element.29.need_ref, f32[1,2048]{1,0:T(1,128)S(1)} %get-tuple-element.30.seg_ref, bf16[320,256]{1,0:T(8,128)(2,1)S(1)} %collective-permute-done.6.refs_0_, bf16[640,256]{1,0:T(8,128)(2,1)S(1)} %collective-permute-done.2.refs_1_, ...), custom_call_target="tpu_custom_call" | custom-call | flops 2000000000 | bytes 2000000 | tf_op jit(solution)/shard_map/pallas_call | solution.py:234
  38.2 2.9 %shard_map.94.own_ref = bf16[320,256]{1,0:T(8,128)(2,1)S(1)} custom-call(s32[1]{0:T(128)} %bitcast.where_ref, s32[8,128]{1,0:T(8,128)S(1)} %get-tuple-element.29.need_ref, f32[1,2048]{1,0:T(1,128)S(1)} %get-tuple-element.30.seg_ref, bf16[320,256]{1,0:T(8,128)(2,1)S(1)} %get-tuple-element.31.refs_0_, bf16[640,256]{1,0:T(8,128)(2,1)S(1)} %collective-permute-done.2.refs_1_, ...), custom_call_target="tpu_custom_call" | custom-call | flops 2000000000 | bytes 2000000 | tf_op jit(solution)/shard_map/pallas_call | solution.py:234
  41.1 2.1 %collective-permute-done.8.other_ref = bf16[320,256]{1,0:T(8,128)(2,1)S(1)} collective-permute-done((bf16[320,256]{1,0:T(8,128)(2,1)S(1)}, bf16[320,256]{1,0:T(8,128)(2,1)S(1)}, u32[]{:S(2)}, u32[]{:S(2)}) %collective-permute-start.8) | collective-permute-done | bytes 163872 | tf_op jit(solution)/shard_map/ppermute | solution.py:399
  43.2 1.5 %shard_map.97 = (bf16[16,5248]{1,0:T(8,128)(2,1)S(1)}, bf16[16,5248]{1,0:T(8,128)(2,1)S(1)}, bf16[16,5248]{1,0:T(8,128)(2,1)S(1)}, bf16[16,5248]{1,0:T(8,128)(2,...) custom-call(s32[1]{0:T(128)} %bitcast.where_ref, ...), custom_call_target="tpu_custom_call" | custom-call | tf_op jit(solution)/shard_map/pallas_call | solution.py:305
  44.8 2.6 %collective-permute-start.11 = (bf16[16,5248]{1,0:T(8,128)(2,1)S(1)}, bf16[16,5248]{1,0:T(8,128)(2,1)S(1)}, u32[]{:S(2)}, u32[]{:S(2)}) collective-permute-start(bf16[16,5248]{1,0:T(8,128)(2,1)S(1)} %get-tuple-element.38), channel_id=1, source_target_pairs={{0,12},{4,16},{8,20},{12,24},{16,28},{20,0},{24,4},{28,8},{1,13},{... | collective-permute-start | bytes 503816 | tf_op jit(solution)/shard_map/ppermute | solution.py:412
  47.3 1.7 %collective-permute-start.12 = (bf16[16,5248]{1,0:T(8,128)(2,1)S(1)}, bf16[16,5248]{1,0:T(8,128)(2,1)S(1)}, u32[]{:S(2)}, u32[]{:S(2)}) collective-permute-start(bf16[16,5248]{1,0:T(8,128)(2,1)S(1)} %get-tuple-element.39), channel_id=1, source_target_pairs={{0,16},{4,20},{8,24},{12,28},{16,0},{20,4},{24,8},{28,12},{1,17},{... | collective-permute-start | bytes 503816 | tf_op jit(solution)/shard_map/ppermute | solution.py:412
  49.6 1.9 %collective-permute-start.14 = (bf16[16,5248]{1,0:T(8,128)(2,1)S(1)}, bf16[16,5248]{1,0:T(8,128)(2,1)S(1)}, u32[]{:S(2)}, u32[]{:S(2)}) collective-permute-start(bf16[16,5248]{1,0:T(8,128)(2,1)S(1)} %get-tuple-element.41), channel_id=1, source_target_pairs={{0,24},{4,28},{8,0},{12,4},{16,8},{20,12},{24,16},{28,20},{1,25},{... | collective-permute-start | bytes 503816 | tf_op jit(solution)/shard_map/ppermute | solution.py:412
  51.5 7.2 %collective-permute-done.10.refs_2_ = bf16[16,5248]{1,0:T(8,128)(2,1)S(1)} collective-permute-done((bf16[16,5248]{1,0:T(8,128)(2,1)S(1)}, bf16[16,5248]{1,0:T(8,128)(2,1)S(1)}, u32[]{:S(2)}, u32[]{:S(2)}) %collective-permute-start.10) | collective-permute-done | bytes 167968 | tf_op jit(solution)/shard_map/ppermute | solution.py:412
  58.7 7.2 %collective-permute-done.11.refs_3_ = bf16[16,5248]{1,0:T(8,128)(2,1)S(1)} collective-permute-done((bf16[16,5248]{1,0:T(8,128)(2,1)S(1)}, bf16[16,5248]{1,0:T(8,128)(2,1)S(1)}, u32[]{:S(2)}, u32[]{:S(2)}) %collective-permute-start.11) | collective-permute-done | bytes 167968 | tf_op jit(solution)/shard_map/ppermute | solution.py:412
  67.0 1.6 %collective-permute-done.12.refs_4_ = bf16[16,5248]{1,0:T(8,128)(2,1)S(1)} collective-permute-done((bf16[16,5248]{1,0:T(8,128)(2,1)S(1)}, bf16[16,5248]{1,0:T(8,128)(2,1)S(1)}, u32[]{:S(2)}, u32[]{:S(2)}) %collective-permute-start.12) | collective-permute-done | bytes 167968 | tf_op jit(solution)/shard_map/ppermute | solution.py:412
  68.7 3.4 %collective-permute-done.14.refs_6_ = bf16[16,5248]{1,0:T(8,128)(2,1)S(1)} collective-permute-done((bf16[16,5248]{1,0:T(8,128)(2,1)S(1)}, bf16[16,5248]{1,0:T(8,128)(2,1)S(1)}, u32[]{:S(2)}, u32[]{:S(2)}) %collective-permute-start.14) | collective-permute-done | bytes 167968 | tf_op jit(solution)/shard_map/ppermute | solution.py:412
  73.1 1.7 %collective-permute-done.9.refs_1_ = bf16[16,5248]{1,0:T(8,128)(2,1)S(1)} collective-permute-done((bf16[16,5248]{1,0:T(8,128)(2,1)S(1)}, bf16[16,5248]{1,0:T(8,128)(2,1)S(1)}, u32[]{:S(2)}, u32[]{:S(2)}) %collective-permute-start.9) | collective-permute-done | bytes 167968 | tf_op jit(solution)/shard_map/ppermute | solution.py:412
  (28 shorter events, 8.5 us)
Async XLA Ops:
  2.1 9.7 %collective-permute-start = (bf16[640,256]{1,0:T(8,128)(2,1)}, bf16[640,256]{1,0:T(8,128)(2,1)S(1)}, u32[]{:S(2)}, u32[]{:S(2)}) collective-permute-start(bf16[640,256]{1,0:T(8,128)(2,1)} %get-tuple-element.24), channel_id=1, source_target_pairs={{0,4},{4,0},{8,12},{12,8},{16,20},{20,16},{24,28},{28,24},{1,5},{5... | collective-permute-start | bytes 983048 | tf_op jit(solution)/shard_map/ppermute | solution.py:381
  2.7 11.1 %collective-permute-start.1 = (bf16[640,256]{1,0:T(8,128)(2,1)S(1)}, bf16[640,256]{1,0:T(8,128)(2,1)S(1)}, u32[]{:S(2)}, u32[]{:S(2)}) collective-permute-start(bf16[640,256]{1,0:T(8,128)(2,1)S(1)} %get-tuple-element.25.refs_1_), channel_id=1, source_target_pairs={{0,8},{8,16},{12,4},{16,24},{20,12},{28,20},{1,9},{9,17},{13,5},{1... | collective-permute-start | bytes 983048 | tf_op jit(solution)/shard_map/ppermute | solution.py:383
  5.0 17.2 %collective-permute-start.5 = (bf16[640,256]{1,0:T(8,128)(2,1)S(1)}, bf16[640,256]{1,0:T(8,128)(2,1)S(1)}, u32[]{:S(2)}, u32[]{:S(2)}) collective-permute-start(bf16[640,256]{1,0:T(8,128)(2,1)S(1)} %get-tuple-element.25.refs_1_), channel_id=1, source_target_pairs={{4,12},{8,0},{12,20},{16,8},{20,28},{24,16},{5,13},{9,1},{13,21},{... | collective-permute-start | bytes 983048 | tf_op jit(solution)/shard_map/ppermute | solution.py:382
  8.5 0.7 copy-start.2
  9.2 0.7 copy-start.3
  13.7 13.1 %collective-permute-start.3 = (bf16[640,256]{1,0:T(8,128)(2,1)S(1)}, bf16[640,256]{1,0:T(8,128)(2,1)S(1)}, u32[]{:S(2)}, u32[]{:S(2)}) collective-permute-start(bf16[640,256]{1,0:T(8,128)(2,1)S(1)} %collective-permute-done.refs_2_), channel_id=1, source_target_pairs={{0,8},{8,16},{12,4},{16,24},{20,12},{28,20},{1,9},{9,17},{13,5},{1... | collective-permute-start | bytes 983048 | tf_op jit(solution)/shard_map/ppermute | solution.py:387
  16.1 14.7 %collective-permute-start.6 = (bf16[320,256]{1,0:T(8,128)(2,1)S(1)}, bf16[320,256]{1,0:T(8,128)(2,1)S(1)}, u32[]{:S(2)}, u32[]{:S(2)}) collective-permute-start(bf16[320,256]{1,0:T(8,128)(2,1)S(1)} %get-tuple-element.34), channel_id=1, source_target_pairs={{0,4},{4,0},{8,12},{12,8},{16,20},{20,16},{24,28},{28,24},{1,5},{5... | collective-permute-start | bytes 491528 | tf_op jit(solution)/shard_map/ppermute | solution.py:388
  18.8 16.6 %collective-permute-start.2 = (bf16[640,256]{1,0:T(8,128)(2,1)S(1)}, bf16[640,256]{1,0:T(8,128)(2,1)S(1)}, u32[]{:S(2)}, u32[]{:S(2)}) collective-permute-start(bf16[640,256]{1,0:T(8,128)(2,1)S(1)} %collective-permute-done.refs_2_), channel_id=1, source_target_pairs={{4,12},{8,0},{12,20},{16,8},{20,28},{24,16},{5,13},{9,1},{13,21},{... | collective-permute-start | bytes 983048 | tf_op jit(solution)/shard_map/ppermute | solution.py:390
  22.3 13.1 %collective-permute-start.7 = (bf16[640,256]{1,0:T(8,128)(2,1)S(1)}, bf16[640,256]{1,0:T(8,128)(2,1)S(1)}, u32[]{:S(2)}, u32[]{:S(2)}) collective-permute-start(bf16[640,256]{1,0:T(8,128)(2,1)S(1)} %collective-permute-done.5.refs_3_), channel_id=1, source_target_pairs={{4,12},{8,0},{12,20},{16,8},{20,28},{24,16},{5,13},{9,1},{13,21},{... | collective-permute-start | bytes 983048 | tf_op jit(solution)/shard_map/ppermute | solution.py:391
  26.8 11.4 %collective-permute-start.4 = (bf16[640,256]{1,0:T(8,128)(2,1)S(1)}, bf16[640,256]{1,0:T(8,128)(2,1)S(1)}, u32[]{:S(2)}, u32[]{:S(2)}) collective-permute-start(bf16[640,256]{1,0:T(8,128)(2,1)S(1)} %collective-permute-done.3.refs_2_), channel_id=1, source_target_pairs={{0,8},{8,16},{12,4},{16,24},{20,12},{28,20},{1,9},{9,17},{13,5},{1... | collective-permute-start | bytes 983048 | tf_op jit(solution)/shard_map/ppermute | solution.py:389
  37.8 5.4 %copy-start = (bf16[640,1280]{1,0:T(8,128)(2,1)S(1)}, bf16[640,1280]{1,0:T(8,128)(2,1)}, u32[]{:S(2)}) copy-start(bf16[640,1280]{1,0:T(8,128)(2,1)} %weight_ref.1) | copy-start | bytes 4915204
  37.8 5.4 %copy-start.1 = (bf16[256,1280]{1,0:T(8,128)(2,1)S(1)}, bf16[256,1280]{1,0:T(8,128)(2,1)}, u32[]{:S(2)}) copy-start(bf16[256,1280]{1,0:T(8,128)(2,1)} %tokens_ref.1) | copy-start | bytes 1966084
  37.8 5.4 %copy-start.4 = (s32[64]{0:T(128)S(1)}, s32[64]{0:T(128)}, u32[]{:S(2)}) copy-start(s32[64]{0:T(128)} %param.16) | copy-start | bytes 772
  37.8 5.4 %copy-start.5 = (s32[64]{0:T(128)S(1)}, s32[64]{0:T(128)}, u32[]{:S(2)}) copy-start(s32[64]{0:T(128)} %param.17) | copy-start | bytes 772
  37.8 5.4 %collective-permute-start.8 = (bf16[320,256]{1,0:T(8,128)(2,1)S(1)}, bf16[320,256]{1,0:T(8,128)(2,1)S(1)}, u32[]{:S(2)}, u32[]{:S(2)}) collective-permute-start(bf16[320,256]{1,0:T(8,128)(2,1)S(1)} %shard_map.96), channel_id=1, source_target_pairs={{0,4},{4,0},{8,12},{12,8},{16,20},{20,16},{24,28},{28,24},{1,5},{5... | collective-permute-start | bytes 491528 | tf_op jit(solution)/shard_map/ppermute | solution.py:399
  44.7 14.0 %collective-permute-start.10 = (bf16[16,5248]{1,0:T(8,128)(2,1)S(1)}, bf16[16,5248]{1,0:T(8,128)(2,1)S(1)}, u32[]{:S(2)}, u32[]{:S(2)}) collective-permute-start(bf16[16,5248]{1,0:T(8,128)(2,1)S(1)} %get-tuple-element.37), channel_id=1, source_target_pairs={{0,8},{4,12},{8,16},{12,20},{16,24},{20,28},{24,0},{28,4},{1,9},{5... | collective-permute-start | bytes 503816 | tf_op jit(solution)/shard_map/ppermute | solution.py:412
  44.8 21.2 %collective-permute-start.11 = (bf16[16,5248]{1,0:T(8,128)(2,1)S(1)}, bf16[16,5248]{1,0:T(8,128)(2,1)S(1)}, u32[]{:S(2)}, u32[]{:S(2)}) collective-permute-start(bf16[16,5248]{1,0:T(8,128)(2,1)S(1)} %get-tuple-element.38), channel_id=1, source_target_pairs={{0,12},{4,16},{8,20},{12,24},{16,28},{20,0},{24,4},{28,8},{1,13},{... | collective-permute-start | bytes 503816 | tf_op jit(solution)/shard_map/ppermute | solution.py:412
  47.3 21.4 %collective-permute-start.12 = (bf16[16,5248]{1,0:T(8,128)(2,1)S(1)}, bf16[16,5248]{1,0:T(8,128)(2,1)S(1)}, u32[]{:S(2)}, u32[]{:S(2)}) collective-permute-start(bf16[16,5248]{1,0:T(8,128)(2,1)S(1)} %get-tuple-element.39), channel_id=1, source_target_pairs={{0,16},{4,20},{8,24},{12,28},{16,0},{20,4},{24,8},{28,12},{1,17},{... | collective-permute-start | bytes 503816 | tf_op jit(solution)/shard_map/ppermute | solution.py:412
  49.0 19.7 %collective-permute-start.13 = (bf16[16,5248]{1,0:T(8,128)(2,1)S(1)}, bf16[16,5248]{1,0:T(8,128)(2,1)S(1)}, u32[]{:S(2)}, u32[]{:S(2)}) collective-permute-start(bf16[16,5248]{1,0:T(8,128)(2,1)S(1)} %get-tuple-element.40), channel_id=1, source_target_pairs={{0,20},{4,24},{8,28},{12,0},{16,4},{20,8},{24,12},{28,16},{1,21},{... | collective-permute-start | bytes 503816 | tf_op jit(solution)/shard_map/ppermute | solution.py:412
  49.6 22.5 %collective-permute-start.14 = (bf16[16,5248]{1,0:T(8,128)(2,1)S(1)}, bf16[16,5248]{1,0:T(8,128)(2,1)S(1)}, u32[]{:S(2)}, u32[]{:S(2)}) collective-permute-start(bf16[16,5248]{1,0:T(8,128)(2,1)S(1)} %get-tuple-element.41), channel_id=1, source_target_pairs={{0,24},{4,28},{8,0},{12,4},{16,8},{20,12},{24,16},{28,20},{1,25},{... | collective-permute-start | bytes 503816 | tf_op jit(solution)/shard_map/ppermute | solution.py:412
  58.7 14.4 %collective-permute-start.15 = (bf16[16,5248]{1,0:T(8,128)(2,1)S(1)}, bf16[16,5248]{1,0:T(8,128)(2,1)S(1)}, u32[]{:S(2)}, u32[]{:S(2)}) collective-permute-start(bf16[16,5248]{1,0:T(8,128)(2,1)S(1)} %get-tuple-element.42), channel_id=1, source_target_pairs={{0,28},{4,0},{8,4},{12,8},{16,12},{20,16},{24,20},{28,24},{1,29},{... | collective-permute-start | bytes 503816 | tf_op jit(solution)/shard_map/ppermute | solution.py:412
  65.9 8.8 %collective-permute-start.9 = (bf16[16,5248]{1,0:T(8,128)(2,1)S(1)}, bf16[16,5248]{1,0:T(8,128)(2,1)S(1)}, u32[]{:S(2)}, u32[]{:S(2)}) collective-permute-start(bf16[16,5248]{1,0:T(8,128)(2,1)S(1)} %get-tuple-element.36), channel_id=1, source_target_pairs={{0,4},{4,8},{8,12},{12,16},{16,20},{20,24},{24,28},{28,0},{1,5},{5... | collective-permute-start | bytes 503816 | tf_op jit(solution)/shard_map/ppermute | solution.py:412

commit v12 on v11

--- a/solution.py
+++ b/solution.py
@@ -381,14 +381,13 @@
     other_kv = swap(swap_kv)
     ahead_own = ahead(own_kv)
     back_own = back(own_kv)
-    ready, back_own, swap_q, segs, need = lax.optimization_barrier(
-        (other_kv, back_own, swap_q, segs, need)
-    )
+    ready, ahead_own, segs, need = lax.optimization_barrier((other_kv, ahead_own, segs, need))
+    ahead_far = ahead(ahead_own)
     back_other = back(ready)
+    ready, back_own, swap_q = lax.optimization_barrier((ready, back_own, swap_q))
     other_q = swap(swap_q)
+    ahead_other = ahead(ready)
     back_far = back(back_other)
-    ahead_other = ahead(other_kv)
-    ahead_far = ahead(ahead_own)
     near = (own_kv, other_kv, ahead_own, back_own)
     near_numbers = (0, 1, 2, 3)
     fixed = (where, need, segs)

time: 77 us -> 77.1 us (level)
  starting transfers between devices: 29.1 us -> 25.8 us
  waiting for transfers between devices: 29.3 us -> 32.5 us
    ppermute x1, waiting for transfers between devices: 0.01 us -> 3.28 us  [per_device(): ahead_own = ahead(own_kv)]
    ppermute x1, waiting for transfers between devices: 1.9 us -> 0.01 us  [per_device(): back_own = back(own_kv)]
    ppermute x1, starting transfers between devices: 2.71 us -> 1.46 us  [per_device(): other_q = swap(swap_q)]
    ppermute x1, starting transfers between devices: 3.93 us -> 2.81 us  [per_device(): back_far = back(back_other)]
    ppermute x7, starting transfers between devices: 7.9 us -> 6.8 us  [per_device(): lax.ppermute(outgoing[d], 'blk', [(i, (i + d) % nblocks) for i in range(n...]
    ppermute x7, waiting for transfers between devices: 22.2 us -> 23.2 us  [per_device(): lax.ppermute(outgoing[d], 'blk', [(i, (i + d) % nblocks) for i in range(n...]
where the time goes in v12:
time: 77.1 us; the launch traced here: 76.7 us
  waiting for transfers between devices  32.5 us (42%)
  starting transfers between devices  25.8 us (33%)
  Pallas kernels  16.7 us (22%)
  local copies, waits for them, and re-layouts  1.4 us (2%)
    ppermute x7, waiting for transfers between devices, per_device(): lax.ppermute(outgoing[d], 'blk', [(i, (i + d) % nblocks) for i in range(n...  23.2 us
    pallas_call x4, Pallas kernels, attention(): pl.pallas_call(functools.partial(attention_kernel, kinds, numbers, follow...  11 us
    ppermute x7, starting transfers between devices, per_device(): lax.ppermute(outgoing[d], 'blk', [(i, (i + d) % nblocks) for i in range(n...  6.8 us
    ppermute x1, starting transfers between devices, per_device(): ahead_own = ahead(own_kv)  3.48 us
    ppermute x1, waiting for transfers between devices, per_device(): ahead_own = ahead(own_kv)  3.28 us
    ppermute x1, starting transfers between devices, per_device(): ahead_other = ahead(ready)  3.05 us
    ppermute x1, starting transfers between devices, per_device(): back_far = back(back_other)  2.81 us
    ppermute x1, waiting for transfers between devices, per_device(): ahead_far = ahead(ahead_own)  2.77 us
  transfers between devices with their start and end apart: 16, of which 10 were waited for; matrix products, arithmetic and copies ran while one was open for 0% of the time, Pallas kernels for 15%

profile of v12, /device:TPU:14, one launch (start us, length us, event | category | flops | bytes accessed | tf_op | source)
XLA Modules:
  0.0 76.7 jit_solution(1505622270590848434)
XLA Ops:
  0.0 2.1 %shard_map.91 = (bf16[320,256]{1,0:T(8,128)(2,1)S(1)}, bf16[640,256]{1,0:T(8,128)(2,1)S(1)}, bf16[320,256]{1,0:T(8,128)(2,1)S(1)}, bf16[640,256]{1,0:T(8,128)(2,1)}) custom-call(s32[1]{0:T(128)} %bitcast.where_ref, bf16[256,640]{1,0:T(8,128)(2,1)} %q_hbm.1, bf16[256,640]{1,0:T(8,128)(2,1)} %k_hbm.1, bf16[256,640]{1,0:T(8,128)(2,1)} %v_hbm.1), custom_call_target="tpu_custom_call" | custom-call | tf_op jit(solution)/shard_map/pallas_call | solution.py:74
  2.1 3.5 %collective-permute-start.1 = (bf16[640,256]{1,0:T(8,128)(2,1)S(1)}, bf16[640,256]{1,0:T(8,128)(2,1)S(1)}, u32[]{:S(2)}, u32[]{:S(2)}) collective-permute-start(bf16[640,256]{1,0:T(8,128)(2,1)S(1)} %get-tuple-element.27.refs_1_), channel_id=1, source_target_pairs={{4,12},{8,0},{12,20},{16,8},{20,28},{24,16},{5,13},{9,1},{13,21},{... | collective-permute-start | bytes 983048 | tf_op jit(solution)/shard_map/ppermute | solution.py:382
  5.7 2.4 %collective-permute-start.2 = (bf16[640,256]{1,0:T(8,128)(2,1)S(1)}, bf16[640,256]{1,0:T(8,128)(2,1)S(1)}, u32[]{:S(2)}, u32[]{:S(2)}) collective-permute-start(bf16[640,256]{1,0:T(8,128)(2,1)S(1)} %get-tuple-element.27.refs_1_), channel_id=1, source_target_pairs={{0,8},{8,16},{12,4},{16,24},{20,12},{28,20},{1,9},{9,17},{13,5},{1... | collective-permute-start | bytes 983048 | tf_op jit(solution)/shard_map/ppermute | solution.py:383
  10.2 3.3 %collective-permute-done.1.refs_3_ = bf16[640,256]{1,0:T(8,128)(2,1)S(1)} collective-permute-done((bf16[640,256]{1,0:T(8,128)(2,1)S(1)}, bf16[640,256]{1,0:T(8,128)(2,1)S(1)}, u32[]{:S(2)}, u32[]{:S(2)}) %collective-permute-start.1) | collective-permute-done | bytes 327712 | tf_op jit(solution)/shard_map/ppermute | solution.py:382
  13.4 1.6 %collective-permute-done.refs_2_ = bf16[640,256]{1,0:T(8,128)(2,1)S(1)} collective-permute-done((bf16[640,256]{1,0:T(8,128)(2,1)}, bf16[640,256]{1,0:T(8,128)(2,1)S(1)}, u32[]{:S(2)}, u32[]{:S(2)}) %collective-permute-start) | collective-permute-done | bytes 327712 | tf_op jit(solution)/shard_map/ppermute | solution.py:381
  15.0 2.4 %collective-permute-start.4 = (bf16[640,256]{1,0:T(8,128)(2,1)S(1)}, bf16[640,256]{1,0:T(8,128)(2,1)S(1)}, u32[]{:S(2)}, u32[]{:S(2)}) collective-permute-start(bf16[640,256]{1,0:T(8,128)(2,1)S(1)} %collective-permute-done.refs_2_), channel_id=1, source_target_pairs={{0,8},{8,16},{12,4},{16,24},{20,12},{28,20},{1,9},{9,17},{13,5},{1... | collective-permute-start | bytes 983048 | tf_op jit(solution)/shard_map/ppermute | solution.py:386
  18.9 3.0 %collective-permute-start.3 = (bf16[640,256]{1,0:T(8,128)(2,1)S(1)}, bf16[640,256]{1,0:T(8,128)(2,1)S(1)}, u32[]{:S(2)}, u32[]{:S(2)}) collective-permute-start(bf16[640,256]{1,0:T(8,128)(2,1)S(1)} %collective-permute-done.refs_2_), channel_id=1, source_target_pairs={{4,12},{8,0},{12,20},{16,8},{20,28},{24,16},{5,13},{9,1},{13,21},{... | collective-permute-start | bytes 983048 | tf_op jit(solution)/shard_map/ppermute | solution.py:389
  21.9 2.5 %collective-permute-start.7 = (bf16[640,256]{1,0:T(8,128)(2,1)S(1)}, bf16[640,256]{1,0:T(8,128)(2,1)S(1)}, u32[]{:S(2)}, u32[]{:S(2)}) collective-permute-start(bf16[640,256]{1,0:T(8,128)(2,1)S(1)} %collective-permute-done.1.refs_3_), channel_id=1, source_target_pairs={{4,12},{8,0},{12,20},{16,8},{20,28},{24,16},{5,13},{9,1},{13,21},{... | collective-permute-start | bytes 983048 | tf_op jit(solution)/shard_map/ppermute | solution.py:385
  24.5 3.1 %shard_map.93.refs_4_ = f32[1,4,256,128]{3,2,1,0:T(8,128)S(1)} custom-call(s32[1]{0:T(128)} %bitcast.where_ref, s32[8,128]{1,0:T(8,128)S(1)} %get-tuple-element.30.need_ref, f32[1,2048]{1,0:T(1,128)S(1)} %get-tuple-element.31.seg_ref, bf16[320,256]{1,0:T(8,128)(2,1)S(1)} %get-tuple-element.32.refs_0_, bf16[640,256]{1,0:T(8,128)(2,1)S(1)} %get-tuple-element.27.refs_1_, ...), custom_call_target="tpu_custom_call" | custom-call | flops 2000000000 | bytes 2000000 | tf_op jit(solution)/shard_map/pallas_call | solution.py:234
  27.6 2.8 %collective-permute-start.5 = (bf16[640,256]{1,0:T(8,128)(2,1)S(1)}, bf16[640,256]{1,0:T(8,128)(2,1)S(1)}, u32[]{:S(2)}, u32[]{:S(2)}) collective-permute-start(bf16[640,256]{1,0:T(8,128)(2,1)S(1)} %collective-permute-done.4.refs_2_), channel_id=1, source_target_pairs={{0,8},{8,16},{12,4},{16,24},{20,12},{28,20},{1,9},{9,17},{13,5},{1... | collective-permute-start | bytes 983048 | tf_op jit(solution)/shard_map/ppermute | solution.py:390
  30.4 2.6 %shard_map.95.refs_4_ = f32[1,4,256,128]{3,2,1,0:T(8,128)S(1)} custom-call(s32[1]{0:T(128)} %bitcast.where_ref, s32[8,128]{1,0:T(8,128)S(1)} %get-tuple-element.30.need_ref, f32[1,2048]{1,0:T(1,128)S(1)} %get-tuple-element.31.seg_ref, bf16[320,256]{1,0:T(8,128)(2,1)S(1)} %collective-permute-done.6.refs_0_, bf16[640,256]{1,0:T(8,128)(2,1)S(1)} %get-tuple-element.27.refs_1_, ...), custom_call_target="tpu_custom_call" | custom-call | flops 2000000000 | bytes 2000000 | tf_op jit(solution)/shard_map/pallas_call | solution.py:234
  33.0 2.8 %collective-permute-done.7.refs_3_ = bf16[640,256]{1,0:T(8,128)(2,1)S(1)} collective-permute-done((bf16[640,256]{1,0:T(8,128)(2,1)S(1)}, bf16[640,256]{1,0:T(8,128)(2,1)S(1)}, u32[]{:S(2)}, u32[]{:S(2)}) %collective-permute-start.7) | collective-permute-done | bytes 327712 | tf_op jit(solution)/shard_map/ppermute | solution.py:385
  35.8 2.4 %shard_map.96 = bf16[320,256]{1,0:T(8,128)(2,1)S(1)} custom-call(s32[1]{0:T(128)} %bitcast.where_ref, s32[8,128]{1,0:T(8,128)S(1)} %get-tuple-element.30.need_ref, f32[1,2048]{1,0:T(1,128)S(1)} %get-tuple-element.31.seg_ref, bf16[320,256]{1,0:T(8,128)(2,1)S(1)} %collective-permute-done.6.refs_0_, bf16[640,256]{1,0:T(8,128)(2,1)S(1)} %collective-permute-done.3.refs_1_, ...), custom_call_target="tpu_custom_call" | custom-call | flops 2000000000 | bytes 2000000 | tf_op jit(solution)/shard_map/pallas_call | solution.py:234
  39.0 2.9 %shard_map.94.own_ref = bf16[320,256]{1,0:T(8,128)(2,1)S(1)} custom-call(s32[1]{0:T(128)} %bitcast.where_ref, s32[8,128]{1,0:T(8,128)S(1)} %get-tuple-element.30.need_ref, f32[1,2048]{1,0:T(1,128)S(1)} %get-tuple-element.31.seg_ref, bf16[320,256]{1,0:T(8,128)(2,1)S(1)} %get-tuple-element.32.refs_0_, bf16[640,256]{1,0:T(8,128)(2,1)S(1)} %collective-permute-done.3.refs_1_, ...), custom_call_target="tpu_custom_call" | custom-call | flops 2000000000 | bytes 2000000 | tf_op jit(solution)/shard_map/pallas_call | solution.py:234
  42.0 1.6 %collective-permute-done.8.other_ref = bf16[320,256]{1,0:T(8,128)(2,1)S(1)} collective-permute-done((bf16[320,256]{1,0:T(8,128)(2,1)S(1)}, bf16[320,256]{1,0:T(8,128)(2,1)S(1)}, u32[]{:S(2)}, u32[]{:S(2)}) %collective-permute-start.8) | collective-permute-done | bytes 163872 | tf_op jit(solution)/shard_map/ppermute | solution.py:398
  43.6 1.5 %shard_map.97 = (bf16[16,5248]{1,0:T(8,128)(2,1)S(1)}, bf16[16,5248]{1,0:T(8,128)(2,1)S(1)}, bf16[16,5248]{1,0:T(8,128)(2,1)S(1)}, bf16[16,5248]{1,0:T(8,128)(2,...) custom-call(s32[1]{0:T(128)} %bitcast.where_ref, ...), custom_call_target="tpu_custom_call" | custom-call | tf_op jit(solution)/shard_map/pallas_call | solution.py:305
  45.2 2.6 %collective-permute-start.11 = (bf16[16,5248]{1,0:T(8,128)(2,1)S(1)}, bf16[16,5248]{1,0:T(8,128)(2,1)S(1)}, u32[]{:S(2)}, u32[]{:S(2)}) collective-permute-start(bf16[16,5248]{1,0:T(8,128)(2,1)S(1)} %get-tuple-element.42), channel_id=1, source_target_pairs={{0,12},{4,16},{8,20},{12,24},{16,28},{20,0},{24,4},{28,8},{1,13},{... | collective-permute-start | bytes 503816 | tf_op jit(solution)/shard_map/ppermute | solution.py:411
  47.7 1.7 %collective-permute-start.12 = (bf16[16,5248]{1,0:T(8,128)(2,1)S(1)}, bf16[16,5248]{1,0:T(8,128)(2,1)S(1)}, u32[]{:S(2)}, u32[]{:S(2)}) collective-permute-start(bf16[16,5248]{1,0:T(8,128)(2,1)S(1)} %get-tuple-element.43), channel_id=1, source_target_pairs={{0,16},{4,20},{8,24},{12,28},{16,0},{20,4},{24,8},{28,12},{1,17},{... | collective-permute-start | bytes 503816 | tf_op jit(solution)/shard_map/ppermute | solution.py:411
  50.0 1.9 %collective-permute-start.14 = (bf16[16,5248]{1,0:T(8,128)(2,1)S(1)}, bf16[16,5248]{1,0:T(8,128)(2,1)S(1)}, u32[]{:S(2)}, u32[]{:S(2)}) collective-permute-start(bf16[16,5248]{1,0:T(8,128)(2,1)S(1)} %get-tuple-element.45), channel_id=1, source_target_pairs={{0,24},{4,28},{8,0},{12,4},{16,8},{20,12},{24,16},{28,20},{1,25},{... | collective-permute-start | bytes 503816 | tf_op jit(solution)/shard_map/ppermute | solution.py:411
  51.9 7.9 %collective-permute-done.10.refs_2_ = bf16[16,5248]{1,0:T(8,128)(2,1)S(1)} collective-permute-done((bf16[16,5248]{1,0:T(8,128)(2,1)S(1)}, bf16[16,5248]{1,0:T(8,128)(2,1)S(1)}, u32[]{:S(2)}, u32[]{:S(2)}) %collective-permute-start.10) | collective-permute-done | bytes 167968 | tf_op jit(solution)/shard_map/ppermute | solution.py:411
  59.8 6.8 %collective-permute-done.11.refs_3_ = bf16[16,5248]{1,0:T(8,128)(2,1)S(1)} collective-permute-done((bf16[16,5248]{1,0:T(8,128)(2,1)S(1)}, bf16[16,5248]{1,0:T(8,128)(2,1)S(1)}, u32[]{:S(2)}, u32[]{:S(2)}) %collective-permute-start.11) | collective-permute-done | bytes 167968 | tf_op jit(solution)/shard_map/ppermute | solution.py:411
  66.6 2.6 %collective-permute-done.12.refs_4_ = bf16[16,5248]{1,0:T(8,128)(2,1)S(1)} collective-permute-done((bf16[16,5248]{1,0:T(8,128)(2,1)S(1)}, bf16[16,5248]{1,0:T(8,128)(2,1)S(1)}, u32[]{:S(2)}, u32[]{:S(2)}) %collective-permute-start.12) | collective-permute-done | bytes 167968 | tf_op jit(solution)/shard_map/ppermute | solution.py:411
  69.2 3.6 %collective-permute-done.14.refs_6_ = bf16[16,5248]{1,0:T(8,128)(2,1)S(1)} collective-permute-done((bf16[16,5248]{1,0:T(8,128)(2,1)S(1)}, bf16[16,5248]{1,0:T(8,128)(2,1)S(1)}, u32[]{:S(2)}, u32[]{:S(2)}) %collective-permute-start.14) | collective-permute-done | bytes 167968 | tf_op jit(solution)/shard_map/ppermute | solution.py:411
  73.6 1.5 %collective-permute-done.9.refs_1_ = bf16[16,5248]{1,0:T(8,128)(2,1)S(1)} collective-permute-done((bf16[16,5248]{1,0:T(8,128)(2,1)S(1)}, bf16[16,5248]{1,0:T(8,128)(2,1)S(1)}, u32[]{:S(2)}, u32[]{:S(2)}) %collective-permute-start.9) | collective-permute-done | bytes 167968 | tf_op jit(solution)/shard_map/ppermute | solution.py:411
  (28 shorter events, 7.4 us)
Async XLA Ops:
  2.1 11.3 %collective-permute-start.1 = (bf16[640,256]{1,0:T(8,128)(2,1)S(1)}, bf16[640,256]{1,0:T(8,128)(2,1)S(1)}, u32[]{:S(2)}, u32[]{:S(2)}) collective-permute-start(bf16[640,256]{1,0:T(8,128)(2,1)S(1)} %get-tuple-element.27.refs_1_), channel_id=1, source_target_pairs={{4,12},{8,0},{12,20},{16,8},{20,28},{24,16},{5,13},{9,1},{13,21},{... | collective-permute-start | bytes 983048 | tf_op jit(solution)/shard_map/ppermute | solution.py:382
  5.6 9.4 %collective-permute-start = (bf16[640,256]{1,0:T(8,128)(2,1)}, bf16[640,256]{1,0:T(8,128)(2,1)S(1)}, u32[]{:S(2)}, u32[]{:S(2)}) collective-permute-start(bf16[640,256]{1,0:T(8,128)(2,1)} %get-tuple-element.26), channel_id=1, source_target_pairs={{0,4},{4,0},{8,12},{12,8},{16,20},{20,16},{24,28},{28,24},{1,5},{5... | collective-permute-start | bytes 983048 | tf_op jit(solution)/shard_map/ppermute | solution.py:381
  5.7 11.7 %collective-permute-start.2 = (bf16[640,256]{1,0:T(8,128)(2,1)S(1)}, bf16[640,256]{1,0:T(8,128)(2,1)S(1)}, u32[]{:S(2)}, u32[]{:S(2)}) collective-permute-start(bf16[640,256]{1,0:T(8,128)(2,1)S(1)} %get-tuple-element.27.refs_1_), channel_id=1, source_target_pairs={{0,8},{8,16},{12,4},{16,24},{20,12},{28,20},{1,9},{9,17},{13,5},{1... | collective-permute-start | bytes 983048 | tf_op jit(solution)/shard_map/ppermute | solution.py:383
  8.0 0.7 copy-start.2
  8.7 0.7 copy-start.3
  15.0 12.6 %collective-permute-start.4 = (bf16[640,256]{1,0:T(8,128)(2,1)S(1)}, bf16[640,256]{1,0:T(8,128)(2,1)S(1)}, u32[]{:S(2)}, u32[]{:S(2)}) collective-permute-start(bf16[640,256]{1,0:T(8,128)(2,1)S(1)} %collective-permute-done.refs_2_), channel_id=1, source_target_pairs={{0,8},{8,16},{12,4},{16,24},{20,12},{28,20},{1,9},{9,17},{13,5},{1... | collective-permute-start | bytes 983048 | tf_op jit(solution)/shard_map/ppermute | solution.py:386
  17.4 13.0 %collective-permute-start.6 = (bf16[320,256]{1,0:T(8,128)(2,1)S(1)}, bf16[320,256]{1,0:T(8,128)(2,1)S(1)}, u32[]{:S(2)}, u32[]{:S(2)}) collective-permute-start(bf16[320,256]{1,0:T(8,128)(2,1)S(1)} %get-tuple-element.38), channel_id=1, source_target_pairs={{0,4},{4,0},{8,12},{12,8},{16,20},{20,16},{24,28},{28,24},{1,5},{5... | collective-permute-start | bytes 491528 | tf_op jit(solution)/shard_map/ppermute | solution.py:388
  18.9 14.1 %collective-permute-start.3 = (bf16[640,256]{1,0:T(8,128)(2,1)S(1)}, bf16[640,256]{1,0:T(8,128)(2,1)S(1)}, u32[]{:S(2)}, u32[]{:S(2)}) collective-permute-start(bf16[640,256]{1,0:T(8,128)(2,1)S(1)} %collective-permute-done.refs_2_), channel_id=1, source_target_pairs={{4,12},{8,0},{12,20},{16,8},{20,28},{24,16},{5,13},{9,1},{13,21},{... | collective-permute-start | bytes 983048 | tf_op jit(solution)/shard_map/ppermute | solution.py:389
  21.9 13.9 %collective-permute-start.7 = (bf16[640,256]{1,0:T(8,128)(2,1)S(1)}, bf16[640,256]{1,0:T(8,128)(2,1)S(1)}, u32[]{:S(2)}, u32[]{:S(2)}) collective-permute-start(bf16[640,256]{1,0:T(8,128)(2,1)S(1)} %collective-permute-done.1.refs_3_), channel_id=1, source_target_pairs={{4,12},{8,0},{12,20},{16,8},{20,28},{24,16},{5,13},{9,1},{13,21},{... | collective-permute-start | bytes 983048 | tf_op jit(solution)/shard_map/ppermute | solution.py:385
  27.6 11.4 %collective-permute-start.5 = (bf16[640,256]{1,0:T(8,128)(2,1)S(1)}, bf16[640,256]{1,0:T(8,128)(2,1)S(1)}, u32[]{:S(2)}, u32[]{:S(2)}) collective-permute-start(bf16[640,256]{1,0:T(8,128)(2,1)S(1)} %collective-permute-done.4.refs_2_), channel_id=1, source_target_pairs={{0,8},{8,16},{12,4},{16,24},{20,12},{28,20},{1,9},{9,17},{13,5},{1... | collective-permute-start | bytes 983048 | tf_op jit(solution)/shard_map/ppermute | solution.py:390
  38.2 5.4 %copy-start = (bf16[640,1280]{1,0:T(8,128)(2,1)S(1)}, bf16[640,1280]{1,0:T(8,128)(2,1)}, u32[]{:S(2)}) copy-start(bf16[640,1280]{1,0:T(8,128)(2,1)} %weight_ref.1) | copy-start | bytes 4915204
  38.2 5.4 %copy-start.1 = (bf16[256,1280]{1,0:T(8,128)(2,1)S(1)}, bf16[256,1280]{1,0:T(8,128)(2,1)}, u32[]{:S(2)}) copy-start(bf16[256,1280]{1,0:T(8,128)(2,1)} %tokens_ref.1) | copy-start | bytes 1966084
  38.2 5.4 %copy-start.4 = (s32[64]{0:T(128)S(1)}, s32[64]{0:T(128)}, u32[]{:S(2)}) copy-start(s32[64]{0:T(128)} %param.16) | copy-start | bytes 772
  38.2 5.4 %copy-start.5 = (s32[64]{0:T(128)S(1)}, s32[64]{0:T(128)}, u32[]{:S(2)}) copy-start(s32[64]{0:T(128)} %param.17) | copy-start | bytes 772
  38.2 5.4 %collective-permute-start.8 = (bf16[320,256]{1,0:T(8,128)(2,1)S(1)}, bf16[320,256]{1,0:T(8,128)(2,1)S(1)}, u32[]{:S(2)}, u32[]{:S(2)}) collective-permute-start(bf16[320,256]{1,0:T(8,128)(2,1)S(1)} %shard_map.96), channel_id=1, source_target_pairs={{0,4},{4,0},{8,12},{12,8},{16,20},{20,16},{24,28},{28,24},{1,5},{5... | collective-permute-start | bytes 491528 | tf_op jit(solution)/shard_map/ppermute | solution.py:398
  45.1 14.7 %collective-permute-start.10 = (bf16[16,5248]{1,0:T(8,128)(2,1)S(1)}, bf16[16,5248]{1,0:T(8,128)(2,1)S(1)}, u32[]{:S(2)}, u32[]{:S(2)}) collective-permute-start(bf16[16,5248]{1,0:T(8,128)(2,1)S(1)} %get-tuple-element.41), channel_id=1, source_target_pairs={{0,8},{4,12},{8,16},{12,20},{16,24},{20,28},{24,0},{28,4},{1,9},{5... | collective-permute-start | bytes 503816 | tf_op jit(solution)/shard_map/ppermute | solution.py:411
  45.2 21.4 %collective-permute-start.11 = (bf16[16,5248]{1,0:T(8,128)(2,1)S(1)}, bf16[16,5248]{1,0:T(8,128)(2,1)S(1)}, u32[]{:S(2)}, u32[]{:S(2)}) collective-permute-start(bf16[16,5248]{1,0:T(8,128)(2,1)S(1)} %get-tuple-element.42), channel_id=1, source_target_pairs={{0,12},{4,16},{8,20},{12,24},{16,28},{20,0},{24,4},{28,8},{1,13},{... | collective-permute-start | bytes 503816 | tf_op jit(solution)/shard_map/ppermute | solution.py:411
  47.7 21.5 %collective-permute-start.12 = (bf16[16,5248]{1,0:T(8,128)(2,1)S(1)}, bf16[16,5248]{1,0:T(8,128)(2,1)S(1)}, u32[]{:S(2)}, u32[]{:S(2)}) collective-permute-start(bf16[16,5248]{1,0:T(8,128)(2,1)S(1)} %get-tuple-element.43), channel_id=1, source_target_pairs={{0,16},{4,20},{8,24},{12,28},{16,0},{20,4},{24,8},{28,12},{1,17},{... | collective-permute-start | bytes 503816 | tf_op jit(solution)/shard_map/ppermute | solution.py:411
  49.4 19.8 %collective-permute-start.13 = (bf16[16,5248]{1,0:T(8,128)(2,1)S(1)}, bf16[16,5248]{1,0:T(8,128)(2,1)S(1)}, u32[]{:S(2)}, u32[]{:S(2)}) collective-permute-start(bf16[16,5248]{1,0:T(8,128)(2,1)S(1)} %get-tuple-element.44), channel_id=1, source_target_pairs={{0,20},{4,24},{8,28},{12,0},{16,4},{20,8},{24,12},{28,16},{1,21},{... | collective-permute-start | bytes 503816 | tf_op jit(solution)/shard_map/ppermute | solution.py:411
  50.0 22.9 %collective-permute-start.14 = (bf16[16,5248]{1,0:T(8,128)(2,1)S(1)}, bf16[16,5248]{1,0:T(8,128)(2,1)S(1)}, u32[]{:S(2)}, u32[]{:S(2)}) collective-permute-start(bf16[16,5248]{1,0:T(8,128)(2,1)S(1)} %get-tuple-element.45), channel_id=1, source_target_pairs={{0,24},{4,28},{8,0},{12,4},{16,8},{20,12},{24,16},{28,20},{1,25},{... | collective-permute-start | bytes 503816 | tf_op jit(solution)/shard_map/ppermute | solution.py:411
  59.8 13.9 %collective-permute-start.15 = (bf16[16,5248]{1,0:T(8,128)(2,1)S(1)}, bf16[16,5248]{1,0:T(8,128)(2,1)S(1)}, u32[]{:S(2)}, u32[]{:S(2)}) collective-permute-start(bf16[16,5248]{1,0:T(8,128)(2,1)S(1)} %get-tuple-element.46), channel_id=1, source_target_pairs={{0,28},{4,0},{8,4},{12,8},{16,12},{20,16},{24,20},{28,24},{1,29},{... | collective-permute-start | bytes 503816 | tf_op jit(solution)/shard_map/ppermute | solution.py:411
  66.6 8.5 %collective-permute-start.9 = (bf16[16,5248]{1,0:T(8,128)(2,1)S(1)}, bf16[16,5248]{1,0:T(8,128)(2,1)S(1)}, u32[]{:S(2)}, u32[]{:S(2)}) collective-permute-start(bf16[16,5248]{1,0:T(8,128)(2,1)S(1)} %get-tuple-element.40), channel_id=1, source_target_pairs={{0,4},{4,8},{8,12},{12,16},{16,20},{20,24},{24,28},{28,0},{1,5},{5... | collective-permute-start | bytes 503816 | tf_op jit(solution)/shard_map/ppermute | solution.py:411

commit v13 on v11

--- a/solution.py
+++ b/solution.py
@@ -160,7 +160,7 @@
         def finish(h, peak, accum, n=n):
             if ends:
                 turned = accum.T
-                lines = pl.ds(pl.multiple_of(h * hdim, 16), hdim)
+                lines = slice(h * hdim, (h + 1) * hdim)
                 out_ref[lines, :] = (turned[:hdim] / turned[hdim : hdim + 1]).astype(out_ref.dtype)
             else:
                 peak = jnp.broadcast_to(peak, (rows, 128 - wide))
@@ -170,12 +170,9 @@
 
             @pl.when(size == 0)
             def _():
-                def one_head(h, carry):
+                for h in range(HALF):
                     state = before[0, h]
                     finish(h, state[:, wide : wide + 1], state[:, :wide])
-                    return carry
-
-                lax.fori_loop(0, HALF, one_head, 0)
 
         for fixed in range(1, len(numbers) + 1):
 
@@ -188,7 +185,7 @@
                 ]
 
                 def one_head(h):
-                    lines = pl.ds(pl.multiple_of(h * hdim, 16), hdim)
+                    lines = slice(h * hdim, (h + 1) * hdim)
                     query = query_s[h]
                     scores = []
                     for b, key_seg in zip(picked, key_segs):
@@ -214,12 +211,8 @@
                         )
                     finish(h, peak, accum)
 
-                def two_heads(i, carry):
-                    one_head(2 * i)
-                    one_head(2 * i + 1)
-                    return carry
-
-                lax.fori_loop(0, HALF // 2, two_heads, 0)
+                for h in range(HALF):
+                    one_head(h)
 
 
 def attention(where, need, segs, queries, kinds, blocks, numbers, before, ends):

time: 77 us -> 76.9 us (level)
  waiting for transfers between devices: 29.3 us -> 32.1 us
  Pallas kernels: 16.2 us -> 14.5 us
  starting transfers between devices: 29.1 us -> 27.9 us
    pallas_call x4, Pallas kernels: 10.5 us -> 8.75 us  [attention(): pl.pallas_call(functools.partial(attention_kernel, kinds, numbers, follow...]
    ppermute x1, waiting for transfers between devices: 2.02 us -> 3.22 us  [per_device(): ahead_far = ahead(ahead_own)]
    ppermute x1, waiting for transfers between devices: 2.05 us -> 3.17 us  [per_device(): other = swap(other)]
  transfers between devices with their start and end apart: 16 -> 16, of which waited for: 10 -> 10; matrix products, arithmetic and copies ran while one was open for 0% -> 0% of each run, Pallas kernels for 15% -> 12%
where the time goes in v13:
time: 76.9 us; the launch traced here: 76.3 us
  waiting for transfers between devices  32.1 us (42%)
  starting transfers between devices  27.9 us (36%)
  Pallas kernels  14.5 us (19%)
  local copies, waits for them, and re-layouts  1.4 us (2%)
    ppermute x7, waiting for transfers between devices, per_device(): lax.ppermute(outgoing[d], 'blk', [(i, (i + d) % nblocks) for i in range(n...  22.6 us
    pallas_call x4, Pallas kernels, attention(): pl.pallas_call(functools.partial(attention_kernel, kinds, numbers, follow...  8.75 us
    ppermute x7, starting transfers between devices, per_device(): lax.ppermute(outgoing[d], 'blk', [(i, (i + d) % nblocks) for i in range(n...  7.36 us
    ppermute x1, starting transfers between devices, per_device(): back_far = back(back_other)  3.5 us
    ppermute x1, starting transfers between devices, per_device(): ahead_own = ahead(own_kv)  3.48 us
    ppermute x1, starting transfers between devices, per_device(): ahead_other = ahead(other_kv)  3.47 us
    ppermute x1, waiting for transfers between devices, per_device(): ahead_far = ahead(ahead_own)  3.22 us
    ppermute x1, waiting for transfers between devices, per_device(): other = swap(other)  3.17 us
  transfers between devices with their start and end apart: 16, of which 10 were waited for; matrix products, arithmetic and copies ran while one was open for 0% of the time, Pallas kernels for 12%

profile of v13, /device:TPU:14, one launch (start us, length us, event | category | flops | bytes accessed | tf_op | source)
XLA Modules:
  0.0 76.3 jit_solution(14709396920180899548)
XLA Ops:
  0.0 2.1 %shard_map.91 = (bf16[320,256]{1,0:T(8,128)(2,1)S(1)}, bf16[640,256]{1,0:T(8,128)(2,1)S(1)}, bf16[320,256]{1,0:T(8,128)(2,1)S(1)}, bf16[640,256]{1,0:T(8,128)(2,1)}) custom-call(s32[1]{0:T(128)} %bitcast.where_ref, bf16[256,640]{1,0:T(8,128)(2,1)} %q_hbm.1, bf16[256,640]{1,0:T(8,128)(2,1)} %k_hbm.1, bf16[256,640]{1,0:T(8,128)(2,1)} %v_hbm.1), custom_call_target="tpu_custom_call" | custom-call | tf_op jit(solution)/shard_map/pallas_call | solution.py:74
  2.7 2.3 %collective-permute-start.1 = (bf16[640,256]{1,0:T(8,128)(2,1)S(1)}, bf16[640,256]{1,0:T(8,128)(2,1)S(1)}, u32[]{:S(2)}, u32[]{:S(2)}) collective-permute-start(bf16[640,256]{1,0:T(8,128)(2,1)S(1)} %get-tuple-element.25.refs_1_), channel_id=1, source_target_pairs={{0,8},{8,16},{12,4},{16,24},{20,12},{28,20},{1,9},{9,17},{13,5},{1... | collective-permute-start | bytes 983048 | tf_op jit(solution)/shard_map/ppermute | solution.py:376
  5.0 3.5 %collective-permute-start.5 = (bf16[640,256]{1,0:T(8,128)(2,1)S(1)}, bf16[640,256]{1,0:T(8,128)(2,1)S(1)}, u32[]{:S(2)}, u32[]{:S(2)}) collective-permute-start(bf16[640,256]{1,0:T(8,128)(2,1)S(1)} %get-tuple-element.25.refs_1_), channel_id=1, source_target_pairs={{4,12},{8,0},{12,20},{16,8},{20,28},{24,16},{5,13},{9,1},{13,21},{... | collective-permute-start | bytes 983048 | tf_op jit(solution)/shard_map/ppermute | solution.py:375
  11.8 1.9 %collective-permute-done.1.refs_4_ = bf16[640,256]{1,0:T(8,128)(2,1)S(1)} collective-permute-done((bf16[640,256]{1,0:T(8,128)(2,1)S(1)}, bf16[640,256]{1,0:T(8,128)(2,1)S(1)}, u32[]{:S(2)}, u32[]{:S(2)}) %collective-permute-start.1) | collective-permute-done | bytes 327712 | tf_op jit(solution)/shard_map/ppermute | solution.py:376
  13.7 2.3 %collective-permute-start.3 = (bf16[640,256]{1,0:T(8,128)(2,1)S(1)}, bf16[640,256]{1,0:T(8,128)(2,1)S(1)}, u32[]{:S(2)}, u32[]{:S(2)}) collective-permute-start(bf16[640,256]{1,0:T(8,128)(2,1)S(1)} %collective-permute-done.refs_2_), channel_id=1, source_target_pairs={{0,8},{8,16},{12,4},{16,24},{20,12},{28,20},{1,9},{9,17},{13,5},{1... | collective-permute-start | bytes 983048 | tf_op jit(solution)/shard_map/ppermute | solution.py:380
  16.1 2.7 %collective-permute-start.6 = (bf16[320,256]{1,0:T(8,128)(2,1)S(1)}, bf16[320,256]{1,0:T(8,128)(2,1)S(1)}, u32[]{:S(2)}, u32[]{:S(2)}) collective-permute-start(bf16[320,256]{1,0:T(8,128)(2,1)S(1)} %get-tuple-element.34), channel_id=1, source_target_pairs={{0,4},{4,0},{8,12},{12,8},{16,20},{20,16},{24,28},{28,24},{1,5},{5... | collective-permute-start | bytes 491528 | tf_op jit(solution)/shard_map/ppermute | solution.py:381
  18.8 3.5 %collective-permute-start.2 = (bf16[640,256]{1,0:T(8,128)(2,1)S(1)}, bf16[640,256]{1,0:T(8,128)(2,1)S(1)}, u32[]{:S(2)}, u32[]{:S(2)}) collective-permute-start(bf16[640,256]{1,0:T(8,128)(2,1)S(1)} %collective-permute-done.refs_2_), channel_id=1, source_target_pairs={{4,12},{8,0},{12,20},{16,8},{20,28},{24,16},{5,13},{9,1},{13,21},{... | collective-permute-start | bytes 983048 | tf_op jit(solution)/shard_map/ppermute | solution.py:383
  22.3 1.9 %collective-permute-start.7 = (bf16[640,256]{1,0:T(8,128)(2,1)S(1)}, bf16[640,256]{1,0:T(8,128)(2,1)S(1)}, u32[]{:S(2)}, u32[]{:S(2)}) collective-permute-start(bf16[640,256]{1,0:T(8,128)(2,1)S(1)} %collective-permute-done.5.refs_3_), channel_id=1, source_target_pairs={{4,12},{8,0},{12,20},{16,8},{20,28},{24,16},{5,13},{9,1},{13,21},{... | collective-permute-start | bytes 983048 | tf_op jit(solution)/shard_map/ppermute | solution.py:384
  24.2 2.4 %shard_map.93.refs_4_ = f32[1,4,256,128]{3,2,1,0:T(8,128)S(1)} custom-call(s32[1]{0:T(128)} %bitcast.where_ref, s32[8,128]{1,0:T(8,128)S(1)} %get-tuple-element.29.need_ref, f32[1,2048]{1,0:T(1,128)S(1)} %get-tuple-element.30.seg_ref, bf16[320,256]{1,0:T(8,128)(2,1)S(1)} %get-tuple-element.31.refs_0_, bf16[640,256]{1,0:T(8,128)(2,1)S(1)} %get-tuple-element.25.refs_1_, ...), custom_call_target="tpu_custom_call" | custom-call | flops 2000000000 | bytes 2000000 | tf_op jit(solution)/shard_map/pallas_call | solution.py:227
  26.6 3.5 %collective-permute-start.4 = (bf16[640,256]{1,0:T(8,128)(2,1)S(1)}, bf16[640,256]{1,0:T(8,128)(2,1)S(1)}, u32[]{:S(2)}, u32[]{:S(2)}) collective-permute-start(bf16[640,256]{1,0:T(8,128)(2,1)S(1)} %collective-permute-done.3.refs_2_), channel_id=1, source_target_pairs={{0,8},{8,16},{12,4},{16,24},{20,12},{28,20},{1,9},{9,17},{13,5},{1... | collective-permute-start | bytes 983048 | tf_op jit(solution)/shard_map/ppermute | solution.py:382
  30.2 2.0 %shard_map.95.refs_4_ = f32[1,4,256,128]{3,2,1,0:T(8,128)S(1)} custom-call(s32[1]{0:T(128)} %bitcast.where_ref, s32[8,128]{1,0:T(8,128)S(1)} %get-tuple-element.29.need_ref, f32[1,2048]{1,0:T(1,128)S(1)} %get-tuple-element.30.seg_ref, bf16[320,256]{1,0:T(8,128)(2,1)S(1)} %collective-permute-done.6.refs_0_, bf16[640,256]{1,0:T(8,128)(2,1)S(1)} %get-tuple-element.25.refs_1_, ...), custom_call_target="tpu_custom_call" | custom-call | flops 2000000000 | bytes 2000000 | tf_op jit(solution)/shard_map/pallas_call | solution.py:227
  32.2 3.2 %collective-permute-done.7.refs_3_ = bf16[640,256]{1,0:T(8,128)(2,1)S(1)} collective-permute-done((bf16[640,256]{1,0:T(8,128)(2,1)S(1)}, bf16[640,256]{1,0:T(8,128)(2,1)S(1)}, u32[]{:S(2)}, u32[]{:S(2)}) %collective-permute-start.7) | collective-permute-done | bytes 327712 | tf_op jit(solution)/shard_map/ppermute | solution.py:384
  35.4 2.3 %shard_map.96 = bf16[320,256]{1,0:T(8,128)(2,1)S(1)} custom-call(s32[1]{0:T(128)} %bitcast.where_ref, s32[8,128]{1,0:T(8,128)S(1)} %get-tuple-element.29.need_ref, f32[1,2048]{1,0:T(1,128)S(1)} %get-tuple-element.30.seg_ref, bf16[320,256]{1,0:T(8,128)(2,1)S(1)} %collective-permute-done.6.refs_0_, bf16[640,256]{1,0:T(8,128)(2,1)S(1)} %collective-permute-done.2.refs_1_, ...), custom_call_target="tpu_custom_call" | custom-call | flops 2000000000 | bytes 2000000 | tf_op jit(solution)/shard_map/pallas_call | solution.py:227
  38.0 2.0 %shard_map.94.own_ref = bf16[320,256]{1,0:T(8,128)(2,1)S(1)} custom-call(s32[1]{0:T(128)} %bitcast.where_ref, s32[8,128]{1,0:T(8,128)S(1)} %get-tuple-element.29.need_ref, f32[1,2048]{1,0:T(1,128)S(1)} %get-tuple-element.30.seg_ref, bf16[320,256]{1,0:T(8,128)(2,1)S(1)} %get-tuple-element.31.refs_0_, bf16[640,256]{1,0:T(8,128)(2,1)S(1)} %collective-permute-done.2.refs_1_, ...), custom_call_target="tpu_custom_call" | custom-call | flops 2000000000 | bytes 2000000 | tf_op jit(solution)/shard_map/pallas_call | solution.py:227
  40.0 3.2 %collective-permute-done.8.other_ref = bf16[320,256]{1,0:T(8,128)(2,1)S(1)} collective-permute-done((bf16[320,256]{1,0:T(8,128)(2,1)S(1)}, bf16[320,256]{1,0:T(8,128)(2,1)S(1)}, u32[]{:S(2)}, u32[]{:S(2)}) %collective-permute-start.8) | collective-permute-done | bytes 163872 | tf_op jit(solution)/shard_map/ppermute | solution.py:392
  43.2 1.5 %shard_map.97 = (bf16[16,5248]{1,0:T(8,128)(2,1)S(1)}, bf16[16,5248]{1,0:T(8,128)(2,1)S(1)}, bf16[16,5248]{1,0:T(8,128)(2,1)S(1)}, bf16[16,5248]{1,0:T(8,128)(2,...) custom-call(s32[1]{0:T(128)} %bitcast.where_ref, ...), custom_call_target="tpu_custom_call" | custom-call | tf_op jit(solution)/shard_map/pallas_call | solution.py:298
  44.7 2.6 %collective-permute-start.11 = (bf16[16,5248]{1,0:T(8,128)(2,1)S(1)}, bf16[16,5248]{1,0:T(8,128)(2,1)S(1)}, u32[]{:S(2)}, u32[]{:S(2)}) collective-permute-start(bf16[16,5248]{1,0:T(8,128)(2,1)S(1)} %get-tuple-element.38), channel_id=1, source_target_pairs={{0,12},{4,16},{8,20},{12,24},{16,28},{20,0},{24,4},{28,8},{1,13},{... | collective-permute-start | bytes 503816 | tf_op jit(solution)/shard_map/ppermute | solution.py:405
  47.3 1.7 %collective-permute-start.12 = (bf16[16,5248]{1,0:T(8,128)(2,1)S(1)}, bf16[16,5248]{1,0:T(8,128)(2,1)S(1)}, u32[]{:S(2)}, u32[]{:S(2)}) collective-permute-start(bf16[16,5248]{1,0:T(8,128)(2,1)S(1)} %get-tuple-element.39), channel_id=1, source_target_pairs={{0,16},{4,20},{8,24},{12,28},{16,0},{20,4},{24,8},{28,12},{1,17},{... | collective-permute-start | bytes 503816 | tf_op jit(solution)/shard_map/ppermute | solution.py:405
  49.6 1.9 %collective-permute-start.14 = (bf16[16,5248]{1,0:T(8,128)(2,1)S(1)}, bf16[16,5248]{1,0:T(8,128)(2,1)S(1)}, u32[]{:S(2)}, u32[]{:S(2)}) collective-permute-start(bf16[16,5248]{1,0:T(8,128)(2,1)S(1)} %get-tuple-element.41), channel_id=1, source_target_pairs={{0,24},{4,28},{8,0},{12,4},{16,8},{20,12},{24,16},{28,20},{1,25},{... | collective-permute-start | bytes 503816 | tf_op jit(solution)/shard_map/ppermute | solution.py:405
  51.5 7.2 %collective-permute-done.10.refs_2_ = bf16[16,5248]{1,0:T(8,128)(2,1)S(1)} collective-permute-done((bf16[16,5248]{1,0:T(8,128)(2,1)S(1)}, bf16[16,5248]{1,0:T(8,128)(2,1)S(1)}, u32[]{:S(2)}, u32[]{:S(2)}) %collective-permute-start.10) | collective-permute-done | bytes 167968 | tf_op jit(solution)/shard_map/ppermute | solution.py:405
  58.7 7.2 %collective-permute-done.11.refs_3_ = bf16[16,5248]{1,0:T(8,128)(2,1)S(1)} collective-permute-done((bf16[16,5248]{1,0:T(8,128)(2,1)S(1)}, bf16[16,5248]{1,0:T(8,128)(2,1)S(1)}, u32[]{:S(2)}, u32[]{:S(2)}) %collective-permute-start.11) | collective-permute-done | bytes 167968 | tf_op jit(solution)/shard_map/ppermute | solution.py:405
  66.5 2.2 %collective-permute-done.12.refs_4_ = bf16[16,5248]{1,0:T(8,128)(2,1)S(1)} collective-permute-done((bf16[16,5248]{1,0:T(8,128)(2,1)S(1)}, bf16[16,5248]{1,0:T(8,128)(2,1)S(1)}, u32[]{:S(2)}, u32[]{:S(2)}) %collective-permute-start.12) | collective-permute-done | bytes 167968 | tf_op jit(solution)/shard_map/ppermute | solution.py:405
  68.7 3.4 %collective-permute-done.14.refs_6_ = bf16[16,5248]{1,0:T(8,128)(2,1)S(1)} collective-permute-done((bf16[16,5248]{1,0:T(8,128)(2,1)S(1)}, bf16[16,5248]{1,0:T(8,128)(2,1)S(1)}, u32[]{:S(2)}, u32[]{:S(2)}) %collective-permute-start.14) | collective-permute-done | bytes 167968 | tf_op jit(solution)/shard_map/ppermute | solution.py:405
  73.1 1.6 %collective-permute-done.9.refs_1_ = bf16[16,5248]{1,0:T(8,128)(2,1)S(1)} collective-permute-done((bf16[16,5248]{1,0:T(8,128)(2,1)S(1)}, bf16[16,5248]{1,0:T(8,128)(2,1)S(1)}, u32[]{:S(2)}, u32[]{:S(2)}) %collective-permute-start.9) | collective-permute-done | bytes 167968 | tf_op jit(solution)/shard_map/ppermute | solution.py:405
  (28 shorter events, 7.8 us)
Async XLA Ops:
  2.1 9.7 %collective-permute-start = (bf16[640,256]{1,0:T(8,128)(2,1)}, bf16[640,256]{1,0:T(8,128)(2,1)S(1)}, u32[]{:S(2)}, u32[]{:S(2)}) collective-permute-start(bf16[640,256]{1,0:T(8,128)(2,1)} %get-tuple-element.24), channel_id=1, source_target_pairs={{0,4},{4,0},{8,12},{12,8},{16,20},{20,16},{24,28},{28,24},{1,5},{5... | collective-permute-start | bytes 983048 | tf_op jit(solution)/shard_map/ppermute | solution.py:374
  2.7 11.1 %collective-permute-start.1 = (bf16[640,256]{1,0:T(8,128)(2,1)S(1)}, bf16[640,256]{1,0:T(8,128)(2,1)S(1)}, u32[]{:S(2)}, u32[]{:S(2)}) collective-permute-start(bf16[640,256]{1,0:T(8,128)(2,1)S(1)} %get-tuple-element.25.refs_1_), channel_id=1, source_target_pairs={{0,8},{8,16},{12,4},{16,24},{20,12},{28,20},{1,9},{9,17},{13,5},{1... | collective-permute-start | bytes 983048 | tf_op jit(solution)/shard_map/ppermute | solution.py:376
  5.0 17.2 %collective-permute-start.5 = (bf16[640,256]{1,0:T(8,128)(2,1)S(1)}, bf16[640,256]{1,0:T(8,128)(2,1)S(1)}, u32[]{:S(2)}, u32[]{:S(2)}) collective-permute-start(bf16[640,256]{1,0:T(8,128)(2,1)S(1)} %get-tuple-element.25.refs_1_), channel_id=1, source_target_pairs={{4,12},{8,0},{12,20},{16,8},{20,28},{24,16},{5,13},{9,1},{13,21},{... | collective-permute-start | bytes 983048 | tf_op jit(solution)/shard_map/ppermute | solution.py:375
  8.5 0.7 copy-start.2
  9.2 0.7 copy-start.3
  13.7 12.9 %collective-permute-start.3 = (bf16[640,256]{1,0:T(8,128)(2,1)S(1)}, bf16[640,256]{1,0:T(8,128)(2,1)S(1)}, u32[]{:S(2)}, u32[]{:S(2)}) collective-permute-start(bf16[640,256]{1,0:T(8,128)(2,1)S(1)} %collective-permute-done.refs_2_), channel_id=1, source_target_pairs={{0,8},{8,16},{12,4},{16,24},{20,12},{28,20},{1,9},{9,17},{13,5},{1... | collective-permute-start | bytes 983048 | tf_op jit(solution)/shard_map/ppermute | solution.py:380
  16.1 14.1 %collective-permute-start.6 = (bf16[320,256]{1,0:T(8,128)(2,1)S(1)}, bf16[320,256]{1,0:T(8,128)(2,1)S(1)}, u32[]{:S(2)}, u32[]{:S(2)}) collective-permute-start(bf16[320,256]{1,0:T(8,128)(2,1)S(1)} %get-tuple-element.34), channel_id=1, source_target_pairs={{0,4},{4,0},{8,12},{12,8},{16,20},{20,16},{24,28},{28,24},{1,5},{5... | collective-permute-start | bytes 491528 | tf_op jit(solution)/shard_map/ppermute | solution.py:381
  18.8 16.6 %collective-permute-start.2 = (bf16[640,256]{1,0:T(8,128)(2,1)S(1)}, bf16[640,256]{1,0:T(8,128)(2,1)S(1)}, u32[]{:S(2)}, u32[]{:S(2)}) collective-permute-start(bf16[640,256]{1,0:T(8,128)(2,1)S(1)} %collective-permute-done.refs_2_), channel_id=1, source_target_pairs={{4,12},{8,0},{12,20},{16,8},{20,28},{24,16},{5,13},{9,1},{13,21},{... | collective-permute-start | bytes 983048 | tf_op jit(solution)/shard_map/ppermute | solution.py:383
  22.3 13.1 %collective-permute-start.7 = (bf16[640,256]{1,0:T(8,128)(2,1)S(1)}, bf16[640,256]{1,0:T(8,128)(2,1)S(1)}, u32[]{:S(2)}, u32[]{:S(2)}) collective-permute-start(bf16[640,256]{1,0:T(8,128)(2,1)S(1)} %collective-permute-done.5.refs_3_), channel_id=1, source_target_pairs={{4,12},{8,0},{12,20},{16,8},{20,28},{24,16},{5,13},{9,1},{13,21},{... | collective-permute-start | bytes 983048 | tf_op jit(solution)/shard_map/ppermute | solution.py:384
  26.6 11.4 %collective-permute-start.4 = (bf16[640,256]{1,0:T(8,128)(2,1)S(1)}, bf16[640,256]{1,0:T(8,128)(2,1)S(1)}, u32[]{:S(2)}, u32[]{:S(2)}) collective-permute-start(bf16[640,256]{1,0:T(8,128)(2,1)S(1)} %collective-permute-done.3.refs_2_), channel_id=1, source_target_pairs={{0,8},{8,16},{12,4},{16,24},{20,12},{28,20},{1,9},{9,17},{13,5},{1... | collective-permute-start | bytes 983048 | tf_op jit(solution)/shard_map/ppermute | solution.py:382
  37.7 5.4 %copy-start = (bf16[640,1280]{1,0:T(8,128)(2,1)S(1)}, bf16[640,1280]{1,0:T(8,128)(2,1)}, u32[]{:S(2)}) copy-start(bf16[640,1280]{1,0:T(8,128)(2,1)} %weight_ref.1) | copy-start | bytes 4915204
  37.7 5.4 %copy-start.1 = (bf16[256,1280]{1,0:T(8,128)(2,1)S(1)}, bf16[256,1280]{1,0:T(8,128)(2,1)}, u32[]{:S(2)}) copy-start(bf16[256,1280]{1,0:T(8,128)(2,1)} %tokens_ref.1) | copy-start | bytes 1966084
  37.8 5.4 %copy-start.4 = (s32[64]{0:T(128)S(1)}, s32[64]{0:T(128)}, u32[]{:S(2)}) copy-start(s32[64]{0:T(128)} %param.16) | copy-start | bytes 772
  37.8 5.4 %copy-start.5 = (s32[64]{0:T(128)S(1)}, s32[64]{0:T(128)}, u32[]{:S(2)}) copy-start(s32[64]{0:T(128)} %param.17) | copy-start | bytes 772
  37.8 5.4 %collective-permute-start.8 = (bf16[320,256]{1,0:T(8,128)(2,1)S(1)}, bf16[320,256]{1,0:T(8,128)(2,1)S(1)}, u32[]{:S(2)}, u32[]{:S(2)}) collective-permute-start(bf16[320,256]{1,0:T(8,128)(2,1)S(1)} %shard_map.96), channel_id=1, source_target_pairs={{0,4},{4,0},{8,12},{12,8},{16,20},{20,16},{24,28},{28,24},{1,5},{5... | collective-permute-start | bytes 491528 | tf_op jit(solution)/shard_map/ppermute | solution.py:392
  44.7 14.0 %collective-permute-start.10 = (bf16[16,5248]{1,0:T(8,128)(2,1)S(1)}, bf16[16,5248]{1,0:T(8,128)(2,1)S(1)}, u32[]{:S(2)}, u32[]{:S(2)}) collective-permute-start(bf16[16,5248]{1,0:T(8,128)(2,1)S(1)} %get-tuple-element.37), channel_id=1, source_target_pairs={{0,8},{4,12},{8,16},{12,20},{16,24},{20,28},{24,0},{28,4},{1,9},{5... | collective-permute-start | bytes 503816 | tf_op jit(solution)/shard_map/ppermute | solution.py:405
  44.7 21.2 %collective-permute-start.11 = (bf16[16,5248]{1,0:T(8,128)(2,1)S(1)}, bf16[16,5248]{1,0:T(8,128)(2,1)S(1)}, u32[]{:S(2)}, u32[]{:S(2)}) collective-permute-start(bf16[16,5248]{1,0:T(8,128)(2,1)S(1)} %get-tuple-element.38), channel_id=1, source_target_pairs={{0,12},{4,16},{8,20},{12,24},{16,28},{20,0},{24,4},{28,8},{1,13},{... | collective-permute-start | bytes 503816 | tf_op jit(solution)/shard_map/ppermute | solution.py:405
  47.3 21.4 %collective-permute-start.12 = (bf16[16,5248]{1,0:T(8,128)(2,1)S(1)}, bf16[16,5248]{1,0:T(8,128)(2,1)S(1)}, u32[]{:S(2)}, u32[]{:S(2)}) collective-permute-start(bf16[16,5248]{1,0:T(8,128)(2,1)S(1)} %get-tuple-element.39), channel_id=1, source_target_pairs={{0,16},{4,20},{8,24},{12,28},{16,0},{20,4},{24,8},{28,12},{1,17},{... | collective-permute-start | bytes 503816 | tf_op jit(solution)/shard_map/ppermute | solution.py:405
  49.0 19.7 %collective-permute-start.13 = (bf16[16,5248]{1,0:T(8,128)(2,1)S(1)}, bf16[16,5248]{1,0:T(8,128)(2,1)S(1)}, u32[]{:S(2)}, u32[]{:S(2)}) collective-permute-start(bf16[16,5248]{1,0:T(8,128)(2,1)S(1)} %get-tuple-element.40), channel_id=1, source_target_pairs={{0,20},{4,24},{8,28},{12,0},{16,4},{20,8},{24,12},{28,16},{1,21},{... | collective-permute-start | bytes 503816 | tf_op jit(solution)/shard_map/ppermute | solution.py:405
  49.6 22.5 %collective-permute-start.14 = (bf16[16,5248]{1,0:T(8,128)(2,1)S(1)}, bf16[16,5248]{1,0:T(8,128)(2,1)S(1)}, u32[]{:S(2)}, u32[]{:S(2)}) collective-permute-start(bf16[16,5248]{1,0:T(8,128)(2,1)S(1)} %get-tuple-element.41), channel_id=1, source_target_pairs={{0,24},{4,28},{8,0},{12,4},{16,8},{20,12},{24,16},{28,20},{1,25},{... | collective-permute-start | bytes 503816 | tf_op jit(solution)/shard_map/ppermute | solution.py:405
  58.7 14.4 %collective-permute-start.15 = (bf16[16,5248]{1,0:T(8,128)(2,1)S(1)}, bf16[16,5248]{1,0:T(8,128)(2,1)S(1)}, u32[]{:S(2)}, u32[]{:S(2)}) collective-permute-start(bf16[16,5248]{1,0:T(8,128)(2,1)S(1)} %get-tuple-element.42), channel_id=1, source_target_pairs={{0,28},{4,0},{8,4},{12,8},{16,12},{20,16},{24,20},{28,24},{1,29},{... | collective-permute-start | bytes 503816 | tf_op jit(solution)/shard_map/ppermute | solution.py:405
  65.9 8.8 %collective-permute-start.9 = (bf16[16,5248]{1,0:T(8,128)(2,1)S(1)}, bf16[16,5248]{1,0:T(8,128)(2,1)S(1)}, u32[]{:S(2)}, u32[]{:S(2)}) collective-permute-start(bf16[16,5248]{1,0:T(8,128)(2,1)S(1)} %get-tuple-element.36), channel_id=1, source_target_pairs={{0,4},{4,8},{8,12},{12,16},{16,20},{20,24},{24,28},{28,0},{1,5},{5... | collective-permute-start | bytes 503816 | tf_op jit(solution)/shard_map/ppermute | solution.py:405

commit v14 on v13

--- a/solution.py
+++ b/solution.py
@@ -113,9 +113,10 @@
     )(where, mask, segs)
 
 
-def attention_kernel(kinds, numbers, follows, ends, where_ref, need_ref, seg_ref, *refs):
+def attention_kernel(kinds, numbers, rows_of, follows, ends, where_ref, need_ref, seg_ref, *refs):
     queries, refs = refs[: len(kinds)], refs[len(kinds) :]
-    blocks, refs = refs[: len(numbers)], refs[len(numbers) :]
+    arrays = max(array for array, _ in rows_of) + 1
+    blocks, refs = refs[:arrays], refs[arrays:]
     if follows:
         before, refs = refs[0], refs[1:]
     out_ref, query_s, key_s, value_s, chosen_s = refs
@@ -141,10 +142,11 @@
 
         @pl.when(wanted > 0)
         def _(b=b):
-            key_s[b] = blocks[b][:part, :]
+            array, first = rows_of[b]
+            key_s[b] = blocks[array][first : first + part, :]
             for h in range(HALF):
-                lines = slice(part + h * hdim, part + (h + 1) * hdim)
-                value_s[b, h, :hdim, :] = blocks[b][lines, :]
+                start = first + part + h * hdim
+                value_s[b, h, :hdim, :] = blocks[array][start : start + hdim, :]
                 value_s[b, h, hdim:, :] = jnp.ones((wide - hdim, rows), jnp.bfloat16)
 
     for n in range(len(kinds)):
@@ -220,14 +222,19 @@
     hdim = part // HALF
     wide = hdim + 16
     follows = before is not None
+    rows_of = [
+        (array, first)
+        for array, block in enumerate(blocks)
+        for first in range(0, block.shape[0], 2 * part)
+    ]
     if ends:
         out = jax.ShapeDtypeStruct((part, rows), jnp.bfloat16)
     else:
         out = jax.ShapeDtypeStruct((len(kinds), HALF, rows, 128), jnp.float32)
     return pl.pallas_call(
-        functools.partial(attention_kernel, kinds, numbers, follows, ends),
+        functools.partial(attention_kernel, kinds, numbers, rows_of, follows, ends),
         out_shape=out,
-        in_specs=[smem()] + [vmem()] * (2 + len(kinds) + len(numbers) + follows),
+        in_specs=[smem()] + [vmem()] * (2 + len(kinds) + len(blocks) + follows),
         out_specs=vmem(),
         scratch_shapes=[
             pltpu.VMEM((HALF, rows, hdim), jnp.bfloat16),
@@ -240,6 +247,25 @@
             flops=2_000_000_000 * len(kinds), bytes_accessed=2_000_000, transcendentals=1_000_000
         ),
     )(where, need, segs, *queries, *blocks, *((before,) if follows else ()))
+
+
+def stack_kernel(*refs):
+    *parts, out_ref = refs
+    first = 0
+    for ref in parts:
+        out_ref[first : first + ref.shape[0], :] = ref[...]
+        first += ref.shape[0]
+
+
+def stack(*parts):
+    lines = sum(part.shape[0] for part in parts)
+    return pl.pallas_call(
+        stack_kernel,
+        out_shape=jax.ShapeDtypeStruct((lines, parts[0].shape[1]), parts[0].dtype),
+        in_specs=[vmem()] * len(parts),
+        out_specs=vmem(),
+        compiler_params=limit(16),
+    )(*parts)
 
 
 def project_kernel(
@@ -378,20 +404,19 @@
         (other_kv, back_own, swap_q, segs, need)
     )
     back_other = back(ready)
+    ahead_both = ahead(stack(other_kv, ahead_own))
     other_q = swap(swap_q)
     back_far = back(back_other)
-    ahead_other = ahead(other_kv)
-    ahead_far = ahead(ahead_own)
     near = (own_kv, other_kv, ahead_own, back_own)
     near_numbers = (0, 1, 2, 3)
     fixed = (where, need, segs)
     own = attention(*fixed, (own_q,), (0,), near, near_numbers, None, False)
     other = attention(*fixed, (other_q,), (1,), near, near_numbers, None, False)
-    far = (ahead_other, back_other, ahead_far)
-    other = attention(*fixed, (other_q,), (1,), far, (4, 5, 6), other, True)
+    far = (ahead_both, back_other)
+    other = attention(*fixed, (other_q,), (1,), far, (4, 6, 5), other, True)
     other = swap(other)
-    far = (ahead_other, back_other, back_far)
-    own = attention(*fixed, (own_q,), (0,), far, (4, 5, 7), own, True)
+    far = (ahead_both, back_other, back_far)
+    own = attention(*fixed, (own_q,), (0,), far, (4, 6, 5, 7), own, True)
 
     pieces = nblocks if nblocks <= 8 else 1
     outgoing = project(

time: 76.9 us -> 74.4 us (0.967)
  local copies, waits for them, and re-layouts: 1.4 us -> 0.03 us
  starting transfers between devices: 27.9 us -> 27 us
    ppermute x1, waiting for transfers between devices: 0.01 us -> 3.93 us  [per_device(): back_other = back(ready)]
    ppermute x2 -> x1, waiting for transfers between devices: 3.23 us -> 0.01 us  [per_device(): ahead_both = ahead(stack(other_kv, ahead_own))]
    ppermute x1, waiting for transfers between devices: 1.19 us -> 3.29 us  [per_device(): other_kv = swap(swap_kv)]
    ppermute x1, waiting for transfers between devices: 3.17 us -> 1.22 us  [per_device(): other = swap(other)]
    ppermute x2 -> x1, starting transfers between devices: 5.39 us -> 3.48 us  [per_device(): ahead_both = ahead(stack(other_kv, ahead_own))]
    ppermute x1, waiting for transfers between devices: 0.01 us -> 1.9 us  [per_device(): ahead_own = ahead(own_kv)]
    ppermute x1, waiting for transfers between devices: 1.9 us -> 0.01 us  [per_device(): back_own = back(own_kv)]
    ppermute x1, starting transfers between devices: 0.21 us -> 1.99 us  [per_device(): other = swap(other)]
  transfers between devices with their start and end apart: 16 -> 15, of which waited for: 10 -> 11; matrix products, arithmetic and copies ran while one was open for 0% -> 0% of each run, Pallas kernels for 12% -> 12%
where the time goes in v14:
time: 74.4 us; the launch traced here: 73.3 us
  waiting for transfers between devices  31.9 us (43%)
  starting transfers between devices  27 us (36%)
  Pallas kernels  14.1 us (19%)
    ppermute x7, waiting for transfers between devices, per_device(): lax.ppermute(outgoing[d], 'blk', [(i, (i + d) % nblocks) for i in range(n...  21.4 us
    ppermute x7, starting transfers between devices, per_device(): lax.ppermute(outgoing[d], 'blk', [(i, (i + d) % nblocks) for i in range(n...  8.73 us
    pallas_call x4, Pallas kernels, attention(): pl.pallas_call(functools.partial(attention_kernel, kinds, numbers, rows_o...  8.3 us
    ppermute x1, waiting for transfers between devices, per_device(): back_other = back(ready)  3.93 us
    ppermute x1, starting transfers between devices, per_device(): ahead_both = ahead(stack(other_kv, ahead_own))  3.48 us
    ppermute x1, starting transfers between devices, per_device(): ahead_own = ahead(own_kv)  3.47 us
    ppermute x1, waiting for transfers between devices, per_device(): other_kv = swap(swap_kv)  3.29 us
    ppermute x1, starting transfers between devices, per_device(): back_other = back(ready)  2.39 us
  transfers between devices with their start and end apart: 15, of which 11 were waited for; matrix products, arithmetic and copies ran while one was open for 0% of the time, Pallas kernels for 12%

profile of v14, /device:TPU:14, one launch (start us, length us, event | category | flops | bytes accessed | tf_op | source)
XLA Modules:
  0.0 73.3 jit_solution(14288492628331900389)
XLA Ops:
  0.0 2.1 %shard_map.91 = (bf16[320,256]{1,0:T(8,128)(2,1)S(1)}, bf16[640,256]{1,0:T(8,128)(2,1)S(1)}, bf16[320,256]{1,0:T(8,128)(2,1)S(1)}, bf16[640,256]{1,0:T(8,128)(2,1)}) custom-call(s32[1]{0:T(128)} %bitcast.where_ref, bf16[256,640]{1,0:T(8,128)(2,1)} %q_hbm.1, bf16[256,640]{1,0:T(8,128)(2,1)} %k_hbm.1, bf16[256,640]{1,0:T(8,128)(2,1)} %v_hbm.1), custom_call_target="tpu_custom_call" | custom-call | tf_op jit(solution)/shard_map/pallas_call | solution.py:74
  2.7 3.5 %collective-permute-start.2 = (bf16[640,256]{1,0:T(8,128)(2,1)S(1)}, bf16[640,256]{1,0:T(8,128)(2,1)S(1)}, u32[]{:S(2)}, u32[]{:S(2)}) collective-permute-start(bf16[640,256]{1,0:T(8,128)(2,1)S(1)} %get-tuple-element.25.refs_1_), channel_id=1, source_target_pairs={{4,12},{8,0},{12,20},{16,8},{20,28},{24,16},{5,13},{9,1},{13,21},{... | collective-permute-start | bytes 983048 | tf_op jit(solution)/shard_map/ppermute | solution.py:401
  6.2 2.4 %collective-permute-start.1 = (bf16[640,256]{1,0:T(8,128)(2,1)S(1)}, bf16[640,256]{1,0:T(8,128)(2,1)S(1)}, u32[]{:S(2)}, u32[]{:S(2)}) collective-permute-start(bf16[640,256]{1,0:T(8,128)(2,1)S(1)} %get-tuple-element.25.refs_1_), channel_id=1, source_target_pairs={{0,8},{8,16},{12,4},{16,24},{20,12},{28,20},{1,9},{9,17},{13,5},{1... | collective-permute-start | bytes 983048 | tf_op jit(solution)/shard_map/ppermute | solution.py:402
  8.5 3.3 %collective-permute-done.refs_0_.refs_2_ = bf16[640,256]{1,0:T(8,128)(2,1)S(1)} collective-permute-done((bf16[640,256]{1,0:T(8,128)(2,1)}, bf16[640,256]{1,0:T(8,128)(2,1)S(1)}, u32[]{:S(2)}, u32[]{:S(2)}) %collective-permute-start) | collective-permute-done | bytes 327712 | tf_op jit(solution)/shard_map/ppermute | solution.py:400
  11.8 1.9 %collective-permute-done.2.refs_1_.refs_3_ = bf16[640,256]{1,0:T(8,128)(2,1)S(1)} collective-permute-done((bf16[640,256]{1,0:T(8,128)(2,1)S(1)}, bf16[640,256]{1,0:T(8,128)(2,1)S(1)}, u32[]{:S(2)}, u32[]{:S(2)}) %collective-permute-start.2) | collective-permute-done | bytes 327712 | tf_op jit(solution)/shard_map/ppermute | solution.py:401
  13.8 3.5 %collective-permute-start.3 = (bf16[1280,256]{1,0:T(8,128)(2,1)S(1)}, bf16[1280,256]{1,0:T(8,128)(2,1)S(1)}, u32[]{:S(2)}, u32[]{:S(2)}) collective-permute-start(bf16[1280,256]{1,0:T(8,128)(2,1)S(1)} %shard_map.93), channel_id=1, source_target_pairs={{4,12},{8,0},{12,20},{16,8},{20,28},{24,16},{5,13},{9,1},{13,21},{... | collective-permute-start | bytes 1966088 | tf_op jit(solution)/shard_map/ppermute | solution.py:407
  18.0 2.4 %collective-permute-start.4 = (bf16[640,256]{1,0:T(8,128)(2,1)S(1)}, bf16[640,256]{1,0:T(8,128)(2,1)S(1)}, u32[]{:S(2)}, u32[]{:S(2)}) collective-permute-start(bf16[640,256]{1,0:T(8,128)(2,1)S(1)} %collective-permute-done.refs_0_.refs_2_), channel_id=1, source_target_pairs={{0,8},{8,16},{12,4},{16,24},{20,12},{28,20},{1,9},{9,17},{13,5},{1... | collective-permute-start | bytes 983048 | tf_op jit(solution)/shard_map/ppermute | solution.py:406
  20.4 1.5 %collective-permute-start.6 = (bf16[320,256]{1,0:T(8,128)(2,1)S(1)}, bf16[320,256]{1,0:T(8,128)(2,1)S(1)}, u32[]{:S(2)}, u32[]{:S(2)}) collective-permute-start(bf16[320,256]{1,0:T(8,128)(2,1)S(1)} %get-tuple-element.34), channel_id=1, source_target_pairs={{0,4},{4,0},{8,12},{12,8},{16,20},{20,16},{24,28},{28,24},{1,5},{5... | collective-permute-start | bytes 491528 | tf_op jit(solution)/shard_map/ppermute | solution.py:408
  22.0 2.0 %shard_map.94.refs_4_ = f32[1,4,256,128]{3,2,1,0:T(8,128)S(1)} custom-call(s32[1]{0:T(128)} %bitcast.where_ref, s32[8,128]{1,0:T(8,128)S(1)} %get-tuple-element.29.need_ref, f32[1,2048]{1,0:T(1,128)S(1)} %get-tuple-element.30.seg_ref, bf16[320,256]{1,0:T(8,128)(2,1)S(1)} %get-tuple-element.31.refs_0_, bf16[640,256]{1,0:T(8,128)(2,1)S(1)} %get-tuple-element.25.refs_1_, ...), custom_call_target="tpu_custom_call" | custom-call | flops 2000000000 | bytes 2000000 | tf_op jit(solution)/shard_map/pallas_call | solution.py:234
  24.0 3.9 %collective-permute-done.4.refs_2_ = bf16[640,256]{1,0:T(8,128)(2,1)S(1)} collective-permute-done((bf16[640,256]{1,0:T(8,128)(2,1)S(1)}, bf16[640,256]{1,0:T(8,128)(2,1)S(1)}, u32[]{:S(2)}, u32[]{:S(2)}) %collective-permute-start.4) | collective-permute-done | bytes 327712 | tf_op jit(solution)/shard_map/ppermute | solution.py:406
  27.9 2.4 %collective-permute-start.5 = (bf16[640,256]{1,0:T(8,128)(2,1)S(1)}, bf16[640,256]{1,0:T(8,128)(2,1)S(1)}, u32[]{:S(2)}, u32[]{:S(2)}) collective-permute-start(bf16[640,256]{1,0:T(8,128)(2,1)S(1)} %collective-permute-done.4.refs_2_), channel_id=1, source_target_pairs={{0,8},{8,16},{12,4},{16,24},{20,12},{28,20},{1,9},{9,17},{13,5},{1... | collective-permute-start | bytes 983048 | tf_op jit(solution)/shard_map/ppermute | solution.py:409
  30.3 2.0 %shard_map.96.refs_3_ = f32[1,4,256,128]{3,2,1,0:T(8,128)S(1)} custom-call(s32[1]{0:T(128)} %bitcast.where_ref, s32[8,128]{1,0:T(8,128)S(1)} %get-tuple-element.29.need_ref, f32[1,2048]{1,0:T(1,128)S(1)} %get-tuple-element.30.seg_ref, bf16[320,256]{1,0:T(8,128)(2,1)S(1)} %collective-permute-done.6.refs_0_, bf16[640,256]{1,0:T(8,128)(2,1)S(1)} %get-tuple-element.25.refs_1_, ...), custom_call_target="tpu_custom_call" | custom-call | flops 2000000000 | bytes 2000000 | tf_op jit(solution)/shard_map/pallas_call | solution.py:234
  32.3 2.3 %shard_map.97 = bf16[320,256]{1,0:T(8,128)(2,1)S(1)} custom-call(s32[1]{0:T(128)} %bitcast.where_ref, s32[8,128]{1,0:T(8,128)S(1)} %get-tuple-element.29.need_ref, f32[1,2048]{1,0:T(1,128)S(1)} %get-tuple-element.30.seg_ref, bf16[320,256]{1,0:T(8,128)(2,1)S(1)} %collective-permute-done.6.refs_0_, bf16[1280,256]{1,0:T(8,128)(2,1)S(1)} %collective-permute-done.3.refs_1_, ...), custom_call_target="tpu_custom_call" | custom-call | flops 2000000000 | bytes 2000000 | tf_op jit(solution)/shard_map/pallas_call | solution.py:234
  34.7 2.0 %collective-permute-start.7 = (bf16[320,256]{1,0:T(8,128)(2,1)S(1)}, bf16[320,256]{1,0:T(8,128)(2,1)S(1)}, u32[]{:S(2)}, u32[]{:S(2)}) collective-permute-start(bf16[320,256]{1,0:T(8,128)(2,1)S(1)} %shard_map.97), channel_id=1, source_target_pairs={{0,4},{4,0},{8,12},{12,8},{16,20},{20,16},{24,28},{28,24},{1,5},{5... | collective-permute-start | bytes 491528 | tf_op jit(solution)/shard_map/ppermute | solution.py:417
  36.9 2.0 %shard_map.95.own_ref = bf16[320,256]{1,0:T(8,128)(2,1)S(1)} custom-call(s32[1]{0:T(128)} %bitcast.where_ref, s32[8,128]{1,0:T(8,128)S(1)} %get-tuple-element.29.need_ref, f32[1,2048]{1,0:T(1,128)S(1)} %get-tuple-element.30.seg_ref, bf16[320,256]{1,0:T(8,128)(2,1)S(1)} %get-tuple-element.31.refs_0_, bf16[1280,256]{1,0:T(8,128)(2,1)S(1)} %collective-permute-done.3.refs_1_, ...), custom_call_target="tpu_custom_call" | custom-call | flops 2000000000 | bytes 2000000 | tf_op jit(solution)/shard_map/pallas_call | solution.py:234
  40.1 1.5 %shard_map.98 = (bf16[16,5248]{1,0:T(8,128)(2,1)S(1)}, bf16[16,5248]{1,0:T(8,128)(2,1)S(1)}, bf16[16,5248]{1,0:T(8,128)(2,1)S(1)}, bf16[16,5248]{1,0:T(8,128)(2,...) custom-call(s32[1]{0:T(128)} %bitcast.where_ref, ...), custom_call_target="tpu_custom_call" | custom-call | tf_op jit(solution)/shard_map/pallas_call | solution.py:324
  41.6 2.6 %collective-permute-start.8 = (bf16[16,5248]{1,0:T(8,128)(2,1)S(1)}, bf16[16,5248]{1,0:T(8,128)(2,1)S(1)}, u32[]{:S(2)}, u32[]{:S(2)}) collective-permute-start(bf16[16,5248]{1,0:T(8,128)(2,1)S(1)} %get-tuple-element.36), channel_id=1, source_target_pairs={{0,4},{4,8},{8,12},{12,16},{16,20},{20,24},{24,28},{28,0},{1,5},{5... | collective-permute-start | bytes 503816 | tf_op jit(solution)/shard_map/ppermute | solution.py:430
  45.5 1.9 %collective-permute-start.11 = (bf16[16,5248]{1,0:T(8,128)(2,1)S(1)}, bf16[16,5248]{1,0:T(8,128)(2,1)S(1)}, u32[]{:S(2)}, u32[]{:S(2)}) collective-permute-start(bf16[16,5248]{1,0:T(8,128)(2,1)S(1)} %get-tuple-element.39), channel_id=1, source_target_pairs={{0,16},{4,20},{8,24},{12,28},{16,0},{20,4},{24,8},{28,12},{1,17},{... | collective-permute-start | bytes 503816 | tf_op jit(solution)/shard_map/ppermute | solution.py:430
  47.4 2.9 %collective-permute-start.12 = (bf16[16,5248]{1,0:T(8,128)(2,1)S(1)}, bf16[16,5248]{1,0:T(8,128)(2,1)S(1)}, u32[]{:S(2)}, u32[]{:S(2)}) collective-permute-start(bf16[16,5248]{1,0:T(8,128)(2,1)S(1)} %get-tuple-element.40), channel_id=1, source_target_pairs={{0,20},{4,24},{8,28},{12,0},{16,4},{20,8},{24,12},{28,16},{1,21},{... | collective-permute-start | bytes 503816 | tf_op jit(solution)/shard_map/ppermute | solution.py:430
  50.3 2.2 %collective-permute-done.8.refs_1_ = bf16[16,5248]{1,0:T(8,128)(2,1)S(1)} collective-permute-done((bf16[16,5248]{1,0:T(8,128)(2,1)S(1)}, bf16[16,5248]{1,0:T(8,128)(2,1)S(1)}, u32[]{:S(2)}, u32[]{:S(2)}) %collective-permute-start.8) | collective-permute-done | bytes 167968 | tf_op jit(solution)/shard_map/ppermute | solution.py:430
  52.6 12.8 %collective-permute-done.9.refs_2_ = bf16[16,5248]{1,0:T(8,128)(2,1)S(1)} collective-permute-done((bf16[16,5248]{1,0:T(8,128)(2,1)S(1)}, bf16[16,5248]{1,0:T(8,128)(2,1)S(1)}, u32[]{:S(2)}, u32[]{:S(2)}) %collective-permute-start.9) | collective-permute-done | bytes 167968 | tf_op jit(solution)/shard_map/ppermute | solution.py:430
  65.4 1.8 %collective-permute-done.10.refs_3_ = bf16[16,5248]{1,0:T(8,128)(2,1)S(1)} collective-permute-done((bf16[16,5248]{1,0:T(8,128)(2,1)S(1)}, bf16[16,5248]{1,0:T(8,128)(2,1)S(1)}, u32[]{:S(2)}, u32[]{:S(2)}) %collective-permute-start.10) | collective-permute-done | bytes 167968 | tf_op jit(solution)/shard_map/ppermute | solution.py:430
  67.2 1.8 %collective-permute-done.11.refs_4_ = bf16[16,5248]{1,0:T(8,128)(2,1)S(1)} collective-permute-done((bf16[16,5248]{1,0:T(8,128)(2,1)S(1)}, bf16[16,5248]{1,0:T(8,128)(2,1)S(1)}, u32[]{:S(2)}, u32[]{:S(2)}) %collective-permute-start.11) | collective-permute-done | bytes 167968 | tf_op jit(solution)/shard_map/ppermute | solution.py:430
  69.0 1.9 %collective-permute-done.13.refs_6_ = bf16[16,5248]{1,0:T(8,128)(2,1)S(1)} collective-permute-done((bf16[16,5248]{1,0:T(8,128)(2,1)S(1)}, bf16[16,5248]{1,0:T(8,128)(2,1)S(1)}, u32[]{:S(2)}, u32[]{:S(2)}) %collective-permute-start.13) | collective-permute-done | bytes 167968 | tf_op jit(solution)/shard_map/ppermute | solution.py:430
  (27 shorter events, 6.4 us)
Async XLA Ops:
  0.0 17.3 %copy-start.3 = (s32[8,8]{1,0:T(8,128)S(1)}, s32[8,8]{1,0:T(8,128)}, u32[]{:S(2)}) copy-start(s32[8,8]{1,0:T(8,128)} %mask_ref.1) | copy-start | bytes 772
  0.0 17.3 %copy-start.2 = (s32[2048]{0:T(1024)S(1)}, s32[2048]{0:T(1024)}, u32[]{:S(2)}) copy-start(s32[2048]{0:T(1024)} %param.9) | copy-start | bytes 24580
  2.1 9.7 %collective-permute-start = (bf16[640,256]{1,0:T(8,128)(2,1)}, bf16[640,256]{1,0:T(8,128)(2,1)S(1)}, u32[]{:S(2)}, u32[]{:S(2)}) collective-permute-start(bf16[640,256]{1,0:T(8,128)(2,1)} %get-tuple-element.24), channel_id=1, source_target_pairs={{0,4},{4,0},{8,12},{12,8},{16,20},{20,16},{24,28},{28,24},{1,5},{5... | collective-permute-start | bytes 983048 | tf_op jit(solution)/shard_map/ppermute | solution.py:400
  2.7 11.1 %collective-permute-start.2 = (bf16[640,256]{1,0:T(8,128)(2,1)S(1)}, bf16[640,256]{1,0:T(8,128)(2,1)S(1)}, u32[]{:S(2)}, u32[]{:S(2)}) collective-permute-start(bf16[640,256]{1,0:T(8,128)(2,1)S(1)} %get-tuple-element.25.refs_1_), channel_id=1, source_target_pairs={{4,12},{8,0},{12,20},{16,8},{20,28},{24,16},{5,13},{9,1},{13,21},{... | collective-permute-start | bytes 983048 | tf_op jit(solution)/shard_map/ppermute | solution.py:401
  6.2 11.9 %collective-permute-start.1 = (bf16[640,256]{1,0:T(8,128)(2,1)S(1)}, bf16[640,256]{1,0:T(8,128)(2,1)S(1)}, u32[]{:S(2)}, u32[]{:S(2)}) collective-permute-start(bf16[640,256]{1,0:T(8,128)(2,1)S(1)} %get-tuple-element.25.refs_1_), channel_id=1, source_target_pairs={{0,8},{8,16},{12,4},{16,24},{20,12},{28,20},{1,9},{9,17},{13,5},{1... | collective-permute-start | bytes 983048 | tf_op jit(solution)/shard_map/ppermute | solution.py:402
  13.8 18.5 %collective-permute-start.3 = (bf16[1280,256]{1,0:T(8,128)(2,1)S(1)}, bf16[1280,256]{1,0:T(8,128)(2,1)S(1)}, u32[]{:S(2)}, u32[]{:S(2)}) collective-permute-start(bf16[1280,256]{1,0:T(8,128)(2,1)S(1)} %shard_map.93), channel_id=1, source_target_pairs={{4,12},{8,0},{12,20},{16,8},{20,28},{24,16},{5,13},{9,1},{13,21},{... | collective-permute-start | bytes 1966088 | tf_op jit(solution)/shard_map/ppermute | solution.py:407
  18.0 9.9 %collective-permute-start.4 = (bf16[640,256]{1,0:T(8,128)(2,1)S(1)}, bf16[640,256]{1,0:T(8,128)(2,1)S(1)}, u32[]{:S(2)}, u32[]{:S(2)}) collective-permute-start(bf16[640,256]{1,0:T(8,128)(2,1)S(1)} %collective-permute-done.refs_0_.refs_2_), channel_id=1, source_target_pairs={{0,8},{8,16},{12,4},{16,24},{20,12},{28,20},{1,9},{9,17},{13,5},{1... | collective-permute-start | bytes 983048 | tf_op jit(solution)/shard_map/ppermute | solution.py:406
  20.4 9.9 %collective-permute-start.6 = (bf16[320,256]{1,0:T(8,128)(2,1)S(1)}, bf16[320,256]{1,0:T(8,128)(2,1)S(1)}, u32[]{:S(2)}, u32[]{:S(2)}) collective-permute-start(bf16[320,256]{1,0:T(8,128)(2,1)S(1)} %get-tuple-element.34), channel_id=1, source_target_pairs={{0,4},{4,0},{8,12},{12,8},{16,20},{20,16},{24,28},{28,24},{1,5},{5... | collective-permute-start | bytes 491528 | tf_op jit(solution)/shard_map/ppermute | solution.py:408
  27.9 9.0 %collective-permute-start.5 = (bf16[640,256]{1,0:T(8,128)(2,1)S(1)}, bf16[640,256]{1,0:T(8,128)(2,1)S(1)}, u32[]{:S(2)}, u32[]{:S(2)}) collective-permute-start(bf16[640,256]{1,0:T(8,128)(2,1)S(1)} %collective-permute-done.4.refs_2_), channel_id=1, source_target_pairs={{0,8},{8,16},{12,4},{16,24},{20,12},{28,20},{1,9},{9,17},{13,5},{1... | collective-permute-start | bytes 983048 | tf_op jit(solution)/shard_map/ppermute | solution.py:409
  34.7 5.4 %copy-start = (bf16[640,1280]{1,0:T(8,128)(2,1)S(1)}, bf16[640,1280]{1,0:T(8,128)(2,1)}, u32[]{:S(2)}) copy-start(bf16[640,1280]{1,0:T(8,128)(2,1)} %weight_ref.1) | copy-start | bytes 4915204
  34.7 5.4 %copy-start.1 = (bf16[256,1280]{1,0:T(8,128)(2,1)S(1)}, bf16[256,1280]{1,0:T(8,128)(2,1)}, u32[]{:S(2)}) copy-start(bf16[256,1280]{1,0:T(8,128)(2,1)} %tokens_ref.1) | copy-start | bytes 1966084
  34.7 5.4 %copy-start.4 = (s32[64]{0:T(128)S(1)}, s32[64]{0:T(128)}, u32[]{:S(2)}) copy-start(s32[64]{0:T(128)} %param.16) | copy-start | bytes 772
  34.7 5.4 %copy-start.5 = (s32[64]{0:T(128)S(1)}, s32[64]{0:T(128)}, u32[]{:S(2)}) copy-start(s32[64]{0:T(128)} %param.17) | copy-start | bytes 772
  34.7 5.4 %collective-permute-start.7 = (bf16[320,256]{1,0:T(8,128)(2,1)S(1)}, bf16[320,256]{1,0:T(8,128)(2,1)S(1)}, u32[]{:S(2)}, u32[]{:S(2)}) collective-permute-start(bf16[320,256]{1,0:T(8,128)(2,1)S(1)} %shard_map.97), channel_id=1, source_target_pairs={{0,4},{4,0},{8,12},{12,8},{16,20},{20,16},{24,28},{28,24},{1,5},{5... | collective-permute-start | bytes 491528 | tf_op jit(solution)/shard_map/ppermute | solution.py:417
  41.6 11.0 %collective-permute-start.8 = (bf16[16,5248]{1,0:T(8,128)(2,1)S(1)}, bf16[16,5248]{1,0:T(8,128)(2,1)S(1)}, u32[]{:S(2)}, u32[]{:S(2)}) collective-permute-start(bf16[16,5248]{1,0:T(8,128)(2,1)S(1)} %get-tuple-element.36), channel_id=1, source_target_pairs={{0,4},{4,8},{8,12},{12,16},{16,20},{20,24},{24,28},{28,0},{1,5},{5... | collective-permute-start | bytes 503816 | tf_op jit(solution)/shard_map/ppermute | solution.py:430
  44.2 21.2 %collective-permute-start.9 = (bf16[16,5248]{1,0:T(8,128)(2,1)S(1)}, bf16[16,5248]{1,0:T(8,128)(2,1)S(1)}, u32[]{:S(2)}, u32[]{:S(2)}) collective-permute-start(bf16[16,5248]{1,0:T(8,128)(2,1)S(1)} %get-tuple-element.37), channel_id=1, source_target_pairs={{0,8},{4,12},{8,16},{12,20},{16,24},{20,28},{24,0},{28,4},{1,9},{5... | collective-permute-start | bytes 503816 | tf_op jit(solution)/shard_map/ppermute | solution.py:430
  44.2 23.0 %collective-permute-start.10 = (bf16[16,5248]{1,0:T(8,128)(2,1)S(1)}, bf16[16,5248]{1,0:T(8,128)(2,1)S(1)}, u32[]{:S(2)}, u32[]{:S(2)}) collective-permute-start(bf16[16,5248]{1,0:T(8,128)(2,1)S(1)} %get-tuple-element.38), channel_id=1, source_target_pairs={{0,12},{4,16},{8,20},{12,24},{16,28},{20,0},{24,4},{28,8},{1,13},{... | collective-permute-start | bytes 503816 | tf_op jit(solution)/shard_map/ppermute | solution.py:430
  45.5 23.5 %collective-permute-start.11 = (bf16[16,5248]{1,0:T(8,128)(2,1)S(1)}, bf16[16,5248]{1,0:T(8,128)(2,1)S(1)}, u32[]{:S(2)}, u32[]{:S(2)}) collective-permute-start(bf16[16,5248]{1,0:T(8,128)(2,1)S(1)} %get-tuple-element.39), channel_id=1, source_target_pairs={{0,16},{4,20},{8,24},{12,28},{16,0},{20,4},{24,8},{28,12},{1,17},{... | collective-permute-start | bytes 503816 | tf_op jit(solution)/shard_map/ppermute | solution.py:430
  47.4 21.5 %collective-permute-start.12 = (bf16[16,5248]{1,0:T(8,128)(2,1)S(1)}, bf16[16,5248]{1,0:T(8,128)(2,1)S(1)}, u32[]{:S(2)}, u32[]{:S(2)}) collective-permute-start(bf16[16,5248]{1,0:T(8,128)(2,1)S(1)} %get-tuple-element.40), channel_id=1, source_target_pairs={{0,20},{4,24},{8,28},{12,0},{16,4},{20,8},{24,12},{28,16},{1,21},{... | collective-permute-start | bytes 503816 | tf_op jit(solution)/shard_map/ppermute | solution.py:430
  52.6 18.3 %collective-permute-start.13 = (bf16[16,5248]{1,0:T(8,128)(2,1)S(1)}, bf16[16,5248]{1,0:T(8,128)(2,1)S(1)}, u32[]{:S(2)}, u32[]{:S(2)}) collective-permute-start(bf16[16,5248]{1,0:T(8,128)(2,1)S(1)} %get-tuple-element.41), channel_id=1, source_target_pairs={{0,24},{4,28},{8,0},{12,4},{16,8},{20,12},{24,16},{28,20},{1,25},{... | collective-permute-start | bytes 503816 | tf_op jit(solution)/shard_map/ppermute | solution.py:430
  65.4 6.4 %collective-permute-start.14 = (bf16[16,5248]{1,0:T(8,128)(2,1)S(1)}, bf16[16,5248]{1,0:T(8,128)(2,1)S(1)}, u32[]{:S(2)}, u32[]{:S(2)}) collective-permute-start(bf16[16,5248]{1,0:T(8,128)(2,1)S(1)} %get-tuple-element.42), channel_id=1, source_target_pairs={{0,28},{4,0},{8,4},{12,8},{16,12},{20,16},{24,20},{28,24},{1,29},{... | collective-permute-start | bytes 503816 | tf_op jit(solution)/shard_map/ppermute | solution.py:430

commit v15 on v14

--- a/solution.py
+++ b/solution.py
@@ -394,24 +394,32 @@
         lax.ppermute, axis_name="blk", perm=route(lambda i: -2 if i % 2 else 2)
     )
 
+    relay = functools.partial(
+        lax.ppermute,
+        axis_name="blk",
+        perm=route(lambda i: -1 if i == 1 else 1 if i == nblocks - 2 else -2 if i % 2 else 2),
+    )
+
     where = block_index[None].astype(jnp.int32)
     own_q, own_kv, swap_q, swap_kv = prepare(where, queries, keys, values)
     segs, need = survey(where, block_mask, segment_ids[None, :])
     other_kv = swap(swap_kv)
     ahead_own = ahead(own_kv)
     back_own = back(own_kv)
-    ready, back_own, swap_q, segs, need = lax.optimization_barrier(
-        (other_kv, back_own, swap_q, segs, need)
-    )
-    back_other = back(ready)
-    ahead_both = ahead(stack(other_kv, ahead_own))
+    back_other = relay(other_kv)
+    both = stack(other_kv, ahead_own)
+    both, back_own, swap_q, segs, need = lax.optimization_barrier(
+        (both, back_own, swap_q, segs, need)
+    )
     other_q = swap(swap_q)
-    back_far = back(back_other)
+    ahead_both = ahead(both)
     near = (own_kv, other_kv, ahead_own, back_own)
     near_numbers = (0, 1, 2, 3)
     fixed = (where, need, segs)
     own = attention(*fixed, (own_q,), (0,), near, near_numbers, None, False)
     other = attention(*fixed, (other_q,), (1,), near, near_numbers, None, False)
+    back_other, other, own = lax.optimization_barrier((back_other, other, own))
+    back_far = relay(back_other)
     far = (ahead_both, back_other)
     other = attention(*fixed, (other_q,), (1,), far, (4, 6, 5), other, True)
     other = swap(other)

time: 74.4 us -> 77.9 us (1.047)
  the two profiles are of different devices: /device:TPU:14 before, /device:TPU:0 now
where the time goes in v15:
time: 77.9 us; the launch traced here: 76.9 us
  starting transfers between devices  31.6 us (41%)
  waiting for transfers between devices  29.4 us (38%)
  Pallas kernels  14.2 us (18%)
  local copies, waits for them, and re-layouts  1.4 us (2%)
    ppermute x7, starting transfers between devices, per_device(): lax.ppermute(outgoing[d], 'blk', [(i, (i + d) % nblocks) for i in range(n...  15.1 us
    ppermute x7, waiting for transfers between devices, per_device(): lax.ppermute(outgoing[d], 'blk', [(i, (i + d) % nblocks) for i in range(n...  14.7 us
    pallas_call x4, Pallas kernels, attention(): pl.pallas_call(functools.partial(attention_kernel, kinds, numbers, rows_o...  8.46 us
    ppermute x1, starting transfers between devices, per_device(): other_kv = swap(swap_kv)  5.24 us
    ppermute x1, starting transfers between devices, per_device(): other_q = swap(swap_q)  3.5 us
    ppermute x1, starting transfers between devices, per_device(): back_own = back(own_kv)  3.47 us
    ppermute x1, waiting for transfers between devices, per_device(): back_far = relay(back_other)  3.25 us
    ppermute x1, waiting for transfers between devices, per_device(): ahead_both = ahead(both)  3.07 us
  transfers between devices with their start and end apart: 15, of which 10 were waited for; matrix products, arithmetic and copies ran while one was open for 0% of the time, Pallas kernels for 12%

profile of v15, /device:TPU:0, one launch (start us, length us, event | category | flops | bytes accessed | tf_op | source)
XLA Modules:
  0.0 76.9 jit_solution(84539843200327080)
XLA Ops:
  0.0 2.1 %shard_map.91 = (bf16[320,256]{1,0:T(8,128)(2,1)S(1)}, bf16[640,256]{1,0:T(8,128)(2,1)S(1)}, bf16[320,256]{1,0:T(8,128)(2,1)S(1)}, bf16[640,256]{1,0:T(8,128)(2,1)}) custom-call(s32[1]{0:T(128)} %bitcast.where_ref, bf16[256,640]{1,0:T(8,128)(2,1)} %q_hbm.1, bf16[256,640]{1,0:T(8,128)(2,1)} %k_hbm.1, bf16[256,640]{1,0:T(8,128)(2,1)} %v_hbm.1), custom_call_target="tpu_custom_call" | custom-call | tf_op jit(solution)/shard_map/pallas_call | solution.py:74
  3.4 5.2 %collective-permute-start = (bf16[640,256]{1,0:T(8,128)(2,1)}, bf16[640,256]{1,0:T(8,128)(2,1)S(1)}, u32[]{:S(2)}, u32[]{:S(2)}) collective-permute-start(bf16[640,256]{1,0:T(8,128)(2,1)} %get-tuple-element.27), channel_id=1, source_target_pairs={{0,4},{4,0},{8,12},{12,8},{16,20},{20,16},{24,28},{28,24},{1,5},{5... | collective-permute-start | bytes 983048 | tf_op jit(solution)/shard_map/ppermute | solution.py:406
  8.6 3.5 %collective-permute-start.2 = (bf16[640,256]{1,0:T(8,128)(2,1)S(1)}, bf16[640,256]{1,0:T(8,128)(2,1)S(1)}, u32[]{:S(2)}, u32[]{:S(2)}) collective-permute-start(bf16[640,256]{1,0:T(8,128)(2,1)S(1)} %get-tuple-element.28.refs_1_), channel_id=1, source_target_pairs={{0,8},{8,16},{12,4},{16,24},{20,12},{28,20},{1,9},{9,17},{13,5},{1... | collective-permute-start | bytes 983048 | tf_op jit(solution)/shard_map/ppermute | solution.py:408
  14.7 1.5 %collective-permute-done.refs_0_.refs_2_ = bf16[640,256]{1,0:T(8,128)(2,1)S(1)} collective-permute-done((bf16[640,256]{1,0:T(8,128)(2,1)}, bf16[640,256]{1,0:T(8,128)(2,1)S(1)}, u32[]{:S(2)}, u32[]{:S(2)}) %collective-permute-start) | collective-permute-done | bytes 327712 | tf_op jit(solution)/shard_map/ppermute | solution.py:406
  16.3 2.2 %collective-permute-done.2.refs_4_ = bf16[640,256]{1,0:T(8,128)(2,1)S(1)} collective-permute-done((bf16[640,256]{1,0:T(8,128)(2,1)S(1)}, bf16[640,256]{1,0:T(8,128)(2,1)S(1)}, u32[]{:S(2)}, u32[]{:S(2)}) %collective-permute-start.2) | collective-permute-done | bytes 327712 | tf_op jit(solution)/shard_map/ppermute | solution.py:408
  19.8 3.5 %collective-permute-start.5 = (bf16[320,256]{1,0:T(8,128)(2,1)S(1)}, bf16[320,256]{1,0:T(8,128)(2,1)S(1)}, u32[]{:S(2)}, u32[]{:S(2)}) collective-permute-start(bf16[320,256]{1,0:T(8,128)(2,1)S(1)} %get-tuple-element.36), channel_id=1, source_target_pairs={{0,4},{4,0},{8,12},{12,8},{16,20},{20,16},{24,28},{28,24},{1,5},{5... | collective-permute-start | bytes 491528 | tf_op jit(solution)/shard_map/ppermute | solution.py:414
  23.3 1.5 %collective-permute-start.4 = (bf16[640,256]{1,0:T(8,128)(2,1)S(1)}, bf16[640,256]{1,0:T(8,128)(2,1)S(1)}, u32[]{:S(2)}, u32[]{:S(2)}) collective-permute-start(bf16[640,256]{1,0:T(8,128)(2,1)S(1)} %collective-permute-done.refs_0_.refs_2_), channel_id=1, source_target_pairs={{0,8},{4,0},{8,16},{12,4},{16,24},{20,12},{24,28},{28,20},{1,9},{5... | collective-permute-start | bytes 983048 | tf_op jit(solution)/shard_map/ppermute | solution.py:409
  24.8 2.0 %shard_map.95.refs_4_ = f32[1,4,256,128]{3,2,1,0:T(8,128)S(1)} custom-call(s32[1]{0:T(128)} %bitcast.where_ref, s32[8,128]{1,0:T(8,128)S(1)} %get-tuple-element.32.need_ref, f32[1,2048]{1,0:T(1,128)S(1)} %get-tuple-element.33.seg_ref, bf16[320,256]{1,0:T(8,128)(2,1)S(1)} %get-tuple-element.34.refs_0_, bf16[640,256]{1,0:T(8,128)(2,1)S(1)} %get-tuple-element.28.refs_1_, ...), custom_call_target="tpu_custom_call" | custom-call | flops 2000000000 | bytes 2000000 | tf_op jit(solution)/shard_map/pallas_call | solution.py:234
  26.8 1.6 %collective-permute-done.5.refs_0_ = bf16[320,256]{1,0:T(8,128)(2,1)S(1)} collective-permute-done((bf16[320,256]{1,0:T(8,128)(2,1)S(1)}, bf16[320,256]{1,0:T(8,128)(2,1)S(1)}, u32[]{:S(2)}, u32[]{:S(2)}) %collective-permute-start.5) | collective-permute-done | bytes 163872 | tf_op jit(solution)/shard_map/ppermute | solution.py:414
  28.4 2.0 %shard_map.94.refs_3_ = f32[1,4,256,128]{3,2,1,0:T(8,128)S(1)} custom-call(s32[1]{0:T(128)} %bitcast.where_ref, s32[8,128]{1,0:T(8,128)S(1)} %get-tuple-element.32.need_ref, f32[1,2048]{1,0:T(1,128)S(1)} %get-tuple-element.33.seg_ref, bf16[320,256]{1,0:T(8,128)(2,1)S(1)} %collective-permute-done.5.refs_0_, bf16[640,256]{1,0:T(8,128)(2,1)S(1)} %get-tuple-element.28.refs_1_, ...), custom_call_target="tpu_custom_call" | custom-call | flops 2000000000 | bytes 2000000 | tf_op jit(solution)/shard_map/pallas_call | solution.py:234
  30.4 2.6 %collective-permute-done.4.refs_2_ = bf16[640,256]{1,0:T(8,128)(2,1)S(1)} collective-permute-done((bf16[640,256]{1,0:T(8,128)(2,1)S(1)}, bf16[640,256]{1,0:T(8,128)(2,1)S(1)}, u32[]{:S(2)}, u32[]{:S(2)}) %collective-permute-start.4) | collective-permute-done | bytes 327712 | tf_op jit(solution)/shard_map/ppermute | solution.py:409
  33.0 3.1 %collective-permute-done.3.refs_1_ = bf16[1280,256]{1,0:T(8,128)(2,1)S(1)} collective-permute-done((bf16[1280,256]{1,0:T(8,128)(2,1)S(1)}, bf16[1280,256]{1,0:T(8,128)(2,1)S(1)}, u32[]{:S(2)}, u32[]{:S(2)}) %collective-permute-start.3) | collective-permute-done | bytes 655392 | tf_op jit(solution)/shard_map/ppermute | solution.py:415
  36.1 2.3 %shard_map.97 = bf16[320,256]{1,0:T(8,128)(2,1)S(1)} custom-call(s32[1]{0:T(128)} %bitcast.where_ref, s32[8,128]{1,0:T(8,128)S(1)} %get-tuple-element.32.need_ref, f32[1,2048]{1,0:T(1,128)S(1)} %get-tuple-element.33.seg_ref, bf16[320,256]{1,0:T(8,128)(2,1)S(1)} %collective-permute-done.5.refs_0_, bf16[1280,256]{1,0:T(8,128)(2,1)S(1)} %collective-permute-done.3.refs_1_, ...), custom_call_target="tpu_custom_call" | custom-call | flops 2000000000 | bytes 2000000 | tf_op jit(solution)/shard_map/pallas_call | solution.py:234
  38.6 3.3 %collective-permute-done.6.refs_3_ = bf16[640,256]{1,0:T(8,128)(2,1)S(1)} collective-permute-done((bf16[640,256]{1,0:T(8,128)(2,1)S(1)}, bf16[640,256]{1,0:T(8,128)(2,1)S(1)}, u32[]{:S(2)}, u32[]{:S(2)}) %collective-permute-start.6) | collective-permute-done | bytes 327712 | tf_op jit(solution)/shard_map/ppermute | solution.py:422
  41.8 2.2 %shard_map.96.own_ref = bf16[320,256]{1,0:T(8,128)(2,1)S(1)} custom-call(s32[1]{0:T(128)} %bitcast.where_ref, s32[8,128]{1,0:T(8,128)S(1)} %get-tuple-element.32.need_ref, f32[1,2048]{1,0:T(1,128)S(1)} %get-tuple-element.33.seg_ref, bf16[320,256]{1,0:T(8,128)(2,1)S(1)} %get-tuple-element.34.refs_0_, bf16[1280,256]{1,0:T(8,128)(2,1)S(1)} %collective-permute-done.3.refs_1_, ...), custom_call_target="tpu_custom_call" | custom-call | flops 2000000000 | bytes 2000000 | tf_op jit(solution)/shard_map/pallas_call | solution.py:234
  44.0 1.5 %shard_map.98 = (bf16[16,5248]{1,0:T(8,128)(2,1)S(1)}, bf16[16,5248]{1,0:T(8,128)(2,1)S(1)}, bf16[16,5248]{1,0:T(8,128)(2,1)S(1)}, bf16[16,5248]{1,0:T(8,128)(2,...) custom-call(s32[1]{0:T(128)} %bitcast.where_ref, ...), custom_call_target="tpu_custom_call" | custom-call | tf_op jit(solution)/shard_map/pallas_call | solution.py:324
  45.5 1.7 %collective-permute-start.10 = (bf16[16,5248]{1,0:T(8,128)(2,1)S(1)}, bf16[16,5248]{1,0:T(8,128)(2,1)S(1)}, u32[]{:S(2)}, u32[]{:S(2)}) collective-permute-start(bf16[16,5248]{1,0:T(8,128)(2,1)S(1)} %get-tuple-element.44), channel_id=1, source_target_pairs={{0,12},{4,16},{8,20},{12,24},{16,28},{20,0},{24,4},{28,8},{1,13},{... | collective-permute-start | bytes 503816 | tf_op jit(solution)/shard_map/ppermute | solution.py:438
  47.2 1.9 %collective-permute-start.11 = (bf16[16,5248]{1,0:T(8,128)(2,1)S(1)}, bf16[16,5248]{1,0:T(8,128)(2,1)S(1)}, u32[]{:S(2)}, u32[]{:S(2)}) collective-permute-start(bf16[16,5248]{1,0:T(8,128)(2,1)S(1)} %get-tuple-element.45), channel_id=1, source_target_pairs={{0,16},{4,20},{8,24},{12,28},{16,0},{20,4},{24,8},{28,12},{1,17},{... | collective-permute-start | bytes 503816 | tf_op jit(solution)/shard_map/ppermute | solution.py:438
  49.1 1.5 %collective-permute-start.12 = (bf16[16,5248]{1,0:T(8,128)(2,1)S(1)}, bf16[16,5248]{1,0:T(8,128)(2,1)S(1)}, u32[]{:S(2)}, u32[]{:S(2)}) collective-permute-start(bf16[16,5248]{1,0:T(8,128)(2,1)S(1)} %get-tuple-element.46), channel_id=1, source_target_pairs={{0,20},{4,24},{8,28},{12,0},{16,4},{20,8},{24,12},{28,16},{1,21},{... | collective-permute-start | bytes 503816 | tf_op jit(solution)/shard_map/ppermute | solution.py:438
  50.6 2.8 %collective-permute-start.13 = (bf16[16,5248]{1,0:T(8,128)(2,1)S(1)}, bf16[16,5248]{1,0:T(8,128)(2,1)S(1)}, u32[]{:S(2)}, u32[]{:S(2)}) collective-permute-start(bf16[16,5248]{1,0:T(8,128)(2,1)S(1)} %get-tuple-element.47), channel_id=1, source_target_pairs={{0,24},{4,28},{8,0},{12,4},{16,8},{20,12},{24,16},{28,20},{1,25},{... | collective-permute-start | bytes 503816 | tf_op jit(solution)/shard_map/ppermute | solution.py:438
  53.3 4.9 %collective-permute-done.10.refs_3_ = bf16[16,5248]{1,0:T(8,128)(2,1)S(1)} collective-permute-done((bf16[16,5248]{1,0:T(8,128)(2,1)S(1)}, bf16[16,5248]{1,0:T(8,128)(2,1)S(1)}, u32[]{:S(2)}, u32[]{:S(2)}) %collective-permute-start.10) | collective-permute-done | bytes 167968 | tf_op jit(solution)/shard_map/ppermute | solution.py:438
  58.3 3.5 %collective-permute-done.11.refs_4_ = bf16[16,5248]{1,0:T(8,128)(2,1)S(1)} collective-permute-done((bf16[16,5248]{1,0:T(8,128)(2,1)S(1)}, bf16[16,5248]{1,0:T(8,128)(2,1)S(1)}, u32[]{:S(2)}, u32[]{:S(2)}) %collective-permute-start.11) | collective-permute-done | bytes 167968 | tf_op jit(solution)/shard_map/ppermute | solution.py:438
  61.8 7.3 %collective-permute-start.9 = (bf16[16,5248]{1,0:T(8,128)(2,1)S(1)}, bf16[16,5248]{1,0:T(8,128)(2,1)S(1)}, u32[]{:S(2)}, u32[]{:S(2)}) collective-permute-start(bf16[16,5248]{1,0:T(8,128)(2,1)S(1)} %get-tuple-element.43), channel_id=1, source_target_pairs={{0,8},{4,12},{8,16},{12,20},{16,24},{20,28},{24,0},{28,4},{1,9},{5... | collective-permute-start | bytes 503816 | tf_op jit(solution)/shard_map/ppermute | solution.py:438
  69.1 6.2 %collective-permute-done.9.refs_2_ = bf16[16,5248]{1,0:T(8,128)(2,1)S(1)} collective-permute-done((bf16[16,5248]{1,0:T(8,128)(2,1)S(1)}, bf16[16,5248]{1,0:T(8,128)(2,1)S(1)}, u32[]{:S(2)}, u32[]{:S(2)}) %collective-permute-start.9) | collective-permute-done | bytes 167968 | tf_op jit(solution)/shard_map/ppermute | solution.py:438
  (27 shorter events, 6.8 us)
Async XLA Ops:
  2.1 12.6 %collective-permute-start.1 = (bf16[640,256]{1,0:T(8,128)(2,1)S(1)}, bf16[640,256]{1,0:T(8,128)(2,1)S(1)}, u32[]{:S(2)}, u32[]{:S(2)}) collective-permute-start(bf16[640,256]{1,0:T(8,128)(2,1)S(1)} %get-tuple-element.28.refs_1_), channel_id=1, source_target_pairs={{4,12},{8,0},{12,20},{16,8},{20,28},{24,16},{5,13},{9,1},{13,21},{... | collective-permute-start | bytes 983048 | tf_op jit(solution)/shard_map/ppermute | solution.py:407
  3.4 12.9 %collective-permute-start = (bf16[640,256]{1,0:T(8,128)(2,1)}, bf16[640,256]{1,0:T(8,128)(2,1)S(1)}, u32[]{:S(2)}, u32[]{:S(2)}) collective-permute-start(bf16[640,256]{1,0:T(8,128)(2,1)} %get-tuple-element.27), channel_id=1, source_target_pairs={{0,4},{4,0},{8,12},{12,8},{16,20},{20,16},{24,28},{28,24},{1,5},{5... | collective-permute-start | bytes 983048 | tf_op jit(solution)/shard_map/ppermute | solution.py:406
  8.6 9.9 %collective-permute-start.2 = (bf16[640,256]{1,0:T(8,128)(2,1)S(1)}, bf16[640,256]{1,0:T(8,128)(2,1)S(1)}, u32[]{:S(2)}, u32[]{:S(2)}) collective-permute-start(bf16[640,256]{1,0:T(8,128)(2,1)S(1)} %get-tuple-element.28.refs_1_), channel_id=1, source_target_pairs={{0,8},{8,16},{12,4},{16,24},{20,12},{28,20},{1,9},{9,17},{13,5},{1... | collective-permute-start | bytes 983048 | tf_op jit(solution)/shard_map/ppermute | solution.py:408
  12.1 0.7 copy-start.2
  12.8 0.7 copy-start.3
  18.5 17.6 %collective-permute-start.3 = (bf16[1280,256]{1,0:T(8,128)(2,1)S(1)}, bf16[1280,256]{1,0:T(8,128)(2,1)S(1)}, u32[]{:S(2)}, u32[]{:S(2)}) collective-permute-start(bf16[1280,256]{1,0:T(8,128)(2,1)S(1)} %shard_map.92), channel_id=1, source_target_pairs={{4,12},{8,0},{12,20},{16,8},{20,28},{24,16},{5,13},{9,1},{13,21},{... | collective-permute-start | bytes 1966088 | tf_op jit(solution)/shard_map/ppermute | solution.py:415
  19.8 8.6 %collective-permute-start.5 = (bf16[320,256]{1,0:T(8,128)(2,1)S(1)}, bf16[320,256]{1,0:T(8,128)(2,1)S(1)}, u32[]{:S(2)}, u32[]{:S(2)}) collective-permute-start(bf16[320,256]{1,0:T(8,128)(2,1)S(1)} %get-tuple-element.36), channel_id=1, source_target_pairs={{0,4},{4,0},{8,12},{12,8},{16,20},{20,16},{24,28},{28,24},{1,5},{5... | collective-permute-start | bytes 491528 | tf_op jit(solution)/shard_map/ppermute | solution.py:414
  23.3 9.8 %collective-permute-start.4 = (bf16[640,256]{1,0:T(8,128)(2,1)S(1)}, bf16[640,256]{1,0:T(8,128)(2,1)S(1)}, u32[]{:S(2)}, u32[]{:S(2)}) collective-permute-start(bf16[640,256]{1,0:T(8,128)(2,1)S(1)} %collective-permute-done.refs_0_.refs_2_), channel_id=1, source_target_pairs={{0,8},{4,0},{8,16},{12,4},{16,24},{20,12},{24,28},{28,20},{1,9},{5... | collective-permute-start | bytes 983048 | tf_op jit(solution)/shard_map/ppermute | solution.py:409
  33.0 8.8 %collective-permute-start.6 = (bf16[640,256]{1,0:T(8,128)(2,1)S(1)}, bf16[640,256]{1,0:T(8,128)(2,1)S(1)}, u32[]{:S(2)}, u32[]{:S(2)}) collective-permute-start(bf16[640,256]{1,0:T(8,128)(2,1)S(1)} %collective-permute-done.4.refs_2_), channel_id=1, source_target_pairs={{0,8},{4,0},{8,16},{12,4},{16,24},{20,12},{24,28},{28,20},{1,9},{5... | collective-permute-start | bytes 983048 | tf_op jit(solution)/shard_map/ppermute | solution.py:422
  38.4 5.6 %copy-start = (bf16[640,1280]{1,0:T(8,128)(2,1)S(1)}, bf16[640,1280]{1,0:T(8,128)(2,1)}, u32[]{:S(2)}) copy-start(bf16[640,1280]{1,0:T(8,128)(2,1)} %weight_ref.1) | copy-start | bytes 4915204
  38.4 5.6 %copy-start.1 = (bf16[256,1280]{1,0:T(8,128)(2,1)S(1)}, bf16[256,1280]{1,0:T(8,128)(2,1)}, u32[]{:S(2)}) copy-start(bf16[256,1280]{1,0:T(8,128)(2,1)} %tokens_ref.1) | copy-start | bytes 1966084
  38.5 5.6 %copy-start.4 = (s32[64]{0:T(128)S(1)}, s32[64]{0:T(128)}, u32[]{:S(2)}) copy-start(s32[64]{0:T(128)} %param.16) | copy-start | bytes 772
  38.5 5.6 %copy-start.5 = (s32[64]{0:T(128)S(1)}, s32[64]{0:T(128)}, u32[]{:S(2)}) copy-start(s32[64]{0:T(128)} %param.17) | copy-start | bytes 772
  38.5 5.5 %collective-permute-start.7 = (bf16[320,256]{1,0:T(8,128)(2,1)S(1)}, bf16[320,256]{1,0:T(8,128)(2,1)S(1)}, u32[]{:S(2)}, u32[]{:S(2)}) collective-permute-start(bf16[320,256]{1,0:T(8,128)(2,1)S(1)} %shard_map.97), channel_id=1, source_target_pairs={{0,4},{4,0},{8,12},{12,8},{16,20},{20,16},{24,28},{28,24},{1,5},{5... | collective-permute-start | bytes 491528 | tf_op jit(solution)/shard_map/ppermute | solution.py:425
  45.5 12.8 %collective-permute-start.10 = (bf16[16,5248]{1,0:T(8,128)(2,1)S(1)}, bf16[16,5248]{1,0:T(8,128)(2,1)S(1)}, u32[]{:S(2)}, u32[]{:S(2)}) collective-permute-start(bf16[16,5248]{1,0:T(8,128)(2,1)S(1)} %get-tuple-element.44), channel_id=1, source_target_pairs={{0,12},{4,16},{8,20},{12,24},{16,28},{20,0},{24,4},{28,8},{1,13},{... | collective-permute-start | bytes 503816 | tf_op jit(solution)/shard_map/ppermute | solution.py:438
  47.2 14.6 %collective-permute-start.11 = (bf16[16,5248]{1,0:T(8,128)(2,1)S(1)}, bf16[16,5248]{1,0:T(8,128)(2,1)S(1)}, u32[]{:S(2)}, u32[]{:S(2)}) collective-permute-start(bf16[16,5248]{1,0:T(8,128)(2,1)S(1)} %get-tuple-element.45), channel_id=1, source_target_pairs={{0,16},{4,20},{8,24},{12,28},{16,0},{20,4},{24,8},{28,12},{1,17},{... | collective-permute-start | bytes 503816 | tf_op jit(solution)/shard_map/ppermute | solution.py:438
  49.1 20.0 %collective-permute-start.12 = (bf16[16,5248]{1,0:T(8,128)(2,1)S(1)}, bf16[16,5248]{1,0:T(8,128)(2,1)S(1)}, u32[]{:S(2)}, u32[]{:S(2)}) collective-permute-start(bf16[16,5248]{1,0:T(8,128)(2,1)S(1)} %get-tuple-element.46), channel_id=1, source_target_pairs={{0,20},{4,24},{8,28},{12,0},{16,4},{20,8},{24,12},{28,16},{1,21},{... | collective-permute-start | bytes 503816 | tf_op jit(solution)/shard_map/ppermute | solution.py:438
  50.6 18.5 %collective-permute-start.13 = (bf16[16,5248]{1,0:T(8,128)(2,1)S(1)}, bf16[16,5248]{1,0:T(8,128)(2,1)S(1)}, u32[]{:S(2)}, u32[]{:S(2)}) collective-permute-start(bf16[16,5248]{1,0:T(8,128)(2,1)S(1)} %get-tuple-element.47), channel_id=1, source_target_pairs={{0,24},{4,28},{8,0},{12,4},{16,8},{20,12},{24,16},{28,20},{1,25},{... | collective-permute-start | bytes 503816 | tf_op jit(solution)/shard_map/ppermute | solution.py:438
  53.3 15.7 %collective-permute-start.14 = (bf16[16,5248]{1,0:T(8,128)(2,1)S(1)}, bf16[16,5248]{1,0:T(8,128)(2,1)S(1)}, u32[]{:S(2)}, u32[]{:S(2)}) collective-permute-start(bf16[16,5248]{1,0:T(8,128)(2,1)S(1)} %get-tuple-element.48), channel_id=1, source_target_pairs={{0,28},{4,0},{8,4},{12,8},{16,12},{20,16},{24,20},{28,24},{1,29},{... | collective-permute-start | bytes 503816 | tf_op jit(solution)/shard_map/ppermute | solution.py:438
  58.3 10.8 %collective-permute-start.8 = (bf16[16,5248]{1,0:T(8,128)(2,1)S(1)}, bf16[16,5248]{1,0:T(8,128)(2,1)S(1)}, u32[]{:S(2)}, u32[]{:S(2)}) collective-permute-start(bf16[16,5248]{1,0:T(8,128)(2,1)S(1)} %get-tuple-element.42), channel_id=1, source_target_pairs={{0,4},{4,8},{8,12},{12,16},{16,20},{20,24},{24,28},{28,0},{1,5},{5... | collective-permute-start | bytes 503816 | tf_op jit(solution)/shard_map/ppermute | solution.py:438
  61.8 13.6 %collective-permute-start.9 = (bf16[16,5248]{1,0:T(8,128)(2,1)S(1)}, bf16[16,5248]{1,0:T(8,128)(2,1)S(1)}, u32[]{:S(2)}, u32[]{:S(2)}) collective-permute-start(bf16[16,5248]{1,0:T(8,128)(2,1)S(1)} %get-tuple-element.43), channel_id=1, source_target_pairs={{0,8},{4,12},{8,16},{12,20},{16,24},{20,28},{24,0},{28,4},{1,9},{5... | collective-permute-start | bytes 503816 | tf_op jit(solution)/shard_map/ppermute | solution.py:438

commit v16 on v14

--- a/solution.py
+++ b/solution.py
@@ -269,14 +269,17 @@
 
 
 def project_kernel(
-    pair_rows, where_ref, owners_ref, offsets_ref, own_ref, other_ref, weight_ref, tokens_ref, *outs
+    pair_rows, order, where_ref, owners_ref, offsets_ref, own_ref, other_ref, weight_ref, tokens_ref, *outs
 ):
     piece = outs[0].shape[0]
     slots = piece * len(outs)
     rows, width = tokens_ref.shape
     mrows = rows // 4
     capacity = 2 * mrows
-    owner = jnp.broadcast_to(owners_ref[...].astype(jnp.float32), (mrows, mrows))
+    owner = owners_ref[...]
+    if len(outs) > 1:
+        owner = owner ^ where_ref[0]
+    owner = jnp.broadcast_to(owner.astype(jnp.float32), (mrows, mrows))
     earlier = lax.broadcasted_iota(jnp.int32, (mrows, mrows), 0)
     later = lax.broadcasted_iota(jnp.int32, (mrows, mrows), 1)
     column = jnp.sum(jnp.where(earlier == later, owner, 0.0), axis=1, keepdims=True)
@@ -299,30 +302,27 @@
             preferred_element_type=jnp.float32,
         )
     hidden = hidden.astype(jnp.bfloat16)
-    place = meta[:1]
-    if len(outs) > 1:
-        place = place - (where_ref[0] * pair_rows).astype(jnp.float32)
-        place = jnp.where(place < 0, place + slots, place)
     slot = lax.broadcasted_iota(jnp.int32, (slots, rows), 0).astype(jnp.float32)
     quarter = lax.broadcasted_iota(jnp.int32, (1, rows), 1) % 4
     for j in range(4):
-        mine = jnp.where(quarter == j, place, -1.0) == slot
+        mine = jnp.where(quarter == j, meta[:1], -1.0) == slot
         if j == 0:
             offset = jnp.where(mine, meta[1:2] - capacity, 0.0)
             offset = capacity + jnp.sum(offset, axis=1, keepdims=True)
             offset = jnp.broadcast_to(offset, (slots, 128)).astype(jnp.bfloat16)
-            for d, out in enumerate(outs):
+            for d, out in zip(order, outs):
                 out[:, 4 * width :] = offset[d * piece : (d + 1) * piece]
         pick = jnp.where(mine, 1.0, 0.0).astype(jnp.bfloat16)
         picked = jnp.dot(pick, hidden, preferred_element_type=jnp.float32).astype(jnp.bfloat16)
-        for d, out in enumerate(outs):
+        for d, out in zip(order, outs):
             out[:, j * width : (j + 1) * width] = picked[d * piece : (d + 1) * piece]
 
 
-def project(where, owners, offsets, own, other, out_weight, tokens, pieces, slots, pair_rows):
+def project(where, owners, offsets, own, other, out_weight, tokens, order, slots, pair_rows):
     rows, width = tokens.shape
-    return pl.pallas_call(
-        functools.partial(project_kernel, pair_rows),
+    pieces = len(order)
+    return pl.pallas_call(
+        functools.partial(project_kernel, pair_rows, order),
         out_shape=[jax.ShapeDtypeStruct((slots // pieces, 4 * width + 128), jnp.bfloat16)] * pieces,
         in_specs=[smem()] + [vmem()] * 6,
         out_specs=[vmem()] * pieces,
@@ -394,6 +394,12 @@
         lax.ppermute, axis_name="blk", perm=route(lambda i: -2 if i % 2 else 2)
     )
 
+    relay = functools.partial(
+        lax.ppermute,
+        axis_name="blk",
+        perm=route(lambda i: -1 if i == 1 else 1 if i == nblocks - 2 else -2 if i % 2 else 2),
+    )
+
     where = block_index[None].astype(jnp.int32)
     own_q, own_kv, swap_q, swap_kv = prepare(where, queries, keys, values)
     segs, need = survey(where, block_mask, segment_ids[None, :])
@@ -403,33 +409,41 @@
     ready, back_own, swap_q, segs, need = lax.optimization_barrier(
         (other_kv, back_own, swap_q, segs, need)
     )
-    back_other = back(ready)
+    back_other = relay(ready)
     ahead_both = ahead(stack(other_kv, ahead_own))
     other_q = swap(swap_q)
-    back_far = back(back_other)
     near = (own_kv, other_kv, ahead_own, back_own)
     near_numbers = (0, 1, 2, 3)
     fixed = (where, need, segs)
     own = attention(*fixed, (own_q,), (0,), near, near_numbers, None, False)
     other = attention(*fixed, (other_q,), (1,), near, near_numbers, None, False)
+    back_other, other = lax.optimization_barrier((back_other, other))
+    back_far = relay(back_other)
     far = (ahead_both, back_other)
     other = attention(*fixed, (other_q,), (1,), far, (4, 6, 5), other, True)
     other = swap(other)
     far = (ahead_both, back_other, back_far)
     own = attention(*fixed, (own_q,), (0,), far, (4, 6, 5, 7), own, True)
 
-    pieces = nblocks if nblocks <= 8 else 1
+    order = tuple(range(nblocks)) if nblocks in (4, 8) else (0,)
     outgoing = project(
         where, owners[None, :], offsets[None, :], own, other, out_weight, tokens,
-        pieces, slots, pair_rows,
-    )
-    if pieces > 1:
-        arrived = [outgoing[0]] + [None] * (nblocks - 1)
-        order = sorted(range(1, nblocks), key=lambda d: (min(d, nblocks - d) == 2, d))
-        for d in order:
-            arrived[d] = lax.ppermute(
-                outgoing[d], "blk", [(i, (i + d) % nblocks) for i in range(nblocks)]
-            )
+        order, slots, pair_rows,
+    )
+    if len(order) > 1:
+        arrived = list(outgoing)
+
+        def cross(d):
+            arrived[d] = lax.ppermute(arrived[d], "blk", [(i, i ^ d) for i in range(nblocks)])
+
+        short, *late = range(nblocks // 2 - 1, 0, -1)
+        for d in (*range(nblocks // 2, nblocks), short):
+            cross(d)
+        group = lax.optimization_barrier([arrived[d] for d in (short, *late)])
+        for d, block in zip((short, *late), group):
+            arrived[d] = block
+        for d in late:
+            cross(d)
     else:
         arrived = [lax.all_to_all(outgoing[0], "blk", split_axis=0, concat_axis=0, tiled=True)]
     return place(arrived, capacity, 4 * width)

time: 74.4 us -> 73.4 us (0.987)
  waiting for transfers between devices: 31.9 us -> 30.7 us
  starting transfers between devices: 27 us -> 27.8 us
    ppermute x9, waiting for transfers between devices: 25.5 us -> 17.9 us  [the longest x7 16.9 us: cross(): lax.ppermute(arrived[d], 'blk', [(i, i ^ d) for i in range(nblocks)])]
    ppermute x1, waiting for transfers between devices: 0.01 us -> 4.77 us  [per_device(): other_q = swap(swap_q)]
    ppermute x9, starting transfers between devices: 13.5 us -> 15.9 us  [the longest x7 14.2 us: cross(): lax.ppermute(arrived[d], 'blk', [(i, i ^ d) for i in range(nblocks)])]
    ppermute x1, starting transfers between devices: 1.55 us -> 0.46 us  [per_device(): other_q = swap(swap_q)]
    ppermute x1, waiting for transfers between devices: 0.01 us -> 1.09 us  [per_device(): ahead_both = ahead(stack(other_kv, ahead_own))]
  transfers between devices with their start and end apart: 15 -> 15, of which waited for: 11 -> 9; matrix products, arithmetic and copies ran while one was open for 0% -> 0% of each run, Pallas kernels for 12% -> 12%
where the time goes in v16:
time: 73.4 us; the launch traced here: 73 us
  waiting for transfers between devices  30.7 us (42%)
  starting transfers between devices  27.8 us (38%)
  Pallas kernels  14.1 us (19%)
    ppermute x7, waiting for transfers between devices, cross(): lax.ppermute(arrived[d], 'blk', [(i, i ^ d) for i in range(nblocks)])  16.9 us
    ppermute x7, starting transfers between devices, cross(): lax.ppermute(arrived[d], 'blk', [(i, i ^ d) for i in range(nblocks)])  14.2 us
    pallas_call x4, Pallas kernels, attention(): pl.pallas_call(functools.partial(attention_kernel, kinds, numbers, rows_o...  8.29 us
    ppermute x1, waiting for transfers between devices, per_device(): other_q = swap(swap_q)  4.77 us
    ppermute x1, starting transfers between devices, per_device(): ahead_both = ahead(stack(other_kv, ahead_own))  3.48 us
    ppermute x1, starting transfers between devices, per_device(): ahead_own = ahead(own_kv)  3.47 us
    ppermute x1, waiting for transfers between devices, per_device(): other_kv = swap(swap_kv)  3.29 us
    ppermute x1, starting transfers between devices, per_device(): back_own = back(own_kv)  2.37 us
  transfers between devices with their start and end apart: 15, of which 9 were waited for; matrix products, arithmetic and copies ran while one was open for 0% of the time, Pallas kernels for 12%

profile of v16, /device:TPU:14, one launch (start us, length us, event | category | flops | bytes accessed | tf_op | source)
XLA Modules:
  0.0 73.0 jit_solution(7442868716851046496)
XLA Ops:
  0.0 2.1 %shard_map.91 = (bf16[320,256]{1,0:T(8,128)(2,1)S(1)}, bf16[640,256]{1,0:T(8,128)(2,1)S(1)}, bf16[320,256]{1,0:T(8,128)(2,1)S(1)}, bf16[640,256]{1,0:T(8,128)(2,1)}) custom-call(s32[1]{0:T(128)} %bitcast.where_ref, bf16[256,640]{1,0:T(8,128)(2,1)} %q_hbm.1, bf16[256,640]{1,0:T(8,128)(2,1)} %k_hbm.1, bf16[256,640]{1,0:T(8,128)(2,1)} %v_hbm.1), custom_call_target="tpu_custom_call" | custom-call | tf_op jit(solution)/shard_map/pallas_call | solution.py:74
  2.7 3.5 %collective-permute-start.2 = (bf16[640,256]{1,0:T(8,128)(2,1)S(1)}, bf16[640,256]{1,0:T(8,128)(2,1)S(1)}, u32[]{:S(2)}, u32[]{:S(2)}) collective-permute-start(bf16[640,256]{1,0:T(8,128)(2,1)S(1)} %get-tuple-element.30.refs_1_), channel_id=1, source_target_pairs={{4,12},{8,0},{12,20},{16,8},{20,28},{24,16},{5,13},{9,1},{13,21},{... | collective-permute-start | bytes 983048 | tf_op jit(solution)/shard_map/ppermute | solution.py:407
  6.2 2.4 %collective-permute-start.1 = (bf16[640,256]{1,0:T(8,128)(2,1)S(1)}, bf16[640,256]{1,0:T(8,128)(2,1)S(1)}, u32[]{:S(2)}, u32[]{:S(2)}) collective-permute-start(bf16[640,256]{1,0:T(8,128)(2,1)S(1)} %get-tuple-element.30.refs_1_), channel_id=1, source_target_pairs={{0,8},{8,16},{12,4},{16,24},{20,12},{28,20},{1,9},{9,17},{13,5},{1... | collective-permute-start | bytes 983048 | tf_op jit(solution)/shard_map/ppermute | solution.py:408
  8.5 3.3 %collective-permute-done.refs_0_.refs_2_ = bf16[640,256]{1,0:T(8,128)(2,1)S(1)} collective-permute-done((bf16[640,256]{1,0:T(8,128)(2,1)}, bf16[640,256]{1,0:T(8,128)(2,1)S(1)}, u32[]{:S(2)}, u32[]{:S(2)}) %collective-permute-start) | collective-permute-done | bytes 327712 | tf_op jit(solution)/shard_map/ppermute | solution.py:406
  11.8 1.9 %collective-permute-done.2.refs_1_.refs_3_ = bf16[640,256]{1,0:T(8,128)(2,1)S(1)} collective-permute-done((bf16[640,256]{1,0:T(8,128)(2,1)S(1)}, bf16[640,256]{1,0:T(8,128)(2,1)S(1)}, u32[]{:S(2)}, u32[]{:S(2)}) %collective-permute-start.2) | collective-permute-done | bytes 327712 | tf_op jit(solution)/shard_map/ppermute | solution.py:407
  13.8 3.5 %collective-permute-start.3 = (bf16[1280,256]{1,0:T(8,128)(2,1)S(1)}, bf16[1280,256]{1,0:T(8,128)(2,1)S(1)}, u32[]{:S(2)}, u32[]{:S(2)}) collective-permute-start(bf16[1280,256]{1,0:T(8,128)(2,1)S(1)} %shard_map.93), channel_id=1, source_target_pairs={{4,12},{8,0},{12,20},{16,8},{20,28},{24,16},{5,13},{9,1},{13,21},{... | collective-permute-start | bytes 1966088 | tf_op jit(solution)/shard_map/ppermute | solution.py:413
  18.7 4.8 %collective-permute-done.5.refs_0_ = bf16[320,256]{1,0:T(8,128)(2,1)S(1)} collective-permute-done((bf16[320,256]{1,0:T(8,128)(2,1)S(1)}, bf16[320,256]{1,0:T(8,128)(2,1)S(1)}, u32[]{:S(2)}, u32[]{:S(2)}) %collective-permute-start.5) | collective-permute-done | bytes 163872 | tf_op jit(solution)/shard_map/ppermute | solution.py:414
  23.4 2.0 %shard_map.94.refs_3_ = f32[1,4,256,128]{3,2,1,0:T(8,128)S(1)} custom-call(s32[1]{0:T(128)} %bitcast.where_ref, s32[8,128]{1,0:T(8,128)S(1)} %get-tuple-element.34.need_ref, f32[1,2048]{1,0:T(1,128)S(1)} %get-tuple-element.35.seg_ref, bf16[320,256]{1,0:T(8,128)(2,1)S(1)} %collective-permute-done.5.refs_0_, bf16[640,256]{1,0:T(8,128)(2,1)S(1)} %get-tuple-element.30.refs_1_, ...), custom_call_target="tpu_custom_call" | custom-call | flops 2000000000 | bytes 2000000 | tf_op jit(solution)/shard_map/pallas_call | solution.py:234
  26.4 1.5 %collective-permute-start.6 = (bf16[640,256]{1,0:T(8,128)(2,1)S(1)}, bf16[640,256]{1,0:T(8,128)(2,1)S(1)}, u32[]{:S(2)}, u32[]{:S(2)}) collective-permute-start(bf16[640,256]{1,0:T(8,128)(2,1)S(1)} %collective-permute-done.4.refs_2_), channel_id=1, source_target_pairs={{0,8},{4,0},{8,16},{12,4},{16,24},{20,12},{24,28},{28,20},{1,9},{5... | collective-permute-start | bytes 983048 | tf_op jit(solution)/shard_map/ppermute | solution.py:421
  27.9 2.0 %shard_map.95.refs_4_ = f32[1,4,256,128]{3,2,1,0:T(8,128)S(1)} custom-call(s32[1]{0:T(128)} %bitcast.where_ref, s32[8,128]{1,0:T(8,128)S(1)} %get-tuple-element.34.need_ref, f32[1,2048]{1,0:T(1,128)S(1)} %get-tuple-element.35.seg_ref, bf16[320,256]{1,0:T(8,128)(2,1)S(1)} %get-tuple-element.36.refs_0_, bf16[640,256]{1,0:T(8,128)(2,1)S(1)} %get-tuple-element.30.refs_1_, ...), custom_call_target="tpu_custom_call" | custom-call | flops 2000000000 | bytes 2000000 | tf_op jit(solution)/shard_map/pallas_call | solution.py:234
  31.0 2.3 %shard_map.97 = bf16[320,256]{1,0:T(8,128)(2,1)S(1)} custom-call(s32[1]{0:T(128)} %bitcast.where_ref, s32[8,128]{1,0:T(8,128)S(1)} %get-tuple-element.34.need_ref, f32[1,2048]{1,0:T(1,128)S(1)} %get-tuple-element.35.seg_ref, bf16[320,256]{1,0:T(8,128)(2,1)S(1)} %collective-permute-done.5.refs_0_, bf16[1280,256]{1,0:T(8,128)(2,1)S(1)} %collective-permute-done.3.refs_1_, ...), custom_call_target="tpu_custom_call" | custom-call | flops 2000000000 | bytes 2000000 | tf_op jit(solution)/shard_map/pallas_call | solution.py:234
  33.3 1.6 %collective-permute-start.7 = (bf16[320,256]{1,0:T(8,128)(2,1)S(1)}, bf16[320,256]{1,0:T(8,128)(2,1)S(1)}, u32[]{:S(2)}, u32[]{:S(2)}) collective-permute-start(bf16[320,256]{1,0:T(8,128)(2,1)S(1)} %shard_map.97), channel_id=1, source_target_pairs={{0,4},{4,0},{8,12},{12,8},{16,20},{20,16},{24,28},{28,24},{1,5},{5... | collective-permute-start | bytes 491528 | tf_op jit(solution)/shard_map/ppermute | solution.py:424
  34.9 2.0 %shard_map.96.own_ref = bf16[320,256]{1,0:T(8,128)(2,1)S(1)} custom-call(s32[1]{0:T(128)} %bitcast.where_ref, s32[8,128]{1,0:T(8,128)S(1)} %get-tuple-element.34.need_ref, f32[1,2048]{1,0:T(1,128)S(1)} %get-tuple-element.35.seg_ref, bf16[320,256]{1,0:T(8,128)(2,1)S(1)} %get-tuple-element.36.refs_0_, bf16[1280,256]{1,0:T(8,128)(2,1)S(1)} %collective-permute-done.3.refs_1_, ...), custom_call_target="tpu_custom_call" | custom-call | flops 2000000000 | bytes 2000000 | tf_op jit(solution)/shard_map/pallas_call | solution.py:234
  36.9 1.8 %collective-permute-done.7.other_ref = bf16[320,256]{1,0:T(8,128)(2,1)S(1)} collective-permute-done((bf16[320,256]{1,0:T(8,128)(2,1)S(1)}, bf16[320,256]{1,0:T(8,128)(2,1)S(1)}, u32[]{:S(2)}, u32[]{:S(2)}) %collective-permute-start.7) | collective-permute-done | bytes 163872 | tf_op jit(solution)/shard_map/ppermute | solution.py:424
  38.8 1.5 %shard_map.98 = (bf16[16,5248]{1,0:T(8,128)(2,1)S(1)}, bf16[16,5248]{1,0:T(8,128)(2,1)S(1)}, bf16[16,5248]{1,0:T(8,128)(2,1)S(1)}, bf16[16,5248]{1,0:T(8,128)(2,...) custom-call(s32[1]{0:T(128)} %bitcast.where_ref, ...), custom_call_target="tpu_custom_call" | custom-call | tf_op jit(solution)/shard_map/pallas_call | solution.py:324
  40.2 2.4 %collective-permute-start.8 = (bf16[16,5248]{1,0:T(8,128)(2,1)S(1)}, bf16[16,5248]{1,0:T(8,128)(2,1)S(1)}, u32[]{:S(2)}, u32[]{:S(2)}) collective-permute-start(bf16[16,5248]{1,0:T(8,128)(2,1)S(1)} %get-tuple-element.43), channel_id=1, source_target_pairs={{0,12},{4,8},{8,4},{12,0},{16,28},{20,24},{24,20},{28,16},{1,13},{... | collective-permute-start | bytes 503816 | tf_op jit(solution)/shard_map/ppermute | solution.py:437
  43.4 2.2 %collective-permute-start.12 = (bf16[16,5248]{1,0:T(8,128)(2,1)S(1)}, bf16[16,5248]{1,0:T(8,128)(2,1)S(1)}, u32[]{:S(2)}, u32[]{:S(2)}) collective-permute-start(bf16[16,5248]{1,0:T(8,128)(2,1)S(1)} %get-tuple-element.50), channel_id=1, source_target_pairs={{0,20},{4,16},{8,28},{12,24},{16,4},{20,0},{24,12},{28,8},{1,21},{... | collective-permute-start | bytes 503816 | tf_op jit(solution)/shard_map/ppermute | solution.py:437
  45.5 2.1 %collective-permute-start.13 = (bf16[16,5248]{1,0:T(8,128)(2,1)S(1)}, bf16[16,5248]{1,0:T(8,128)(2,1)S(1)}, u32[]{:S(2)}, u32[]{:S(2)}) collective-permute-start(bf16[16,5248]{1,0:T(8,128)(2,1)S(1)} %get-tuple-element.51), channel_id=1, source_target_pairs={{0,24},{4,28},{8,16},{12,20},{16,8},{20,12},{24,0},{28,4},{1,25},{... | collective-permute-start | bytes 503816 | tf_op jit(solution)/shard_map/ppermute | solution.py:437
  48.5 1.5 %collective-permute-start.9 = (bf16[16,5248]{1,0:T(8,128)(2,1)S(1)}, bf16[16,5248]{1,0:T(8,128)(2,1)S(1)}, u32[]{:S(2)}, u32[]{:S(2)}) collective-permute-start(bf16[16,5248]{1,0:T(8,128)(2,1)S(1)} %get-tuple-element.46), channel_id=1, source_target_pairs={{0,4},{4,0},{8,12},{12,8},{16,20},{20,16},{24,28},{28,24},{1,5},{5... | collective-permute-start | bytes 503816 | tf_op jit(solution)/shard_map/ppermute | solution.py:437
  50.1 9.4 %collective-permute-done.11.refs_4_ = bf16[16,5248]{1,0:T(8,128)(2,1)S(1)} collective-permute-done((bf16[16,5248]{1,0:T(8,128)(2,1)S(1)}, bf16[16,5248]{1,0:T(8,128)(2,1)S(1)}, u32[]{:S(2)}, u32[]{:S(2)}) %collective-permute-start.11) | collective-permute-done | bytes 167968 | tf_op jit(solution)/shard_map/ppermute | solution.py:437
  59.5 4.4 %collective-permute-start.10 = (bf16[16,5248]{1,0:T(8,128)(2,1)S(1)}, bf16[16,5248]{1,0:T(8,128)(2,1)S(1)}, u32[]{:S(2)}, u32[]{:S(2)}) collective-permute-start(bf16[16,5248]{1,0:T(8,128)(2,1)S(1)} %get-tuple-element.47), channel_id=1, source_target_pairs={{0,8},{4,12},{8,0},{12,4},{16,24},{20,28},{24,16},{28,20},{1,9},{5... | collective-permute-start | bytes 503816 | tf_op jit(solution)/shard_map/ppermute | solution.py:437
  63.8 5.0 %collective-permute-done.13.refs_6_ = bf16[16,5248]{1,0:T(8,128)(2,1)S(1)} collective-permute-done((bf16[16,5248]{1,0:T(8,128)(2,1)S(1)}, bf16[16,5248]{1,0:T(8,128)(2,1)S(1)}, u32[]{:S(2)}, u32[]{:S(2)}) %collective-permute-start.13) | collective-permute-done | bytes 167968 | tf_op jit(solution)/shard_map/ppermute | solution.py:437
  68.8 2.5 %collective-permute-done.14.refs_7_ = bf16[16,5248]{1,0:T(8,128)(2,1)S(1)} collective-permute-done((bf16[16,5248]{1,0:T(8,128)(2,1)S(1)}, bf16[16,5248]{1,0:T(8,128)(2,1)S(1)}, u32[]{:S(2)}, u32[]{:S(2)}) %collective-permute-start.14) | collective-permute-done | bytes 167968 | tf_op jit(solution)/shard_map/ppermute | solution.py:437
  71.4 1.5 %shard_map.99 = bf16[128,5120]{1,0:T(8,128)(2,1)} custom-call(bf16[16,5248]{1,0:T(8,128)(2,1)S(1)} %get-tuple-element.42.refs_0_, bf16[16,5248]{1,0:T(8,128)(2,1)S(1)} %collective-permute-done.9.refs_1_, bf16[16,5248]{1,0:T(8,128)(2,1)S(1)} %collective-permute-done.10.refs_2_, bf16[16,5248]{1,0:T(8,128)(2,1)S(1)} %collective-permute-done.8.refs_3_, ...), custom_call_target="tpu_custom_call" | custom-call | tf_op jit(solution)/shard_map/pallas_call | solution.py:360
  (27 shorter events, 5.6 us)
Async XLA Ops:
  0.0 17.3 %copy-start.3 = (s32[8,8]{1,0:T(8,128)S(1)}, s32[8,8]{1,0:T(8,128)}, u32[]{:S(2)}) copy-start(s32[8,8]{1,0:T(8,128)} %mask_ref.1) | copy-start | bytes 772
  0.0 17.3 %copy-start.2 = (s32[2048]{0:T(1024)S(1)}, s32[2048]{0:T(1024)}, u32[]{:S(2)}) copy-start(s32[2048]{0:T(1024)} %param.9) | copy-start | bytes 24580
  2.1 9.7 %collective-permute-start = (bf16[640,256]{1,0:T(8,128)(2,1)}, bf16[640,256]{1,0:T(8,128)(2,1)S(1)}, u32[]{:S(2)}, u32[]{:S(2)}) collective-permute-start(bf16[640,256]{1,0:T(8,128)(2,1)} %get-tuple-element.29), channel_id=1, source_target_pairs={{0,4},{4,0},{8,12},{12,8},{16,20},{20,16},{24,28},{28,24},{1,5},{5... | collective-permute-start | bytes 983048 | tf_op jit(solution)/shard_map/ppermute | solution.py:406
  2.7 11.1 %collective-permute-start.2 = (bf16[640,256]{1,0:T(8,128)(2,1)S(1)}, bf16[640,256]{1,0:T(8,128)(2,1)S(1)}, u32[]{:S(2)}, u32[]{:S(2)}) collective-permute-start(bf16[640,256]{1,0:T(8,128)(2,1)S(1)} %get-tuple-element.30.refs_1_), channel_id=1, source_target_pairs={{4,12},{8,0},{12,20},{16,8},{20,28},{24,16},{5,13},{9,1},{13,21},{... | collective-permute-start | bytes 983048 | tf_op jit(solution)/shard_map/ppermute | solution.py:407
  6.2 11.9 %collective-permute-start.1 = (bf16[640,256]{1,0:T(8,128)(2,1)S(1)}, bf16[640,256]{1,0:T(8,128)(2,1)S(1)}, u32[]{:S(2)}, u32[]{:S(2)}) collective-permute-start(bf16[640,256]{1,0:T(8,128)(2,1)S(1)} %get-tuple-element.30.refs_1_), channel_id=1, source_target_pairs={{0,8},{8,16},{12,4},{16,24},{20,12},{28,20},{1,9},{9,17},{13,5},{1... | collective-permute-start | bytes 983048 | tf_op jit(solution)/shard_map/ppermute | solution.py:408
  13.8 17.2 %collective-permute-start.3 = (bf16[1280,256]{1,0:T(8,128)(2,1)S(1)}, bf16[1280,256]{1,0:T(8,128)(2,1)S(1)}, u32[]{:S(2)}, u32[]{:S(2)}) collective-permute-start(bf16[1280,256]{1,0:T(8,128)(2,1)S(1)} %shard_map.93), channel_id=1, source_target_pairs={{4,12},{8,0},{12,20},{16,8},{20,28},{24,16},{5,13},{9,1},{13,21},{... | collective-permute-start | bytes 1966088 | tf_op jit(solution)/shard_map/ppermute | solution.py:413
  18.0 5.4 %collective-permute-start.5 = (bf16[320,256]{1,0:T(8,128)(2,1)S(1)}, bf16[320,256]{1,0:T(8,128)(2,1)S(1)}, u32[]{:S(2)}, u32[]{:S(2)}) collective-permute-start(bf16[320,256]{1,0:T(8,128)(2,1)S(1)} %get-tuple-element.38), channel_id=1, source_target_pairs={{0,4},{4,0},{8,12},{12,8},{16,20},{20,16},{24,28},{28,24},{1,5},{5... | collective-permute-start | bytes 491528 | tf_op jit(solution)/shard_map/ppermute | solution.py:414
  18.5 7.9 %collective-permute-start.4 = (bf16[640,256]{1,0:T(8,128)(2,1)S(1)}, bf16[640,256]{1,0:T(8,128)(2,1)S(1)}, u32[]{:S(2)}, u32[]{:S(2)}) collective-permute-start(bf16[640,256]{1,0:T(8,128)(2,1)S(1)} %collective-permute-done.refs_0_.refs_2_), channel_id=1, source_target_pairs={{0,8},{4,0},{8,16},{12,4},{16,24},{20,12},{24,28},{28,20},{1,9},{5... | collective-permute-start | bytes 983048 | tf_op jit(solution)/shard_map/ppermute | solution.py:412
  26.4 8.6 %collective-permute-start.6 = (bf16[640,256]{1,0:T(8,128)(2,1)S(1)}, bf16[640,256]{1,0:T(8,128)(2,1)S(1)}, u32[]{:S(2)}, u32[]{:S(2)}) collective-permute-start(bf16[640,256]{1,0:T(8,128)(2,1)S(1)} %collective-permute-done.4.refs_2_), channel_id=1, source_target_pairs={{0,8},{4,0},{8,16},{12,4},{16,24},{20,12},{24,28},{28,20},{1,9},{5... | collective-permute-start | bytes 983048 | tf_op jit(solution)/shard_map/ppermute | solution.py:421
  33.3 5.4 %copy-start = (bf16[640,1280]{1,0:T(8,128)(2,1)S(1)}, bf16[640,1280]{1,0:T(8,128)(2,1)}, u32[]{:S(2)}) copy-start(bf16[640,1280]{1,0:T(8,128)(2,1)} %weight_ref.1) | copy-start | bytes 4915204
  33.3 5.4 %copy-start.1 = (bf16[256,1280]{1,0:T(8,128)(2,1)S(1)}, bf16[256,1280]{1,0:T(8,128)(2,1)}, u32[]{:S(2)}) copy-start(bf16[256,1280]{1,0:T(8,128)(2,1)} %tokens_ref.1) | copy-start | bytes 1966084
  33.3 5.4 %copy-start.4 = (s32[64]{0:T(128)S(1)}, s32[64]{0:T(128)}, u32[]{:S(2)}) copy-start(s32[64]{0:T(128)} %param.16) | copy-start | bytes 772
  33.3 5.4 %copy-start.5 = (s32[64]{0:T(128)S(1)}, s32[64]{0:T(128)}, u32[]{:S(2)}) copy-start(s32[64]{0:T(128)} %param.17) | copy-start | bytes 772
  33.3 5.4 %collective-permute-start.7 = (bf16[320,256]{1,0:T(8,128)(2,1)S(1)}, bf16[320,256]{1,0:T(8,128)(2,1)S(1)}, u32[]{:S(2)}, u32[]{:S(2)}) collective-permute-start(bf16[320,256]{1,0:T(8,128)(2,1)S(1)} %shard_map.97), channel_id=1, source_target_pairs={{0,4},{4,0},{8,12},{12,8},{16,20},{20,16},{24,28},{28,24},{1,5},{5... | collective-permute-start | bytes 491528 | tf_op jit(solution)/shard_map/ppermute | solution.py:424
  40.2 8.3 %collective-permute-start.8 = (bf16[16,5248]{1,0:T(8,128)(2,1)S(1)}, bf16[16,5248]{1,0:T(8,128)(2,1)S(1)}, u32[]{:S(2)}, u32[]{:S(2)}) collective-permute-start(bf16[16,5248]{1,0:T(8,128)(2,1)S(1)} %get-tuple-element.43), channel_id=1, source_target_pairs={{0,12},{4,8},{8,4},{12,0},{16,28},{20,24},{24,20},{28,16},{1,13},{... | collective-permute-start | bytes 503816 | tf_op jit(solution)/shard_map/ppermute | solution.py:437
  42.7 16.8 %collective-permute-start.11 = (bf16[16,5248]{1,0:T(8,128)(2,1)S(1)}, bf16[16,5248]{1,0:T(8,128)(2,1)S(1)}, u32[]{:S(2)}, u32[]{:S(2)}) collective-permute-start(bf16[16,5248]{1,0:T(8,128)(2,1)S(1)} %get-tuple-element.49), channel_id=1, source_target_pairs={{0,16},{4,20},{8,24},{12,28},{16,0},{20,4},{24,8},{28,12},{1,17},{... | collective-permute-start | bytes 503816 | tf_op jit(solution)/shard_map/ppermute | solution.py:437
  43.4 20.5 %collective-permute-start.12 = (bf16[16,5248]{1,0:T(8,128)(2,1)S(1)}, bf16[16,5248]{1,0:T(8,128)(2,1)S(1)}, u32[]{:S(2)}, u32[]{:S(2)}) collective-permute-start(bf16[16,5248]{1,0:T(8,128)(2,1)S(1)} %get-tuple-element.50), channel_id=1, source_target_pairs={{0,20},{4,16},{8,28},{12,24},{16,4},{20,0},{24,12},{28,8},{1,21},{... | collective-permute-start | bytes 503816 | tf_op jit(solution)/shard_map/ppermute | solution.py:437
  45.5 23.3 %collective-permute-start.13 = (bf16[16,5248]{1,0:T(8,128)(2,1)S(1)}, bf16[16,5248]{1,0:T(8,128)(2,1)S(1)}, u32[]{:S(2)}, u32[]{:S(2)}) collective-permute-start(bf16[16,5248]{1,0:T(8,128)(2,1)S(1)} %get-tuple-element.51), channel_id=1, source_target_pairs={{0,24},{4,28},{8,16},{12,20},{16,8},{20,12},{24,0},{28,4},{1,25},{... | collective-permute-start | bytes 503816 | tf_op jit(solution)/shard_map/ppermute | solution.py:437
  47.7 23.7 %collective-permute-start.14 = (bf16[16,5248]{1,0:T(8,128)(2,1)S(1)}, bf16[16,5248]{1,0:T(8,128)(2,1)S(1)}, u32[]{:S(2)}, u32[]{:S(2)}) collective-permute-start(bf16[16,5248]{1,0:T(8,128)(2,1)S(1)} %get-tuple-element.52), channel_id=1, source_target_pairs={{0,28},{4,24},{8,20},{12,16},{16,12},{20,8},{24,4},{28,0},{1,29},{... | collective-permute-start | bytes 503816 | tf_op jit(solution)/shard_map/ppermute | solution.py:437
  48.5 22.8 %collective-permute-start.9 = (bf16[16,5248]{1,0:T(8,128)(2,1)S(1)}, bf16[16,5248]{1,0:T(8,128)(2,1)S(1)}, u32[]{:S(2)}, u32[]{:S(2)}) collective-permute-start(bf16[16,5248]{1,0:T(8,128)(2,1)S(1)} %get-tuple-element.46), channel_id=1, source_target_pairs={{0,4},{4,0},{8,12},{12,8},{16,20},{20,16},{24,28},{28,24},{1,5},{5... | collective-permute-start | bytes 503816 | tf_op jit(solution)/shard_map/ppermute | solution.py:437
  59.5 11.9 %collective-permute-start.10 = (bf16[16,5248]{1,0:T(8,128)(2,1)S(1)}, bf16[16,5248]{1,0:T(8,128)(2,1)S(1)}, u32[]{:S(2)}, u32[]{:S(2)}) collective-permute-start(bf16[16,5248]{1,0:T(8,128)(2,1)S(1)} %get-tuple-element.47), channel_id=1, source_target_pairs={{0,8},{4,12},{8,0},{12,4},{16,24},{20,28},{24,16},{28,20},{1,9},{5... | collective-permute-start | bytes 503816 | tf_op jit(solution)/shard_map/ppermute | solution.py:437

commit v17 on v16

--- a/solution.py
+++ b/solution.py
@@ -406,16 +406,15 @@
     other_kv = swap(swap_kv)
     ahead_own = ahead(own_kv)
     back_own = back(own_kv)
-    ready, back_own, swap_q, segs, need = lax.optimization_barrier(
-        (other_kv, back_own, swap_q, segs, need)
-    )
+    ready, back_own, segs, need = lax.optimization_barrier((other_kv, back_own, segs, need))
     back_other = relay(ready)
     ahead_both = ahead(stack(other_kv, ahead_own))
-    other_q = swap(swap_q)
     near = (own_kv, other_kv, ahead_own, back_own)
     near_numbers = (0, 1, 2, 3)
     fixed = (where, need, segs)
     own = attention(*fixed, (own_q,), (0,), near, near_numbers, None, False)
+    swap_q, own = lax.optimization_barrier((swap_q, own))
+    other_q = swap(swap_q)
     other = attention(*fixed, (other_q,), (1,), near, near_numbers, None, False)
     back_other, other = lax.optimization_barrier((back_other, other))
     back_far = relay(back_other)

time: 73.4 us -> 77.2 us (1.052)
  waiting for transfers between devices: 30.7 us -> 32.3 us
  local copies, waits for them, and re-layouts: 0.03 us -> 1.4 us
  starting transfers between devices: 27.8 us -> 28.9 us
    ppermute x1, waiting for transfers between devices: 3.29 us -> 1.19 us  [per_device(): other_kv = swap(swap_kv)]
    ppermute x1, waiting for transfers between devices: 0.01 us -> 1.9 us  [per_device(): back_own = back(own_kv)]
    ppermute x7, waiting for transfers between devices: 16.9 us -> 18.7 us  [cross(): lax.ppermute(arrived[d], 'blk', [(i, i ^ d) for i in range(nblocks)])]
    unnamed x12, local copies, waits for them, and re-layouts: 0.03 us -> 1.4 us
    ppermute x1, starting transfers between devices: 0.46 us -> 1.6 us  [per_device(): other_q = swap(swap_q)]
    ppermute x1, starting transfers between devices: 1.59 us -> 2.71 us  [per_device(): other = swap(other)]
    ppermute x1, waiting for transfers between devices: 4.77 us -> 3.78 us  [per_device(): other_q = swap(swap_q)]
    ppermute x1, waiting for transfers between devices: 0.96 us -> 1.88 us  [per_device(): back_other = relay(ready)]
  transfers between devices with their start and end apart: 15 -> 15, of which waited for: 9 -> 11; matrix products, arithmetic and copies ran while one was open for 0% -> 0% of each run, Pallas kernels for 12% -> 12%
where the time goes in v17:
time: 77.2 us; the launch traced here: 76.9 us
  waiting for transfers between devices  32.3 us (42%)
  starting transfers between devices  28.9 us (37%)
  Pallas kernels  14.1 us (18%)
  local copies, waits for them, and re-layouts  1.4 us (2%)
    ppermute x7, waiting for transfers between devices, cross(): lax.ppermute(arrived[d], 'blk', [(i, i ^ d) for i in range(nblocks)])  18.7 us
    ppermute x7, starting transfers between devices, cross(): lax.ppermute(arrived[d], 'blk', [(i, i ^ d) for i in range(nblocks)])  13.9 us
    pallas_call x4, Pallas kernels, attention(): pl.pallas_call(functools.partial(attention_kernel, kinds, numbers, rows_o...  8.3 us
    ppermute x1, waiting for transfers between devices, per_device(): other_q = swap(swap_q)  3.78 us
    ppermute x1, starting transfers between devices, per_device(): ahead_own = ahead(own_kv)  3.48 us
    ppermute x1, starting transfers between devices, per_device(): ahead_both = ahead(stack(other_kv, ahead_own))  3.48 us
    ppermute x1, starting transfers between devices, per_device(): other = swap(other)  2.71 us
    ppermute x1, starting transfers between devices, per_device(): back_own = back(own_kv)  2.35 us
  transfers between devices with their start and end apart: 15, of which 11 were waited for; matrix products, arithmetic and copies ran while one was open for 0% of the time, Pallas kernels for 12%

profile of v17, /device:TPU:14, one launch (start us, length us, event | category | flops | bytes accessed | tf_op | source)
XLA Modules:
  0.0 76.9 jit_solution(9122472908259086339)
XLA Ops:
  0.0 2.1 %shard_map.91 = (bf16[320,256]{1,0:T(8,128)(2,1)S(1)}, bf16[640,256]{1,0:T(8,128)(2,1)S(1)}, bf16[320,256]{1,0:T(8,128)(2,1)S(1)}, bf16[640,256]{1,0:T(8,128)(2,1)}) custom-call(s32[1]{0:T(128)} %bitcast.where_ref, bf16[256,640]{1,0:T(8,128)(2,1)} %q_hbm.1, bf16[256,640]{1,0:T(8,128)(2,1)} %k_hbm.1, bf16[256,640]{1,0:T(8,128)(2,1)} %v_hbm.1), custom_call_target="tpu_custom_call" | custom-call | tf_op jit(solution)/shard_map/pallas_call | solution.py:74
  2.7 2.3 %collective-permute-start.1 = (bf16[640,256]{1,0:T(8,128)(2,1)S(1)}, bf16[640,256]{1,0:T(8,128)(2,1)S(1)}, u32[]{:S(2)}, u32[]{:S(2)}) collective-permute-start(bf16[640,256]{1,0:T(8,128)(2,1)S(1)} %get-tuple-element.31.refs_1_), channel_id=1, source_target_pairs={{0,8},{8,16},{12,4},{16,24},{20,12},{28,20},{1,9},{9,17},{13,5},{1... | collective-permute-start | bytes 983048 | tf_op jit(solution)/shard_map/ppermute | solution.py:408
  5.0 3.5 %collective-permute-start.2 = (bf16[640,256]{1,0:T(8,128)(2,1)S(1)}, bf16[640,256]{1,0:T(8,128)(2,1)S(1)}, u32[]{:S(2)}, u32[]{:S(2)}) collective-permute-start(bf16[640,256]{1,0:T(8,128)(2,1)S(1)} %get-tuple-element.31.refs_1_), channel_id=1, source_target_pairs={{4,12},{8,0},{12,20},{16,8},{20,28},{24,16},{5,13},{9,1},{13,21},{... | collective-permute-start | bytes 983048 | tf_op jit(solution)/shard_map/ppermute | solution.py:407
  11.8 1.9 %collective-permute-done.1.refs_4_ = bf16[640,256]{1,0:T(8,128)(2,1)S(1)} collective-permute-done((bf16[640,256]{1,0:T(8,128)(2,1)S(1)}, bf16[640,256]{1,0:T(8,128)(2,1)S(1)}, u32[]{:S(2)}, u32[]{:S(2)}) %collective-permute-start.1) | collective-permute-done | bytes 327712 | tf_op jit(solution)/shard_map/ppermute | solution.py:408
  13.7 2.1 %collective-permute-done.2.refs_1_.refs_3_ = bf16[640,256]{1,0:T(8,128)(2,1)S(1)} collective-permute-done((bf16[640,256]{1,0:T(8,128)(2,1)S(1)}, bf16[640,256]{1,0:T(8,128)(2,1)S(1)}, u32[]{:S(2)}, u32[]{:S(2)}) %collective-permute-start.2) | collective-permute-done | bytes 327712 | tf_op jit(solution)/shard_map/ppermute | solution.py:407
  15.8 3.5 %collective-permute-start.3 = (bf16[1280,256]{1,0:T(8,128)(2,1)S(1)}, bf16[1280,256]{1,0:T(8,128)(2,1)S(1)}, u32[]{:S(2)}, u32[]{:S(2)}) collective-permute-start(bf16[1280,256]{1,0:T(8,128)(2,1)S(1)} %shard_map.93), channel_id=1, source_target_pairs={{4,12},{8,0},{12,20},{16,8},{20,28},{24,16},{5,13},{9,1},{13,21},{... | collective-permute-start | bytes 1966088 | tf_op jit(solution)/shard_map/ppermute | solution.py:411
  19.3 2.0 %shard_map.94.refs_4_ = f32[1,4,256,128]{3,2,1,0:T(8,128)S(1)} custom-call(s32[1]{0:T(128)} %bitcast.where_ref, s32[8,128]{1,0:T(8,128)S(1)} %get-tuple-element.34.need_ref, f32[1,2048]{1,0:T(1,128)S(1)} %get-tuple-element.35.seg_ref, bf16[320,256]{1,0:T(8,128)(2,1)S(1)} %get-tuple-element.36.refs_0_, bf16[640,256]{1,0:T(8,128)(2,1)S(1)} %get-tuple-element.31.refs_1_, ...), custom_call_target="tpu_custom_call" | custom-call | flops 2000000000 | bytes 2000000 | tf_op jit(solution)/shard_map/pallas_call | solution.py:234
  21.3 1.6 %collective-permute-start.5 = (bf16[320,256]{1,0:T(8,128)(2,1)S(1)}, bf16[320,256]{1,0:T(8,128)(2,1)S(1)}, u32[]{:S(2)}, u32[]{:S(2)}) collective-permute-start(bf16[320,256]{1,0:T(8,128)(2,1)S(1)} %get-tuple-element.40), channel_id=1, source_target_pairs={{0,4},{4,0},{8,12},{12,8},{16,20},{20,16},{24,28},{28,24},{1,5},{5... | collective-permute-start | bytes 491528 | tf_op jit(solution)/shard_map/ppermute | solution.py:417
  22.9 3.8 %collective-permute-done.5.refs_0_ = bf16[320,256]{1,0:T(8,128)(2,1)S(1)} collective-permute-done((bf16[320,256]{1,0:T(8,128)(2,1)S(1)}, bf16[320,256]{1,0:T(8,128)(2,1)S(1)}, u32[]{:S(2)}, u32[]{:S(2)}) %collective-permute-start.5) | collective-permute-done | bytes 163872 | tf_op jit(solution)/shard_map/ppermute | solution.py:417
  26.7 2.0 %shard_map.95.refs_3_ = f32[1,4,256,128]{3,2,1,0:T(8,128)S(1)} custom-call(s32[1]{0:T(128)} %bitcast.where_ref, s32[8,128]{1,0:T(8,128)S(1)} %get-tuple-element.34.need_ref, f32[1,2048]{1,0:T(1,128)S(1)} %get-tuple-element.35.seg_ref, bf16[320,256]{1,0:T(8,128)(2,1)S(1)} %collective-permute-done.5.refs_0_, bf16[640,256]{1,0:T(8,128)(2,1)S(1)} %get-tuple-element.31.refs_1_, ...), custom_call_target="tpu_custom_call" | custom-call | flops 2000000000 | bytes 2000000 | tf_op jit(solution)/shard_map/pallas_call | solution.py:234
  28.7 1.9 %collective-permute-done.4.refs_2_ = bf16[640,256]{1,0:T(8,128)(2,1)S(1)} collective-permute-done((bf16[640,256]{1,0:T(8,128)(2,1)S(1)}, bf16[640,256]{1,0:T(8,128)(2,1)S(1)}, u32[]{:S(2)}, u32[]{:S(2)}) %collective-permute-start.4) | collective-permute-done | bytes 327712 | tf_op jit(solution)/shard_map/ppermute | solution.py:410
  32.7 2.3 %shard_map.97 = bf16[320,256]{1,0:T(8,128)(2,1)S(1)} custom-call(s32[1]{0:T(128)} %bitcast.where_ref, s32[8,128]{1,0:T(8,128)S(1)} %get-tuple-element.34.need_ref, f32[1,2048]{1,0:T(1,128)S(1)} %get-tuple-element.35.seg_ref, bf16[320,256]{1,0:T(8,128)(2,1)S(1)} %collective-permute-done.5.refs_0_, bf16[1280,256]{1,0:T(8,128)(2,1)S(1)} %collective-permute-done.3.refs_1_, ...), custom_call_target="tpu_custom_call" | custom-call | flops 2000000000 | bytes 2000000 | tf_op jit(solution)/shard_map/pallas_call | solution.py:234
  35.1 2.7 %collective-permute-start.7 = (bf16[320,256]{1,0:T(8,128)(2,1)S(1)}, bf16[320,256]{1,0:T(8,128)(2,1)S(1)}, u32[]{:S(2)}, u32[]{:S(2)}) collective-permute-start(bf16[320,256]{1,0:T(8,128)(2,1)S(1)} %shard_map.97), channel_id=1, source_target_pairs={{0,4},{4,0},{8,12},{12,8},{16,20},{20,16},{24,28},{28,24},{1,5},{5... | collective-permute-start | bytes 491528 | tf_op jit(solution)/shard_map/ppermute | solution.py:423
  37.8 2.0 %shard_map.96.own_ref = bf16[320,256]{1,0:T(8,128)(2,1)S(1)} custom-call(s32[1]{0:T(128)} %bitcast.where_ref, s32[8,128]{1,0:T(8,128)S(1)} %get-tuple-element.34.need_ref, f32[1,2048]{1,0:T(1,128)S(1)} %get-tuple-element.35.seg_ref, bf16[320,256]{1,0:T(8,128)(2,1)S(1)} %get-tuple-element.36.refs_0_, bf16[1280,256]{1,0:T(8,128)(2,1)S(1)} %collective-permute-done.3.refs_1_, ...), custom_call_target="tpu_custom_call" | custom-call | flops 2000000000 | bytes 2000000 | tf_op jit(solution)/shard_map/pallas_call | solution.py:234
  41.1 1.5 %shard_map.98 = (bf16[16,5248]{1,0:T(8,128)(2,1)S(1)}, bf16[16,5248]{1,0:T(8,128)(2,1)S(1)}, bf16[16,5248]{1,0:T(8,128)(2,1)S(1)}, bf16[16,5248]{1,0:T(8,128)(2,...) custom-call(s32[1]{0:T(128)} %bitcast.where_ref, ...), custom_call_target="tpu_custom_call" | custom-call | tf_op jit(solution)/shard_map/pallas_call | solution.py:324
  42.6 3.2 %collective-permute-start.8 = (bf16[16,5248]{1,0:T(8,128)(2,1)S(1)}, bf16[16,5248]{1,0:T(8,128)(2,1)S(1)}, u32[]{:S(2)}, u32[]{:S(2)}) collective-permute-start(bf16[16,5248]{1,0:T(8,128)(2,1)S(1)} %get-tuple-element.45), channel_id=1, source_target_pairs={{0,12},{4,8},{8,4},{12,0},{16,28},{20,24},{24,20},{28,16},{1,13},{... | collective-permute-start | bytes 503816 | tf_op jit(solution)/shard_map/ppermute | solution.py:436
  45.8 1.8 %collective-permute-start.11 = (bf16[16,5248]{1,0:T(8,128)(2,1)S(1)}, bf16[16,5248]{1,0:T(8,128)(2,1)S(1)}, u32[]{:S(2)}, u32[]{:S(2)}) collective-permute-start(bf16[16,5248]{1,0:T(8,128)(2,1)S(1)} %get-tuple-element.51), channel_id=1, source_target_pairs={{0,16},{4,20},{8,24},{12,28},{16,0},{20,4},{24,8},{28,12},{1,17},{... | collective-permute-start | bytes 503816 | tf_op jit(solution)/shard_map/ppermute | solution.py:436
  47.7 4.2 %collective-permute-start.13 = (bf16[16,5248]{1,0:T(8,128)(2,1)S(1)}, bf16[16,5248]{1,0:T(8,128)(2,1)S(1)}, u32[]{:S(2)}, u32[]{:S(2)}) collective-permute-start(bf16[16,5248]{1,0:T(8,128)(2,1)S(1)} %get-tuple-element.53), channel_id=1, source_target_pairs={{0,24},{4,28},{8,16},{12,20},{16,8},{20,12},{24,0},{28,4},{1,25},{... | collective-permute-start | bytes 503816 | tf_op jit(solution)/shard_map/ppermute | solution.py:436
  51.9 2.4 %collective-permute-start.10 = (bf16[16,5248]{1,0:T(8,128)(2,1)S(1)}, bf16[16,5248]{1,0:T(8,128)(2,1)S(1)}, u32[]{:S(2)}, u32[]{:S(2)}) collective-permute-start(bf16[16,5248]{1,0:T(8,128)(2,1)S(1)} %get-tuple-element.49), channel_id=1, source_target_pairs={{0,8},{4,12},{8,0},{12,4},{16,24},{20,28},{24,16},{28,20},{1,9},{5... | collective-permute-start | bytes 503816 | tf_op jit(solution)/shard_map/ppermute | solution.py:436
  54.3 9.7 %collective-permute-done.11.refs_4_ = bf16[16,5248]{1,0:T(8,128)(2,1)S(1)} collective-permute-done((bf16[16,5248]{1,0:T(8,128)(2,1)S(1)}, bf16[16,5248]{1,0:T(8,128)(2,1)S(1)}, u32[]{:S(2)}, u32[]{:S(2)}) %collective-permute-start.11) | collective-permute-done | bytes 167968 | tf_op jit(solution)/shard_map/ppermute | solution.py:436
  64.0 2.3 %collective-permute-start.9 = (bf16[16,5248]{1,0:T(8,128)(2,1)S(1)}, bf16[16,5248]{1,0:T(8,128)(2,1)S(1)}, u32[]{:S(2)}, u32[]{:S(2)}) collective-permute-start(bf16[16,5248]{1,0:T(8,128)(2,1)S(1)} %get-tuple-element.48), channel_id=1, source_target_pairs={{0,4},{4,0},{8,12},{12,8},{16,20},{20,16},{24,28},{28,24},{1,5},{5... | collective-permute-start | bytes 503816 | tf_op jit(solution)/shard_map/ppermute | solution.py:436
  67.6 4.7 %collective-permute-done.13.refs_6_ = bf16[16,5248]{1,0:T(8,128)(2,1)S(1)} collective-permute-done((bf16[16,5248]{1,0:T(8,128)(2,1)S(1)}, bf16[16,5248]{1,0:T(8,128)(2,1)S(1)}, u32[]{:S(2)}, u32[]{:S(2)}) %collective-permute-start.13) | collective-permute-done | bytes 167968 | tf_op jit(solution)/shard_map/ppermute | solution.py:436
  72.3 3.0 %collective-permute-done.14.refs_7_ = bf16[16,5248]{1,0:T(8,128)(2,1)S(1)} collective-permute-done((bf16[16,5248]{1,0:T(8,128)(2,1)S(1)}, bf16[16,5248]{1,0:T(8,128)(2,1)S(1)}, u32[]{:S(2)}, u32[]{:S(2)}) %collective-permute-start.14) | collective-permute-done | bytes 167968 | tf_op jit(solution)/shard_map/ppermute | solution.py:436
  75.3 1.5 %shard_map.99 = bf16[128,5120]{1,0:T(8,128)(2,1)} custom-call(bf16[16,5248]{1,0:T(8,128)(2,1)S(1)} %get-tuple-element.44.refs_0_, bf16[16,5248]{1,0:T(8,128)(2,1)S(1)} %collective-permute-done.9.refs_1_, bf16[16,5248]{1,0:T(8,128)(2,1)S(1)} %collective-permute-done.10.refs_2_, bf16[16,5248]{1,0:T(8,128)(2,1)S(1)} %collective-permute-done.8.refs_3_, ...), custom_call_target="tpu_custom_call" | custom-call | tf_op jit(solution)/shard_map/pallas_call | solution.py:360
  (27 shorter events, 8.8 us)
Async XLA Ops:
  2.1 9.7 %collective-permute-start = (bf16[640,256]{1,0:T(8,128)(2,1)}, bf16[640,256]{1,0:T(8,128)(2,1)S(1)}, u32[]{:S(2)}, u32[]{:S(2)}) collective-permute-start(bf16[640,256]{1,0:T(8,128)(2,1)} %get-tuple-element.30), channel_id=1, source_target_pairs={{0,4},{4,0},{8,12},{12,8},{16,20},{20,16},{24,28},{28,24},{1,5},{5... | collective-permute-start | bytes 983048 | tf_op jit(solution)/shard_map/ppermute | solution.py:406
  2.7 11.1 %collective-permute-start.1 = (bf16[640,256]{1,0:T(8,128)(2,1)S(1)}, bf16[640,256]{1,0:T(8,128)(2,1)S(1)}, u32[]{:S(2)}, u32[]{:S(2)}) collective-permute-start(bf16[640,256]{1,0:T(8,128)(2,1)S(1)} %get-tuple-element.31.refs_1_), channel_id=1, source_target_pairs={{0,8},{8,16},{12,4},{16,24},{20,12},{28,20},{1,9},{9,17},{13,5},{1... | collective-permute-start | bytes 983048 | tf_op jit(solution)/shard_map/ppermute | solution.py:408
  5.0 10.8 %collective-permute-start.2 = (bf16[640,256]{1,0:T(8,128)(2,1)S(1)}, bf16[640,256]{1,0:T(8,128)(2,1)S(1)}, u32[]{:S(2)}, u32[]{:S(2)}) collective-permute-start(bf16[640,256]{1,0:T(8,128)(2,1)S(1)} %get-tuple-element.31.refs_1_), channel_id=1, source_target_pairs={{4,12},{8,0},{12,20},{16,8},{20,28},{24,16},{5,13},{9,1},{13,21},{... | collective-permute-start | bytes 983048 | tf_op jit(solution)/shard_map/ppermute | solution.py:407
  8.5 0.7 copy-start.2
  9.2 0.7 copy-start.3
  15.8 16.9 %collective-permute-start.3 = (bf16[1280,256]{1,0:T(8,128)(2,1)S(1)}, bf16[1280,256]{1,0:T(8,128)(2,1)S(1)}, u32[]{:S(2)}, u32[]{:S(2)}) collective-permute-start(bf16[1280,256]{1,0:T(8,128)(2,1)S(1)} %shard_map.93), channel_id=1, source_target_pairs={{4,12},{8,0},{12,20},{16,8},{20,28},{24,16},{5,13},{9,1},{13,21},{... | collective-permute-start | bytes 1966088 | tf_op jit(solution)/shard_map/ppermute | solution.py:411
  21.3 5.4 %collective-permute-start.5 = (bf16[320,256]{1,0:T(8,128)(2,1)S(1)}, bf16[320,256]{1,0:T(8,128)(2,1)S(1)}, u32[]{:S(2)}, u32[]{:S(2)}) collective-permute-start(bf16[320,256]{1,0:T(8,128)(2,1)S(1)} %get-tuple-element.40), channel_id=1, source_target_pairs={{0,4},{4,0},{8,12},{12,8},{16,20},{20,16},{24,28},{28,24},{1,5},{5... | collective-permute-start | bytes 491528 | tf_op jit(solution)/shard_map/ppermute | solution.py:417
  22.9 7.7 %collective-permute-start.4 = (bf16[640,256]{1,0:T(8,128)(2,1)S(1)}, bf16[640,256]{1,0:T(8,128)(2,1)S(1)}, u32[]{:S(2)}, u32[]{:S(2)}) collective-permute-start(bf16[640,256]{1,0:T(8,128)(2,1)S(1)} %collective-permute-done.refs_0_.refs_2_), channel_id=1, source_target_pairs={{0,8},{4,0},{8,16},{12,4},{16,24},{20,12},{24,28},{28,20},{1,9},{5... | collective-permute-start | bytes 983048 | tf_op jit(solution)/shard_map/ppermute | solution.py:410
  30.6 7.2 %collective-permute-start.6 = (bf16[640,256]{1,0:T(8,128)(2,1)S(1)}, bf16[640,256]{1,0:T(8,128)(2,1)S(1)}, u32[]{:S(2)}, u32[]{:S(2)}) collective-permute-start(bf16[640,256]{1,0:T(8,128)(2,1)S(1)} %collective-permute-done.4.refs_2_), channel_id=1, source_target_pairs={{0,8},{4,0},{8,16},{12,4},{16,24},{20,12},{24,28},{28,20},{1,9},{5... | collective-permute-start | bytes 983048 | tf_op jit(solution)/shard_map/ppermute | solution.py:420
  35.1 6.1 %copy-start = (bf16[640,1280]{1,0:T(8,128)(2,1)S(1)}, bf16[640,1280]{1,0:T(8,128)(2,1)}, u32[]{:S(2)}) copy-start(bf16[640,1280]{1,0:T(8,128)(2,1)} %weight_ref.1) | copy-start | bytes 4915204
  35.1 6.1 %copy-start.1 = (bf16[256,1280]{1,0:T(8,128)(2,1)S(1)}, bf16[256,1280]{1,0:T(8,128)(2,1)}, u32[]{:S(2)}) copy-start(bf16[256,1280]{1,0:T(8,128)(2,1)} %tokens_ref.1) | copy-start | bytes 1966084
  35.1 6.0 %copy-start.4 = (s32[64]{0:T(128)S(1)}, s32[64]{0:T(128)}, u32[]{:S(2)}) copy-start(s32[64]{0:T(128)} %param.16) | copy-start | bytes 772
  35.1 6.0 %copy-start.5 = (s32[64]{0:T(128)S(1)}, s32[64]{0:T(128)}, u32[]{:S(2)}) copy-start(s32[64]{0:T(128)} %param.17) | copy-start | bytes 772
  35.1 6.0 %collective-permute-start.7 = (bf16[320,256]{1,0:T(8,128)(2,1)S(1)}, bf16[320,256]{1,0:T(8,128)(2,1)S(1)}, u32[]{:S(2)}, u32[]{:S(2)}) collective-permute-start(bf16[320,256]{1,0:T(8,128)(2,1)S(1)} %shard_map.97), channel_id=1, source_target_pairs={{0,4},{4,0},{8,12},{12,8},{16,20},{20,16},{24,28},{28,24},{1,5},{5... | collective-permute-start | bytes 491528 | tf_op jit(solution)/shard_map/ppermute | solution.py:423
  42.6 9.3 %collective-permute-start.8 = (bf16[16,5248]{1,0:T(8,128)(2,1)S(1)}, bf16[16,5248]{1,0:T(8,128)(2,1)S(1)}, u32[]{:S(2)}, u32[]{:S(2)}) collective-permute-start(bf16[16,5248]{1,0:T(8,128)(2,1)S(1)} %get-tuple-element.45), channel_id=1, source_target_pairs={{0,12},{4,8},{8,4},{12,0},{16,28},{20,24},{24,20},{28,16},{1,13},{... | collective-permute-start | bytes 503816 | tf_op jit(solution)/shard_map/ppermute | solution.py:436
  45.8 18.1 %collective-permute-start.11 = (bf16[16,5248]{1,0:T(8,128)(2,1)S(1)}, bf16[16,5248]{1,0:T(8,128)(2,1)S(1)}, u32[]{:S(2)}, u32[]{:S(2)}) collective-permute-start(bf16[16,5248]{1,0:T(8,128)(2,1)S(1)} %get-tuple-element.51), channel_id=1, source_target_pairs={{0,16},{4,20},{8,24},{12,28},{16,0},{20,4},{24,8},{28,12},{1,17},{... | collective-permute-start | bytes 503816 | tf_op jit(solution)/shard_map/ppermute | solution.py:436
  47.6 19.9 %collective-permute-start.12 = (bf16[16,5248]{1,0:T(8,128)(2,1)S(1)}, bf16[16,5248]{1,0:T(8,128)(2,1)S(1)}, u32[]{:S(2)}, u32[]{:S(2)}) collective-permute-start(bf16[16,5248]{1,0:T(8,128)(2,1)S(1)} %get-tuple-element.52), channel_id=1, source_target_pairs={{0,20},{4,16},{8,28},{12,24},{16,4},{20,0},{24,12},{28,8},{1,21},{... | collective-permute-start | bytes 503816 | tf_op jit(solution)/shard_map/ppermute | solution.py:436
  47.7 24.6 %collective-permute-start.13 = (bf16[16,5248]{1,0:T(8,128)(2,1)S(1)}, bf16[16,5248]{1,0:T(8,128)(2,1)S(1)}, u32[]{:S(2)}, u32[]{:S(2)}) collective-permute-start(bf16[16,5248]{1,0:T(8,128)(2,1)S(1)} %get-tuple-element.53), channel_id=1, source_target_pairs={{0,24},{4,28},{8,16},{12,20},{16,8},{20,12},{24,0},{28,4},{1,25},{... | collective-permute-start | bytes 503816 | tf_op jit(solution)/shard_map/ppermute | solution.py:436
  51.9 23.4 %collective-permute-start.14 = (bf16[16,5248]{1,0:T(8,128)(2,1)S(1)}, bf16[16,5248]{1,0:T(8,128)(2,1)S(1)}, u32[]{:S(2)}, u32[]{:S(2)}) collective-permute-start(bf16[16,5248]{1,0:T(8,128)(2,1)S(1)} %get-tuple-element.54), channel_id=1, source_target_pairs={{0,28},{4,24},{8,20},{12,16},{16,12},{20,8},{24,4},{28,0},{1,29},{... | collective-permute-start | bytes 503816 | tf_op jit(solution)/shard_map/ppermute | solution.py:436
  51.9 23.4 %collective-permute-start.10 = (bf16[16,5248]{1,0:T(8,128)(2,1)S(1)}, bf16[16,5248]{1,0:T(8,128)(2,1)S(1)}, u32[]{:S(2)}, u32[]{:S(2)}) collective-permute-start(bf16[16,5248]{1,0:T(8,128)(2,1)S(1)} %get-tuple-element.49), channel_id=1, source_target_pairs={{0,8},{4,12},{8,0},{12,4},{16,24},{20,28},{24,16},{28,20},{1,9},{5... | collective-permute-start | bytes 503816 | tf_op jit(solution)/shard_map/ppermute | solution.py:436
  64.0 11.3 %collective-permute-start.9 = (bf16[16,5248]{1,0:T(8,128)(2,1)S(1)}, bf16[16,5248]{1,0:T(8,128)(2,1)S(1)}, u32[]{:S(2)}, u32[]{:S(2)}) collective-permute-start(bf16[16,5248]{1,0:T(8,128)(2,1)S(1)} %get-tuple-element.48), channel_id=1, source_target_pairs={{0,4},{4,0},{8,12},{12,8},{16,20},{20,16},{24,28},{28,24},{1,5},{5... | collective-permute-start | bytes 503816 | tf_op jit(solution)/shard_map/ppermute | solution.py:436

commit v18 on v16

--- a/solution.py
+++ b/solution.py
@@ -243,9 +243,7 @@
             pltpu.SMEM((len(numbers) + 1,), jnp.int32),
         ],
         compiler_params=limit(16),
-        cost_estimate=pl.CostEstimate(
-            flops=2_000_000_000 * len(kinds), bytes_accessed=2_000_000, transcendentals=1_000_000
-        ),
+        cost_estimate=pl.CostEstimate(flops=1000, bytes_accessed=1000, transcendentals=0),
     )(where, need, segs, *queries, *blocks, *((before,) if follows else ()))
 
 
@@ -406,9 +404,7 @@
     other_kv = swap(swap_kv)
     ahead_own = ahead(own_kv)
     back_own = back(own_kv)
-    ready, back_own, swap_q, segs, need = lax.optimization_barrier(
-        (other_kv, back_own, swap_q, segs, need)
-    )
+    ready, back_own, swap_q = lax.optimization_barrier((other_kv, back_own, swap_q))
     back_other = relay(ready)
     ahead_both = ahead(stack(other_kv, ahead_own))
     other_q = swap(swap_q)

time: 73.4 us -> 74.1 us (level)
  starting transfers between devices: 27.8 us -> 30 us
  waiting for transfers between devices: 30.7 us -> 29.3 us
    ppermute x1, starting transfers between devices: 1.51 us -> 3.86 us  [per_device(): back_far = relay(back_other)]
    ppermute x7, waiting for transfers between devices: 16.9 us -> 19.1 us  [cross(): lax.ppermute(arrived[d], 'blk', [(i, i ^ d) for i in range(nblocks)])]
    ppermute x1, waiting for transfers between devices: 1.79 us -> 0.01 us  [per_device(): other = swap(other)]
    ppermute x1, waiting for transfers between devices: 4.77 us -> 3.1 us  [per_device(): other_q = swap(swap_q)]
    ppermute x7, starting transfers between devices: 14.2 us -> 12.7 us  [cross(): lax.ppermute(arrived[d], 'blk', [(i, i ^ d) for i in range(nblocks)])]
    ppermute x1, starting transfers between devices: 0.46 us -> 1.48 us  [per_device(): other_q = swap(swap_q)]
    ppermute x1, waiting for transfers between devices: 0.96 us -> 0.18 us  [per_device(): back_other = relay(ready)]
where the time goes in v18:
time: 74.1 us; the launch traced here: 73.8 us
  starting transfers between devices  30 us (40%)
  waiting for transfers between devices  29.3 us (40%)
  Pallas kernels  14.1 us (19%)
    ppermute x7, waiting for transfers between devices, cross(): lax.ppermute(arrived[d], 'blk', [(i, i ^ d) for i in range(nblocks)])  19.1 us
    ppermute x7, starting transfers between devices, cross(): lax.ppermute(arrived[d], 'blk', [(i, i ^ d) for i in range(nblocks)])  12.7 us
    pallas_call x4, Pallas kernels, attention(): pl.pallas_call(functools.partial(attention_kernel, kinds, numbers, rows_o...  8.31 us
    ppermute x1, starting transfers between devices, per_device(): back_far = relay(back_other)  3.86 us
    ppermute x1, starting transfers between devices, per_device(): ahead_both = ahead(stack(other_kv, ahead_own))  3.48 us
    ppermute x1, starting transfers between devices, per_device(): ahead_own = ahead(own_kv)  3.47 us
    ppermute x1, waiting for transfers between devices, per_device(): other_kv = swap(swap_kv)  3.29 us
    ppermute x1, waiting for transfers between devices, per_device(): other_q = swap(swap_q)  3.1 us
  transfers between devices with their start and end apart: 15, of which 9 were waited for; matrix products, arithmetic and copies ran while one was open for 0% of the time, Pallas kernels for 12%

profile of v18, /device:TPU:14, one launch (start us, length us, event | category | flops | bytes accessed | tf_op | source)
XLA Modules:
  0.0 73.8 jit_solution(16553716432249435246)
XLA Ops:
  0.0 2.1 %shard_map.92 = (bf16[320,256]{1,0:T(8,128)(2,1)S(1)}, bf16[640,256]{1,0:T(8,128)(2,1)S(1)}, bf16[320,256]{1,0:T(8,128)(2,1)S(1)}, bf16[640,256]{1,0:T(8,128)(2,1)}) custom-call(s32[1]{0:T(128)} %bitcast.where_ref, bf16[256,640]{1,0:T(8,128)(2,1)} %q_hbm.1, bf16[256,640]{1,0:T(8,128)(2,1)} %k_hbm.1, bf16[256,640]{1,0:T(8,128)(2,1)} %v_hbm.1), custom_call_target="tpu_custom_call" | custom-call | tf_op jit(solution)/shard_map/pallas_call | solution.py:74
  2.7 3.5 %collective-permute-start.1 = (bf16[640,256]{1,0:T(8,128)(2,1)S(1)}, bf16[640,256]{1,0:T(8,128)(2,1)S(1)}, u32[]{:S(2)}, u32[]{:S(2)}) collective-permute-start(bf16[640,256]{1,0:T(8,128)(2,1)S(1)} %get-tuple-element.31.refs_1_), channel_id=1, source_target_pairs={{4,12},{8,0},{12,20},{16,8},{20,28},{24,16},{5,13},{9,1},{13,21},{... | collective-permute-start | bytes 983048 | tf_op jit(solution)/shard_map/ppermute | solution.py:405
  6.2 2.4 %collective-permute-start.3 = (bf16[640,256]{1,0:T(8,128)(2,1)S(1)}, bf16[640,256]{1,0:T(8,128)(2,1)S(1)}, u32[]{:S(2)}, u32[]{:S(2)}) collective-permute-start(bf16[640,256]{1,0:T(8,128)(2,1)S(1)} %get-tuple-element.31.refs_1_), channel_id=1, source_target_pairs={{0,8},{8,16},{12,4},{16,24},{20,12},{28,20},{1,9},{9,17},{13,5},{1... | collective-permute-start | bytes 983048 | tf_op jit(solution)/shard_map/ppermute | solution.py:406
  8.5 3.3 %collective-permute-done.refs_0_.refs_2_ = bf16[640,256]{1,0:T(8,128)(2,1)S(1)} collective-permute-done((bf16[640,256]{1,0:T(8,128)(2,1)}, bf16[640,256]{1,0:T(8,128)(2,1)S(1)}, u32[]{:S(2)}, u32[]{:S(2)}) %collective-permute-start) | collective-permute-done | bytes 327712 | tf_op jit(solution)/shard_map/ppermute | solution.py:404
  11.8 1.9 %collective-permute-done.1.refs_1_.refs_3_ = bf16[640,256]{1,0:T(8,128)(2,1)S(1)} collective-permute-done((bf16[640,256]{1,0:T(8,128)(2,1)S(1)}, bf16[640,256]{1,0:T(8,128)(2,1)S(1)}, u32[]{:S(2)}, u32[]{:S(2)}) %collective-permute-start.1) | collective-permute-done | bytes 327712 | tf_op jit(solution)/shard_map/ppermute | solution.py:405
  13.8 3.5 %collective-permute-start.2 = (bf16[1280,256]{1,0:T(8,128)(2,1)S(1)}, bf16[1280,256]{1,0:T(8,128)(2,1)S(1)}, u32[]{:S(2)}, u32[]{:S(2)}) collective-permute-start(bf16[1280,256]{1,0:T(8,128)(2,1)S(1)} %shard_map.93), channel_id=1, source_target_pairs={{4,12},{8,0},{12,20},{16,8},{20,28},{24,16},{5,13},{9,1},{13,21},{... | collective-permute-start | bytes 1966088 | tf_op jit(solution)/shard_map/ppermute | solution.py:409
  17.8 1.5 %collective-permute-start.5 = (bf16[320,256]{1,0:T(8,128)(2,1)S(1)}, bf16[320,256]{1,0:T(8,128)(2,1)S(1)}, u32[]{:S(2)}, u32[]{:S(2)}) collective-permute-start(bf16[320,256]{1,0:T(8,128)(2,1)S(1)} %get-tuple-element.34), channel_id=1, source_target_pairs={{0,4},{4,0},{8,12},{12,8},{16,20},{20,16},{24,28},{28,24},{1,5},{5... | collective-permute-start | bytes 491528 | tf_op jit(solution)/shard_map/ppermute | solution.py:410
  20.0 3.1 %collective-permute-done.5.refs_0_ = bf16[320,256]{1,0:T(8,128)(2,1)S(1)} collective-permute-done((bf16[320,256]{1,0:T(8,128)(2,1)S(1)}, bf16[320,256]{1,0:T(8,128)(2,1)S(1)}, u32[]{:S(2)}, u32[]{:S(2)}) %collective-permute-start.5) | collective-permute-done | bytes 163872 | tf_op jit(solution)/shard_map/ppermute | solution.py:410
  23.1 2.0 %shard_map.94.refs_3_ = f32[1,4,256,128]{3,2,1,0:T(8,128)S(1)} custom-call(s32[1]{0:T(128)} %bitcast.where_ref, s32[8,128]{1,0:T(8,128)S(1)} %get-tuple-element.27.need_ref, f32[1,2048]{1,0:T(1,128)S(1)} %get-tuple-element.28.seg_ref, bf16[320,256]{1,0:T(8,128)(2,1)S(1)} %collective-permute-done.5.refs_0_, bf16[640,256]{1,0:T(8,128)(2,1)S(1)} %get-tuple-element.31.refs_1_, ...), custom_call_target="tpu_custom_call" | custom-call | flops 1000 | bytes 1000 | tf_op jit(solution)/shard_map/pallas_call | solution.py:234
  25.3 3.9 %collective-permute-start.6 = (bf16[640,256]{1,0:T(8,128)(2,1)S(1)}, bf16[640,256]{1,0:T(8,128)(2,1)S(1)}, u32[]{:S(2)}, u32[]{:S(2)}) collective-permute-start(bf16[640,256]{1,0:T(8,128)(2,1)S(1)} %collective-permute-done.4.refs_2_), channel_id=1, source_target_pairs={{0,8},{4,0},{8,16},{12,4},{16,24},{20,12},{24,28},{28,20},{1,9},{5... | collective-permute-start | bytes 983048 | tf_op jit(solution)/shard_map/ppermute | solution.py:417
  29.2 1.8 %collective-permute-done.2.refs_1_ = bf16[1280,256]{1,0:T(8,128)(2,1)S(1)} collective-permute-done((bf16[1280,256]{1,0:T(8,128)(2,1)S(1)}, bf16[1280,256]{1,0:T(8,128)(2,1)S(1)}, u32[]{:S(2)}, u32[]{:S(2)}) %collective-permute-start.2) | collective-permute-done | bytes 655392 | tf_op jit(solution)/shard_map/ppermute | solution.py:409
  31.0 2.1 %shard_map.97 = bf16[320,256]{1,0:T(8,128)(2,1)S(1)} custom-call(s32[1]{0:T(128)} %bitcast.where_ref, s32[8,128]{1,0:T(8,128)S(1)} %get-tuple-element.27.need_ref, f32[1,2048]{1,0:T(1,128)S(1)} %get-tuple-element.28.seg_ref, bf16[320,256]{1,0:T(8,128)(2,1)S(1)} %collective-permute-done.5.refs_0_, bf16[1280,256]{1,0:T(8,128)(2,1)S(1)} %collective-permute-done.2.refs_1_, ...), custom_call_target="tpu_custom_call" | custom-call | flops 1000 | bytes 1000 | tf_op jit(solution)/shard_map/pallas_call | solution.py:234
  33.1 1.6 %collective-permute-start.7 = (bf16[320,256]{1,0:T(8,128)(2,1)S(1)}, bf16[320,256]{1,0:T(8,128)(2,1)S(1)}, u32[]{:S(2)}, u32[]{:S(2)}) collective-permute-start(bf16[320,256]{1,0:T(8,128)(2,1)S(1)} %shard_map.97), channel_id=1, source_target_pairs={{0,4},{4,0},{8,12},{12,8},{16,20},{20,16},{24,28},{28,24},{1,5},{5... | collective-permute-start | bytes 491528 | tf_op jit(solution)/shard_map/ppermute | solution.py:420
  34.7 2.2 %shard_map.95.refs_4_ = f32[1,4,256,128]{3,2,1,0:T(8,128)S(1)} custom-call(s32[1]{0:T(128)} %bitcast.where_ref, s32[8,128]{1,0:T(8,128)S(1)} %get-tuple-element.27.need_ref, f32[1,2048]{1,0:T(1,128)S(1)} %get-tuple-element.28.seg_ref, bf16[320,256]{1,0:T(8,128)(2,1)S(1)} %get-tuple-element.29.refs_0_, bf16[640,256]{1,0:T(8,128)(2,1)S(1)} %get-tuple-element.31.refs_1_, ...), custom_call_target="tpu_custom_call" | custom-call | flops 1000 | bytes 1000 | tf_op jit(solution)/shard_map/pallas_call | solution.py:234
  36.9 2.0 %shard_map.96.own_ref = bf16[320,256]{1,0:T(8,128)(2,1)S(1)} custom-call(s32[1]{0:T(128)} %bitcast.where_ref, s32[8,128]{1,0:T(8,128)S(1)} %get-tuple-element.27.need_ref, f32[1,2048]{1,0:T(1,128)S(1)} %get-tuple-element.28.seg_ref, bf16[320,256]{1,0:T(8,128)(2,1)S(1)} %get-tuple-element.29.refs_0_, bf16[1280,256]{1,0:T(8,128)(2,1)S(1)} %collective-permute-done.2.refs_1_, ...), custom_call_target="tpu_custom_call" | custom-call | flops 1000 | bytes 1000 | tf_op jit(solution)/shard_map/pallas_call | solution.py:234
  39.0 1.5 %shard_map.98 = (bf16[16,5248]{1,0:T(8,128)(2,1)S(1)}, bf16[16,5248]{1,0:T(8,128)(2,1)S(1)}, bf16[16,5248]{1,0:T(8,128)(2,1)S(1)}, bf16[16,5248]{1,0:T(8,128)(2,...) custom-call(s32[1]{0:T(128)} %bitcast.where_ref, ...), custom_call_target="tpu_custom_call" | custom-call | tf_op jit(solution)/shard_map/pallas_call | solution.py:322
  40.5 3.5 %collective-permute-start.8 = (bf16[16,5248]{1,0:T(8,128)(2,1)S(1)}, bf16[16,5248]{1,0:T(8,128)(2,1)S(1)}, u32[]{:S(2)}, u32[]{:S(2)}) collective-permute-start(bf16[16,5248]{1,0:T(8,128)(2,1)S(1)} %get-tuple-element.39), channel_id=1, source_target_pairs={{0,12},{4,8},{8,4},{12,0},{16,28},{20,24},{24,20},{28,16},{1,13},{... | collective-permute-start | bytes 503816 | tf_op jit(solution)/shard_map/ppermute | solution.py:433
  45.9 3.6 %collective-permute-start.13 = (bf16[16,5248]{1,0:T(8,128)(2,1)S(1)}, bf16[16,5248]{1,0:T(8,128)(2,1)S(1)}, u32[]{:S(2)}, u32[]{:S(2)}) collective-permute-start(bf16[16,5248]{1,0:T(8,128)(2,1)S(1)} %get-tuple-element.47), channel_id=1, source_target_pairs={{0,24},{4,28},{8,16},{12,20},{16,8},{20,12},{24,0},{28,4},{1,25},{... | collective-permute-start | bytes 503816 | tf_op jit(solution)/shard_map/ppermute | solution.py:433
  50.9 10.4 %collective-permute-done.11.refs_4_ = bf16[16,5248]{1,0:T(8,128)(2,1)S(1)} collective-permute-done((bf16[16,5248]{1,0:T(8,128)(2,1)S(1)}, bf16[16,5248]{1,0:T(8,128)(2,1)S(1)}, u32[]{:S(2)}, u32[]{:S(2)}) %collective-permute-start.11) | collective-permute-done | bytes 167968 | tf_op jit(solution)/shard_map/ppermute | solution.py:433
  61.3 2.2 %collective-permute-start.10 = (bf16[16,5248]{1,0:T(8,128)(2,1)S(1)}, bf16[16,5248]{1,0:T(8,128)(2,1)S(1)}, u32[]{:S(2)}, u32[]{:S(2)}) collective-permute-start(bf16[16,5248]{1,0:T(8,128)(2,1)S(1)} %get-tuple-element.43), channel_id=1, source_target_pairs={{0,8},{4,12},{8,0},{12,4},{16,24},{20,28},{24,16},{28,20},{1,9},{5... | collective-permute-start | bytes 503816 | tf_op jit(solution)/shard_map/ppermute | solution.py:433
  63.6 1.4 %collective-permute-done.12.refs_5_ = bf16[16,5248]{1,0:T(8,128)(2,1)S(1)} collective-permute-done((bf16[16,5248]{1,0:T(8,128)(2,1)S(1)}, bf16[16,5248]{1,0:T(8,128)(2,1)S(1)}, u32[]{:S(2)}, u32[]{:S(2)}) %collective-permute-start.12) | collective-permute-done | bytes 167968 | tf_op jit(solution)/shard_map/ppermute | solution.py:433
  64.9 4.4 %collective-permute-done.13.refs_6_ = bf16[16,5248]{1,0:T(8,128)(2,1)S(1)} collective-permute-done((bf16[16,5248]{1,0:T(8,128)(2,1)S(1)}, bf16[16,5248]{1,0:T(8,128)(2,1)S(1)}, u32[]{:S(2)}, u32[]{:S(2)}) %collective-permute-start.13) | collective-permute-done | bytes 167968 | tf_op jit(solution)/shard_map/ppermute | solution.py:433
  69.3 2.9 %collective-permute-done.14.refs_7_ = bf16[16,5248]{1,0:T(8,128)(2,1)S(1)} collective-permute-done((bf16[16,5248]{1,0:T(8,128)(2,1)S(1)}, bf16[16,5248]{1,0:T(8,128)(2,1)S(1)}, u32[]{:S(2)}, u32[]{:S(2)}) %collective-permute-start.14) | collective-permute-done | bytes 167968 | tf_op jit(solution)/shard_map/ppermute | solution.py:433
  72.2 1.4 %shard_map.99 = bf16[128,5120]{1,0:T(8,128)(2,1)} custom-call(bf16[16,5248]{1,0:T(8,128)(2,1)S(1)} %get-tuple-element.38.refs_0_, bf16[16,5248]{1,0:T(8,128)(2,1)S(1)} %collective-permute-done.9.refs_1_, bf16[16,5248]{1,0:T(8,128)(2,1)S(1)} %collective-permute-done.10.refs_2_, bf16[16,5248]{1,0:T(8,128)(2,1)S(1)} %collective-permute-done.8.refs_3_, ...), custom_call_target="tpu_custom_call" | custom-call | tf_op jit(solution)/shard_map/pallas_call | solution.py:358
  (27 shorter events, 5.5 us)
Async XLA Ops:
  0.0 19.3 %copy-start.3 = (s32[8,8]{1,0:T(8,128)S(1)}, s32[8,8]{1,0:T(8,128)}, u32[]{:S(2)}) copy-start(s32[8,8]{1,0:T(8,128)} %mask_ref.1) | copy-start | bytes 772
  0.0 19.3 %copy-start.2 = (s32[2048]{0:T(1024)S(1)}, s32[2048]{0:T(1024)}, u32[]{:S(2)}) copy-start(s32[2048]{0:T(1024)} %param.9) | copy-start | bytes 24580
  2.1 9.7 %collective-permute-start = (bf16[640,256]{1,0:T(8,128)(2,1)}, bf16[640,256]{1,0:T(8,128)(2,1)S(1)}, u32[]{:S(2)}, u32[]{:S(2)}) collective-permute-start(bf16[640,256]{1,0:T(8,128)(2,1)} %get-tuple-element.30), channel_id=1, source_target_pairs={{0,4},{4,0},{8,12},{12,8},{16,20},{20,16},{24,28},{28,24},{1,5},{5... | collective-permute-start | bytes 983048 | tf_op jit(solution)/shard_map/ppermute | solution.py:404
  2.7 11.1 %collective-permute-start.1 = (bf16[640,256]{1,0:T(8,128)(2,1)S(1)}, bf16[640,256]{1,0:T(8,128)(2,1)S(1)}, u32[]{:S(2)}, u32[]{:S(2)}) collective-permute-start(bf16[640,256]{1,0:T(8,128)(2,1)S(1)} %get-tuple-element.31.refs_1_), channel_id=1, source_target_pairs={{4,12},{8,0},{12,20},{16,8},{20,28},{24,16},{5,13},{9,1},{13,21},{... | collective-permute-start | bytes 983048 | tf_op jit(solution)/shard_map/ppermute | solution.py:405
  6.2 11.1 %collective-permute-start.3 = (bf16[640,256]{1,0:T(8,128)(2,1)S(1)}, bf16[640,256]{1,0:T(8,128)(2,1)S(1)}, u32[]{:S(2)}, u32[]{:S(2)}) collective-permute-start(bf16[640,256]{1,0:T(8,128)(2,1)S(1)} %get-tuple-element.31.refs_1_), channel_id=1, source_target_pairs={{0,8},{8,16},{12,4},{16,24},{20,12},{28,20},{1,9},{9,17},{13,5},{1... | collective-permute-start | bytes 983048 | tf_op jit(solution)/shard_map/ppermute | solution.py:406
  13.8 17.2 %collective-permute-start.2 = (bf16[1280,256]{1,0:T(8,128)(2,1)S(1)}, bf16[1280,256]{1,0:T(8,128)(2,1)S(1)}, u32[]{:S(2)}, u32[]{:S(2)}) collective-permute-start(bf16[1280,256]{1,0:T(8,128)(2,1)S(1)} %shard_map.93), channel_id=1, source_target_pairs={{4,12},{8,0},{12,20},{16,8},{20,28},{24,16},{5,13},{9,1},{13,21},{... | collective-permute-start | bytes 1966088 | tf_op jit(solution)/shard_map/ppermute | solution.py:409
  17.3 8.0 %collective-permute-start.4 = (bf16[640,256]{1,0:T(8,128)(2,1)S(1)}, bf16[640,256]{1,0:T(8,128)(2,1)S(1)}, u32[]{:S(2)}, u32[]{:S(2)}) collective-permute-start(bf16[640,256]{1,0:T(8,128)(2,1)S(1)} %collective-permute-done.refs_0_.refs_2_), channel_id=1, source_target_pairs={{0,8},{4,0},{8,16},{12,4},{16,24},{20,12},{24,28},{28,20},{1,9},{5... | collective-permute-start | bytes 983048 | tf_op jit(solution)/shard_map/ppermute | solution.py:408
  17.8 5.3 %collective-permute-start.5 = (bf16[320,256]{1,0:T(8,128)(2,1)S(1)}, bf16[320,256]{1,0:T(8,128)(2,1)S(1)}, u32[]{:S(2)}, u32[]{:S(2)}) collective-permute-start(bf16[320,256]{1,0:T(8,128)(2,1)S(1)} %get-tuple-element.34), channel_id=1, source_target_pairs={{0,4},{4,0},{8,12},{12,8},{16,20},{20,16},{24,28},{28,24},{1,5},{5... | collective-permute-start | bytes 491528 | tf_op jit(solution)/shard_map/ppermute | solution.py:410
  25.3 11.6 %collective-permute-start.6 = (bf16[640,256]{1,0:T(8,128)(2,1)S(1)}, bf16[640,256]{1,0:T(8,128)(2,1)S(1)}, u32[]{:S(2)}, u32[]{:S(2)}) collective-permute-start(bf16[640,256]{1,0:T(8,128)(2,1)S(1)} %collective-permute-done.4.refs_2_), channel_id=1, source_target_pairs={{0,8},{4,0},{8,16},{12,4},{16,24},{20,12},{24,28},{28,20},{1,9},{5... | collective-permute-start | bytes 983048 | tf_op jit(solution)/shard_map/ppermute | solution.py:417
  33.1 5.8 %collective-permute-start.7 = (bf16[320,256]{1,0:T(8,128)(2,1)S(1)}, bf16[320,256]{1,0:T(8,128)(2,1)S(1)}, u32[]{:S(2)}, u32[]{:S(2)}) collective-permute-start(bf16[320,256]{1,0:T(8,128)(2,1)S(1)} %shard_map.97), channel_id=1, source_target_pairs={{0,4},{4,0},{8,12},{12,8},{16,20},{20,16},{24,28},{28,24},{1,5},{5... | collective-permute-start | bytes 491528 | tf_op jit(solution)/shard_map/ppermute | solution.py:420
  34.7 4.2 %copy-start = (bf16[640,1280]{1,0:T(8,128)(2,1)S(1)}, bf16[640,1280]{1,0:T(8,128)(2,1)}, u32[]{:S(2)}) copy-start(bf16[640,1280]{1,0:T(8,128)(2,1)} %weight_ref.1) | copy-start | bytes 4915204
  34.7 4.2 %copy-start.1 = (bf16[256,1280]{1,0:T(8,128)(2,1)S(1)}, bf16[256,1280]{1,0:T(8,128)(2,1)}, u32[]{:S(2)}) copy-start(bf16[256,1280]{1,0:T(8,128)(2,1)} %tokens_ref.1) | copy-start | bytes 1966084
  34.7 4.2 %copy-start.4 = (s32[64]{0:T(128)S(1)}, s32[64]{0:T(128)}, u32[]{:S(2)}) copy-start(s32[64]{0:T(128)} %param.16) | copy-start | bytes 772
  34.7 4.2 %copy-start.5 = (s32[64]{0:T(128)S(1)}, s32[64]{0:T(128)}, u32[]{:S(2)}) copy-start(s32[64]{0:T(128)} %param.17) | copy-start | bytes 772
  40.5 9.4 %collective-permute-start.8 = (bf16[16,5248]{1,0:T(8,128)(2,1)S(1)}, bf16[16,5248]{1,0:T(8,128)(2,1)S(1)}, u32[]{:S(2)}, u32[]{:S(2)}) collective-permute-start(bf16[16,5248]{1,0:T(8,128)(2,1)S(1)} %get-tuple-element.39), channel_id=1, source_target_pairs={{0,12},{4,8},{8,4},{12,0},{16,28},{20,24},{24,20},{28,16},{1,13},{... | collective-permute-start | bytes 503816 | tf_op jit(solution)/shard_map/ppermute | solution.py:433
  44.0 17.4 %collective-permute-start.11 = (bf16[16,5248]{1,0:T(8,128)(2,1)S(1)}, bf16[16,5248]{1,0:T(8,128)(2,1)S(1)}, u32[]{:S(2)}, u32[]{:S(2)}) collective-permute-start(bf16[16,5248]{1,0:T(8,128)(2,1)S(1)} %get-tuple-element.45), channel_id=1, source_target_pairs={{0,16},{4,20},{8,24},{12,28},{16,0},{20,4},{24,8},{28,12},{1,17},{... | collective-permute-start | bytes 503816 | tf_op jit(solution)/shard_map/ppermute | solution.py:433
  45.1 19.8 %collective-permute-start.12 = (bf16[16,5248]{1,0:T(8,128)(2,1)S(1)}, bf16[16,5248]{1,0:T(8,128)(2,1)S(1)}, u32[]{:S(2)}, u32[]{:S(2)}) collective-permute-start(bf16[16,5248]{1,0:T(8,128)(2,1)S(1)} %get-tuple-element.46), channel_id=1, source_target_pairs={{0,20},{4,16},{8,28},{12,24},{16,4},{20,0},{24,12},{28,8},{1,21},{... | collective-permute-start | bytes 503816 | tf_op jit(solution)/shard_map/ppermute | solution.py:433
  45.9 23.4 %collective-permute-start.13 = (bf16[16,5248]{1,0:T(8,128)(2,1)S(1)}, bf16[16,5248]{1,0:T(8,128)(2,1)S(1)}, u32[]{:S(2)}, u32[]{:S(2)}) collective-permute-start(bf16[16,5248]{1,0:T(8,128)(2,1)S(1)} %get-tuple-element.47), channel_id=1, source_target_pairs={{0,24},{4,28},{8,16},{12,20},{16,8},{20,12},{24,0},{28,4},{1,25},{... | collective-permute-start | bytes 503816 | tf_op jit(solution)/shard_map/ppermute | solution.py:433
  49.4 22.8 %collective-permute-start.14 = (bf16[16,5248]{1,0:T(8,128)(2,1)S(1)}, bf16[16,5248]{1,0:T(8,128)(2,1)S(1)}, u32[]{:S(2)}, u32[]{:S(2)}) collective-permute-start(bf16[16,5248]{1,0:T(8,128)(2,1)S(1)} %get-tuple-element.48), channel_id=1, source_target_pairs={{0,28},{4,24},{8,20},{12,16},{16,12},{20,8},{24,4},{28,0},{1,29},{... | collective-permute-start | bytes 503816 | tf_op jit(solution)/shard_map/ppermute | solution.py:433
  49.8 22.4 %collective-permute-start.9 = (bf16[16,5248]{1,0:T(8,128)(2,1)S(1)}, bf16[16,5248]{1,0:T(8,128)(2,1)S(1)}, u32[]{:S(2)}, u32[]{:S(2)}) collective-permute-start(bf16[16,5248]{1,0:T(8,128)(2,1)S(1)} %get-tuple-element.42), channel_id=1, source_target_pairs={{0,4},{4,0},{8,12},{12,8},{16,20},{20,16},{24,28},{28,24},{1,5},{5... | collective-permute-start | bytes 503816 | tf_op jit(solution)/shard_map/ppermute | solution.py:433
  61.3 10.9 %collective-permute-start.10 = (bf16[16,5248]{1,0:T(8,128)(2,1)S(1)}, bf16[16,5248]{1,0:T(8,128)(2,1)S(1)}, u32[]{:S(2)}, u32[]{:S(2)}) collective-permute-start(bf16[16,5248]{1,0:T(8,128)(2,1)S(1)} %get-tuple-element.43), channel_id=1, source_target_pairs={{0,8},{4,12},{8,0},{12,4},{16,24},{20,28},{24,16},{28,20},{1,9},{5... | collective-permute-start | bytes 503816 | tf_op jit(solution)/shard_map/ppermute | solution.py:433

commit v19 on v18

--- a/solution.py
+++ b/solution.py
@@ -412,9 +412,9 @@
     near_numbers = (0, 1, 2, 3)
     fixed = (where, need, segs)
     own = attention(*fixed, (own_q,), (0,), near, near_numbers, None, False)
+    back_other, own = lax.optimization_barrier((back_other, own))
+    back_far = relay(back_other)
     other = attention(*fixed, (other_q,), (1,), near, near_numbers, None, False)
-    back_other, other = lax.optimization_barrier((back_other, other))
-    back_far = relay(back_other)
     far = (ahead_both, back_other)
     other = attention(*fixed, (other_q,), (1,), far, (4, 6, 5), other, True)
     other = swap(other)

time: 74.1 us -> 73.4 us (level)
  starting transfers between devices: 30 us -> 28 us
    ppermute x1, starting transfers between devices: 3.86 us -> 0.68 us  [per_device(): back_far = relay(back_other)]
    ppermute x1, waiting for transfers between devices: 3.1 us -> 0.01 us  [per_device(): other_q = swap(swap_q)]
    ppermute x1, waiting for transfers between devices: 0.18 us -> 3.22 us  [per_device(): back_other = relay(ready)]
    ppermute x7, waiting for transfers between devices: 19.1 us -> 16.8 us  [cross(): lax.ppermute(arrived[d], 'blk', [(i, i ^ d) for i in range(nblocks)])]
    ppermute x1, waiting for transfers between devices: 0.01 us -> 1.79 us  [per_device(): other = swap(other)]
    ppermute x1, waiting for transfers between devices: 1.78 us -> 2.92 us  [per_device(): ahead_both = ahead(stack(other_kv, ahead_own))]
    ppermute x7, starting transfers between devices: 12.7 us -> 13.8 us  [cross(): lax.ppermute(arrived[d], 'blk', [(i, i ^ d) for i in range(nblocks)])]
  transfers between devices with their start and end apart: 15 -> 15, of which waited for: 9 -> 9; matrix products, arithmetic and copies ran while one was open for 0% -> 0% of each run, Pallas kernels for 12% -> 13%
where the time goes in v19:
time: 73.4 us; the launch traced here: 72.4 us
  waiting for transfers between devices  29.9 us (41%)
  starting transfers between devices  28 us (38%)
  Pallas kernels  14.1 us (19%)
    ppermute x7, waiting for transfers between devices, cross(): lax.ppermute(arrived[d], 'blk', [(i, i ^ d) for i in range(nblocks)])  16.8 us
    ppermute x7, starting transfers between devices, cross(): lax.ppermute(arrived[d], 'blk', [(i, i ^ d) for i in range(nblocks)])  13.8 us
    pallas_call x4, Pallas kernels, attention(): pl.pallas_call(functools.partial(attention_kernel, kinds, numbers, rows_o...  8.3 us
    ppermute x1, starting transfers between devices, per_device(): ahead_both = ahead(stack(other_kv, ahead_own))  3.48 us
    ppermute x1, starting transfers between devices, per_device(): ahead_own = ahead(own_kv)  3.47 us
    ppermute x1, waiting for transfers between devices, per_device(): other_kv = swap(swap_kv)  3.29 us
    ppermute x1, waiting for transfers between devices, per_device(): back_other = relay(ready)  3.22 us
    ppermute x1, waiting for transfers between devices, per_device(): ahead_both = ahead(stack(other_kv, ahead_own))  2.92 us
  transfers between devices with their start and end apart: 15, of which 9 were waited for; matrix products, arithmetic and copies ran while one was open for 0% of the time, Pallas kernels for 13%

profile of v19, /device:TPU:14, one launch (start us, length us, event | category | flops | bytes accessed | tf_op | source)
XLA Modules:
  0.0 72.4 jit_solution(6597357204008737015)
XLA Ops:
  0.0 2.1 %shard_map.92 = (bf16[320,256]{1,0:T(8,128)(2,1)S(1)}, bf16[640,256]{1,0:T(8,128)(2,1)S(1)}, bf16[320,256]{1,0:T(8,128)(2,1)S(1)}, bf16[640,256]{1,0:T(8,128)(2,1)}) custom-call(s32[1]{0:T(128)} %bitcast.where_ref, bf16[256,640]{1,0:T(8,128)(2,1)} %q_hbm.1, bf16[256,640]{1,0:T(8,128)(2,1)} %k_hbm.1, bf16[256,640]{1,0:T(8,128)(2,1)} %v_hbm.1), custom_call_target="tpu_custom_call" | custom-call | tf_op jit(solution)/shard_map/pallas_call | solution.py:74
  2.7 3.5 %collective-permute-start.1 = (bf16[640,256]{1,0:T(8,128)(2,1)S(1)}, bf16[640,256]{1,0:T(8,128)(2,1)S(1)}, u32[]{:S(2)}, u32[]{:S(2)}) collective-permute-start(bf16[640,256]{1,0:T(8,128)(2,1)S(1)} %get-tuple-element.31.refs_1_), channel_id=1, source_target_pairs={{4,12},{8,0},{12,20},{16,8},{20,28},{24,16},{5,13},{9,1},{13,21},{... | collective-permute-start | bytes 983048 | tf_op jit(solution)/shard_map/ppermute | solution.py:405
  6.2 2.4 %collective-permute-start.3 = (bf16[640,256]{1,0:T(8,128)(2,1)S(1)}, bf16[640,256]{1,0:T(8,128)(2,1)S(1)}, u32[]{:S(2)}, u32[]{:S(2)}) collective-permute-start(bf16[640,256]{1,0:T(8,128)(2,1)S(1)} %get-tuple-element.31.refs_1_), channel_id=1, source_target_pairs={{0,8},{8,16},{12,4},{16,24},{20,12},{28,20},{1,9},{9,17},{13,5},{1... | collective-permute-start | bytes 983048 | tf_op jit(solution)/shard_map/ppermute | solution.py:406
  8.5 3.3 %collective-permute-done.refs_0_.refs_2_ = bf16[640,256]{1,0:T(8,128)(2,1)S(1)} collective-permute-done((bf16[640,256]{1,0:T(8,128)(2,1)}, bf16[640,256]{1,0:T(8,128)(2,1)S(1)}, u32[]{:S(2)}, u32[]{:S(2)}) %collective-permute-start) | collective-permute-done | bytes 327712 | tf_op jit(solution)/shard_map/ppermute | solution.py:404
  11.8 1.9 %collective-permute-done.1.refs_1_.refs_3_ = bf16[640,256]{1,0:T(8,128)(2,1)S(1)} collective-permute-done((bf16[640,256]{1,0:T(8,128)(2,1)S(1)}, bf16[640,256]{1,0:T(8,128)(2,1)S(1)}, u32[]{:S(2)}, u32[]{:S(2)}) %collective-permute-start.1) | collective-permute-done | bytes 327712 | tf_op jit(solution)/shard_map/ppermute | solution.py:405
  13.8 3.5 %collective-permute-start.2 = (bf16[1280,256]{1,0:T(8,128)(2,1)S(1)}, bf16[1280,256]{1,0:T(8,128)(2,1)S(1)}, u32[]{:S(2)}, u32[]{:S(2)}) collective-permute-start(bf16[1280,256]{1,0:T(8,128)(2,1)S(1)} %shard_map.93), channel_id=1, source_target_pairs={{4,12},{8,0},{12,20},{16,8},{20,28},{24,16},{5,13},{9,1},{13,21},{... | collective-permute-start | bytes 1966088 | tf_op jit(solution)/shard_map/ppermute | solution.py:409
  18.6 1.5 %collective-permute-start.6 = (bf16[320,256]{1,0:T(8,128)(2,1)S(1)}, bf16[320,256]{1,0:T(8,128)(2,1)S(1)}, u32[]{:S(2)}, u32[]{:S(2)}) collective-permute-start(bf16[320,256]{1,0:T(8,128)(2,1)S(1)} %get-tuple-element.37), channel_id=1, source_target_pairs={{0,4},{4,0},{8,12},{12,8},{16,20},{20,16},{24,28},{28,24},{1,5},{5... | collective-permute-start | bytes 491528 | tf_op jit(solution)/shard_map/ppermute | solution.py:410
  20.1 2.0 %shard_map.94.refs_4_ = f32[1,4,256,128]{3,2,1,0:T(8,128)S(1)} custom-call(s32[1]{0:T(128)} %bitcast.where_ref, s32[8,128]{1,0:T(8,128)S(1)} %get-tuple-element.27.need_ref, f32[1,2048]{1,0:T(1,128)S(1)} %get-tuple-element.28.seg_ref, bf16[320,256]{1,0:T(8,128)(2,1)S(1)} %get-tuple-element.29.refs_0_, bf16[640,256]{1,0:T(8,128)(2,1)S(1)} %get-tuple-element.31.refs_1_, ...), custom_call_target="tpu_custom_call" | custom-call | flops 1000 | bytes 1000 | tf_op jit(solution)/shard_map/pallas_call | solution.py:234
  22.1 3.2 %collective-permute-done.4.refs_2_ = bf16[640,256]{1,0:T(8,128)(2,1)S(1)} collective-permute-done((bf16[640,256]{1,0:T(8,128)(2,1)S(1)}, bf16[640,256]{1,0:T(8,128)(2,1)S(1)}, u32[]{:S(2)}, u32[]{:S(2)}) %collective-permute-start.4) | collective-permute-done | bytes 327712 | tf_op jit(solution)/shard_map/ppermute | solution.py:408
  26.0 2.0 %shard_map.96.refs_3_ = f32[1,4,256,128]{3,2,1,0:T(8,128)S(1)} custom-call(s32[1]{0:T(128)} %bitcast.where_ref, s32[8,128]{1,0:T(8,128)S(1)} %get-tuple-element.27.need_ref, f32[1,2048]{1,0:T(1,128)S(1)} %get-tuple-element.28.seg_ref, bf16[320,256]{1,0:T(8,128)(2,1)S(1)} %collective-permute-done.6.refs_0_, bf16[640,256]{1,0:T(8,128)(2,1)S(1)} %get-tuple-element.31.refs_1_, ...), custom_call_target="tpu_custom_call" | custom-call | flops 1000 | bytes 1000 | tf_op jit(solution)/shard_map/pallas_call | solution.py:234
  28.0 2.9 %collective-permute-done.2.refs_1_ = bf16[1280,256]{1,0:T(8,128)(2,1)S(1)} collective-permute-done((bf16[1280,256]{1,0:T(8,128)(2,1)S(1)}, bf16[1280,256]{1,0:T(8,128)(2,1)S(1)}, u32[]{:S(2)}, u32[]{:S(2)}) %collective-permute-start.2) | collective-permute-done | bytes 655392 | tf_op jit(solution)/shard_map/ppermute | solution.py:409
  31.0 2.3 %shard_map.97 = bf16[320,256]{1,0:T(8,128)(2,1)S(1)} custom-call(s32[1]{0:T(128)} %bitcast.where_ref, s32[8,128]{1,0:T(8,128)S(1)} %get-tuple-element.27.need_ref, f32[1,2048]{1,0:T(1,128)S(1)} %get-tuple-element.28.seg_ref, bf16[320,256]{1,0:T(8,128)(2,1)S(1)} %collective-permute-done.6.refs_0_, bf16[1280,256]{1,0:T(8,128)(2,1)S(1)} %collective-permute-done.2.refs_1_, ...), custom_call_target="tpu_custom_call" | custom-call | flops 1000 | bytes 1000 | tf_op jit(solution)/shard_map/pallas_call | solution.py:234
  33.3 1.6 %collective-permute-start.7 = (bf16[320,256]{1,0:T(8,128)(2,1)S(1)}, bf16[320,256]{1,0:T(8,128)(2,1)S(1)}, u32[]{:S(2)}, u32[]{:S(2)}) collective-permute-start(bf16[320,256]{1,0:T(8,128)(2,1)S(1)} %shard_map.97), channel_id=1, source_target_pairs={{0,4},{4,0},{8,12},{12,8},{16,20},{20,16},{24,28},{28,24},{1,5},{5... | collective-permute-start | bytes 491528 | tf_op jit(solution)/shard_map/ppermute | solution.py:420
  34.9 2.0 %shard_map.95.own_ref = bf16[320,256]{1,0:T(8,128)(2,1)S(1)} custom-call(s32[1]{0:T(128)} %bitcast.where_ref, s32[8,128]{1,0:T(8,128)S(1)} %get-tuple-element.27.need_ref, f32[1,2048]{1,0:T(1,128)S(1)} %get-tuple-element.28.seg_ref, bf16[320,256]{1,0:T(8,128)(2,1)S(1)} %get-tuple-element.29.refs_0_, bf16[1280,256]{1,0:T(8,128)(2,1)S(1)} %collective-permute-done.2.refs_1_, ...), custom_call_target="tpu_custom_call" | custom-call | flops 1000 | bytes 1000 | tf_op jit(solution)/shard_map/pallas_call | solution.py:234
  36.9 1.8 %collective-permute-done.7.other_ref = bf16[320,256]{1,0:T(8,128)(2,1)S(1)} collective-permute-done((bf16[320,256]{1,0:T(8,128)(2,1)S(1)}, bf16[320,256]{1,0:T(8,128)(2,1)S(1)}, u32[]{:S(2)}, u32[]{:S(2)}) %collective-permute-start.7) | collective-permute-done | bytes 163872 | tf_op jit(solution)/shard_map/ppermute | solution.py:420
  40.2 2.6 %collective-permute-start.8 = (bf16[16,5248]{1,0:T(8,128)(2,1)S(1)}, bf16[16,5248]{1,0:T(8,128)(2,1)S(1)}, u32[]{:S(2)}, u32[]{:S(2)}) collective-permute-start(bf16[16,5248]{1,0:T(8,128)(2,1)S(1)} %get-tuple-element.39), channel_id=1, source_target_pairs={{0,12},{4,8},{8,4},{12,0},{16,28},{20,24},{24,20},{28,16},{1,13},{... | collective-permute-start | bytes 503816 | tf_op jit(solution)/shard_map/ppermute | solution.py:433
  42.8 2.4 %collective-permute-start.12 = (bf16[16,5248]{1,0:T(8,128)(2,1)S(1)}, bf16[16,5248]{1,0:T(8,128)(2,1)S(1)}, u32[]{:S(2)}, u32[]{:S(2)}) collective-permute-start(bf16[16,5248]{1,0:T(8,128)(2,1)S(1)} %get-tuple-element.46), channel_id=1, source_target_pairs={{0,20},{4,16},{8,28},{12,24},{16,4},{20,0},{24,12},{28,8},{1,21},{... | collective-permute-start | bytes 503816 | tf_op jit(solution)/shard_map/ppermute | solution.py:433
  46.6 2.0 %collective-permute-start.14 = (bf16[16,5248]{1,0:T(8,128)(2,1)S(1)}, bf16[16,5248]{1,0:T(8,128)(2,1)S(1)}, u32[]{:S(2)}, u32[]{:S(2)}) collective-permute-start(bf16[16,5248]{1,0:T(8,128)(2,1)S(1)} %get-tuple-element.48), channel_id=1, source_target_pairs={{0,28},{4,24},{8,20},{12,16},{16,12},{20,8},{24,4},{28,0},{1,29},{... | collective-permute-start | bytes 503816 | tf_op jit(solution)/shard_map/ppermute | solution.py:433
  48.6 2.3 %collective-permute-start.10 = (bf16[16,5248]{1,0:T(8,128)(2,1)S(1)}, bf16[16,5248]{1,0:T(8,128)(2,1)S(1)}, u32[]{:S(2)}, u32[]{:S(2)}) collective-permute-start(bf16[16,5248]{1,0:T(8,128)(2,1)S(1)} %get-tuple-element.43), channel_id=1, source_target_pairs={{0,8},{4,12},{8,0},{12,4},{16,24},{20,28},{24,16},{28,20},{1,9},{5... | collective-permute-start | bytes 503816 | tf_op jit(solution)/shard_map/ppermute | solution.py:433
  50.9 5.1 %collective-permute-done.11.refs_4_ = bf16[16,5248]{1,0:T(8,128)(2,1)S(1)} collective-permute-done((bf16[16,5248]{1,0:T(8,128)(2,1)S(1)}, bf16[16,5248]{1,0:T(8,128)(2,1)S(1)}, u32[]{:S(2)}, u32[]{:S(2)}) %collective-permute-start.11) | collective-permute-done | bytes 167968 | tf_op jit(solution)/shard_map/ppermute | solution.py:433
  56.0 3.1 %collective-permute-start.9 = (bf16[16,5248]{1,0:T(8,128)(2,1)S(1)}, bf16[16,5248]{1,0:T(8,128)(2,1)S(1)}, u32[]{:S(2)}, u32[]{:S(2)}) collective-permute-start(bf16[16,5248]{1,0:T(8,128)(2,1)S(1)} %get-tuple-element.42), channel_id=1, source_target_pairs={{0,4},{4,0},{8,12},{12,8},{16,20},{20,16},{24,28},{28,24},{1,5},{5... | collective-permute-start | bytes 503816 | tf_op jit(solution)/shard_map/ppermute | solution.py:433
  59.1 3.6 %collective-permute-done.12.refs_5_ = bf16[16,5248]{1,0:T(8,128)(2,1)S(1)} collective-permute-done((bf16[16,5248]{1,0:T(8,128)(2,1)S(1)}, bf16[16,5248]{1,0:T(8,128)(2,1)S(1)}, u32[]{:S(2)}, u32[]{:S(2)}) %collective-permute-start.12) | collective-permute-done | bytes 167968 | tf_op jit(solution)/shard_map/ppermute | solution.py:433
  62.7 6.1 %collective-permute-done.13.refs_6_ = bf16[16,5248]{1,0:T(8,128)(2,1)S(1)} collective-permute-done((bf16[16,5248]{1,0:T(8,128)(2,1)S(1)}, bf16[16,5248]{1,0:T(8,128)(2,1)S(1)}, u32[]{:S(2)}, u32[]{:S(2)}) %collective-permute-start.13) | collective-permute-done | bytes 167968 | tf_op jit(solution)/shard_map/ppermute | solution.py:433
  68.8 2.0 %collective-permute-done.14.refs_7_ = bf16[16,5248]{1,0:T(8,128)(2,1)S(1)} collective-permute-done((bf16[16,5248]{1,0:T(8,128)(2,1)S(1)}, bf16[16,5248]{1,0:T(8,128)(2,1)S(1)}, u32[]{:S(2)}, u32[]{:S(2)}) %collective-permute-start.14) | collective-permute-done | bytes 167968 | tf_op jit(solution)/shard_map/ppermute | solution.py:433
  (27 shorter events, 7.0 us)
Async XLA Ops:
  0.0 17.8 %copy-start.2 = (s32[2048]{0:T(1024)S(1)}, s32[2048]{0:T(1024)}, u32[]{:S(2)}) copy-start(s32[2048]{0:T(1024)} %param.9) | copy-start | bytes 24580
  0.0 17.8 %copy-start.3 = (s32[8,8]{1,0:T(8,128)S(1)}, s32[8,8]{1,0:T(8,128)}, u32[]{:S(2)}) copy-start(s32[8,8]{1,0:T(8,128)} %mask_ref.1) | copy-start | bytes 772
  2.1 9.7 %collective-permute-start = (bf16[640,256]{1,0:T(8,128)(2,1)}, bf16[640,256]{1,0:T(8,128)(2,1)S(1)}, u32[]{:S(2)}, u32[]{:S(2)}) collective-permute-start(bf16[640,256]{1,0:T(8,128)(2,1)} %get-tuple-element.30), channel_id=1, source_target_pairs={{0,4},{4,0},{8,12},{12,8},{16,20},{20,16},{24,28},{28,24},{1,5},{5... | collective-permute-start | bytes 983048 | tf_op jit(solution)/shard_map/ppermute | solution.py:404
  2.7 11.1 %collective-permute-start.1 = (bf16[640,256]{1,0:T(8,128)(2,1)S(1)}, bf16[640,256]{1,0:T(8,128)(2,1)S(1)}, u32[]{:S(2)}, u32[]{:S(2)}) collective-permute-start(bf16[640,256]{1,0:T(8,128)(2,1)S(1)} %get-tuple-element.31.refs_1_), channel_id=1, source_target_pairs={{4,12},{8,0},{12,20},{16,8},{20,28},{24,16},{5,13},{9,1},{13,21},{... | collective-permute-start | bytes 983048 | tf_op jit(solution)/shard_map/ppermute | solution.py:405
  6.2 11.1 %collective-permute-start.3 = (bf16[640,256]{1,0:T(8,128)(2,1)S(1)}, bf16[640,256]{1,0:T(8,128)(2,1)S(1)}, u32[]{:S(2)}, u32[]{:S(2)}) collective-permute-start(bf16[640,256]{1,0:T(8,128)(2,1)S(1)} %get-tuple-element.31.refs_1_), channel_id=1, source_target_pairs={{0,8},{8,16},{12,4},{16,24},{20,12},{28,20},{1,9},{9,17},{13,5},{1... | collective-permute-start | bytes 983048 | tf_op jit(solution)/shard_map/ppermute | solution.py:406
  13.8 17.2 %collective-permute-start.2 = (bf16[1280,256]{1,0:T(8,128)(2,1)S(1)}, bf16[1280,256]{1,0:T(8,128)(2,1)S(1)}, u32[]{:S(2)}, u32[]{:S(2)}) collective-permute-start(bf16[1280,256]{1,0:T(8,128)(2,1)S(1)} %shard_map.93), channel_id=1, source_target_pairs={{4,12},{8,0},{12,20},{16,8},{20,28},{24,16},{5,13},{9,1},{13,21},{... | collective-permute-start | bytes 1966088 | tf_op jit(solution)/shard_map/ppermute | solution.py:409
  17.3 8.0 %collective-permute-start.4 = (bf16[640,256]{1,0:T(8,128)(2,1)S(1)}, bf16[640,256]{1,0:T(8,128)(2,1)S(1)}, u32[]{:S(2)}, u32[]{:S(2)}) collective-permute-start(bf16[640,256]{1,0:T(8,128)(2,1)S(1)} %collective-permute-done.refs_0_.refs_2_), channel_id=1, source_target_pairs={{0,8},{4,0},{8,16},{12,4},{16,24},{20,12},{24,28},{28,20},{1,9},{5... | collective-permute-start | bytes 983048 | tf_op jit(solution)/shard_map/ppermute | solution.py:408
  18.6 7.4 %collective-permute-start.6 = (bf16[320,256]{1,0:T(8,128)(2,1)S(1)}, bf16[320,256]{1,0:T(8,128)(2,1)S(1)}, u32[]{:S(2)}, u32[]{:S(2)}) collective-permute-start(bf16[320,256]{1,0:T(8,128)(2,1)S(1)} %get-tuple-element.37), channel_id=1, source_target_pairs={{0,4},{4,0},{8,12},{12,8},{16,20},{20,16},{24,28},{28,24},{1,5},{5... | collective-permute-start | bytes 491528 | tf_op jit(solution)/shard_map/ppermute | solution.py:410
  25.3 9.6 %collective-permute-start.5 = (bf16[640,256]{1,0:T(8,128)(2,1)S(1)}, bf16[640,256]{1,0:T(8,128)(2,1)S(1)}, u32[]{:S(2)}, u32[]{:S(2)}) collective-permute-start(bf16[640,256]{1,0:T(8,128)(2,1)S(1)} %collective-permute-done.4.refs_2_), channel_id=1, source_target_pairs={{0,8},{4,0},{8,16},{12,4},{16,24},{20,12},{24,28},{28,20},{1,9},{5... | collective-permute-start | bytes 983048 | tf_op jit(solution)/shard_map/ppermute | solution.py:416
  28.0 10.7 %copy-start = (bf16[640,1280]{1,0:T(8,128)(2,1)S(1)}, bf16[640,1280]{1,0:T(8,128)(2,1)}, u32[]{:S(2)}) copy-start(bf16[640,1280]{1,0:T(8,128)(2,1)} %weight_ref.1) | copy-start | bytes 4915204
  28.0 10.7 %copy-start.1 = (bf16[256,1280]{1,0:T(8,128)(2,1)S(1)}, bf16[256,1280]{1,0:T(8,128)(2,1)}, u32[]{:S(2)}) copy-start(bf16[256,1280]{1,0:T(8,128)(2,1)} %tokens_ref.1) | copy-start | bytes 1966084
  28.0 10.7 %copy-start.4 = (s32[64]{0:T(128)S(1)}, s32[64]{0:T(128)}, u32[]{:S(2)}) copy-start(s32[64]{0:T(128)} %param.16) | copy-start | bytes 772
  28.0 10.7 %copy-start.5 = (s32[64]{0:T(128)S(1)}, s32[64]{0:T(128)}, u32[]{:S(2)}) copy-start(s32[64]{0:T(128)} %param.17) | copy-start | bytes 772
  33.3 5.4 %collective-permute-start.7 = (bf16[320,256]{1,0:T(8,128)(2,1)S(1)}, bf16[320,256]{1,0:T(8,128)(2,1)S(1)}, u32[]{:S(2)}, u32[]{:S(2)}) collective-permute-start(bf16[320,256]{1,0:T(8,128)(2,1)S(1)} %shard_map.97), channel_id=1, source_target_pairs={{0,4},{4,0},{8,12},{12,8},{16,20},{20,16},{24,28},{28,24},{1,5},{5... | collective-permute-start | bytes 491528 | tf_op jit(solution)/shard_map/ppermute | solution.py:420
  40.2 8.4 %collective-permute-start.8 = (bf16[16,5248]{1,0:T(8,128)(2,1)S(1)}, bf16[16,5248]{1,0:T(8,128)(2,1)S(1)}, u32[]{:S(2)}, u32[]{:S(2)}) collective-permute-start(bf16[16,5248]{1,0:T(8,128)(2,1)S(1)} %get-tuple-element.39), channel_id=1, source_target_pairs={{0,12},{4,8},{8,4},{12,0},{16,28},{20,24},{24,20},{28,16},{1,13},{... | collective-permute-start | bytes 503816 | tf_op jit(solution)/shard_map/ppermute | solution.py:433
  42.8 13.3 %collective-permute-start.11 = (bf16[16,5248]{1,0:T(8,128)(2,1)S(1)}, bf16[16,5248]{1,0:T(8,128)(2,1)S(1)}, u32[]{:S(2)}, u32[]{:S(2)}) collective-permute-start(bf16[16,5248]{1,0:T(8,128)(2,1)S(1)} %get-tuple-element.45), channel_id=1, source_target_pairs={{0,16},{4,20},{8,24},{12,28},{16,0},{20,4},{24,8},{28,12},{1,17},{... | collective-permute-start | bytes 503816 | tf_op jit(solution)/shard_map/ppermute | solution.py:433
  42.8 19.9 %collective-permute-start.12 = (bf16[16,5248]{1,0:T(8,128)(2,1)S(1)}, bf16[16,5248]{1,0:T(8,128)(2,1)S(1)}, u32[]{:S(2)}, u32[]{:S(2)}) collective-permute-start(bf16[16,5248]{1,0:T(8,128)(2,1)S(1)} %get-tuple-element.46), channel_id=1, source_target_pairs={{0,20},{4,16},{8,28},{12,24},{16,4},{20,0},{24,12},{28,8},{1,21},{... | collective-permute-start | bytes 503816 | tf_op jit(solution)/shard_map/ppermute | solution.py:433
  45.1 23.6 %collective-permute-start.13 = (bf16[16,5248]{1,0:T(8,128)(2,1)S(1)}, bf16[16,5248]{1,0:T(8,128)(2,1)S(1)}, u32[]{:S(2)}, u32[]{:S(2)}) collective-permute-start(bf16[16,5248]{1,0:T(8,128)(2,1)S(1)} %get-tuple-element.47), channel_id=1, source_target_pairs={{0,24},{4,28},{8,16},{12,20},{16,8},{20,12},{24,0},{28,4},{1,25},{... | collective-permute-start | bytes 503816 | tf_op jit(solution)/shard_map/ppermute | solution.py:433
  46.6 24.2 %collective-permute-start.14 = (bf16[16,5248]{1,0:T(8,128)(2,1)S(1)}, bf16[16,5248]{1,0:T(8,128)(2,1)S(1)}, u32[]{:S(2)}, u32[]{:S(2)}) collective-permute-start(bf16[16,5248]{1,0:T(8,128)(2,1)S(1)} %get-tuple-element.48), channel_id=1, source_target_pairs={{0,28},{4,24},{8,20},{12,16},{16,12},{20,8},{24,4},{28,0},{1,29},{... | collective-permute-start | bytes 503816 | tf_op jit(solution)/shard_map/ppermute | solution.py:433
  48.6 22.2 %collective-permute-start.10 = (bf16[16,5248]{1,0:T(8,128)(2,1)S(1)}, bf16[16,5248]{1,0:T(8,128)(2,1)S(1)}, u32[]{:S(2)}, u32[]{:S(2)}) collective-permute-start(bf16[16,5248]{1,0:T(8,128)(2,1)S(1)} %get-tuple-element.43), channel_id=1, source_target_pairs={{0,8},{4,12},{8,0},{12,4},{16,24},{20,28},{24,16},{28,20},{1,9},{5... | collective-permute-start | bytes 503816 | tf_op jit(solution)/shard_map/ppermute | solution.py:433
  56.0 14.8 %collective-permute-start.9 = (bf16[16,5248]{1,0:T(8,128)(2,1)S(1)}, bf16[16,5248]{1,0:T(8,128)(2,1)S(1)}, u32[]{:S(2)}, u32[]{:S(2)}) collective-permute-start(bf16[16,5248]{1,0:T(8,128)(2,1)S(1)} %get-tuple-element.42), channel_id=1, source_target_pairs={{0,4},{4,0},{8,12},{12,8},{16,20},{20,16},{24,28},{28,24},{1,5},{5... | collective-permute-start | bytes 503816 | tf_op jit(solution)/shard_map/ppermute | solution.py:433

commit v20 on v19

--- a/solution.py
+++ b/solution.py
@@ -404,9 +404,12 @@
     other_kv = swap(swap_kv)
     ahead_own = ahead(own_kv)
     back_own = back(own_kv)
-    ready, back_own, swap_q = lax.optimization_barrier((other_kv, back_own, swap_q))
-    back_other = relay(ready)
-    ahead_both = ahead(stack(other_kv, ahead_own))
+    ready, back_own, swap_q, segs, need = lax.optimization_barrier(
+        (other_kv, back_own, swap_q, segs, need)
+    )
+    back_other = back(ready)
+    ahead_other = ahead(other_kv)
+    ahead_far = ahead(ahead_own)
     other_q = swap(swap_q)
     near = (own_kv, other_kv, ahead_own, back_own)
     near_numbers = (0, 1, 2, 3)
@@ -415,11 +418,11 @@
     back_other, own = lax.optimization_barrier((back_other, own))
     back_far = relay(back_other)
     other = attention(*fixed, (other_q,), (1,), near, near_numbers, None, False)
-    far = (ahead_both, back_other)
-    other = attention(*fixed, (other_q,), (1,), far, (4, 6, 5), other, True)
+    middle = (ahead_other, back_other)
+    other = attention(*fixed, (other_q,), (1,), middle, (4, 5), other, False)
+    other = attention(*fixed, (other_q,), (1,), (ahead_far,), (6,), other, True)
     other = swap(other)
-    far = (ahead_both, back_other, back_far)
-    own = attention(*fixed, (own_q,), (0,), far, (4, 6, 5, 7), own, True)
+    own = attention(*fixed, (own_q,), (0,), (*middle, back_far), (4, 5, 7), own, True)
 
     order = tuple(range(nblocks)) if nblocks in (4, 8) else (0,)
     outgoing = project(

time: 73.4 us -> 75.1 us (1.023)
  the two profiles are of different devices: /device:TPU:14 before, /device:TPU:10 now
where the time goes in v20:
time: 75.1 us; the launch traced here: 74 us
  waiting for transfers between devices  30.7 us (41%)
  starting transfers between devices  26.5 us (35%)
  Pallas kernels  14.9 us (20%)
  local copies, waits for them, and re-layouts  1.4 us (2%)
    ppermute x7, waiting for transfers between devices, cross(): lax.ppermute(arrived[d], 'blk', [(i, i ^ d) for i in range(nblocks)])  20.8 us
    pallas_call x5, Pallas kernels, attention(): pl.pallas_call(functools.partial(attention_kernel, kinds, numbers, rows_o...  9.22 us
    ppermute x7, starting transfers between devices, cross(): lax.ppermute(arrived[d], 'blk', [(i, i ^ d) for i in range(nblocks)])  9.07 us
    ppermute x1, starting transfers between devices, per_device(): back_other = back(ready)  3.47 us
    ppermute x1, starting transfers between devices, per_device(): back_own = back(own_kv)  3.47 us
    ppermute x1, waiting for transfers between devices, per_device(): other = swap(other)  3.13 us
    ppermute x1, waiting for transfers between devices, per_device(): back_own = back(own_kv)  2.91 us
    ppermute x1, starting transfers between devices, per_device(): ahead_own = ahead(own_kv)  2.37 us
  transfers between devices with their start and end apart: 16, of which 11 were waited for; matrix products, arithmetic and copies ran while one was open for 0% of the time, Pallas kernels for 13%

profile of v20, /device:TPU:10, one launch (start us, length us, event | category | flops | bytes accessed | tf_op | source)
XLA Modules:
  0.0 74.0 jit_solution(10246886180360551712)
XLA Ops:
  0.0 2.1 %shard_map.91 = (bf16[320,256]{1,0:T(8,128)(2,1)S(1)}, bf16[640,256]{1,0:T(8,128)(2,1)S(1)}, bf16[320,256]{1,0:T(8,128)(2,1)S(1)}, bf16[640,256]{1,0:T(8,128)(2,1)}) custom-call(s32[1]{0:T(128)} %bitcast.where_ref, bf16[256,640]{1,0:T(8,128)(2,1)} %q_hbm.1, bf16[256,640]{1,0:T(8,128)(2,1)} %k_hbm.1, bf16[256,640]{1,0:T(8,128)(2,1)} %v_hbm.1), custom_call_target="tpu_custom_call" | custom-call | tf_op jit(solution)/shard_map/pallas_call | solution.py:74
  2.1 1.6 %collective-permute-start = (bf16[640,256]{1,0:T(8,128)(2,1)}, bf16[640,256]{1,0:T(8,128)(2,1)S(1)}, u32[]{:S(2)}, u32[]{:S(2)}) collective-permute-start(bf16[640,256]{1,0:T(8,128)(2,1)} %get-tuple-element.29), channel_id=1, source_target_pairs={{0,4},{4,0},{8,12},{12,8},{16,20},{20,16},{24,28},{28,24},{1,5},{5... | collective-permute-start | bytes 983048 | tf_op jit(solution)/shard_map/ppermute | solution.py:404
  3.7 3.5 %collective-permute-start.1 = (bf16[640,256]{1,0:T(8,128)(2,1)S(1)}, bf16[640,256]{1,0:T(8,128)(2,1)S(1)}, u32[]{:S(2)}, u32[]{:S(2)}) collective-permute-start(bf16[640,256]{1,0:T(8,128)(2,1)S(1)} %get-tuple-element.30.refs_1_), channel_id=1, source_target_pairs={{0,8},{8,16},{12,4},{16,24},{20,12},{28,20},{1,9},{9,17},{13,5},{1... | collective-permute-start | bytes 983048 | tf_op jit(solution)/shard_map/ppermute | solution.py:406
  7.1 2.4 %collective-permute-start.4 = (bf16[640,256]{1,0:T(8,128)(2,1)S(1)}, bf16[640,256]{1,0:T(8,128)(2,1)S(1)}, u32[]{:S(2)}, u32[]{:S(2)}) collective-permute-start(bf16[640,256]{1,0:T(8,128)(2,1)S(1)} %get-tuple-element.30.refs_1_), channel_id=1, source_target_pairs={{4,12},{8,0},{12,20},{16,8},{20,28},{24,16},{5,13},{9,1},{13,21},{... | collective-permute-start | bytes 983048 | tf_op jit(solution)/shard_map/ppermute | solution.py:405
  11.8 2.9 %collective-permute-done.1.refs_4_ = bf16[640,256]{1,0:T(8,128)(2,1)S(1)} collective-permute-done((bf16[640,256]{1,0:T(8,128)(2,1)S(1)}, bf16[640,256]{1,0:T(8,128)(2,1)S(1)}, u32[]{:S(2)}, u32[]{:S(2)}) %collective-permute-start.1) | collective-permute-done | bytes 327712 | tf_op jit(solution)/shard_map/ppermute | solution.py:406
  14.7 3.5 %collective-permute-start.3 = (bf16[640,256]{1,0:T(8,128)(2,1)S(1)}, bf16[640,256]{1,0:T(8,128)(2,1)S(1)}, u32[]{:S(2)}, u32[]{:S(2)}) collective-permute-start(bf16[640,256]{1,0:T(8,128)(2,1)S(1)} %collective-permute-done.refs_2_), channel_id=1, source_target_pairs={{0,8},{8,16},{12,4},{16,24},{20,12},{28,20},{1,9},{9,17},{13,5},{1... | collective-permute-start | bytes 983048 | tf_op jit(solution)/shard_map/ppermute | solution.py:410
  18.2 2.4 %collective-permute-start.2 = (bf16[640,256]{1,0:T(8,128)(2,1)S(1)}, bf16[640,256]{1,0:T(8,128)(2,1)S(1)}, u32[]{:S(2)}, u32[]{:S(2)}) collective-permute-start(bf16[640,256]{1,0:T(8,128)(2,1)S(1)} %collective-permute-done.refs_2_), channel_id=1, source_target_pairs={{4,12},{8,0},{12,20},{16,8},{20,28},{24,16},{5,13},{9,1},{13,21},{... | collective-permute-start | bytes 983048 | tf_op jit(solution)/shard_map/ppermute | solution.py:411
  20.6 1.9 %collective-permute-start.7 = (bf16[640,256]{1,0:T(8,128)(2,1)S(1)}, bf16[640,256]{1,0:T(8,128)(2,1)S(1)}, u32[]{:S(2)}, u32[]{:S(2)}) collective-permute-start(bf16[640,256]{1,0:T(8,128)(2,1)S(1)} %collective-permute-done.4.refs_3_), channel_id=1, source_target_pairs={{4,12},{8,0},{12,20},{16,8},{20,28},{24,16},{5,13},{9,1},{13,21},{... | collective-permute-start | bytes 983048 | tf_op jit(solution)/shard_map/ppermute | solution.py:412
  22.5 2.1 %collective-permute-start.6 = (bf16[320,256]{1,0:T(8,128)(2,1)S(1)}, bf16[320,256]{1,0:T(8,128)(2,1)S(1)}, u32[]{:S(2)}, u32[]{:S(2)}) collective-permute-start(bf16[320,256]{1,0:T(8,128)(2,1)S(1)} %get-tuple-element.41), channel_id=1, source_target_pairs={{0,4},{4,0},{8,12},{12,8},{16,20},{20,16},{24,28},{28,24},{1,5},{5... | collective-permute-start | bytes 491528 | tf_op jit(solution)/shard_map/ppermute | solution.py:413
  24.7 2.0 %shard_map.93.refs_4_ = f32[1,4,256,128]{3,2,1,0:T(8,128)S(1)} custom-call(s32[1]{0:T(128)} %bitcast.where_ref, s32[8,128]{1,0:T(8,128)S(1)} %get-tuple-element.34.need_ref, f32[1,2048]{1,0:T(1,128)S(1)} %get-tuple-element.35.seg_ref, bf16[320,256]{1,0:T(8,128)(2,1)S(1)} %get-tuple-element.36.refs_0_, bf16[640,256]{1,0:T(8,128)(2,1)S(1)} %get-tuple-element.30.refs_1_, ...), custom_call_target="tpu_custom_call" | custom-call | flops 1000 | bytes 1000 | tf_op jit(solution)/shard_map/pallas_call | solution.py:234
  28.0 2.4 %shard_map.95.refs_3_ = f32[1,4,256,128]{3,2,1,0:T(8,128)S(1)} custom-call(s32[1]{0:T(128)} %bitcast.where_ref, s32[8,128]{1,0:T(8,128)S(1)} %get-tuple-element.34.need_ref, f32[1,2048]{1,0:T(1,128)S(1)} %get-tuple-element.35.seg_ref, bf16[320,256]{1,0:T(8,128)(2,1)S(1)} %collective-permute-done.6.refs_0_, bf16[640,256]{1,0:T(8,128)(2,1)S(1)} %get-tuple-element.30.refs_1_, ...), custom_call_target="tpu_custom_call" | custom-call | flops 1000 | bytes 1000 | tf_op jit(solution)/shard_map/pallas_call | solution.py:234
  30.7 2.1 %shard_map.96.refs_2_ = f32[1,4,256,128]{3,2,1,0:T(8,128)S(1)} custom-call(s32[1]{0:T(128)} %bitcast.where_ref, s32[8,128]{1,0:T(8,128)S(1)} %get-tuple-element.34.need_ref, f32[1,2048]{1,0:T(1,128)S(1)} %get-tuple-element.35.seg_ref, bf16[320,256]{1,0:T(8,128)(2,1)S(1)} %collective-permute-done.6.refs_0_, ...), custom_call_target="tpu_custom_call" | custom-call | flops 1000 | bytes 1000 | tf_op jit(solution)/shard_map/pallas_call | solution.py:234
  32.9 2.2 %collective-permute-done.7.refs_1_ = bf16[640,256]{1,0:T(8,128)(2,1)S(1)} collective-permute-done((bf16[640,256]{1,0:T(8,128)(2,1)S(1)}, bf16[640,256]{1,0:T(8,128)(2,1)S(1)}, u32[]{:S(2)}, u32[]{:S(2)}) %collective-permute-start.7) | collective-permute-done | bytes 327712 | tf_op jit(solution)/shard_map/ppermute | solution.py:412
  35.7 2.2 %shard_map.94.own_ref = bf16[320,256]{1,0:T(8,128)(2,1)S(1)} custom-call(s32[1]{0:T(128)} %bitcast.where_ref, s32[8,128]{1,0:T(8,128)S(1)} %get-tuple-element.34.need_ref, f32[1,2048]{1,0:T(1,128)S(1)} %get-tuple-element.35.seg_ref, bf16[320,256]{1,0:T(8,128)(2,1)S(1)} %get-tuple-element.36.refs_0_, bf16[640,256]{1,0:T(8,128)(2,1)S(1)} %collective-permute-done.2.refs_1_, ...), custom_call_target="tpu_custom_call" | custom-call | flops 1000 | bytes 1000 | tf_op jit(solution)/shard_map/pallas_call | solution.py:234
  37.9 3.1 %collective-permute-done.8.other_ref = bf16[320,256]{1,0:T(8,128)(2,1)S(1)} collective-permute-done((bf16[320,256]{1,0:T(8,128)(2,1)S(1)}, bf16[320,256]{1,0:T(8,128)(2,1)S(1)}, u32[]{:S(2)}, u32[]{:S(2)}) %collective-permute-start.8) | collective-permute-done | bytes 163872 | tf_op jit(solution)/shard_map/ppermute | solution.py:424
  41.0 1.5 %shard_map.98 = (bf16[16,5248]{1,0:T(8,128)(2,1)S(1)}, bf16[16,5248]{1,0:T(8,128)(2,1)S(1)}, bf16[16,5248]{1,0:T(8,128)(2,1)S(1)}, bf16[16,5248]{1,0:T(8,128)(2,...) custom-call(s32[1]{0:T(128)} %bitcast.where_ref, ...), custom_call_target="tpu_custom_call" | custom-call | tf_op jit(solution)/shard_map/pallas_call | solution.py:322
  42.6 2.5 %collective-permute-start.12 = (bf16[16,5248]{1,0:T(8,128)(2,1)S(1)}, bf16[16,5248]{1,0:T(8,128)(2,1)S(1)}, u32[]{:S(2)}, u32[]{:S(2)}) collective-permute-start(bf16[16,5248]{1,0:T(8,128)(2,1)S(1)} %get-tuple-element.49), channel_id=1, source_target_pairs={{0,16},{4,20},{8,24},{12,28},{16,0},{20,4},{24,8},{28,12},{1,17},{... | collective-permute-start | bytes 503816 | tf_op jit(solution)/shard_map/ppermute | solution.py:436
  45.1 1.8 %collective-permute-start.13 = (bf16[16,5248]{1,0:T(8,128)(2,1)S(1)}, bf16[16,5248]{1,0:T(8,128)(2,1)S(1)}, u32[]{:S(2)}, u32[]{:S(2)}) collective-permute-start(bf16[16,5248]{1,0:T(8,128)(2,1)S(1)} %get-tuple-element.50), channel_id=1, source_target_pairs={{0,20},{4,16},{8,28},{12,24},{16,4},{20,0},{24,12},{28,8},{1,21},{... | collective-permute-start | bytes 503816 | tf_op jit(solution)/shard_map/ppermute | solution.py:436
  48.6 2.2 %collective-permute-done.9.refs_3_ = bf16[16,5248]{1,0:T(8,128)(2,1)S(1)} collective-permute-done((bf16[16,5248]{1,0:T(8,128)(2,1)S(1)}, bf16[16,5248]{1,0:T(8,128)(2,1)S(1)}, u32[]{:S(2)}, u32[]{:S(2)}) %collective-permute-start.9) | collective-permute-done | bytes 167968 | tf_op jit(solution)/shard_map/ppermute | solution.py:436
  50.9 9.9 %collective-permute-done.12.refs_4_ = bf16[16,5248]{1,0:T(8,128)(2,1)S(1)} collective-permute-done((bf16[16,5248]{1,0:T(8,128)(2,1)S(1)}, bf16[16,5248]{1,0:T(8,128)(2,1)S(1)}, u32[]{:S(2)}, u32[]{:S(2)}) %collective-permute-start.12) | collective-permute-done | bytes 167968 | tf_op jit(solution)/shard_map/ppermute | solution.py:436
  60.9 2.9 %collective-permute-start.11 = (bf16[16,5248]{1,0:T(8,128)(2,1)S(1)}, bf16[16,5248]{1,0:T(8,128)(2,1)S(1)}, u32[]{:S(2)}, u32[]{:S(2)}) collective-permute-start(bf16[16,5248]{1,0:T(8,128)(2,1)S(1)} %get-tuple-element.47), channel_id=1, source_target_pairs={{0,8},{4,12},{8,0},{12,4},{16,24},{20,28},{24,16},{28,20},{1,9},{5... | collective-permute-start | bytes 503816 | tf_op jit(solution)/shard_map/ppermute | solution.py:436
  64.5 4.9 %collective-permute-done.14.refs_6_ = bf16[16,5248]{1,0:T(8,128)(2,1)S(1)} collective-permute-done((bf16[16,5248]{1,0:T(8,128)(2,1)S(1)}, bf16[16,5248]{1,0:T(8,128)(2,1)S(1)}, u32[]{:S(2)}, u32[]{:S(2)}) %collective-permute-start.14) | collective-permute-done | bytes 167968 | tf_op jit(solution)/shard_map/ppermute | solution.py:436
  69.4 3.0 %collective-permute-done.15.refs_7_ = bf16[16,5248]{1,0:T(8,128)(2,1)S(1)} collective-permute-done((bf16[16,5248]{1,0:T(8,128)(2,1)S(1)}, bf16[16,5248]{1,0:T(8,128)(2,1)S(1)}, u32[]{:S(2)}, u32[]{:S(2)}) %collective-permute-start.15) | collective-permute-done | bytes 167968 | tf_op jit(solution)/shard_map/ppermute | solution.py:436
  72.4 1.4 %shard_map.99 = bf16[128,5120]{1,0:T(8,128)(2,1)} custom-call(bf16[16,5248]{1,0:T(8,128)(2,1)S(1)} %get-tuple-element.42.refs_0_, bf16[16,5248]{1,0:T(8,128)(2,1)S(1)} %collective-permute-done.10.refs_1_, bf16[16,5248]{1,0:T(8,128)(2,1)S(1)} %collective-permute-done.11.refs_2_, bf16[16,5248]{1,0:T(8,128)(2,1)S(1)} %collective-permute-done.9.refs_3_, ...), custom_call_target="tpu_custom_call" | custom-call | tf_op jit(solution)/shard_map/pallas_call | solution.py:358
  (29 shorter events, 7.1 us)
Async XLA Ops:
  2.1 9.7 %collective-permute-start = (bf16[640,256]{1,0:T(8,128)(2,1)}, bf16[640,256]{1,0:T(8,128)(2,1)S(1)}, u32[]{:S(2)}, u32[]{:S(2)}) collective-permute-start(bf16[640,256]{1,0:T(8,128)(2,1)} %get-tuple-element.29), channel_id=1, source_target_pairs={{0,4},{4,0},{8,12},{12,8},{16,20},{20,16},{24,28},{28,24},{1,5},{5... | collective-permute-start | bytes 983048 | tf_op jit(solution)/shard_map/ppermute | solution.py:404
  3.7 11.1 %collective-permute-start.1 = (bf16[640,256]{1,0:T(8,128)(2,1)S(1)}, bf16[640,256]{1,0:T(8,128)(2,1)S(1)}, u32[]{:S(2)}, u32[]{:S(2)}) collective-permute-start(bf16[640,256]{1,0:T(8,128)(2,1)S(1)} %get-tuple-element.30.refs_1_), channel_id=1, source_target_pairs={{0,8},{8,16},{12,4},{16,24},{20,12},{28,20},{1,9},{9,17},{13,5},{1... | collective-permute-start | bytes 983048 | tf_op jit(solution)/shard_map/ppermute | solution.py:406
  7.1 13.4 %collective-permute-start.4 = (bf16[640,256]{1,0:T(8,128)(2,1)S(1)}, bf16[640,256]{1,0:T(8,128)(2,1)S(1)}, u32[]{:S(2)}, u32[]{:S(2)}) collective-permute-start(bf16[640,256]{1,0:T(8,128)(2,1)S(1)} %get-tuple-element.30.refs_1_), channel_id=1, source_target_pairs={{4,12},{8,0},{12,20},{16,8},{20,28},{24,16},{5,13},{9,1},{13,21},{... | collective-permute-start | bytes 983048 | tf_op jit(solution)/shard_map/ppermute | solution.py:405
  9.5 0.7 copy-start.2
  10.2 0.7 copy-start.3
  14.7 11.9 %collective-permute-start.3 = (bf16[640,256]{1,0:T(8,128)(2,1)S(1)}, bf16[640,256]{1,0:T(8,128)(2,1)S(1)}, u32[]{:S(2)}, u32[]{:S(2)}) collective-permute-start(bf16[640,256]{1,0:T(8,128)(2,1)S(1)} %collective-permute-done.refs_2_), channel_id=1, source_target_pairs={{0,8},{8,16},{12,4},{16,24},{20,12},{28,20},{1,9},{9,17},{13,5},{1... | collective-permute-start | bytes 983048 | tf_op jit(solution)/shard_map/ppermute | solution.py:410
  18.2 12.5 %collective-permute-start.2 = (bf16[640,256]{1,0:T(8,128)(2,1)S(1)}, bf16[640,256]{1,0:T(8,128)(2,1)S(1)}, u32[]{:S(2)}, u32[]{:S(2)}) collective-permute-start(bf16[640,256]{1,0:T(8,128)(2,1)S(1)} %collective-permute-done.refs_2_), channel_id=1, source_target_pairs={{4,12},{8,0},{12,20},{16,8},{20,28},{24,16},{5,13},{9,1},{13,21},{... | collective-permute-start | bytes 983048 | tf_op jit(solution)/shard_map/ppermute | solution.py:411
  20.6 14.5 %collective-permute-start.7 = (bf16[640,256]{1,0:T(8,128)(2,1)S(1)}, bf16[640,256]{1,0:T(8,128)(2,1)S(1)}, u32[]{:S(2)}, u32[]{:S(2)}) collective-permute-start(bf16[640,256]{1,0:T(8,128)(2,1)S(1)} %collective-permute-done.4.refs_3_), channel_id=1, source_target_pairs={{4,12},{8,0},{12,20},{16,8},{20,28},{24,16},{5,13},{9,1},{13,21},{... | collective-permute-start | bytes 983048 | tf_op jit(solution)/shard_map/ppermute | solution.py:412
  22.5 5.4 %collective-permute-start.6 = (bf16[320,256]{1,0:T(8,128)(2,1)S(1)}, bf16[320,256]{1,0:T(8,128)(2,1)S(1)}, u32[]{:S(2)}, u32[]{:S(2)}) collective-permute-start(bf16[320,256]{1,0:T(8,128)(2,1)S(1)} %get-tuple-element.41), channel_id=1, source_target_pairs={{0,4},{4,0},{8,12},{12,8},{16,20},{20,16},{24,28},{28,24},{1,5},{5... | collective-permute-start | bytes 491528 | tf_op jit(solution)/shard_map/ppermute | solution.py:413
  26.7 9.0 %collective-permute-start.5 = (bf16[640,256]{1,0:T(8,128)(2,1)S(1)}, bf16[640,256]{1,0:T(8,128)(2,1)S(1)}, u32[]{:S(2)}, u32[]{:S(2)}) collective-permute-start(bf16[640,256]{1,0:T(8,128)(2,1)S(1)} %collective-permute-done.3.refs_2_), channel_id=1, source_target_pairs={{0,8},{4,0},{8,16},{12,4},{16,24},{20,12},{24,28},{28,20},{1,9},{5... | collective-permute-start | bytes 983048 | tf_op jit(solution)/shard_map/ppermute | solution.py:419
  32.9 8.1 %copy-start = (bf16[640,1280]{1,0:T(8,128)(2,1)S(1)}, bf16[640,1280]{1,0:T(8,128)(2,1)}, u32[]{:S(2)}) copy-start(bf16[640,1280]{1,0:T(8,128)(2,1)} %weight_ref.1) | copy-start | bytes 4915204
  32.9 8.1 %copy-start.1 = (bf16[256,1280]{1,0:T(8,128)(2,1)S(1)}, bf16[256,1280]{1,0:T(8,128)(2,1)}, u32[]{:S(2)}) copy-start(bf16[256,1280]{1,0:T(8,128)(2,1)} %tokens_ref.1) | copy-start | bytes 1966084
  32.9 8.1 %copy-start.4 = (s32[64]{0:T(128)S(1)}, s32[64]{0:T(128)}, u32[]{:S(2)}) copy-start(s32[64]{0:T(128)} %param.16) | copy-start | bytes 772
  32.9 8.1 %copy-start.5 = (s32[64]{0:T(128)S(1)}, s32[64]{0:T(128)}, u32[]{:S(2)}) copy-start(s32[64]{0:T(128)} %param.17) | copy-start | bytes 772
  35.6 5.4 %collective-permute-start.8 = (bf16[320,256]{1,0:T(8,128)(2,1)S(1)}, bf16[320,256]{1,0:T(8,128)(2,1)S(1)}, u32[]{:S(2)}, u32[]{:S(2)}) collective-permute-start(bf16[320,256]{1,0:T(8,128)(2,1)S(1)} %shard_map.97), channel_id=1, source_target_pairs={{0,4},{4,0},{8,12},{12,8},{16,20},{20,16},{24,28},{28,24},{1,5},{5... | collective-permute-start | bytes 491528 | tf_op jit(solution)/shard_map/ppermute | solution.py:424
  42.5 8.3 %collective-permute-start.9 = (bf16[16,5248]{1,0:T(8,128)(2,1)S(1)}, bf16[16,5248]{1,0:T(8,128)(2,1)S(1)}, u32[]{:S(2)}, u32[]{:S(2)}) collective-permute-start(bf16[16,5248]{1,0:T(8,128)(2,1)S(1)} %get-tuple-element.43), channel_id=1, source_target_pairs={{0,12},{4,8},{8,4},{12,0},{16,28},{20,24},{24,20},{28,16},{1,13},{... | collective-permute-start | bytes 503816 | tf_op jit(solution)/shard_map/ppermute | solution.py:436
  42.6 18.3 %collective-permute-start.12 = (bf16[16,5248]{1,0:T(8,128)(2,1)S(1)}, bf16[16,5248]{1,0:T(8,128)(2,1)S(1)}, u32[]{:S(2)}, u32[]{:S(2)}) collective-permute-start(bf16[16,5248]{1,0:T(8,128)(2,1)S(1)} %get-tuple-element.49), channel_id=1, source_target_pairs={{0,16},{4,20},{8,24},{12,28},{16,0},{20,4},{24,8},{28,12},{1,17},{... | collective-permute-start | bytes 503816 | tf_op jit(solution)/shard_map/ppermute | solution.py:436
  45.1 19.4 %collective-permute-start.13 = (bf16[16,5248]{1,0:T(8,128)(2,1)S(1)}, bf16[16,5248]{1,0:T(8,128)(2,1)S(1)}, u32[]{:S(2)}, u32[]{:S(2)}) collective-permute-start(bf16[16,5248]{1,0:T(8,128)(2,1)S(1)} %get-tuple-element.50), channel_id=1, source_target_pairs={{0,20},{4,16},{8,28},{12,24},{16,4},{20,0},{24,12},{28,8},{1,21},{... | collective-permute-start | bytes 503816 | tf_op jit(solution)/shard_map/ppermute | solution.py:436
  46.9 22.5 %collective-permute-start.14 = (bf16[16,5248]{1,0:T(8,128)(2,1)S(1)}, bf16[16,5248]{1,0:T(8,128)(2,1)S(1)}, u32[]{:S(2)}, u32[]{:S(2)}) collective-permute-start(bf16[16,5248]{1,0:T(8,128)(2,1)S(1)} %get-tuple-element.51), channel_id=1, source_target_pairs={{0,24},{4,28},{8,16},{12,20},{16,8},{20,12},{24,0},{28,4},{1,25},{... | collective-permute-start | bytes 503816 | tf_op jit(solution)/shard_map/ppermute | solution.py:436
  47.5 24.8 %collective-permute-start.15 = (bf16[16,5248]{1,0:T(8,128)(2,1)S(1)}, bf16[16,5248]{1,0:T(8,128)(2,1)S(1)}, u32[]{:S(2)}, u32[]{:S(2)}) collective-permute-start(bf16[16,5248]{1,0:T(8,128)(2,1)S(1)} %get-tuple-element.52), channel_id=1, source_target_pairs={{0,28},{4,24},{8,20},{12,16},{16,12},{20,8},{24,4},{28,0},{1,29},{... | collective-permute-start | bytes 503816 | tf_op jit(solution)/shard_map/ppermute | solution.py:436
  50.8 21.6 %collective-permute-start.10 = (bf16[16,5248]{1,0:T(8,128)(2,1)S(1)}, bf16[16,5248]{1,0:T(8,128)(2,1)S(1)}, u32[]{:S(2)}, u32[]{:S(2)}) collective-permute-start(bf16[16,5248]{1,0:T(8,128)(2,1)S(1)} %get-tuple-element.46), channel_id=1, source_target_pairs={{0,4},{4,0},{8,12},{12,8},{16,20},{20,16},{24,28},{28,24},{1,5},{5... | collective-permute-start | bytes 503816 | tf_op jit(solution)/shard_map/ppermute | solution.py:436
  60.9 11.5 %collective-permute-start.11 = (bf16[16,5248]{1,0:T(8,128)(2,1)S(1)}, bf16[16,5248]{1,0:T(8,128)(2,1)S(1)}, u32[]{:S(2)}, u32[]{:S(2)}) collective-permute-start(bf16[16,5248]{1,0:T(8,128)(2,1)S(1)} %get-tuple-element.47), channel_id=1, source_target_pairs={{0,8},{4,12},{8,0},{12,4},{16,24},{20,28},{24,16},{28,20},{1,9},{5... | collective-permute-start | bytes 503816 | tf_op jit(solution)/shard_map/ppermute | solution.py:436

commit v21 on v19

--- a/solution.py
+++ b/solution.py
@@ -404,10 +404,10 @@
     other_kv = swap(swap_kv)
     ahead_own = ahead(own_kv)
     back_own = back(own_kv)
-    ready, back_own, swap_q = lax.optimization_barrier((other_kv, back_own, swap_q))
+    other_q = swap(swap_q)
+    ready, back_own, other_q = lax.optimization_barrier((other_kv, back_own, other_q))
     back_other = relay(ready)
     ahead_both = ahead(stack(other_kv, ahead_own))
-    other_q = swap(swap_q)
     near = (own_kv, other_kv, ahead_own, back_own)
     near_numbers = (0, 1, 2, 3)
     fixed = (where, need, segs)

time: 73.4 us -> 73.2 us (level)
  starting transfers between devices: 28 us -> 24.9 us
  waiting for transfers between devices: 29.9 us -> 32.9 us
    ppermute x7, starting transfers between devices: 13.8 us -> 10.8 us  [cross(): lax.ppermute(arrived[d], 'blk', [(i, i ^ d) for i in range(nblocks)])]
    ppermute x7, waiting for transfers between devices: 16.8 us -> 19.6 us  [cross(): lax.ppermute(arrived[d], 'blk', [(i, i ^ d) for i in range(nblocks)])]
    ppermute x1, waiting for transfers between devices: 3.22 us -> 4.76 us  [per_device(): back_other = relay(ready)]
    ppermute x1, waiting for transfers between devices: 1.9 us -> 0.75 us  [per_device(): ahead_own = ahead(own_kv)]
  transfers between devices with their start and end apart: 15 -> 15, of which waited for: 9 -> 10; matrix products, arithmetic and copies ran while one was open for 0% -> 0% of each run, Pallas kernels for 13% -> 13%
where the time goes in v21:
time: 73.2 us; the launch traced here: 72.2 us
  waiting for transfers between devices  32.9 us (45%)
  starting transfers between devices  24.9 us (34%)
  Pallas kernels  14.1 us (19%)
    ppermute x7, waiting for transfers between devices, cross(): lax.ppermute(arrived[d], 'blk', [(i, i ^ d) for i in range(nblocks)])  19.6 us
    ppermute x7, starting transfers between devices, cross(): lax.ppermute(arrived[d], 'blk', [(i, i ^ d) for i in range(nblocks)])  10.8 us
    pallas_call x4, Pallas kernels, attention(): pl.pallas_call(functools.partial(attention_kernel, kinds, numbers, rows_o...  8.3 us
    ppermute x1, waiting for transfers between devices, per_device(): back_other = relay(ready)  4.76 us
    ppermute x1, starting transfers between devices, per_device(): ahead_both = ahead(stack(other_kv, ahead_own))  3.48 us
    ppermute x1, starting transfers between devices, per_device(): ahead_own = ahead(own_kv)  3.47 us
    ppermute x1, waiting for transfers between devices, per_device(): ahead_both = ahead(stack(other_kv, ahead_own))  3.1 us
    ppermute x1, waiting for transfers between devices, per_device(): other_kv = swap(swap_kv)  2.87 us
  transfers between devices with their start and end apart: 15, of which 10 were waited for; matrix products, arithmetic and copies ran while one was open for 0% of the time, Pallas kernels for 13%

profile of v21, /device:TPU:14, one launch (start us, length us, event | category | flops | bytes accessed | tf_op | source)
XLA Modules:
  0.0 72.2 jit_solution(5723764360194989319)
XLA Ops:
  0.0 2.1 %shard_map.92 = (bf16[320,256]{1,0:T(8,128)(2,1)S(1)}, bf16[640,256]{1,0:T(8,128)(2,1)S(1)}, bf16[320,256]{1,0:T(8,128)(2,1)S(1)}, bf16[640,256]{1,0:T(8,128)(2,1)}) custom-call(s32[1]{0:T(128)} %bitcast.where_ref, bf16[256,640]{1,0:T(8,128)(2,1)} %q_hbm.1, bf16[256,640]{1,0:T(8,128)(2,1)} %k_hbm.1, bf16[256,640]{1,0:T(8,128)(2,1)} %v_hbm.1), custom_call_target="tpu_custom_call" | custom-call | tf_op jit(solution)/shard_map/pallas_call | solution.py:74
  2.7 3.5 %collective-permute-start.1 = (bf16[640,256]{1,0:T(8,128)(2,1)S(1)}, bf16[640,256]{1,0:T(8,128)(2,1)S(1)}, u32[]{:S(2)}, u32[]{:S(2)}) collective-permute-start(bf16[640,256]{1,0:T(8,128)(2,1)S(1)} %get-tuple-element.31.refs_1_), channel_id=1, source_target_pairs={{4,12},{8,0},{12,20},{16,8},{20,28},{24,16},{5,13},{9,1},{13,21},{... | collective-permute-start | bytes 983048 | tf_op jit(solution)/shard_map/ppermute | solution.py:405
  6.2 2.4 %collective-permute-start.3 = (bf16[640,256]{1,0:T(8,128)(2,1)S(1)}, bf16[640,256]{1,0:T(8,128)(2,1)S(1)}, u32[]{:S(2)}, u32[]{:S(2)}) collective-permute-start(bf16[640,256]{1,0:T(8,128)(2,1)S(1)} %get-tuple-element.31.refs_1_), channel_id=1, source_target_pairs={{0,8},{8,16},{12,4},{16,24},{20,12},{28,20},{1,9},{9,17},{13,5},{1... | collective-permute-start | bytes 983048 | tf_op jit(solution)/shard_map/ppermute | solution.py:406
  8.5 1.6 %collective-permute-start.4 = (bf16[320,256]{1,0:T(8,128)(2,1)S(1)}, bf16[320,256]{1,0:T(8,128)(2,1)S(1)}, u32[]{:S(2)}, u32[]{:S(2)}) collective-permute-start(bf16[320,256]{1,0:T(8,128)(2,1)S(1)} %get-tuple-element.32), channel_id=1, source_target_pairs={{0,4},{4,0},{8,12},{12,8},{16,20},{20,16},{24,28},{28,24},{1,5},{5... | collective-permute-start | bytes 491528 | tf_op jit(solution)/shard_map/ppermute | solution.py:407
  10.1 2.9 %collective-permute-done.refs_0_.refs_2_ = bf16[640,256]{1,0:T(8,128)(2,1)S(1)} collective-permute-done((bf16[640,256]{1,0:T(8,128)(2,1)}, bf16[640,256]{1,0:T(8,128)(2,1)S(1)}, u32[]{:S(2)}, u32[]{:S(2)}) %collective-permute-start) | collective-permute-done | bytes 327712 | tf_op jit(solution)/shard_map/ppermute | solution.py:404
  13.8 3.5 %collective-permute-start.2 = (bf16[1280,256]{1,0:T(8,128)(2,1)S(1)}, bf16[1280,256]{1,0:T(8,128)(2,1)S(1)}, u32[]{:S(2)}, u32[]{:S(2)}) collective-permute-start(bf16[1280,256]{1,0:T(8,128)(2,1)S(1)} %shard_map.93), channel_id=1, source_target_pairs={{4,12},{8,0},{12,20},{16,8},{20,28},{24,16},{5,13},{9,1},{13,21},{... | collective-permute-start | bytes 1966088 | tf_op jit(solution)/shard_map/ppermute | solution.py:410
  18.6 2.0 %shard_map.94.refs_4_ = f32[1,4,256,128]{3,2,1,0:T(8,128)S(1)} custom-call(s32[1]{0:T(128)} %bitcast.where_ref, s32[8,128]{1,0:T(8,128)S(1)} %get-tuple-element.27.need_ref, f32[1,2048]{1,0:T(1,128)S(1)} %get-tuple-element.28.seg_ref, bf16[320,256]{1,0:T(8,128)(2,1)S(1)} %get-tuple-element.29.refs_0_, bf16[640,256]{1,0:T(8,128)(2,1)S(1)} %get-tuple-element.31.refs_1_, ...), custom_call_target="tpu_custom_call" | custom-call | flops 1000 | bytes 1000 | tf_op jit(solution)/shard_map/pallas_call | solution.py:234
  20.6 4.8 %collective-permute-done.5.refs_2_ = bf16[640,256]{1,0:T(8,128)(2,1)S(1)} collective-permute-done((bf16[640,256]{1,0:T(8,128)(2,1)S(1)}, bf16[640,256]{1,0:T(8,128)(2,1)S(1)}, u32[]{:S(2)}, u32[]{:S(2)}) %collective-permute-start.5) | collective-permute-done | bytes 327712 | tf_op jit(solution)/shard_map/ppermute | solution.py:409
  25.8 2.0 %shard_map.96.refs_3_ = f32[1,4,256,128]{3,2,1,0:T(8,128)S(1)} custom-call(s32[1]{0:T(128)} %bitcast.where_ref, s32[8,128]{1,0:T(8,128)S(1)} %get-tuple-element.27.need_ref, f32[1,2048]{1,0:T(1,128)S(1)} %get-tuple-element.28.seg_ref, bf16[320,256]{1,0:T(8,128)(2,1)S(1)} %collective-permute-done.4.refs_0_, bf16[640,256]{1,0:T(8,128)(2,1)S(1)} %get-tuple-element.31.refs_1_, ...), custom_call_target="tpu_custom_call" | custom-call | flops 1000 | bytes 1000 | tf_op jit(solution)/shard_map/pallas_call | solution.py:234
  27.9 3.1 %collective-permute-done.2.refs_1_ = bf16[1280,256]{1,0:T(8,128)(2,1)S(1)} collective-permute-done((bf16[1280,256]{1,0:T(8,128)(2,1)S(1)}, bf16[1280,256]{1,0:T(8,128)(2,1)S(1)}, u32[]{:S(2)}, u32[]{:S(2)}) %collective-permute-start.2) | collective-permute-done | bytes 655392 | tf_op jit(solution)/shard_map/ppermute | solution.py:410
  31.0 2.3 %shard_map.97 = bf16[320,256]{1,0:T(8,128)(2,1)S(1)} custom-call(s32[1]{0:T(128)} %bitcast.where_ref, s32[8,128]{1,0:T(8,128)S(1)} %get-tuple-element.27.need_ref, f32[1,2048]{1,0:T(1,128)S(1)} %get-tuple-element.28.seg_ref, bf16[320,256]{1,0:T(8,128)(2,1)S(1)} %collective-permute-done.4.refs_0_, bf16[1280,256]{1,0:T(8,128)(2,1)S(1)} %collective-permute-done.2.refs_1_, ...), custom_call_target="tpu_custom_call" | custom-call | flops 1000 | bytes 1000 | tf_op jit(solution)/shard_map/pallas_call | solution.py:234
  33.3 1.6 %collective-permute-start.7 = (bf16[320,256]{1,0:T(8,128)(2,1)S(1)}, bf16[320,256]{1,0:T(8,128)(2,1)S(1)}, u32[]{:S(2)}, u32[]{:S(2)}) collective-permute-start(bf16[320,256]{1,0:T(8,128)(2,1)S(1)} %shard_map.97), channel_id=1, source_target_pairs={{0,4},{4,0},{8,12},{12,8},{16,20},{20,16},{24,28},{28,24},{1,5},{5... | collective-permute-start | bytes 491528 | tf_op jit(solution)/shard_map/ppermute | solution.py:420
  34.9 2.0 %shard_map.95.own_ref = bf16[320,256]{1,0:T(8,128)(2,1)S(1)} custom-call(s32[1]{0:T(128)} %bitcast.where_ref, s32[8,128]{1,0:T(8,128)S(1)} %get-tuple-element.27.need_ref, f32[1,2048]{1,0:T(1,128)S(1)} %get-tuple-element.28.seg_ref, bf16[320,256]{1,0:T(8,128)(2,1)S(1)} %get-tuple-element.29.refs_0_, bf16[1280,256]{1,0:T(8,128)(2,1)S(1)} %collective-permute-done.2.refs_1_, ...), custom_call_target="tpu_custom_call" | custom-call | flops 1000 | bytes 1000 | tf_op jit(solution)/shard_map/pallas_call | solution.py:234
  36.9 1.8 %collective-permute-done.7.other_ref = bf16[320,256]{1,0:T(8,128)(2,1)S(1)} collective-permute-done((bf16[320,256]{1,0:T(8,128)(2,1)S(1)}, bf16[320,256]{1,0:T(8,128)(2,1)S(1)}, u32[]{:S(2)}, u32[]{:S(2)}) %collective-permute-start.7) | collective-permute-done | bytes 163872 | tf_op jit(solution)/shard_map/ppermute | solution.py:420
  38.7 1.5 %shard_map.98 = (bf16[16,5248]{1,0:T(8,128)(2,1)S(1)}, bf16[16,5248]{1,0:T(8,128)(2,1)S(1)}, bf16[16,5248]{1,0:T(8,128)(2,1)S(1)}, bf16[16,5248]{1,0:T(8,128)(2,...) custom-call(s32[1]{0:T(128)} %bitcast.where_ref, ...), custom_call_target="tpu_custom_call" | custom-call | tf_op jit(solution)/shard_map/pallas_call | solution.py:322
  40.2 1.5 %collective-permute-start.8 = (bf16[16,5248]{1,0:T(8,128)(2,1)S(1)}, bf16[16,5248]{1,0:T(8,128)(2,1)S(1)}, u32[]{:S(2)}, u32[]{:S(2)}) collective-permute-start(bf16[16,5248]{1,0:T(8,128)(2,1)S(1)} %get-tuple-element.39), channel_id=1, source_target_pairs={{0,12},{4,8},{8,4},{12,0},{16,28},{20,24},{24,20},{28,16},{1,13},{... | collective-permute-start | bytes 503816 | tf_op jit(solution)/shard_map/ppermute | solution.py:433
  41.7 2.6 %collective-permute-start.11 = (bf16[16,5248]{1,0:T(8,128)(2,1)S(1)}, bf16[16,5248]{1,0:T(8,128)(2,1)S(1)}, u32[]{:S(2)}, u32[]{:S(2)}) collective-permute-start(bf16[16,5248]{1,0:T(8,128)(2,1)S(1)} %get-tuple-element.45), channel_id=1, source_target_pairs={{0,16},{4,20},{8,24},{12,28},{16,0},{20,4},{24,8},{28,12},{1,17},{... | collective-permute-start | bytes 503816 | tf_op jit(solution)/shard_map/ppermute | solution.py:433
  44.3 1.5 %collective-permute-start.13 = (bf16[16,5248]{1,0:T(8,128)(2,1)S(1)}, bf16[16,5248]{1,0:T(8,128)(2,1)S(1)}, u32[]{:S(2)}, u32[]{:S(2)}) collective-permute-start(bf16[16,5248]{1,0:T(8,128)(2,1)S(1)} %get-tuple-element.47), channel_id=1, source_target_pairs={{0,24},{4,28},{8,16},{12,20},{16,8},{20,12},{24,0},{28,4},{1,25},{... | collective-permute-start | bytes 503816 | tf_op jit(solution)/shard_map/ppermute | solution.py:433
  45.8 1.7 %collective-permute-start.14 = (bf16[16,5248]{1,0:T(8,128)(2,1)S(1)}, bf16[16,5248]{1,0:T(8,128)(2,1)S(1)}, u32[]{:S(2)}, u32[]{:S(2)}) collective-permute-start(bf16[16,5248]{1,0:T(8,128)(2,1)S(1)} %get-tuple-element.48), channel_id=1, source_target_pairs={{0,28},{4,24},{8,20},{12,16},{16,12},{20,8},{24,4},{28,0},{1,29},{... | collective-permute-start | bytes 503816 | tf_op jit(solution)/shard_map/ppermute | solution.py:433
  48.5 2.4 %collective-permute-start.10 = (bf16[16,5248]{1,0:T(8,128)(2,1)S(1)}, bf16[16,5248]{1,0:T(8,128)(2,1)S(1)}, u32[]{:S(2)}, u32[]{:S(2)}) collective-permute-start(bf16[16,5248]{1,0:T(8,128)(2,1)S(1)} %get-tuple-element.43), channel_id=1, source_target_pairs={{0,8},{4,12},{8,0},{12,4},{16,24},{20,28},{24,16},{28,20},{1,9},{5... | collective-permute-start | bytes 503816 | tf_op jit(solution)/shard_map/ppermute | solution.py:433
  50.9 9.1 %collective-permute-done.11.refs_4_ = bf16[16,5248]{1,0:T(8,128)(2,1)S(1)} collective-permute-done((bf16[16,5248]{1,0:T(8,128)(2,1)S(1)}, bf16[16,5248]{1,0:T(8,128)(2,1)S(1)}, u32[]{:S(2)}, u32[]{:S(2)}) %collective-permute-start.11) | collective-permute-done | bytes 167968 | tf_op jit(solution)/shard_map/ppermute | solution.py:433
  61.1 2.5 %collective-permute-done.12.refs_5_ = bf16[16,5248]{1,0:T(8,128)(2,1)S(1)} collective-permute-done((bf16[16,5248]{1,0:T(8,128)(2,1)S(1)}, bf16[16,5248]{1,0:T(8,128)(2,1)S(1)}, u32[]{:S(2)}, u32[]{:S(2)}) %collective-permute-start.12) | collective-permute-done | bytes 167968 | tf_op jit(solution)/shard_map/ppermute | solution.py:433
  63.6 5.0 %collective-permute-done.13.refs_6_ = bf16[16,5248]{1,0:T(8,128)(2,1)S(1)} collective-permute-done((bf16[16,5248]{1,0:T(8,128)(2,1)S(1)}, bf16[16,5248]{1,0:T(8,128)(2,1)S(1)}, u32[]{:S(2)}, u32[]{:S(2)}) %collective-permute-start.13) | collective-permute-done | bytes 167968 | tf_op jit(solution)/shard_map/ppermute | solution.py:433
  68.6 2.0 %collective-permute-done.14.refs_7_ = bf16[16,5248]{1,0:T(8,128)(2,1)S(1)} collective-permute-done((bf16[16,5248]{1,0:T(8,128)(2,1)S(1)}, bf16[16,5248]{1,0:T(8,128)(2,1)S(1)}, u32[]{:S(2)}, u32[]{:S(2)}) %collective-permute-start.14) | collective-permute-done | bytes 167968 | tf_op jit(solution)/shard_map/ppermute | solution.py:433
  (27 shorter events, 6.7 us)
Async XLA Ops:
  0.0 17.8 %copy-start.2 = (s32[2048]{0:T(1024)S(1)}, s32[2048]{0:T(1024)}, u32[]{:S(2)}) copy-start(s32[2048]{0:T(1024)} %param.9) | copy-start | bytes 24580
  0.0 17.8 %copy-start.3 = (s32[8,8]{1,0:T(8,128)S(1)}, s32[8,8]{1,0:T(8,128)}, u32[]{:S(2)}) copy-start(s32[8,8]{1,0:T(8,128)} %mask_ref.1) | copy-start | bytes 772
  2.1 10.9 %collective-permute-start = (bf16[640,256]{1,0:T(8,128)(2,1)}, bf16[640,256]{1,0:T(8,128)(2,1)S(1)}, u32[]{:S(2)}, u32[]{:S(2)}) collective-permute-start(bf16[640,256]{1,0:T(8,128)(2,1)} %get-tuple-element.30), channel_id=1, source_target_pairs={{0,4},{4,0},{8,12},{12,8},{16,20},{20,16},{24,28},{28,24},{1,5},{5... | collective-permute-start | bytes 983048 | tf_op jit(solution)/shard_map/ppermute | solution.py:404
  2.7 11.1 %collective-permute-start.1 = (bf16[640,256]{1,0:T(8,128)(2,1)S(1)}, bf16[640,256]{1,0:T(8,128)(2,1)S(1)}, u32[]{:S(2)}, u32[]{:S(2)}) collective-permute-start(bf16[640,256]{1,0:T(8,128)(2,1)S(1)} %get-tuple-element.31.refs_1_), channel_id=1, source_target_pairs={{4,12},{8,0},{12,20},{16,8},{20,28},{24,16},{5,13},{9,1},{13,21},{... | collective-permute-start | bytes 983048 | tf_op jit(solution)/shard_map/ppermute | solution.py:405
  6.2 11.1 %collective-permute-start.3 = (bf16[640,256]{1,0:T(8,128)(2,1)S(1)}, bf16[640,256]{1,0:T(8,128)(2,1)S(1)}, u32[]{:S(2)}, u32[]{:S(2)}) collective-permute-start(bf16[640,256]{1,0:T(8,128)(2,1)S(1)} %get-tuple-element.31.refs_1_), channel_id=1, source_target_pairs={{0,8},{8,16},{12,4},{16,24},{20,12},{28,20},{1,9},{9,17},{13,5},{1... | collective-permute-start | bytes 983048 | tf_op jit(solution)/shard_map/ppermute | solution.py:406
  8.5 8.7 %collective-permute-start.4 = (bf16[320,256]{1,0:T(8,128)(2,1)S(1)}, bf16[320,256]{1,0:T(8,128)(2,1)S(1)}, u32[]{:S(2)}, u32[]{:S(2)}) collective-permute-start(bf16[320,256]{1,0:T(8,128)(2,1)S(1)} %get-tuple-element.32), channel_id=1, source_target_pairs={{0,4},{4,0},{8,12},{12,8},{16,20},{20,16},{24,28},{28,24},{1,5},{5... | collective-permute-start | bytes 491528 | tf_op jit(solution)/shard_map/ppermute | solution.py:407
  13.8 17.2 %collective-permute-start.2 = (bf16[1280,256]{1,0:T(8,128)(2,1)S(1)}, bf16[1280,256]{1,0:T(8,128)(2,1)S(1)}, u32[]{:S(2)}, u32[]{:S(2)}) collective-permute-start(bf16[1280,256]{1,0:T(8,128)(2,1)S(1)} %shard_map.93), channel_id=1, source_target_pairs={{4,12},{8,0},{12,20},{16,8},{20,28},{24,16},{5,13},{9,1},{13,21},{... | collective-permute-start | bytes 1966088 | tf_op jit(solution)/shard_map/ppermute | solution.py:410
  17.3 8.0 %collective-permute-start.5 = (bf16[640,256]{1,0:T(8,128)(2,1)S(1)}, bf16[640,256]{1,0:T(8,128)(2,1)S(1)}, u32[]{:S(2)}, u32[]{:S(2)}) collective-permute-start(bf16[640,256]{1,0:T(8,128)(2,1)S(1)} %collective-permute-done.refs_0_.refs_2_), channel_id=1, source_target_pairs={{0,8},{4,0},{8,16},{12,4},{16,24},{20,12},{24,28},{28,20},{1,9},{5... | collective-permute-start | bytes 983048 | tf_op jit(solution)/shard_map/ppermute | solution.py:409
  25.3 9.6 %collective-permute-start.6 = (bf16[640,256]{1,0:T(8,128)(2,1)S(1)}, bf16[640,256]{1,0:T(8,128)(2,1)S(1)}, u32[]{:S(2)}, u32[]{:S(2)}) collective-permute-start(bf16[640,256]{1,0:T(8,128)(2,1)S(1)} %collective-permute-done.5.refs_2_), channel_id=1, source_target_pairs={{0,8},{4,0},{8,16},{12,4},{16,24},{20,12},{24,28},{28,20},{1,9},{5... | collective-permute-start | bytes 983048 | tf_op jit(solution)/shard_map/ppermute | solution.py:416
  27.8 10.9 %copy-start = (bf16[640,1280]{1,0:T(8,128)(2,1)S(1)}, bf16[640,1280]{1,0:T(8,128)(2,1)}, u32[]{:S(2)}) copy-start(bf16[640,1280]{1,0:T(8,128)(2,1)} %weight_ref.1) | copy-start | bytes 4915204
  27.8 10.9 %copy-start.1 = (bf16[256,1280]{1,0:T(8,128)(2,1)S(1)}, bf16[256,1280]{1,0:T(8,128)(2,1)}, u32[]{:S(2)}) copy-start(bf16[256,1280]{1,0:T(8,128)(2,1)} %tokens_ref.1) | copy-start | bytes 1966084
  27.8 10.9 %copy-start.4 = (s32[64]{0:T(128)S(1)}, s32[64]{0:T(128)}, u32[]{:S(2)}) copy-start(s32[64]{0:T(128)} %param.16) | copy-start | bytes 772
  27.8 10.8 %copy-start.5 = (s32[64]{0:T(128)S(1)}, s32[64]{0:T(128)}, u32[]{:S(2)}) copy-start(s32[64]{0:T(128)} %param.17) | copy-start | bytes 772
  33.3 5.4 %collective-permute-start.7 = (bf16[320,256]{1,0:T(8,128)(2,1)S(1)}, bf16[320,256]{1,0:T(8,128)(2,1)S(1)}, u32[]{:S(2)}, u32[]{:S(2)}) collective-permute-start(bf16[320,256]{1,0:T(8,128)(2,1)S(1)} %shard_map.97), channel_id=1, source_target_pairs={{0,4},{4,0},{8,12},{12,8},{16,20},{20,16},{24,28},{28,24},{1,5},{5... | collective-permute-start | bytes 491528 | tf_op jit(solution)/shard_map/ppermute | solution.py:420
  40.2 8.3 %collective-permute-start.8 = (bf16[16,5248]{1,0:T(8,128)(2,1)S(1)}, bf16[16,5248]{1,0:T(8,128)(2,1)S(1)}, u32[]{:S(2)}, u32[]{:S(2)}) collective-permute-start(bf16[16,5248]{1,0:T(8,128)(2,1)S(1)} %get-tuple-element.39), channel_id=1, source_target_pairs={{0,12},{4,8},{8,4},{12,0},{16,28},{20,24},{24,20},{28,16},{1,13},{... | collective-permute-start | bytes 503816 | tf_op jit(solution)/shard_map/ppermute | solution.py:433
  41.7 18.4 %collective-permute-start.11 = (bf16[16,5248]{1,0:T(8,128)(2,1)S(1)}, bf16[16,5248]{1,0:T(8,128)(2,1)S(1)}, u32[]{:S(2)}, u32[]{:S(2)}) collective-permute-start(bf16[16,5248]{1,0:T(8,128)(2,1)S(1)} %get-tuple-element.45), channel_id=1, source_target_pairs={{0,16},{4,20},{8,24},{12,28},{16,0},{20,4},{24,8},{28,12},{1,17},{... | collective-permute-start | bytes 503816 | tf_op jit(solution)/shard_map/ppermute | solution.py:433
  44.3 19.4 %collective-permute-start.12 = (bf16[16,5248]{1,0:T(8,128)(2,1)S(1)}, bf16[16,5248]{1,0:T(8,128)(2,1)S(1)}, u32[]{:S(2)}, u32[]{:S(2)}) collective-permute-start(bf16[16,5248]{1,0:T(8,128)(2,1)S(1)} %get-tuple-element.46), channel_id=1, source_target_pairs={{0,20},{4,16},{8,28},{12,24},{16,4},{20,0},{24,12},{28,8},{1,21},{... | collective-permute-start | bytes 503816 | tf_op jit(solution)/shard_map/ppermute | solution.py:433
  44.3 24.3 %collective-permute-start.13 = (bf16[16,5248]{1,0:T(8,128)(2,1)S(1)}, bf16[16,5248]{1,0:T(8,128)(2,1)S(1)}, u32[]{:S(2)}, u32[]{:S(2)}) collective-permute-start(bf16[16,5248]{1,0:T(8,128)(2,1)S(1)} %get-tuple-element.47), channel_id=1, source_target_pairs={{0,24},{4,28},{8,16},{12,20},{16,8},{20,12},{24,0},{28,4},{1,25},{... | collective-permute-start | bytes 503816 | tf_op jit(solution)/shard_map/ppermute | solution.py:433
  45.8 24.8 %collective-permute-start.14 = (bf16[16,5248]{1,0:T(8,128)(2,1)S(1)}, bf16[16,5248]{1,0:T(8,128)(2,1)S(1)}, u32[]{:S(2)}, u32[]{:S(2)}) collective-permute-start(bf16[16,5248]{1,0:T(8,128)(2,1)S(1)} %get-tuple-element.48), channel_id=1, source_target_pairs={{0,28},{4,24},{8,20},{12,16},{16,12},{20,8},{24,4},{28,0},{1,29},{... | collective-permute-start | bytes 503816 | tf_op jit(solution)/shard_map/ppermute | solution.py:433
  48.5 22.1 %collective-permute-start.10 = (bf16[16,5248]{1,0:T(8,128)(2,1)S(1)}, bf16[16,5248]{1,0:T(8,128)(2,1)S(1)}, u32[]{:S(2)}, u32[]{:S(2)}) collective-permute-start(bf16[16,5248]{1,0:T(8,128)(2,1)S(1)} %get-tuple-element.43), channel_id=1, source_target_pairs={{0,8},{4,12},{8,0},{12,4},{16,24},{20,28},{24,16},{28,20},{1,9},{5... | collective-permute-start | bytes 503816 | tf_op jit(solution)/shard_map/ppermute | solution.py:433
  60.0 10.6 %collective-permute-start.9 = (bf16[16,5248]{1,0:T(8,128)(2,1)S(1)}, bf16[16,5248]{1,0:T(8,128)(2,1)S(1)}, u32[]{:S(2)}, u32[]{:S(2)}) collective-permute-start(bf16[16,5248]{1,0:T(8,128)(2,1)S(1)} %get-tuple-element.42), channel_id=1, source_target_pairs={{0,4},{4,0},{8,12},{12,8},{16,20},{20,16},{24,28},{28,24},{1,5},{5... | collective-permute-start | bytes 503816 | tf_op jit(solution)/shard_map/ppermute | solution.py:433

commit v22 on v21

--- a/solution.py
+++ b/solution.py
@@ -266,16 +266,19 @@
     )(*parts)
 
 
-def project_kernel(
-    pair_rows, order, where_ref, owners_ref, offsets_ref, own_ref, other_ref, weight_ref, tokens_ref, *outs
+def half_of(where_ref, weight_ref, part, own):
+    half = where_ref[0] % 2 if own else 1 - where_ref[0] % 2
+    return weight_ref[pl.ds(pl.multiple_of(half * part, 16), part), :]
+
+
+def begin_kernel(
+    pair_rows, pieces, where_ref, owners_ref, offsets_ref, own_ref, weight_ref, tokens_ref,
+    hidden_ref, meta_ref,
 ):
-    piece = outs[0].shape[0]
-    slots = piece * len(outs)
-    rows, width = tokens_ref.shape
+    rows = tokens_ref.shape[0]
     mrows = rows // 4
-    capacity = 2 * mrows
     owner = owners_ref[...]
-    if len(outs) > 1:
+    if pieces > 1:
         owner = owner ^ where_ref[0]
     owner = jnp.broadcast_to(owner.astype(jnp.float32), (mrows, mrows))
     earlier = lax.broadcasted_iota(jnp.int32, (mrows, mrows), 0)
@@ -288,17 +291,42 @@
     row = lax.broadcasted_iota(jnp.int32, (mrows, rows), 0)
     patch = lax.broadcasted_iota(jnp.int32, (mrows, rows), 1)
     spread = jnp.where(patch // 4 == row, 1.0, 0.0).astype(jnp.bfloat16)
-    meta = jnp.dot(meta.astype(jnp.bfloat16), spread, preferred_element_type=jnp.float32)
-    part = own_ref.shape[0]
-    half = where_ref[0] % 2
-    hidden = tokens_ref[...].astype(jnp.float32)
-    for ref, which in ((own_ref, half), (other_ref, 1 - half)):
-        hidden += lax.dot_general(
-            ref[...],
-            weight_ref[pl.ds(pl.multiple_of(which * part, 16), part), :],
-            (((0,), (0,)), ((), ())),
-            preferred_element_type=jnp.float32,
-        )
+    meta_ref[...] = jnp.dot(
+        meta.astype(jnp.bfloat16), spread, preferred_element_type=jnp.float32
+    )
+    hidden_ref[...] = tokens_ref[...].astype(jnp.float32) + lax.dot_general(
+        own_ref[...],
+        half_of(where_ref, weight_ref, own_ref.shape[0], True),
+        (((0,), (0,)), ((), ())),
+        preferred_element_type=jnp.float32,
+    )
+
+
+def begin(where, owners, offsets, own, out_weight, tokens, pieces, pair_rows):
+    return pl.pallas_call(
+        functools.partial(begin_kernel, pair_rows, pieces),
+        out_shape=[
+            jax.ShapeDtypeStruct(tokens.shape, jnp.float32),
+            jax.ShapeDtypeStruct((16, tokens.shape[0]), jnp.float32),
+        ],
+        in_specs=[smem()] + [vmem()] * 5,
+        out_specs=[vmem()] * 2,
+        compiler_params=limit(24),
+    )(where, owners, offsets, own, out_weight, tokens)
+
+
+def project_kernel(order, where_ref, hidden_ref, meta_ref, other_ref, weight_ref, *outs):
+    piece = outs[0].shape[0]
+    slots = piece * len(outs)
+    rows, width = hidden_ref.shape
+    capacity = rows // 2
+    meta = meta_ref[...]
+    hidden = hidden_ref[...] + lax.dot_general(
+        other_ref[...],
+        half_of(where_ref, weight_ref, other_ref.shape[0], False),
+        (((0,), (0,)), ((), ())),
+        preferred_element_type=jnp.float32,
+    )
     hidden = hidden.astype(jnp.bfloat16)
     slot = lax.broadcasted_iota(jnp.int32, (slots, rows), 0).astype(jnp.float32)
     quarter = lax.broadcasted_iota(jnp.int32, (1, rows), 1) % 4
@@ -316,16 +344,16 @@
             out[:, j * width : (j + 1) * width] = picked[d * piece : (d + 1) * piece]
 
 
-def project(where, owners, offsets, own, other, out_weight, tokens, order, slots, pair_rows):
-    rows, width = tokens.shape
+def project(where, hidden, meta, other, out_weight, order, slots):
+    width = hidden.shape[1]
     pieces = len(order)
     return pl.pallas_call(
-        functools.partial(project_kernel, pair_rows, order),
+        functools.partial(project_kernel, order),
         out_shape=[jax.ShapeDtypeStruct((slots // pieces, 4 * width + 128), jnp.bfloat16)] * pieces,
-        in_specs=[smem()] + [vmem()] * 6,
+        in_specs=[smem()] + [vmem()] * 4,
         out_specs=[vmem()] * pieces,
         compiler_params=limit(24),
-    )(where, owners, offsets, own, other, out_weight, tokens)
+    )(where, hidden, meta, other, out_weight)
 
 
 def place_kernel(*refs):
@@ -414,18 +442,19 @@
     own = attention(*fixed, (own_q,), (0,), near, near_numbers, None, False)
     back_other, own = lax.optimization_barrier((back_other, own))
     back_far = relay(back_other)
-    other = attention(*fixed, (other_q,), (1,), near, near_numbers, None, False)
-    far = (ahead_both, back_other)
-    other = attention(*fixed, (other_q,), (1,), far, (4, 6, 5), other, True)
+    other = attention(
+        *fixed, (other_q,), (1,), (*near, back_other), (*near_numbers, 5), None, False
+    )
+    other = attention(*fixed, (other_q,), (1,), (ahead_both,), (4, 6), other, True)
     other = swap(other)
     far = (ahead_both, back_other, back_far)
     own = attention(*fixed, (own_q,), (0,), far, (4, 6, 5, 7), own, True)
 
     order = tuple(range(nblocks)) if nblocks in (4, 8) else (0,)
-    outgoing = project(
-        where, owners[None, :], offsets[None, :], own, other, out_weight, tokens,
-        order, slots, pair_rows,
-    )
+    hidden, meta = begin(
+        where, owners[None, :], offsets[None, :], own, out_weight, tokens, len(order), pair_rows
+    )
+    outgoing = project(where, hidden, meta, other, out_weight, order, slots)
     if len(order) > 1:
         arrived = list(outgoing)
 

time: 73.2 us -> 72.7 us (level)
  starting transfers between devices: 24.9 us -> 21.1 us
  waiting for transfers between devices: 32.9 us -> 35.6 us
    ppermute x7, starting transfers between devices: 10.8 us -> 8.54 us  [cross(): lax.ppermute(arrived[d], 'blk', [(i, i ^ d) for i in range(nblocks)])]
    ppermute x7, waiting for transfers between devices: 19.6 us -> 21.6 us  [cross(): lax.ppermute(arrived[d], 'blk', [(i, i ^ d) for i in range(nblocks)])]
    ppermute x1, starting transfers between devices: 1.59 us -> 0.07 us  [per_device(): other = swap(other)]
    ppermute x1, waiting for transfers between devices: 1.79 us -> 2.63 us  [per_device(): other = swap(other)]
    pallas_call x1 -> x2, Pallas kernels: 1.48 us -> 1.61 us  [the longest x1 1 us: project(): pl.pallas_call(functools.partial(project_kernel, order), out_shape=[jax.S...]
  transfers between devices with their start and end apart: 15 -> 15, of which waited for: 10 -> 10; matrix products, arithmetic and copies ran while one was open for 0% -> 0% of each run, Pallas kernels for 13% -> 14%
where the time goes in v22:
time: 72.7 us; the launch traced here: 71.3 us
  waiting for transfers between devices  35.6 us (49%)
  starting transfers between devices  21.1 us (29%)
  Pallas kernels  14.2 us (20%)
    ppermute x7, waiting for transfers between devices, cross(): lax.ppermute(arrived[d], 'blk', [(i, i ^ d) for i in range(nblocks)])  21.6 us
    ppermute x7, starting transfers between devices, cross(): lax.ppermute(arrived[d], 'blk', [(i, i ^ d) for i in range(nblocks)])  8.54 us
    pallas_call x4, Pallas kernels, attention(): pl.pallas_call(functools.partial(attention_kernel, kinds, numbers, rows_o...  8.3 us
    ppermute x1, waiting for transfers between devices, per_device(): back_other = relay(ready)  4.76 us
    ppermute x1, starting transfers between devices, per_device(): ahead_both = ahead(stack(other_kv, ahead_own))  3.48 us
    ppermute x1, starting transfers between devices, per_device(): ahead_own = ahead(own_kv)  3.47 us
    ppermute x1, waiting for transfers between devices, per_device(): ahead_both = ahead(stack(other_kv, ahead_own))  2.96 us
    ppermute x1, waiting for transfers between devices, per_device(): other_kv = swap(swap_kv)  2.87 us
  transfers between devices with their start and end apart: 15, of which 10 were waited for; matrix products, arithmetic and copies ran while one was open for 0% of the time, Pallas kernels for 14%

profile of v22, /device:TPU:14, one launch (start us, length us, event | category | flops | bytes accessed | tf_op | source)
XLA Modules:
  0.0 71.3 jit_solution(15322986990472101105)
XLA Ops:
  0.0 2.1 %shard_map.92 = (bf16[320,256]{1,0:T(8,128)(2,1)S(1)}, bf16[640,256]{1,0:T(8,128)(2,1)S(1)}, bf16[320,256]{1,0:T(8,128)(2,1)S(1)}, bf16[640,256]{1,0:T(8,128)(2,1)}) custom-call(s32[1]{0:T(128)} %bitcast.where_ref, bf16[256,640]{1,0:T(8,128)(2,1)} %q_hbm.1, bf16[256,640]{1,0:T(8,128)(2,1)} %k_hbm.1, bf16[256,640]{1,0:T(8,128)(2,1)} %v_hbm.1), custom_call_target="tpu_custom_call" | custom-call | tf_op jit(solution)/shard_map/pallas_call | solution.py:74
  2.7 3.5 %collective-permute-start.1 = (bf16[640,256]{1,0:T(8,128)(2,1)S(1)}, bf16[640,256]{1,0:T(8,128)(2,1)S(1)}, u32[]{:S(2)}, u32[]{:S(2)}) collective-permute-start(bf16[640,256]{1,0:T(8,128)(2,1)S(1)} %get-tuple-element.33.refs_1_), channel_id=1, source_target_pairs={{4,12},{8,0},{12,20},{16,8},{20,28},{24,16},{5,13},{9,1},{13,21},{... | collective-permute-start | bytes 983048 | tf_op jit(solution)/shard_map/ppermute | solution.py:433
  6.2 2.4 %collective-permute-start.3 = (bf16[640,256]{1,0:T(8,128)(2,1)S(1)}, bf16[640,256]{1,0:T(8,128)(2,1)S(1)}, u32[]{:S(2)}, u32[]{:S(2)}) collective-permute-start(bf16[640,256]{1,0:T(8,128)(2,1)S(1)} %get-tuple-element.33.refs_1_), channel_id=1, source_target_pairs={{0,8},{8,16},{12,4},{16,24},{20,12},{28,20},{1,9},{9,17},{13,5},{1... | collective-permute-start | bytes 983048 | tf_op jit(solution)/shard_map/ppermute | solution.py:434
  8.5 1.6 %collective-permute-start.4 = (bf16[320,256]{1,0:T(8,128)(2,1)S(1)}, bf16[320,256]{1,0:T(8,128)(2,1)S(1)}, u32[]{:S(2)}, u32[]{:S(2)}) collective-permute-start(bf16[320,256]{1,0:T(8,128)(2,1)S(1)} %get-tuple-element.34), channel_id=1, source_target_pairs={{0,4},{4,0},{8,12},{12,8},{16,20},{20,16},{24,28},{28,24},{1,5},{5... | collective-permute-start | bytes 491528 | tf_op jit(solution)/shard_map/ppermute | solution.py:435
  10.1 2.9 %collective-permute-done.refs_0_.refs_2_ = bf16[640,256]{1,0:T(8,128)(2,1)S(1)} collective-permute-done((bf16[640,256]{1,0:T(8,128)(2,1)}, bf16[640,256]{1,0:T(8,128)(2,1)S(1)}, u32[]{:S(2)}, u32[]{:S(2)}) %collective-permute-start) | collective-permute-done | bytes 327712 | tf_op jit(solution)/shard_map/ppermute | solution.py:432
  13.8 3.5 %collective-permute-start.2 = (bf16[1280,256]{1,0:T(8,128)(2,1)S(1)}, bf16[1280,256]{1,0:T(8,128)(2,1)S(1)}, u32[]{:S(2)}, u32[]{:S(2)}) collective-permute-start(bf16[1280,256]{1,0:T(8,128)(2,1)S(1)} %shard_map.93), channel_id=1, source_target_pairs={{4,12},{8,0},{12,20},{16,8},{20,28},{24,16},{5,13},{9,1},{13,21},{... | collective-permute-start | bytes 1966088 | tf_op jit(solution)/shard_map/ppermute | solution.py:438
  18.6 2.0 %shard_map.94.refs_4_ = f32[1,4,256,128]{3,2,1,0:T(8,128)S(1)} custom-call(s32[1]{0:T(128)} %bitcast.where_ref, s32[8,128]{1,0:T(8,128)S(1)} %get-tuple-element.29.need_ref, f32[1,2048]{1,0:T(1,128)S(1)} %get-tuple-element.30.seg_ref, bf16[320,256]{1,0:T(8,128)(2,1)S(1)} %get-tuple-element.31.refs_0_, bf16[640,256]{1,0:T(8,128)(2,1)S(1)} %get-tuple-element.33.refs_1_, ...), custom_call_target="tpu_custom_call" | custom-call | flops 1000 | bytes 1000 | tf_op jit(solution)/shard_map/pallas_call | solution.py:234
  20.6 4.8 %collective-permute-done.5.refs_2_.refs_5_ = bf16[640,256]{1,0:T(8,128)(2,1)S(1)} collective-permute-done((bf16[640,256]{1,0:T(8,128)(2,1)S(1)}, bf16[640,256]{1,0:T(8,128)(2,1)S(1)}, u32[]{:S(2)}, u32[]{:S(2)}) %collective-permute-start.5) | collective-permute-done | bytes 327712 | tf_op jit(solution)/shard_map/ppermute | solution.py:437
  25.8 2.2 %shard_map.97.refs_2_ = f32[1,4,256,128]{3,2,1,0:T(8,128)S(1)} custom-call(s32[1]{0:T(128)} %bitcast.where_ref, s32[8,128]{1,0:T(8,128)S(1)} %get-tuple-element.29.need_ref, f32[1,2048]{1,0:T(1,128)S(1)} %get-tuple-element.30.seg_ref, bf16[320,256]{1,0:T(8,128)(2,1)S(1)} %collective-permute-done.4.refs_0_, bf16[640,256]{1,0:T(8,128)(2,1)S(1)} %get-tuple-element.33.refs_1_, ...), custom_call_target="tpu_custom_call" | custom-call | flops 1000 | bytes 1000 | tf_op jit(solution)/shard_map/pallas_call | solution.py:234
  28.0 3.0 %collective-permute-done.2.refs_1_ = bf16[1280,256]{1,0:T(8,128)(2,1)S(1)} collective-permute-done((bf16[1280,256]{1,0:T(8,128)(2,1)S(1)}, bf16[1280,256]{1,0:T(8,128)(2,1)S(1)}, u32[]{:S(2)}, u32[]{:S(2)}) %collective-permute-start.2) | collective-permute-done | bytes 655392 | tf_op jit(solution)/shard_map/ppermute | solution.py:438
  31.0 2.1 %shard_map.98 = bf16[320,256]{1,0:T(8,128)(2,1)S(1)} custom-call(s32[1]{0:T(128)} %bitcast.where_ref, s32[8,128]{1,0:T(8,128)S(1)} %get-tuple-element.29.need_ref, f32[1,2048]{1,0:T(1,128)S(1)} %get-tuple-element.30.seg_ref, bf16[320,256]{1,0:T(8,128)(2,1)S(1)} %collective-permute-done.4.refs_0_, bf16[1280,256]{1,0:T(8,128)(2,1)S(1)} %collective-permute-done.2.refs_1_, ...), custom_call_target="tpu_custom_call" | custom-call | flops 1000 | bytes 1000 | tf_op jit(solution)/shard_map/pallas_call | solution.py:234
  33.2 2.0 %shard_map.95.own_ref = bf16[320,256]{1,0:T(8,128)(2,1)S(1)} custom-call(s32[1]{0:T(128)} %bitcast.where_ref, s32[8,128]{1,0:T(8,128)S(1)} %get-tuple-element.29.need_ref, f32[1,2048]{1,0:T(1,128)S(1)} %get-tuple-element.30.seg_ref, bf16[320,256]{1,0:T(8,128)(2,1)S(1)} %get-tuple-element.31.refs_0_, bf16[1280,256]{1,0:T(8,128)(2,1)S(1)} %collective-permute-done.2.refs_1_, ...), custom_call_target="tpu_custom_call" | custom-call | flops 1000 | bytes 1000 | tf_op jit(solution)/shard_map/pallas_call | solution.py:234
  35.9 2.6 %collective-permute-done.7.other_ref = bf16[320,256]{1,0:T(8,128)(2,1)S(1)} collective-permute-done((bf16[320,256]{1,0:T(8,128)(2,1)S(1)}, bf16[320,256]{1,0:T(8,128)(2,1)S(1)}, u32[]{:S(2)}, u32[]{:S(2)}) %collective-permute-start.7) | collective-permute-done | bytes 163872 | tf_op jit(solution)/shard_map/ppermute | solution.py:449
  38.5 1.0 %shard_map.99 = (bf16[16,5248]{1,0:T(8,128)(2,1)S(1)}, bf16[16,5248]{1,0:T(8,128)(2,1)S(1)}, bf16[16,5248]{1,0:T(8,128)(2,1)S(1)}, bf16[16,5248]{1,0:T(8,128)(2,...) custom-call(s32[1]{0:T(128)} %bitcast.where_ref, ...), custom_call_target="tpu_custom_call" | custom-call | tf_op jit(solution)/shard_map/pallas_call | solution.py:350
  39.5 1.5 %collective-permute-start.8 = (bf16[16,5248]{1,0:T(8,128)(2,1)S(1)}, bf16[16,5248]{1,0:T(8,128)(2,1)S(1)}, u32[]{:S(2)}, u32[]{:S(2)}) collective-permute-start(bf16[16,5248]{1,0:T(8,128)(2,1)S(1)} %get-tuple-element.43), channel_id=1, source_target_pairs={{0,12},{4,8},{8,4},{12,0},{16,28},{20,24},{24,20},{28,16},{1,13},{... | collective-permute-start | bytes 503816 | tf_op jit(solution)/shard_map/ppermute | solution.py:462
  41.0 1.3 %collective-permute-start.11 = (bf16[16,5248]{1,0:T(8,128)(2,1)S(1)}, bf16[16,5248]{1,0:T(8,128)(2,1)S(1)}, u32[]{:S(2)}, u32[]{:S(2)}) collective-permute-start(bf16[16,5248]{1,0:T(8,128)(2,1)S(1)} %get-tuple-element.49), channel_id=1, source_target_pairs={{0,16},{4,20},{8,24},{12,28},{16,0},{20,4},{24,8},{28,12},{1,17},{... | collective-permute-start | bytes 503816 | tf_op jit(solution)/shard_map/ppermute | solution.py:462
  42.3 1.1 %collective-permute-start.12 = (bf16[16,5248]{1,0:T(8,128)(2,1)S(1)}, bf16[16,5248]{1,0:T(8,128)(2,1)S(1)}, u32[]{:S(2)}, u32[]{:S(2)}) collective-permute-start(bf16[16,5248]{1,0:T(8,128)(2,1)S(1)} %get-tuple-element.50), channel_id=1, source_target_pairs={{0,20},{4,16},{8,28},{12,24},{16,4},{20,0},{24,12},{28,8},{1,21},{... | collective-permute-start | bytes 503816 | tf_op jit(solution)/shard_map/ppermute | solution.py:462
  43.4 3.2 %collective-permute-start.13 = (bf16[16,5248]{1,0:T(8,128)(2,1)S(1)}, bf16[16,5248]{1,0:T(8,128)(2,1)S(1)}, u32[]{:S(2)}, u32[]{:S(2)}) collective-permute-start(bf16[16,5248]{1,0:T(8,128)(2,1)S(1)} %get-tuple-element.51), channel_id=1, source_target_pairs={{0,24},{4,28},{8,16},{12,20},{16,8},{20,12},{24,0},{28,4},{1,25},{... | collective-permute-start | bytes 503816 | tf_op jit(solution)/shard_map/ppermute | solution.py:462
  47.7 1.2 %collective-permute-start.10 = (bf16[16,5248]{1,0:T(8,128)(2,1)S(1)}, bf16[16,5248]{1,0:T(8,128)(2,1)S(1)}, u32[]{:S(2)}, u32[]{:S(2)}) collective-permute-start(bf16[16,5248]{1,0:T(8,128)(2,1)S(1)} %get-tuple-element.47), channel_id=1, source_target_pairs={{0,8},{4,12},{8,0},{12,4},{16,24},{20,28},{24,16},{28,20},{1,9},{5... | collective-permute-start | bytes 503816 | tf_op jit(solution)/shard_map/ppermute | solution.py:462
  48.9 10.4 %collective-permute-done.11.refs_4_ = bf16[16,5248]{1,0:T(8,128)(2,1)S(1)} collective-permute-done((bf16[16,5248]{1,0:T(8,128)(2,1)S(1)}, bf16[16,5248]{1,0:T(8,128)(2,1)S(1)}, u32[]{:S(2)}, u32[]{:S(2)}) %collective-permute-start.11) | collective-permute-done | bytes 167968 | tf_op jit(solution)/shard_map/ppermute | solution.py:462
  59.4 3.6 %collective-permute-done.12.refs_5_ = bf16[16,5248]{1,0:T(8,128)(2,1)S(1)} collective-permute-done((bf16[16,5248]{1,0:T(8,128)(2,1)S(1)}, bf16[16,5248]{1,0:T(8,128)(2,1)S(1)}, u32[]{:S(2)}, u32[]{:S(2)}) %collective-permute-start.12) | collective-permute-done | bytes 167968 | tf_op jit(solution)/shard_map/ppermute | solution.py:462
  63.0 3.8 %collective-permute-done.13.refs_6_ = bf16[16,5248]{1,0:T(8,128)(2,1)S(1)} collective-permute-done((bf16[16,5248]{1,0:T(8,128)(2,1)S(1)}, bf16[16,5248]{1,0:T(8,128)(2,1)S(1)}, u32[]{:S(2)}, u32[]{:S(2)}) %collective-permute-start.13) | collective-permute-done | bytes 167968 | tf_op jit(solution)/shard_map/ppermute | solution.py:462
  66.7 3.0 %collective-permute-done.14.refs_7_ = bf16[16,5248]{1,0:T(8,128)(2,1)S(1)} collective-permute-done((bf16[16,5248]{1,0:T(8,128)(2,1)S(1)}, bf16[16,5248]{1,0:T(8,128)(2,1)S(1)}, u32[]{:S(2)}, u32[]{:S(2)}) %collective-permute-start.14) | collective-permute-done | bytes 167968 | tf_op jit(solution)/shard_map/ppermute | solution.py:462
  69.7 1.5 %shard_map.100 = bf16[128,5120]{1,0:T(8,128)(2,1)} custom-call(bf16[16,5248]{1,0:T(8,128)(2,1)S(1)} %get-tuple-element.42.refs_0_, bf16[16,5248]{1,0:T(8,128)(2,1)S(1)} %collective-permute-done.9.refs_1_, bf16[16,5248]{1,0:T(8,128)(2,1)S(1)} %collective-permute-done.10.refs_2_, bf16[16,5248]{1,0:T(8,128)(2,1)S(1)} %collective-permute-done.8.refs_3_, ...), custom_call_target="tpu_custom_call" | custom-call | tf_op jit(solution)/shard_map/pallas_call | solution.py:386
  (28 shorter events, 5.0 us)
Async XLA Ops:
  0.0 17.8 %copy-start.2 = (s32[2048]{0:T(1024)S(1)}, s32[2048]{0:T(1024)}, u32[]{:S(2)}) copy-start(s32[2048]{0:T(1024)} %param.9) | copy-start | bytes 24580
  0.0 17.8 %copy-start.3 = (s32[8,8]{1,0:T(8,128)S(1)}, s32[8,8]{1,0:T(8,128)}, u32[]{:S(2)}) copy-start(s32[8,8]{1,0:T(8,128)} %mask_ref.1) | copy-start | bytes 772
  2.1 10.9 %collective-permute-start = (bf16[640,256]{1,0:T(8,128)(2,1)}, bf16[640,256]{1,0:T(8,128)(2,1)S(1)}, u32[]{:S(2)}, u32[]{:S(2)}) collective-permute-start(bf16[640,256]{1,0:T(8,128)(2,1)} %get-tuple-element.32), channel_id=1, source_target_pairs={{0,4},{4,0},{8,12},{12,8},{16,20},{20,16},{24,28},{28,24},{1,5},{5... | collective-permute-start | bytes 983048 | tf_op jit(solution)/shard_map/ppermute | solution.py:432
  2.7 11.1 %collective-permute-start.1 = (bf16[640,256]{1,0:T(8,128)(2,1)S(1)}, bf16[640,256]{1,0:T(8,128)(2,1)S(1)}, u32[]{:S(2)}, u32[]{:S(2)}) collective-permute-start(bf16[640,256]{1,0:T(8,128)(2,1)S(1)} %get-tuple-element.33.refs_1_), channel_id=1, source_target_pairs={{4,12},{8,0},{12,20},{16,8},{20,28},{24,16},{5,13},{9,1},{13,21},{... | collective-permute-start | bytes 983048 | tf_op jit(solution)/shard_map/ppermute | solution.py:433
  6.2 11.1 %collective-permute-start.3 = (bf16[640,256]{1,0:T(8,128)(2,1)S(1)}, bf16[640,256]{1,0:T(8,128)(2,1)S(1)}, u32[]{:S(2)}, u32[]{:S(2)}) collective-permute-start(bf16[640,256]{1,0:T(8,128)(2,1)S(1)} %get-tuple-element.33.refs_1_), channel_id=1, source_target_pairs={{0,8},{8,16},{12,4},{16,24},{20,12},{28,20},{1,9},{9,17},{13,5},{1... | collective-permute-start | bytes 983048 | tf_op jit(solution)/shard_map/ppermute | solution.py:434
  8.5 8.7 %collective-permute-start.4 = (bf16[320,256]{1,0:T(8,128)(2,1)S(1)}, bf16[320,256]{1,0:T(8,128)(2,1)S(1)}, u32[]{:S(2)}, u32[]{:S(2)}) collective-permute-start(bf16[320,256]{1,0:T(8,128)(2,1)S(1)} %get-tuple-element.34), channel_id=1, source_target_pairs={{0,4},{4,0},{8,12},{12,8},{16,20},{20,16},{24,28},{28,24},{1,5},{5... | collective-permute-start | bytes 491528 | tf_op jit(solution)/shard_map/ppermute | solution.py:435
  13.8 17.2 %collective-permute-start.2 = (bf16[1280,256]{1,0:T(8,128)(2,1)S(1)}, bf16[1280,256]{1,0:T(8,128)(2,1)S(1)}, u32[]{:S(2)}, u32[]{:S(2)}) collective-permute-start(bf16[1280,256]{1,0:T(8,128)(2,1)S(1)} %shard_map.93), channel_id=1, source_target_pairs={{4,12},{8,0},{12,20},{16,8},{20,28},{24,16},{5,13},{9,1},{13,21},{... | collective-permute-start | bytes 1966088 | tf_op jit(solution)/shard_map/ppermute | solution.py:438
  17.3 8.0 %collective-permute-start.5 = (bf16[640,256]{1,0:T(8,128)(2,1)S(1)}, bf16[640,256]{1,0:T(8,128)(2,1)S(1)}, u32[]{:S(2)}, u32[]{:S(2)}) collective-permute-start(bf16[640,256]{1,0:T(8,128)(2,1)S(1)} %collective-permute-done.refs_0_.refs_2_), channel_id=1, source_target_pairs={{0,8},{4,0},{8,16},{12,4},{16,24},{20,12},{24,28},{28,20},{1,9},{5... | collective-permute-start | bytes 983048 | tf_op jit(solution)/shard_map/ppermute | solution.py:437
  25.3 7.9 %collective-permute-start.6 = (bf16[640,256]{1,0:T(8,128)(2,1)S(1)}, bf16[640,256]{1,0:T(8,128)(2,1)S(1)}, u32[]{:S(2)}, u32[]{:S(2)}) collective-permute-start(bf16[640,256]{1,0:T(8,128)(2,1)S(1)} %collective-permute-done.5.refs_2_.refs_5_), channel_id=1, source_target_pairs={{0,8},{4,0},{8,16},{12,4},{16,24},{20,12},{24,28},{28,20},{1,9},{5... | collective-permute-start | bytes 983048 | tf_op jit(solution)/shard_map/ppermute | solution.py:444
  31.0 4.3 %copy-start.1 = (bf16[256,1280]{1,0:T(8,128)(2,1)S(1)}, bf16[256,1280]{1,0:T(8,128)(2,1)}, u32[]{:S(2)}) copy-start(bf16[256,1280]{1,0:T(8,128)(2,1)} %tokens_ref.1) | copy-start | bytes 1966084
  33.1 2.1 %copy-start = (bf16[640,1280]{1,0:T(8,128)(2,1)S(1)}, bf16[640,1280]{1,0:T(8,128)(2,1)}, u32[]{:S(2)}) copy-start(bf16[640,1280]{1,0:T(8,128)(2,1)} %weight_ref.3) | copy-start | bytes 4915204
  33.1 2.1 %copy-start.4 = (s32[64]{0:T(128)S(1)}, s32[64]{0:T(128)}, u32[]{:S(2)}) copy-start(s32[64]{0:T(128)} %param.16) | copy-start | bytes 772
  33.1 2.1 %copy-start.5 = (s32[64]{0:T(128)S(1)}, s32[64]{0:T(128)}, u32[]{:S(2)}) copy-start(s32[64]{0:T(128)} %param.17) | copy-start | bytes 772
  33.1 5.4 %collective-permute-start.7 = (bf16[320,256]{1,0:T(8,128)(2,1)S(1)}, bf16[320,256]{1,0:T(8,128)(2,1)S(1)}, u32[]{:S(2)}, u32[]{:S(2)}) collective-permute-start(bf16[320,256]{1,0:T(8,128)(2,1)S(1)} %shard_map.98), channel_id=1, source_target_pairs={{0,4},{4,0},{8,12},{12,8},{16,20},{20,16},{24,28},{28,24},{1,5},{5... | collective-permute-start | bytes 491528 | tf_op jit(solution)/shard_map/ppermute | solution.py:449
  39.5 8.2 %collective-permute-start.8 = (bf16[16,5248]{1,0:T(8,128)(2,1)S(1)}, bf16[16,5248]{1,0:T(8,128)(2,1)S(1)}, u32[]{:S(2)}, u32[]{:S(2)}) collective-permute-start(bf16[16,5248]{1,0:T(8,128)(2,1)S(1)} %get-tuple-element.43), channel_id=1, source_target_pairs={{0,12},{4,8},{8,4},{12,0},{16,28},{20,24},{24,20},{28,16},{1,13},{... | collective-permute-start | bytes 503816 | tf_op jit(solution)/shard_map/ppermute | solution.py:462
  41.0 18.3 %collective-permute-start.11 = (bf16[16,5248]{1,0:T(8,128)(2,1)S(1)}, bf16[16,5248]{1,0:T(8,128)(2,1)S(1)}, u32[]{:S(2)}, u32[]{:S(2)}) collective-permute-start(bf16[16,5248]{1,0:T(8,128)(2,1)S(1)} %get-tuple-element.49), channel_id=1, source_target_pairs={{0,16},{4,20},{8,24},{12,28},{16,0},{20,4},{24,8},{28,12},{1,17},{... | collective-permute-start | bytes 503816 | tf_op jit(solution)/shard_map/ppermute | solution.py:462
  42.3 20.7 %collective-permute-start.12 = (bf16[16,5248]{1,0:T(8,128)(2,1)S(1)}, bf16[16,5248]{1,0:T(8,128)(2,1)S(1)}, u32[]{:S(2)}, u32[]{:S(2)}) collective-permute-start(bf16[16,5248]{1,0:T(8,128)(2,1)S(1)} %get-tuple-element.50), channel_id=1, source_target_pairs={{0,20},{4,16},{8,28},{12,24},{16,4},{20,0},{24,12},{28,8},{1,21},{... | collective-permute-start | bytes 503816 | tf_op jit(solution)/shard_map/ppermute | solution.py:462
  43.4 23.3 %collective-permute-start.13 = (bf16[16,5248]{1,0:T(8,128)(2,1)S(1)}, bf16[16,5248]{1,0:T(8,128)(2,1)S(1)}, u32[]{:S(2)}, u32[]{:S(2)}) collective-permute-start(bf16[16,5248]{1,0:T(8,128)(2,1)S(1)} %get-tuple-element.51), channel_id=1, source_target_pairs={{0,24},{4,28},{8,16},{12,20},{16,8},{20,12},{24,0},{28,4},{1,25},{... | collective-permute-start | bytes 503816 | tf_op jit(solution)/shard_map/ppermute | solution.py:462
  46.6 23.1 %collective-permute-start.14 = (bf16[16,5248]{1,0:T(8,128)(2,1)S(1)}, bf16[16,5248]{1,0:T(8,128)(2,1)S(1)}, u32[]{:S(2)}, u32[]{:S(2)}) collective-permute-start(bf16[16,5248]{1,0:T(8,128)(2,1)S(1)} %get-tuple-element.52), channel_id=1, source_target_pairs={{0,28},{4,24},{8,20},{12,16},{16,12},{20,8},{24,4},{28,0},{1,29},{... | collective-permute-start | bytes 503816 | tf_op jit(solution)/shard_map/ppermute | solution.py:462
  47.7 22.0 %collective-permute-start.10 = (bf16[16,5248]{1,0:T(8,128)(2,1)S(1)}, bf16[16,5248]{1,0:T(8,128)(2,1)S(1)}, u32[]{:S(2)}, u32[]{:S(2)}) collective-permute-start(bf16[16,5248]{1,0:T(8,128)(2,1)S(1)} %get-tuple-element.47), channel_id=1, source_target_pairs={{0,8},{4,12},{8,0},{12,4},{16,24},{20,28},{24,16},{28,20},{1,9},{5... | collective-permute-start | bytes 503816 | tf_op jit(solution)/shard_map/ppermute | solution.py:462
  59.4 10.3 %collective-permute-start.9 = (bf16[16,5248]{1,0:T(8,128)(2,1)S(1)}, bf16[16,5248]{1,0:T(8,128)(2,1)S(1)}, u32[]{:S(2)}, u32[]{:S(2)}) collective-permute-start(bf16[16,5248]{1,0:T(8,128)(2,1)S(1)} %get-tuple-element.46), channel_id=1, source_target_pairs={{0,4},{4,0},{8,12},{12,8},{16,20},{20,16},{24,28},{28,24},{1,5},{5... | collective-permute-start | bytes 503816 | tf_op jit(solution)/shard_map/ppermute | solution.py:462

commit v23 on v22

--- a/solution.py
+++ b/solution.py
@@ -43,46 +43,40 @@
     return me - half - SPAN + PLACES[number][0] + PLACES[number][1] * half
 
 
-def prepare_kernel(where_ref, q_hbm, k_hbm, v_hbm, own_q, own_kv, swap_q, swap_kv, held, turned, sems):
-    part = q_hbm.shape[1] // 2
+def prepare_kernel(number, where_ref, *refs):
+    sources, (own, swap, held, turned, sems) = refs[:number], refs[number:]
+    part = held.shape[2] // 2
     loads = [
-        pltpu.make_async_copy(ref, held.at[i], sems.at[i])
-        for i, ref in enumerate((k_hbm, v_hbm, q_hbm))
+        pltpu.make_async_copy(ref, held.at[i], sems.at[i]) for i, ref in enumerate(sources)
     ]
     for load in loads:
         load.start()
-    me = where_ref[0]
-    half = me % 2
+    half = where_ref[0] % 2
     mine = pl.multiple_of(half * part, 16)
     other = pl.multiple_of((1 - half) * part, 16)
-    for i in range(3):
+    for i in range(number):
         loads[i].wait()
         turned[i] = held[i].T
-        if i < 2:
-            own_kv[i * part : (i + 1) * part, :] = turned[i, pl.ds(mine, part), :]
-            swap_kv[i * part : (i + 1) * part, :] = turned[i, pl.ds(other, part), :]
-        else:
-            own_q[...] = turned[i, pl.ds(mine, part), :]
-            swap_q[...] = turned[i, pl.ds(other, part), :]
-
-
-def prepare(where, queries, keys, values):
-    rows, features = queries.shape
-    part = features // 2
-    single = jax.ShapeDtypeStruct((part, rows), queries.dtype)
-    double = jax.ShapeDtypeStruct((2 * part, rows), queries.dtype)
-    return pl.pallas_call(
-        prepare_kernel,
-        out_shape=[single, double, single, double],
-        in_specs=[smem()] + [anywhere()] * 3,
-        out_specs=[vmem()] * 4,
+        own[i * part : (i + 1) * part, :] = turned[i, pl.ds(mine, part), :]
+        swap[i * part : (i + 1) * part, :] = turned[i, pl.ds(other, part), :]
+
+
+def prepare(where, *arrays):
+    number = len(arrays)
+    rows, features = arrays[0].shape
+    out = jax.ShapeDtypeStruct((number * features // 2, rows), arrays[0].dtype)
+    return pl.pallas_call(
+        functools.partial(prepare_kernel, number),
+        out_shape=[out] * 2,
+        in_specs=[smem()] + [anywhere()] * number,
+        out_specs=[vmem()] * 2,
         scratch_shapes=[
-            pltpu.VMEM((3, rows, features), queries.dtype),
-            pltpu.VMEM((3, features, rows), queries.dtype),
-            pltpu.SemaphoreType.DMA((3,)),
+            pltpu.VMEM((number, rows, features), arrays[0].dtype),
+            pltpu.VMEM((number, features, rows), arrays[0].dtype),
+            pltpu.SemaphoreType.DMA((number,)),
         ],
         compiler_params=limit(53),
-    )(where, queries, keys, values)
+    )(where, *arrays)
 
 
 def survey_kernel(where_ref, mask_ref, segs_ref, seg_out, need_out):
@@ -118,8 +112,11 @@
     arrays = max(array for array, _ in rows_of) + 1
     blocks, refs = refs[:arrays], refs[arrays:]
     if follows:
-        before, refs = refs[0], refs[1:]
-    out_ref, query_s, key_s, value_s, chosen_s = refs
+        (accum_b, peak_b), refs = refs[:2], refs[2:]
+    if ends:
+        out_ref, query_s, key_s, value_s, chosen_s = refs
+    else:
+        accum_ref, peak_ref, query_s, key_s, value_s, chosen_s = refs
     part, rows = queries[0].shape
     hdim = part // HALF
     wide = value_s.shape[2]
@@ -165,16 +162,15 @@
                 lines = slice(h * hdim, (h + 1) * hdim)
                 out_ref[lines, :] = (turned[:hdim] / turned[hdim : hdim + 1]).astype(out_ref.dtype)
             else:
-                peak = jnp.broadcast_to(peak, (rows, 128 - wide))
-                out_ref[n, h] = jnp.concatenate([accum, peak], axis=1)
+                accum_ref[n, h] = accum
+                peak_ref[n, h] = peak
 
         if follows:
 
             @pl.when(size == 0)
             def _():
                 for h in range(HALF):
-                    state = before[0, h]
-                    finish(h, state[:, wide : wide + 1], state[:, :wide])
+                    finish(h, peak_b[0, h], accum_b[0, h])
 
         for fixed in range(1, len(numbers) + 1):
 
@@ -197,14 +193,15 @@
                         scores.append(jnp.where(query_seg == key_seg, score, NEG))
                     peak = functools.reduce(jnp.maximum, scores)
                     peak = jnp.max(peak, axis=1, keepdims=True)
+                    peak = jnp.broadcast_to(peak, (rows, wide))
                     accum = jnp.zeros((rows, wide), jnp.float32)
                     if follows:
-                        state = before[0, h]
-                        old = state[:, wide : wide + 1]
+                        old = peak_b[0, h]
                         peak = jnp.maximum(peak, old)
-                        accum = state[:, :wide] * jnp.exp2((old - peak) * factor)
+                        accum = accum_b[0, h] * jnp.exp2((old - peak) * factor)
+                    spread = jnp.concatenate([peak] * (rows // wide), axis=1)
                     for b, score in zip(picked, scores):
-                        weights = jnp.exp2((score - peak) * factor).astype(jnp.bfloat16)
+                        weights = jnp.exp2((score - spread) * factor).astype(jnp.bfloat16)
                         accum += lax.dot_general(
                             weights,
                             value_s[b, h],
@@ -220,7 +217,7 @@
 def attention(where, need, segs, queries, kinds, blocks, numbers, before, ends):
     part, rows = queries[0].shape
     hdim = part // HALF
-    wide = hdim + 16
+    wide = 128
     follows = before is not None
     rows_of = [
         (array, first)
@@ -230,12 +227,12 @@
     if ends:
         out = jax.ShapeDtypeStruct((part, rows), jnp.bfloat16)
     else:
-        out = jax.ShapeDtypeStruct((len(kinds), HALF, rows, 128), jnp.float32)
+        out = [jax.ShapeDtypeStruct((len(kinds), HALF, rows, wide), jnp.float32)] * 2
     return pl.pallas_call(
         functools.partial(attention_kernel, kinds, numbers, rows_of, follows, ends),
         out_shape=out,
-        in_specs=[smem()] + [vmem()] * (2 + len(kinds) + len(blocks) + follows),
-        out_specs=vmem(),
+        in_specs=[smem()] + [vmem()] * (2 + len(kinds) + len(blocks) + 2 * follows),
+        out_specs=vmem() if ends else [vmem()] * 2,
         scratch_shapes=[
             pltpu.VMEM((HALF, rows, hdim), jnp.bfloat16),
             pltpu.VMEM((len(numbers), part, rows), jnp.bfloat16),
@@ -244,7 +241,7 @@
         ],
         compiler_params=limit(16),
         cost_estimate=pl.CostEstimate(flops=1000, bytes_accessed=1000, transcendentals=0),
-    )(where, need, segs, *queries, *blocks, *((before,) if follows else ()))
+    )(where, need, segs, *queries, *blocks, *(before or ()))
 
 
 def stack_kernel(*refs):
@@ -427,7 +424,9 @@
     )
 
     where = block_index[None].astype(jnp.int32)
-    own_q, own_kv, swap_q, swap_kv = prepare(where, queries, keys, values)
+    own_kv, swap_kv = prepare(where, keys, values)
+    queries, own_kv, swap_kv = lax.optimization_barrier((queries, own_kv, swap_kv))
+    own_q, swap_q = prepare(where, queries)
     segs, need = survey(where, block_mask, segment_ids[None, :])
     other_kv = swap(swap_kv)
     ahead_own = ahead(own_kv)

time: 72.7 us -> 70.6 us (0.971)
  waiting for transfers between devices: 35.6 us -> 30 us
  starting transfers between devices: 21.1 us -> 25.2 us
  Pallas kernels: 14.2 us -> 13.1 us
  local copies, waits for them, and re-layouts: 0.03 us -> 1 us
    ppermute x7, waiting for transfers between devices: 21.6 us -> 19 us  [cross(): lax.ppermute(arrived[d], 'blk', [(i, i ^ d) for i in range(nblocks)])]
    ppermute x1, waiting for transfers between devices: 2.87 us -> 0.34 us  [per_device(): other_kv = swap(swap_kv)]
    ppermute x7, starting transfers between devices: 8.54 us -> 11.1 us  [cross(): lax.ppermute(arrived[d], 'blk', [(i, i ^ d) for i in range(nblocks)])]
    ppermute x1, starting transfers between devices: 0.07 us -> 1.59 us  [per_device(): other = swap(other)]
    ppermute x1, waiting for transfers between devices: 0.75 us -> 2.01 us  [per_device(): ahead_own = ahead(own_kv)]
    ppermute x1, waiting for transfers between devices: 2.63 us -> 1.38 us  [per_device(): other = swap(other)]
    unnamed x12 -> x14, local copies, waits for them, and re-layouts: 0.03 us -> 1 us
    pallas_call x1 -> x2, Pallas kernels: 2.1 us -> 1.64 us  [prepare(): pl.pallas_call(functools.partial(prepare_kernel, number), out_shape=[out]...]
  transfers between devices with their start and end apart: 15 -> 15, of which waited for: 10 -> 10; matrix products, arithmetic and copies ran while one was open for 0% -> 0% of each run, Pallas kernels for 14% -> 13%
where the time goes in v23:
time: 70.6 us; the launch traced here: 69.6 us
  waiting for transfers between devices  30 us (42%)
  starting transfers between devices  25.2 us (36%)
  Pallas kernels  13.1 us (19%)
  local copies, waits for them, and re-layouts  1 us (1%)
    ppermute x7, waiting for transfers between devices, cross(): lax.ppermute(arrived[d], 'blk', [(i, i ^ d) for i in range(nblocks)])  19 us
    ppermute x7, starting transfers between devices, cross(): lax.ppermute(arrived[d], 'blk', [(i, i ^ d) for i in range(nblocks)])  11.1 us
    pallas_call x4, Pallas kernels, attention(): pl.pallas_call(functools.partial(attention_kernel, kinds, numbers, rows_o...  7.61 us
    ppermute x1, waiting for transfers between devices, per_device(): back_other = relay(ready)  4.28 us
    ppermute x1, starting transfers between devices, per_device(): ahead_both = ahead(stack(other_kv, ahead_own))  3.48 us
    ppermute x1, starting transfers between devices, per_device(): ahead_own = ahead(own_kv)  3.47 us
    ppermute x1, waiting for transfers between devices, per_device(): ahead_both = ahead(stack(other_kv, ahead_own))  2.96 us
    ppermute x1, starting transfers between devices, per_device(): back_own = back(own_kv)  2.37 us
  transfers between devices with their start and end apart: 15, of which 10 were waited for; matrix products, arithmetic and copies ran while one was open for 0% of the time, Pallas kernels for 13%

profile of v23, /device:TPU:14, one launch (start us, length us, event | category | flops | bytes accessed | tf_op | source)
XLA Modules:
  0.0 69.6 jit_solution(16817058827231134149)
XLA Ops:
  0.0 1.4 %shard_map.92 = (bf16[640,256]{1,0:T(8,128)(2,1)S(1)}, bf16[640,256]{1,0:T(8,128)(2,1)S(1)}) custom-call(s32[1]{0:T(128)} %bitcast.where_ref, bf16[256,640]{1,0:T(8,128)(2,1)} %refs_0_.1, bf16[256,640]{1,0:T(8,128)(2,1)} %refs_1_.1), custom_call_target="tpu_custom_call" | custom-call | tf_op jit(solution)/shard_map/pallas_call | solution.py:68
  1.9 3.5 %collective-permute-start.1 = (bf16[640,256]{1,0:T(8,128)(2,1)S(1)}, bf16[640,256]{1,0:T(8,128)(2,1)S(1)}, u32[]{:S(2)}, u32[]{:S(2)}) collective-permute-start(bf16[640,256]{1,0:T(8,128)(2,1)S(1)} %get-tuple-element.44.refs_1_), channel_id=1, source_target_pairs={{4,12},{8,0},{12,20},{16,8},{20,28},{24,16},{5,13},{9,1},{13,21},{... | collective-permute-start | bytes 983048 | tf_op jit(solution)/shard_map/ppermute | solution.py:432
  5.4 2.4 %collective-permute-start.3 = (bf16[640,256]{1,0:T(8,128)(2,1)S(1)}, bf16[640,256]{1,0:T(8,128)(2,1)S(1)}, u32[]{:S(2)}, u32[]{:S(2)}) collective-permute-start(bf16[640,256]{1,0:T(8,128)(2,1)S(1)} %get-tuple-element.44.refs_1_), channel_id=1, source_target_pairs={{0,8},{8,16},{12,4},{16,24},{20,12},{28,20},{1,9},{9,17},{13,5},{1... | collective-permute-start | bytes 983048 | tf_op jit(solution)/shard_map/ppermute | solution.py:433
  9.1 1.6 %collective-permute-start.4 = (bf16[320,256]{1,0:T(8,128)(2,1)S(1)}, bf16[320,256]{1,0:T(8,128)(2,1)S(1)}, u32[]{:S(2)}, u32[]{:S(2)}) collective-permute-start(bf16[320,256]{1,0:T(8,128)(2,1)S(1)} %get-tuple-element.45), channel_id=1, source_target_pairs={{0,4},{4,0},{8,12},{12,8},{16,20},{20,16},{24,28},{28,24},{1,5},{5... | collective-permute-start | bytes 491528 | tf_op jit(solution)/shard_map/ppermute | solution.py:434
  11.0 2.0 %collective-permute-done.1.refs_1_.refs_3_ = bf16[640,256]{1,0:T(8,128)(2,1)S(1)} collective-permute-done((bf16[640,256]{1,0:T(8,128)(2,1)S(1)}, bf16[640,256]{1,0:T(8,128)(2,1)S(1)}, u32[]{:S(2)}, u32[]{:S(2)}) %collective-permute-start.1) | collective-permute-done | bytes 327712 | tf_op jit(solution)/shard_map/ppermute | solution.py:432
  13.0 3.5 %collective-permute-start.2 = (bf16[1280,256]{1,0:T(8,128)(2,1)S(1)}, bf16[1280,256]{1,0:T(8,128)(2,1)S(1)}, u32[]{:S(2)}, u32[]{:S(2)}) collective-permute-start(bf16[1280,256]{1,0:T(8,128)(2,1)S(1)} %shard_map.94), channel_id=1, source_target_pairs={{4,12},{8,0},{12,20},{16,8},{20,28},{24,16},{5,13},{9,1},{13,21},{... | collective-permute-start | bytes 1966088 | tf_op jit(solution)/shard_map/ppermute | solution.py:437
  17.8 2.5 %shard_map.95 = (f32[1,4,256,128]{3,2,1,0:T(8,128)S(1)}, f32[1,4,256,128]{3,2,1,0:T(8,128)S(1)}) custom-call(s32[1]{0:T(128)} %bitcast.where_ref, s32[8,128]{1,0:T(8,128)S(1)} %get-tuple-element.37.need_ref, f32[1,2048]{1,0:T(1,128)S(1)} %get-tuple-element.38.seg_ref, bf16[320,256]{1,0:T(8,128)(2,1)S(1)} %get-tuple-element.42.refs_0_, ...), custom_call_target="tpu_custom_call" | custom-call | flops 1000 | bytes 1000 | tf_op jit(solution)/shard_map/pallas_call | solution.py:231
  20.3 4.3 %collective-permute-done.5.refs_2_.refs_5_ = bf16[640,256]{1,0:T(8,128)(2,1)S(1)} collective-permute-done((bf16[640,256]{1,0:T(8,128)(2,1)S(1)}, bf16[640,256]{1,0:T(8,128)(2,1)S(1)}, u32[]{:S(2)}, u32[]{:S(2)}) %collective-permute-start.5) | collective-permute-done | bytes 327712 | tf_op jit(solution)/shard_map/ppermute | solution.py:436
  25.1 2.2 %shard_map.98 = (f32[1,4,256,128]{3,2,1,0:T(8,128)S(1)}, f32[1,4,256,128]{3,2,1,0:T(8,128)S(1)}) custom-call(s32[1]{0:T(128)} %bitcast.where_ref, s32[8,128]{1,0:T(8,128)S(1)} %get-tuple-element.37.need_ref, f32[1,2048]{1,0:T(1,128)S(1)} %get-tuple-element.38.seg_ref, bf16[320,256]{1,0:T(8,128)(2,1)S(1)} %collective-permute-done.4.refs_0_, ...), custom_call_target="tpu_custom_call" | custom-call | flops 1000 | bytes 1000 | tf_op jit(solution)/shard_map/pallas_call | solution.py:231
  27.3 3.0 %collective-permute-done.2.refs_1_ = bf16[1280,256]{1,0:T(8,128)(2,1)S(1)} collective-permute-done((bf16[1280,256]{1,0:T(8,128)(2,1)S(1)}, bf16[1280,256]{1,0:T(8,128)(2,1)S(1)}, u32[]{:S(2)}, u32[]{:S(2)}) %collective-permute-start.2) | collective-permute-done | bytes 655392 | tf_op jit(solution)/shard_map/ppermute | solution.py:437
  30.2 1.2 %shard_map.99 = bf16[320,256]{1,0:T(8,128)(2,1)S(1)} custom-call(s32[1]{0:T(128)} %bitcast.where_ref, s32[8,128]{1,0:T(8,128)S(1)} %get-tuple-element.37.need_ref, f32[1,2048]{1,0:T(1,128)S(1)} %get-tuple-element.38.seg_ref, bf16[320,256]{1,0:T(8,128)(2,1)S(1)} %collective-permute-done.4.refs_0_, bf16[1280,256]{1,0:T(8,128)(2,1)S(1)} %collective-permute-done.2.refs_1_, ...), custom_call_target="tpu_custom_call" | custom-call | flops 1000 | bytes 1000 | tf_op jit(solution)/shard_map/pallas_call | solution.py:231
  31.5 1.6 %collective-permute-start.7 = (bf16[320,256]{1,0:T(8,128)(2,1)S(1)}, bf16[320,256]{1,0:T(8,128)(2,1)S(1)}, u32[]{:S(2)}, u32[]{:S(2)}) collective-permute-start(bf16[320,256]{1,0:T(8,128)(2,1)S(1)} %shard_map.99), channel_id=1, source_target_pairs={{0,4},{4,0},{8,12},{12,8},{16,20},{20,16},{24,28},{28,24},{1,5},{5... | collective-permute-start | bytes 491528 | tf_op jit(solution)/shard_map/ppermute | solution.py:448
  33.1 1.7 %shard_map.96.own_ref = bf16[320,256]{1,0:T(8,128)(2,1)S(1)} custom-call(s32[1]{0:T(128)} %bitcast.where_ref, s32[8,128]{1,0:T(8,128)S(1)} %get-tuple-element.37.need_ref, f32[1,2048]{1,0:T(1,128)S(1)} %get-tuple-element.38.seg_ref, bf16[320,256]{1,0:T(8,128)(2,1)S(1)} %get-tuple-element.42.refs_0_, bf16[1280,256]{1,0:T(8,128)(2,1)S(1)} %collective-permute-done.2.refs_1_, ...), custom_call_target="tpu_custom_call" | custom-call | flops 1000 | bytes 1000 | tf_op jit(solution)/shard_map/pallas_call | solution.py:231
  35.5 1.4 %collective-permute-done.7.other_ref = bf16[320,256]{1,0:T(8,128)(2,1)S(1)} collective-permute-done((bf16[320,256]{1,0:T(8,128)(2,1)S(1)}, bf16[320,256]{1,0:T(8,128)(2,1)S(1)}, u32[]{:S(2)}, u32[]{:S(2)}) %collective-permute-start.7) | collective-permute-done | bytes 163872 | tf_op jit(solution)/shard_map/ppermute | solution.py:448
  37.9 1.5 %collective-permute-start.8 = (bf16[16,5248]{1,0:T(8,128)(2,1)S(1)}, bf16[16,5248]{1,0:T(8,128)(2,1)S(1)}, u32[]{:S(2)}, u32[]{:S(2)}) collective-permute-start(bf16[16,5248]{1,0:T(8,128)(2,1)S(1)} %get-tuple-element.59), channel_id=1, source_target_pairs={{0,12},{4,8},{8,4},{12,0},{16,28},{20,24},{24,20},{28,16},{1,13},{... | collective-permute-start | bytes 503816 | tf_op jit(solution)/shard_map/ppermute | solution.py:461
  39.4 1.9 %collective-permute-start.11 = (bf16[16,5248]{1,0:T(8,128)(2,1)S(1)}, bf16[16,5248]{1,0:T(8,128)(2,1)S(1)}, u32[]{:S(2)}, u32[]{:S(2)}) collective-permute-start(bf16[16,5248]{1,0:T(8,128)(2,1)S(1)} %get-tuple-element.65), channel_id=1, source_target_pairs={{0,16},{4,20},{8,24},{12,28},{16,0},{20,4},{24,8},{28,12},{1,17},{... | collective-permute-start | bytes 503816 | tf_op jit(solution)/shard_map/ppermute | solution.py:461
  41.9 2.3 %collective-permute-start.13 = (bf16[16,5248]{1,0:T(8,128)(2,1)S(1)}, bf16[16,5248]{1,0:T(8,128)(2,1)S(1)}, u32[]{:S(2)}, u32[]{:S(2)}) collective-permute-start(bf16[16,5248]{1,0:T(8,128)(2,1)S(1)} %get-tuple-element.67), channel_id=1, source_target_pairs={{0,24},{4,28},{8,16},{12,20},{16,8},{20,12},{24,0},{28,4},{1,25},{... | collective-permute-start | bytes 503816 | tf_op jit(solution)/shard_map/ppermute | solution.py:461
  46.1 2.5 %collective-permute-start.10 = (bf16[16,5248]{1,0:T(8,128)(2,1)S(1)}, bf16[16,5248]{1,0:T(8,128)(2,1)S(1)}, u32[]{:S(2)}, u32[]{:S(2)}) collective-permute-start(bf16[16,5248]{1,0:T(8,128)(2,1)S(1)} %get-tuple-element.63), channel_id=1, source_target_pairs={{0,8},{4,12},{8,0},{12,4},{16,24},{20,28},{24,16},{28,20},{1,9},{5... | collective-permute-start | bytes 503816 | tf_op jit(solution)/shard_map/ppermute | solution.py:461
  48.6 8.0 %collective-permute-done.11.refs_4_ = bf16[16,5248]{1,0:T(8,128)(2,1)S(1)} collective-permute-done((bf16[16,5248]{1,0:T(8,128)(2,1)S(1)}, bf16[16,5248]{1,0:T(8,128)(2,1)S(1)}, u32[]{:S(2)}, u32[]{:S(2)}) %collective-permute-start.11) | collective-permute-done | bytes 167968 | tf_op jit(solution)/shard_map/ppermute | solution.py:461
  56.6 1.2 %collective-permute-start.9 = (bf16[16,5248]{1,0:T(8,128)(2,1)S(1)}, bf16[16,5248]{1,0:T(8,128)(2,1)S(1)}, u32[]{:S(2)}, u32[]{:S(2)}) collective-permute-start(bf16[16,5248]{1,0:T(8,128)(2,1)S(1)} %get-tuple-element.62), channel_id=1, source_target_pairs={{0,4},{4,0},{8,12},{12,8},{16,20},{20,16},{24,28},{28,24},{1,5},{5... | collective-permute-start | bytes 503816 | tf_op jit(solution)/shard_map/ppermute | solution.py:461
  57.8 2.5 %collective-permute-done.12.refs_5_ = bf16[16,5248]{1,0:T(8,128)(2,1)S(1)} collective-permute-done((bf16[16,5248]{1,0:T(8,128)(2,1)S(1)}, bf16[16,5248]{1,0:T(8,128)(2,1)S(1)}, u32[]{:S(2)}, u32[]{:S(2)}) %collective-permute-start.12) | collective-permute-done | bytes 167968 | tf_op jit(solution)/shard_map/ppermute | solution.py:461
  60.3 5.3 %collective-permute-done.13.refs_6_ = bf16[16,5248]{1,0:T(8,128)(2,1)S(1)} collective-permute-done((bf16[16,5248]{1,0:T(8,128)(2,1)S(1)}, bf16[16,5248]{1,0:T(8,128)(2,1)S(1)}, u32[]{:S(2)}, u32[]{:S(2)}) %collective-permute-start.13) | collective-permute-done | bytes 167968 | tf_op jit(solution)/shard_map/ppermute | solution.py:461
  65.6 2.4 %collective-permute-done.14.refs_7_ = bf16[16,5248]{1,0:T(8,128)(2,1)S(1)} collective-permute-done((bf16[16,5248]{1,0:T(8,128)(2,1)S(1)}, bf16[16,5248]{1,0:T(8,128)(2,1)S(1)}, u32[]{:S(2)}, u32[]{:S(2)}) %collective-permute-start.14) | collective-permute-done | bytes 167968 | tf_op jit(solution)/shard_map/ppermute | solution.py:461
  68.0 1.5 %shard_map.101 = bf16[128,5120]{1,0:T(8,128)(2,1)} custom-call(bf16[16,5248]{1,0:T(8,128)(2,1)S(1)} %get-tuple-element.58.refs_0_, bf16[16,5248]{1,0:T(8,128)(2,1)S(1)} %collective-permute-done.9.refs_1_, bf16[16,5248]{1,0:T(8,128)(2,1)S(1)} %collective-permute-done.10.refs_2_, bf16[16,5248]{1,0:T(8,128)(2,1)S(1)} %collective-permute-done.8.refs_3_, ...), custom_call_target="tpu_custom_call" | custom-call | tf_op jit(solution)/shard_map/pallas_call | solution.py:383
  (31 shorter events, 8.1 us)
Async XLA Ops:
  0.0 17.1 %copy-start.3 = (s32[2048]{0:T(1024)S(1)}, s32[2048]{0:T(1024)}, u32[]{:S(2)}) copy-start(s32[2048]{0:T(1024)} %param.9) | copy-start | bytes 24580
  0.0 17.1 %copy-start.4 = (s32[8,8]{1,0:T(8,128)S(1)}, s32[8,8]{1,0:T(8,128)}, u32[]{:S(2)}) copy-start(s32[8,8]{1,0:T(8,128)} %mask_ref.1) | copy-start | bytes 772
  1.4 9.6 %collective-permute-start = (bf16[640,256]{1,0:T(8,128)(2,1)S(1)}, bf16[640,256]{1,0:T(8,128)(2,1)S(1)}, u32[]{:S(2)}, u32[]{:S(2)}) collective-permute-start(bf16[640,256]{1,0:T(8,128)(2,1)S(1)} %get-tuple-element.43), channel_id=1, source_target_pairs={{0,4},{4,0},{8,12},{12,8},{16,20},{20,16},{24,28},{28,24},{1,5},{5... | collective-permute-start | bytes 983048 | tf_op jit(solution)/shard_map/ppermute | solution.py:431
  1.9 11.1 %collective-permute-start.1 = (bf16[640,256]{1,0:T(8,128)(2,1)S(1)}, bf16[640,256]{1,0:T(8,128)(2,1)S(1)}, u32[]{:S(2)}, u32[]{:S(2)}) collective-permute-start(bf16[640,256]{1,0:T(8,128)(2,1)S(1)} %get-tuple-element.44.refs_1_), channel_id=1, source_target_pairs={{4,12},{8,0},{12,20},{16,8},{20,28},{24,16},{5,13},{9,1},{13,21},{... | collective-permute-start | bytes 983048 | tf_op jit(solution)/shard_map/ppermute | solution.py:432
  5.4 11.1 %collective-permute-start.3 = (bf16[640,256]{1,0:T(8,128)(2,1)S(1)}, bf16[640,256]{1,0:T(8,128)(2,1)S(1)}, u32[]{:S(2)}, u32[]{:S(2)}) collective-permute-start(bf16[640,256]{1,0:T(8,128)(2,1)S(1)} %get-tuple-element.44.refs_1_), channel_id=1, source_target_pairs={{0,8},{8,16},{12,4},{16,24},{20,12},{28,20},{1,9},{9,17},{13,5},{1... | collective-permute-start | bytes 983048 | tf_op jit(solution)/shard_map/ppermute | solution.py:433
  7.8 1.0 %copy-start.2 = (bf16[256,640]{1,0:T(8,128)(2,1)S(1)}, bf16[256,640]{1,0:T(8,128)(2,1)}, u32[]{:S(2)}) copy-start(bf16[256,640]{1,0:T(8,128)(2,1)} %refs_0_.2) | copy-start | bytes 983044
  9.1 7.5 %collective-permute-start.4 = (bf16[320,256]{1,0:T(8,128)(2,1)S(1)}, bf16[320,256]{1,0:T(8,128)(2,1)S(1)}, u32[]{:S(2)}, u32[]{:S(2)}) collective-permute-start(bf16[320,256]{1,0:T(8,128)(2,1)S(1)} %get-tuple-element.45), channel_id=1, source_target_pairs={{0,4},{4,0},{8,12},{12,8},{16,20},{20,16},{24,28},{28,24},{1,5},{5... | collective-permute-start | bytes 491528 | tf_op jit(solution)/shard_map/ppermute | solution.py:434
  13.0 17.2 %collective-permute-start.2 = (bf16[1280,256]{1,0:T(8,128)(2,1)S(1)}, bf16[1280,256]{1,0:T(8,128)(2,1)S(1)}, u32[]{:S(2)}, u32[]{:S(2)}) collective-permute-start(bf16[1280,256]{1,0:T(8,128)(2,1)S(1)} %shard_map.94), channel_id=1, source_target_pairs={{4,12},{8,0},{12,20},{16,8},{20,28},{24,16},{5,13},{9,1},{13,21},{... | collective-permute-start | bytes 1966088 | tf_op jit(solution)/shard_map/ppermute | solution.py:437
  16.6 8.0 %collective-permute-start.5 = (bf16[640,256]{1,0:T(8,128)(2,1)S(1)}, bf16[640,256]{1,0:T(8,128)(2,1)S(1)}, u32[]{:S(2)}, u32[]{:S(2)}) collective-permute-start(bf16[640,256]{1,0:T(8,128)(2,1)S(1)} %collective-permute-done.refs_0_.refs_2_), channel_id=1, source_target_pairs={{0,8},{4,0},{8,16},{12,4},{16,24},{20,12},{24,28},{28,20},{1,9},{5... | collective-permute-start | bytes 983048 | tf_op jit(solution)/shard_map/ppermute | solution.py:436
  24.6 8.5 %collective-permute-start.6 = (bf16[640,256]{1,0:T(8,128)(2,1)S(1)}, bf16[640,256]{1,0:T(8,128)(2,1)S(1)}, u32[]{:S(2)}, u32[]{:S(2)}) collective-permute-start(bf16[640,256]{1,0:T(8,128)(2,1)S(1)} %collective-permute-done.5.refs_2_.refs_5_), channel_id=1, source_target_pairs={{0,8},{4,0},{8,16},{12,4},{16,24},{20,12},{24,28},{28,20},{1,9},{5... | collective-permute-start | bytes 983048 | tf_op jit(solution)/shard_map/ppermute | solution.py:443
  31.5 3.4 %copy-start = (bf16[640,1280]{1,0:T(8,128)(2,1)S(1)}, bf16[640,1280]{1,0:T(8,128)(2,1)}, u32[]{:S(2)}) copy-start(bf16[640,1280]{1,0:T(8,128)(2,1)} %weight_ref.3) | copy-start | bytes 4915204
  31.5 3.4 %copy-start.1 = (bf16[256,1280]{1,0:T(8,128)(2,1)S(1)}, bf16[256,1280]{1,0:T(8,128)(2,1)}, u32[]{:S(2)}) copy-start(bf16[256,1280]{1,0:T(8,128)(2,1)} %tokens_ref.1) | copy-start | bytes 1966084
  31.5 3.4 %copy-start.5 = (s32[64]{0:T(128)S(1)}, s32[64]{0:T(128)}, u32[]{:S(2)}) copy-start(s32[64]{0:T(128)} %param.16) | copy-start | bytes 772
  31.5 3.4 %copy-start.6 = (s32[64]{0:T(128)S(1)}, s32[64]{0:T(128)}, u32[]{:S(2)}) copy-start(s32[64]{0:T(128)} %param.17) | copy-start | bytes 772
  31.5 5.4 %collective-permute-start.7 = (bf16[320,256]{1,0:T(8,128)(2,1)S(1)}, bf16[320,256]{1,0:T(8,128)(2,1)S(1)}, u32[]{:S(2)}, u32[]{:S(2)}) collective-permute-start(bf16[320,256]{1,0:T(8,128)(2,1)S(1)} %shard_map.99), channel_id=1, source_target_pairs={{0,4},{4,0},{8,12},{12,8},{16,20},{20,16},{24,28},{28,24},{1,5},{5... | collective-permute-start | bytes 491528 | tf_op jit(solution)/shard_map/ppermute | solution.py:448
  37.9 8.2 %collective-permute-start.8 = (bf16[16,5248]{1,0:T(8,128)(2,1)S(1)}, bf16[16,5248]{1,0:T(8,128)(2,1)S(1)}, u32[]{:S(2)}, u32[]{:S(2)}) collective-permute-start(bf16[16,5248]{1,0:T(8,128)(2,1)S(1)} %get-tuple-element.59), channel_id=1, source_target_pairs={{0,12},{4,8},{8,4},{12,0},{16,28},{20,24},{24,20},{28,16},{1,13},{... | collective-permute-start | bytes 503816 | tf_op jit(solution)/shard_map/ppermute | solution.py:461
  39.4 17.2 %collective-permute-start.11 = (bf16[16,5248]{1,0:T(8,128)(2,1)S(1)}, bf16[16,5248]{1,0:T(8,128)(2,1)S(1)}, u32[]{:S(2)}, u32[]{:S(2)}) collective-permute-start(bf16[16,5248]{1,0:T(8,128)(2,1)S(1)} %get-tuple-element.65), channel_id=1, source_target_pairs={{0,16},{4,20},{8,24},{12,28},{16,0},{20,4},{24,8},{28,12},{1,17},{... | collective-permute-start | bytes 503816 | tf_op jit(solution)/shard_map/ppermute | solution.py:461
  41.3 19.0 %collective-permute-start.12 = (bf16[16,5248]{1,0:T(8,128)(2,1)S(1)}, bf16[16,5248]{1,0:T(8,128)(2,1)S(1)}, u32[]{:S(2)}, u32[]{:S(2)}) collective-permute-start(bf16[16,5248]{1,0:T(8,128)(2,1)S(1)} %get-tuple-element.66), channel_id=1, source_target_pairs={{0,20},{4,16},{8,28},{12,24},{16,4},{20,0},{24,12},{28,8},{1,21},{... | collective-permute-start | bytes 503816 | tf_op jit(solution)/shard_map/ppermute | solution.py:461
  41.9 23.7 %collective-permute-start.13 = (bf16[16,5248]{1,0:T(8,128)(2,1)S(1)}, bf16[16,5248]{1,0:T(8,128)(2,1)S(1)}, u32[]{:S(2)}, u32[]{:S(2)}) collective-permute-start(bf16[16,5248]{1,0:T(8,128)(2,1)S(1)} %get-tuple-element.67), channel_id=1, source_target_pairs={{0,24},{4,28},{8,16},{12,20},{16,8},{20,12},{24,0},{28,4},{1,25},{... | collective-permute-start | bytes 503816 | tf_op jit(solution)/shard_map/ppermute | solution.py:461
  44.2 23.8 %collective-permute-start.14 = (bf16[16,5248]{1,0:T(8,128)(2,1)S(1)}, bf16[16,5248]{1,0:T(8,128)(2,1)S(1)}, u32[]{:S(2)}, u32[]{:S(2)}) collective-permute-start(bf16[16,5248]{1,0:T(8,128)(2,1)S(1)} %get-tuple-element.68), channel_id=1, source_target_pairs={{0,28},{4,24},{8,20},{12,16},{16,12},{20,8},{24,4},{28,0},{1,29},{... | collective-permute-start | bytes 503816 | tf_op jit(solution)/shard_map/ppermute | solution.py:461
  46.1 21.9 %collective-permute-start.10 = (bf16[16,5248]{1,0:T(8,128)(2,1)S(1)}, bf16[16,5248]{1,0:T(8,128)(2,1)S(1)}, u32[]{:S(2)}, u32[]{:S(2)}) collective-permute-start(bf16[16,5248]{1,0:T(8,128)(2,1)S(1)} %get-tuple-element.63), channel_id=1, source_target_pairs={{0,8},{4,12},{8,0},{12,4},{16,24},{20,28},{24,16},{28,20},{1,9},{5... | collective-permute-start | bytes 503816 | tf_op jit(solution)/shard_map/ppermute | solution.py:461
  56.6 11.5 %collective-permute-start.9 = (bf16[16,5248]{1,0:T(8,128)(2,1)S(1)}, bf16[16,5248]{1,0:T(8,128)(2,1)S(1)}, u32[]{:S(2)}, u32[]{:S(2)}) collective-permute-start(bf16[16,5248]{1,0:T(8,128)(2,1)S(1)} %get-tuple-element.62), channel_id=1, source_target_pairs={{0,4},{4,0},{8,12},{12,8},{16,20},{20,16},{24,28},{28,24},{1,5},{5... | collective-permute-start | bytes 503816 | tf_op jit(solution)/shard_map/ppermute | solution.py:461

commit v24 on v23

--- a/solution.py
+++ b/solution.py
@@ -315,6 +315,7 @@
 def project_kernel(order, where_ref, hidden_ref, meta_ref, other_ref, weight_ref, *outs):
     piece = outs[0].shape[0]
     slots = piece * len(outs)
+    first = piece * order[0]
     rows, width = hidden_ref.shape
     capacity = rows // 2
     meta = meta_ref[...]
@@ -325,7 +326,7 @@
         preferred_element_type=jnp.float32,
     )
     hidden = hidden.astype(jnp.bfloat16)
-    slot = lax.broadcasted_iota(jnp.int32, (slots, rows), 0).astype(jnp.float32)
+    slot = first + lax.broadcasted_iota(jnp.int32, (slots, rows), 0).astype(jnp.float32)
     quarter = lax.broadcasted_iota(jnp.int32, (1, rows), 1) % 4
     for j in range(4):
         mine = jnp.where(quarter == j, meta[:1], -1.0) == slot
@@ -333,22 +334,21 @@
             offset = jnp.where(mine, meta[1:2] - capacity, 0.0)
             offset = capacity + jnp.sum(offset, axis=1, keepdims=True)
             offset = jnp.broadcast_to(offset, (slots, 128)).astype(jnp.bfloat16)
-            for d, out in zip(order, outs):
+            for d, out in enumerate(outs):
                 out[:, 4 * width :] = offset[d * piece : (d + 1) * piece]
         pick = jnp.where(mine, 1.0, 0.0).astype(jnp.bfloat16)
         picked = jnp.dot(pick, hidden, preferred_element_type=jnp.float32).astype(jnp.bfloat16)
-        for d, out in zip(order, outs):
+        for d, out in enumerate(outs):
             out[:, j * width : (j + 1) * width] = picked[d * piece : (d + 1) * piece]
 
 
-def project(where, hidden, meta, other, out_weight, order, slots):
+def project(where, hidden, meta, other, out_weight, order, rows):
     width = hidden.shape[1]
-    pieces = len(order)
     return pl.pallas_call(
         functools.partial(project_kernel, order),
-        out_shape=[jax.ShapeDtypeStruct((slots // pieces, 4 * width + 128), jnp.bfloat16)] * pieces,
+        out_shape=[jax.ShapeDtypeStruct((rows, 4 * width + 128), jnp.bfloat16)] * len(order),
         in_specs=[smem()] + [vmem()] * 4,
-        out_specs=[vmem()] * pieces,
+        out_specs=[vmem()] * len(order),
         compiler_params=limit(24),
     )(where, hidden, meta, other, out_weight)
 
@@ -453,23 +453,24 @@
     hidden, meta = begin(
         where, owners[None, :], offsets[None, :], own, out_weight, tokens, len(order), pair_rows
     )
-    outgoing = project(where, hidden, meta, other, out_weight, order, slots)
     if len(order) > 1:
-        arrived = list(outgoing)
+        middle = nblocks // 2
+        far = project(where, hidden, meta, other, out_weight, order[middle:], pair_rows)
+        *far, hidden = lax.optimization_barrier((*far, hidden))
+        near = project(where, hidden, meta, other, out_weight, order[:middle], pair_rows)
+        arrived = [*near, *far]
 
         def cross(d):
             arrived[d] = lax.ppermute(arrived[d], "blk", [(i, i ^ d) for i in range(nblocks)])
 
-        short, *late = range(nblocks // 2 - 1, 0, -1)
-        for d in (*range(nblocks // 2, nblocks), short):
+        for d in (*order[middle:], middle - 1):
             cross(d)
-        group = lax.optimization_barrier([arrived[d] for d in (short, *late)])
-        for d, block in zip((short, *late), group):
-            arrived[d] = block
-        for d in late:
+        arrived[1:middle] = lax.optimization_barrier(arrived[1:middle])
+        for d in range(1, middle - 1):
             cross(d)
     else:
-        arrived = [lax.all_to_all(outgoing[0], "blk", split_axis=0, concat_axis=0, tiled=True)]
+        (outgoing,) = project(where, hidden, meta, other, out_weight, order, slots)
+        arrived = [lax.all_to_all(outgoing, "blk", split_axis=0, concat_axis=0, tiled=True)]
     return place(arrived, capacity, 4 * width)
 
 

time: 70.6 us -> 72.1 us (1.021)
  waiting for transfers between devices: 30 us -> 33 us
  starting transfers between devices: 25.2 us -> 22.5 us
  Pallas kernels: 13.1 us -> 13.9 us
    ppermute x7, waiting for transfers between devices: 19 us -> 21 us  [cross(): lax.ppermute(arrived[d], 'blk', [(i, i ^ d) for i in range(nblocks)])]
    ppermute x7, starting transfers between devices: 11.1 us -> 9.12 us  [cross(): lax.ppermute(arrived[d], 'blk', [(i, i ^ d) for i in range(nblocks)])]
    pallas_call x1 -> x2, Pallas kernels: 1 us -> 2.13 us  [project(): pl.pallas_call(functools.partial(project_kernel, order), out_shape=[jax.S...]
where the time goes in v24:
time: 72.1 us; the launch traced here: 70.8 us
  waiting for transfers between devices  33 us (46%)
  starting transfers between devices  22.5 us (31%)
  Pallas kernels  13.9 us (19%)
  local copies, waits for them, and re-layouts  1 us (1%)
    ppermute x7, waiting for transfers between devices, cross(): lax.ppermute(arrived[d], 'blk', [(i, i ^ d) for i in range(nblocks)])  21 us
    ppermute x7, starting transfers between devices, cross(): lax.ppermute(arrived[d], 'blk', [(i, i ^ d) for i in range(nblocks)])  9.12 us
    pallas_call x4, Pallas kernels, attention(): pl.pallas_call(functools.partial(attention_kernel, kinds, numbers, rows_o...  7.35 us
    ppermute x1, waiting for transfers between devices, per_device(): back_other = relay(ready)  4.77 us
    ppermute x1, starting transfers between devices, per_device(): ahead_both = ahead(stack(other_kv, ahead_own))  3.48 us
    ppermute x1, starting transfers between devices, per_device(): ahead_own = ahead(own_kv)  3.47 us
    ppermute x1, waiting for transfers between devices, per_device(): ahead_both = ahead(stack(other_kv, ahead_own))  2.96 us
    ppermute x1, starting transfers between devices, per_device(): back_own = back(own_kv)  2.37 us
  transfers between devices with their start and end apart: 15, of which 10 were waited for; matrix products, arithmetic and copies ran while one was open for 0% of the time, Pallas kernels for 13%

profile of v24, /device:TPU:14, one launch (start us, length us, event | category | flops | bytes accessed | tf_op | source)
XLA Modules:
  0.0 70.8 jit_solution(884658585401035476)
XLA Ops:
  0.0 1.4 %shard_map.92 = (bf16[640,256]{1,0:T(8,128)(2,1)S(1)}, bf16[640,256]{1,0:T(8,128)(2,1)S(1)}) custom-call(s32[1]{0:T(128)} %bitcast.where_ref, bf16[256,640]{1,0:T(8,128)(2,1)} %refs_0_.1, bf16[256,640]{1,0:T(8,128)(2,1)} %refs_1_.1), custom_call_target="tpu_custom_call" | custom-call | tf_op jit(solution)/shard_map/pallas_call | solution.py:68
  1.9 3.5 %collective-permute-start.1 = (bf16[640,256]{1,0:T(8,128)(2,1)S(1)}, bf16[640,256]{1,0:T(8,128)(2,1)S(1)}, u32[]{:S(2)}, u32[]{:S(2)}) collective-permute-start(bf16[640,256]{1,0:T(8,128)(2,1)S(1)} %get-tuple-element.49.refs_1_), channel_id=1, source_target_pairs={{4,12},{8,0},{12,20},{16,8},{20,28},{24,16},{5,13},{9,1},{13,21},{... | collective-permute-start | bytes 983048 | tf_op jit(solution)/shard_map/ppermute | solution.py:432
  5.4 2.4 %collective-permute-start.3 = (bf16[640,256]{1,0:T(8,128)(2,1)S(1)}, bf16[640,256]{1,0:T(8,128)(2,1)S(1)}, u32[]{:S(2)}, u32[]{:S(2)}) collective-permute-start(bf16[640,256]{1,0:T(8,128)(2,1)S(1)} %get-tuple-element.49.refs_1_), channel_id=1, source_target_pairs={{0,8},{8,16},{12,4},{16,24},{20,12},{28,20},{1,9},{9,17},{13,5},{1... | collective-permute-start | bytes 983048 | tf_op jit(solution)/shard_map/ppermute | solution.py:433
  9.1 1.6 %collective-permute-start.4 = (bf16[320,256]{1,0:T(8,128)(2,1)S(1)}, bf16[320,256]{1,0:T(8,128)(2,1)S(1)}, u32[]{:S(2)}, u32[]{:S(2)}) collective-permute-start(bf16[320,256]{1,0:T(8,128)(2,1)S(1)} %get-tuple-element.50), channel_id=1, source_target_pairs={{0,4},{4,0},{8,12},{12,8},{16,20},{20,16},{24,28},{28,24},{1,5},{5... | collective-permute-start | bytes 491528 | tf_op jit(solution)/shard_map/ppermute | solution.py:434
  11.0 2.0 %collective-permute-done.1.refs_1_.refs_3_ = bf16[640,256]{1,0:T(8,128)(2,1)S(1)} collective-permute-done((bf16[640,256]{1,0:T(8,128)(2,1)S(1)}, bf16[640,256]{1,0:T(8,128)(2,1)S(1)}, u32[]{:S(2)}, u32[]{:S(2)}) %collective-permute-start.1) | collective-permute-done | bytes 327712 | tf_op jit(solution)/shard_map/ppermute | solution.py:432
  13.0 3.5 %collective-permute-start.2 = (bf16[1280,256]{1,0:T(8,128)(2,1)S(1)}, bf16[1280,256]{1,0:T(8,128)(2,1)S(1)}, u32[]{:S(2)}, u32[]{:S(2)}) collective-permute-start(bf16[1280,256]{1,0:T(8,128)(2,1)S(1)} %shard_map.94), channel_id=1, source_target_pairs={{4,12},{8,0},{12,20},{16,8},{20,28},{24,16},{5,13},{9,1},{13,21},{... | collective-permute-start | bytes 1966088 | tf_op jit(solution)/shard_map/ppermute | solution.py:437
  17.8 2.0 %shard_map.95 = (f32[1,4,256,128]{3,2,1,0:T(8,128)S(1)}, f32[1,4,256,128]{3,2,1,0:T(8,128)S(1)}) custom-call(s32[1]{0:T(128)} %bitcast.where_ref, s32[8,128]{1,0:T(8,128)S(1)} %get-tuple-element.42.need_ref, f32[1,2048]{1,0:T(1,128)S(1)} %get-tuple-element.43.seg_ref, bf16[320,256]{1,0:T(8,128)(2,1)S(1)} %get-tuple-element.47.refs_0_, ...), custom_call_target="tpu_custom_call" | custom-call | flops 1000 | bytes 1000 | tf_op jit(solution)/shard_map/pallas_call | solution.py:231
  19.8 4.8 %collective-permute-done.5.refs_2_.refs_5_ = bf16[640,256]{1,0:T(8,128)(2,1)S(1)} collective-permute-done((bf16[640,256]{1,0:T(8,128)(2,1)S(1)}, bf16[640,256]{1,0:T(8,128)(2,1)S(1)}, u32[]{:S(2)}, u32[]{:S(2)}) %collective-permute-start.5) | collective-permute-done | bytes 327712 | tf_op jit(solution)/shard_map/ppermute | solution.py:436
  25.1 2.2 %shard_map.98 = (f32[1,4,256,128]{3,2,1,0:T(8,128)S(1)}, f32[1,4,256,128]{3,2,1,0:T(8,128)S(1)}) custom-call(s32[1]{0:T(128)} %bitcast.where_ref, s32[8,128]{1,0:T(8,128)S(1)} %get-tuple-element.42.need_ref, f32[1,2048]{1,0:T(1,128)S(1)} %get-tuple-element.43.seg_ref, bf16[320,256]{1,0:T(8,128)(2,1)S(1)} %collective-permute-done.4.refs_0_, ...), custom_call_target="tpu_custom_call" | custom-call | flops 1000 | bytes 1000 | tf_op jit(solution)/shard_map/pallas_call | solution.py:231
  27.3 3.0 %collective-permute-done.2.refs_1_ = bf16[1280,256]{1,0:T(8,128)(2,1)S(1)} collective-permute-done((bf16[1280,256]{1,0:T(8,128)(2,1)S(1)}, bf16[1280,256]{1,0:T(8,128)(2,1)S(1)}, u32[]{:S(2)}, u32[]{:S(2)}) %collective-permute-start.2) | collective-permute-done | bytes 655392 | tf_op jit(solution)/shard_map/ppermute | solution.py:437
  30.2 1.2 %shard_map.99 = bf16[320,256]{1,0:T(8,128)(2,1)S(1)} custom-call(s32[1]{0:T(128)} %bitcast.where_ref, s32[8,128]{1,0:T(8,128)S(1)} %get-tuple-element.42.need_ref, f32[1,2048]{1,0:T(1,128)S(1)} %get-tuple-element.43.seg_ref, bf16[320,256]{1,0:T(8,128)(2,1)S(1)} %collective-permute-done.4.refs_0_, bf16[1280,256]{1,0:T(8,128)(2,1)S(1)} %collective-permute-done.2.refs_1_, ...), custom_call_target="tpu_custom_call" | custom-call | flops 1000 | bytes 1000 | tf_op jit(solution)/shard_map/pallas_call | solution.py:231
  32.4 2.0 %shard_map.96.own_ref = bf16[320,256]{1,0:T(8,128)(2,1)S(1)} custom-call(s32[1]{0:T(128)} %bitcast.where_ref, s32[8,128]{1,0:T(8,128)S(1)} %get-tuple-element.42.need_ref, f32[1,2048]{1,0:T(1,128)S(1)} %get-tuple-element.43.seg_ref, bf16[320,256]{1,0:T(8,128)(2,1)S(1)} %get-tuple-element.47.refs_0_, bf16[1280,256]{1,0:T(8,128)(2,1)S(1)} %collective-permute-done.2.refs_1_, ...), custom_call_target="tpu_custom_call" | custom-call | flops 1000 | bytes 1000 | tf_op jit(solution)/shard_map/pallas_call | solution.py:231
  35.0 1.9 %collective-permute-done.7.other_ref = bf16[320,256]{1,0:T(8,128)(2,1)S(1)} collective-permute-done((bf16[320,256]{1,0:T(8,128)(2,1)S(1)}, bf16[320,256]{1,0:T(8,128)(2,1)S(1)}, u32[]{:S(2)}, u32[]{:S(2)}) %collective-permute-start.7) | collective-permute-done | bytes 163872 | tf_op jit(solution)/shard_map/ppermute | solution.py:448
  36.9 1.1 %shard_map.100 = (bf16[16,5248]{1,0:T(8,128)(2,1)S(1)}, bf16[16,5248]{1,0:T(8,128)(2,1)S(1)}, bf16[16,5248]{1,0:T(8,128)(2,1)S(1)}, bf16[16,5248]{1,0:T(8,128)(2,1)S(1)}) custom-call(s32[1]{0:T(128)} %bitcast.where_ref, f32[256,1280]{1,0:T(8,128)S(1)} %get-tuple-element.67.hidden_ref, f32[16,256]{1,0:T(8,128)S(1)} %get-tuple-element.59.meta_ref, ...), custom_call_target="tpu_custom_call" | custom-call | tf_op jit(solution)/shard_map/pallas_call | solution.py:347
  38.0 1.1 %shard_map.101 = (bf16[16,5248]{1,0:T(8,128)(2,1)S(1)}, bf16[16,5248]{1,0:T(8,128)(2,1)S(1)}, bf16[16,5248]{1,0:T(8,128)(2,1)S(1)}, bf16[16,5248]{1,0:T(8,128)(2,1)S(1)}) custom-call(s32[1]{0:T(128)} %bitcast.where_ref, f32[256,1280]{1,0:T(8,128)S(1)} %get-tuple-element.67.hidden_ref, f32[16,256]{1,0:T(8,128)S(1)} %get-tuple-element.59.meta_ref, ...), custom_call_target="tpu_custom_call" | custom-call | tf_op jit(solution)/shard_map/pallas_call | solution.py:347
  39.0 1.5 %collective-permute-start.8 = (bf16[16,5248]{1,0:T(8,128)(2,1)S(1)}, bf16[16,5248]{1,0:T(8,128)(2,1)S(1)}, u32[]{:S(2)}, u32[]{:S(2)}) collective-permute-start(bf16[16,5248]{1,0:T(8,128)(2,1)S(1)} %get-tuple-element.71), channel_id=1, source_target_pairs={{0,12},{4,8},{8,4},{12,0},{16,28},{20,24},{24,20},{28,16},{1,13},{... | collective-permute-start | bytes 503816 | tf_op jit(solution)/shard_map/ppermute | solution.py:464
  40.5 2.6 %collective-permute-start.11 = (bf16[16,5248]{1,0:T(8,128)(2,1)S(1)}, bf16[16,5248]{1,0:T(8,128)(2,1)S(1)}, u32[]{:S(2)}, u32[]{:S(2)}) collective-permute-start(bf16[16,5248]{1,0:T(8,128)(2,1)S(1)} %get-tuple-element.75), channel_id=1, source_target_pairs={{0,16},{4,20},{8,24},{12,28},{16,0},{20,4},{24,8},{28,12},{1,17},{... | collective-permute-start | bytes 503816 | tf_op jit(solution)/shard_map/ppermute | solution.py:464
  43.1 2.3 %collective-permute-start.13 = (bf16[16,5248]{1,0:T(8,128)(2,1)S(1)}, bf16[16,5248]{1,0:T(8,128)(2,1)S(1)}, u32[]{:S(2)}, u32[]{:S(2)}) collective-permute-start(bf16[16,5248]{1,0:T(8,128)(2,1)S(1)} %get-tuple-element.77), channel_id=1, source_target_pairs={{0,24},{4,28},{8,16},{12,20},{16,8},{20,12},{24,0},{28,4},{1,25},{... | collective-permute-start | bytes 503816 | tf_op jit(solution)/shard_map/ppermute | solution.py:464
  47.2 1.8 %collective-permute-start.10 = (bf16[16,5248]{1,0:T(8,128)(2,1)S(1)}, bf16[16,5248]{1,0:T(8,128)(2,1)S(1)}, u32[]{:S(2)}, u32[]{:S(2)}) collective-permute-start(bf16[16,5248]{1,0:T(8,128)(2,1)S(1)} %get-tuple-element.73), channel_id=1, source_target_pairs={{0,8},{4,12},{8,0},{12,4},{16,24},{20,28},{24,16},{28,20},{1,9},{5... | collective-permute-start | bytes 503816 | tf_op jit(solution)/shard_map/ppermute | solution.py:464
  49.0 10.2 %collective-permute-done.11.refs_4_ = bf16[16,5248]{1,0:T(8,128)(2,1)S(1)} collective-permute-done((bf16[16,5248]{1,0:T(8,128)(2,1)S(1)}, bf16[16,5248]{1,0:T(8,128)(2,1)S(1)}, u32[]{:S(2)}, u32[]{:S(2)}) %collective-permute-start.11) | collective-permute-done | bytes 167968 | tf_op jit(solution)/shard_map/ppermute | solution.py:464
  59.2 3.6 %collective-permute-done.12.refs_5_ = bf16[16,5248]{1,0:T(8,128)(2,1)S(1)} collective-permute-done((bf16[16,5248]{1,0:T(8,128)(2,1)S(1)}, bf16[16,5248]{1,0:T(8,128)(2,1)S(1)}, u32[]{:S(2)}, u32[]{:S(2)}) %collective-permute-start.12) | collective-permute-done | bytes 167968 | tf_op jit(solution)/shard_map/ppermute | solution.py:464
  62.8 4.6 %collective-permute-done.13.refs_6_ = bf16[16,5248]{1,0:T(8,128)(2,1)S(1)} collective-permute-done((bf16[16,5248]{1,0:T(8,128)(2,1)S(1)}, bf16[16,5248]{1,0:T(8,128)(2,1)S(1)}, u32[]{:S(2)}, u32[]{:S(2)}) %collective-permute-start.13) | collective-permute-done | bytes 167968 | tf_op jit(solution)/shard_map/ppermute | solution.py:464
  67.4 1.8 %collective-permute-done.14.refs_7_ = bf16[16,5248]{1,0:T(8,128)(2,1)S(1)} collective-permute-done((bf16[16,5248]{1,0:T(8,128)(2,1)S(1)}, bf16[16,5248]{1,0:T(8,128)(2,1)S(1)}, u32[]{:S(2)}, u32[]{:S(2)}) %collective-permute-start.14) | collective-permute-done | bytes 167968 | tf_op jit(solution)/shard_map/ppermute | solution.py:464
  69.2 1.5 %shard_map.102 = bf16[128,5120]{1,0:T(8,128)(2,1)} custom-call(bf16[16,5248]{1,0:T(8,128)(2,1)S(1)} %get-tuple-element.68.refs_0_, bf16[16,5248]{1,0:T(8,128)(2,1)S(1)} %collective-permute-done.9.refs_1_, bf16[16,5248]{1,0:T(8,128)(2,1)S(1)} %collective-permute-done.10.refs_2_, bf16[16,5248]{1,0:T(8,128)(2,1)S(1)} %collective-permute-done.8.refs_3_, ...), custom_call_target="tpu_custom_call" | custom-call | tf_op jit(solution)/shard_map/pallas_call | solution.py:383
  (32 shorter events, 7.4 us)
Async XLA Ops:
  0.0 17.1 %copy-start.3 = (s32[2048]{0:T(1024)S(1)}, s32[2048]{0:T(1024)}, u32[]{:S(2)}) copy-start(s32[2048]{0:T(1024)} %param.9) | copy-start | bytes 24580
  0.0 17.1 %copy-start.4 = (s32[8,8]{1,0:T(8,128)S(1)}, s32[8,8]{1,0:T(8,128)}, u32[]{:S(2)}) copy-start(s32[8,8]{1,0:T(8,128)} %mask_ref.1) | copy-start | bytes 772
  1.4 9.6 %collective-permute-start = (bf16[640,256]{1,0:T(8,128)(2,1)S(1)}, bf16[640,256]{1,0:T(8,128)(2,1)S(1)}, u32[]{:S(2)}, u32[]{:S(2)}) collective-permute-start(bf16[640,256]{1,0:T(8,128)(2,1)S(1)} %get-tuple-element.48), channel_id=1, source_target_pairs={{0,4},{4,0},{8,12},{12,8},{16,20},{20,16},{24,28},{28,24},{1,5},{5... | collective-permute-start | bytes 983048 | tf_op jit(solution)/shard_map/ppermute | solution.py:431
  1.9 11.1 %collective-permute-start.1 = (bf16[640,256]{1,0:T(8,128)(2,1)S(1)}, bf16[640,256]{1,0:T(8,128)(2,1)S(1)}, u32[]{:S(2)}, u32[]{:S(2)}) collective-permute-start(bf16[640,256]{1,0:T(8,128)(2,1)S(1)} %get-tuple-element.49.refs_1_), channel_id=1, source_target_pairs={{4,12},{8,0},{12,20},{16,8},{20,28},{24,16},{5,13},{9,1},{13,21},{... | collective-permute-start | bytes 983048 | tf_op jit(solution)/shard_map/ppermute | solution.py:432
  5.4 11.1 %collective-permute-start.3 = (bf16[640,256]{1,0:T(8,128)(2,1)S(1)}, bf16[640,256]{1,0:T(8,128)(2,1)S(1)}, u32[]{:S(2)}, u32[]{:S(2)}) collective-permute-start(bf16[640,256]{1,0:T(8,128)(2,1)S(1)} %get-tuple-element.49.refs_1_), channel_id=1, source_target_pairs={{0,8},{8,16},{12,4},{16,24},{20,12},{28,20},{1,9},{9,17},{13,5},{1... | collective-permute-start | bytes 983048 | tf_op jit(solution)/shard_map/ppermute | solution.py:433
  7.8 1.0 %copy-start.2 = (bf16[256,640]{1,0:T(8,128)(2,1)S(1)}, bf16[256,640]{1,0:T(8,128)(2,1)}, u32[]{:S(2)}) copy-start(bf16[256,640]{1,0:T(8,128)(2,1)} %refs_0_.2) | copy-start | bytes 983044
  9.1 7.5 %collective-permute-start.4 = (bf16[320,256]{1,0:T(8,128)(2,1)S(1)}, bf16[320,256]{1,0:T(8,128)(2,1)S(1)}, u32[]{:S(2)}, u32[]{:S(2)}) collective-permute-start(bf16[320,256]{1,0:T(8,128)(2,1)S(1)} %get-tuple-element.50), channel_id=1, source_target_pairs={{0,4},{4,0},{8,12},{12,8},{16,20},{20,16},{24,28},{28,24},{1,5},{5... | collective-permute-start | bytes 491528 | tf_op jit(solution)/shard_map/ppermute | solution.py:434
  13.0 17.2 %collective-permute-start.2 = (bf16[1280,256]{1,0:T(8,128)(2,1)S(1)}, bf16[1280,256]{1,0:T(8,128)(2,1)S(1)}, u32[]{:S(2)}, u32[]{:S(2)}) collective-permute-start(bf16[1280,256]{1,0:T(8,128)(2,1)S(1)} %shard_map.94), channel_id=1, source_target_pairs={{4,12},{8,0},{12,20},{16,8},{20,28},{24,16},{5,13},{9,1},{13,21},{... | collective-permute-start | bytes 1966088 | tf_op jit(solution)/shard_map/ppermute | solution.py:437
  16.6 8.0 %collective-permute-start.5 = (bf16[640,256]{1,0:T(8,128)(2,1)S(1)}, bf16[640,256]{1,0:T(8,128)(2,1)S(1)}, u32[]{:S(2)}, u32[]{:S(2)}) collective-permute-start(bf16[640,256]{1,0:T(8,128)(2,1)S(1)} %collective-permute-done.refs_0_.refs_2_), channel_id=1, source_target_pairs={{0,8},{4,0},{8,16},{12,4},{16,24},{20,12},{24,28},{28,20},{1,9},{5... | collective-permute-start | bytes 983048 | tf_op jit(solution)/shard_map/ppermute | solution.py:436
  24.6 7.8 %collective-permute-start.6 = (bf16[640,256]{1,0:T(8,128)(2,1)S(1)}, bf16[640,256]{1,0:T(8,128)(2,1)S(1)}, u32[]{:S(2)}, u32[]{:S(2)}) collective-permute-start(bf16[640,256]{1,0:T(8,128)(2,1)S(1)} %collective-permute-done.5.refs_2_.refs_5_), channel_id=1, source_target_pairs={{0,8},{4,0},{8,16},{12,4},{16,24},{20,12},{24,28},{28,20},{1,9},{5... | collective-permute-start | bytes 983048 | tf_op jit(solution)/shard_map/ppermute | solution.py:443
  31.5 2.9 %copy-start = (bf16[640,1280]{1,0:T(8,128)(2,1)S(1)}, bf16[640,1280]{1,0:T(8,128)(2,1)}, u32[]{:S(2)}) copy-start(bf16[640,1280]{1,0:T(8,128)(2,1)} %weight_ref.5) | copy-start | bytes 4915204
  31.5 2.9 %copy-start.1 = (bf16[256,1280]{1,0:T(8,128)(2,1)S(1)}, bf16[256,1280]{1,0:T(8,128)(2,1)}, u32[]{:S(2)}) copy-start(bf16[256,1280]{1,0:T(8,128)(2,1)} %tokens_ref.1) | copy-start | bytes 1966084
  31.5 2.9 %copy-start.5 = (s32[64]{0:T(128)S(1)}, s32[64]{0:T(128)}, u32[]{:S(2)}) copy-start(s32[64]{0:T(128)} %param.16) | copy-start | bytes 772
  31.5 2.9 %copy-start.6 = (s32[64]{0:T(128)S(1)}, s32[64]{0:T(128)}, u32[]{:S(2)}) copy-start(s32[64]{0:T(128)} %param.17) | copy-start | bytes 772
  31.5 5.4 %collective-permute-start.7 = (bf16[320,256]{1,0:T(8,128)(2,1)S(1)}, bf16[320,256]{1,0:T(8,128)(2,1)S(1)}, u32[]{:S(2)}, u32[]{:S(2)}) collective-permute-start(bf16[320,256]{1,0:T(8,128)(2,1)S(1)} %shard_map.99), channel_id=1, source_target_pairs={{0,4},{4,0},{8,12},{12,8},{16,20},{20,16},{24,28},{28,24},{1,5},{5... | collective-permute-start | bytes 491528 | tf_op jit(solution)/shard_map/ppermute | solution.py:448
  39.0 8.2 %collective-permute-start.8 = (bf16[16,5248]{1,0:T(8,128)(2,1)S(1)}, bf16[16,5248]{1,0:T(8,128)(2,1)S(1)}, u32[]{:S(2)}, u32[]{:S(2)}) collective-permute-start(bf16[16,5248]{1,0:T(8,128)(2,1)S(1)} %get-tuple-element.71), channel_id=1, source_target_pairs={{0,12},{4,8},{8,4},{12,0},{16,28},{20,24},{24,20},{28,16},{1,13},{... | collective-permute-start | bytes 503816 | tf_op jit(solution)/shard_map/ppermute | solution.py:464
  40.5 18.7 %collective-permute-start.11 = (bf16[16,5248]{1,0:T(8,128)(2,1)S(1)}, bf16[16,5248]{1,0:T(8,128)(2,1)S(1)}, u32[]{:S(2)}, u32[]{:S(2)}) collective-permute-start(bf16[16,5248]{1,0:T(8,128)(2,1)S(1)} %get-tuple-element.75), channel_id=1, source_target_pairs={{0,16},{4,20},{8,24},{12,28},{16,0},{20,4},{24,8},{28,12},{1,17},{... | collective-permute-start | bytes 503816 | tf_op jit(solution)/shard_map/ppermute | solution.py:464
  43.1 19.7 %collective-permute-start.12 = (bf16[16,5248]{1,0:T(8,128)(2,1)S(1)}, bf16[16,5248]{1,0:T(8,128)(2,1)S(1)}, u32[]{:S(2)}, u32[]{:S(2)}) collective-permute-start(bf16[16,5248]{1,0:T(8,128)(2,1)S(1)} %get-tuple-element.76), channel_id=1, source_target_pairs={{0,20},{4,16},{8,28},{12,24},{16,4},{20,0},{24,12},{28,8},{1,21},{... | collective-permute-start | bytes 503816 | tf_op jit(solution)/shard_map/ppermute | solution.py:464
  43.1 24.3 %collective-permute-start.13 = (bf16[16,5248]{1,0:T(8,128)(2,1)S(1)}, bf16[16,5248]{1,0:T(8,128)(2,1)S(1)}, u32[]{:S(2)}, u32[]{:S(2)}) collective-permute-start(bf16[16,5248]{1,0:T(8,128)(2,1)S(1)} %get-tuple-element.77), channel_id=1, source_target_pairs={{0,24},{4,28},{8,16},{12,20},{16,8},{20,12},{24,0},{28,4},{1,25},{... | collective-permute-start | bytes 503816 | tf_op jit(solution)/shard_map/ppermute | solution.py:464
  45.4 23.8 %collective-permute-start.14 = (bf16[16,5248]{1,0:T(8,128)(2,1)S(1)}, bf16[16,5248]{1,0:T(8,128)(2,1)S(1)}, u32[]{:S(2)}, u32[]{:S(2)}) collective-permute-start(bf16[16,5248]{1,0:T(8,128)(2,1)S(1)} %get-tuple-element.78), channel_id=1, source_target_pairs={{0,28},{4,24},{8,20},{12,16},{16,12},{20,8},{24,4},{28,0},{1,29},{... | collective-permute-start | bytes 503816 | tf_op jit(solution)/shard_map/ppermute | solution.py:464
  47.2 21.9 %collective-permute-start.10 = (bf16[16,5248]{1,0:T(8,128)(2,1)S(1)}, bf16[16,5248]{1,0:T(8,128)(2,1)S(1)}, u32[]{:S(2)}, u32[]{:S(2)}) collective-permute-start(bf16[16,5248]{1,0:T(8,128)(2,1)S(1)} %get-tuple-element.73), channel_id=1, source_target_pairs={{0,8},{4,12},{8,0},{12,4},{16,24},{20,28},{24,16},{28,20},{1,9},{5... | collective-permute-start | bytes 503816 | tf_op jit(solution)/shard_map/ppermute | solution.py:464
  59.2 10.0 %collective-permute-start.9 = (bf16[16,5248]{1,0:T(8,128)(2,1)S(1)}, bf16[16,5248]{1,0:T(8,128)(2,1)S(1)}, u32[]{:S(2)}, u32[]{:S(2)}) collective-permute-start(bf16[16,5248]{1,0:T(8,128)(2,1)S(1)} %get-tuple-element.72), channel_id=1, source_target_pairs={{0,4},{4,0},{8,12},{12,8},{16,20},{20,16},{24,28},{28,24},{1,5},{5... | collective-permute-start | bytes 503816 | tf_op jit(solution)/shard_map/ppermute | solution.py:464

commit v25 on v23

--- a/solution.py
+++ b/solution.py
@@ -269,13 +269,13 @@
 
 
 def begin_kernel(
-    pair_rows, pieces, where_ref, owners_ref, offsets_ref, own_ref, weight_ref, tokens_ref,
+    pair_rows, few, where_ref, owners_ref, offsets_ref, own_ref, weight_ref, tokens_ref,
     hidden_ref, meta_ref,
 ):
     rows = tokens_ref.shape[0]
     mrows = rows // 4
     owner = owners_ref[...]
-    if pieces > 1:
+    if few:
         owner = owner ^ where_ref[0]
     owner = jnp.broadcast_to(owner.astype(jnp.float32), (mrows, mrows))
     earlier = lax.broadcasted_iota(jnp.int32, (mrows, mrows), 0)
@@ -299,9 +299,9 @@
     )
 
 
-def begin(where, owners, offsets, own, out_weight, tokens, pieces, pair_rows):
-    return pl.pallas_call(
-        functools.partial(begin_kernel, pair_rows, pieces),
+def begin(where, owners, offsets, own, out_weight, tokens, few, pair_rows):
+    return pl.pallas_call(
+        functools.partial(begin_kernel, pair_rows, few),
         out_shape=[
             jax.ShapeDtypeStruct(tokens.shape, jnp.float32),
             jax.ShapeDtypeStruct((16, tokens.shape[0]), jnp.float32),
@@ -312,9 +312,15 @@
     )(where, owners, offsets, own, out_weight, tokens)
 
 
-def project_kernel(order, where_ref, hidden_ref, meta_ref, other_ref, weight_ref, *outs):
-    piece = outs[0].shape[0]
-    slots = piece * len(outs)
+def share(outs, columns, block):
+    first = 0
+    for out in outs:
+        out[:, columns] = block[first : first + out.shape[0]]
+        first += out.shape[0]
+
+
+def project_kernel(where_ref, hidden_ref, meta_ref, other_ref, weight_ref, *outs):
+    slots = sum(out.shape[0] for out in outs)
     rows, width = hidden_ref.shape
     capacity = rows // 2
     meta = meta_ref[...]
@@ -333,33 +339,47 @@
             offset = jnp.where(mine, meta[1:2] - capacity, 0.0)
             offset = capacity + jnp.sum(offset, axis=1, keepdims=True)
             offset = jnp.broadcast_to(offset, (slots, 128)).astype(jnp.bfloat16)
-            for d, out in zip(order, outs):
-                out[:, 4 * width :] = offset[d * piece : (d + 1) * piece]
+            share(outs, slice(4 * width, None), offset)
         pick = jnp.where(mine, 1.0, 0.0).astype(jnp.bfloat16)
         picked = jnp.dot(pick, hidden, preferred_element_type=jnp.float32).astype(jnp.bfloat16)
-        for d, out in zip(order, outs):
-            out[:, j * width : (j + 1) * width] = picked[d * piece : (d + 1) * piece]
-
-
-def project(where, hidden, meta, other, out_weight, order, slots):
+        share(outs, slice(j * width, (j + 1) * width), picked)
+
+
+def project(where, hidden, meta, other, out_weight, sizes):
     width = hidden.shape[1]
-    pieces = len(order)
-    return pl.pallas_call(
-        functools.partial(project_kernel, order),
-        out_shape=[jax.ShapeDtypeStruct((slots // pieces, 4 * width + 128), jnp.bfloat16)] * pieces,
+    return pl.pallas_call(
+        project_kernel,
+        out_shape=[jax.ShapeDtypeStruct((rows, 4 * width + 128), jnp.bfloat16) for rows in sizes],
         in_specs=[smem()] + [vmem()] * 4,
-        out_specs=[vmem()] * pieces,
+        out_specs=[vmem()] * len(sizes),
         compiler_params=limit(24),
     )(where, hidden, meta, other, out_weight)
 
 
-def place_kernel(*refs):
+def join_kernel(rows, first_ref, second_ref, out_ref):
+    out_ref[:rows, :] = first_ref[...]
+    out_ref[rows:, :] = second_ref[rows:, :]
+
+
+def join(first, second):
+    return pl.pallas_call(
+        functools.partial(join_kernel, first.shape[0]),
+        out_shape=jax.ShapeDtypeStruct(second.shape, second.dtype),
+        in_specs=[vmem()] * 2,
+        out_specs=vmem(),
+        compiler_params=limit(16),
+    )(first, second)
+
+
+def place_kernel(kept, *refs):
     *arrived, out_hbm, held, sems = refs
     capacity, merged = out_hbm.shape
     step = merged // 4
 
     def columns_of(start, size):
-        return jnp.concatenate([ref[:, start : start + size] for ref in arrived], axis=0)
+        return jnp.concatenate(
+            [ref[:rows, start : start + size] for rows, ref in zip(kept, arrived)], axis=0
+        )
 
     offset = columns_of(merged, 128).astype(jnp.float32)[:, :1]
     row = lax.broadcasted_iota(jnp.int32, (offset.shape[0], capacity), 1).astype(jnp.float32)
@@ -379,9 +399,9 @@
         store.wait()
 
 
-def place(arrived, capacity, merged):
-    return pl.pallas_call(
-        place_kernel,
+def place(arrived, kept, capacity, merged):
+    return pl.pallas_call(
+        functools.partial(place_kernel, kept),
         out_shape=jax.ShapeDtypeStruct((capacity, merged), jnp.bfloat16),
         in_specs=[vmem()] * len(arrived),
         out_specs=anywhere(),
@@ -449,28 +469,27 @@
     far = (ahead_both, back_other, back_far)
     own = attention(*fixed, (own_q,), (0,), far, (4, 6, 5, 7), own, True)
 
-    order = tuple(range(nblocks)) if nblocks in (4, 8) else (0,)
+    few = nblocks == 8
     hidden, meta = begin(
-        where, owners[None, :], offsets[None, :], own, out_weight, tokens, len(order), pair_rows
-    )
-    outgoing = project(where, hidden, meta, other, out_weight, order, slots)
-    if len(order) > 1:
-        arrived = list(outgoing)
-
-        def cross(d):
-            arrived[d] = lax.ppermute(arrived[d], "blk", [(i, i ^ d) for i in range(nblocks)])
-
-        short, *late = range(nblocks // 2 - 1, 0, -1)
-        for d in (*range(nblocks // 2, nblocks), short):
-            cross(d)
-        group = lax.optimization_barrier([arrived[d] for d in (short, *late)])
-        for d, block in zip((short, *late), group):
-            arrived[d] = block
-        for d in late:
-            cross(d)
+        where, owners[None, :], offsets[None, :], own, out_weight, tokens, few, pair_rows
+    )
+    if few:
+        def cross(block, d):
+            return lax.ppermute(block, "blk", [(i, i ^ d) for i in range(nblocks)])
+
+        own, one, two, *far = project(
+            where, hidden, meta, other, out_weight, [pair_rows * n for n in (1, 1, 2, 1, 1, 1, 1)]
+        )
+        far = [cross(block, d) for d, block in zip(range(4, 8), far)]
+        two = cross(two, 2)
+        one = cross(join(one, two), 1)
+        arrived = [own, one, two, *far]
+        kept = [pair_rows * n for n in (1, 2, 1, 1, 1, 1, 1)]
     else:
+        outgoing = project(where, hidden, meta, other, out_weight, [slots])
         arrived = [lax.all_to_all(outgoing[0], "blk", split_axis=0, concat_axis=0, tiled=True)]
-    return place(arrived, capacity, 4 * width)
+        kept = [slots]
+    return place(arrived, kept, capacity, 4 * width)
 
 
 def solution(mesh):

time: 70.6 us -> 76 us (1.076)
  waiting for transfers between devices: 30 us -> 37.8 us
  starting transfers between devices: 25.2 us -> 22.9 us
    ppermute x7 -> x6, waiting for transfers between devices: 19 us -> 26.8 us  [cross(): return lax.ppermute(block, 'blk', [(i, i ^ d) for i in range(nblocks)])]
    ppermute x7 -> x6, starting transfers between devices: 11.1 us -> 8.77 us  [cross(): return lax.ppermute(block, 'blk', [(i, i ^ d) for i in range(nblocks)])]
    pallas_call x3 -> x4, Pallas kernels: 3.06 us -> 3.08 us  [the longest x1 1.45 us: place(): pl.pallas_call(functools.partial(place_kernel, kept), out_shape=jax.Shape...]
  transfers between devices with their start and end apart: 15 -> 14, of which waited for: 10 -> 10; matrix products, arithmetic and copies ran while one was open for 0% -> 0% of each run, Pallas kernels for 13% -> 12%
where the time goes in v25:
time: 76 us; the launch traced here: 75.1 us
  waiting for transfers between devices  37.8 us (50%)
  starting transfers between devices  22.9 us (30%)
  Pallas kernels  13.1 us (17%)
  local copies, waits for them, and re-layouts  1 us (1%)
    ppermute x6, waiting for transfers between devices, cross(): return lax.ppermute(block, 'blk', [(i, i ^ d) for i in range(nblocks)])  26.8 us
    ppermute x6, starting transfers between devices, cross(): return lax.ppermute(block, 'blk', [(i, i ^ d) for i in range(nblocks)])  8.77 us
    pallas_call x4, Pallas kernels, attention(): pl.pallas_call(functools.partial(attention_kernel, kinds, numbers, rows_o...  7.61 us
    ppermute x1, waiting for transfers between devices, per_device(): back_other = relay(ready)  4.28 us
    ppermute x1, starting transfers between devices, per_device(): ahead_both = ahead(stack(other_kv, ahead_own))  3.48 us
    ppermute x1, starting transfers between devices, per_device(): ahead_own = ahead(own_kv)  3.47 us
    ppermute x1, waiting for transfers between devices, per_device(): ahead_both = ahead(stack(other_kv, ahead_own))  2.96 us
    ppermute x1, starting transfers between devices, per_device(): back_own = back(own_kv)  2.37 us
  transfers between devices with their start and end apart: 14, of which 10 were waited for; matrix products, arithmetic and copies ran while one was open for 0% of the time, Pallas kernels for 12%

profile of v25, /device:TPU:14, one launch (start us, length us, event | category | flops | bytes accessed | tf_op | source)
XLA Modules:
  0.0 75.1 jit_solution(13364567163177804786)
XLA Ops:
  0.0 1.4 %shard_map.92 = (bf16[640,256]{1,0:T(8,128)(2,1)S(1)}, bf16[640,256]{1,0:T(8,128)(2,1)S(1)}) custom-call(s32[1]{0:T(128)} %bitcast.where_ref, bf16[256,640]{1,0:T(8,128)(2,1)} %refs_0_.1, bf16[256,640]{1,0:T(8,128)(2,1)} %refs_1_.1), custom_call_target="tpu_custom_call" | custom-call | tf_op jit(solution)/shard_map/pallas_call | solution.py:68
  1.9 3.5 %collective-permute-start.1 = (bf16[640,256]{1,0:T(8,128)(2,1)S(1)}, bf16[640,256]{1,0:T(8,128)(2,1)S(1)}, u32[]{:S(2)}, u32[]{:S(2)}) collective-permute-start(bf16[640,256]{1,0:T(8,128)(2,1)S(1)} %get-tuple-element.40.refs_1_), channel_id=1, source_target_pairs={{4,12},{8,0},{12,20},{16,8},{20,28},{24,16},{5,13},{9,1},{13,21},{... | collective-permute-start | bytes 983048 | tf_op jit(solution)/shard_map/ppermute | solution.py:452
  5.4 2.4 %collective-permute-start.3 = (bf16[640,256]{1,0:T(8,128)(2,1)S(1)}, bf16[640,256]{1,0:T(8,128)(2,1)S(1)}, u32[]{:S(2)}, u32[]{:S(2)}) collective-permute-start(bf16[640,256]{1,0:T(8,128)(2,1)S(1)} %get-tuple-element.40.refs_1_), channel_id=1, source_target_pairs={{0,8},{8,16},{12,4},{16,24},{20,12},{28,20},{1,9},{9,17},{13,5},{1... | collective-permute-start | bytes 983048 | tf_op jit(solution)/shard_map/ppermute | solution.py:453
  9.1 1.6 %collective-permute-start.4 = (bf16[320,256]{1,0:T(8,128)(2,1)S(1)}, bf16[320,256]{1,0:T(8,128)(2,1)S(1)}, u32[]{:S(2)}, u32[]{:S(2)}) collective-permute-start(bf16[320,256]{1,0:T(8,128)(2,1)S(1)} %get-tuple-element.41), channel_id=1, source_target_pairs={{0,4},{4,0},{8,12},{12,8},{16,20},{20,16},{24,28},{28,24},{1,5},{5... | collective-permute-start | bytes 491528 | tf_op jit(solution)/shard_map/ppermute | solution.py:454
  11.0 2.0 %collective-permute-done.1.refs_1_.refs_3_ = bf16[640,256]{1,0:T(8,128)(2,1)S(1)} collective-permute-done((bf16[640,256]{1,0:T(8,128)(2,1)S(1)}, bf16[640,256]{1,0:T(8,128)(2,1)S(1)}, u32[]{:S(2)}, u32[]{:S(2)}) %collective-permute-start.1) | collective-permute-done | bytes 327712 | tf_op jit(solution)/shard_map/ppermute | solution.py:452
  13.0 3.5 %collective-permute-start.2 = (bf16[1280,256]{1,0:T(8,128)(2,1)S(1)}, bf16[1280,256]{1,0:T(8,128)(2,1)S(1)}, u32[]{:S(2)}, u32[]{:S(2)}) collective-permute-start(bf16[1280,256]{1,0:T(8,128)(2,1)S(1)} %shard_map.94), channel_id=1, source_target_pairs={{4,12},{8,0},{12,20},{16,8},{20,28},{24,16},{5,13},{9,1},{13,21},{... | collective-permute-start | bytes 1966088 | tf_op jit(solution)/shard_map/ppermute | solution.py:457
  17.8 2.5 %shard_map.95 = (f32[1,4,256,128]{3,2,1,0:T(8,128)S(1)}, f32[1,4,256,128]{3,2,1,0:T(8,128)S(1)}) custom-call(s32[1]{0:T(128)} %bitcast.where_ref, s32[8,128]{1,0:T(8,128)S(1)} %get-tuple-element.33.need_ref, f32[1,2048]{1,0:T(1,128)S(1)} %get-tuple-element.34.seg_ref, bf16[320,256]{1,0:T(8,128)(2,1)S(1)} %get-tuple-element.38.refs_0_, ...), custom_call_target="tpu_custom_call" | custom-call | flops 1000 | bytes 1000 | tf_op jit(solution)/shard_map/pallas_call | solution.py:231
  20.3 4.3 %collective-permute-done.5.refs_2_.refs_5_ = bf16[640,256]{1,0:T(8,128)(2,1)S(1)} collective-permute-done((bf16[640,256]{1,0:T(8,128)(2,1)S(1)}, bf16[640,256]{1,0:T(8,128)(2,1)S(1)}, u32[]{:S(2)}, u32[]{:S(2)}) %collective-permute-start.5) | collective-permute-done | bytes 327712 | tf_op jit(solution)/shard_map/ppermute | solution.py:456
  25.1 2.2 %shard_map.98 = (f32[1,4,256,128]{3,2,1,0:T(8,128)S(1)}, f32[1,4,256,128]{3,2,1,0:T(8,128)S(1)}) custom-call(s32[1]{0:T(128)} %bitcast.where_ref, s32[8,128]{1,0:T(8,128)S(1)} %get-tuple-element.33.need_ref, f32[1,2048]{1,0:T(1,128)S(1)} %get-tuple-element.34.seg_ref, bf16[320,256]{1,0:T(8,128)(2,1)S(1)} %collective-permute-done.4.refs_0_, ...), custom_call_target="tpu_custom_call" | custom-call | flops 1000 | bytes 1000 | tf_op jit(solution)/shard_map/pallas_call | solution.py:231
  27.3 3.0 %collective-permute-done.2.refs_1_ = bf16[1280,256]{1,0:T(8,128)(2,1)S(1)} collective-permute-done((bf16[1280,256]{1,0:T(8,128)(2,1)S(1)}, bf16[1280,256]{1,0:T(8,128)(2,1)S(1)}, u32[]{:S(2)}, u32[]{:S(2)}) %collective-permute-start.2) | collective-permute-done | bytes 655392 | tf_op jit(solution)/shard_map/ppermute | solution.py:457
  30.2 1.2 %shard_map.99 = bf16[320,256]{1,0:T(8,128)(2,1)S(1)} custom-call(s32[1]{0:T(128)} %bitcast.where_ref, s32[8,128]{1,0:T(8,128)S(1)} %get-tuple-element.33.need_ref, f32[1,2048]{1,0:T(1,128)S(1)} %get-tuple-element.34.seg_ref, bf16[320,256]{1,0:T(8,128)(2,1)S(1)} %collective-permute-done.4.refs_0_, bf16[1280,256]{1,0:T(8,128)(2,1)S(1)} %collective-permute-done.2.refs_1_, ...), custom_call_target="tpu_custom_call" | custom-call | flops 1000 | bytes 1000 | tf_op jit(solution)/shard_map/pallas_call | solution.py:231
  31.5 1.6 %collective-permute-start.7 = (bf16[320,256]{1,0:T(8,128)(2,1)S(1)}, bf16[320,256]{1,0:T(8,128)(2,1)S(1)}, u32[]{:S(2)}, u32[]{:S(2)}) collective-permute-start(bf16[320,256]{1,0:T(8,128)(2,1)S(1)} %shard_map.99), channel_id=1, source_target_pairs={{0,4},{4,0},{8,12},{12,8},{16,20},{20,16},{24,28},{28,24},{1,5},{5... | collective-permute-start | bytes 491528 | tf_op jit(solution)/shard_map/ppermute | solution.py:468
  33.1 1.7 %shard_map.96.own_ref = bf16[320,256]{1,0:T(8,128)(2,1)S(1)} custom-call(s32[1]{0:T(128)} %bitcast.where_ref, s32[8,128]{1,0:T(8,128)S(1)} %get-tuple-element.33.need_ref, f32[1,2048]{1,0:T(1,128)S(1)} %get-tuple-element.34.seg_ref, bf16[320,256]{1,0:T(8,128)(2,1)S(1)} %get-tuple-element.38.refs_0_, bf16[1280,256]{1,0:T(8,128)(2,1)S(1)} %collective-permute-done.2.refs_1_, ...), custom_call_target="tpu_custom_call" | custom-call | flops 1000 | bytes 1000 | tf_op jit(solution)/shard_map/pallas_call | solution.py:231
  35.5 1.4 %collective-permute-done.7.other_ref = bf16[320,256]{1,0:T(8,128)(2,1)S(1)} collective-permute-done((bf16[320,256]{1,0:T(8,128)(2,1)S(1)}, bf16[320,256]{1,0:T(8,128)(2,1)S(1)}, u32[]{:S(2)}, u32[]{:S(2)}) %collective-permute-start.7) | collective-permute-done | bytes 163872 | tf_op jit(solution)/shard_map/ppermute | solution.py:468
  38.0 7.1 %collective-permute-done.8.second_ref.refs_2_ = bf16[32,5248]{1,0:T(8,128)(2,1)S(1)} collective-permute-done((bf16[32,5248]{1,0:T(8,128)(2,1)S(1)}, bf16[32,5248]{1,0:T(8,128)(2,1)S(1)}, u32[]{:S(2)}, u32[]{:S(2)}) %collective-permute-start.8) | collective-permute-done | bytes 335904 | tf_op jit(solution)/shard_map/ppermute | solution.py:478
  45.1 2.3 %collective-permute-start.9 = (bf16[32,5248]{1,0:T(8,128)(2,1)S(1)}, bf16[32,5248]{1,0:T(8,128)(2,1)S(1)}, u32[]{:S(2)}, u32[]{:S(2)}) collective-permute-start(bf16[32,5248]{1,0:T(8,128)(2,1)S(1)} %shard_map.101), channel_id=1, source_target_pairs={{0,4},{4,0},{8,12},{12,8},{16,20},{20,16},{24,28},{28,24},{1,5},{5... | collective-permute-start | bytes 1007624 | tf_op jit(solution)/shard_map/ppermute | solution.py:478
  47.5 1.5 %collective-permute-start.10 = (bf16[16,5248]{1,0:T(8,128)(2,1)S(1)}, bf16[16,5248]{1,0:T(8,128)(2,1)S(1)}, u32[]{:S(2)}, u32[]{:S(2)}) collective-permute-start(bf16[16,5248]{1,0:T(8,128)(2,1)S(1)} %get-tuple-element.57), channel_id=1, source_target_pairs={{0,16},{4,20},{8,24},{12,28},{16,0},{20,4},{24,8},{28,12},{1,17},{... | collective-permute-start | bytes 503816 | tf_op jit(solution)/shard_map/ppermute | solution.py:478
  49.9 2.5 %collective-permute-start.12 = (bf16[16,5248]{1,0:T(8,128)(2,1)S(1)}, bf16[16,5248]{1,0:T(8,128)(2,1)S(1)}, u32[]{:S(2)}, u32[]{:S(2)}) collective-permute-start(bf16[16,5248]{1,0:T(8,128)(2,1)S(1)} %get-tuple-element.59), channel_id=1, source_target_pairs={{0,24},{4,28},{8,16},{12,20},{16,8},{20,12},{24,0},{28,4},{1,25},{... | collective-permute-start | bytes 503816 | tf_op jit(solution)/shard_map/ppermute | solution.py:478
  52.5 1.4 %collective-permute-start.13 = (bf16[16,5248]{1,0:T(8,128)(2,1)S(1)}, bf16[16,5248]{1,0:T(8,128)(2,1)S(1)}, u32[]{:S(2)}, u32[]{:S(2)}) collective-permute-start(bf16[16,5248]{1,0:T(8,128)(2,1)S(1)} %get-tuple-element.60), channel_id=1, source_target_pairs={{0,28},{4,24},{8,20},{12,16},{16,12},{20,8},{24,4},{28,0},{1,29},{... | collective-permute-start | bytes 503816 | tf_op jit(solution)/shard_map/ppermute | solution.py:478
  53.8 8.8 %collective-permute-done.10.refs_3_ = bf16[16,5248]{1,0:T(8,128)(2,1)S(1)} collective-permute-done((bf16[16,5248]{1,0:T(8,128)(2,1)S(1)}, bf16[16,5248]{1,0:T(8,128)(2,1)S(1)}, u32[]{:S(2)}, u32[]{:S(2)}) %collective-permute-start.10) | collective-permute-done | bytes 167968 | tf_op jit(solution)/shard_map/ppermute | solution.py:478
  62.6 3.6 %collective-permute-done.11.refs_4_ = bf16[16,5248]{1,0:T(8,128)(2,1)S(1)} collective-permute-done((bf16[16,5248]{1,0:T(8,128)(2,1)S(1)}, bf16[16,5248]{1,0:T(8,128)(2,1)S(1)}, u32[]{:S(2)}, u32[]{:S(2)}) %collective-permute-start.11) | collective-permute-done | bytes 167968 | tf_op jit(solution)/shard_map/ppermute | solution.py:478
  66.2 4.8 %collective-permute-done.12.refs_5_ = bf16[16,5248]{1,0:T(8,128)(2,1)S(1)} collective-permute-done((bf16[16,5248]{1,0:T(8,128)(2,1)S(1)}, bf16[16,5248]{1,0:T(8,128)(2,1)S(1)}, u32[]{:S(2)}, u32[]{:S(2)}) %collective-permute-start.12) | collective-permute-done | bytes 167968 | tf_op jit(solution)/shard_map/ppermute | solution.py:478
  71.0 2.5 %collective-permute-done.13.refs_6_ = bf16[16,5248]{1,0:T(8,128)(2,1)S(1)} collective-permute-done((bf16[16,5248]{1,0:T(8,128)(2,1)S(1)}, bf16[16,5248]{1,0:T(8,128)(2,1)S(1)}, u32[]{:S(2)}, u32[]{:S(2)}) %collective-permute-start.13) | collective-permute-done | bytes 167968 | tf_op jit(solution)/shard_map/ppermute | solution.py:478
  73.5 1.5 %shard_map.102 = bf16[128,5120]{1,0:T(8,128)(2,1)} custom-call(bf16[16,5248]{1,0:T(8,128)(2,1)S(1)} %get-tuple-element.54.refs_0_, bf16[32,5248]{1,0:T(8,128)(2,1)S(1)} %collective-permute-done.9.refs_1_, bf16[32,5248]{1,0:T(8,128)(2,1)S(1)} %collective-permute-done.8.second_ref.refs_2_, bf16[16,5248]{1,0:T(8,128)(2,1)S(1)} %collective-permute-done.10.refs_3_, ...), custom_call_target="tpu_custom_call" | custom-call | tf_op jit(solution)/shard_map/pallas_call | solution.py:403
  (30 shorter events, 6.6 us)
Async XLA Ops:
  0.0 17.1 %copy-start.3 = (s32[2048]{0:T(1024)S(1)}, s32[2048]{0:T(1024)}, u32[]{:S(2)}) copy-start(s32[2048]{0:T(1024)} %param.9) | copy-start | bytes 24580
  0.0 17.1 %copy-start.4 = (s32[8,8]{1,0:T(8,128)S(1)}, s32[8,8]{1,0:T(8,128)}, u32[]{:S(2)}) copy-start(s32[8,8]{1,0:T(8,128)} %mask_ref.1) | copy-start | bytes 772
  1.4 9.6 %collective-permute-start = (bf16[640,256]{1,0:T(8,128)(2,1)S(1)}, bf16[640,256]{1,0:T(8,128)(2,1)S(1)}, u32[]{:S(2)}, u32[]{:S(2)}) collective-permute-start(bf16[640,256]{1,0:T(8,128)(2,1)S(1)} %get-tuple-element.39), channel_id=1, source_target_pairs={{0,4},{4,0},{8,12},{12,8},{16,20},{20,16},{24,28},{28,24},{1,5},{5... | collective-permute-start | bytes 983048 | tf_op jit(solution)/shard_map/ppermute | solution.py:451
  1.9 11.1 %collective-permute-start.1 = (bf16[640,256]{1,0:T(8,128)(2,1)S(1)}, bf16[640,256]{1,0:T(8,128)(2,1)S(1)}, u32[]{:S(2)}, u32[]{:S(2)}) collective-permute-start(bf16[640,256]{1,0:T(8,128)(2,1)S(1)} %get-tuple-element.40.refs_1_), channel_id=1, source_target_pairs={{4,12},{8,0},{12,20},{16,8},{20,28},{24,16},{5,13},{9,1},{13,21},{... | collective-permute-start | bytes 983048 | tf_op jit(solution)/shard_map/ppermute | solution.py:452
  5.4 11.1 %collective-permute-start.3 = (bf16[640,256]{1,0:T(8,128)(2,1)S(1)}, bf16[640,256]{1,0:T(8,128)(2,1)S(1)}, u32[]{:S(2)}, u32[]{:S(2)}) collective-permute-start(bf16[640,256]{1,0:T(8,128)(2,1)S(1)} %get-tuple-element.40.refs_1_), channel_id=1, source_target_pairs={{0,8},{8,16},{12,4},{16,24},{20,12},{28,20},{1,9},{9,17},{13,5},{1... | collective-permute-start | bytes 983048 | tf_op jit(solution)/shard_map/ppermute | solution.py:453
  7.8 1.0 %copy-start.2 = (bf16[256,640]{1,0:T(8,128)(2,1)S(1)}, bf16[256,640]{1,0:T(8,128)(2,1)}, u32[]{:S(2)}) copy-start(bf16[256,640]{1,0:T(8,128)(2,1)} %refs_0_.2) | copy-start | bytes 983044
  9.1 7.5 %collective-permute-start.4 = (bf16[320,256]{1,0:T(8,128)(2,1)S(1)}, bf16[320,256]{1,0:T(8,128)(2,1)S(1)}, u32[]{:S(2)}, u32[]{:S(2)}) collective-permute-start(bf16[320,256]{1,0:T(8,128)(2,1)S(1)} %get-tuple-element.41), channel_id=1, source_target_pairs={{0,4},{4,0},{8,12},{12,8},{16,20},{20,16},{24,28},{28,24},{1,5},{5... | collective-permute-start | bytes 491528 | tf_op jit(solution)/shard_map/ppermute | solution.py:454
  13.0 17.2 %collective-permute-start.2 = (bf16[1280,256]{1,0:T(8,128)(2,1)S(1)}, bf16[1280,256]{1,0:T(8,128)(2,1)S(1)}, u32[]{:S(2)}, u32[]{:S(2)}) collective-permute-start(bf16[1280,256]{1,0:T(8,128)(2,1)S(1)} %shard_map.94), channel_id=1, source_target_pairs={{4,12},{8,0},{12,20},{16,8},{20,28},{24,16},{5,13},{9,1},{13,21},{... | collective-permute-start | bytes 1966088 | tf_op jit(solution)/shard_map/ppermute | solution.py:457
  16.6 8.0 %collective-permute-start.5 = (bf16[640,256]{1,0:T(8,128)(2,1)S(1)}, bf16[640,256]{1,0:T(8,128)(2,1)S(1)}, u32[]{:S(2)}, u32[]{:S(2)}) collective-permute-start(bf16[640,256]{1,0:T(8,128)(2,1)S(1)} %collective-permute-done.refs_0_.refs_2_), channel_id=1, source_target_pairs={{0,8},{4,0},{8,16},{12,4},{16,24},{20,12},{24,28},{28,20},{1,9},{5... | collective-permute-start | bytes 983048 | tf_op jit(solution)/shard_map/ppermute | solution.py:456
  24.6 8.5 %collective-permute-start.6 = (bf16[640,256]{1,0:T(8,128)(2,1)S(1)}, bf16[640,256]{1,0:T(8,128)(2,1)S(1)}, u32[]{:S(2)}, u32[]{:S(2)}) collective-permute-start(bf16[640,256]{1,0:T(8,128)(2,1)S(1)} %collective-permute-done.5.refs_2_.refs_5_), channel_id=1, source_target_pairs={{0,8},{4,0},{8,16},{12,4},{16,24},{20,12},{24,28},{28,20},{1,9},{5... | collective-permute-start | bytes 983048 | tf_op jit(solution)/shard_map/ppermute | solution.py:463
  31.5 3.4 %copy-start = (bf16[640,1280]{1,0:T(8,128)(2,1)S(1)}, bf16[640,1280]{1,0:T(8,128)(2,1)}, u32[]{:S(2)}) copy-start(bf16[640,1280]{1,0:T(8,128)(2,1)} %weight_ref.3) | copy-start | bytes 4915204
  31.5 3.4 %copy-start.1 = (bf16[256,1280]{1,0:T(8,128)(2,1)S(1)}, bf16[256,1280]{1,0:T(8,128)(2,1)}, u32[]{:S(2)}) copy-start(bf16[256,1280]{1,0:T(8,128)(2,1)} %tokens_ref.1) | copy-start | bytes 1966084
  31.5 3.4 %copy-start.5 = (s32[64]{0:T(128)S(1)}, s32[64]{0:T(128)}, u32[]{:S(2)}) copy-start(s32[64]{0:T(128)} %param.16) | copy-start | bytes 772
  31.5 3.4 %copy-start.6 = (s32[64]{0:T(128)S(1)}, s32[64]{0:T(128)}, u32[]{:S(2)}) copy-start(s32[64]{0:T(128)} %param.17) | copy-start | bytes 772
  31.5 5.4 %collective-permute-start.7 = (bf16[320,256]{1,0:T(8,128)(2,1)S(1)}, bf16[320,256]{1,0:T(8,128)(2,1)S(1)}, u32[]{:S(2)}, u32[]{:S(2)}) collective-permute-start(bf16[320,256]{1,0:T(8,128)(2,1)S(1)} %shard_map.99), channel_id=1, source_target_pairs={{0,4},{4,0},{8,12},{12,8},{16,20},{20,16},{24,28},{28,24},{1,5},{5... | collective-permute-start | bytes 491528 | tf_op jit(solution)/shard_map/ppermute | solution.py:468
  37.9 7.2 %collective-permute-start.8 = (bf16[32,5248]{1,0:T(8,128)(2,1)S(1)}, bf16[32,5248]{1,0:T(8,128)(2,1)S(1)}, u32[]{:S(2)}, u32[]{:S(2)}) collective-permute-start(bf16[32,5248]{1,0:T(8,128)(2,1)S(1)} %get-tuple-element.56), channel_id=1, source_target_pairs={{0,8},{4,12},{8,0},{12,4},{16,24},{20,28},{24,16},{28,20},{1,9},{5... | collective-permute-start | bytes 1007624 | tf_op jit(solution)/shard_map/ppermute | solution.py:478
  45.1 28.3 %collective-permute-start.9 = (bf16[32,5248]{1,0:T(8,128)(2,1)S(1)}, bf16[32,5248]{1,0:T(8,128)(2,1)S(1)}, u32[]{:S(2)}, u32[]{:S(2)}) collective-permute-start(bf16[32,5248]{1,0:T(8,128)(2,1)S(1)} %shard_map.101), channel_id=1, source_target_pairs={{0,4},{4,0},{8,12},{12,8},{16,20},{20,16},{24,28},{28,24},{1,5},{5... | collective-permute-start | bytes 1007624 | tf_op jit(solution)/shard_map/ppermute | solution.py:478
  47.5 15.2 %collective-permute-start.10 = (bf16[16,5248]{1,0:T(8,128)(2,1)S(1)}, bf16[16,5248]{1,0:T(8,128)(2,1)S(1)}, u32[]{:S(2)}, u32[]{:S(2)}) collective-permute-start(bf16[16,5248]{1,0:T(8,128)(2,1)S(1)} %get-tuple-element.57), channel_id=1, source_target_pairs={{0,16},{4,20},{8,24},{12,28},{16,0},{20,4},{24,8},{28,12},{1,17},{... | collective-permute-start | bytes 503816 | tf_op jit(solution)/shard_map/ppermute | solution.py:478
  49.0 17.2 %collective-permute-start.11 = (bf16[16,5248]{1,0:T(8,128)(2,1)S(1)}, bf16[16,5248]{1,0:T(8,128)(2,1)S(1)}, u32[]{:S(2)}, u32[]{:S(2)}) collective-permute-start(bf16[16,5248]{1,0:T(8,128)(2,1)S(1)} %get-tuple-element.58), channel_id=1, source_target_pairs={{0,20},{4,16},{8,28},{12,24},{16,4},{20,0},{24,12},{28,8},{1,21},{... | collective-permute-start | bytes 503816 | tf_op jit(solution)/shard_map/ppermute | solution.py:478
  49.9 21.1 %collective-permute-start.12 = (bf16[16,5248]{1,0:T(8,128)(2,1)S(1)}, bf16[16,5248]{1,0:T(8,128)(2,1)S(1)}, u32[]{:S(2)}, u32[]{:S(2)}) collective-permute-start(bf16[16,5248]{1,0:T(8,128)(2,1)S(1)} %get-tuple-element.59), channel_id=1, source_target_pairs={{0,24},{4,28},{8,16},{12,20},{16,8},{20,12},{24,0},{28,4},{1,25},{... | collective-permute-start | bytes 503816 | tf_op jit(solution)/shard_map/ppermute | solution.py:478
  52.5 21.0 %collective-permute-start.13 = (bf16[16,5248]{1,0:T(8,128)(2,1)S(1)}, bf16[16,5248]{1,0:T(8,128)(2,1)S(1)}, u32[]{:S(2)}, u32[]{:S(2)}) collective-permute-start(bf16[16,5248]{1,0:T(8,128)(2,1)S(1)} %get-tuple-element.60), channel_id=1, source_target_pairs={{0,28},{4,24},{8,20},{12,16},{16,12},{20,8},{24,4},{28,0},{1,29},{... | collective-permute-start | bytes 503816 | tf_op jit(solution)/shard_map/ppermute | solution.py:478

commit v26 on v23

--- a/solution.py
+++ b/solution.py
@@ -422,6 +422,11 @@
         axis_name="blk",
         perm=route(lambda i: -1 if i == 1 else 1 if i == nblocks - 2 else -2 if i % 2 else 2),
     )
+    ahead_all = functools.partial(
+        lax.ppermute,
+        axis_name="blk",
+        perm=route(lambda i: 1 if i == 0 else -1 if i == nblocks - 1 else 2 if i % 2 else -2),
+    )
 
     where = block_index[None].astype(jnp.int32)
     own_kv, swap_kv = prepare(where, keys, values)
@@ -434,7 +439,7 @@
     other_q = swap(swap_q)
     ready, back_own, other_q = lax.optimization_barrier((other_kv, back_own, other_q))
     back_other = relay(ready)
-    ahead_both = ahead(stack(other_kv, ahead_own))
+    ahead_both = ahead_all(stack(other_kv, ahead_own))
     near = (own_kv, other_kv, ahead_own, back_own)
     near_numbers = (0, 1, 2, 3)
     fixed = (where, need, segs)

time: 70.6 us -> 69 us (0.977)
  starting transfers between devices: 25.2 us -> 21.6 us
  waiting for transfers between devices: 30 us -> 32.4 us
    ppermute x1, starting transfers between devices: 3.48 us -> 1.63 us  [per_device(): ahead_both = ahead_all(stack(other_kv, ahead_own))]
    ppermute x1, waiting for transfers between devices: 0.01 us -> 1.53 us  [per_device(): back_own = back(own_kv)]
    ppermute x1, waiting for transfers between devices: 2.96 us -> 1.56 us  [per_device(): ahead_both = ahead_all(stack(other_kv, ahead_own))]
    ppermute x7, waiting for transfers between devices: 19 us -> 20.1 us  [cross(): lax.ppermute(arrived[d], 'blk', [(i, i ^ d) for i in range(nblocks)])]
    ppermute x7, starting transfers between devices: 11.1 us -> 10.1 us  [cross(): lax.ppermute(arrived[d], 'blk', [(i, i ^ d) for i in range(nblocks)])]
    ppermute x1, starting transfers between devices: 1.59 us -> 0.88 us  [per_device(): other = swap(other)]
  transfers between devices with their start and end apart: 15 -> 15, of which waited for: 10 -> 12; matrix products, arithmetic and copies ran while one was open for 0% -> 0% of each run, Pallas kernels for 13% -> 13%
where the time goes in v26:
time: 69 us; the launch traced here: 67.9 us
  waiting for transfers between devices  32.4 us (47%)
  starting transfers between devices  21.6 us (31%)
  Pallas kernels  12.6 us (18%)
  local copies, waits for them, and re-layouts  1 us (1%)
    ppermute x7, waiting for transfers between devices, cross(): lax.ppermute(arrived[d], 'blk', [(i, i ^ d) for i in range(nblocks)])  20.1 us
    ppermute x7, starting transfers between devices, cross(): lax.ppermute(arrived[d], 'blk', [(i, i ^ d) for i in range(nblocks)])  10.1 us
    pallas_call x4, Pallas kernels, attention(): pl.pallas_call(functools.partial(attention_kernel, kinds, numbers, rows_o...  7.14 us
    ppermute x1, waiting for transfers between devices, per_device(): back_other = relay(ready)  4.77 us
    ppermute x1, starting transfers between devices, per_device(): ahead_own = ahead(own_kv)  3.47 us
    ppermute x1, starting transfers between devices, per_device(): back_own = back(own_kv)  2.37 us
    ppermute x1, waiting for transfers between devices, per_device(): ahead_own = ahead(own_kv)  2.01 us
    pallas_call x2, Pallas kernels, prepare(): pl.pallas_call(functools.partial(prepare_kernel, number), out_shape=[out]...  1.64 us
  transfers between devices with their start and end apart: 15, of which 12 were waited for; matrix products, arithmetic and copies ran while one was open for 0% of the time, Pallas kernels for 13%

profile of v26, /device:TPU:14, one launch (start us, length us, event | category | flops | bytes accessed | tf_op | source)
XLA Modules:
  0.0 67.9 jit_solution(12779903783063965514)
XLA Ops:
  0.0 1.4 %shard_map.92 = (bf16[640,256]{1,0:T(8,128)(2,1)S(1)}, bf16[640,256]{1,0:T(8,128)(2,1)S(1)}) custom-call(s32[1]{0:T(128)} %bitcast.where_ref, bf16[256,640]{1,0:T(8,128)(2,1)} %refs_0_.1, bf16[256,640]{1,0:T(8,128)(2,1)} %refs_1_.1), custom_call_target="tpu_custom_call" | custom-call | tf_op jit(solution)/shard_map/pallas_call | solution.py:68
  1.9 3.5 %collective-permute-start.1 = (bf16[640,256]{1,0:T(8,128)(2,1)S(1)}, bf16[640,256]{1,0:T(8,128)(2,1)S(1)}, u32[]{:S(2)}, u32[]{:S(2)}) collective-permute-start(bf16[640,256]{1,0:T(8,128)(2,1)S(1)} %get-tuple-element.44.refs_1_), channel_id=1, source_target_pairs={{4,12},{8,0},{12,20},{16,8},{20,28},{24,16},{5,13},{9,1},{13,21},{... | collective-permute-start | bytes 983048 | tf_op jit(solution)/shard_map/ppermute | solution.py:437
  5.4 2.4 %collective-permute-start.3 = (bf16[640,256]{1,0:T(8,128)(2,1)S(1)}, bf16[640,256]{1,0:T(8,128)(2,1)S(1)}, u32[]{:S(2)}, u32[]{:S(2)}) collective-permute-start(bf16[640,256]{1,0:T(8,128)(2,1)S(1)} %get-tuple-element.44.refs_1_), channel_id=1, source_target_pairs={{0,8},{8,16},{12,4},{16,24},{20,12},{28,20},{1,9},{9,17},{13,5},{1... | collective-permute-start | bytes 983048 | tf_op jit(solution)/shard_map/ppermute | solution.py:438
  9.1 1.6 %collective-permute-start.4 = (bf16[320,256]{1,0:T(8,128)(2,1)S(1)}, bf16[320,256]{1,0:T(8,128)(2,1)S(1)}, u32[]{:S(2)}, u32[]{:S(2)}) collective-permute-start(bf16[320,256]{1,0:T(8,128)(2,1)S(1)} %get-tuple-element.45), channel_id=1, source_target_pairs={{0,4},{4,0},{8,12},{12,8},{16,20},{20,16},{24,28},{28,24},{1,5},{5... | collective-permute-start | bytes 491528 | tf_op jit(solution)/shard_map/ppermute | solution.py:439
  11.0 2.0 %collective-permute-done.1.refs_1_.refs_3_ = bf16[640,256]{1,0:T(8,128)(2,1)S(1)} collective-permute-done((bf16[640,256]{1,0:T(8,128)(2,1)S(1)}, bf16[640,256]{1,0:T(8,128)(2,1)S(1)}, u32[]{:S(2)}, u32[]{:S(2)}) %collective-permute-start.1) | collective-permute-done | bytes 327712 | tf_op jit(solution)/shard_map/ppermute | solution.py:437
  13.0 1.6 %collective-permute-start.2 = (bf16[1280,256]{1,0:T(8,128)(2,1)S(1)}, bf16[1280,256]{1,0:T(8,128)(2,1)S(1)}, u32[]{:S(2)}, u32[]{:S(2)}) collective-permute-start(bf16[1280,256]{1,0:T(8,128)(2,1)S(1)} %shard_map.94), channel_id=1, source_target_pairs={{0,4},{4,12},{8,0},{12,20},{16,8},{20,28},{24,16},{28,24},{1,5},{5... | collective-permute-start | bytes 1966088 | tf_op jit(solution)/shard_map/ppermute | solution.py:442
  14.7 1.5 %collective-permute-done.3.refs_4_ = bf16[640,256]{1,0:T(8,128)(2,1)S(1)} collective-permute-done((bf16[640,256]{1,0:T(8,128)(2,1)S(1)}, bf16[640,256]{1,0:T(8,128)(2,1)S(1)}, u32[]{:S(2)}, u32[]{:S(2)}) %collective-permute-start.3) | collective-permute-done | bytes 327712 | tf_op jit(solution)/shard_map/ppermute | solution.py:438
  17.4 2.0 %shard_map.95 = (f32[1,4,256,128]{3,2,1,0:T(8,128)S(1)}, f32[1,4,256,128]{3,2,1,0:T(8,128)S(1)}) custom-call(s32[1]{0:T(128)} %bitcast.where_ref, s32[8,128]{1,0:T(8,128)S(1)} %get-tuple-element.37.need_ref, f32[1,2048]{1,0:T(1,128)S(1)} %get-tuple-element.38.seg_ref, bf16[320,256]{1,0:T(8,128)(2,1)S(1)} %get-tuple-element.42.refs_0_, ...), custom_call_target="tpu_custom_call" | custom-call | flops 1000 | bytes 1000 | tf_op jit(solution)/shard_map/pallas_call | solution.py:231
  19.4 4.8 %collective-permute-done.5.refs_2_.refs_5_ = bf16[640,256]{1,0:T(8,128)(2,1)S(1)} collective-permute-done((bf16[640,256]{1,0:T(8,128)(2,1)S(1)}, bf16[640,256]{1,0:T(8,128)(2,1)S(1)}, u32[]{:S(2)}, u32[]{:S(2)}) %collective-permute-start.5) | collective-permute-done | bytes 327712 | tf_op jit(solution)/shard_map/ppermute | solution.py:441
  24.6 2.2 %shard_map.98 = (f32[1,4,256,128]{3,2,1,0:T(8,128)S(1)}, f32[1,4,256,128]{3,2,1,0:T(8,128)S(1)}) custom-call(s32[1]{0:T(128)} %bitcast.where_ref, s32[8,128]{1,0:T(8,128)S(1)} %get-tuple-element.37.need_ref, f32[1,2048]{1,0:T(1,128)S(1)} %get-tuple-element.38.seg_ref, bf16[320,256]{1,0:T(8,128)(2,1)S(1)} %collective-permute-done.4.refs_0_, ...), custom_call_target="tpu_custom_call" | custom-call | flops 1000 | bytes 1000 | tf_op jit(solution)/shard_map/pallas_call | solution.py:231
  26.8 1.6 %collective-permute-done.2.refs_1_ = bf16[1280,256]{1,0:T(8,128)(2,1)S(1)} collective-permute-done((bf16[1280,256]{1,0:T(8,128)(2,1)S(1)}, bf16[1280,256]{1,0:T(8,128)(2,1)S(1)}, u32[]{:S(2)}, u32[]{:S(2)}) %collective-permute-start.2) | collective-permute-done | bytes 655392 | tf_op jit(solution)/shard_map/ppermute | solution.py:442
  28.4 1.2 %shard_map.99 = bf16[320,256]{1,0:T(8,128)(2,1)S(1)} custom-call(s32[1]{0:T(128)} %bitcast.where_ref, s32[8,128]{1,0:T(8,128)S(1)} %get-tuple-element.37.need_ref, f32[1,2048]{1,0:T(1,128)S(1)} %get-tuple-element.38.seg_ref, bf16[320,256]{1,0:T(8,128)(2,1)S(1)} %collective-permute-done.4.refs_0_, bf16[1280,256]{1,0:T(8,128)(2,1)S(1)} %collective-permute-done.2.refs_1_, ...), custom_call_target="tpu_custom_call" | custom-call | flops 1000 | bytes 1000 | tf_op jit(solution)/shard_map/pallas_call | solution.py:231
  31.2 1.7 %shard_map.96.own_ref = bf16[320,256]{1,0:T(8,128)(2,1)S(1)} custom-call(s32[1]{0:T(128)} %bitcast.where_ref, s32[8,128]{1,0:T(8,128)S(1)} %get-tuple-element.37.need_ref, f32[1,2048]{1,0:T(1,128)S(1)} %get-tuple-element.38.seg_ref, bf16[320,256]{1,0:T(8,128)(2,1)S(1)} %get-tuple-element.42.refs_0_, bf16[1280,256]{1,0:T(8,128)(2,1)S(1)} %collective-permute-done.2.refs_1_, ...), custom_call_target="tpu_custom_call" | custom-call | flops 1000 | bytes 1000 | tf_op jit(solution)/shard_map/pallas_call | solution.py:231
  33.7 1.4 %collective-permute-done.7.other_ref = bf16[320,256]{1,0:T(8,128)(2,1)S(1)} collective-permute-done((bf16[320,256]{1,0:T(8,128)(2,1)S(1)}, bf16[320,256]{1,0:T(8,128)(2,1)S(1)}, u32[]{:S(2)}, u32[]{:S(2)}) %collective-permute-start.7) | collective-permute-done | bytes 163872 | tf_op jit(solution)/shard_map/ppermute | solution.py:453
  36.1 1.5 %collective-permute-start.8 = (bf16[16,5248]{1,0:T(8,128)(2,1)S(1)}, bf16[16,5248]{1,0:T(8,128)(2,1)S(1)}, u32[]{:S(2)}, u32[]{:S(2)}) collective-permute-start(bf16[16,5248]{1,0:T(8,128)(2,1)S(1)} %get-tuple-element.59), channel_id=1, source_target_pairs={{0,12},{4,8},{8,4},{12,0},{16,28},{20,24},{24,20},{28,16},{1,13},{... | collective-permute-start | bytes 503816 | tf_op jit(solution)/shard_map/ppermute | solution.py:466
  37.5 2.6 %collective-permute-start.11 = (bf16[16,5248]{1,0:T(8,128)(2,1)S(1)}, bf16[16,5248]{1,0:T(8,128)(2,1)S(1)}, u32[]{:S(2)}, u32[]{:S(2)}) collective-permute-start(bf16[16,5248]{1,0:T(8,128)(2,1)S(1)} %get-tuple-element.65), channel_id=1, source_target_pairs={{0,16},{4,20},{8,24},{12,28},{16,0},{20,4},{24,8},{28,12},{1,17},{... | collective-permute-start | bytes 503816 | tf_op jit(solution)/shard_map/ppermute | solution.py:466
  40.1 3.0 %collective-permute-start.13 = (bf16[16,5248]{1,0:T(8,128)(2,1)S(1)}, bf16[16,5248]{1,0:T(8,128)(2,1)S(1)}, u32[]{:S(2)}, u32[]{:S(2)}) collective-permute-start(bf16[16,5248]{1,0:T(8,128)(2,1)S(1)} %get-tuple-element.67), channel_id=1, source_target_pairs={{0,24},{4,28},{8,16},{12,20},{16,8},{20,12},{24,0},{28,4},{1,25},{... | collective-permute-start | bytes 503816 | tf_op jit(solution)/shard_map/ppermute | solution.py:466
  44.3 1.8 %collective-permute-start.10 = (bf16[16,5248]{1,0:T(8,128)(2,1)S(1)}, bf16[16,5248]{1,0:T(8,128)(2,1)S(1)}, u32[]{:S(2)}, u32[]{:S(2)}) collective-permute-start(bf16[16,5248]{1,0:T(8,128)(2,1)S(1)} %get-tuple-element.63), channel_id=1, source_target_pairs={{0,8},{4,12},{8,0},{12,4},{16,24},{20,28},{24,16},{28,20},{1,9},{5... | collective-permute-start | bytes 503816 | tf_op jit(solution)/shard_map/ppermute | solution.py:466
  46.1 9.6 %collective-permute-done.11.refs_4_ = bf16[16,5248]{1,0:T(8,128)(2,1)S(1)} collective-permute-done((bf16[16,5248]{1,0:T(8,128)(2,1)S(1)}, bf16[16,5248]{1,0:T(8,128)(2,1)S(1)}, u32[]{:S(2)}, u32[]{:S(2)}) %collective-permute-start.11) | collective-permute-done | bytes 167968 | tf_op jit(solution)/shard_map/ppermute | solution.py:466
  55.7 1.0 %collective-permute-start.9 = (bf16[16,5248]{1,0:T(8,128)(2,1)S(1)}, bf16[16,5248]{1,0:T(8,128)(2,1)S(1)}, u32[]{:S(2)}, u32[]{:S(2)}) collective-permute-start(bf16[16,5248]{1,0:T(8,128)(2,1)S(1)} %get-tuple-element.62), channel_id=1, source_target_pairs={{0,4},{4,0},{8,12},{12,8},{16,20},{20,16},{24,28},{28,24},{1,5},{5... | collective-permute-start | bytes 503816 | tf_op jit(solution)/shard_map/ppermute | solution.py:466
  56.7 2.6 %collective-permute-done.12.refs_5_ = bf16[16,5248]{1,0:T(8,128)(2,1)S(1)} collective-permute-done((bf16[16,5248]{1,0:T(8,128)(2,1)S(1)}, bf16[16,5248]{1,0:T(8,128)(2,1)S(1)}, u32[]{:S(2)}, u32[]{:S(2)}) %collective-permute-start.12) | collective-permute-done | bytes 167968 | tf_op jit(solution)/shard_map/ppermute | solution.py:466
  59.3 5.0 %collective-permute-done.13.refs_6_ = bf16[16,5248]{1,0:T(8,128)(2,1)S(1)} collective-permute-done((bf16[16,5248]{1,0:T(8,128)(2,1)S(1)}, bf16[16,5248]{1,0:T(8,128)(2,1)S(1)}, u32[]{:S(2)}, u32[]{:S(2)}) %collective-permute-start.13) | collective-permute-done | bytes 167968 | tf_op jit(solution)/shard_map/ppermute | solution.py:466
  64.3 2.0 %collective-permute-done.14.refs_7_ = bf16[16,5248]{1,0:T(8,128)(2,1)S(1)} collective-permute-done((bf16[16,5248]{1,0:T(8,128)(2,1)S(1)}, bf16[16,5248]{1,0:T(8,128)(2,1)S(1)}, u32[]{:S(2)}, u32[]{:S(2)}) %collective-permute-start.14) | collective-permute-done | bytes 167968 | tf_op jit(solution)/shard_map/ppermute | solution.py:466
  66.3 1.5 %shard_map.101 = bf16[128,5120]{1,0:T(8,128)(2,1)} custom-call(bf16[16,5248]{1,0:T(8,128)(2,1)S(1)} %get-tuple-element.58.refs_0_, bf16[16,5248]{1,0:T(8,128)(2,1)S(1)} %collective-permute-done.9.refs_1_, bf16[16,5248]{1,0:T(8,128)(2,1)S(1)} %collective-permute-done.10.refs_2_, bf16[16,5248]{1,0:T(8,128)(2,1)S(1)} %collective-permute-done.8.refs_3_, ...), custom_call_target="tpu_custom_call" | custom-call | tf_op jit(solution)/shard_map/pallas_call | solution.py:383
  (31 shorter events, 8.2 us)
Async XLA Ops:
  0.0 16.7 %copy-start.3 = (s32[2048]{0:T(1024)S(1)}, s32[2048]{0:T(1024)}, u32[]{:S(2)}) copy-start(s32[2048]{0:T(1024)} %param.9) | copy-start | bytes 24580
  0.0 16.7 %copy-start.4 = (s32[8,8]{1,0:T(8,128)S(1)}, s32[8,8]{1,0:T(8,128)}, u32[]{:S(2)}) copy-start(s32[8,8]{1,0:T(8,128)} %mask_ref.1) | copy-start | bytes 772
  1.4 9.6 %collective-permute-start = (bf16[640,256]{1,0:T(8,128)(2,1)S(1)}, bf16[640,256]{1,0:T(8,128)(2,1)S(1)}, u32[]{:S(2)}, u32[]{:S(2)}) collective-permute-start(bf16[640,256]{1,0:T(8,128)(2,1)S(1)} %get-tuple-element.43), channel_id=1, source_target_pairs={{0,4},{4,0},{8,12},{12,8},{16,20},{20,16},{24,28},{28,24},{1,5},{5... | collective-permute-start | bytes 983048 | tf_op jit(solution)/shard_map/ppermute | solution.py:436
  1.9 11.1 %collective-permute-start.1 = (bf16[640,256]{1,0:T(8,128)(2,1)S(1)}, bf16[640,256]{1,0:T(8,128)(2,1)S(1)}, u32[]{:S(2)}, u32[]{:S(2)}) collective-permute-start(bf16[640,256]{1,0:T(8,128)(2,1)S(1)} %get-tuple-element.44.refs_1_), channel_id=1, source_target_pairs={{4,12},{8,0},{12,20},{16,8},{20,28},{24,16},{5,13},{9,1},{13,21},{... | collective-permute-start | bytes 983048 | tf_op jit(solution)/shard_map/ppermute | solution.py:437
  5.4 10.8 %collective-permute-start.3 = (bf16[640,256]{1,0:T(8,128)(2,1)S(1)}, bf16[640,256]{1,0:T(8,128)(2,1)S(1)}, u32[]{:S(2)}, u32[]{:S(2)}) collective-permute-start(bf16[640,256]{1,0:T(8,128)(2,1)S(1)} %get-tuple-element.44.refs_1_), channel_id=1, source_target_pairs={{0,8},{8,16},{12,4},{16,24},{20,12},{28,20},{1,9},{9,17},{13,5},{1... | collective-permute-start | bytes 983048 | tf_op jit(solution)/shard_map/ppermute | solution.py:438
  7.8 1.0 %copy-start.2 = (bf16[256,640]{1,0:T(8,128)(2,1)S(1)}, bf16[256,640]{1,0:T(8,128)(2,1)}, u32[]{:S(2)}) copy-start(bf16[256,640]{1,0:T(8,128)(2,1)} %refs_0_.2) | copy-start | bytes 983044
  9.1 5.6 %collective-permute-start.4 = (bf16[320,256]{1,0:T(8,128)(2,1)S(1)}, bf16[320,256]{1,0:T(8,128)(2,1)S(1)}, u32[]{:S(2)}, u32[]{:S(2)}) collective-permute-start(bf16[320,256]{1,0:T(8,128)(2,1)S(1)} %get-tuple-element.45), channel_id=1, source_target_pairs={{0,4},{4,0},{8,12},{12,8},{16,20},{20,16},{24,28},{28,24},{1,5},{5... | collective-permute-start | bytes 491528 | tf_op jit(solution)/shard_map/ppermute | solution.py:439
  13.0 15.3 %collective-permute-start.2 = (bf16[1280,256]{1,0:T(8,128)(2,1)S(1)}, bf16[1280,256]{1,0:T(8,128)(2,1)S(1)}, u32[]{:S(2)}, u32[]{:S(2)}) collective-permute-start(bf16[1280,256]{1,0:T(8,128)(2,1)S(1)} %shard_map.94), channel_id=1, source_target_pairs={{0,4},{4,12},{8,0},{12,20},{16,8},{20,28},{24,16},{28,24},{1,5},{5... | collective-permute-start | bytes 1966088 | tf_op jit(solution)/shard_map/ppermute | solution.py:442
  16.2 8.0 %collective-permute-start.5 = (bf16[640,256]{1,0:T(8,128)(2,1)S(1)}, bf16[640,256]{1,0:T(8,128)(2,1)S(1)}, u32[]{:S(2)}, u32[]{:S(2)}) collective-permute-start(bf16[640,256]{1,0:T(8,128)(2,1)S(1)} %collective-permute-done.refs_0_.refs_2_), channel_id=1, source_target_pairs={{0,8},{4,0},{8,16},{12,4},{16,24},{20,12},{24,28},{28,20},{1,9},{5... | collective-permute-start | bytes 983048 | tf_op jit(solution)/shard_map/ppermute | solution.py:441
  24.2 7.1 %collective-permute-start.6 = (bf16[640,256]{1,0:T(8,128)(2,1)S(1)}, bf16[640,256]{1,0:T(8,128)(2,1)S(1)}, u32[]{:S(2)}, u32[]{:S(2)}) collective-permute-start(bf16[640,256]{1,0:T(8,128)(2,1)S(1)} %collective-permute-done.5.refs_2_.refs_5_), channel_id=1, source_target_pairs={{0,8},{4,0},{8,16},{12,4},{16,24},{20,12},{24,28},{28,20},{1,9},{5... | collective-permute-start | bytes 983048 | tf_op jit(solution)/shard_map/ppermute | solution.py:448
  29.6 3.4 %copy-start = (bf16[640,1280]{1,0:T(8,128)(2,1)S(1)}, bf16[640,1280]{1,0:T(8,128)(2,1)}, u32[]{:S(2)}) copy-start(bf16[640,1280]{1,0:T(8,128)(2,1)} %weight_ref.3) | copy-start | bytes 4915204
  29.6 3.4 %copy-start.1 = (bf16[256,1280]{1,0:T(8,128)(2,1)S(1)}, bf16[256,1280]{1,0:T(8,128)(2,1)}, u32[]{:S(2)}) copy-start(bf16[256,1280]{1,0:T(8,128)(2,1)} %tokens_ref.1) | copy-start | bytes 1966084
  29.6 3.4 %copy-start.5 = (s32[64]{0:T(128)S(1)}, s32[64]{0:T(128)}, u32[]{:S(2)}) copy-start(s32[64]{0:T(128)} %param.16) | copy-start | bytes 772
  29.7 3.4 %copy-start.6 = (s32[64]{0:T(128)S(1)}, s32[64]{0:T(128)}, u32[]{:S(2)}) copy-start(s32[64]{0:T(128)} %param.17) | copy-start | bytes 772
  29.7 5.4 %collective-permute-start.7 = (bf16[320,256]{1,0:T(8,128)(2,1)S(1)}, bf16[320,256]{1,0:T(8,128)(2,1)S(1)}, u32[]{:S(2)}, u32[]{:S(2)}) collective-permute-start(bf16[320,256]{1,0:T(8,128)(2,1)S(1)} %shard_map.99), channel_id=1, source_target_pairs={{0,4},{4,0},{8,12},{12,8},{16,20},{20,16},{24,28},{28,24},{1,5},{5... | collective-permute-start | bytes 491528 | tf_op jit(solution)/shard_map/ppermute | solution.py:453
  36.1 8.2 %collective-permute-start.8 = (bf16[16,5248]{1,0:T(8,128)(2,1)S(1)}, bf16[16,5248]{1,0:T(8,128)(2,1)S(1)}, u32[]{:S(2)}, u32[]{:S(2)}) collective-permute-start(bf16[16,5248]{1,0:T(8,128)(2,1)S(1)} %get-tuple-element.59), channel_id=1, source_target_pairs={{0,12},{4,8},{8,4},{12,0},{16,28},{20,24},{24,20},{28,16},{1,13},{... | collective-permute-start | bytes 503816 | tf_op jit(solution)/shard_map/ppermute | solution.py:466
  37.5 18.2 %collective-permute-start.11 = (bf16[16,5248]{1,0:T(8,128)(2,1)S(1)}, bf16[16,5248]{1,0:T(8,128)(2,1)S(1)}, u32[]{:S(2)}, u32[]{:S(2)}) collective-permute-start(bf16[16,5248]{1,0:T(8,128)(2,1)S(1)} %get-tuple-element.65), channel_id=1, source_target_pairs={{0,16},{4,20},{8,24},{12,28},{16,0},{20,4},{24,8},{28,12},{1,17},{... | collective-permute-start | bytes 503816 | tf_op jit(solution)/shard_map/ppermute | solution.py:466
  40.1 19.2 %collective-permute-start.12 = (bf16[16,5248]{1,0:T(8,128)(2,1)S(1)}, bf16[16,5248]{1,0:T(8,128)(2,1)S(1)}, u32[]{:S(2)}, u32[]{:S(2)}) collective-permute-start(bf16[16,5248]{1,0:T(8,128)(2,1)S(1)} %get-tuple-element.66), channel_id=1, source_target_pairs={{0,20},{4,16},{8,28},{12,24},{16,4},{20,0},{24,12},{28,8},{1,21},{... | collective-permute-start | bytes 503816 | tf_op jit(solution)/shard_map/ppermute | solution.py:466
  40.1 24.2 %collective-permute-start.13 = (bf16[16,5248]{1,0:T(8,128)(2,1)S(1)}, bf16[16,5248]{1,0:T(8,128)(2,1)S(1)}, u32[]{:S(2)}, u32[]{:S(2)}) collective-permute-start(bf16[16,5248]{1,0:T(8,128)(2,1)S(1)} %get-tuple-element.67), channel_id=1, source_target_pairs={{0,24},{4,28},{8,16},{12,20},{16,8},{20,12},{24,0},{28,4},{1,25},{... | collective-permute-start | bytes 503816 | tf_op jit(solution)/shard_map/ppermute | solution.py:466
  43.1 23.2 %collective-permute-start.14 = (bf16[16,5248]{1,0:T(8,128)(2,1)S(1)}, bf16[16,5248]{1,0:T(8,128)(2,1)S(1)}, u32[]{:S(2)}, u32[]{:S(2)}) collective-permute-start(bf16[16,5248]{1,0:T(8,128)(2,1)S(1)} %get-tuple-element.68), channel_id=1, source_target_pairs={{0,28},{4,24},{8,20},{12,16},{16,12},{20,8},{24,4},{28,0},{1,29},{... | collective-permute-start | bytes 503816 | tf_op jit(solution)/shard_map/ppermute | solution.py:466
  44.3 22.0 %collective-permute-start.10 = (bf16[16,5248]{1,0:T(8,128)(2,1)S(1)}, bf16[16,5248]{1,0:T(8,128)(2,1)S(1)}, u32[]{:S(2)}, u32[]{:S(2)}) collective-permute-start(bf16[16,5248]{1,0:T(8,128)(2,1)S(1)} %get-tuple-element.63), channel_id=1, source_target_pairs={{0,8},{4,12},{8,0},{12,4},{16,24},{20,28},{24,16},{28,20},{1,9},{5... | collective-permute-start | bytes 503816 | tf_op jit(solution)/shard_map/ppermute | solution.py:466
  55.7 10.6 %collective-permute-start.9 = (bf16[16,5248]{1,0:T(8,128)(2,1)S(1)}, bf16[16,5248]{1,0:T(8,128)(2,1)S(1)}, u32[]{:S(2)}, u32[]{:S(2)}) collective-permute-start(bf16[16,5248]{1,0:T(8,128)(2,1)S(1)} %get-tuple-element.62), channel_id=1, source_target_pairs={{0,4},{4,0},{8,12},{12,8},{16,20},{20,16},{24,28},{28,24},{1,5},{5... | collective-permute-start | bytes 503816 | tf_op jit(solution)/shard_map/ppermute | solution.py:466

commit v27 on v26

--- a/solution.py
+++ b/solution.py
@@ -410,9 +410,6 @@
     swap = functools.partial(
         lax.ppermute, axis_name="blk", perm=route(lambda i: 1 - 2 * (i % 2))
     )
-    ahead = functools.partial(
-        lax.ppermute, axis_name="blk", perm=route(lambda i: 2 if i % 2 else -2)
-    )
     back = functools.partial(
         lax.ppermute, axis_name="blk", perm=route(lambda i: -2 if i % 2 else 2)
     )
@@ -422,7 +419,7 @@
         axis_name="blk",
         perm=route(lambda i: -1 if i == 1 else 1 if i == nblocks - 2 else -2 if i % 2 else 2),
     )
-    ahead_all = functools.partial(
+    ahead = functools.partial(
         lax.ppermute,
         axis_name="blk",
         perm=route(lambda i: 1 if i == 0 else -1 if i == nblocks - 1 else 2 if i % 2 else -2),
@@ -439,7 +436,7 @@
     other_q = swap(swap_q)
     ready, back_own, other_q = lax.optimization_barrier((other_kv, back_own, other_q))
     back_other = relay(ready)
-    ahead_both = ahead_all(stack(other_kv, ahead_own))
+    ahead_both = ahead(stack(other_kv, ahead_own))
     near = (own_kv, other_kv, ahead_own, back_own)
     near_numbers = (0, 1, 2, 3)
     fixed = (where, need, segs)

time: 69 us -> 75.4 us (1.093)
  starting transfers between devices: 21.6 us -> 31.4 us
  waiting for transfers between devices: 32.4 us -> 28.6 us
    ppermute x1, starting transfers between devices: 0.47 us -> 8.62 us  [per_device(): back_other = relay(ready)]
    ppermute x1, waiting for transfers between devices: 0.34 us -> 3.31 us  [per_device(): other_kv = swap(swap_kv)]
    ppermute x1, waiting for transfers between devices: 4.77 us -> 2.67 us  [per_device(): back_other = relay(ready)]
    ppermute x1, starting transfers between devices: 0.47 us -> 2.48 us  [per_device(): back_far = relay(back_other)]
    ppermute x1, waiting for transfers between devices: 2.01 us -> 0.01 us  [per_device(): ahead_own = ahead(own_kv)]
    ppermute x1, starting transfers between devices: 3.47 us -> 1.58 us  [per_device(): ahead_own = ahead(own_kv)]
    ppermute x1, waiting for transfers between devices: 1.56 us -> 0.01 us  [per_device(): ahead_both = ahead(stack(other_kv, ahead_own))]
    ppermute x1, waiting for transfers between devices: 1.53 us -> 0.01 us  [per_device(): back_own = back(own_kv)]
  transfers between devices with their start and end apart: 15 -> 15, of which waited for: 12 -> 9; matrix products, arithmetic and copies ran while one was open for 0% -> 0% of each run, Pallas kernels for 13% -> 12%
where the time goes in v27:
time: 75.4 us; the launch traced here: 74 us
  starting transfers between devices  31.4 us (42%)
  waiting for transfers between devices  28.6 us (38%)
  Pallas kernels  12.6 us (17%)
  local copies, waits for them, and re-layouts  1 us (1%)
    ppermute x7, waiting for transfers between devices, cross(): lax.ppermute(arrived[d], 'blk', [(i, i ^ d) for i in range(nblocks)])  20 us
    ppermute x7, starting transfers between devices, cross(): lax.ppermute(arrived[d], 'blk', [(i, i ^ d) for i in range(nblocks)])  11.6 us
    ppermute x1, starting transfers between devices, per_device(): back_other = relay(ready)  8.62 us
    pallas_call x4, Pallas kernels, attention(): pl.pallas_call(functools.partial(attention_kernel, kinds, numbers, rows_o...  7.13 us
    ppermute x1, waiting for transfers between devices, per_device(): other_kv = swap(swap_kv)  3.31 us
    ppermute x1, waiting for transfers between devices, per_device(): back_other = relay(ready)  2.67 us
    ppermute x1, starting transfers between devices, per_device(): back_far = relay(back_other)  2.48 us
    ppermute x1, starting transfers between devices, per_device(): back_own = back(own_kv)  2.35 us
  transfers between devices with their start and end apart: 15, of which 9 were waited for; matrix products, arithmetic and copies ran while one was open for 0% of the time, Pallas kernels for 12%

profile of v27, /device:TPU:14, one launch (start us, length us, event | category | flops | bytes accessed | tf_op | source)
XLA Modules:
  0.0 74.0 jit_solution(16782755528202457273)
XLA Ops:
  0.0 1.4 %shard_map.92 = (bf16[640,256]{1,0:T(8,128)(2,1)S(1)}, bf16[640,256]{1,0:T(8,128)(2,1)S(1)}) custom-call(s32[1]{0:T(128)} %bitcast.where_ref, bf16[256,640]{1,0:T(8,128)(2,1)} %refs_0_.1, bf16[256,640]{1,0:T(8,128)(2,1)} %refs_1_.1), custom_call_target="tpu_custom_call" | custom-call | tf_op jit(solution)/shard_map/pallas_call | solution.py:68
  1.9 1.6 %collective-permute-start.1 = (bf16[640,256]{1,0:T(8,128)(2,1)S(1)}, bf16[640,256]{1,0:T(8,128)(2,1)S(1)}, u32[]{:S(2)}, u32[]{:S(2)}) collective-permute-start(bf16[640,256]{1,0:T(8,128)(2,1)S(1)} %get-tuple-element.44.refs_1_), channel_id=1, source_target_pairs={{0,4},{4,12},{8,0},{12,20},{16,8},{20,28},{24,16},{28,24},{1,5},{5... | collective-permute-start | bytes 983048 | tf_op jit(solution)/shard_map/ppermute | solution.py:434
  3.5 2.3 %collective-permute-start.3 = (bf16[640,256]{1,0:T(8,128)(2,1)S(1)}, bf16[640,256]{1,0:T(8,128)(2,1)S(1)}, u32[]{:S(2)}, u32[]{:S(2)}) collective-permute-start(bf16[640,256]{1,0:T(8,128)(2,1)S(1)} %get-tuple-element.44.refs_1_), channel_id=1, source_target_pairs={{0,8},{8,16},{12,4},{16,24},{20,12},{28,20},{1,9},{9,17},{13,5},{1... | collective-permute-start | bytes 983048 | tf_op jit(solution)/shard_map/ppermute | solution.py:435
  7.1 1.6 %collective-permute-start.4 = (bf16[320,256]{1,0:T(8,128)(2,1)S(1)}, bf16[320,256]{1,0:T(8,128)(2,1)S(1)}, u32[]{:S(2)}, u32[]{:S(2)}) collective-permute-start(bf16[320,256]{1,0:T(8,128)(2,1)S(1)} %get-tuple-element.45), channel_id=1, source_target_pairs={{0,4},{4,0},{8,12},{12,8},{16,20},{20,16},{24,28},{28,24},{1,5},{5... | collective-permute-start | bytes 491528 | tf_op jit(solution)/shard_map/ppermute | solution.py:436
  8.7 3.3 %collective-permute-done.refs_0_.refs_2_ = bf16[640,256]{1,0:T(8,128)(2,1)S(1)} collective-permute-done((bf16[640,256]{1,0:T(8,128)(2,1)S(1)}, bf16[640,256]{1,0:T(8,128)(2,1)S(1)}, u32[]{:S(2)}, u32[]{:S(2)}) %collective-permute-start) | collective-permute-done | bytes 327712 | tf_op jit(solution)/shard_map/ppermute | solution.py:433
  12.1 1.6 %collective-permute-start.2 = (bf16[1280,256]{1,0:T(8,128)(2,1)S(1)}, bf16[1280,256]{1,0:T(8,128)(2,1)S(1)}, u32[]{:S(2)}, u32[]{:S(2)}) collective-permute-start(bf16[1280,256]{1,0:T(8,128)(2,1)S(1)} %shard_map.94), channel_id=1, source_target_pairs={{0,4},{4,12},{8,0},{12,20},{16,8},{20,28},{24,16},{28,24},{1,5},{5... | collective-permute-start | bytes 1966088 | tf_op jit(solution)/shard_map/ppermute | solution.py:439
  14.4 8.6 %collective-permute-start.5 = (bf16[640,256]{1,0:T(8,128)(2,1)S(1)}, bf16[640,256]{1,0:T(8,128)(2,1)S(1)}, u32[]{:S(2)}, u32[]{:S(2)}) collective-permute-start(bf16[640,256]{1,0:T(8,128)(2,1)S(1)} %collective-permute-done.refs_0_.refs_2_), channel_id=1, source_target_pairs={{0,8},{4,0},{8,16},{12,4},{16,24},{20,12},{24,28},{28,20},{1,9},{5... | collective-permute-start | bytes 983048 | tf_op jit(solution)/shard_map/ppermute | solution.py:438
  23.8 2.0 %shard_map.95 = (f32[1,4,256,128]{3,2,1,0:T(8,128)S(1)}, f32[1,4,256,128]{3,2,1,0:T(8,128)S(1)}) custom-call(s32[1]{0:T(128)} %bitcast.where_ref, s32[8,128]{1,0:T(8,128)S(1)} %get-tuple-element.37.need_ref, f32[1,2048]{1,0:T(1,128)S(1)} %get-tuple-element.38.seg_ref, bf16[320,256]{1,0:T(8,128)(2,1)S(1)} %get-tuple-element.42.refs_0_, ...), custom_call_target="tpu_custom_call" | custom-call | flops 1000 | bytes 1000 | tf_op jit(solution)/shard_map/pallas_call | solution.py:231
  25.7 2.7 %collective-permute-done.5.refs_2_.refs_5_ = bf16[640,256]{1,0:T(8,128)(2,1)S(1)} collective-permute-done((bf16[640,256]{1,0:T(8,128)(2,1)S(1)}, bf16[640,256]{1,0:T(8,128)(2,1)S(1)}, u32[]{:S(2)}, u32[]{:S(2)}) %collective-permute-start.5) | collective-permute-done | bytes 327712 | tf_op jit(solution)/shard_map/ppermute | solution.py:438
  28.4 2.5 %collective-permute-start.6 = (bf16[640,256]{1,0:T(8,128)(2,1)S(1)}, bf16[640,256]{1,0:T(8,128)(2,1)S(1)}, u32[]{:S(2)}, u32[]{:S(2)}) collective-permute-start(bf16[640,256]{1,0:T(8,128)(2,1)S(1)} %collective-permute-done.5.refs_2_.refs_5_), channel_id=1, source_target_pairs={{0,8},{4,0},{8,16},{12,4},{16,24},{20,12},{24,28},{28,20},{1,9},{5... | collective-permute-start | bytes 983048 | tf_op jit(solution)/shard_map/ppermute | solution.py:445
  30.9 2.2 %shard_map.98 = (f32[1,4,256,128]{3,2,1,0:T(8,128)S(1)}, f32[1,4,256,128]{3,2,1,0:T(8,128)S(1)}) custom-call(s32[1]{0:T(128)} %bitcast.where_ref, s32[8,128]{1,0:T(8,128)S(1)} %get-tuple-element.37.need_ref, f32[1,2048]{1,0:T(1,128)S(1)} %get-tuple-element.38.seg_ref, bf16[320,256]{1,0:T(8,128)(2,1)S(1)} %collective-permute-done.4.refs_0_, ...), custom_call_target="tpu_custom_call" | custom-call | flops 1000 | bytes 1000 | tf_op jit(solution)/shard_map/pallas_call | solution.py:231
  33.1 1.2 %shard_map.99 = bf16[320,256]{1,0:T(8,128)(2,1)S(1)} custom-call(s32[1]{0:T(128)} %bitcast.where_ref, s32[8,128]{1,0:T(8,128)S(1)} %get-tuple-element.37.need_ref, f32[1,2048]{1,0:T(1,128)S(1)} %get-tuple-element.38.seg_ref, bf16[320,256]{1,0:T(8,128)(2,1)S(1)} %collective-permute-done.4.refs_0_, bf16[1280,256]{1,0:T(8,128)(2,1)S(1)} %collective-permute-done.2.refs_1_, ...), custom_call_target="tpu_custom_call" | custom-call | flops 1000 | bytes 1000 | tf_op jit(solution)/shard_map/pallas_call | solution.py:231
  35.5 1.7 %shard_map.96.own_ref = bf16[320,256]{1,0:T(8,128)(2,1)S(1)} custom-call(s32[1]{0:T(128)} %bitcast.where_ref, s32[8,128]{1,0:T(8,128)S(1)} %get-tuple-element.37.need_ref, f32[1,2048]{1,0:T(1,128)S(1)} %get-tuple-element.38.seg_ref, bf16[320,256]{1,0:T(8,128)(2,1)S(1)} %get-tuple-element.42.refs_0_, bf16[1280,256]{1,0:T(8,128)(2,1)S(1)} %collective-permute-done.2.refs_1_, ...), custom_call_target="tpu_custom_call" | custom-call | flops 1000 | bytes 1000 | tf_op jit(solution)/shard_map/pallas_call | solution.py:231
  37.9 1.9 %collective-permute-done.7.other_ref = bf16[320,256]{1,0:T(8,128)(2,1)S(1)} collective-permute-done((bf16[320,256]{1,0:T(8,128)(2,1)S(1)}, bf16[320,256]{1,0:T(8,128)(2,1)S(1)}, u32[]{:S(2)}, u32[]{:S(2)}) %collective-permute-start.7) | collective-permute-done | bytes 163872 | tf_op jit(solution)/shard_map/ppermute | solution.py:450
  40.8 1.9 %collective-permute-start.8 = (bf16[16,5248]{1,0:T(8,128)(2,1)S(1)}, bf16[16,5248]{1,0:T(8,128)(2,1)S(1)}, u32[]{:S(2)}, u32[]{:S(2)}) collective-permute-start(bf16[16,5248]{1,0:T(8,128)(2,1)S(1)} %get-tuple-element.59), channel_id=1, source_target_pairs={{0,12},{4,8},{8,4},{12,0},{16,28},{20,24},{24,20},{28,16},{1,13},{... | collective-permute-start | bytes 503816 | tf_op jit(solution)/shard_map/ppermute | solution.py:463
  42.6 1.6 %collective-permute-start.11 = (bf16[16,5248]{1,0:T(8,128)(2,1)S(1)}, bf16[16,5248]{1,0:T(8,128)(2,1)S(1)}, u32[]{:S(2)}, u32[]{:S(2)}) collective-permute-start(bf16[16,5248]{1,0:T(8,128)(2,1)S(1)} %get-tuple-element.65), channel_id=1, source_target_pairs={{0,16},{4,20},{8,24},{12,28},{16,0},{20,4},{24,8},{28,12},{1,17},{... | collective-permute-start | bytes 503816 | tf_op jit(solution)/shard_map/ppermute | solution.py:463
  44.2 2.5 %collective-permute-start.12 = (bf16[16,5248]{1,0:T(8,128)(2,1)S(1)}, bf16[16,5248]{1,0:T(8,128)(2,1)S(1)}, u32[]{:S(2)}, u32[]{:S(2)}) collective-permute-start(bf16[16,5248]{1,0:T(8,128)(2,1)S(1)} %get-tuple-element.66), channel_id=1, source_target_pairs={{0,20},{4,16},{8,28},{12,24},{16,4},{20,0},{24,12},{28,8},{1,21},{... | collective-permute-start | bytes 503816 | tf_op jit(solution)/shard_map/ppermute | solution.py:463
  46.8 1.4 %collective-permute-start.13 = (bf16[16,5248]{1,0:T(8,128)(2,1)S(1)}, bf16[16,5248]{1,0:T(8,128)(2,1)S(1)}, u32[]{:S(2)}, u32[]{:S(2)}) collective-permute-start(bf16[16,5248]{1,0:T(8,128)(2,1)S(1)} %get-tuple-element.67), channel_id=1, source_target_pairs={{0,24},{4,28},{8,16},{12,20},{16,8},{20,12},{24,0},{28,4},{1,25},{... | collective-permute-start | bytes 503816 | tf_op jit(solution)/shard_map/ppermute | solution.py:463
  49.4 2.4 %collective-permute-start.10 = (bf16[16,5248]{1,0:T(8,128)(2,1)S(1)}, bf16[16,5248]{1,0:T(8,128)(2,1)S(1)}, u32[]{:S(2)}, u32[]{:S(2)}) collective-permute-start(bf16[16,5248]{1,0:T(8,128)(2,1)S(1)} %get-tuple-element.63), channel_id=1, source_target_pairs={{0,8},{4,12},{8,0},{12,4},{16,24},{20,28},{24,16},{28,20},{1,9},{5... | collective-permute-start | bytes 503816 | tf_op jit(solution)/shard_map/ppermute | solution.py:463
  51.8 10.9 %collective-permute-done.11.refs_4_ = bf16[16,5248]{1,0:T(8,128)(2,1)S(1)} collective-permute-done((bf16[16,5248]{1,0:T(8,128)(2,1)S(1)}, bf16[16,5248]{1,0:T(8,128)(2,1)S(1)}, u32[]{:S(2)}, u32[]{:S(2)}) %collective-permute-start.11) | collective-permute-done | bytes 167968 | tf_op jit(solution)/shard_map/ppermute | solution.py:463
  63.3 3.0 %collective-permute-done.12.refs_5_ = bf16[16,5248]{1,0:T(8,128)(2,1)S(1)} collective-permute-done((bf16[16,5248]{1,0:T(8,128)(2,1)S(1)}, bf16[16,5248]{1,0:T(8,128)(2,1)S(1)}, u32[]{:S(2)}, u32[]{:S(2)}) %collective-permute-start.12) | collective-permute-done | bytes 167968 | tf_op jit(solution)/shard_map/ppermute | solution.py:463
  66.3 3.8 %collective-permute-done.13.refs_6_ = bf16[16,5248]{1,0:T(8,128)(2,1)S(1)} collective-permute-done((bf16[16,5248]{1,0:T(8,128)(2,1)S(1)}, bf16[16,5248]{1,0:T(8,128)(2,1)S(1)}, u32[]{:S(2)}, u32[]{:S(2)}) %collective-permute-start.13) | collective-permute-done | bytes 167968 | tf_op jit(solution)/shard_map/ppermute | solution.py:463
  70.1 2.3 %collective-permute-done.14.refs_7_ = bf16[16,5248]{1,0:T(8,128)(2,1)S(1)} collective-permute-done((bf16[16,5248]{1,0:T(8,128)(2,1)S(1)}, bf16[16,5248]{1,0:T(8,128)(2,1)S(1)}, u32[]{:S(2)}, u32[]{:S(2)}) %collective-permute-start.14) | collective-permute-done | bytes 167968 | tf_op jit(solution)/shard_map/ppermute | solution.py:463
  72.4 1.5 %shard_map.101 = bf16[128,5120]{1,0:T(8,128)(2,1)} custom-call(bf16[16,5248]{1,0:T(8,128)(2,1)S(1)} %get-tuple-element.58.refs_0_, bf16[16,5248]{1,0:T(8,128)(2,1)S(1)} %collective-permute-done.9.refs_1_, bf16[16,5248]{1,0:T(8,128)(2,1)S(1)} %collective-permute-done.10.refs_2_, bf16[16,5248]{1,0:T(8,128)(2,1)S(1)} %collective-permute-done.8.refs_3_, ...), custom_call_target="tpu_custom_call" | custom-call | tf_op jit(solution)/shard_map/pallas_call | solution.py:383
  (31 shorter events, 7.8 us)
Async XLA Ops:
  0.0 23.0 %copy-start.3 = (s32[2048]{0:T(1024)S(1)}, s32[2048]{0:T(1024)}, u32[]{:S(2)}) copy-start(s32[2048]{0:T(1024)} %param.9) | copy-start | bytes 24580
  0.0 23.0 %copy-start.4 = (s32[8,8]{1,0:T(8,128)S(1)}, s32[8,8]{1,0:T(8,128)}, u32[]{:S(2)}) copy-start(s32[8,8]{1,0:T(8,128)} %mask_ref.1) | copy-start | bytes 772
  1.4 10.7 %collective-permute-start = (bf16[640,256]{1,0:T(8,128)(2,1)S(1)}, bf16[640,256]{1,0:T(8,128)(2,1)S(1)}, u32[]{:S(2)}, u32[]{:S(2)}) collective-permute-start(bf16[640,256]{1,0:T(8,128)(2,1)S(1)} %get-tuple-element.43), channel_id=1, source_target_pairs={{0,4},{4,0},{8,12},{12,8},{16,20},{20,16},{24,28},{28,24},{1,5},{5... | collective-permute-start | bytes 983048 | tf_op jit(solution)/shard_map/ppermute | solution.py:433
  1.9 10.1 %collective-permute-start.1 = (bf16[640,256]{1,0:T(8,128)(2,1)S(1)}, bf16[640,256]{1,0:T(8,128)(2,1)S(1)}, u32[]{:S(2)}, u32[]{:S(2)}) collective-permute-start(bf16[640,256]{1,0:T(8,128)(2,1)S(1)} %get-tuple-element.44.refs_1_), channel_id=1, source_target_pairs={{0,4},{4,12},{8,0},{12,20},{16,8},{20,28},{24,16},{28,24},{1,5},{5... | collective-permute-start | bytes 983048 | tf_op jit(solution)/shard_map/ppermute | solution.py:434
  3.5 10.9 %collective-permute-start.3 = (bf16[640,256]{1,0:T(8,128)(2,1)S(1)}, bf16[640,256]{1,0:T(8,128)(2,1)S(1)}, u32[]{:S(2)}, u32[]{:S(2)}) collective-permute-start(bf16[640,256]{1,0:T(8,128)(2,1)S(1)} %get-tuple-element.44.refs_1_), channel_id=1, source_target_pairs={{0,8},{8,16},{12,4},{16,24},{20,12},{28,20},{1,9},{9,17},{13,5},{1... | collective-permute-start | bytes 983048 | tf_op jit(solution)/shard_map/ppermute | solution.py:435
  5.9 1.0 %copy-start.2 = (bf16[256,640]{1,0:T(8,128)(2,1)S(1)}, bf16[256,640]{1,0:T(8,128)(2,1)}, u32[]{:S(2)}) copy-start(bf16[256,640]{1,0:T(8,128)(2,1)} %refs_0_.2) | copy-start | bytes 983044
  7.1 7.3 %collective-permute-start.4 = (bf16[320,256]{1,0:T(8,128)(2,1)S(1)}, bf16[320,256]{1,0:T(8,128)(2,1)S(1)}, u32[]{:S(2)}, u32[]{:S(2)}) collective-permute-start(bf16[320,256]{1,0:T(8,128)(2,1)S(1)} %get-tuple-element.45), channel_id=1, source_target_pairs={{0,4},{4,0},{8,12},{12,8},{16,20},{20,16},{24,28},{28,24},{1,5},{5... | collective-permute-start | bytes 491528 | tf_op jit(solution)/shard_map/ppermute | solution.py:436
  12.1 21.0 %collective-permute-start.2 = (bf16[1280,256]{1,0:T(8,128)(2,1)S(1)}, bf16[1280,256]{1,0:T(8,128)(2,1)S(1)}, u32[]{:S(2)}, u32[]{:S(2)}) collective-permute-start(bf16[1280,256]{1,0:T(8,128)(2,1)S(1)} %shard_map.94), channel_id=1, source_target_pairs={{0,4},{4,12},{8,0},{12,20},{16,8},{20,28},{24,16},{28,24},{1,5},{5... | collective-permute-start | bytes 1966088 | tf_op jit(solution)/shard_map/ppermute | solution.py:439
  14.4 14.0 %collective-permute-start.5 = (bf16[640,256]{1,0:T(8,128)(2,1)S(1)}, bf16[640,256]{1,0:T(8,128)(2,1)S(1)}, u32[]{:S(2)}, u32[]{:S(2)}) collective-permute-start(bf16[640,256]{1,0:T(8,128)(2,1)S(1)} %collective-permute-done.refs_0_.refs_2_), channel_id=1, source_target_pairs={{0,8},{4,0},{8,16},{12,4},{16,24},{20,12},{24,28},{28,20},{1,9},{5... | collective-permute-start | bytes 983048 | tf_op jit(solution)/shard_map/ppermute | solution.py:438
  28.4 7.1 %collective-permute-start.6 = (bf16[640,256]{1,0:T(8,128)(2,1)S(1)}, bf16[640,256]{1,0:T(8,128)(2,1)S(1)}, u32[]{:S(2)}, u32[]{:S(2)}) collective-permute-start(bf16[640,256]{1,0:T(8,128)(2,1)S(1)} %collective-permute-done.5.refs_2_.refs_5_), channel_id=1, source_target_pairs={{0,8},{4,0},{8,16},{12,4},{16,24},{20,12},{24,28},{28,20},{1,9},{5... | collective-permute-start | bytes 983048 | tf_op jit(solution)/shard_map/ppermute | solution.py:445
  34.3 2.9 %copy-start = (bf16[640,1280]{1,0:T(8,128)(2,1)S(1)}, bf16[640,1280]{1,0:T(8,128)(2,1)}, u32[]{:S(2)}) copy-start(bf16[640,1280]{1,0:T(8,128)(2,1)} %weight_ref.3) | copy-start | bytes 4915204
  34.3 2.9 %copy-start.1 = (bf16[256,1280]{1,0:T(8,128)(2,1)S(1)}, bf16[256,1280]{1,0:T(8,128)(2,1)}, u32[]{:S(2)}) copy-start(bf16[256,1280]{1,0:T(8,128)(2,1)} %tokens_ref.1) | copy-start | bytes 1966084
  34.4 2.9 %copy-start.5 = (s32[64]{0:T(128)S(1)}, s32[64]{0:T(128)}, u32[]{:S(2)}) copy-start(s32[64]{0:T(128)} %param.16) | copy-start | bytes 772
  34.4 2.9 %copy-start.6 = (s32[64]{0:T(128)S(1)}, s32[64]{0:T(128)}, u32[]{:S(2)}) copy-start(s32[64]{0:T(128)} %param.17) | copy-start | bytes 772
  34.4 5.4 %collective-permute-start.7 = (bf16[320,256]{1,0:T(8,128)(2,1)S(1)}, bf16[320,256]{1,0:T(8,128)(2,1)S(1)}, u32[]{:S(2)}, u32[]{:S(2)}) collective-permute-start(bf16[320,256]{1,0:T(8,128)(2,1)S(1)} %shard_map.99), channel_id=1, source_target_pairs={{0,4},{4,0},{8,12},{12,8},{16,20},{20,16},{24,28},{28,24},{1,5},{5... | collective-permute-start | bytes 491528 | tf_op jit(solution)/shard_map/ppermute | solution.py:450
  40.8 8.7 %collective-permute-start.8 = (bf16[16,5248]{1,0:T(8,128)(2,1)S(1)}, bf16[16,5248]{1,0:T(8,128)(2,1)S(1)}, u32[]{:S(2)}, u32[]{:S(2)}) collective-permute-start(bf16[16,5248]{1,0:T(8,128)(2,1)S(1)} %get-tuple-element.59), channel_id=1, source_target_pairs={{0,12},{4,8},{8,4},{12,0},{16,28},{20,24},{24,20},{28,16},{1,13},{... | collective-permute-start | bytes 503816 | tf_op jit(solution)/shard_map/ppermute | solution.py:463
  42.6 20.1 %collective-permute-start.11 = (bf16[16,5248]{1,0:T(8,128)(2,1)S(1)}, bf16[16,5248]{1,0:T(8,128)(2,1)S(1)}, u32[]{:S(2)}, u32[]{:S(2)}) collective-permute-start(bf16[16,5248]{1,0:T(8,128)(2,1)S(1)} %get-tuple-element.65), channel_id=1, source_target_pairs={{0,16},{4,20},{8,24},{12,28},{16,0},{20,4},{24,8},{28,12},{1,17},{... | collective-permute-start | bytes 503816 | tf_op jit(solution)/shard_map/ppermute | solution.py:463
  44.2 22.1 %collective-permute-start.12 = (bf16[16,5248]{1,0:T(8,128)(2,1)S(1)}, bf16[16,5248]{1,0:T(8,128)(2,1)S(1)}, u32[]{:S(2)}, u32[]{:S(2)}) collective-permute-start(bf16[16,5248]{1,0:T(8,128)(2,1)S(1)} %get-tuple-element.66), channel_id=1, source_target_pairs={{0,20},{4,16},{8,28},{12,24},{16,4},{20,0},{24,12},{28,8},{1,21},{... | collective-permute-start | bytes 503816 | tf_op jit(solution)/shard_map/ppermute | solution.py:463
  46.8 23.3 %collective-permute-start.13 = (bf16[16,5248]{1,0:T(8,128)(2,1)S(1)}, bf16[16,5248]{1,0:T(8,128)(2,1)S(1)}, u32[]{:S(2)}, u32[]{:S(2)}) collective-permute-start(bf16[16,5248]{1,0:T(8,128)(2,1)S(1)} %get-tuple-element.67), channel_id=1, source_target_pairs={{0,24},{4,28},{8,16},{12,20},{16,8},{20,12},{24,0},{28,4},{1,25},{... | collective-permute-start | bytes 503816 | tf_op jit(solution)/shard_map/ppermute | solution.py:463
  48.2 24.2 %collective-permute-start.14 = (bf16[16,5248]{1,0:T(8,128)(2,1)S(1)}, bf16[16,5248]{1,0:T(8,128)(2,1)S(1)}, u32[]{:S(2)}, u32[]{:S(2)}) collective-permute-start(bf16[16,5248]{1,0:T(8,128)(2,1)S(1)} %get-tuple-element.68), channel_id=1, source_target_pairs={{0,28},{4,24},{8,20},{12,16},{16,12},{20,8},{24,4},{28,0},{1,29},{... | collective-permute-start | bytes 503816 | tf_op jit(solution)/shard_map/ppermute | solution.py:463
  49.4 22.9 %collective-permute-start.10 = (bf16[16,5248]{1,0:T(8,128)(2,1)S(1)}, bf16[16,5248]{1,0:T(8,128)(2,1)S(1)}, u32[]{:S(2)}, u32[]{:S(2)}) collective-permute-start(bf16[16,5248]{1,0:T(8,128)(2,1)S(1)} %get-tuple-element.63), channel_id=1, source_target_pairs={{0,8},{4,12},{8,0},{12,4},{16,24},{20,28},{24,16},{28,20},{1,9},{5... | collective-permute-start | bytes 503816 | tf_op jit(solution)/shard_map/ppermute | solution.py:463
  62.7 9.7 %collective-permute-start.9 = (bf16[16,5248]{1,0:T(8,128)(2,1)S(1)}, bf16[16,5248]{1,0:T(8,128)(2,1)S(1)}, u32[]{:S(2)}, u32[]{:S(2)}) collective-permute-start(bf16[16,5248]{1,0:T(8,128)(2,1)S(1)} %get-tuple-element.62), channel_id=1, source_target_pairs={{0,4},{4,0},{8,12},{12,8},{16,20},{20,16},{24,28},{28,24},{1,5},{5... | collective-permute-start | bytes 503816 | tf_op jit(solution)/shard_map/ppermute | solution.py:463

commit v28 on v26

--- a/solution.py
+++ b/solution.py
@@ -46,17 +46,27 @@
 def prepare_kernel(number, where_ref, *refs):
     sources, (own, swap, held, turned, sems) = refs[:number], refs[number:]
     part = held.shape[2] // 2
+    cut = held.shape[1] // 2
     loads = [
-        pltpu.make_async_copy(ref, held.at[i], sems.at[i]) for i, ref in enumerate(sources)
+        [
+            pltpu.make_async_copy(
+                ref.at[pl.ds(k * cut, cut)], held.at[i, pl.ds(k * cut, cut)], sems.at[2 * i + k]
+            )
+            for k in range(2)
+        ]
+        for i, ref in enumerate(sources)
     ]
-    for load in loads:
-        load.start()
+    for pair in loads:
+        for load in pair:
+            load.start()
     half = where_ref[0] % 2
     mine = pl.multiple_of(half * part, 16)
     other = pl.multiple_of((1 - half) * part, 16)
     for i in range(number):
-        loads[i].wait()
-        turned[i] = held[i].T
+        for k in range(2):
+            loads[i][k].wait()
+            piece = slice(k * cut, (k + 1) * cut)
+            turned[i, :, piece] = held[i, piece, :].T
         own[i * part : (i + 1) * part, :] = turned[i, pl.ds(mine, part), :]
         swap[i * part : (i + 1) * part, :] = turned[i, pl.ds(other, part), :]
 
@@ -73,7 +83,7 @@
         scratch_shapes=[
             pltpu.VMEM((number, rows, features), arrays[0].dtype),
             pltpu.VMEM((number, features, rows), arrays[0].dtype),
-            pltpu.SemaphoreType.DMA((number,)),
+            pltpu.SemaphoreType.DMA((2 * number,)),
         ],
         compiler_params=limit(53),
     )(where, *arrays)
@@ -356,7 +366,7 @@
 def place_kernel(*refs):
     *arrived, out_hbm, held, sems = refs
     capacity, merged = out_hbm.shape
-    step = merged // 4
+    step = merged // 8
 
     def columns_of(start, size):
         return jnp.concatenate([ref[:, start : start + size] for ref in arrived], axis=0)
@@ -365,7 +375,7 @@
     row = lax.broadcasted_iota(jnp.int32, (offset.shape[0], capacity), 1).astype(jnp.float32)
     pick = jnp.where(offset == row, 1.0, 0.0).astype(jnp.bfloat16)
     stores = []
-    for j in range(4):
+    for j in range(8):
         held[j] = lax.dot_general(
             pick,
             columns_of(j * step, step),
@@ -386,8 +396,8 @@
         in_specs=[vmem()] * len(arrived),
         out_specs=anywhere(),
         scratch_shapes=[
-            pltpu.VMEM((4, capacity, merged // 4), jnp.bfloat16),
-            pltpu.SemaphoreType.DMA((4,)),
+            pltpu.VMEM((8, capacity, merged // 8), jnp.bfloat16),
+            pltpu.SemaphoreType.DMA((8,)),
         ],
         compiler_params=limit(24),
     )(*arrived)

time: 69 us -> 69.3 us (level)
  the two profiles are of different devices: /device:TPU:14 before, /device:TPU:8 now
where the time goes in v28:
time: 69.3 us; the launch traced here: 69.4 us
  waiting for transfers between devices  33.6 us (48%)
  starting transfers between devices  21 us (30%)
  Pallas kernels  13.5 us (19%)
  local copies, waits for them, and re-layouts  1 us (1%)
    ppermute x7, waiting for transfers between devices, cross(): lax.ppermute(arrived[d], 'blk', [(i, i ^ d) for i in range(nblocks)])  21.9 us
    ppermute x7, starting transfers between devices, cross(): lax.ppermute(arrived[d], 'blk', [(i, i ^ d) for i in range(nblocks)])  8.73 us
    pallas_call x4, Pallas kernels, attention(): pl.pallas_call(functools.partial(attention_kernel, kinds, numbers, rows_o...  7.58 us
    ppermute x1, waiting for transfers between devices, per_device(): back_other = relay(ready)  3.66 us
    ppermute x1, starting transfers between devices, per_device(): back_own = back(own_kv)  3.48 us
    ppermute x1, waiting for transfers between devices, per_device(): ahead_own = ahead(own_kv)  2.97 us
    ppermute x1, waiting for transfers between devices, per_device(): other = swap(other)  2.89 us
    ppermute x1, starting transfers between devices, per_device(): ahead_own = ahead(own_kv)  2.35 us
  transfers between devices with their start and end apart: 15, of which 11 were waited for; matrix products, arithmetic and copies ran while one was open for 0% of the time, Pallas kernels for 14%

profile of v28, /device:TPU:8, one launch (start us, length us, event | category | flops | bytes accessed | tf_op | source)
XLA Modules:
  0.0 69.4 jit_solution(16121177215147776422)
XLA Ops:
  0.0 1.5 %shard_map.92 = (bf16[640,256]{1,0:T(8,128)(2,1)S(1)}, bf16[640,256]{1,0:T(8,128)(2,1)S(1)}) custom-call(s32[1]{0:T(128)} %bitcast.where_ref, bf16[256,640]{1,0:T(8,128)(2,1)} %refs_0_.1, bf16[256,640]{1,0:T(8,128)(2,1)} %refs_1_.1), custom_call_target="tpu_custom_call" | custom-call | tf_op jit(solution)/shard_map/pallas_call | solution.py:78
  1.5 1.6 %collective-permute-start = (bf16[640,256]{1,0:T(8,128)(2,1)S(1)}, bf16[640,256]{1,0:T(8,128)(2,1)S(1)}, u32[]{:S(2)}, u32[]{:S(2)}) collective-permute-start(bf16[640,256]{1,0:T(8,128)(2,1)S(1)} %get-tuple-element.43), channel_id=1, source_target_pairs={{0,4},{4,0},{8,12},{12,8},{16,20},{20,16},{24,28},{28,24},{1,5},{5... | collective-permute-start | bytes 983048 | tf_op jit(solution)/shard_map/ppermute | solution.py:446
  3.1 2.3 %collective-permute-start.1 = (bf16[640,256]{1,0:T(8,128)(2,1)S(1)}, bf16[640,256]{1,0:T(8,128)(2,1)S(1)}, u32[]{:S(2)}, u32[]{:S(2)}) collective-permute-start(bf16[640,256]{1,0:T(8,128)(2,1)S(1)} %get-tuple-element.44.refs_1_), channel_id=1, source_target_pairs={{4,12},{8,0},{12,20},{16,8},{20,28},{24,16},{5,13},{9,1},{13,21},{... | collective-permute-start | bytes 983048 | tf_op jit(solution)/shard_map/ppermute | solution.py:447
  5.4 3.5 %collective-permute-start.3 = (bf16[640,256]{1,0:T(8,128)(2,1)S(1)}, bf16[640,256]{1,0:T(8,128)(2,1)S(1)}, u32[]{:S(2)}, u32[]{:S(2)}) collective-permute-start(bf16[640,256]{1,0:T(8,128)(2,1)S(1)} %get-tuple-element.44.refs_1_), channel_id=1, source_target_pairs={{0,8},{8,16},{12,4},{16,24},{20,12},{28,20},{1,9},{9,17},{13,5},{1... | collective-permute-start | bytes 983048 | tf_op jit(solution)/shard_map/ppermute | solution.py:448
  11.1 3.0 %collective-permute-done.1.refs_1_.refs_3_ = bf16[640,256]{1,0:T(8,128)(2,1)S(1)} collective-permute-done((bf16[640,256]{1,0:T(8,128)(2,1)S(1)}, bf16[640,256]{1,0:T(8,128)(2,1)S(1)}, u32[]{:S(2)}, u32[]{:S(2)}) %collective-permute-start.1) | collective-permute-done | bytes 327712 | tf_op jit(solution)/shard_map/ppermute | solution.py:447
  14.7 1.3 %collective-permute-done.4.refs_0_ = bf16[320,256]{1,0:T(8,128)(2,1)S(1)} collective-permute-done((bf16[320,256]{1,0:T(8,128)(2,1)S(1)}, bf16[320,256]{1,0:T(8,128)(2,1)S(1)}, u32[]{:S(2)}, u32[]{:S(2)}) %collective-permute-start.4) | collective-permute-done | bytes 163872 | tf_op jit(solution)/shard_map/ppermute | solution.py:449
  16.2 1.6 %collective-permute-start.5 = (bf16[640,256]{1,0:T(8,128)(2,1)S(1)}, bf16[640,256]{1,0:T(8,128)(2,1)S(1)}, u32[]{:S(2)}, u32[]{:S(2)}) collective-permute-start(bf16[640,256]{1,0:T(8,128)(2,1)S(1)} %collective-permute-done.refs_0_.refs_2_), channel_id=1, source_target_pairs={{0,8},{4,0},{8,16},{12,4},{16,24},{20,12},{24,28},{28,20},{1,9},{5... | collective-permute-start | bytes 983048 | tf_op jit(solution)/shard_map/ppermute | solution.py:451
  18.5 2.0 %shard_map.95 = (f32[1,4,256,128]{3,2,1,0:T(8,128)S(1)}, f32[1,4,256,128]{3,2,1,0:T(8,128)S(1)}) custom-call(s32[1]{0:T(128)} %bitcast.where_ref, s32[8,128]{1,0:T(8,128)S(1)} %get-tuple-element.37.need_ref, f32[1,2048]{1,0:T(1,128)S(1)} %get-tuple-element.38.seg_ref, bf16[320,256]{1,0:T(8,128)(2,1)S(1)} %get-tuple-element.42.refs_0_, ...), custom_call_target="tpu_custom_call" | custom-call | flops 1000 | bytes 1000 | tf_op jit(solution)/shard_map/pallas_call | solution.py:241
  20.5 3.7 %collective-permute-done.5.refs_2_.refs_5_ = bf16[640,256]{1,0:T(8,128)(2,1)S(1)} collective-permute-done((bf16[640,256]{1,0:T(8,128)(2,1)S(1)}, bf16[640,256]{1,0:T(8,128)(2,1)S(1)}, u32[]{:S(2)}, u32[]{:S(2)}) %collective-permute-start.5) | collective-permute-done | bytes 327712 | tf_op jit(solution)/shard_map/ppermute | solution.py:451
  24.2 1.6 %collective-permute-start.6 = (bf16[640,256]{1,0:T(8,128)(2,1)S(1)}, bf16[640,256]{1,0:T(8,128)(2,1)S(1)}, u32[]{:S(2)}, u32[]{:S(2)}) collective-permute-start(bf16[640,256]{1,0:T(8,128)(2,1)S(1)} %collective-permute-done.5.refs_2_.refs_5_), channel_id=1, source_target_pairs={{0,8},{4,0},{8,16},{12,4},{16,24},{20,12},{24,28},{28,20},{1,9},{5... | collective-permute-start | bytes 983048 | tf_op jit(solution)/shard_map/ppermute | solution.py:458
  25.8 3.1 %shard_map.98 = (f32[1,4,256,128]{3,2,1,0:T(8,128)S(1)}, f32[1,4,256,128]{3,2,1,0:T(8,128)S(1)}) custom-call(s32[1]{0:T(128)} %bitcast.where_ref, s32[8,128]{1,0:T(8,128)S(1)} %get-tuple-element.37.need_ref, f32[1,2048]{1,0:T(1,128)S(1)} %get-tuple-element.38.seg_ref, bf16[320,256]{1,0:T(8,128)(2,1)S(1)} %collective-permute-done.4.refs_0_, ...), custom_call_target="tpu_custom_call" | custom-call | flops 1000 | bytes 1000 | tf_op jit(solution)/shard_map/pallas_call | solution.py:241
  29.5 1.2 %shard_map.99 = bf16[320,256]{1,0:T(8,128)(2,1)S(1)} custom-call(s32[1]{0:T(128)} %bitcast.where_ref, s32[8,128]{1,0:T(8,128)S(1)} %get-tuple-element.37.need_ref, f32[1,2048]{1,0:T(1,128)S(1)} %get-tuple-element.38.seg_ref, bf16[320,256]{1,0:T(8,128)(2,1)S(1)} %collective-permute-done.4.refs_0_, bf16[1280,256]{1,0:T(8,128)(2,1)S(1)} %collective-permute-done.2.refs_1_, ...), custom_call_target="tpu_custom_call" | custom-call | flops 1000 | bytes 1000 | tf_op jit(solution)/shard_map/pallas_call | solution.py:241
  31.4 1.3 %shard_map.96.own_ref = bf16[320,256]{1,0:T(8,128)(2,1)S(1)} custom-call(s32[1]{0:T(128)} %bitcast.where_ref, s32[8,128]{1,0:T(8,128)S(1)} %get-tuple-element.37.need_ref, f32[1,2048]{1,0:T(1,128)S(1)} %get-tuple-element.38.seg_ref, bf16[320,256]{1,0:T(8,128)(2,1)S(1)} %get-tuple-element.42.refs_0_, bf16[1280,256]{1,0:T(8,128)(2,1)S(1)} %collective-permute-done.2.refs_1_, ...), custom_call_target="tpu_custom_call" | custom-call | flops 1000 | bytes 1000 | tf_op jit(solution)/shard_map/pallas_call | solution.py:241
  33.3 2.9 %collective-permute-done.7.other_ref = bf16[320,256]{1,0:T(8,128)(2,1)S(1)} collective-permute-done((bf16[320,256]{1,0:T(8,128)(2,1)S(1)}, bf16[320,256]{1,0:T(8,128)(2,1)S(1)}, u32[]{:S(2)}, u32[]{:S(2)}) %collective-permute-start.7) | collective-permute-done | bytes 163872 | tf_op jit(solution)/shard_map/ppermute | solution.py:463
  37.3 2.3 %collective-permute-start.11 = (bf16[16,5248]{1,0:T(8,128)(2,1)S(1)}, bf16[16,5248]{1,0:T(8,128)(2,1)S(1)}, u32[]{:S(2)}, u32[]{:S(2)}) collective-permute-start(bf16[16,5248]{1,0:T(8,128)(2,1)S(1)} %get-tuple-element.65), channel_id=1, source_target_pairs={{0,16},{4,20},{8,24},{12,28},{16,0},{20,4},{24,8},{28,12},{1,17},{... | collective-permute-start | bytes 503816 | tf_op jit(solution)/shard_map/ppermute | solution.py:476
  39.5 2.0 %collective-permute-start.12 = (bf16[16,5248]{1,0:T(8,128)(2,1)S(1)}, bf16[16,5248]{1,0:T(8,128)(2,1)S(1)}, u32[]{:S(2)}, u32[]{:S(2)}) collective-permute-start(bf16[16,5248]{1,0:T(8,128)(2,1)S(1)} %get-tuple-element.66), channel_id=1, source_target_pairs={{0,20},{4,16},{8,28},{12,24},{16,4},{20,0},{24,12},{28,8},{1,21},{... | collective-permute-start | bytes 503816 | tf_op jit(solution)/shard_map/ppermute | solution.py:476
  41.5 1.0 %collective-permute-start.13 = (bf16[16,5248]{1,0:T(8,128)(2,1)S(1)}, bf16[16,5248]{1,0:T(8,128)(2,1)S(1)}, u32[]{:S(2)}, u32[]{:S(2)}) collective-permute-start(bf16[16,5248]{1,0:T(8,128)(2,1)S(1)} %get-tuple-element.67), channel_id=1, source_target_pairs={{0,24},{4,28},{8,16},{12,20},{16,8},{20,12},{24,0},{28,4},{1,25},{... | collective-permute-start | bytes 503816 | tf_op jit(solution)/shard_map/ppermute | solution.py:476
  43.5 1.9 %collective-permute-done.8.refs_3_ = bf16[16,5248]{1,0:T(8,128)(2,1)S(1)} collective-permute-done((bf16[16,5248]{1,0:T(8,128)(2,1)S(1)}, bf16[16,5248]{1,0:T(8,128)(2,1)S(1)}, u32[]{:S(2)}, u32[]{:S(2)}) %collective-permute-start.8) | collective-permute-done | bytes 167968 | tf_op jit(solution)/shard_map/ppermute | solution.py:476
  45.4 1.5 %collective-permute-start.10 = (bf16[16,5248]{1,0:T(8,128)(2,1)S(1)}, bf16[16,5248]{1,0:T(8,128)(2,1)S(1)}, u32[]{:S(2)}, u32[]{:S(2)}) collective-permute-start(bf16[16,5248]{1,0:T(8,128)(2,1)S(1)} %get-tuple-element.63), channel_id=1, source_target_pairs={{0,8},{4,12},{8,0},{12,4},{16,24},{20,28},{24,16},{28,20},{1,9},{5... | collective-permute-start | bytes 503816 | tf_op jit(solution)/shard_map/ppermute | solution.py:476
  46.9 9.7 %collective-permute-done.11.refs_4_ = bf16[16,5248]{1,0:T(8,128)(2,1)S(1)} collective-permute-done((bf16[16,5248]{1,0:T(8,128)(2,1)S(1)}, bf16[16,5248]{1,0:T(8,128)(2,1)S(1)}, u32[]{:S(2)}, u32[]{:S(2)}) %collective-permute-start.11) | collective-permute-done | bytes 167968 | tf_op jit(solution)/shard_map/ppermute | solution.py:476
  57.5 2.8 %collective-permute-done.12.refs_5_ = bf16[16,5248]{1,0:T(8,128)(2,1)S(1)} collective-permute-done((bf16[16,5248]{1,0:T(8,128)(2,1)S(1)}, bf16[16,5248]{1,0:T(8,128)(2,1)S(1)}, u32[]{:S(2)}, u32[]{:S(2)}) %collective-permute-start.12) | collective-permute-done | bytes 167968 | tf_op jit(solution)/shard_map/ppermute | solution.py:476
  60.3 4.4 %collective-permute-done.13.refs_6_ = bf16[16,5248]{1,0:T(8,128)(2,1)S(1)} collective-permute-done((bf16[16,5248]{1,0:T(8,128)(2,1)S(1)}, bf16[16,5248]{1,0:T(8,128)(2,1)S(1)}, u32[]{:S(2)}, u32[]{:S(2)}) %collective-permute-start.13) | collective-permute-done | bytes 167968 | tf_op jit(solution)/shard_map/ppermute | solution.py:476
  64.7 3.1 %collective-permute-done.14.refs_7_ = bf16[16,5248]{1,0:T(8,128)(2,1)S(1)} collective-permute-done((bf16[16,5248]{1,0:T(8,128)(2,1)S(1)}, bf16[16,5248]{1,0:T(8,128)(2,1)S(1)}, u32[]{:S(2)}, u32[]{:S(2)}) %collective-permute-start.14) | collective-permute-done | bytes 167968 | tf_op jit(solution)/shard_map/ppermute | solution.py:476
  67.8 1.4 %shard_map.101 = bf16[128,5120]{1,0:T(8,128)(2,1)} custom-call(bf16[16,5248]{1,0:T(8,128)(2,1)S(1)} %get-tuple-element.58.refs_0_, bf16[16,5248]{1,0:T(8,128)(2,1)S(1)} %collective-permute-done.9.refs_1_, bf16[16,5248]{1,0:T(8,128)(2,1)S(1)} %collective-permute-done.10.refs_2_, bf16[16,5248]{1,0:T(8,128)(2,1)S(1)} %collective-permute-done.8.refs_3_, ...), custom_call_target="tpu_custom_call" | custom-call | tf_op jit(solution)/shard_map/pallas_call | solution.py:393
  (31 shorter events, 8.5 us)
Async XLA Ops:
  0.0 17.8 %copy-start.3 = (s32[2048]{0:T(1024)S(1)}, s32[2048]{0:T(1024)}, u32[]{:S(2)}) copy-start(s32[2048]{0:T(1024)} %param.9) | copy-start | bytes 24580
  0.0 17.8 %copy-start.4 = (s32[8,8]{1,0:T(8,128)S(1)}, s32[8,8]{1,0:T(8,128)}, u32[]{:S(2)}) copy-start(s32[8,8]{1,0:T(8,128)} %mask_ref.1) | copy-start | bytes 772
  1.5 9.7 %collective-permute-start = (bf16[640,256]{1,0:T(8,128)(2,1)S(1)}, bf16[640,256]{1,0:T(8,128)(2,1)S(1)}, u32[]{:S(2)}, u32[]{:S(2)}) collective-permute-start(bf16[640,256]{1,0:T(8,128)(2,1)S(1)} %get-tuple-element.43), channel_id=1, source_target_pairs={{0,4},{4,0},{8,12},{12,8},{16,20},{20,16},{24,28},{28,24},{1,5},{5... | collective-permute-start | bytes 983048 | tf_op jit(solution)/shard_map/ppermute | solution.py:446
  3.1 11.1 %collective-permute-start.1 = (bf16[640,256]{1,0:T(8,128)(2,1)S(1)}, bf16[640,256]{1,0:T(8,128)(2,1)S(1)}, u32[]{:S(2)}, u32[]{:S(2)}) collective-permute-start(bf16[640,256]{1,0:T(8,128)(2,1)S(1)} %get-tuple-element.44.refs_1_), channel_id=1, source_target_pairs={{4,12},{8,0},{12,20},{16,8},{20,28},{24,16},{5,13},{9,1},{13,21},{... | collective-permute-start | bytes 983048 | tf_op jit(solution)/shard_map/ppermute | solution.py:447
  5.4 10.8 %collective-permute-start.3 = (bf16[640,256]{1,0:T(8,128)(2,1)S(1)}, bf16[640,256]{1,0:T(8,128)(2,1)S(1)}, u32[]{:S(2)}, u32[]{:S(2)}) collective-permute-start(bf16[640,256]{1,0:T(8,128)(2,1)S(1)} %get-tuple-element.44.refs_1_), channel_id=1, source_target_pairs={{0,8},{8,16},{12,4},{16,24},{20,12},{28,20},{1,9},{9,17},{13,5},{1... | collective-permute-start | bytes 983048 | tf_op jit(solution)/shard_map/ppermute | solution.py:448
  8.9 1.0 %copy-start.2 = (bf16[256,640]{1,0:T(8,128)(2,1)S(1)}, bf16[256,640]{1,0:T(8,128)(2,1)}, u32[]{:S(2)}) copy-start(bf16[256,640]{1,0:T(8,128)(2,1)} %refs_0_.2) | copy-start | bytes 983044
  10.6 5.4 %collective-permute-start.4 = (bf16[320,256]{1,0:T(8,128)(2,1)S(1)}, bf16[320,256]{1,0:T(8,128)(2,1)S(1)}, u32[]{:S(2)}, u32[]{:S(2)}) collective-permute-start(bf16[320,256]{1,0:T(8,128)(2,1)S(1)} %get-tuple-element.45), channel_id=1, source_target_pairs={{0,4},{4,0},{8,12},{12,8},{16,20},{20,16},{24,28},{28,24},{1,5},{5... | collective-permute-start | bytes 491528 | tf_op jit(solution)/shard_map/ppermute | solution.py:449
  14.2 15.3 %collective-permute-start.2 = (bf16[1280,256]{1,0:T(8,128)(2,1)S(1)}, bf16[1280,256]{1,0:T(8,128)(2,1)S(1)}, u32[]{:S(2)}, u32[]{:S(2)}) collective-permute-start(bf16[1280,256]{1,0:T(8,128)(2,1)S(1)} %shard_map.94), channel_id=1, source_target_pairs={{0,4},{4,12},{8,0},{12,20},{16,8},{20,28},{24,16},{28,24},{1,5},{5... | collective-permute-start | bytes 1966088 | tf_op jit(solution)/shard_map/ppermute | solution.py:452
  16.2 8.0 %collective-permute-start.5 = (bf16[640,256]{1,0:T(8,128)(2,1)S(1)}, bf16[640,256]{1,0:T(8,128)(2,1)S(1)}, u32[]{:S(2)}, u32[]{:S(2)}) collective-permute-start(bf16[640,256]{1,0:T(8,128)(2,1)S(1)} %collective-permute-done.refs_0_.refs_2_), channel_id=1, source_target_pairs={{0,8},{4,0},{8,16},{12,4},{16,24},{20,12},{24,28},{28,20},{1,9},{5... | collective-permute-start | bytes 983048 | tf_op jit(solution)/shard_map/ppermute | solution.py:451
  24.2 7.2 %collective-permute-start.6 = (bf16[640,256]{1,0:T(8,128)(2,1)S(1)}, bf16[640,256]{1,0:T(8,128)(2,1)S(1)}, u32[]{:S(2)}, u32[]{:S(2)}) collective-permute-start(bf16[640,256]{1,0:T(8,128)(2,1)S(1)} %collective-permute-done.5.refs_2_.refs_5_), channel_id=1, source_target_pairs={{0,8},{4,0},{8,16},{12,4},{16,24},{20,12},{24,28},{28,20},{1,9},{5... | collective-permute-start | bytes 983048 | tf_op jit(solution)/shard_map/ppermute | solution.py:458
  30.7 1.9 %copy-start = (bf16[640,1280]{1,0:T(8,128)(2,1)S(1)}, bf16[640,1280]{1,0:T(8,128)(2,1)}, u32[]{:S(2)}) copy-start(bf16[640,1280]{1,0:T(8,128)(2,1)} %weight_ref.3) | copy-start | bytes 4915204
  30.8 1.9 %copy-start.1 = (bf16[256,1280]{1,0:T(8,128)(2,1)S(1)}, bf16[256,1280]{1,0:T(8,128)(2,1)}, u32[]{:S(2)}) copy-start(bf16[256,1280]{1,0:T(8,128)(2,1)} %tokens_ref.1) | copy-start | bytes 1966084
  30.8 1.9 %copy-start.5 = (s32[64]{0:T(128)S(1)}, s32[64]{0:T(128)}, u32[]{:S(2)}) copy-start(s32[64]{0:T(128)} %param.16) | copy-start | bytes 772
  30.8 1.9 %copy-start.6 = (s32[64]{0:T(128)S(1)}, s32[64]{0:T(128)}, u32[]{:S(2)}) copy-start(s32[64]{0:T(128)} %param.17) | copy-start | bytes 772
  30.8 5.4 %collective-permute-start.7 = (bf16[320,256]{1,0:T(8,128)(2,1)S(1)}, bf16[320,256]{1,0:T(8,128)(2,1)S(1)}, u32[]{:S(2)}, u32[]{:S(2)}) collective-permute-start(bf16[320,256]{1,0:T(8,128)(2,1)S(1)} %shard_map.99), channel_id=1, source_target_pairs={{0,4},{4,0},{8,12},{12,8},{16,20},{20,16},{24,28},{28,24},{1,5},{5... | collective-permute-start | bytes 491528 | tf_op jit(solution)/shard_map/ppermute | solution.py:463
  37.2 8.2 %collective-permute-start.8 = (bf16[16,5248]{1,0:T(8,128)(2,1)S(1)}, bf16[16,5248]{1,0:T(8,128)(2,1)S(1)}, u32[]{:S(2)}, u32[]{:S(2)}) collective-permute-start(bf16[16,5248]{1,0:T(8,128)(2,1)S(1)} %get-tuple-element.59), channel_id=1, source_target_pairs={{0,12},{4,8},{8,4},{12,0},{16,28},{20,24},{24,20},{28,16},{1,13},{... | collective-permute-start | bytes 503816 | tf_op jit(solution)/shard_map/ppermute | solution.py:476
  37.3 19.3 %collective-permute-start.11 = (bf16[16,5248]{1,0:T(8,128)(2,1)S(1)}, bf16[16,5248]{1,0:T(8,128)(2,1)S(1)}, u32[]{:S(2)}, u32[]{:S(2)}) collective-permute-start(bf16[16,5248]{1,0:T(8,128)(2,1)S(1)} %get-tuple-element.65), channel_id=1, source_target_pairs={{0,16},{4,20},{8,24},{12,28},{16,0},{20,4},{24,8},{28,12},{1,17},{... | collective-permute-start | bytes 503816 | tf_op jit(solution)/shard_map/ppermute | solution.py:476
  39.5 20.8 %collective-permute-start.12 = (bf16[16,5248]{1,0:T(8,128)(2,1)S(1)}, bf16[16,5248]{1,0:T(8,128)(2,1)S(1)}, u32[]{:S(2)}, u32[]{:S(2)}) collective-permute-start(bf16[16,5248]{1,0:T(8,128)(2,1)S(1)} %get-tuple-element.66), channel_id=1, source_target_pairs={{0,20},{4,16},{8,28},{12,24},{16,4},{20,0},{24,12},{28,8},{1,21},{... | collective-permute-start | bytes 503816 | tf_op jit(solution)/shard_map/ppermute | solution.py:476
  41.5 23.2 %collective-permute-start.13 = (bf16[16,5248]{1,0:T(8,128)(2,1)S(1)}, bf16[16,5248]{1,0:T(8,128)(2,1)S(1)}, u32[]{:S(2)}, u32[]{:S(2)}) collective-permute-start(bf16[16,5248]{1,0:T(8,128)(2,1)S(1)} %get-tuple-element.67), channel_id=1, source_target_pairs={{0,24},{4,28},{8,16},{12,20},{16,8},{20,12},{24,0},{28,4},{1,25},{... | collective-permute-start | bytes 503816 | tf_op jit(solution)/shard_map/ppermute | solution.py:476
  42.6 25.2 %collective-permute-start.14 = (bf16[16,5248]{1,0:T(8,128)(2,1)S(1)}, bf16[16,5248]{1,0:T(8,128)(2,1)S(1)}, u32[]{:S(2)}, u32[]{:S(2)}) collective-permute-start(bf16[16,5248]{1,0:T(8,128)(2,1)S(1)} %get-tuple-element.68), channel_id=1, source_target_pairs={{0,28},{4,24},{8,20},{12,16},{16,12},{20,8},{24,4},{28,0},{1,29},{... | collective-permute-start | bytes 503816 | tf_op jit(solution)/shard_map/ppermute | solution.py:476
  45.4 22.4 %collective-permute-start.10 = (bf16[16,5248]{1,0:T(8,128)(2,1)S(1)}, bf16[16,5248]{1,0:T(8,128)(2,1)S(1)}, u32[]{:S(2)}, u32[]{:S(2)}) collective-permute-start(bf16[16,5248]{1,0:T(8,128)(2,1)S(1)} %get-tuple-element.63), channel_id=1, source_target_pairs={{0,8},{4,12},{8,0},{12,4},{16,24},{20,28},{24,16},{28,20},{1,9},{5... | collective-permute-start | bytes 503816 | tf_op jit(solution)/shard_map/ppermute | solution.py:476
  56.5 11.2 %collective-permute-start.9 = (bf16[16,5248]{1,0:T(8,128)(2,1)S(1)}, bf16[16,5248]{1,0:T(8,128)(2,1)S(1)}, u32[]{:S(2)}, u32[]{:S(2)}) collective-permute-start(bf16[16,5248]{1,0:T(8,128)(2,1)S(1)} %get-tuple-element.62), channel_id=1, source_target_pairs={{0,4},{4,0},{8,12},{12,8},{16,20},{20,16},{24,28},{28,24},{1,5},{5... | collective-permute-start | bytes 503816 | tf_op jit(solution)/shard_map/ppermute | solution.py:476

commit v29 on v26

--- a/solution.py
+++ b/solution.py
@@ -445,7 +445,7 @@
     fixed = (where, need, segs)
     own = attention(*fixed, (own_q,), (0,), near, near_numbers, None, False)
     back_other, own = lax.optimization_barrier((back_other, own))
-    back_far = relay(back_other)
+    back_far = back(back_other)
     other = attention(
         *fixed, (other_q,), (1,), (*near, back_other), (*near_numbers, 5), None, False
     )

time: 69 us -> 69.8 us (1.012)
  starting transfers between devices: 21.6 us -> 25.6 us
  waiting for transfers between devices: 32.4 us -> 28.6 us
    ppermute x1, starting transfers between devices: 0.47 us -> 2.36 us  [per_device(): back_far = back(back_other)]
    ppermute x1, starting transfers between devices: 0.88 us -> 2.5 us  [per_device(): other = swap(other)]
    ppermute x1, waiting for transfers between devices: 1.56 us -> 0.01 us  [per_device(): ahead_both = ahead_all(stack(other_kv, ahead_own))]
    ppermute x1, waiting for transfers between devices: 1.4 us -> 0.3 us  [per_device(): other = swap(other)]
  transfers between devices with their start and end apart: 15 -> 15, of which waited for: 12 -> 11; matrix products, arithmetic and copies ran while one was open for 0% -> 0% of each run, Pallas kernels for 13% -> 14%
where the time goes in v29:
time: 69.8 us; the launch traced here: 68.6 us
  waiting for transfers between devices  28.6 us (41%)
  starting transfers between devices  25.6 us (37%)
  Pallas kernels  13.1 us (19%)
  local copies, waits for them, and re-layouts  1 us (1%)
    ppermute x7, waiting for transfers between devices, cross(): lax.ppermute(arrived[d], 'blk', [(i, i ^ d) for i in range(nblocks)])  19.5 us
    ppermute x7, starting transfers between devices, cross(): lax.ppermute(arrived[d], 'blk', [(i, i ^ d) for i in range(nblocks)])  10.6 us
    pallas_call x4, Pallas kernels, attention(): pl.pallas_call(functools.partial(attention_kernel, kinds, numbers, rows_o...  7.63 us
    ppermute x1, waiting for transfers between devices, per_device(): back_other = relay(ready)  4.29 us
    ppermute x1, starting transfers between devices, per_device(): ahead_own = ahead(own_kv)  3.47 us
    ppermute x1, starting transfers between devices, per_device(): other = swap(other)  2.5 us
    ppermute x1, starting transfers between devices, per_device(): back_own = back(own_kv)  2.37 us
    ppermute x1, starting transfers between devices, per_device(): back_far = back(back_other)  2.36 us
  transfers between devices with their start and end apart: 15, of which 11 were waited for; matrix products, arithmetic and copies ran while one was open for 0% of the time, Pallas kernels for 14%

profile of v29, /device:TPU:14, one launch (start us, length us, event | category | flops | bytes accessed | tf_op | source)
XLA Modules:
  0.0 68.6 jit_solution(10326444218132427050)
XLA Ops:
  0.0 1.4 %shard_map.92 = (bf16[640,256]{1,0:T(8,128)(2,1)S(1)}, bf16[640,256]{1,0:T(8,128)(2,1)S(1)}) custom-call(s32[1]{0:T(128)} %bitcast.where_ref, bf16[256,640]{1,0:T(8,128)(2,1)} %refs_0_.1, bf16[256,640]{1,0:T(8,128)(2,1)} %refs_1_.1), custom_call_target="tpu_custom_call" | custom-call | tf_op jit(solution)/shard_map/pallas_call | solution.py:68
  1.9 3.5 %collective-permute-start.1 = (bf16[640,256]{1,0:T(8,128)(2,1)S(1)}, bf16[640,256]{1,0:T(8,128)(2,1)S(1)}, u32[]{:S(2)}, u32[]{:S(2)}) collective-permute-start(bf16[640,256]{1,0:T(8,128)(2,1)S(1)} %get-tuple-element.44.refs_1_), channel_id=1, source_target_pairs={{4,12},{8,0},{12,20},{16,8},{20,28},{24,16},{5,13},{9,1},{13,21},{... | collective-permute-start | bytes 983048 | tf_op jit(solution)/shard_map/ppermute | solution.py:437
  5.4 2.4 %collective-permute-start.3 = (bf16[640,256]{1,0:T(8,128)(2,1)S(1)}, bf16[640,256]{1,0:T(8,128)(2,1)S(1)}, u32[]{:S(2)}, u32[]{:S(2)}) collective-permute-start(bf16[640,256]{1,0:T(8,128)(2,1)S(1)} %get-tuple-element.44.refs_1_), channel_id=1, source_target_pairs={{0,8},{8,16},{12,4},{16,24},{20,12},{28,20},{1,9},{9,17},{13,5},{1... | collective-permute-start | bytes 983048 | tf_op jit(solution)/shard_map/ppermute | solution.py:438
  9.1 1.6 %collective-permute-start.4 = (bf16[320,256]{1,0:T(8,128)(2,1)S(1)}, bf16[320,256]{1,0:T(8,128)(2,1)S(1)}, u32[]{:S(2)}, u32[]{:S(2)}) collective-permute-start(bf16[320,256]{1,0:T(8,128)(2,1)S(1)} %get-tuple-element.45), channel_id=1, source_target_pairs={{0,4},{4,0},{8,12},{12,8},{16,20},{20,16},{24,28},{28,24},{1,5},{5... | collective-permute-start | bytes 491528 | tf_op jit(solution)/shard_map/ppermute | solution.py:439
  11.0 2.0 %collective-permute-done.1.refs_1_.refs_3_ = bf16[640,256]{1,0:T(8,128)(2,1)S(1)} collective-permute-done((bf16[640,256]{1,0:T(8,128)(2,1)S(1)}, bf16[640,256]{1,0:T(8,128)(2,1)S(1)}, u32[]{:S(2)}, u32[]{:S(2)}) %collective-permute-start.1) | collective-permute-done | bytes 327712 | tf_op jit(solution)/shard_map/ppermute | solution.py:437
  13.0 1.6 %collective-permute-start.2 = (bf16[1280,256]{1,0:T(8,128)(2,1)S(1)}, bf16[1280,256]{1,0:T(8,128)(2,1)S(1)}, u32[]{:S(2)}, u32[]{:S(2)}) collective-permute-start(bf16[1280,256]{1,0:T(8,128)(2,1)S(1)} %shard_map.94), channel_id=1, source_target_pairs={{0,4},{4,12},{8,0},{12,20},{16,8},{20,28},{24,16},{28,24},{1,5},{5... | collective-permute-start | bytes 1966088 | tf_op jit(solution)/shard_map/ppermute | solution.py:442
  14.7 1.5 %collective-permute-done.3.refs_4_ = bf16[640,256]{1,0:T(8,128)(2,1)S(1)} collective-permute-done((bf16[640,256]{1,0:T(8,128)(2,1)S(1)}, bf16[640,256]{1,0:T(8,128)(2,1)S(1)}, u32[]{:S(2)}, u32[]{:S(2)}) %collective-permute-start.3) | collective-permute-done | bytes 327712 | tf_op jit(solution)/shard_map/ppermute | solution.py:438
  17.4 2.5 %shard_map.95 = (f32[1,4,256,128]{3,2,1,0:T(8,128)S(1)}, f32[1,4,256,128]{3,2,1,0:T(8,128)S(1)}) custom-call(s32[1]{0:T(128)} %bitcast.where_ref, s32[8,128]{1,0:T(8,128)S(1)} %get-tuple-element.37.need_ref, f32[1,2048]{1,0:T(1,128)S(1)} %get-tuple-element.38.seg_ref, bf16[320,256]{1,0:T(8,128)(2,1)S(1)} %get-tuple-element.42.refs_0_, ...), custom_call_target="tpu_custom_call" | custom-call | flops 1000 | bytes 1000 | tf_op jit(solution)/shard_map/pallas_call | solution.py:231
  19.9 4.3 %collective-permute-done.5.refs_2_.refs_5_ = bf16[640,256]{1,0:T(8,128)(2,1)S(1)} collective-permute-done((bf16[640,256]{1,0:T(8,128)(2,1)S(1)}, bf16[640,256]{1,0:T(8,128)(2,1)S(1)}, u32[]{:S(2)}, u32[]{:S(2)}) %collective-permute-start.5) | collective-permute-done | bytes 327712 | tf_op jit(solution)/shard_map/ppermute | solution.py:441
  24.2 2.4 %collective-permute-start.6 = (bf16[640,256]{1,0:T(8,128)(2,1)S(1)}, bf16[640,256]{1,0:T(8,128)(2,1)S(1)}, u32[]{:S(2)}, u32[]{:S(2)}) collective-permute-start(bf16[640,256]{1,0:T(8,128)(2,1)S(1)} %collective-permute-done.5.refs_2_.refs_5_), channel_id=1, source_target_pairs={{0,8},{8,16},{12,4},{16,24},{20,12},{28,20},{1,9},{9,17},{13,5},{1... | collective-permute-start | bytes 983048 | tf_op jit(solution)/shard_map/ppermute | solution.py:448
  26.5 2.2 %shard_map.98 = (f32[1,4,256,128]{3,2,1,0:T(8,128)S(1)}, f32[1,4,256,128]{3,2,1,0:T(8,128)S(1)}) custom-call(s32[1]{0:T(128)} %bitcast.where_ref, s32[8,128]{1,0:T(8,128)S(1)} %get-tuple-element.37.need_ref, f32[1,2048]{1,0:T(1,128)S(1)} %get-tuple-element.38.seg_ref, bf16[320,256]{1,0:T(8,128)(2,1)S(1)} %collective-permute-done.4.refs_0_, ...), custom_call_target="tpu_custom_call" | custom-call | flops 1000 | bytes 1000 | tf_op jit(solution)/shard_map/pallas_call | solution.py:231
  28.7 1.2 %shard_map.99 = bf16[320,256]{1,0:T(8,128)(2,1)S(1)} custom-call(s32[1]{0:T(128)} %bitcast.where_ref, s32[8,128]{1,0:T(8,128)S(1)} %get-tuple-element.37.need_ref, f32[1,2048]{1,0:T(1,128)S(1)} %get-tuple-element.38.seg_ref, bf16[320,256]{1,0:T(8,128)(2,1)S(1)} %collective-permute-done.4.refs_0_, bf16[1280,256]{1,0:T(8,128)(2,1)S(1)} %collective-permute-done.2.refs_1_, ...), custom_call_target="tpu_custom_call" | custom-call | flops 1000 | bytes 1000 | tf_op jit(solution)/shard_map/pallas_call | solution.py:231
  30.0 2.5 %collective-permute-start.7 = (bf16[320,256]{1,0:T(8,128)(2,1)S(1)}, bf16[320,256]{1,0:T(8,128)(2,1)S(1)}, u32[]{:S(2)}, u32[]{:S(2)}) collective-permute-start(bf16[320,256]{1,0:T(8,128)(2,1)S(1)} %shard_map.99), channel_id=1, source_target_pairs={{0,4},{4,0},{8,12},{12,8},{16,20},{20,16},{24,28},{28,24},{1,5},{5... | collective-permute-start | bytes 491528 | tf_op jit(solution)/shard_map/ppermute | solution.py:453
  33.1 1.7 %shard_map.96.own_ref = bf16[320,256]{1,0:T(8,128)(2,1)S(1)} custom-call(s32[1]{0:T(128)} %bitcast.where_ref, s32[8,128]{1,0:T(8,128)S(1)} %get-tuple-element.37.need_ref, f32[1,2048]{1,0:T(1,128)S(1)} %get-tuple-element.38.seg_ref, bf16[320,256]{1,0:T(8,128)(2,1)S(1)} %get-tuple-element.42.refs_0_, bf16[1280,256]{1,0:T(8,128)(2,1)S(1)} %collective-permute-done.2.refs_1_, ...), custom_call_target="tpu_custom_call" | custom-call | flops 1000 | bytes 1000 | tf_op jit(solution)/shard_map/pallas_call | solution.py:231
  37.9 3.1 %collective-permute-start.11 = (bf16[16,5248]{1,0:T(8,128)(2,1)S(1)}, bf16[16,5248]{1,0:T(8,128)(2,1)S(1)}, u32[]{:S(2)}, u32[]{:S(2)}) collective-permute-start(bf16[16,5248]{1,0:T(8,128)(2,1)S(1)} %get-tuple-element.65), channel_id=1, source_target_pairs={{0,16},{4,20},{8,24},{12,28},{16,0},{20,4},{24,8},{28,12},{1,17},{... | collective-permute-start | bytes 503816 | tf_op jit(solution)/shard_map/ppermute | solution.py:466
  41.4 1.4 %collective-permute-start.13 = (bf16[16,5248]{1,0:T(8,128)(2,1)S(1)}, bf16[16,5248]{1,0:T(8,128)(2,1)S(1)}, u32[]{:S(2)}, u32[]{:S(2)}) collective-permute-start(bf16[16,5248]{1,0:T(8,128)(2,1)S(1)} %get-tuple-element.67), channel_id=1, source_target_pairs={{0,24},{4,28},{8,16},{12,20},{16,8},{20,12},{24,0},{28,4},{1,25},{... | collective-permute-start | bytes 503816 | tf_op jit(solution)/shard_map/ppermute | solution.py:466
  42.8 1.1 %collective-permute-start.14 = (bf16[16,5248]{1,0:T(8,128)(2,1)S(1)}, bf16[16,5248]{1,0:T(8,128)(2,1)S(1)}, u32[]{:S(2)}, u32[]{:S(2)}) collective-permute-start(bf16[16,5248]{1,0:T(8,128)(2,1)S(1)} %get-tuple-element.68), channel_id=1, source_target_pairs={{0,28},{4,24},{8,20},{12,16},{16,12},{20,8},{24,4},{28,0},{1,29},{... | collective-permute-start | bytes 503816 | tf_op jit(solution)/shard_map/ppermute | solution.py:466
  43.9 1.1 %collective-permute-done.8.refs_3_ = bf16[16,5248]{1,0:T(8,128)(2,1)S(1)} collective-permute-done((bf16[16,5248]{1,0:T(8,128)(2,1)S(1)}, bf16[16,5248]{1,0:T(8,128)(2,1)S(1)}, u32[]{:S(2)}, u32[]{:S(2)}) %collective-permute-start.8) | collective-permute-done | bytes 167968 | tf_op jit(solution)/shard_map/ppermute | solution.py:466
  45.0 3.0 %collective-permute-start.10 = (bf16[16,5248]{1,0:T(8,128)(2,1)S(1)}, bf16[16,5248]{1,0:T(8,128)(2,1)S(1)}, u32[]{:S(2)}, u32[]{:S(2)}) collective-permute-start(bf16[16,5248]{1,0:T(8,128)(2,1)S(1)} %get-tuple-element.63), channel_id=1, source_target_pairs={{0,8},{4,12},{8,0},{12,4},{16,24},{20,28},{24,16},{28,20},{1,9},{5... | collective-permute-start | bytes 503816 | tf_op jit(solution)/shard_map/ppermute | solution.py:466
  48.0 8.2 %collective-permute-done.11.refs_4_ = bf16[16,5248]{1,0:T(8,128)(2,1)S(1)} collective-permute-done((bf16[16,5248]{1,0:T(8,128)(2,1)S(1)}, bf16[16,5248]{1,0:T(8,128)(2,1)S(1)}, u32[]{:S(2)}, u32[]{:S(2)}) %collective-permute-start.11) | collective-permute-done | bytes 167968 | tf_op jit(solution)/shard_map/ppermute | solution.py:466
  56.8 3.2 %collective-permute-done.12.refs_5_ = bf16[16,5248]{1,0:T(8,128)(2,1)S(1)} collective-permute-done((bf16[16,5248]{1,0:T(8,128)(2,1)S(1)}, bf16[16,5248]{1,0:T(8,128)(2,1)S(1)}, u32[]{:S(2)}, u32[]{:S(2)}) %collective-permute-start.12) | collective-permute-done | bytes 167968 | tf_op jit(solution)/shard_map/ppermute | solution.py:466
  60.0 5.1 %collective-permute-done.13.refs_6_ = bf16[16,5248]{1,0:T(8,128)(2,1)S(1)} collective-permute-done((bf16[16,5248]{1,0:T(8,128)(2,1)S(1)}, bf16[16,5248]{1,0:T(8,128)(2,1)S(1)}, u32[]{:S(2)}, u32[]{:S(2)}) %collective-permute-start.13) | collective-permute-done | bytes 167968 | tf_op jit(solution)/shard_map/ppermute | solution.py:466
  65.2 1.8 %collective-permute-done.14.refs_7_ = bf16[16,5248]{1,0:T(8,128)(2,1)S(1)} collective-permute-done((bf16[16,5248]{1,0:T(8,128)(2,1)S(1)}, bf16[16,5248]{1,0:T(8,128)(2,1)S(1)}, u32[]{:S(2)}, u32[]{:S(2)}) %collective-permute-start.14) | collective-permute-done | bytes 167968 | tf_op jit(solution)/shard_map/ppermute | solution.py:466
  67.0 1.4 %shard_map.101 = bf16[128,5120]{1,0:T(8,128)(2,1)} custom-call(bf16[16,5248]{1,0:T(8,128)(2,1)S(1)} %get-tuple-element.58.refs_0_, bf16[16,5248]{1,0:T(8,128)(2,1)S(1)} %collective-permute-done.9.refs_1_, bf16[16,5248]{1,0:T(8,128)(2,1)S(1)} %collective-permute-done.10.refs_2_, bf16[16,5248]{1,0:T(8,128)(2,1)S(1)} %collective-permute-done.8.refs_3_, ...), custom_call_target="tpu_custom_call" | custom-call | tf_op jit(solution)/shard_map/pallas_call | solution.py:383
  (31 shorter events, 7.9 us)
Async XLA Ops:
  0.0 16.7 %copy-start.3 = (s32[2048]{0:T(1024)S(1)}, s32[2048]{0:T(1024)}, u32[]{:S(2)}) copy-start(s32[2048]{0:T(1024)} %param.9) | copy-start | bytes 24580
  0.0 16.7 %copy-start.4 = (s32[8,8]{1,0:T(8,128)S(1)}, s32[8,8]{1,0:T(8,128)}, u32[]{:S(2)}) copy-start(s32[8,8]{1,0:T(8,128)} %mask_ref.1) | copy-start | bytes 772
  1.4 9.6 %collective-permute-start = (bf16[640,256]{1,0:T(8,128)(2,1)S(1)}, bf16[640,256]{1,0:T(8,128)(2,1)S(1)}, u32[]{:S(2)}, u32[]{:S(2)}) collective-permute-start(bf16[640,256]{1,0:T(8,128)(2,1)S(1)} %get-tuple-element.43), channel_id=1, source_target_pairs={{0,4},{4,0},{8,12},{12,8},{16,20},{20,16},{24,28},{28,24},{1,5},{5... | collective-permute-start | bytes 983048 | tf_op jit(solution)/shard_map/ppermute | solution.py:436
  1.9 11.1 %collective-permute-start.1 = (bf16[640,256]{1,0:T(8,128)(2,1)S(1)}, bf16[640,256]{1,0:T(8,128)(2,1)S(1)}, u32[]{:S(2)}, u32[]{:S(2)}) collective-permute-start(bf16[640,256]{1,0:T(8,128)(2,1)S(1)} %get-tuple-element.44.refs_1_), channel_id=1, source_target_pairs={{4,12},{8,0},{12,20},{16,8},{20,28},{24,16},{5,13},{9,1},{13,21},{... | collective-permute-start | bytes 983048 | tf_op jit(solution)/shard_map/ppermute | solution.py:437
  5.4 10.8 %collective-permute-start.3 = (bf16[640,256]{1,0:T(8,128)(2,1)S(1)}, bf16[640,256]{1,0:T(8,128)(2,1)S(1)}, u32[]{:S(2)}, u32[]{:S(2)}) collective-permute-start(bf16[640,256]{1,0:T(8,128)(2,1)S(1)} %get-tuple-element.44.refs_1_), channel_id=1, source_target_pairs={{0,8},{8,16},{12,4},{16,24},{20,12},{28,20},{1,9},{9,17},{13,5},{1... | collective-permute-start | bytes 983048 | tf_op jit(solution)/shard_map/ppermute | solution.py:438
  7.8 1.0 %copy-start.2 = (bf16[256,640]{1,0:T(8,128)(2,1)S(1)}, bf16[256,640]{1,0:T(8,128)(2,1)}, u32[]{:S(2)}) copy-start(bf16[256,640]{1,0:T(8,128)(2,1)} %refs_0_.2) | copy-start | bytes 983044
  9.1 5.6 %collective-permute-start.4 = (bf16[320,256]{1,0:T(8,128)(2,1)S(1)}, bf16[320,256]{1,0:T(8,128)(2,1)S(1)}, u32[]{:S(2)}, u32[]{:S(2)}) collective-permute-start(bf16[320,256]{1,0:T(8,128)(2,1)S(1)} %get-tuple-element.45), channel_id=1, source_target_pairs={{0,4},{4,0},{8,12},{12,8},{16,20},{20,16},{24,28},{28,24},{1,5},{5... | collective-permute-start | bytes 491528 | tf_op jit(solution)/shard_map/ppermute | solution.py:439
  13.0 15.7 %collective-permute-start.2 = (bf16[1280,256]{1,0:T(8,128)(2,1)S(1)}, bf16[1280,256]{1,0:T(8,128)(2,1)S(1)}, u32[]{:S(2)}, u32[]{:S(2)}) collective-permute-start(bf16[1280,256]{1,0:T(8,128)(2,1)S(1)} %shard_map.94), channel_id=1, source_target_pairs={{0,4},{4,12},{8,0},{12,20},{16,8},{20,28},{24,16},{28,24},{1,5},{5... | collective-permute-start | bytes 1966088 | tf_op jit(solution)/shard_map/ppermute | solution.py:442
  16.2 8.0 %collective-permute-start.5 = (bf16[640,256]{1,0:T(8,128)(2,1)S(1)}, bf16[640,256]{1,0:T(8,128)(2,1)S(1)}, u32[]{:S(2)}, u32[]{:S(2)}) collective-permute-start(bf16[640,256]{1,0:T(8,128)(2,1)S(1)} %collective-permute-done.refs_0_.refs_2_), channel_id=1, source_target_pairs={{0,8},{4,0},{8,16},{12,4},{16,24},{20,12},{24,28},{28,20},{1,9},{5... | collective-permute-start | bytes 983048 | tf_op jit(solution)/shard_map/ppermute | solution.py:441
  24.2 9.0 %collective-permute-start.6 = (bf16[640,256]{1,0:T(8,128)(2,1)S(1)}, bf16[640,256]{1,0:T(8,128)(2,1)S(1)}, u32[]{:S(2)}, u32[]{:S(2)}) collective-permute-start(bf16[640,256]{1,0:T(8,128)(2,1)S(1)} %collective-permute-done.5.refs_2_.refs_5_), channel_id=1, source_target_pairs={{0,8},{8,16},{12,4},{16,24},{20,12},{28,20},{1,9},{9,17},{13,5},{1... | collective-permute-start | bytes 983048 | tf_op jit(solution)/shard_map/ppermute | solution.py:448
  30.0 4.9 %copy-start = (bf16[640,1280]{1,0:T(8,128)(2,1)S(1)}, bf16[640,1280]{1,0:T(8,128)(2,1)}, u32[]{:S(2)}) copy-start(bf16[640,1280]{1,0:T(8,128)(2,1)} %weight_ref.3) | copy-start | bytes 4915204
  30.0 4.9 %copy-start.1 = (bf16[256,1280]{1,0:T(8,128)(2,1)S(1)}, bf16[256,1280]{1,0:T(8,128)(2,1)}, u32[]{:S(2)}) copy-start(bf16[256,1280]{1,0:T(8,128)(2,1)} %tokens_ref.1) | copy-start | bytes 1966084
  30.0 4.9 %copy-start.5 = (s32[64]{0:T(128)S(1)}, s32[64]{0:T(128)}, u32[]{:S(2)}) copy-start(s32[64]{0:T(128)} %param.16) | copy-start | bytes 772
  30.0 4.9 %copy-start.6 = (s32[64]{0:T(128)S(1)}, s32[64]{0:T(128)}, u32[]{:S(2)}) copy-start(s32[64]{0:T(128)} %param.17) | copy-start | bytes 772
  30.0 5.8 %collective-permute-start.7 = (bf16[320,256]{1,0:T(8,128)(2,1)S(1)}, bf16[320,256]{1,0:T(8,128)(2,1)S(1)}, u32[]{:S(2)}, u32[]{:S(2)}) collective-permute-start(bf16[320,256]{1,0:T(8,128)(2,1)S(1)} %shard_map.99), channel_id=1, source_target_pairs={{0,4},{4,0},{8,12},{12,8},{16,20},{20,16},{24,28},{28,24},{1,5},{5... | collective-permute-start | bytes 491528 | tf_op jit(solution)/shard_map/ppermute | solution.py:453
  36.8 8.2 %collective-permute-start.8 = (bf16[16,5248]{1,0:T(8,128)(2,1)S(1)}, bf16[16,5248]{1,0:T(8,128)(2,1)S(1)}, u32[]{:S(2)}, u32[]{:S(2)}) collective-permute-start(bf16[16,5248]{1,0:T(8,128)(2,1)S(1)} %get-tuple-element.59), channel_id=1, source_target_pairs={{0,12},{4,8},{8,4},{12,0},{16,28},{20,24},{24,20},{28,16},{1,13},{... | collective-permute-start | bytes 503816 | tf_op jit(solution)/shard_map/ppermute | solution.py:466
  37.9 18.4 %collective-permute-start.11 = (bf16[16,5248]{1,0:T(8,128)(2,1)S(1)}, bf16[16,5248]{1,0:T(8,128)(2,1)S(1)}, u32[]{:S(2)}, u32[]{:S(2)}) collective-permute-start(bf16[16,5248]{1,0:T(8,128)(2,1)S(1)} %get-tuple-element.65), channel_id=1, source_target_pairs={{0,16},{4,20},{8,24},{12,28},{16,0},{20,4},{24,8},{28,12},{1,17},{... | collective-permute-start | bytes 503816 | tf_op jit(solution)/shard_map/ppermute | solution.py:466
  41.0 19.0 %collective-permute-start.12 = (bf16[16,5248]{1,0:T(8,128)(2,1)S(1)}, bf16[16,5248]{1,0:T(8,128)(2,1)S(1)}, u32[]{:S(2)}, u32[]{:S(2)}) collective-permute-start(bf16[16,5248]{1,0:T(8,128)(2,1)S(1)} %get-tuple-element.66), channel_id=1, source_target_pairs={{0,20},{4,16},{8,28},{12,24},{16,4},{20,0},{24,12},{28,8},{1,21},{... | collective-permute-start | bytes 503816 | tf_op jit(solution)/shard_map/ppermute | solution.py:466
  41.4 23.8 %collective-permute-start.13 = (bf16[16,5248]{1,0:T(8,128)(2,1)S(1)}, bf16[16,5248]{1,0:T(8,128)(2,1)S(1)}, u32[]{:S(2)}, u32[]{:S(2)}) collective-permute-start(bf16[16,5248]{1,0:T(8,128)(2,1)S(1)} %get-tuple-element.67), channel_id=1, source_target_pairs={{0,24},{4,28},{8,16},{12,20},{16,8},{20,12},{24,0},{28,4},{1,25},{... | collective-permute-start | bytes 503816 | tf_op jit(solution)/shard_map/ppermute | solution.py:466
  42.8 24.2 %collective-permute-start.14 = (bf16[16,5248]{1,0:T(8,128)(2,1)S(1)}, bf16[16,5248]{1,0:T(8,128)(2,1)S(1)}, u32[]{:S(2)}, u32[]{:S(2)}) collective-permute-start(bf16[16,5248]{1,0:T(8,128)(2,1)S(1)} %get-tuple-element.68), channel_id=1, source_target_pairs={{0,28},{4,24},{8,20},{12,16},{16,12},{20,8},{24,4},{28,0},{1,29},{... | collective-permute-start | bytes 503816 | tf_op jit(solution)/shard_map/ppermute | solution.py:466
  45.0 22.0 %collective-permute-start.10 = (bf16[16,5248]{1,0:T(8,128)(2,1)S(1)}, bf16[16,5248]{1,0:T(8,128)(2,1)S(1)}, u32[]{:S(2)}, u32[]{:S(2)}) collective-permute-start(bf16[16,5248]{1,0:T(8,128)(2,1)S(1)} %get-tuple-element.63), channel_id=1, source_target_pairs={{0,8},{4,12},{8,0},{12,4},{16,24},{20,28},{24,16},{28,20},{1,9},{5... | collective-permute-start | bytes 503816 | tf_op jit(solution)/shard_map/ppermute | solution.py:466
  56.3 10.7 %collective-permute-start.9 = (bf16[16,5248]{1,0:T(8,128)(2,1)S(1)}, bf16[16,5248]{1,0:T(8,128)(2,1)S(1)}, u32[]{:S(2)}, u32[]{:S(2)}) collective-permute-start(bf16[16,5248]{1,0:T(8,128)(2,1)S(1)} %get-tuple-element.62), channel_id=1, source_target_pairs={{0,4},{4,0},{8,12},{12,8},{16,20},{20,16},{24,28},{28,24},{1,5},{5... | collective-permute-start | bytes 503816 | tf_op jit(solution)/shard_map/ppermute | solution.py:466
